TPU v7x, 32 devices: a whole 2x2x4 slice. The times are simulated.
32 devices in a mesh: groups: 2 (over x), tile: 16 (over z, y, core).
Axes of the slice: x: 2, y: 2, z: 4, core: 2. Of those that a mesh axis runs over, the one named last changes fastest.
Arguments:
- grid_nodes: bfloat16 [8192, 512], P(('groups', 'tile')), parts along dimension 0, may hold values from -6 to 6
- mesh_nodes: bfloat16 [2048, 512], P(('groups', 'tile')), parts along dimension 0, may hold values from -6 to 6
- enc_edges: bfloat16 [12288, 512], P(('groups', 'tile')), parts along dimension 0, may hold values from -6 to 6
- dec_edges: bfloat16 [24576, 512], P(('groups', 'tile')), parts along dimension 0, may hold values from -6 to 6
- grid_cot: bfloat16 [8192, 512], P(('groups', 'tile')), parts along dimension 0, may hold values from -6 to 6
- mesh_cot: bfloat16 [2048, 512], P(('groups', 'tile')), parts along dimension 0, may hold values from -6 to 6
- enc_first: bfloat16 [1536, 512], replicated, may hold values from -0.15625 to 0.15625
- enc_second: bfloat16 [512, 512], replicated, may hold values from -0.25 to 0.25
- mesh_first: bfloat16 [1024, 512], replicated, may hold values from -0.1875 to 0.1875
- mesh_second: bfloat16 [512, 512], replicated, may hold values from -0.25 to 0.25
- dec_first: bfloat16 [1536, 512], replicated, may hold values from -0.15625 to 0.15625
- dec_second: bfloat16 [512, 512], replicated, may hold values from -0.25 to 0.25
- grid_first: bfloat16 [1024, 512], replicated, may hold values from -0.1875 to 0.1875
- grid_second: bfloat16 [512, 512], replicated, may hold values from -0.25 to 0.25
- send_index: int32 [288, 16], P(('groups', 'tile')), parts along dimension 0, may hold values from 0 to 255, as said below
- send_count: int32 [288], P(('groups', 'tile')), parts along dimension 0, may hold values from 4 to 16, as said below
- enc_grid: int32 [12288], P(('groups', 'tile')), parts along dimension 0, may hold values from 0 to 399, as said below
- enc_mesh: int32 [12288], P(('groups', 'tile')), parts along dimension 0, may hold values from 0 to 63
- dec_grid: int32 [24576], P(('groups', 'tile')), parts along dimension 0, may hold values from 0 to 399, as said below
- dec_mesh: int32 [24576], P(('groups', 'tile')), parts along dimension 0, may hold values from 0 to 63
Outputs:
- grid_out: bfloat16 [8192, 512], P(('groups', 'tile')), parts along dimension 0
- mesh_out: bfloat16 [2048, 512], P(('groups', 'tile')), parts along dimension 0
- grad_grid: float32 [8192, 512], P(('groups', 'tile')), parts along dimension 0
- grad_mesh: float32 [2048, 512], P(('groups', 'tile')), parts along dimension 0
There are 2 independent parts, one for each index of `groups`. A program takes and returns all parts, laid end to end along the dimension named above; an argument that names none is the same for every part. Nothing has to cross between parts.
Inputs may be any that keep to these rules, and one draw needn't show every extreme that they name: `send_index`: row s * 9 + j holds distinct local grid rows of device s for its neighbour (s + o_j) mod 16; entries from send_count[s * 9 + j] on carry no row; no row of a device goes to two neighbours. `send_count`: rows from device s to its neighbour j; the count from (s + o_j) mod 16 back to s is the same, under entry (j + 4) mod 8 for j < 8 and under entry 8 for j = 8; in every draw one device receives 16 rows from each of its nine neighbours. `enc_grid`: a spot of the edge's device that is live; every live slot of a device is named by exactly one of its encoder edges. `dec_grid`: a spot of the edge's device that is live; every live slot of a device is named by exactly one of its decoder edges, and every grid node has exactly three decoder edges over all devices. `enc_mesh`: the encoder edge's mesh node among the 64 of the edge's device. `dec_mesh`: the decoder edge's mesh node among the 64 of the edge's device.
All inputs are finite; a program needn't handle non-finite values.
Results may differ from a plain program's by a relative error of at most 0.01.
Values may be sent and summed in bfloat16 or wider, within the bound.
No kernel may reach another device: no remote copies, remote signals or barrier semaphores. Data moves between devices by JAX's collectives and lax.ppermute only.
A program may use at most 128 MiB of HBM per device.

v0:
```python
import jax
import jax.numpy as jnp
from jax import lax
from jax.sharding import PartitionSpec as P

TW = 4


def mixed_dot(left, right):
    return jnp.dot(left, right, preferred_element_type=jnp.float32)


def back_dot(left, right):
    return lax.dot_general(
        left, right, (((1,), (1,)), ((), ())), preferred_element_type=jnp.float32
    )


def exact_back(left, right):
    return lax.dot_general(
        left,
        right.astype(jnp.float32),
        (((1,), (1,)), ((), ())),
        precision=lax.Precision.HIGHEST,
        preferred_element_type=jnp.float32,
    )


def pick_rows(onehot, values):
    return jnp.dot(
        onehot, values, precision=lax.Precision.HIGHEST, preferred_element_type=jnp.float32
    )


def pool_rows(onehot, values):
    return lax.dot_general(
        onehot,
        values,
        (((0,), (0,)), ((), ())),
        precision=lax.Precision.HIGHEST,
        preferred_element_type=jnp.float32,
    )


def normalize(values):
    centre = values - jnp.mean(values, axis=-1, keepdims=True)
    scale_inv = lax.rsqrt(jnp.mean(centre * centre, axis=-1, keepdims=True) + 1e-05)
    return (centre * scale_inv, scale_inv)


def normalize_back(normed, scale_inv, upstream):
    return scale_inv * (
        upstream
        - jnp.mean(upstream, axis=-1, keepdims=True)
        - normed * jnp.mean(upstream * normed, axis=-1, keepdims=True)
    )


def swish_slope(values):
    sigmoid = jax.nn.sigmoid(values)
    return sigmoid * (1.0 + values * (1.0 - sigmoid))


def neighbour_offsets(peer_count):
    forward_half = [1, TW, TW + 1, TW - 1]
    return forward_half + [-offset for offset in forward_half] + [peer_count // 2]


def peer_onehot(offsets, direction, peer_count, wire_type):
    own_index = lax.axis_index("tile")
    targets = (own_index + direction * jnp.array(offsets, dtype=jnp.int32)[:, None]) % peer_count
    peer_ids = lax.broadcasted_iota(jnp.int32, (len(offsets), peer_count), 1)
    return (peer_ids == targets).astype(wire_type)


def spread_blocks(selector, blocks):
    return jnp.einsum(
        "jp,jcd->pcd",
        selector,
        blocks,
        precision=lax.Precision.HIGHEST,
        preferred_element_type=jnp.float32,
    ).astype(blocks.dtype)


def collect_blocks(selector, arrived):
    return jnp.einsum(
        "jp,pcd->jcd",
        selector,
        arrived,
        precision=lax.Precision.HIGHEST,
        preferred_element_type=jnp.float32,
    ).astype(arrived.dtype)


def node_forward(node_rows, incoming, first, second):
    features = node_rows.shape[1]
    pre_node = mixed_dot(node_rows, first[:features]) + mixed_dot(incoming, first[features:])
    act_node = jax.nn.silu(pre_node).astype(jnp.bfloat16)
    normed, scale_inv = normalize(mixed_dot(act_node, second))
    updated = (node_rows.astype(jnp.float32) + normed).astype(jnp.bfloat16)
    return (updated, (pre_node, normed, scale_inv))


def node_backward(stored, upstream, first, second):
    pre_node, normed, scale_inv = stored
    features = upstream.shape[1]
    grad_out = normalize_back(normed, scale_inv, upstream).astype(jnp.bfloat16)
    grad_pre = (back_dot(grad_out, second) * swish_slope(pre_node)).astype(jnp.bfloat16)
    return (upstream + back_dot(grad_pre, first[:features]), back_dot(grad_pre, first[features:]))


def edge_forward(pre_edge, second):
    act_edge = jax.nn.silu(pre_edge).astype(jnp.bfloat16)
    normed, scale_inv = normalize(mixed_dot(act_edge, second))
    return (normed, (pre_edge, normed, scale_inv))


def edge_backward(stored, upstream, second):
    pre_edge, normed, scale_inv = stored
    grad_out = normalize_back(normed, scale_inv, upstream).astype(jnp.bfloat16)
    return back_dot(grad_out, second) * swish_slope(pre_edge)


def per_device(
    grid_nodes,
    mesh_nodes,
    enc_edges,
    dec_edges,
    grid_cot,
    mesh_cot,
    enc_first,
    enc_second,
    mesh_first,
    mesh_second,
    dec_first,
    dec_second,
    grid_first,
    grid_second,
    send_index,
    send_count,
    enc_grid,
    enc_mesh,
    dec_grid,
    dec_mesh,
):
    features = grid_nodes.shape[1]
    grid_count = grid_nodes.shape[0]
    mesh_count = mesh_nodes.shape[0]
    slot_width = send_index.shape[1]
    peer_count = lax.axis_size("tile")
    offsets = neighbour_offsets(peer_count)
    link_count = len(offsets)
    spot_count = grid_count + link_count * slot_width
    live_mask = lax.broadcasted_iota(jnp.int32, (link_count, slot_width), 1) < send_count[:, None]
    live_rows = live_mask[..., None]
    live_flat = live_mask.reshape(-1, 1)
    flat_index = send_index.reshape(-1)
    zero_row = jnp.zeros((), jnp.bfloat16)
    mesh_range = lax.broadcasted_iota(jnp.int32, (1, mesh_count), 1)
    enc_onehot = (enc_mesh[:, None] == mesh_range).astype(jnp.float32)
    dec_onehot = (dec_mesh[:, None] == mesh_range).astype(jnp.float32)
    outgoing = jnp.where(live_rows, grid_nodes[send_index], zero_row)
    buffer = spread_blocks(peer_onehot(offsets, 1, peer_count, jnp.bfloat16), outgoing)
    arrived = collect_blocks(
        peer_onehot(offsets, -1, peer_count, jnp.bfloat16),
        lax.all_to_all(buffer, "tile", split_axis=0, concat_axis=0, tiled=True),
    )
    spot_rows = jnp.concatenate([grid_nodes, arrived.reshape(-1, features)], axis=0)
    spot_pe = mixed_dot(spot_rows, enc_first[:features]).astype(jnp.bfloat16)
    spot_pd = mixed_dot(spot_rows, dec_first[:features]).astype(jnp.bfloat16)
    enc_pre = (
        spot_pe[enc_grid].astype(jnp.float32)
        + pick_rows(enc_onehot, mixed_dot(mesh_nodes, enc_first[features : 2 * features]))
        + mixed_dot(enc_edges, enc_first[2 * features :])
    )
    enc_msg, enc_stored = edge_forward(enc_pre, enc_second)
    mesh_agg = pool_rows(enc_onehot, enc_msg).astype(jnp.bfloat16)
    mesh_out, mesh_stored = node_forward(mesh_nodes, mesh_agg, mesh_first, mesh_second)
    dec_pre = (
        spot_pd[dec_grid].astype(jnp.float32)
        + pick_rows(dec_onehot, mixed_dot(mesh_out, dec_first[features : 2 * features]))
        + mixed_dot(dec_edges, dec_first[2 * features :])
    )
    dec_msg, dec_stored = edge_forward(dec_pre, dec_second)
    spot_msgs = jax.ops.segment_sum(dec_msg, dec_grid, num_segments=spot_count)
    slot_msgs = (
        spot_msgs[grid_count:].astype(jnp.bfloat16).reshape(link_count, slot_width, features)
    )
    buffer = spread_blocks(peer_onehot(offsets, -1, peer_count, jnp.bfloat16), slot_msgs)
    returned = collect_blocks(
        peer_onehot(offsets, 1, peer_count, jnp.bfloat16),
        lax.all_to_all(buffer, "tile", split_axis=0, concat_axis=0, tiled=True),
    )
    grid_sum = spot_msgs[:grid_count] + jnp.zeros((grid_count, features), jnp.float32).at[
        flat_index
    ].add(jnp.where(live_flat, returned.reshape(-1, features).astype(jnp.float32), 0.0))
    grid_out, grid_stored = node_forward(
        grid_nodes, grid_sum.astype(jnp.bfloat16), grid_first, grid_second
    )
    grid_grow, grid_gagg = node_backward(
        grid_stored, grid_cot.astype(jnp.float32), grid_first, grid_second
    )
    grad_proj = grid_gagg.astype(jnp.bfloat16)
    outgoing_grad = jnp.where(live_rows, grad_proj[send_index], zero_row)
    buffer = spread_blocks(peer_onehot(offsets, 1, peer_count, jnp.bfloat16), outgoing_grad)
    arrived_grad = collect_blocks(
        peer_onehot(offsets, -1, peer_count, jnp.bfloat16),
        lax.all_to_all(buffer, "tile", split_axis=0, concat_axis=0, tiled=True),
    )
    spot_grad = jnp.concatenate([grad_proj, arrived_grad.reshape(-1, features)], axis=0)
    dec_gpre = edge_backward(dec_stored, spot_grad[dec_grid].astype(jnp.float32), dec_second)
    spot_gpd = jax.ops.segment_sum(dec_gpre, dec_grid, num_segments=spot_count)
    mesh_gin = mesh_cot.astype(jnp.float32) + exact_back(
        pool_rows(dec_onehot, dec_gpre), dec_first[features : 2 * features]
    )
    mesh_grow, mesh_gagg = node_backward(mesh_stored, mesh_gin, mesh_first, mesh_second)
    enc_gpre = edge_backward(enc_stored, pick_rows(enc_onehot, mesh_gagg), enc_second)
    spot_gpe = jax.ops.segment_sum(enc_gpre, enc_grid, num_segments=spot_count)
    grad_mesh = mesh_grow + exact_back(
        pool_rows(enc_onehot, enc_gpre), enc_first[features : 2 * features]
    )
    spot_grads = exact_back(spot_gpe, enc_first[:features]) + exact_back(
        spot_gpd, dec_first[:features]
    )
    slot_grads = spot_grads[grid_count:].reshape(link_count, slot_width, features)
    buffer = spread_blocks(peer_onehot(offsets, -1, peer_count, jnp.float32), slot_grads)
    back_rows = collect_blocks(
        peer_onehot(offsets, 1, peer_count, jnp.float32),
        lax.all_to_all(
            buffer.astype(jnp.bfloat16), "tile", split_axis=0, concat_axis=0, tiled=True
        ).astype(buffer.dtype),
    )
    node_grads = spot_grads[:grid_count] + jnp.zeros((grid_count, features), jnp.float32).at[
        flat_index
    ].add(jnp.where(live_flat, back_rows.reshape(-1, features), 0.0))
    return (grid_out, mesh_out, grid_grow + node_grads, grad_mesh)


def solution(mesh):
    in_specs = (
        P(("groups", "tile"), None),
        P(("groups", "tile"), None),
        P(("groups", "tile"), None),
        P(("groups", "tile"), None),
        P(("groups", "tile"), None),
        P(("groups", "tile"), None),
        P(),
        P(),
        P(),
        P(),
        P(),
        P(),
        P(),
        P(),
        P(("groups", "tile"), None),
        P(("groups", "tile")),
        P(("groups", "tile")),
        P(("groups", "tile")),
        P(("groups", "tile")),
        P(("groups", "tile")),
    )
    out_specs = (
        P(("groups", "tile"), None),
        P(("groups", "tile"), None),
        P(("groups", "tile"), None),
        P(("groups", "tile"), None),
    )
    return jax.shard_map(
        per_device, mesh=mesh, in_specs=in_specs, out_specs=out_specs, check_vma=False
    )
```

profile of v0, /device:TPU:0, one launch (start us, length us, event | category | flops | bytes accessed | tf_op | source)
XLA Modules:
  0.0 141.8 jit_solution(7891286538227908271)
XLA Ops:
  3.1 2.0 %gather_fusion = bf16[144,512]{1,0:T(8,128)(2,1)S(1)} fusion(bf16[256,512]{1,0:T(8,128)(2,1)} %param.28, s32[1024]{0:T(1024)S(1)} %pad_clamp_fusion.2), kind=kCustom, calls=%fused_computation | custom fusion | bytes 295488 | tf_op jit(solution)/shard_map/gather | solution.py:163
  6.3 7.5 %all-to-all-start = ((bf16[16,16,512]{2,1,0:T(8,128)(2,1)}), bf16[16,16,512]{2,1,0:T(8,128)(2,1)S(1)}, u32[]{:S(2)}, u32[]{:S(2)}) async-start(bf16[16,16,512]{2,1,0:T(8,128)(2,1)} %copy.65), calls=%async_computation | async-start | bytes 524288 | tf_op jit(solution)/shard_map/all_to_all | solution.py:167
  13.9 1.9 %fusion.29 = f32[64,512]{1,0:T(8,128)} fusion(bf16[64,512]{1,0:T(8,128)(2,1)S(1)} %copy-done.19, bf16[1536,512]{1,0:T(8,128)(2,1)} %param.34), kind=kOutput, calls=%fused_computation.84 | convolution fusion | flops 33554432 | bytes 720896 | tf_op jit(solution)/shard_map/dot_general | solution.py:10
  16.7 7.2 %all-to-all-done = bf16[16,16,512]{2,1,0:T(8,128)(2,1)S(1)} async-done(((bf16[16,16,512]{2,1,0:T(8,128)(2,1)}), bf16[16,16,512]{2,1,0:T(8,128)(2,1)S(1)}, u32[]{:S(2)}, u32[]{:S(2)}) %all-to-all-start) | async-done | bytes 262176 | tf_op jit(solution)/shard_map/all_to_all | solution.py:167
  26.3 2.1 %gather_fusion.2 = bf16[384,512]{1,0:T(8,128)(2,1)S(1)} fusion(bf16[400,512]{1,0:T(8,128)(2,1)S(1)} %convolution_convert_fusion, s32[1024]{0:T(1024)S(1)} %pad_clamp_fusion), kind=kCustom, calls=%fused_computation.2 | custom fusion | bytes 787968 | tf_op jit(solution)/shard_map/gather | solution.py:173
  35.4 3.3 %gather_fusion.1 = bf16[768,512]{1,0:T(8,128)(2,1)} fusion(bf16[400,512]{1,0:T(8,128)(2,1)S(1)} %convolution_convert_fusion.1, s32[1024]{0:T(1024)S(1)} %pad_clamp_fusion.1), kind=kCustom, calls=%fused_computation.1 | custom fusion | bytes 1575936 | tf_op jit(solution)/shard_map/gather | solution.py:181
  38.8 1.9 %add_add_fusion = f32[768,512]{1,0:T(8,128)S(1)} fusion(f32[768,512]{1,0:T(8,128)S(1)} %fusion.55, bf16[768,512]{1,0:T(8,128)(2,1)} %gather_fusion.1, bf16[768,512]{1,0:T(8,128)(2,1)S(1)} %copy-done, bf16[1536,512]{1,0:T(8,128)(2,1)} %param.38), kind=kOutput, calls=%fused_computation.21 | convolution fusion | flops 403832832 | bytes 5242880 | tf_op jit(solution)/shard_map/dot_general | solution.py:10
  43.4 3.0 %copy.69 = f32[768,512]{1,0:T(8,128)} copy(f32[768,512]{0,1:T(8,128)} %subtract_multiply_fusion) | data formatting | bytes 3145728 | tf_op jit(solution)/shard_map/mul | solution.py:48
  46.4 7.6 %scatter_custom_fusion = f32[400,512]{1,0:T(8,128)S(1)} fusion(s32[768]{0:T(1024)S(1)} %copy-done.36, f32[768,512]{1,0:T(8,128)} %copy.69, f32[]{:T(128)} %constant.101.clone.1), kind=kCustom, calls=%fused_computation.103 | custom fusion | flops 393216 | bytes 819712 | tf_op jit(solution)/shard_map/scatter-add | solution.py:186
  55.2 4.2 %all-to-all-start.1 = ((bf16[16,16,512]{2,1,0:T(8,128)(2,1)}), bf16[16,16,512]{2,1,0:T(8,128)(2,1)}, u32[]{:S(2)}, u32[]{:S(2)}) async-start(bf16[16,16,512]{2,1,0:T(8,128)(2,1)} %copy.71), calls=%async_computation.1 | async-start | bytes 524288 | tf_op jit(solution)/shard_map/all_to_all | solution.py:193
  59.6 2.1 %fusion.40 = f32[256,512]{1,0:T(8,128)} fusion(bf16[256,512]{1,0:T(8,128)(2,1)S(1)} %copy-done.3, bf16[1024,512]{1,0:T(8,128)(2,1)} %param.40), kind=kOutput, calls=%fused_computation.95 | convolution fusion | flops 134217728 | bytes 1310720 | tf_op jit(solution)/shard_map/dot_general | solution.py:10
  61.7 7.7 %all-to-all-done.1 = bf16[16,16,512]{2,1,0:T(8,128)(2,1)} async-done(((bf16[16,16,512]{2,1,0:T(8,128)(2,1)}), bf16[16,16,512]{2,1,0:T(8,128)(2,1)}, u32[]{:S(2)}, u32[]{:S(2)}) %all-to-all-start.1) | async-done | bytes 262176 | tf_op jit(solution)/shard_map/all_to_all | solution.py:193
  71.7 2.1 %scatter_fusion = f32[256,512]{1,0:T(8,128)S(1)} fusion(f32[256,512]{1,0:T(8,128)S(1)} %slice-done, s32[144]{0:T(256)S(1)} %bitcast.62, f32[144,512]{1,0:T(8,128)} %bitcast_select_fusion.1), kind=kCustom, calls=%fused_computation.6 | custom fusion | flops 73728 | bytes 885312 | tf_op jit(solution)/shard_map/scatter-add | solution.py:197
  80.2 12.8 %all_to_all.20 = bf16[16,16,512]{2,1,0:T(8,128)(2,1)S(1)} all-to-all(bf16[16,16,512]{2,1,0:T(8,128)(2,1)S(1)} %copy.76), channel_id=1, replica_groups=mesh['groups'=2,'tile'=16] {'tile'}, dimensions={0} | all-to-all | bytes 524288 | tf_op jit(solution)/shard_map/all_to_all | solution.py:209
  93.4 3.3 %gather_fusion.4 = bf16[768,512]{1,0:T(8,128)(2,1)} fusion(bf16[400,512]{1,0:T(8,128)(2,1)S(1)} %pad_maximum_fusion.1, s32[1024]{0:T(1024)S(1)} %pad_clamp_fusion.1), kind=kCustom, calls=%fused_computation.4 | custom fusion | bytes 1575936 | tf_op jit(solution)/shard_map/gather | solution.py:212
  99.7 2.3 %multiply_multiply_fusion = f32[768,512]{1,0:T(8,128)S(1)} fusion(f32[768,512]{1,0:T(8,128)} %copy-done.13, bf16[512,512]{1,0:T(8,128)(2,1)S(1)} %copy-done.42, bf16[768,512]{0,1:T(8,128)(2,1)S(1)} %copy.80, f32[768,512]{0,1:T(8,128)S(1)} %copy-done.6, f32[768]{0:T(1024)S(1)} %broadcast_multiply_fusion, f32[768]{0:T(1024)S(1)} %broadcast_multiply_fusion.1, ...), kind=kOutput, calls=%fused_computation.17 | convolution fusion | flops 408158208 | bytes 6038528 | tf_op jit(solution)/shard_map/dot_general | solution.py:14
  103.2 1.8 %fusion.118 = (f32[64]{0:T(128)S(1)}, f32[64]{0:T(128)S(1)}, f32[64,512]{1,0:T(8,128)S(1)}) fusion(f32[64]{0:T(128)S(1)} %copy-done.38, f32[64,512]{1,0:T(8,128)S(1)} %copy-done.15, f32[64]{0:T(128)S(1)} %broadcast_multiply_fusion.11, f32[64,512]{1,0:T(8,128)S(1)} %fusion.54, bf16[1536,512]{1,0:T(8,128)(2,1)} %param.38, bf16[64,512]{1,0:T(8,128)(2,1)S(1)} %copy-done.30), kind=kOutput, calls=%fused_computation.212 | convolution fusion | flops 201555840 | bytes 984064 | tf_op jit(solution)/shard_map/dot_general | solution.py:20
  109.2 3.2 %scatter_custom_fusion.2 = f32[400,512]{1,0:T(8,128)S(1)} fusion(s32[384]{0:T(512)} %param.44, f32[384,512]{1,0:T(8,128)S(1)} %convolution_multiply_fusion, f32[]{:T(128)} %constant.101.clone.1), kind=kCustom, calls=%fused_computation.101 | custom fusion | flops 196608 | bytes 819712 | tf_op jit(solution)/shard_map/scatter-add | solution.py:219
  112.3 7.7 %scatter_custom_fusion.3 = f32[400,512]{1,0:T(8,128)S(1)} fusion(s32[768]{0:T(1024)} %param.46, f32[768,512]{1,0:T(8,128)} %copy-done.12, f32[]{:T(128)} %constant.101.clone.1), kind=kCustom, calls=%fused_computation.99 | custom fusion | flops 393216 | bytes 819712 | tf_op jit(solution)/shard_map/scatter-add | solution.py:213
  120.0 1.9 %fusion.31 = f32[400,512]{1,0:T(8,128)S(1)} fusion(f32[400,512]{1,0:T(8,128)S(1)} %scatter_custom_fusion.2, bf16[1536,512]{1,0:T(8,128)(2,1)} %param.34), kind=kOutput, calls=%fused_computation.86 | convolution fusion | flops 1258291200 | bytes 2162688 | tf_op jit(solution)/shard_map/dot_general | solution.py:20
  121.9 1.9 %convolution_add_fusion = f32[400,512]{1,0:T(8,128)S(1)} fusion(f32[400,512]{1,0:T(8,128)S(1)} %fusion.31, f32[400,512]{1,0:T(8,128)S(1)} %scatter_custom_fusion.3, bf16[1536,512]{1,0:T(8,128)(2,1)} %param.38), kind=kOutput, calls=%fused_computation.23 | convolution fusion | flops 1258496000 | bytes 2981888 | tf_op jit(solution)/shard_map/dot_general | solution.py:20
  125.2 3.5 %all-to-all-start.3 = ((bf16[16,16,512]{2,1,0:T(8,128)(2,1)}), bf16[16,16,512]{2,1,0:T(8,128)(2,1)S(1)}, u32[]{:S(2)}, u32[]{:S(2)}) async-start(bf16[16,16,512]{2,1,0:T(8,128)(2,1)} %copy.82), calls=%async_computation.3 | async-start | bytes 524288 | tf_op jit(solution)/shard_map/all_to_all | solution.py:230
  128.8 2.3 %convolution_add_fusion.5 = f32[64,512]{1,0:T(8,128)} fusion(f32[64,512]{1,0:T(8,128)} %convolution_add_fusion.6, f32[64,512]{1,0:T(8,128)S(1)} %copy-done.20, bf16[1536,512]{1,0:T(8,128)(2,1)} %param.34), kind=kOutput, calls=%fused_computation.43 | convolution fusion | flops 201359360 | bytes 917504 | tf_op jit(solution)/shard_map/dot_general | solution.py:20
  132.5 6.3 %all-to-all-done.3 = bf16[16,16,512]{2,1,0:T(8,128)(2,1)S(1)} async-done(((bf16[16,16,512]{2,1,0:T(8,128)(2,1)}), bf16[16,16,512]{2,1,0:T(8,128)(2,1)S(1)}, u32[]{:S(2)}, u32[]{:S(2)}) %all-to-all-start.3) | async-done | bytes 262176 | tf_op jit(solution)/shard_map/all_to_all | solution.py:230
  (183 shorter events, 40.4 us)
Async XLA Ops:
  0.6 38.1 %copy-start = (bf16[768,512]{1,0:T(8,128)(2,1)S(1)}, bf16[768,512]{1,0:T(8,128)(2,1)}, u32[]{:S(2)}) copy-start(bf16[768,512]{1,0:T(8,128)(2,1)} %param.31) | copy-start | bytes 2359300
  0.6 13.1 %copy-start.47 = (s32[9]{0:T(128)S(1)}, s32[9]{0:T(128)}, u32[]{:S(2)}) copy-start(s32[9]{0:T(128)} %constant.116) | copy-start | bytes 112
  0.7 13.1 %copy-start.39 = (s32[384]{0:T(512)S(1)}, s32[384]{0:T(512)}, u32[]{:S(2)}) copy-start(s32[384]{0:T(512)} %param.44) | copy-start | bytes 4612
  0.7 13.2 %copy-start.36 = (s32[768]{0:T(1024)S(1)}, s32[768]{0:T(1024)}, u32[]{:S(2)}) copy-start(s32[768]{0:T(1024)} %param.46) | copy-start | bytes 9220
  0.7 13.2 %copy-start.19 = (bf16[64,512]{1,0:T(8,128)(2,1)S(1)}, bf16[64,512]{1,0:T(8,128)(2,1)}, u32[]{:S(2)}) copy-start(bf16[64,512]{1,0:T(8,128)(2,1)} %param.29) | copy-start | bytes 196612
  3.1 12.7 %copy-start.7 = (bf16[1024,512]{1,0:T(8,128)(2,1)S(1)}, bf16[1024,512]{1,0:T(8,128)(2,1)}, u32[]{:S(2)}) copy-start(bf16[1024,512]{1,0:T(8,128)(2,1)} %param.36) | copy-start | bytes 3145732
  6.3 18.6 %copy-start.3 = (bf16[256,512]{1,0:T(8,128)(2,1)S(1)}, bf16[256,512]{1,0:T(8,128)(2,1)}, u32[]{:S(2)}) copy-start(bf16[256,512]{1,0:T(8,128)(2,1)} %param.28) | copy-start | bytes 786436
  6.3 17.6 %all-to-all-start = ((bf16[16,16,512]{2,1,0:T(8,128)(2,1)}), bf16[16,16,512]{2,1,0:T(8,128)(2,1)S(1)}, u32[]{:S(2)}, u32[]{:S(2)}) async-start(bf16[16,16,512]{2,1,0:T(8,128)(2,1)} %copy.65), calls=%async_computation | async-start | bytes 524288 | tf_op jit(solution)/shard_map/all_to_all | solution.py:167
  26.3 2.1 %copy-start.21 = (f32[64,512]{1,0:T(8,128)S(1)}, f32[64,512]{1,0:T(8,128)}, u32[]{:S(2)}) copy-start(f32[64,512]{1,0:T(8,128)} %fusion.29) | copy-start | bytes 393220
  26.3 2.1 %copy-start.31 = (s32[384]{0:T(512)S(1)}, s32[384]{0:T(512)}, u32[]{:S(2)}) copy-start(s32[384]{0:T(512)} %param.45) | copy-start | bytes 4612
  46.4 13.0 %copy-start.32 = (s32[9,16]{1,0:T(8,128)S(1)}, s32[9,16]{1,0:T(8,128)}, u32[]{:S(2)}) copy-start(s32[9,16]{1,0:T(8,128)} %param.42) | copy-start | bytes 1732
  54.0 7.6 %copy-start.1 = (f32[400,512]{1,0:T(8,128)}, f32[400,512]{1,0:T(8,128)S(1)}, u32[]{:S(2)}) copy-start(f32[400,512]{1,0:T(8,128)S(1)} %scatter_custom_fusion) | copy-start | bytes 2457604
  55.2 14.2 %all-to-all-start.1 = ((bf16[16,16,512]{2,1,0:T(8,128)(2,1)}), bf16[16,16,512]{2,1,0:T(8,128)(2,1)}, u32[]{:S(2)}, u32[]{:S(2)}) async-start(bf16[16,16,512]{2,1,0:T(8,128)(2,1)} %copy.71), calls=%async_computation.1 | async-start | bytes 524288 | tf_op jit(solution)/shard_map/all_to_all | solution.py:193
  59.5 11.4 %copy-start.34 = (pred[144]{0:T(512)(128)(4,1)}, pred[144]{0:T(512)(128)(4,1)S(1)}, u32[]{:S(2)}) copy-start(pred[144]{0:T(512)(128)(4,1)S(1)} %lt.87) | copy-start | bytes 436
  61.7 10.0 %slice-start = ((f32[400,512]{1,0:T(8,128)}), f32[256,512]{1,0:T(8,128)S(1)}, s32[]{:S(2)}) async-start(f32[400,512]{1,0:T(8,128)} %copy-done.1), calls=%async_computation.4 | async-start | bytes 1048576 | tf_op jit(solution)/shard_map/slice | solution.py:195
  102.0 3.3 %copy-start.12 = (f32[768,512]{1,0:T(8,128)}, f32[768,512]{1,0:T(8,128)S(1)}, u32[]{:S(2)}) copy-start(f32[768,512]{1,0:T(8,128)S(1)} %multiply_multiply_fusion) | copy-start | bytes 4718596
  102.1 3.0 %copy-start.29 = (f32[64,512]{1,0:T(8,128)S(1)}, f32[64,512]{1,0:T(8,128)}, u32[]{:S(2)}) copy-start(f32[64,512]{1,0:T(8,128)} %copy-done.28) | copy-start | bytes 393220
  102.1 3.0 %copy-start.44 = (bf16[512,512]{1,0:T(8,128)(2,1)S(1)}, bf16[512,512]{1,0:T(8,128)(2,1)}, u32[]{:S(2)}) copy-start(bf16[512,512]{1,0:T(8,128)(2,1)} %param.37) | copy-start | bytes 1572868
  103.2 2.2 %copy-start.8 = (bf16[1024,512]{1,0:T(8,128)(2,1)S(1)}, bf16[1024,512]{1,0:T(8,128)(2,1)}, u32[]{:S(2)}) copy-start(bf16[1024,512]{1,0:T(8,128)(2,1)} %param.36) | copy-start | bytes 3145732
  105.4 2.0 %copy-start.18 = (f32[384,512]{1,0:T(8,128)S(1)}, f32[384,512]{1,0:T(8,128)}, u32[]{:S(2)}) copy-start(f32[384,512]{1,0:T(8,128)} %copy-done.17) | copy-start | bytes 2359300
  123.8 5.0 %copy-start.20 = (f32[64,512]{1,0:T(8,128)S(1)}, f32[64,512]{1,0:T(8,128)}, u32[]{:S(2)}) copy-start(f32[64,512]{1,0:T(8,128)} %fusion.73) | copy-start | bytes 393220
  123.8 7.3 %copy-start.11 = (bf16[1024,512]{1,0:T(8,128)(2,1)S(1)}, bf16[1024,512]{1,0:T(8,128)(2,1)}, u32[]{:S(2)}) copy-start(bf16[1024,512]{1,0:T(8,128)(2,1)} %param.40) | copy-start | bytes 3145732
  125.2 13.5 %all-to-all-start.3 = ((bf16[16,16,512]{2,1,0:T(8,128)(2,1)}), bf16[16,16,512]{2,1,0:T(8,128)(2,1)S(1)}, u32[]{:S(2)}, u32[]{:S(2)}) async-start(bf16[16,16,512]{2,1,0:T(8,128)(2,1)} %copy.82), calls=%async_computation.3 | async-start | bytes 524288 | tf_op jit(solution)/shard_map/all_to_all | solution.py:230
  131.1 8.1 %copy-start.35 = (pred[144]{0:T(512)(128)(4,1)S(1)}, pred[144]{0:T(512)(128)(4,1)}, u32[]{:S(2)}) copy-start(pred[144]{0:T(512)(128)(4,1)} %copy-done.34) | copy-start | bytes 436
  (28 other events, 35.7 us)
where the time goes:
time: 143 us; the launch traced here: 142 us
  matrix products  36.6 us (26%)
  other arithmetic  28.9 us (20%)
  local copies, waits for them, and re-layouts  25.4 us (18%)
  waiting for transfers between devices  21.2 us (15%)
  starting transfers between devices  15.2 us (11%)
  blocking collectives  12.8 us (9%)
  between operations  1.63 us (1%)
    all_to_all x2, waiting for transfers between devices, per_device(): lax.all_to_all(buffer, 'tile', split_axis=0, concat_axis=0, tiled=True)  14.9 us
    dot_general x14, matrix products, mixed_dot(): return jnp.dot(left, right, preferred_element_type=jnp.float32)  13.9 us
    all_to_all x1, blocking collectives, per_device(): lax.all_to_all(buffer, 'tile', split_axis=0, concat_axis=0, tiled=True)  12.8 us
    all_to_all x2, starting transfers between devices, per_device(): lax.all_to_all(buffer, 'tile', split_axis=0, concat_axis=0, tiled=True)  11.7 us
    dot_general x4, matrix products, exact_back(): lax.dot_general(left, right.astype(jnp.float32), (((1,), (1,)), ((), ()))...  7.94 us
    scatter-add x1, other arithmetic, per_device(): spot_gpd = jax.ops.segment_sum(dec_gpre, dec_grid, num_segments=spot_count)  7.68 us
    scatter-add x1, other arithmetic, per_device(): spot_msgs = jax.ops.segment_sum(dec_msg, dec_grid, num_segments=spot_count)  7.63 us
    dot_general x8, matrix products, back_dot(): lax.dot_general(left, right, (((1,), (1,)), ((), ())), preferred_element_...  6.64 us
  transfers between devices with their start and end apart: 3, of which 3 were waited for; matrix products, arithmetic and copies ran while one was open for 6% of the time, Pallas kernels for 0%

commit v1 on v0

v1 whole, which is shorter than its diff:
```python
import jax
import jax.numpy as jnp
from jax import lax
from jax.experimental import pallas as pl
from jax.experimental.pallas import tpu as pltpu
from jax.sharding import PartitionSpec as P

TW = 4
CHUNK = 32
F32 = jnp.float32
BF16 = jnp.bfloat16
VMEM_LIMIT = 30 * 1024 * 1024


def mm(left, right):
    return jnp.dot(left, right, preferred_element_type=F32)


def mm_t(left, right):
    return lax.dot_general(left, right, (((1,), (1,)), ((), ())), preferred_element_type=F32)


def sigmoid(values):
    return 0.5 * jnp.tanh(0.5 * values) + 0.5


def norm_rows(values):
    centre = values - jnp.mean(values, axis=-1, keepdims=True)
    scale_inv = lax.rsqrt(jnp.mean(centre * centre, axis=-1, keepdims=True) + 1e-05)
    return centre * scale_inv, scale_inv


def norm_back(normed, scale_inv, upstream):
    return scale_inv * (
        upstream
        - jnp.mean(upstream, axis=-1, keepdims=True)
        - normed * jnp.mean(upstream * normed, axis=-1, keepdims=True)
    )


def row_chunks(rows, size=CHUNK):
    return [slice(start, min(start + size, rows)) for start in range(0, rows, size)]


def activate(pre, act_ref, slope_ref):
    for rows in row_chunks(pre.shape[0]):
        part = pre[rows, :]
        gate = sigmoid(part)
        act = part * gate
        act_ref[rows, :] = act.astype(BF16)
        slope_ref[rows, :] = (gate + act * (1.0 - gate)).astype(BF16)


def norm_forward(raw, normed_ref, scale_ref):
    for rows in row_chunks(raw.shape[0]):
        normed, scale_inv = norm_rows(raw[rows, :])
        normed_ref[rows, :] = normed.astype(normed_ref.dtype)
        scale_ref[rows, :] = scale_inv


def norm_backward(normed_ref, scale_ref, upstream, out_ref):
    for rows in row_chunks(out_ref.shape[0]):
        out_ref[rows, :] = norm_back(
            normed_ref[rows, :].astype(F32), scale_ref[rows, :], upstream[rows, :].astype(F32)
        ).astype(BF16)


def times_slope(raw, slope_ref, out_ref):
    for rows in row_chunks(out_ref.shape[0]):
        out_ref[rows, :] = (raw[rows, :] * slope_ref[rows, :].astype(F32)).astype(BF16)


def stack(refs, columns):
    return jnp.concatenate([ref[:, columns] for ref in refs], axis=0)


def neighbour_offsets(peer_count):
    forward_half = [1, TW, TW + 1, TW - 1]
    return forward_half + [-offset for offset in forward_half] + [peer_count // 2]


def onehot_pair(spot_ref, mesh_ref, spots, by_edge_ref, by_spot_ref):
    edges, total = by_edge_ref.shape
    spot_row = spot_ref[...].astype(F32)
    mesh_row = mesh_ref[...].astype(F32) + float(spots)
    for rows in row_chunks(total, 64):
        ids = lax.broadcasted_iota(jnp.int32, (rows.stop - rows.start, edges), 0) + rows.start
        ids = ids.astype(F32)
        hit = (ids == spot_row) | (ids == mesh_row)
        by_spot_ref[rows, :] = jnp.where(hit, 1.0, 0.0).astype(BF16)
    for rows in row_chunks(edges, 128):
        spot_col = jnp.broadcast_to(spot_row[:, rows], (128, 128)).T
        mesh_col = jnp.broadcast_to(mesh_row[:, rows], (128, 128)).T
        for columns in row_chunks(total, 128):
            ids = lax.broadcasted_iota(jnp.int32, (128, 128), 1) + columns.start
            ids = ids.astype(F32)
            hit = (ids == spot_col) | (ids == mesh_col)
            by_edge_ref[rows, columns] = jnp.where(hit, 1.0, 0.0).astype(BF16)


class Fetched:
    def __init__(self, source, target, semaphore):
        self.copy = pltpu.make_async_copy(source, target, semaphore)
        self.target = target
        self.landed = False
        self.copy.start()

    def land(self):
        if not self.landed:
            self.copy.wait()
            self.landed = True

    def __getitem__(self, key):
        self.land()
        return self.target[key]


def call(body, name, inputs, outputs, scratch=(), flops=0):
    arrays, specs, moved, fetches = [], [], 0, []
    for place, entry in enumerate(inputs):
        if isinstance(entry, tuple):
            array, first, rows = entry
            specs.append(pl.BlockSpec(memory_space=pl.ANY))
            fetches.append((place, first, rows, (rows, array.shape[1]), array.dtype))
            moved += rows * array.shape[1] * array.dtype.itemsize
        else:
            array = entry
            smem = array.dtype == jnp.int32 and array.ndim == 1
            specs.append(pl.BlockSpec(memory_space=pltpu.SMEM if smem else pltpu.VMEM))
            moved += array.size * array.dtype.itemsize
        arrays.append(array)
    shapes = [jax.ShapeDtypeStruct(shape, dtype) for shape, dtype in outputs]
    for shape in shapes:
        moved += shape.size * shape.dtype.itemsize
    buffers = [pltpu.VMEM(shape, dtype) for _, _, _, shape, dtype in fetches]
    if fetches:
        buffers.append(pltpu.SemaphoreType.DMA((len(fetches),)))

    def kernel(*refs):
        refs = list(refs)
        if not fetches:
            body(*refs)
            return
        refs, targets, semaphores = (
            refs[: -len(buffers)],
            refs[-len(buffers) : -1],
            refs[-1],
        )
        waiting = []
        for slot, (place, first, rows, _, _) in enumerate(fetches):
            refs[place] = Fetched(
                refs[place].at[pl.ds(first, rows), :], targets[slot], semaphores.at[slot]
            )
            waiting.append(refs[place])
        body(*refs)
        for fetched in waiting:
            fetched.land()

    return pl.pallas_call(
        kernel,
        name=name,
        in_specs=specs,
        out_specs=[pl.BlockSpec(memory_space=pltpu.VMEM) for _ in shapes],
        out_shape=shapes,
        scratch_shapes=[pltpu.VMEM(shape, dtype) for shape, dtype in scratch] + buffers,
        compiler_params=pltpu.CompilerParams(vmem_limit_bytes=VMEM_LIMIT),
        cost_estimate=pl.CostEstimate(flops=flops, bytes_accessed=moved, transcendentals=0),
    )(*arrays)


def per_device(
    grid_nodes,
    mesh_nodes,
    enc_edges,
    dec_edges,
    grid_cot,
    mesh_cot,
    enc_first,
    enc_second,
    mesh_first,
    mesh_second,
    dec_first,
    dec_second,
    grid_first,
    grid_second,
    send_index,
    send_count,
    enc_grid,
    enc_mesh,
    dec_grid,
    dec_mesh,
):
    grid_count, feat = grid_nodes.shape
    mesh_count = mesh_nodes.shape[0]
    enc_count = enc_edges.shape[0]
    dec_count = dec_edges.shape[0]
    links, width = send_index.shape
    slots = links * width
    slots_pad = -(-slots // 128) * 128
    spots = grid_count + slots
    total = -(-(spots + mesh_count) // 128) * 128
    peer_count = lax.axis_size("tile")
    offsets = neighbour_offsets(peer_count)
    half = (links - 1) // 2
    reverse = [(j + half) % (links - 1) for j in range(links - 1)] + [links - 1]
    low, high = slice(0, feat), slice(feat, 2 * feat)
    mesh_rows = slice(spots, spots + mesh_count)

    def exchange(parts):
        return [
            lax.ppermute(part, "tile", [(s, (s + offset) % peer_count) for s in range(peer_count)])
            for part, offset in zip(parts, offsets)
        ]

    def pack(index_ref, count_ref, nodes_ref, cot_ref, select_ref, *out_refs):
        shape = (width, grid_count)
        eye = lax.broadcasted_iota(jnp.int32, (width, width), 0) == lax.broadcasted_iota(
            jnp.int32, (width, width), 1
        )
        lane = lax.broadcasted_iota(jnp.int32, shape, 1).astype(F32)
        place = lax.broadcasted_iota(jnp.int32, shape, 0)
        index = index_ref[...].astype(F32)
        picks = []
        for j in range(links):
            row = jnp.broadcast_to(index[j : j + 1, :], (width, width))
            column = jnp.sum(jnp.where(eye, row, 0.0), axis=1, keepdims=True)
            hit = (lane == column) & (place < count_ref[j])
            picks.append(jnp.where(hit, 1.0, 0.0).astype(BF16))
        select = jnp.concatenate(picks, axis=0)
        select_ref[:slots, :] = select
        select_ref[slots:, :] = jnp.zeros((slots_pad - slots, grid_count), BF16)
        sent_nodes = mm(select, nodes_ref[...]).astype(BF16)
        sent_cot = mm(select, cot_ref[...]).astype(BF16)
        for j, out_ref in enumerate(out_refs):
            rows = slice(j * width, (j + 1) * width)
            out_ref[:, low] = sent_nodes[rows, :]
            out_ref[:, high] = sent_cot[rows, :]

    select, *outgoing = call(
        pack,
        "pack_rows",
        [send_index, send_count, grid_nodes, grid_cot],
        [((slots_pad, grid_count), BF16)] + [((width, 2 * feat), BF16)] * links,
        flops=4 * slots * grid_count * feat,
    )
    arrived = exchange(outgoing)

    def local(
        select_ref,
        nodes_ref,
        mesh_ref,
        enc_edges_ref,
        dec_edges_ref,
        enc_wg_ref,
        enc_wm_ref,
        enc_we_ref,
        dec_wg_ref,
        dec_we_ref,
        mesh_wn_ref,
        enc_grid_ref,
        enc_mesh_ref,
        dec_grid_ref,
        dec_mesh_ref,
        select_t_ref,
        enc_part_ref,
        dec_part_ref,
        mesh_part_ref,
        enc_pick_ref,
        enc_pool_ref,
        dec_pick_ref,
        dec_pool_ref,
        table_ref,
    ):
        onehot_pair(enc_grid_ref, enc_mesh_ref, spots, enc_pick_ref, enc_pool_ref)
        onehot_pair(dec_grid_ref, dec_mesh_ref, spots, dec_pick_ref, dec_pool_ref)
        select_t_ref[...] = select_ref[...].astype(F32).T.astype(BF16)
        nodes = nodes_ref[...]
        mesh_part_ref[...] = mm(mesh_ref[...], mesh_wn_ref[...])
        table_ref[:grid_count, :] = mm(nodes, enc_wg_ref[...]).astype(BF16)
        table_ref[grid_count:, :] = jnp.zeros((total - grid_count, feat), BF16)
        table_ref[mesh_rows, :] = mm(mesh_ref[...], enc_wm_ref[...]).astype(BF16)
        enc_part_ref[...] = mm(enc_edges_ref[...], enc_we_ref[...])
        enc_part_ref[...] += mm(enc_pick_ref[...], table_ref[...])
        pd = mm(nodes, dec_wg_ref[...]).astype(BF16)
        dec_part_ref[...] = mm(dec_edges_ref[...], dec_we_ref[...])
        dec_part_ref[...] += mm(dec_pick_ref[:, :grid_count], pd)

    select_t, enc_part, dec_part, mesh_part, enc_pick, enc_pool, dec_pick, dec_pool = call(
        local,
        "local_products",
        [
            select,
            grid_nodes,
            mesh_nodes,
            enc_edges,
            dec_edges,
            (enc_first, 0, feat),
            (enc_first, feat, feat),
            (enc_first, 2 * feat, feat),
            (dec_first, 0, feat),
            (dec_first, 2 * feat, feat),
            (mesh_first, 0, feat),
            enc_grid.reshape(1, -1),
            enc_mesh.reshape(1, -1),
            dec_grid.reshape(1, -1),
            dec_mesh.reshape(1, -1),
        ],
        [
            ((grid_count, slots_pad), BF16),
            ((enc_count, feat), F32),
            ((dec_count, feat), F32),
            ((mesh_count, feat), F32),
            ((enc_count, total), BF16),
            ((total, enc_count), BF16),
            ((dec_count, total), BF16),
            ((total, dec_count), BF16),
        ],
        scratch=[((total, feat), BF16)],
        flops=2 * feat * (feat * (2 * grid_count + enc_count + dec_count) + total * dec_count),
    )

    def forward(*refs):
        arrived_refs, refs = refs[:links], refs[links:]
        (
            select_ref,
            enc_part_ref,
            dec_part_ref,
            mesh_part_ref,
            enc_pick_ref,
            enc_pool_ref,
            dec_pick_ref,
            dec_pool_ref,
            mesh_ref,
            enc_wg_ref,
            dec_wg_ref,
            enc_w2_ref,
            mesh_wa_ref,
            mesh_w2_ref,
            dec_wm_ref,
            dec_w2_ref,
        ) = refs[:16]
        refs = refs[16:]
        out_refs, refs = refs[:links], refs[links:]
        (
            mesh_out_ref,
            spot_ref,
            enc_normed_ref,
            enc_scale_ref,
            enc_slope_ref,
            dec_normed_ref,
            dec_scale_ref,
            dec_slope_ref,
            mesh_normed_ref,
            mesh_scale_ref,
            mesh_slope_ref,
            enc_act_ref,
            dec_act_ref,
            mesh_act_ref,
            table_ref,
        ) = refs
        rows = stack(arrived_refs, low)
        pe = mm(rows, enc_wg_ref[...]).astype(BF16)
        pre = enc_part_ref[...] + mm(enc_pick_ref[:, grid_count:spots], pe)
        activate(pre, enc_act_ref, enc_slope_ref)
        norm_forward(mm(enc_act_ref[...], enc_w2_ref[...]), enc_normed_ref, enc_scale_ref)
        agg = mm(enc_pool_ref[mesh_rows, :], enc_normed_ref[...]).astype(BF16)
        activate(mesh_part_ref[...] + mm(agg, mesh_wa_ref[...]), mesh_act_ref, mesh_slope_ref)
        norm_forward(mm(mesh_act_ref[...], mesh_w2_ref[...]), mesh_normed_ref, mesh_scale_ref)
        mesh_out = (mesh_ref[...].astype(F32) + mesh_normed_ref[...]).astype(BF16)
        mesh_out_ref[...] = mesh_out
        table_ref[:slots, :] = mm(rows, dec_wg_ref[...]).astype(BF16)
        table_ref[slots : slots + mesh_count, :] = mm(mesh_out, dec_wm_ref[...]).astype(BF16)
        table_ref[slots + mesh_count :, :] = jnp.zeros(
            (total - spots - mesh_count, feat), BF16
        )
        pre = dec_part_ref[...] + mm(dec_pick_ref[:, grid_count:], table_ref[...])
        activate(pre, dec_act_ref, dec_slope_ref)
        norm_forward(mm(dec_act_ref[...], dec_w2_ref[...]), dec_normed_ref, dec_scale_ref)
        spot_ref[...] = mm(dec_pool_ref[:spots, :], dec_normed_ref[...])
        shared = mm(select_ref[:slots, :], spot_ref[:grid_count, :].astype(BF16)).astype(BF16)
        for j, out_ref in enumerate(out_refs):
            start = grid_count + reverse[j] * width
            out_ref[:, low] = spot_ref[start : start + width, :].astype(BF16)
            out_ref[:, high] = shared[j * width : (j + 1) * width, :]

    edge_saved = [
        ((enc_count, feat), BF16),
        ((enc_count, 1), F32),
        ((enc_count, feat), BF16),
        ((dec_count, feat), BF16),
        ((dec_count, 1), F32),
        ((dec_count, feat), BF16),
        ((mesh_count, feat), F32),
        ((mesh_count, 1), F32),
        ((mesh_count, feat), BF16),
    ]
    results = call(
        forward,
        "edges_forward",
        [
            *arrived,
            select,
            enc_part,
            dec_part,
            mesh_part,
            enc_pick,
            enc_pool,
            dec_pick,
            dec_pool,
            mesh_nodes,
            (enc_first, 0, feat),
            (dec_first, 0, feat),
            (enc_second, 0, feat),
            (mesh_first, feat, feat),
            (mesh_second, 0, feat),
            (dec_first, feat, feat),
            (dec_second, 0, feat),
        ],
        [((width, 2 * feat), BF16)] * links
        + [((mesh_count, feat), BF16), ((spots, feat), F32)]
        + edge_saved,
        scratch=[
            ((enc_count, feat), BF16),
            ((dec_count, feat), BF16),
            ((mesh_count, feat), BF16),
            ((total - grid_count, feat), BF16),
        ],
        flops=2 * feat * feat * 2 * (enc_count + dec_count),
    )
    outgoing, results = results[:links], results[links:]
    mesh_out, spot_msg, *saved = results
    returned = exchange(outgoing)

    def node_part(*refs):
        arrived_refs, (nodes_ref, weight_ref, out_ref) = refs[:links], refs[links:]
        out_ref[:grid_count, :] = mm(nodes_ref[...], weight_ref[...])
        out_ref[grid_count:, :] = mm(stack(arrived_refs, low), weight_ref[...])

    (grid_part,) = call(
        node_part,
        "node_products",
        [*arrived, grid_nodes, (grid_first, 0, feat)],
        [((spots, feat), F32)],
        flops=2 * spots * feat * feat,
    )

    def backward(*refs):
        arrived_refs, returned_refs, refs = refs[:links], refs[links : 2 * links], refs[2 * links :]
        (
            spot_ref,
            grid_part_ref,
            select_t_ref,
            nodes_ref,
            cot_ref,
            mesh_cot_ref,
            enc_pick_ref,
            enc_pool_ref,
            dec_pick_ref,
            dec_pool_ref,
            grid_wa_ref,
            grid_w2_ref,
            dec_w2_ref,
            dec_wm_ref,
            mesh_wa_ref,
            mesh_w2_ref,
            enc_w2_ref,
            enc_wg_ref,
            dec_wg_ref,
            enc_normed_ref,
            enc_scale_ref,
            enc_slope_ref,
            dec_normed_ref,
            dec_scale_ref,
            dec_slope_ref,
            mesh_normed_ref,
            mesh_scale_ref,
            mesh_slope_ref,
        ) = refs[:28]
        refs = refs[28:]
        out_refs, refs = refs[:links], refs[links:]
        (
            grid_out_ref,
            grid_gpre_ref,
            gpe_ref,
            gpd_ref,
            mesh_gin_ref,
            mesh_gpre_ref,
            mesh_pool_ref,
            agg_ref,
            grid_act_ref,
            grid_slope_ref,
            grid_normed_ref,
            grid_scale_ref,
            grid_gout_ref,
            grid_gall_ref,
            spot_grad_ref,
            dec_gout_ref,
            mesh_gout_ref,
            enc_gout_ref,
        ) = refs
        back = [returned_refs[reverse[j]] for j in range(links)]
        agg_ref[:grid_count, :] = (
            spot_ref[:grid_count, :] + mm(select_t_ref[:, :slots], stack(back, low))
        ).astype(BF16)
        agg_ref[grid_count:, :] = (
            spot_ref[grid_count:, :] + stack(returned_refs, high).astype(F32)
        ).astype(BF16)
        activate(
            grid_part_ref[...] + mm(agg_ref[...], grid_wa_ref[...]), grid_act_ref, grid_slope_ref
        )
        norm_forward(mm(grid_act_ref[...], grid_w2_ref[...]), grid_normed_ref, grid_scale_ref)
        grid_out_ref[...] = (
            nodes_ref[...].astype(F32) + grid_normed_ref[:grid_count, :]
        ).astype(BF16)
        cot = jnp.concatenate([cot_ref[...], stack(arrived_refs, high)], axis=0)
        norm_backward(grid_normed_ref, grid_scale_ref, cot, grid_gout_ref)
        times_slope(mm_t(grid_gout_ref[...], grid_w2_ref[...]), grid_slope_ref, grid_gall_ref)
        grid_gpre_ref[...] = grid_gall_ref[:grid_count, :]
        spot_grad_ref[:spots, :] = mm_t(grid_gall_ref[...], grid_wa_ref[...]).astype(BF16)
        spot_grad_ref[spots:, :] = jnp.zeros((total - spots, feat), BF16)
        norm_backward(
            dec_normed_ref, dec_scale_ref, mm(dec_pick_ref[...], spot_grad_ref[...]), dec_gout_ref
        )
        times_slope(mm_t(dec_gout_ref[...], dec_w2_ref[...]), dec_slope_ref, dec_gout_ref)
        pooled = mm(dec_pool_ref[...], dec_gout_ref[...]).astype(BF16)
        gpd_ref[...] = pooled[:grid_count, :]
        slot_back = mm_t(pooled[grid_count:spots, :], dec_wg_ref[...])
        mesh_gin = mesh_cot_ref[...].astype(F32) + mm_t(pooled[mesh_rows, :], dec_wm_ref[...])
        mesh_gin_ref[...] = mesh_gin
        norm_backward(mesh_normed_ref, mesh_scale_ref, mesh_gin, mesh_gout_ref)
        times_slope(mm_t(mesh_gout_ref[...], mesh_w2_ref[...]), mesh_slope_ref, mesh_gpre_ref)
        gagg = mm_t(mesh_gpre_ref[...], mesh_wa_ref[...]).astype(BF16)
        norm_backward(
            enc_normed_ref, enc_scale_ref, mm(enc_pick_ref[:, mesh_rows], gagg), enc_gout_ref
        )
        times_slope(mm_t(enc_gout_ref[...], enc_w2_ref[...]), enc_slope_ref, enc_gout_ref)
        pooled = mm(enc_pool_ref[...], enc_gout_ref[...]).astype(BF16)
        gpe_ref[...] = pooled[:grid_count, :]
        mesh_pool_ref[...] = pooled[mesh_rows, :]
        slot_back = (slot_back + mm_t(pooled[grid_count:spots, :], enc_wg_ref[...])).astype(BF16)
        for j, out_ref in enumerate(out_refs):
            start = reverse[j] * width
            out_ref[...] = slot_back[start : start + width, :]

    results = call(
        backward,
        "edges_backward",
        [
            *arrived,
            *returned,
            spot_msg,
            grid_part,
            select_t,
            grid_nodes,
            grid_cot,
            mesh_cot,
            enc_pick,
            enc_pool,
            dec_pick,
            dec_pool,
            (grid_first, feat, feat),
            (grid_second, 0, feat),
            (dec_second, 0, feat),
            (dec_first, feat, feat),
            (mesh_first, feat, feat),
            (mesh_second, 0, feat),
            (enc_second, 0, feat),
            (enc_first, 0, feat),
            (dec_first, 0, feat),
            *saved,
        ],
        [((width, feat), BF16)] * links
        + [((grid_count, feat), BF16)] * 4
        + [((mesh_count, feat), F32), ((mesh_count, feat), BF16), ((mesh_count, feat), BF16)],
        scratch=[
            ((spots, feat), BF16),
            ((spots, feat), BF16),
            ((spots, feat), BF16),
            ((spots, feat), F32),
            ((spots, 1), F32),
            ((spots, feat), BF16),
            ((spots, feat), BF16),
            ((total, feat), BF16),
            ((dec_count, feat), BF16),
            ((mesh_count, feat), BF16),
            ((enc_count, feat), BF16),
        ],
        flops=2 * feat * feat * (4 * spots + 3 * dec_count + 2 * enc_count),
    )
    outgoing, results = results[:links], results[links:]
    grid_out, grid_gpre, gpe, gpd, mesh_gin, mesh_gpre, mesh_pool = results
    final = exchange(outgoing)

    def tail(
        cot_ref,
        grid_gpre_ref,
        gpe_ref,
        gpd_ref,
        mesh_gin_ref,
        mesh_gpre_ref,
        mesh_pool_ref,
        grid_wn_ref,
        enc_wg_ref,
        dec_wg_ref,
        mesh_wn_ref,
        enc_wm_ref,
        base_ref,
        grad_mesh_ref,
    ):
        base_ref[...] = (
            cot_ref[...].astype(F32)
            + mm_t(grid_gpre_ref[...], grid_wn_ref[...])
            + mm_t(gpe_ref[...], enc_wg_ref[...])
            + mm_t(gpd_ref[...], dec_wg_ref[...])
        )
        grad_mesh_ref[...] = (
            mesh_gin_ref[...]
            + mm_t(mesh_gpre_ref[...], mesh_wn_ref[...])
            + mm_t(mesh_pool_ref[...], enc_wm_ref[...])
        )

    base, grad_mesh = call(
        tail,
        "local_gradients",
        [
            grid_cot,
            grid_gpre,
            gpe,
            gpd,
            mesh_gin,
            mesh_gpre,
            mesh_pool,
            (grid_first, 0, feat),
            (enc_first, 0, feat),
            (dec_first, 0, feat),
            (mesh_first, 0, feat),
            (enc_first, feat, feat),
        ],
        [((grid_count, feat), F32), ((mesh_count, feat), F32)],
        flops=2 * feat * feat * 3 * grid_count,
    )

    def finish(*refs):
        back_refs, (base_ref, select_t_ref, out_ref) = refs[:links], refs[links:]
        back = [back_refs[reverse[j]] for j in range(links)]
        out_ref[...] = base_ref[...] + mm(
            select_t_ref[:, :slots], stack(back, slice(0, feat))
        )

    (grad_grid,) = call(
        finish,
        "add_returned",
        [*final, base, select_t],
        [((grid_count, feat), F32)],
        flops=2 * grid_count * slots * feat,
    )
    return (grid_out, mesh_out, grad_grid, grad_mesh)


def solution(mesh):
    rows = P(("groups", "tile"), None)
    flat = P(("groups", "tile"))
    in_specs = (rows,) * 6 + (P(),) * 8 + (rows,) + (flat,) * 5
    return jax.shard_map(
        per_device, mesh=mesh, in_specs=in_specs, out_specs=(rows,) * 4, check_vma=False
    )
```

time: 143 us -> 77 us (0.54)
  matrix products: 36.6 us -> 0 us
  other arithmetic: 28.9 us -> 0 us
  Pallas kernels: 0 us -> 20.1 us
  starting transfers between devices: 15.2 us -> 32 us
  blocking collectives: 12.8 us -> 0 us
  waiting for transfers between devices: 21.2 us -> 9.37 us
  local copies, waits for them, and re-layouts: 25.4 us -> 14 us
    dot_general x40 -> x0, matrix products: 36.6 us -> none  [the longest x14 13.9 us: mixed_dot(): return jnp.dot(left, right, preferred_element_type=jnp.float32)]
    ppermute x0 -> x27, starting transfers between devices: none -> 32 us  [exchange(): lax.ppermute(part, 'tile', [(s, (s + offset) % peer_count) for s in range...]
    scatter-add x5 -> x0, other arithmetic: 22.2 us -> none  [the longest x1 7.68 us: per_device(): spot_gpd = jax.ops.segment_sum(dec_gpre, dec_grid, num_segments=spot_count)]
    all_to_all x3 -> x0, waiting for transfers between devices: 21.2 us -> none  [the longest x2 14.9 us: per_device(): lax.all_to_all(buffer, 'tile', split_axis=0, concat_axis=0, tiled=True)]
    pallas_call x0 -> x7, Pallas kernels: none -> 20.1 us  [call(): pl.pallas_call(kernel, name=name, in_specs=specs, out_specs=[pl.BlockSpec...]
    all_to_all x3 -> x0, starting transfers between devices: 15.2 us -> none  [the longest x2 11.7 us: per_device(): lax.all_to_all(buffer, 'tile', split_axis=0, concat_axis=0, tiled=True)]
    gather x6 -> x0, local copies, waits for them, and re-layouts: 13 us -> none  [the longest x2 4.72 us: per_device(): spot_grad[dec_grid].astype(jnp.float32)]
    all_to_all x1 -> x0, blocking collectives: 12.8 us -> none  [per_device(): lax.all_to_all(buffer, 'tile', split_axis=0, concat_axis=0, tiled=True)]
  transfers between devices with their start and end apart: 3 -> 27, of which waited for: 3 -> 7; matrix products, arithmetic and copies ran while one was open for 6% -> 4% of each run, Pallas kernels for 0% -> 8%
where the time goes in v1:
time: 77 us; the launch traced here: 76.4 us
  starting transfers between devices  32 us (42%)
  Pallas kernels  20.1 us (26%)
  local copies, waits for them, and re-layouts  14 us (18%)
  waiting for transfers between devices  9.37 us (12%)
  between operations  0.96 us (1%)
    ppermute x27, starting transfers between devices, exchange(): lax.ppermute(part, 'tile', [(s, (s + offset) % peer_count) for s in range...  32 us
    pallas_call x7, Pallas kernels, call(): pl.pallas_call(kernel, name=name, in_specs=specs, out_specs=[pl.BlockSpec...  20.1 us
    unnamed x44, local copies, waits for them, and re-layouts  11.3 us
    ppermute x27, waiting for transfers between devices, exchange(): lax.ppermute(part, 'tile', [(s, (s + offset) % peer_count) for s in range...  9.37 us
  transfers between devices with their start and end apart: 27, of which 7 were waited for; matrix products, arithmetic and copies ran while one was open for 4% of the time, Pallas kernels for 8%

profile of v1, /device:TPU:0, one launch (start us, length us, event | category | flops | bytes accessed | tf_op | source)
XLA Modules:
  0.0 76.4 jit_solution(14868880098163238932)
XLA Ops:
  5.2 2.6 %collective-permute-start.1 = (bf16[16,1024]{1,0:T(8,128)(2,1)S(1)}, bf16[16,1024]{1,0:T(8,128)(2,1)S(1)}, u32[]{:S(2)}, u32[]{:S(2)}) collective-permute-start(bf16[16,1024]{1,0:T(8,128)(2,1)S(1)} %get-tuple-element.61), channel_id=1, source_target_pairs={{0,4},{1,5},{2,6},{3,7},{4,8},{5,9},{6,10},{7,11},{8,12},{9,13},{1... | collective-permute-start | bytes 98312 | tf_op jit(solution)/shard_map/ppermute | solution.py:211
  7.9 2.5 %collective-permute-start.2 = (bf16[16,1024]{1,0:T(8,128)(2,1)S(1)}, bf16[16,1024]{1,0:T(8,128)(2,1)S(1)}, u32[]{:S(2)}, u32[]{:S(2)}) collective-permute-start(bf16[16,1024]{1,0:T(8,128)(2,1)S(1)} %get-tuple-element.62), channel_id=1, source_target_pairs={{0,5},{1,6},{2,7},{3,8},{4,9},{5,10},{6,11},{7,12},{8,13},{9,14},{... | collective-permute-start | bytes 98312 | tf_op jit(solution)/shard_map/ppermute | solution.py:211
  10.3 1.3 %collective-permute-start.3 = (bf16[16,1024]{1,0:T(8,128)(2,1)S(1)}, bf16[16,1024]{1,0:T(8,128)(2,1)S(1)}, u32[]{:S(2)}, u32[]{:S(2)}) collective-permute-start(bf16[16,1024]{1,0:T(8,128)(2,1)S(1)} %get-tuple-element.63), channel_id=1, source_target_pairs={{0,3},{1,4},{2,5},{3,6},{4,7},{5,8},{6,9},{7,10},{8,11},{9,12},{10... | collective-permute-start | bytes 98312 | tf_op jit(solution)/shard_map/ppermute | solution.py:211
  11.6 3.2 %collective-permute-start.4 = (bf16[16,1024]{1,0:T(8,128)(2,1)S(1)}, bf16[16,1024]{1,0:T(8,128)(2,1)S(1)}, u32[]{:S(2)}, u32[]{:S(2)}) collective-permute-start(bf16[16,1024]{1,0:T(8,128)(2,1)S(1)} %get-tuple-element.64), channel_id=1, source_target_pairs={{0,15},{1,0},{2,1},{3,2},{4,3},{5,4},{6,5},{7,6},{8,7},{9,8},{10,9... | collective-permute-start | bytes 98312 | tf_op jit(solution)/shard_map/ppermute | solution.py:211
  18.8 2.5 %collective-permute-start.8 = (bf16[16,1024]{1,0:T(8,128)(2,1)S(1)}, bf16[16,1024]{1,0:T(8,128)(2,1)S(1)}, u32[]{:S(2)}, u32[]{:S(2)}) collective-permute-start(bf16[16,1024]{1,0:T(8,128)(2,1)S(1)} %get-tuple-element.68), channel_id=1, source_target_pairs={{0,8},{1,9},{2,10},{3,11},{4,12},{5,13},{6,14},{7,15},{8,0},{9,1},... | collective-permute-start | bytes 98312 | tf_op jit(solution)/shard_map/ppermute | solution.py:211
  21.3 1.4 %copy-done = bf16[1536,512]{1,0:T(8,128)(2,1)S(1)} copy-done((bf16[1536,512]{1,0:T(8,128)(2,1)S(1)}, bf16[1536,512]{1,0:T(8,128)(2,1)}, u32[]{:S(2)}) %copy-start) | copy-done | bytes 1572888
  22.7 1.4 %copy-done.2 = bf16[1536,512]{1,0:T(8,128)(2,1)S(1)} copy-done((bf16[1536,512]{1,0:T(8,128)(2,1)S(1)}, bf16[1536,512]{1,0:T(8,128)(2,1)}, u32[]{:S(2)}) %copy-start.2) | copy-done | bytes 1572888
  24.1 1.2 %copy-done.4 = bf16[1024,512]{1,0:T(8,128)(2,1)S(1)} copy-done((bf16[1024,512]{1,0:T(8,128)(2,1)S(1)}, bf16[1024,512]{1,0:T(8,128)(2,1)}, u32[]{:S(2)}) %copy-start.4) | copy-done | bytes 1048600
  26.2 1.1 %copy-done.15 = bf16[768,512]{1,0:T(8,128)(2,1)S(1)} copy-done((bf16[768,512]{1,0:T(8,128)(2,1)S(1)}, bf16[768,512]{1,0:T(8,128)(2,1)}, u32[]{:S(2)}) %copy-start.15) | copy-done | bytes 786456
  29.2 3.5 %local_products.1 = (bf16[256,256]{1,0:T(8,128)(2,1)S(1)}, f32[384,512]{1,0:T(8,128)S(1)}, f32[768,512]{1,0:T(8,128)S(1)}, f32[64,512]{1,0:T(8,128)S(1)}, bf16[3...) custom-call(bf16[256,256]{1,0:T(8,128)(2,1)S(1)} %get-tuple-element., ...), custom_call_target="tpu_custom_call" | custom-call | flops 1275068416 | bytes 9774080 | tf_op jit(solution)/shard_map/local_products/pallas_call | solution.py:159
  32.8 4.8 %edges_forward.1 = (bf16[16,1024]{1,0:T(8,128)(2,1)S(1)}, bf16[16,1024]{1,0:T(8,128)(2,1)S(1)}, bf16[16,1024]{1,0:T(8,128)(2,1)S(1)}, bf16[16,1024]{1,0:T(8,128)...) custom-call(bf16[16,1024]{1,0:T(8,128)(2,1)S(1)} %collective-permute, ...), custom_call_target="tpu_custom_call" | custom-call | flops 1207959552 | bytes 12751616 | tf_op jit(solution)/shard_map/edges_forward/pallas_call | solution.py:159
  37.7 1.6 %collective-permute-start.10 = (bf16[16,1024]{1,0:T(8,128)(2,1)S(1)}, bf16[16,1024]{1,0:T(8,128)(2,1)S(1)}, u32[]{:S(2)}, u32[]{:S(2)}) collective-permute-start(bf16[16,1024]{1,0:T(8,128)(2,1)S(1)} %get-tuple-element.78), channel_id=1, source_target_pairs={{0,4},{1,5},{2,6},{3,7},{4,8},{5,9},{6,10},{7,11},{8,12},{9,13},{1... | collective-permute-start | bytes 98312 | tf_op jit(solution)/shard_map/ppermute | solution.py:211
  39.3 1.5 %collective-permute-start.12 = (bf16[16,1024]{1,0:T(8,128)(2,1)S(1)}, bf16[16,1024]{1,0:T(8,128)(2,1)S(1)}, u32[]{:S(2)}, u32[]{:S(2)}) collective-permute-start(bf16[16,1024]{1,0:T(8,128)(2,1)S(1)} %get-tuple-element.80), channel_id=1, source_target_pairs={{0,3},{1,4},{2,5},{3,6},{4,7},{5,8},{6,9},{7,10},{8,11},{9,12},{10... | collective-permute-start | bytes 98312 | tf_op jit(solution)/shard_map/ppermute | solution.py:211
  40.8 1.5 %collective-permute-start.13 = (bf16[16,1024]{1,0:T(8,128)(2,1)S(1)}, bf16[16,1024]{1,0:T(8,128)(2,1)S(1)}, u32[]{:S(2)}, u32[]{:S(2)}) collective-permute-start(bf16[16,1024]{1,0:T(8,128)(2,1)S(1)} %get-tuple-element.81), channel_id=1, source_target_pairs={{0,15},{1,0},{2,1},{3,2},{4,3},{5,4},{6,5},{7,6},{8,7},{9,8},{10,9... | collective-permute-start | bytes 98312 | tf_op jit(solution)/shard_map/ppermute | solution.py:211
  42.3 2.0 %collective-permute-start.14 = (bf16[16,1024]{1,0:T(8,128)(2,1)S(1)}, bf16[16,1024]{1,0:T(8,128)(2,1)S(1)}, u32[]{:S(2)}, u32[]{:S(2)}) collective-permute-start(bf16[16,1024]{1,0:T(8,128)(2,1)S(1)} %get-tuple-element.82), channel_id=1, source_target_pairs={{0,12},{1,13},{2,14},{3,15},{4,0},{5,1},{6,2},{7,3},{8,4},{9,5},{1... | collective-permute-start | bytes 98312 | tf_op jit(solution)/shard_map/ppermute | solution.py:211
  45.9 1.6 %collective-permute-start.17 = (bf16[16,1024]{1,0:T(8,128)(2,1)S(1)}, bf16[16,1024]{1,0:T(8,128)(2,1)S(1)}, u32[]{:S(2)}, u32[]{:S(2)}) collective-permute-start(bf16[16,1024]{1,0:T(8,128)(2,1)S(1)} %get-tuple-element.85), channel_id=1, source_target_pairs={{0,8},{1,9},{2,10},{3,11},{4,12},{5,13},{6,14},{7,15},{8,0},{9,1},... | collective-permute-start | bytes 98312 | tf_op jit(solution)/shard_map/ppermute | solution.py:211
  48.6 2.7 %collective-permute-done.17.refs_17_ = bf16[16,1024]{1,0:T(8,128)(2,1)S(1)} collective-permute-done((bf16[16,1024]{1,0:T(8,128)(2,1)S(1)}, bf16[16,1024]{1,0:T(8,128)(2,1)S(1)}, u32[]{:S(2)}, u32[]{:S(2)}) %collective-permute-start.17) | collective-permute-done | bytes 32800 | tf_op jit(solution)/shard_map/ppermute | solution.py:211
  51.3 2.3 %collective-permute-done.9.refs_9_ = bf16[16,1024]{1,0:T(8,128)(2,1)S(1)} collective-permute-done((bf16[16,1024]{1,0:T(8,128)(2,1)S(1)}, bf16[16,1024]{1,0:T(8,128)(2,1)S(1)}, u32[]{:S(2)}, u32[]{:S(2)}) %collective-permute-start.9) | collective-permute-done | bytes 32800 | tf_op jit(solution)/shard_map/ppermute | solution.py:211
  53.6 7.4 %edges_backward.1 = (bf16[16,512]{1,0:T(8,128)(2,1)S(1)}, bf16[16,512]{1,0:T(8,128)(2,1)S(1)}, bf16[16,512]{1,0:T(8,128)(2,1)S(1)}, bf16[16,512]{1,0:T(8,128)(2,...) custom-call(bf16[16,1024]{1,0:T(8,128)(2,1)S(1)} %collective-permute, ...), custom_call_target="tpu_custom_call" | custom-call | flops 2449473536 | bytes 14045952 | tf_op jit(solution)/shard_map/edges_backward/pallas_call | solution.py:159
  61.2 2.1 %collective-permute-start.21 = (bf16[16,512]{1,0:T(8,128)(2,1)S(1)}, bf16[16,512]{1,0:T(8,128)(2,1)S(1)}, u32[]{:S(2)}, u32[]{:S(2)}) collective-permute-start(bf16[16,512]{1,0:T(8,128)(2,1)S(1)} %get-tuple-element.102), channel_id=1, source_target_pairs={{0,3},{1,4},{2,5},{3,6},{4,7},{5,8},{6,9},{7,10},{8,11},{9,12},{10... | collective-permute-start | bytes 49160 | tf_op jit(solution)/shard_map/ppermute | solution.py:211
  63.3 3.2 %collective-permute-start.22 = (bf16[16,512]{1,0:T(8,128)(2,1)S(1)}, bf16[16,512]{1,0:T(8,128)(2,1)S(1)}, u32[]{:S(2)}, u32[]{:S(2)}) collective-permute-start(bf16[16,512]{1,0:T(8,128)(2,1)S(1)} %get-tuple-element.103), channel_id=1, source_target_pairs={{0,15},{1,0},{2,1},{3,2},{4,3},{5,4},{6,5},{7,6},{8,7},{9,8},{10,9... | collective-permute-start | bytes 49160 | tf_op jit(solution)/shard_map/ppermute | solution.py:211
  68.0 2.8 %collective-permute-start.25 = (bf16[16,512]{1,0:T(8,128)(2,1)S(1)}, bf16[16,512]{1,0:T(8,128)(2,1)S(1)}, u32[]{:S(2)}, u32[]{:S(2)}) collective-permute-start(bf16[16,512]{1,0:T(8,128)(2,1)S(1)} %get-tuple-element.106), channel_id=1, source_target_pairs={{0,13},{1,14},{2,15},{3,0},{4,1},{5,2},{6,3},{7,4},{8,5},{9,6},{10... | collective-permute-start | bytes 49160 | tf_op jit(solution)/shard_map/ppermute | solution.py:211
  70.7 2.2 %local_gradients.1 = (f32[256,512]{1,0:T(8,128)S(1)}, f32[64,512]{1,0:T(8,128)}) custom-call(bf16[256,512]{1,0:T(8,128)(2,1)S(1)} %copy-done.11, bf16[256,512]{1,0:T(8,128)(2,1)S(1)} %get-tuple-element.108.refs_1_, bf16[256,512]{1,0:T(8,128)(2,1)S(1)} %get-tuple-element.109.refs_2_, bf16[256,512]{1,0:T(8,128)(2,1)S(1)} %get-tuple-element.110.refs_3_, ...), custom_call_target="tpu_custom_call" | custom-call | flops 402653184 | bytes 4587520 | tf_op jit(solution)/shard_map/local_gradients/pallas_call | solution.py:159
  73.0 2.4 %collective-permute-done.26.refs_8_ = bf16[16,512]{1,0:T(8,128)(2,1)S(1)} collective-permute-done((bf16[16,512]{1,0:T(8,128)(2,1)S(1)}, bf16[16,512]{1,0:T(8,128)(2,1)S(1)}, u32[]{:S(2)}, u32[]{:S(2)}) %collective-permute-start.26) | collective-permute-done | bytes 16416 | tf_op jit(solution)/shard_map/ppermute | solution.py:211
  (85 shorter events, 16.7 us)
Async XLA Ops:
  4.7 12.9 %collective-permute-start = (bf16[16,1024]{1,0:T(8,128)(2,1)S(1)}, bf16[16,1024]{1,0:T(8,128)(2,1)S(1)}, u32[]{:S(2)}, u32[]{:S(2)}) collective-permute-start(bf16[16,1024]{1,0:T(8,128)(2,1)S(1)} %get-tuple-element.60), channel_id=1, source_target_pairs={{0,1},{1,2},{2,3},{3,4},{4,5},{5,6},{6,7},{7,8},{8,9},{9,10},{10,1... | collective-permute-start | bytes 98312 | tf_op jit(solution)/shard_map/ppermute | solution.py:211
  5.2 12.8 %collective-permute-start.1 = (bf16[16,1024]{1,0:T(8,128)(2,1)S(1)}, bf16[16,1024]{1,0:T(8,128)(2,1)S(1)}, u32[]{:S(2)}, u32[]{:S(2)}) collective-permute-start(bf16[16,1024]{1,0:T(8,128)(2,1)S(1)} %get-tuple-element.61), channel_id=1, source_target_pairs={{0,4},{1,5},{2,6},{3,7},{4,8},{5,9},{6,10},{7,11},{8,12},{9,13},{1... | collective-permute-start | bytes 98312 | tf_op jit(solution)/shard_map/ppermute | solution.py:211
  7.9 10.2 %collective-permute-start.2 = (bf16[16,1024]{1,0:T(8,128)(2,1)S(1)}, bf16[16,1024]{1,0:T(8,128)(2,1)S(1)}, u32[]{:S(2)}, u32[]{:S(2)}) collective-permute-start(bf16[16,1024]{1,0:T(8,128)(2,1)S(1)} %get-tuple-element.62), channel_id=1, source_target_pairs={{0,5},{1,6},{2,7},{3,8},{4,9},{5,10},{6,11},{7,12},{8,13},{9,14},{... | collective-permute-start | bytes 98312 | tf_op jit(solution)/shard_map/ppermute | solution.py:211
  10.3 8.4 %collective-permute-start.3 = (bf16[16,1024]{1,0:T(8,128)(2,1)S(1)}, bf16[16,1024]{1,0:T(8,128)(2,1)S(1)}, u32[]{:S(2)}, u32[]{:S(2)}) collective-permute-start(bf16[16,1024]{1,0:T(8,128)(2,1)S(1)} %get-tuple-element.63), channel_id=1, source_target_pairs={{0,3},{1,4},{2,5},{3,6},{4,7},{5,8},{6,9},{7,10},{8,11},{9,12},{10... | collective-permute-start | bytes 98312 | tf_op jit(solution)/shard_map/ppermute | solution.py:211
  11.6 21.1 %collective-permute-start.4 = (bf16[16,1024]{1,0:T(8,128)(2,1)S(1)}, bf16[16,1024]{1,0:T(8,128)(2,1)S(1)}, u32[]{:S(2)}, u32[]{:S(2)}) collective-permute-start(bf16[16,1024]{1,0:T(8,128)(2,1)S(1)} %get-tuple-element.64), channel_id=1, source_target_pairs={{0,15},{1,0},{2,1},{3,2},{4,3},{5,4},{6,5},{7,6},{8,7},{9,8},{10,9... | collective-permute-start | bytes 98312 | tf_op jit(solution)/shard_map/ppermute | solution.py:211
  17.6 15.1 %collective-permute-start.5 = (bf16[16,1024]{1,0:T(8,128)(2,1)S(1)}, bf16[16,1024]{1,0:T(8,128)(2,1)S(1)}, u32[]{:S(2)}, u32[]{:S(2)}) collective-permute-start(bf16[16,1024]{1,0:T(8,128)(2,1)S(1)} %get-tuple-element.65), channel_id=1, source_target_pairs={{0,12},{1,13},{2,14},{3,15},{4,0},{5,1},{6,2},{7,3},{8,4},{9,5},{1... | collective-permute-start | bytes 98312 | tf_op jit(solution)/shard_map/ppermute | solution.py:211
  18.0 14.7 %collective-permute-start.6 = (bf16[16,1024]{1,0:T(8,128)(2,1)S(1)}, bf16[16,1024]{1,0:T(8,128)(2,1)S(1)}, u32[]{:S(2)}, u32[]{:S(2)}) collective-permute-start(bf16[16,1024]{1,0:T(8,128)(2,1)S(1)} %get-tuple-element.66), channel_id=1, source_target_pairs={{0,11},{1,12},{2,13},{3,14},{4,15},{5,0},{6,1},{7,2},{8,3},{9,4},{... | collective-permute-start | bytes 98312 | tf_op jit(solution)/shard_map/ppermute | solution.py:211
  18.0 14.7 %collective-permute-start.7 = (bf16[16,1024]{1,0:T(8,128)(2,1)S(1)}, bf16[16,1024]{1,0:T(8,128)(2,1)S(1)}, u32[]{:S(2)}, u32[]{:S(2)}) collective-permute-start(bf16[16,1024]{1,0:T(8,128)(2,1)S(1)} %get-tuple-element.67), channel_id=1, source_target_pairs={{0,13},{1,14},{2,15},{3,0},{4,1},{5,2},{6,3},{7,4},{8,5},{9,6},{10... | collective-permute-start | bytes 98312 | tf_op jit(solution)/shard_map/ppermute | solution.py:211
  18.8 14.0 %collective-permute-start.8 = (bf16[16,1024]{1,0:T(8,128)(2,1)S(1)}, bf16[16,1024]{1,0:T(8,128)(2,1)S(1)}, u32[]{:S(2)}, u32[]{:S(2)}) collective-permute-start(bf16[16,1024]{1,0:T(8,128)(2,1)S(1)} %get-tuple-element.68), channel_id=1, source_target_pairs={{0,8},{1,9},{2,10},{3,11},{4,12},{5,13},{6,14},{7,15},{8,0},{9,1},... | collective-permute-start | bytes 98312 | tf_op jit(solution)/shard_map/ppermute | solution.py:211
  37.7 6.6 %collective-permute-start.10 = (bf16[16,1024]{1,0:T(8,128)(2,1)S(1)}, bf16[16,1024]{1,0:T(8,128)(2,1)S(1)}, u32[]{:S(2)}, u32[]{:S(2)}) collective-permute-start(bf16[16,1024]{1,0:T(8,128)(2,1)S(1)} %get-tuple-element.78), channel_id=1, source_target_pairs={{0,4},{1,5},{2,6},{3,7},{4,8},{5,9},{6,10},{7,11},{8,12},{9,13},{1... | collective-permute-start | bytes 98312 | tf_op jit(solution)/shard_map/ppermute | solution.py:211
  39.3 6.0 %collective-permute-start.11 = (bf16[16,1024]{1,0:T(8,128)(2,1)S(1)}, bf16[16,1024]{1,0:T(8,128)(2,1)S(1)}, u32[]{:S(2)}, u32[]{:S(2)}) collective-permute-start(bf16[16,1024]{1,0:T(8,128)(2,1)S(1)} %get-tuple-element.79), channel_id=1, source_target_pairs={{0,5},{1,6},{2,7},{3,8},{4,9},{5,10},{6,11},{7,12},{8,13},{9,14},{... | collective-permute-start | bytes 98312 | tf_op jit(solution)/shard_map/ppermute | solution.py:211
  39.3 6.7 %collective-permute-start.12 = (bf16[16,1024]{1,0:T(8,128)(2,1)S(1)}, bf16[16,1024]{1,0:T(8,128)(2,1)S(1)}, u32[]{:S(2)}, u32[]{:S(2)}) collective-permute-start(bf16[16,1024]{1,0:T(8,128)(2,1)S(1)} %get-tuple-element.80), channel_id=1, source_target_pairs={{0,3},{1,4},{2,5},{3,6},{4,7},{5,8},{6,9},{7,10},{8,11},{9,12},{10... | collective-permute-start | bytes 98312 | tf_op jit(solution)/shard_map/ppermute | solution.py:211
  40.8 6.7 %collective-permute-start.13 = (bf16[16,1024]{1,0:T(8,128)(2,1)S(1)}, bf16[16,1024]{1,0:T(8,128)(2,1)S(1)}, u32[]{:S(2)}, u32[]{:S(2)}) collective-permute-start(bf16[16,1024]{1,0:T(8,128)(2,1)S(1)} %get-tuple-element.81), channel_id=1, source_target_pairs={{0,15},{1,0},{2,1},{3,2},{4,3},{5,4},{6,5},{7,6},{8,7},{9,8},{10,9... | collective-permute-start | bytes 98312 | tf_op jit(solution)/shard_map/ppermute | solution.py:211
  42.3 5.7 %collective-permute-start.14 = (bf16[16,1024]{1,0:T(8,128)(2,1)S(1)}, bf16[16,1024]{1,0:T(8,128)(2,1)S(1)}, u32[]{:S(2)}, u32[]{:S(2)}) collective-permute-start(bf16[16,1024]{1,0:T(8,128)(2,1)S(1)} %get-tuple-element.82), channel_id=1, source_target_pairs={{0,12},{1,13},{2,14},{3,15},{4,0},{5,1},{6,2},{7,3},{8,4},{9,5},{1... | collective-permute-start | bytes 98312 | tf_op jit(solution)/shard_map/ppermute | solution.py:211
  45.9 5.4 %collective-permute-start.17 = (bf16[16,1024]{1,0:T(8,128)(2,1)S(1)}, bf16[16,1024]{1,0:T(8,128)(2,1)S(1)}, u32[]{:S(2)}, u32[]{:S(2)}) collective-permute-start(bf16[16,1024]{1,0:T(8,128)(2,1)S(1)} %get-tuple-element.85), channel_id=1, source_target_pairs={{0,8},{1,9},{2,10},{3,11},{4,12},{5,13},{6,14},{7,15},{8,0},{9,1},... | collective-permute-start | bytes 98312 | tf_op jit(solution)/shard_map/ppermute | solution.py:211
  47.5 6.0 %collective-permute-start.9 = (bf16[16,1024]{1,0:T(8,128)(2,1)S(1)}, bf16[16,1024]{1,0:T(8,128)(2,1)S(1)}, u32[]{:S(2)}, u32[]{:S(2)}) collective-permute-start(bf16[16,1024]{1,0:T(8,128)(2,1)S(1)} %get-tuple-element.77), channel_id=1, source_target_pairs={{0,1},{1,2},{2,3},{3,4},{4,5},{5,6},{6,7},{7,8},{8,9},{9,10},{10,1... | collective-permute-start | bytes 98312 | tf_op jit(solution)/shard_map/ppermute | solution.py:211
  61.0 5.9 %collective-permute-start.18 = (bf16[16,512]{1,0:T(8,128)(2,1)S(1)}, bf16[16,512]{1,0:T(8,128)(2,1)S(1)}, u32[]{:S(2)}, u32[]{:S(2)}) collective-permute-start(bf16[16,512]{1,0:T(8,128)(2,1)S(1)} %get-tuple-element.99), channel_id=1, source_target_pairs={{0,1},{1,2},{2,3},{3,4},{4,5},{5,6},{6,7},{7,8},{8,9},{9,10},{10,1... | collective-permute-start | bytes 49160 | tf_op jit(solution)/shard_map/ppermute | solution.py:211
  61.1 6.2 %collective-permute-start.19 = (bf16[16,512]{1,0:T(8,128)(2,1)S(1)}, bf16[16,512]{1,0:T(8,128)(2,1)S(1)}, u32[]{:S(2)}, u32[]{:S(2)}) collective-permute-start(bf16[16,512]{1,0:T(8,128)(2,1)S(1)} %get-tuple-element.100), channel_id=1, source_target_pairs={{0,4},{1,5},{2,6},{3,7},{4,8},{5,9},{6,10},{7,11},{8,12},{9,13},{1... | collective-permute-start | bytes 49160 | tf_op jit(solution)/shard_map/ppermute | solution.py:211
  61.1 6.8 %collective-permute-start.20 = (bf16[16,512]{1,0:T(8,128)(2,1)S(1)}, bf16[16,512]{1,0:T(8,128)(2,1)S(1)}, u32[]{:S(2)}, u32[]{:S(2)}) collective-permute-start(bf16[16,512]{1,0:T(8,128)(2,1)S(1)} %get-tuple-element.101), channel_id=1, source_target_pairs={{0,5},{1,6},{2,7},{3,8},{4,9},{5,10},{6,11},{7,12},{8,13},{9,14},{... | collective-permute-start | bytes 49160 | tf_op jit(solution)/shard_map/ppermute | solution.py:211
  61.2 9.6 %collective-permute-start.21 = (bf16[16,512]{1,0:T(8,128)(2,1)S(1)}, bf16[16,512]{1,0:T(8,128)(2,1)S(1)}, u32[]{:S(2)}, u32[]{:S(2)}) collective-permute-start(bf16[16,512]{1,0:T(8,128)(2,1)S(1)} %get-tuple-element.102), channel_id=1, source_target_pairs={{0,3},{1,4},{2,5},{3,6},{4,7},{5,8},{6,9},{7,10},{8,11},{9,12},{10... | collective-permute-start | bytes 49160 | tf_op jit(solution)/shard_map/ppermute | solution.py:211
  63.3 9.6 %collective-permute-start.22 = (bf16[16,512]{1,0:T(8,128)(2,1)S(1)}, bf16[16,512]{1,0:T(8,128)(2,1)S(1)}, u32[]{:S(2)}, u32[]{:S(2)}) collective-permute-start(bf16[16,512]{1,0:T(8,128)(2,1)S(1)} %get-tuple-element.103), channel_id=1, source_target_pairs={{0,15},{1,0},{2,1},{3,2},{4,3},{5,4},{6,5},{7,6},{8,7},{9,8},{10,9... | collective-permute-start | bytes 49160 | tf_op jit(solution)/shard_map/ppermute | solution.py:211
  66.9 6.0 %collective-permute-start.23 = (bf16[16,512]{1,0:T(8,128)(2,1)S(1)}, bf16[16,512]{1,0:T(8,128)(2,1)S(1)}, u32[]{:S(2)}, u32[]{:S(2)}) collective-permute-start(bf16[16,512]{1,0:T(8,128)(2,1)S(1)} %get-tuple-element.104), channel_id=1, source_target_pairs={{0,12},{1,13},{2,14},{3,15},{4,0},{5,1},{6,2},{7,3},{8,4},{9,5},{1... | collective-permute-start | bytes 49160 | tf_op jit(solution)/shard_map/ppermute | solution.py:211
  67.2 5.7 %collective-permute-start.24 = (bf16[16,512]{1,0:T(8,128)(2,1)S(1)}, bf16[16,512]{1,0:T(8,128)(2,1)S(1)}, u32[]{:S(2)}, u32[]{:S(2)}) collective-permute-start(bf16[16,512]{1,0:T(8,128)(2,1)S(1)} %get-tuple-element.105), channel_id=1, source_target_pairs={{0,11},{1,12},{2,13},{3,14},{4,15},{5,0},{6,1},{7,2},{8,3},{9,4},{... | collective-permute-start | bytes 49160 | tf_op jit(solution)/shard_map/ppermute | solution.py:211
  68.0 5.0 %collective-permute-start.25 = (bf16[16,512]{1,0:T(8,128)(2,1)S(1)}, bf16[16,512]{1,0:T(8,128)(2,1)S(1)}, u32[]{:S(2)}, u32[]{:S(2)}) collective-permute-start(bf16[16,512]{1,0:T(8,128)(2,1)S(1)} %get-tuple-element.106), channel_id=1, source_target_pairs={{0,13},{1,14},{2,15},{3,0},{4,1},{5,2},{6,3},{7,4},{8,5},{9,6},{10... | collective-permute-start | bytes 49160 | tf_op jit(solution)/shard_map/ppermute | solution.py:211
  (25 other events, 133.9 us)

commit v2 on v1

--- a/solution.py
+++ b/solution.py
@@ -81,8 +81,8 @@
 
 def onehot_pair(spot_ref, mesh_ref, spots, by_edge_ref, by_spot_ref):
     edges, total = by_edge_ref.shape
-    spot_row = spot_ref[...].astype(F32)
-    mesh_row = mesh_ref[...].astype(F32) + float(spots)
+    spot_row = spot_ref[...].reshape(1, -1).astype(F32)
+    mesh_row = mesh_ref[...].reshape(1, -1).astype(F32) + float(spots)
     for rows in row_chunks(total, 64):
         ids = lax.broadcasted_iota(jnp.int32, (rows.stop - rows.start, edges), 0) + rows.start
         ids = ids.astype(F32)
@@ -120,13 +120,13 @@
     for place, entry in enumerate(inputs):
         if isinstance(entry, tuple):
             array, first, rows = entry
-            specs.append(pl.BlockSpec(memory_space=pl.ANY))
-            fetches.append((place, first, rows, (rows, array.shape[1]), array.dtype))
-            moved += rows * array.shape[1] * array.dtype.itemsize
+            specs.append(pl.BlockSpec(memory_space=pltpu.HBM))
+            shape = (rows,) + array.shape[1:]
+            fetches.append((place, first, rows, shape, array.dtype))
+            moved += rows * (array.size // array.shape[0]) * array.dtype.itemsize
         else:
             array = entry
-            smem = array.dtype == jnp.int32 and array.ndim == 1
-            specs.append(pl.BlockSpec(memory_space=pltpu.SMEM if smem else pltpu.VMEM))
+            specs.append(pl.BlockSpec(memory_space=pltpu.VMEM))
             moved += array.size * array.dtype.itemsize
         arrays.append(array)
     shapes = [jax.ShapeDtypeStruct(shape, dtype) for shape, dtype in outputs]
@@ -147,10 +147,11 @@
             refs[-1],
         )
         waiting = []
-        for slot, (place, first, rows, _, _) in enumerate(fetches):
-            refs[place] = Fetched(
-                refs[place].at[pl.ds(first, rows), :], targets[slot], semaphores.at[slot]
-            )
+        for slot, (place, first, rows, shape, _) in enumerate(fetches):
+            source = refs[place]
+            if source.shape != shape:
+                source = source.at[pl.ds(first, rows)]
+            refs[place] = Fetched(source, targets[slot], semaphores.at[slot])
             waiting.append(refs[place])
         body(*refs)
         for fetched in waiting:
@@ -213,19 +214,23 @@
         ]
 
     def pack(index_ref, count_ref, nodes_ref, cot_ref, select_ref, *out_refs):
-        shape = (width, grid_count)
-        eye = lax.broadcasted_iota(jnp.int32, (width, width), 0) == lax.broadcasted_iota(
-            jnp.int32, (width, width), 1
-        )
-        lane = lax.broadcasted_iota(jnp.int32, shape, 1).astype(F32)
-        place = lax.broadcasted_iota(jnp.int32, shape, 0)
-        index = index_ref[...].astype(F32)
-        picks = []
-        for j in range(links):
-            row = jnp.broadcast_to(index[j : j + 1, :], (width, width))
-            column = jnp.sum(jnp.where(eye, row, 0.0), axis=1, keepdims=True)
-            hit = (lane == column) & (place < count_ref[j])
-            picks.append(jnp.where(hit, 1.0, 0.0).astype(BF16))
+        def column(row):
+            count = row.shape[1]
+            eye = lax.broadcasted_iota(jnp.int32, (count, count), 0) == lax.broadcasted_iota(
+                jnp.int32, (count, count), 1
+            )
+            return jnp.sum(
+                jnp.where(eye, jnp.broadcast_to(row, (count, count)), 0.0), axis=1, keepdims=True
+            )
+
+        counts = column(count_ref[...].reshape(1, -1).astype(F32))
+        place = lax.broadcasted_iota(jnp.int32, (links, width), 1).astype(F32)
+        index = jnp.where(place < counts, index_ref[...].astype(F32), -1.0)
+        lane = lax.broadcasted_iota(jnp.int32, (width, grid_count), 1).astype(F32)
+        picks = [
+            jnp.where(lane == column(index[j : j + 1, :]), 1.0, 0.0).astype(BF16)
+            for j in range(links)
+        ]
         select = jnp.concatenate(picks, axis=0)
         select_ref[:slots, :] = select
         select_ref[slots:, :] = jnp.zeros((slots_pad - slots, grid_count), BF16)
@@ -239,7 +244,12 @@
     select, *outgoing = call(
         pack,
         "pack_rows",
-        [send_index, send_count, grid_nodes, grid_cot],
+        [
+            (send_index, 0, links),
+            (send_count, 0, links),
+            (grid_nodes, 0, grid_count),
+            (grid_cot, 0, grid_count),
+        ],
         [((slots_pad, grid_count), BF16)] + [((width, 2 * feat), BF16)] * links,
         flops=4 * slots * grid_count * feat,
     )
@@ -290,20 +300,20 @@
         "local_products",
         [
             select,
-            grid_nodes,
-            mesh_nodes,
-            enc_edges,
-            dec_edges,
+            (grid_nodes, 0, grid_count),
+            (mesh_nodes, 0, mesh_count),
+            (enc_edges, 0, enc_count),
+            (dec_edges, 0, dec_count),
             (enc_first, 0, feat),
             (enc_first, feat, feat),
             (enc_first, 2 * feat, feat),
             (dec_first, 0, feat),
             (dec_first, 2 * feat, feat),
             (mesh_first, 0, feat),
-            enc_grid.reshape(1, -1),
-            enc_mesh.reshape(1, -1),
-            dec_grid.reshape(1, -1),
-            dec_mesh.reshape(1, -1),
+            (enc_grid, 0, enc_grid.shape[0]),
+            (enc_mesh, 0, enc_mesh.shape[0]),
+            (dec_grid, 0, dec_grid.shape[0]),
+            (dec_mesh, 0, dec_mesh.shape[0]),
         ],
         [
             ((grid_count, slots_pad), BF16),
@@ -359,17 +369,17 @@
             table_ref,
         ) = refs
         rows = stack(arrived_refs, low)
-        pe = mm(rows, enc_wg_ref[...]).astype(BF16)
+        pe = mm(rows, enc_wg_ref[low, :]).astype(BF16)
         pre = enc_part_ref[...] + mm(enc_pick_ref[:, grid_count:spots], pe)
         activate(pre, enc_act_ref, enc_slope_ref)
         norm_forward(mm(enc_act_ref[...], enc_w2_ref[...]), enc_normed_ref, enc_scale_ref)
         agg = mm(enc_pool_ref[mesh_rows, :], enc_normed_ref[...]).astype(BF16)
-        activate(mesh_part_ref[...] + mm(agg, mesh_wa_ref[...]), mesh_act_ref, mesh_slope_ref)
+        activate(mesh_part_ref[...] + mm(agg, mesh_wa_ref[high, :]), mesh_act_ref, mesh_slope_ref)
         norm_forward(mm(mesh_act_ref[...], mesh_w2_ref[...]), mesh_normed_ref, mesh_scale_ref)
         mesh_out = (mesh_ref[...].astype(F32) + mesh_normed_ref[...]).astype(BF16)
         mesh_out_ref[...] = mesh_out
-        table_ref[:slots, :] = mm(rows, dec_wg_ref[...]).astype(BF16)
-        table_ref[slots : slots + mesh_count, :] = mm(mesh_out, dec_wm_ref[...]).astype(BF16)
+        table_ref[:slots, :] = mm(rows, dec_wg_ref[low, :]).astype(BF16)
+        table_ref[slots : slots + mesh_count, :] = mm(mesh_out, dec_wm_ref[high, :]).astype(BF16)
         table_ref[slots + mesh_count :, :] = jnp.zeros(
             (total - spots - mesh_count, feat), BF16
         )
@@ -408,13 +418,13 @@
             dec_pick,
             dec_pool,
             mesh_nodes,
-            (enc_first, 0, feat),
-            (dec_first, 0, feat),
-            (enc_second, 0, feat),
-            (mesh_first, feat, feat),
-            (mesh_second, 0, feat),
-            (dec_first, feat, feat),
-            (dec_second, 0, feat),
+            enc_first,
+            dec_first,
+            enc_second,
+            mesh_first,
+            mesh_second,
+            dec_first,
+            dec_second,
         ],
         [((width, 2 * feat), BF16)] * links
         + [((mesh_count, feat), BF16), ((spots, feat), F32)]
@@ -433,13 +443,13 @@
 
     def node_part(*refs):
         arrived_refs, (nodes_ref, weight_ref, out_ref) = refs[:links], refs[links:]
-        out_ref[:grid_count, :] = mm(nodes_ref[...], weight_ref[...])
-        out_ref[grid_count:, :] = mm(stack(arrived_refs, low), weight_ref[...])
+        out_ref[:grid_count, :] = mm(nodes_ref[...], weight_ref[low, :])
+        out_ref[grid_count:, :] = mm(stack(arrived_refs, low), weight_ref[low, :])
 
     (grid_part,) = call(
         node_part,
         "node_products",
-        [*arrived, grid_nodes, (grid_first, 0, feat)],
+        [*arrived, grid_nodes, grid_first],
         [((spots, feat), F32)],
         flops=2 * spots * feat * feat,
     )
@@ -477,8 +487,8 @@
             mesh_slope_ref,
         ) = refs[:28]
         refs = refs[28:]
-        out_refs, refs = refs[:links], refs[links:]
         (
+            slot_back_ref,
             grid_out_ref,
             grid_gpre_ref,
             gpe_ref,
@@ -506,7 +516,7 @@
             spot_ref[grid_count:, :] + stack(returned_refs, high).astype(F32)
         ).astype(BF16)
         activate(
-            grid_part_ref[...] + mm(agg_ref[...], grid_wa_ref[...]), grid_act_ref, grid_slope_ref
+            grid_part_ref[...] + mm(agg_ref[...], grid_wa_ref[high, :]), grid_act_ref, grid_slope_ref
         )
         norm_forward(mm(grid_act_ref[...], grid_w2_ref[...]), grid_normed_ref, grid_scale_ref)
         grid_out_ref[...] = (
@@ -516,7 +526,7 @@
         norm_backward(grid_normed_ref, grid_scale_ref, cot, grid_gout_ref)
         times_slope(mm_t(grid_gout_ref[...], grid_w2_ref[...]), grid_slope_ref, grid_gall_ref)
         grid_gpre_ref[...] = grid_gall_ref[:grid_count, :]
-        spot_grad_ref[:spots, :] = mm_t(grid_gall_ref[...], grid_wa_ref[...]).astype(BF16)
+        spot_grad_ref[:spots, :] = mm_t(grid_gall_ref[...], grid_wa_ref[high, :]).astype(BF16)
         spot_grad_ref[spots:, :] = jnp.zeros((total - spots, feat), BF16)
         norm_backward(
             dec_normed_ref, dec_scale_ref, mm(dec_pick_ref[...], spot_grad_ref[...]), dec_gout_ref
@@ -524,12 +534,12 @@
         times_slope(mm_t(dec_gout_ref[...], dec_w2_ref[...]), dec_slope_ref, dec_gout_ref)
         pooled = mm(dec_pool_ref[...], dec_gout_ref[...]).astype(BF16)
         gpd_ref[...] = pooled[:grid_count, :]
-        slot_back = mm_t(pooled[grid_count:spots, :], dec_wg_ref[...])
-        mesh_gin = mesh_cot_ref[...].astype(F32) + mm_t(pooled[mesh_rows, :], dec_wm_ref[...])
+        slot_back = mm_t(pooled[grid_count:spots, :], dec_wg_ref[low, :])
+        mesh_gin = mesh_cot_ref[...].astype(F32) + mm_t(pooled[mesh_rows, :], dec_wm_ref[high, :])
         mesh_gin_ref[...] = mesh_gin
         norm_backward(mesh_normed_ref, mesh_scale_ref, mesh_gin, mesh_gout_ref)
         times_slope(mm_t(mesh_gout_ref[...], mesh_w2_ref[...]), mesh_slope_ref, mesh_gpre_ref)
-        gagg = mm_t(mesh_gpre_ref[...], mesh_wa_ref[...]).astype(BF16)
+        gagg = mm_t(mesh_gpre_ref[...], mesh_wa_ref[high, :]).astype(BF16)
         norm_backward(
             enc_normed_ref, enc_scale_ref, mm(enc_pick_ref[:, mesh_rows], gagg), enc_gout_ref
         )
@@ -537,10 +547,8 @@
         pooled = mm(enc_pool_ref[...], enc_gout_ref[...]).astype(BF16)
         gpe_ref[...] = pooled[:grid_count, :]
         mesh_pool_ref[...] = pooled[mesh_rows, :]
-        slot_back = (slot_back + mm_t(pooled[grid_count:spots, :], enc_wg_ref[...])).astype(BF16)
-        for j, out_ref in enumerate(out_refs):
-            start = reverse[j] * width
-            out_ref[...] = slot_back[start : start + width, :]
+        slot_back = (slot_back + mm_t(pooled[grid_count:spots, :], enc_wg_ref[low, :])).astype(BF16)
+        slot_back_ref[...] = slot_back
 
     results = call(
         backward,
@@ -558,18 +566,18 @@
             enc_pool,
             dec_pick,
             dec_pool,
-            (grid_first, feat, feat),
-            (grid_second, 0, feat),
-            (dec_second, 0, feat),
-            (dec_first, feat, feat),
-            (mesh_first, feat, feat),
-            (mesh_second, 0, feat),
-            (enc_second, 0, feat),
-            (enc_first, 0, feat),
-            (dec_first, 0, feat),
+            grid_first,
+            grid_second,
+            dec_second,
+            dec_first,
+            mesh_first,
+            mesh_second,
+            enc_second,
+            enc_first,
+            dec_first,
             *saved,
         ],
-        [((width, feat), BF16)] * links
+        [((slots, feat), BF16)]
         + [((grid_count, feat), BF16)] * 4
         + [((mesh_count, feat), F32), ((mesh_count, feat), BF16), ((mesh_count, feat), BF16)],
         scratch=[
@@ -587,9 +595,8 @@
         ],
         flops=2 * feat * feat * (4 * spots + 3 * dec_count + 2 * enc_count),
     )
-    outgoing, results = results[:links], results[links:]
-    grid_out, grid_gpre, gpe, gpd, mesh_gin, mesh_gpre, mesh_pool = results
-    final = exchange(outgoing)
+    slot_back, grid_out, grid_gpre, gpe, gpd, mesh_gin, mesh_gpre, mesh_pool = results
+    final = lax.all_gather(slot_back, "tile", axis=0, tiled=True)
 
     def tail(
         cot_ref,
@@ -609,14 +616,14 @@
     ):
         base_ref[...] = (
             cot_ref[...].astype(F32)
-            + mm_t(grid_gpre_ref[...], grid_wn_ref[...])
-            + mm_t(gpe_ref[...], enc_wg_ref[...])
-            + mm_t(gpd_ref[...], dec_wg_ref[...])
+            + mm_t(grid_gpre_ref[...], grid_wn_ref[low, :])
+            + mm_t(gpe_ref[...], enc_wg_ref[low, :])
+            + mm_t(gpd_ref[...], dec_wg_ref[low, :])
         )
         grad_mesh_ref[...] = (
             mesh_gin_ref[...]
-            + mm_t(mesh_gpre_ref[...], mesh_wn_ref[...])
-            + mm_t(mesh_pool_ref[...], enc_wm_ref[...])
+            + mm_t(mesh_gpre_ref[...], mesh_wn_ref[low, :])
+            + mm_t(mesh_pool_ref[...], enc_wm_ref[high, :])
         )
 
     base, grad_mesh = call(
@@ -630,30 +637,46 @@
             mesh_gin,
             mesh_gpre,
             mesh_pool,
-            (grid_first, 0, feat),
-            (enc_first, 0, feat),
-            (dec_first, 0, feat),
-            (mesh_first, 0, feat),
-            (enc_first, feat, feat),
+            grid_first,
+            enc_first,
+            dec_first,
+            mesh_first,
+            enc_first,
         ],
         [((grid_count, feat), F32), ((mesh_count, feat), F32)],
         flops=2 * feat * feat * 3 * grid_count,
     )
 
-    def finish(*refs):
-        back_refs, (base_ref, select_t_ref, out_ref) = refs[:links], refs[links:]
-        back = [back_refs[reverse[j]] for j in range(links)]
-        out_ref[...] = base_ref[...] + mm(
-            select_t_ref[:, :slots], stack(back, slice(0, feat))
-        )
-
-    (grad_grid,) = call(
+    def finish(all_ref, base_ref, select_t_ref, out_ref, back_ref, semaphores):
+        own = lax.axis_index("tile")
+        copies = []
+        for j, offset in enumerate(offsets):
+            holder = lax.rem(own + (offset + peer_count), peer_count)
+            start = pl.multiple_of(holder * slots + j * width, width)
+            rows = pl.ds(j * width, width)
+            copies.append(
+                pltpu.make_async_copy(
+                    all_ref.at[pl.ds(start, width), :], back_ref.at[rows, :], semaphores.at[j]
+                )
+            )
+            copies[-1].start()
+        for copy in copies:
+            copy.wait()
+        out_ref[...] = base_ref[...] + mm(select_t_ref[:, :slots], back_ref[...])
+
+    grad_grid = pl.pallas_call(
         finish,
-        "add_returned",
-        [*final, base, select_t],
-        [((grid_count, feat), F32)],
-        flops=2 * grid_count * slots * feat,
-    )
+        name="add_returned",
+        in_specs=[
+            pl.BlockSpec(memory_space=pl.ANY),
+            pl.BlockSpec(memory_space=pltpu.VMEM),
+            pl.BlockSpec(memory_space=pltpu.VMEM),
+        ],
+        out_specs=pl.BlockSpec(memory_space=pltpu.VMEM),
+        out_shape=jax.ShapeDtypeStruct((grid_count, feat), F32),
+        scratch_shapes=[pltpu.VMEM((slots, feat), BF16), pltpu.SemaphoreType.DMA((links,))],
+        compiler_params=pltpu.CompilerParams(vmem_limit_bytes=VMEM_LIMIT),
+    )(final, base, select_t)
     return (grid_out, mesh_out, grad_grid, grad_mesh)
 
 

time: 77 us -> 121 us (1.57)
  waiting for transfers between devices: 9.37 us -> 35.3 us
  local copies, waits for them, and re-layouts: 14 us -> 30 us
  between operations: 0.96 us -> 14.3 us
  starting transfers between devices: 32 us -> 23.4 us
  Pallas kernels: 20.1 us -> 17.4 us
    all_gather x0 -> x1, waiting for transfers between devices: none -> 29.4 us  [per_device(): final = lax.all_gather(slot_back, 'tile', axis=0, tiled=True)]
    unnamed x44 -> x88, local copies, waits for them, and re-layouts: 11.3 us -> 30 us
    ppermute x27 -> x18, starting transfers between devices: 32 us -> 23.4 us  [exchange(): lax.ppermute(part, 'tile', [(s, (s + offset) % peer_count) for s in range...]
    pallas_call x7 -> x6, Pallas kernels: 20.1 us -> 16.1 us  [call(): pl.pallas_call(kernel, name=name, in_specs=specs, out_specs=[pl.BlockSpec...]
    ppermute x27 -> x18, waiting for transfers between devices: 9.37 us -> 5.91 us  [exchange(): lax.ppermute(part, 'tile', [(s, (s + offset) % peer_count) for s in range...]
    reshape x4 -> x0, local copies, waits for them, and re-layouts: 2.74 us -> none  [the longest x1 0.69 us: per_device(): dec_grid.reshape(1, -1)]
    pallas_call x0 -> x1, Pallas kernels: none -> 1.3 us  [per_device(): pl.pallas_call(finish, name='add_returned', in_specs=[pl.BlockSpec(memory...]
  transfers between devices with their start and end apart: 27 -> 19, of which waited for: 7 -> 5; matrix products, arithmetic and copies ran while one was open for 4% -> 0% of each run, Pallas kernels for 8% -> 5%
where the time goes in v2:
time: 121 us
  waiting for transfers between devices  35.3 us (29%)
  local copies, waits for them, and re-layouts  30 us (25%)
  starting transfers between devices  23.4 us (19%)
  Pallas kernels  17.4 us (14%)
  between operations  14.3 us (12%)
    unnamed x88, local copies, waits for them, and re-layouts  30 us
    all_gather x1, waiting for transfers between devices, per_device(): final = lax.all_gather(slot_back, 'tile', axis=0, tiled=True)  29.4 us
    ppermute x18, starting transfers between devices, exchange(): lax.ppermute(part, 'tile', [(s, (s + offset) % peer_count) for s in range...  23.4 us
    pallas_call x6, Pallas kernels, call(): pl.pallas_call(kernel, name=name, in_specs=specs, out_specs=[pl.BlockSpec...  16.1 us
    ppermute x18, waiting for transfers between devices, exchange(): lax.ppermute(part, 'tile', [(s, (s + offset) % peer_count) for s in range...  5.91 us
  transfers between devices with their start and end apart: 19, of which 5 were waited for; matrix products, arithmetic and copies ran while one was open for 0% of the time, Pallas kernels for 5%

profile of v2, /device:TPU:0, one launch (start us, length us, event | category | flops | bytes accessed | tf_op | source)
XLA Modules:
  0.0 120.5 jit_solution(1668097720224428627)
XLA Ops:
  11.6 2.6 %collective-permute-start.1 = (bf16[16,1024]{1,0:T(8,128)(2,1)S(1)}, bf16[16,1024]{1,0:T(8,128)(2,1)S(1)}, u32[]{:S(2)}, u32[]{:S(2)}) collective-permute-start(bf16[16,1024]{1,0:T(8,128)(2,1)S(1)} %get-tuple-element.53), channel_id=1, source_target_pairs={{0,4},{1,5},{2,6},{3,7},{4,8},{5,9},{6,10},{7,11},{8,12},{9,13},{1... | collective-permute-start | bytes 98312 | tf_op jit(solution)/shard_map/ppermute | solution.py:212
  14.3 2.5 %collective-permute-start.2 = (bf16[16,1024]{1,0:T(8,128)(2,1)S(1)}, bf16[16,1024]{1,0:T(8,128)(2,1)S(1)}, u32[]{:S(2)}, u32[]{:S(2)}) collective-permute-start(bf16[16,1024]{1,0:T(8,128)(2,1)S(1)} %get-tuple-element.54), channel_id=1, source_target_pairs={{0,5},{1,6},{2,7},{3,8},{4,9},{5,10},{6,11},{7,12},{8,13},{9,14},{... | collective-permute-start | bytes 98312 | tf_op jit(solution)/shard_map/ppermute | solution.py:212
  16.7 1.3 %collective-permute-start.3 = (bf16[16,1024]{1,0:T(8,128)(2,1)S(1)}, bf16[16,1024]{1,0:T(8,128)(2,1)S(1)}, u32[]{:S(2)}, u32[]{:S(2)}) collective-permute-start(bf16[16,1024]{1,0:T(8,128)(2,1)S(1)} %get-tuple-element.55), channel_id=1, source_target_pairs={{0,3},{1,4},{2,5},{3,6},{4,7},{5,8},{6,9},{7,10},{8,11},{9,12},{10... | collective-permute-start | bytes 98312 | tf_op jit(solution)/shard_map/ppermute | solution.py:212
  18.1 3.2 %collective-permute-start.4 = (bf16[16,1024]{1,0:T(8,128)(2,1)S(1)}, bf16[16,1024]{1,0:T(8,128)(2,1)S(1)}, u32[]{:S(2)}, u32[]{:S(2)}) collective-permute-start(bf16[16,1024]{1,0:T(8,128)(2,1)S(1)} %get-tuple-element.56), channel_id=1, source_target_pairs={{0,15},{1,0},{2,1},{3,2},{4,3},{5,4},{6,5},{7,6},{8,7},{9,8},{10,9... | collective-permute-start | bytes 98312 | tf_op jit(solution)/shard_map/ppermute | solution.py:212
  22.4 2.5 %collective-permute-start.8 = (bf16[16,1024]{1,0:T(8,128)(2,1)S(1)}, bf16[16,1024]{1,0:T(8,128)(2,1)S(1)}, u32[]{:S(2)}, u32[]{:S(2)}) collective-permute-start(bf16[16,1024]{1,0:T(8,128)(2,1)S(1)} %get-tuple-element.60), channel_id=1, source_target_pairs={{0,8},{1,9},{2,10},{3,11},{4,12},{5,13},{6,14},{7,15},{8,0},{9,1},... | collective-permute-start | bytes 98312 | tf_op jit(solution)/shard_map/ppermute | solution.py:212
  24.9 1.4 %copy-done = bf16[1536,512]{1,0:T(8,128)(2,1)S(1)} copy-done((bf16[1536,512]{1,0:T(8,128)(2,1)S(1)}, bf16[1536,512]{1,0:T(8,128)(2,1)}, u32[]{:S(2)}) %copy-start) | copy-done | bytes 1572888
  26.3 1.4 %copy-done.2 = bf16[1536,512]{1,0:T(8,128)(2,1)S(1)} copy-done((bf16[1536,512]{1,0:T(8,128)(2,1)S(1)}, bf16[1536,512]{1,0:T(8,128)(2,1)}, u32[]{:S(2)}) %copy-start.2) | copy-done | bytes 1572888
  27.7 1.2 %copy-done.4 = bf16[1024,512]{1,0:T(8,128)(2,1)S(1)} copy-done((bf16[1024,512]{1,0:T(8,128)(2,1)S(1)}, bf16[1024,512]{1,0:T(8,128)(2,1)}, u32[]{:S(2)}) %copy-start.4) | copy-done | bytes 1048600
  35.6 4.0 %local_products.1 = (bf16[256,256]{1,0:T(8,128)(2,1)S(1)}, f32[384,512]{1,0:T(8,128)S(1)}, f32[768,512]{1,0:T(8,128)S(1)}, f32[64,512]{1,0:T(8,128)S(1)}, bf16[3...) custom-call(bf16[256,256]{1,0:T(8,128)(2,1)S(1)} %get-tuple-element., ...), custom_call_target="tpu_custom_call" | custom-call | flops 1275068416 | bytes 9774080 | tf_op jit(solution)/shard_map/local_products/pallas_call | solution.py:160
  39.8 3.6 %edges_forward.1 = (bf16[16,1024]{1,0:T(8,128)(2,1)S(1)}, bf16[16,1024]{1,0:T(8,128)(2,1)S(1)}, bf16[16,1024]{1,0:T(8,128)(2,1)S(1)}, bf16[16,1024]{1,0:T(8,128)...) custom-call(bf16[16,1024]{1,0:T(8,128)(2,1)S(1)} %collective-permute, ...), custom_call_target="tpu_custom_call" | custom-call | flops 1207959552 | bytes 16421632 | tf_op jit(solution)/shard_map/edges_forward/pallas_call | solution.py:160
  43.5 1.6 %collective-permute-start.10 = (bf16[16,1024]{1,0:T(8,128)(2,1)S(1)}, bf16[16,1024]{1,0:T(8,128)(2,1)S(1)}, u32[]{:S(2)}, u32[]{:S(2)}) collective-permute-start(bf16[16,1024]{1,0:T(8,128)(2,1)S(1)} %get-tuple-element.70), channel_id=1, source_target_pairs={{0,4},{1,5},{2,6},{3,7},{4,8},{5,9},{6,10},{7,11},{8,12},{9,13},{1... | collective-permute-start | bytes 98312 | tf_op jit(solution)/shard_map/ppermute | solution.py:212
  45.1 1.5 %collective-permute-start.12 = (bf16[16,1024]{1,0:T(8,128)(2,1)S(1)}, bf16[16,1024]{1,0:T(8,128)(2,1)S(1)}, u32[]{:S(2)}, u32[]{:S(2)}) collective-permute-start(bf16[16,1024]{1,0:T(8,128)(2,1)S(1)} %get-tuple-element.72), channel_id=1, source_target_pairs={{0,3},{1,4},{2,5},{3,6},{4,7},{5,8},{6,9},{7,10},{8,11},{9,12},{10... | collective-permute-start | bytes 98312 | tf_op jit(solution)/shard_map/ppermute | solution.py:212
  46.6 1.5 %collective-permute-start.13 = (bf16[16,1024]{1,0:T(8,128)(2,1)S(1)}, bf16[16,1024]{1,0:T(8,128)(2,1)S(1)}, u32[]{:S(2)}, u32[]{:S(2)}) collective-permute-start(bf16[16,1024]{1,0:T(8,128)(2,1)S(1)} %get-tuple-element.73), channel_id=1, source_target_pairs={{0,15},{1,0},{2,1},{3,2},{4,3},{5,4},{6,5},{7,6},{8,7},{9,8},{10,9... | collective-permute-start | bytes 98312 | tf_op jit(solution)/shard_map/ppermute | solution.py:212
  48.2 2.0 %collective-permute-start.14 = (bf16[16,1024]{1,0:T(8,128)(2,1)S(1)}, bf16[16,1024]{1,0:T(8,128)(2,1)S(1)}, u32[]{:S(2)}, u32[]{:S(2)}) collective-permute-start(bf16[16,1024]{1,0:T(8,128)(2,1)S(1)} %get-tuple-element.74), channel_id=1, source_target_pairs={{0,12},{1,13},{2,14},{3,15},{4,0},{5,1},{6,2},{7,3},{8,4},{9,5},{1... | collective-permute-start | bytes 98312 | tf_op jit(solution)/shard_map/ppermute | solution.py:212
  51.8 1.6 %collective-permute-start.17 = (bf16[16,1024]{1,0:T(8,128)(2,1)S(1)}, bf16[16,1024]{1,0:T(8,128)(2,1)S(1)}, u32[]{:S(2)}, u32[]{:S(2)}) collective-permute-start(bf16[16,1024]{1,0:T(8,128)(2,1)S(1)} %get-tuple-element.77), channel_id=1, source_target_pairs={{0,8},{1,9},{2,10},{3,11},{4,12},{5,13},{6,14},{7,15},{8,0},{9,1},... | collective-permute-start | bytes 98312 | tf_op jit(solution)/shard_map/ppermute | solution.py:212
  54.1 3.1 %collective-permute-done.17.refs_17_ = bf16[16,1024]{1,0:T(8,128)(2,1)S(1)} collective-permute-done((bf16[16,1024]{1,0:T(8,128)(2,1)S(1)}, bf16[16,1024]{1,0:T(8,128)(2,1)S(1)}, u32[]{:S(2)}, u32[]{:S(2)}) %collective-permute-start.17) | collective-permute-done | bytes 32800 | tf_op jit(solution)/shard_map/ppermute | solution.py:212
  57.1 2.3 %collective-permute-done.9.refs_9_ = bf16[16,1024]{1,0:T(8,128)(2,1)S(1)} collective-permute-done((bf16[16,1024]{1,0:T(8,128)(2,1)S(1)}, bf16[16,1024]{1,0:T(8,128)(2,1)S(1)}, u32[]{:S(2)}, u32[]{:S(2)}) %collective-permute-start.9) | collective-permute-done | bytes 32800 | tf_op jit(solution)/shard_map/ppermute | solution.py:212
  59.4 5.9 %edges_backward.1 = (bf16[144,512]{1,0:T(8,128)(2,1)S(1)}, bf16[256,512]{1,0:T(8,128)(2,1)}, bf16[256,512]{1,0:T(8,128)(2,1)S(1)}, bf16[256,512]{1,0:T(8,128)(2,...) custom-call(bf16[16,1024]{1,0:T(8,128)(2,1)S(1)} %collective-permute, ...), custom_call_target="tpu_custom_call" | custom-call | flops 2449473536 | bytes 18240256 | tf_op jit(solution)/shard_map/edges_backward/pallas_call | solution.py:160
  70.0 1.2 %copy-done.6 = bf16[1024,512]{1,0:T(8,128)(2,1)S(1)} copy-done((bf16[1024,512]{1,0:T(8,128)(2,1)S(1)}, bf16[1024,512]{1,0:T(8,128)(2,1)}, u32[]{:S(2)}) %copy-start.6) | copy-done | bytes 1048600
  71.3 1.2 %copy-done.8 = bf16[1024,512]{1,0:T(8,128)(2,1)S(1)} copy-done((bf16[1024,512]{1,0:T(8,128)(2,1)S(1)}, bf16[1024,512]{1,0:T(8,128)(2,1)}, u32[]{:S(2)}) %copy-start.8) | copy-done | bytes 1048600
  78.0 1.5 %local_gradients.1 = (f32[256,512]{1,0:T(8,128)S(1)}, f32[64,512]{1,0:T(8,128)}) custom-call(bf16[256,512]{1,0:T(8,128)(2,1)S(1)} %copy-done.13, bf16[256,512]{1,0:T(8,128)(2,1)S(1)} %copy-done.25, bf16[256,512]{1,0:T(8,128)(2,1)S(1)} %copy-done.27, bf16[256,512]{1,0:T(8,128)(2,1)S(1)} %copy-done.29, f32[64,512]{1,0:T(8,128)S(1)} %copy-done.32, ...), custom_call_target="tpu_custom_call" | custom-call | flops 402653184 | bytes 8781824 | tf_op jit(solution)/shard_map/local_gradients/pallas_call | solution.py:160
  80.3 29.4 %all-gather.2.cloned.1.call-done.all_ref = bf16[2304,512]{1,0:T(8,128)(2,1)} async-done(((bf16[144,512]{1,0:T(8,128)(2,1)}), bf16[2304,512]{1,0:T(8,128)(2,1)}) %all-gather.2.cloned.1.call-update) | async-done | bytes 2359312 | tf_op jit(solution)/shard_map/all_gather | solution.py:599
  109.7 1.7 %copy-done.14 = bf16[2304,512]{1,0:T(8,128)(2,1)S(1)} copy-done((bf16[2304,512]{1,0:T(8,128)(2,1)S(1)}, bf16[2304,512]{1,0:T(8,128)(2,1)}, u32[]{:S(2)}) %copy-start.14) | copy-done | bytes 2359320
  112.4 1.3 %add_returned.1 = f32[256,512]{1,0:T(8,128)} custom-call(bf16[2304,512]{1,0:T(8,128)(2,1)S(1)} %copy-done.14, f32[256,512]{1,0:T(8,128)S(1)} %copy-done.21, bf16[256,256]{1,0:T(8,128)(2,1)S(1)} %get-tuple-element.79.refs_20_.select_t_ref), custom_call_target="tpu_custom_call" | custom-call | tf_op jit(solution)/shard_map/add_returned/pallas_call | solution.py:667
  (110 shorter events, 26.6 us)
Async XLA Ops:
  7.2 102.5 %all-gather.2.cloned.1.call-start = ((), (), s32[]{:S(2)}) async-start(), calls=%async_computation | async-start | bytes 2506752 | tf_op jit(solution)/shard_map/all_gather | solution.py:599
  11.1 10.1 %collective-permute-start = (bf16[16,1024]{1,0:T(8,128)(2,1)S(1)}, bf16[16,1024]{1,0:T(8,128)(2,1)S(1)}, u32[]{:S(2)}, u32[]{:S(2)}) collective-permute-start(bf16[16,1024]{1,0:T(8,128)(2,1)S(1)} %get-tuple-element.52), channel_id=1, source_target_pairs={{0,1},{1,2},{2,3},{3,4},{4,5},{5,6},{6,7},{7,8},{8,9},{9,10},{10,1... | collective-permute-start | bytes 98312 | tf_op jit(solution)/shard_map/ppermute | solution.py:212
  11.6 10.1 %collective-permute-start.1 = (bf16[16,1024]{1,0:T(8,128)(2,1)S(1)}, bf16[16,1024]{1,0:T(8,128)(2,1)S(1)}, u32[]{:S(2)}, u32[]{:S(2)}) collective-permute-start(bf16[16,1024]{1,0:T(8,128)(2,1)S(1)} %get-tuple-element.53), channel_id=1, source_target_pairs={{0,4},{1,5},{2,6},{3,7},{4,8},{5,9},{6,10},{7,11},{8,12},{9,13},{1... | collective-permute-start | bytes 98312 | tf_op jit(solution)/shard_map/ppermute | solution.py:212
  14.3 7.4 %collective-permute-start.2 = (bf16[16,1024]{1,0:T(8,128)(2,1)S(1)}, bf16[16,1024]{1,0:T(8,128)(2,1)S(1)}, u32[]{:S(2)}, u32[]{:S(2)}) collective-permute-start(bf16[16,1024]{1,0:T(8,128)(2,1)S(1)} %get-tuple-element.54), channel_id=1, source_target_pairs={{0,5},{1,6},{2,7},{3,8},{4,9},{5,10},{6,11},{7,12},{8,13},{9,14},{... | collective-permute-start | bytes 98312 | tf_op jit(solution)/shard_map/ppermute | solution.py:212
  16.7 5.7 %collective-permute-start.3 = (bf16[16,1024]{1,0:T(8,128)(2,1)S(1)}, bf16[16,1024]{1,0:T(8,128)(2,1)S(1)}, u32[]{:S(2)}, u32[]{:S(2)}) collective-permute-start(bf16[16,1024]{1,0:T(8,128)(2,1)S(1)} %get-tuple-element.55), channel_id=1, source_target_pairs={{0,3},{1,4},{2,5},{3,6},{4,7},{5,8},{6,9},{7,10},{8,11},{9,12},{10... | collective-permute-start | bytes 98312 | tf_op jit(solution)/shard_map/ppermute | solution.py:212
  18.1 21.6 %collective-permute-start.4 = (bf16[16,1024]{1,0:T(8,128)(2,1)S(1)}, bf16[16,1024]{1,0:T(8,128)(2,1)S(1)}, u32[]{:S(2)}, u32[]{:S(2)}) collective-permute-start(bf16[16,1024]{1,0:T(8,128)(2,1)S(1)} %get-tuple-element.56), channel_id=1, source_target_pairs={{0,15},{1,0},{2,1},{3,2},{4,3},{5,4},{6,5},{7,6},{8,7},{9,8},{10,9... | collective-permute-start | bytes 98312 | tf_op jit(solution)/shard_map/ppermute | solution.py:212
  21.3 18.4 %collective-permute-start.5 = (bf16[16,1024]{1,0:T(8,128)(2,1)S(1)}, bf16[16,1024]{1,0:T(8,128)(2,1)S(1)}, u32[]{:S(2)}, u32[]{:S(2)}) collective-permute-start(bf16[16,1024]{1,0:T(8,128)(2,1)S(1)} %get-tuple-element.57), channel_id=1, source_target_pairs={{0,12},{1,13},{2,14},{3,15},{4,0},{5,1},{6,2},{7,3},{8,4},{9,5},{1... | collective-permute-start | bytes 98312 | tf_op jit(solution)/shard_map/ppermute | solution.py:212
  21.7 18.0 %collective-permute-start.6 = (bf16[16,1024]{1,0:T(8,128)(2,1)S(1)}, bf16[16,1024]{1,0:T(8,128)(2,1)S(1)}, u32[]{:S(2)}, u32[]{:S(2)}) collective-permute-start(bf16[16,1024]{1,0:T(8,128)(2,1)S(1)} %get-tuple-element.58), channel_id=1, source_target_pairs={{0,11},{1,12},{2,13},{3,14},{4,15},{5,0},{6,1},{7,2},{8,3},{9,4},{... | collective-permute-start | bytes 98312 | tf_op jit(solution)/shard_map/ppermute | solution.py:212
  21.7 18.0 %collective-permute-start.7 = (bf16[16,1024]{1,0:T(8,128)(2,1)S(1)}, bf16[16,1024]{1,0:T(8,128)(2,1)S(1)}, u32[]{:S(2)}, u32[]{:S(2)}) collective-permute-start(bf16[16,1024]{1,0:T(8,128)(2,1)S(1)} %get-tuple-element.59), channel_id=1, source_target_pairs={{0,13},{1,14},{2,15},{3,0},{4,1},{5,2},{6,3},{7,4},{8,5},{9,6},{10... | collective-permute-start | bytes 98312 | tf_op jit(solution)/shard_map/ppermute | solution.py:212
  22.4 17.3 %collective-permute-start.8 = (bf16[16,1024]{1,0:T(8,128)(2,1)S(1)}, bf16[16,1024]{1,0:T(8,128)(2,1)S(1)}, u32[]{:S(2)}, u32[]{:S(2)}) collective-permute-start(bf16[16,1024]{1,0:T(8,128)(2,1)S(1)} %get-tuple-element.60), channel_id=1, source_target_pairs={{0,8},{1,9},{2,10},{3,11},{4,12},{5,13},{6,14},{7,15},{8,0},{9,1},... | collective-permute-start | bytes 98312 | tf_op jit(solution)/shard_map/ppermute | solution.py:212
  39.8 13.6 %copy-start.7 = (bf16[1024,512]{1,0:T(8,128)(2,1)S(1)}, bf16[1024,512]{1,0:T(8,128)(2,1)}, u32[]{:S(2)}) copy-start(bf16[1024,512]{1,0:T(8,128)(2,1)} %refs_7_.3) | copy-start | bytes 3145732
  43.4 16.0 %copy-start.3 = (bf16[1536,512]{1,0:T(8,128)(2,1)S(1)}, bf16[1536,512]{1,0:T(8,128)(2,1)}, u32[]{:S(2)}) copy-start(bf16[1536,512]{1,0:T(8,128)(2,1)} %refs_11_.3) | copy-start | bytes 4718596
  43.4 16.0 %copy-start.13 = (bf16[256,512]{1,0:T(8,128)(2,1)S(1)}, bf16[256,512]{1,0:T(8,128)(2,1)}, u32[]{:S(2)}) copy-start(bf16[256,512]{1,0:T(8,128)(2,1)} %refs_0_.3) | copy-start | bytes 786436
  43.5 15.9 %copy-start.19 = (bf16[512,512]{1,0:T(8,128)(2,1)S(1)}, bf16[512,512]{1,0:T(8,128)(2,1)}, u32[]{:S(2)}) copy-start(bf16[512,512]{1,0:T(8,128)(2,1)} %refs_29_.1) | copy-start | bytes 1572868
  43.5 15.9 %copy-start.33 = (bf16[64,512]{1,0:T(8,128)(2,1)S(1)}, bf16[64,512]{1,0:T(8,128)(2,1)}, u32[]{:S(2)}) copy-start(bf16[64,512]{1,0:T(8,128)(2,1)} %refs_23_.3) | copy-start | bytes 196612
  43.5 6.7 %collective-permute-start.10 = (bf16[16,1024]{1,0:T(8,128)(2,1)S(1)}, bf16[16,1024]{1,0:T(8,128)(2,1)S(1)}, u32[]{:S(2)}, u32[]{:S(2)}) collective-permute-start(bf16[16,1024]{1,0:T(8,128)(2,1)S(1)} %get-tuple-element.70), channel_id=1, source_target_pairs={{0,4},{1,5},{2,6},{3,7},{4,8},{5,9},{6,10},{7,11},{8,12},{9,13},{1... | collective-permute-start | bytes 98312 | tf_op jit(solution)/shard_map/ppermute | solution.py:212
  45.1 5.6 %collective-permute-start.11 = (bf16[16,1024]{1,0:T(8,128)(2,1)S(1)}, bf16[16,1024]{1,0:T(8,128)(2,1)S(1)}, u32[]{:S(2)}, u32[]{:S(2)}) collective-permute-start(bf16[16,1024]{1,0:T(8,128)(2,1)S(1)} %get-tuple-element.71), channel_id=1, source_target_pairs={{0,5},{1,6},{2,7},{3,8},{4,9},{5,10},{6,11},{7,12},{8,13},{9,14},{... | collective-permute-start | bytes 98312 | tf_op jit(solution)/shard_map/ppermute | solution.py:212
  45.1 6.6 %collective-permute-start.12 = (bf16[16,1024]{1,0:T(8,128)(2,1)S(1)}, bf16[16,1024]{1,0:T(8,128)(2,1)S(1)}, u32[]{:S(2)}, u32[]{:S(2)}) collective-permute-start(bf16[16,1024]{1,0:T(8,128)(2,1)S(1)} %get-tuple-element.72), channel_id=1, source_target_pairs={{0,3},{1,4},{2,5},{3,6},{4,7},{5,8},{6,9},{7,10},{8,11},{9,12},{10... | collective-permute-start | bytes 98312 | tf_op jit(solution)/shard_map/ppermute | solution.py:212
  46.6 6.7 %collective-permute-start.13 = (bf16[16,1024]{1,0:T(8,128)(2,1)S(1)}, bf16[16,1024]{1,0:T(8,128)(2,1)S(1)}, u32[]{:S(2)}, u32[]{:S(2)}) collective-permute-start(bf16[16,1024]{1,0:T(8,128)(2,1)S(1)} %get-tuple-element.73), channel_id=1, source_target_pairs={{0,15},{1,0},{2,1},{3,2},{4,3},{5,4},{6,5},{7,6},{8,7},{9,8},{10,9... | collective-permute-start | bytes 98312 | tf_op jit(solution)/shard_map/ppermute | solution.py:212
  48.2 5.6 %collective-permute-start.14 = (bf16[16,1024]{1,0:T(8,128)(2,1)S(1)}, bf16[16,1024]{1,0:T(8,128)(2,1)S(1)}, u32[]{:S(2)}, u32[]{:S(2)}) collective-permute-start(bf16[16,1024]{1,0:T(8,128)(2,1)S(1)} %get-tuple-element.74), channel_id=1, source_target_pairs={{0,12},{1,13},{2,14},{3,15},{4,0},{5,1},{6,2},{7,3},{8,4},{9,5},{1... | collective-permute-start | bytes 98312 | tf_op jit(solution)/shard_map/ppermute | solution.py:212
  50.1 3.6 %collective-permute-start.15 = (bf16[16,1024]{1,0:T(8,128)(2,1)S(1)}, bf16[16,1024]{1,0:T(8,128)(2,1)S(1)}, u32[]{:S(2)}, u32[]{:S(2)}) collective-permute-start(bf16[16,1024]{1,0:T(8,128)(2,1)S(1)} %get-tuple-element.75), channel_id=1, source_target_pairs={{0,11},{1,12},{2,13},{3,14},{4,15},{5,0},{6,1},{7,2},{8,3},{9,4},{... | collective-permute-start | bytes 98312 | tf_op jit(solution)/shard_map/ppermute | solution.py:212
  50.7 3.3 %collective-permute-start.16 = (bf16[16,1024]{1,0:T(8,128)(2,1)S(1)}, bf16[16,1024]{1,0:T(8,128)(2,1)S(1)}, u32[]{:S(2)}, u32[]{:S(2)}) collective-permute-start(bf16[16,1024]{1,0:T(8,128)(2,1)S(1)} %get-tuple-element.76), channel_id=1, source_target_pairs={{0,13},{1,14},{2,15},{3,0},{4,1},{5,2},{6,3},{7,4},{8,5},{9,6},{10... | collective-permute-start | bytes 98312 | tf_op jit(solution)/shard_map/ppermute | solution.py:212
  51.8 5.4 %collective-permute-start.17 = (bf16[16,1024]{1,0:T(8,128)(2,1)S(1)}, bf16[16,1024]{1,0:T(8,128)(2,1)S(1)}, u32[]{:S(2)}, u32[]{:S(2)}) collective-permute-start(bf16[16,1024]{1,0:T(8,128)(2,1)S(1)} %get-tuple-element.77), channel_id=1, source_target_pairs={{0,8},{1,9},{2,10},{3,11},{4,12},{5,13},{6,14},{7,15},{8,0},{9,1},... | collective-permute-start | bytes 98312 | tf_op jit(solution)/shard_map/ppermute | solution.py:212
  53.4 6.0 %collective-permute-start.9 = (bf16[16,1024]{1,0:T(8,128)(2,1)S(1)}, bf16[16,1024]{1,0:T(8,128)(2,1)S(1)}, u32[]{:S(2)}, u32[]{:S(2)}) collective-permute-start(bf16[16,1024]{1,0:T(8,128)(2,1)S(1)} %get-tuple-element.69), channel_id=1, source_target_pairs={{0,1},{1,2},{2,3},{3,4},{4,5},{5,6},{6,7},{7,8},{8,9},{9,10},{10,1... | collective-permute-start | bytes 98312 | tf_op jit(solution)/shard_map/ppermute | solution.py:212
  (39 other events, 64.1 us)
Sparse Core Ops, SparseCore 0:
  70.2 39.4 all-gather.1

commit v3 on v2

--- a/solution.py
+++ b/solution.py
@@ -68,10 +68,6 @@
 def times_slope(raw, slope_ref, out_ref):
     for rows in row_chunks(out_ref.shape[0]):
         out_ref[rows, :] = (raw[rows, :] * slope_ref[rows, :].astype(F32)).astype(BF16)
-
-
-def stack(refs, columns):
-    return jnp.concatenate([ref[:, columns] for ref in refs], axis=0)
 
 
 def neighbour_offsets(peer_count):
@@ -120,6 +116,7 @@
     for place, entry in enumerate(inputs):
         if isinstance(entry, tuple):
             array, first, rows = entry
+            array = pltpu.with_memory_space_constraint(array, pltpu.HBM)
             specs.append(pl.BlockSpec(memory_space=pltpu.HBM))
             shape = (rows,) + array.shape[1:]
             fetches.append((place, first, rows, shape, array.dtype))
@@ -207,11 +204,91 @@
     low, high = slice(0, feat), slice(feat, 2 * feat)
     mesh_rows = slice(spots, spots + mesh_count)
 
+    one, four, five, three = range(half)
+    minus = [j + half for j in range(half)]
+    across = links - 1
+    peers = range(peer_count)
+
+    def permute(part, even_step, odd_step):
+        steps = (even_step, odd_step)
+        return lax.ppermute(part, "tile", [(s, (s + steps[s % 2]) % peer_count) for s in peers])
+
     def exchange(parts):
+        plus_two, minus_two, own_chip, plus_one, minus_one, three_off, opposite = parts
+        plus_two = permute(plus_two, 4, 4)
+        minus_two = permute(minus_two, -4, -4)
+        own_chip = permute(own_chip, 1, -1)
+        plus_one = permute(plus_one, 3, 1)
+        minus_one = permute(minus_one, -1, -3)
+        three_off = permute(three_off, -5, 5)
+        opposite = permute(opposite, peer_count // 2, peer_count // 2)
+        plus_passed = permute(plus_two, 1, -1)
+        minus_passed = permute(minus_two, 1, -1)
         return [
-            lax.ppermute(part, "tile", [(s, (s + offset) % peer_count) for s in range(peer_count)])
-            for part, offset in zip(parts, offsets)
+            plus_two,
+            minus_two,
+            own_chip,
+            plus_one,
+            minus_one,
+            three_off,
+            opposite,
+            plus_passed,
+            minus_passed,
         ]
+
+    def sent_shapes(columns):
+        rows = (2, 2, 1, 1, 1, 1, 1)
+        return [((count * width, columns), BF16) for count in rows]
+
+    sent_count = len(sent_shapes(feat))
+
+    def is_odd():
+        return lax.rem(lax.axis_index("tile"), 2) == 1
+
+    def send(refs, message, columns=slice(None)):
+        odd = is_odd()
+
+        def by_parity(even, odd_one):
+            return jnp.where(odd, message(odd_one), message(even))
+
+        plus_two, minus_two, own_chip, plus_one, minus_one, three_off, opposite = refs
+        plus_two[:width, columns] = message(four)
+        plus_two[width:, columns] = by_parity(five, three)
+        minus_two[:width, columns] = message(minus[four])
+        minus_two[width:, columns] = by_parity(minus[three], minus[five])
+        own_chip[:, columns] = by_parity(one, minus[one])
+        plus_one[:, columns] = by_parity(three, one)
+        minus_one[:, columns] = by_parity(minus[one], minus[three])
+        three_off[:, columns] = by_parity(minus[five], five)
+        opposite[:, columns] = message(across)
+
+    def receive(refs, columns=slice(None)):
+        odd = is_odd()
+        plus_two, minus_two, own_chip, plus_one, minus_one, three_off, opposite = refs[:7]
+        plus_passed, minus_passed = refs[7:]
+        first, second = slice(0, width), slice(width, 2 * width)
+        own = own_chip[:, columns]
+        near_plus, near_minus = plus_one[:, columns], minus_one[:, columns]
+        far = three_off[:, columns]
+        passed_plus, passed_minus = plus_passed[second, columns], minus_passed[second, columns]
+        slot_rows = [None] * links
+        slot_rows[one] = jnp.where(odd, own, near_plus)
+        slot_rows[minus[one]] = jnp.where(odd, near_minus, own)
+        slot_rows[three] = jnp.where(odd, near_plus, passed_plus)
+        slot_rows[minus[three]] = jnp.where(odd, passed_minus, near_minus)
+        slot_rows[five] = jnp.where(odd, passed_plus, far)
+        slot_rows[minus[five]] = jnp.where(odd, far, passed_minus)
+        slot_rows[four] = plus_two[first, columns]
+        slot_rows[minus[four]] = minus_two[first, columns]
+        slot_rows[across] = opposite[:, columns]
+        return slot_rows
+
+    def by_slot(refs, columns=slice(None)):
+        return jnp.concatenate(receive(refs, columns), axis=0)
+
+    def by_row(refs, columns=slice(None)):
+        slot_rows = receive(refs, columns)
+        return jnp.concatenate([slot_rows[reverse[j]] for j in range(links)], axis=0)
 
     def pack(index_ref, count_ref, nodes_ref, cot_ref, select_ref, *out_refs):
         def column(row):
@@ -236,10 +313,8 @@
         select_ref[slots:, :] = jnp.zeros((slots_pad - slots, grid_count), BF16)
         sent_nodes = mm(select, nodes_ref[...]).astype(BF16)
         sent_cot = mm(select, cot_ref[...]).astype(BF16)
-        for j, out_ref in enumerate(out_refs):
-            rows = slice(j * width, (j + 1) * width)
-            out_ref[:, low] = sent_nodes[rows, :]
-            out_ref[:, high] = sent_cot[rows, :]
+        send(out_refs, lambda j: sent_nodes[j * width : (j + 1) * width, :], low)
+        send(out_refs, lambda j: sent_cot[j * width : (j + 1) * width, :], high)
 
     select, *outgoing = call(
         pack,
@@ -250,7 +325,7 @@
             (grid_nodes, 0, grid_count),
             (grid_cot, 0, grid_count),
         ],
-        [((slots_pad, grid_count), BF16)] + [((width, 2 * feat), BF16)] * links,
+        [((slots_pad, grid_count), BF16)] + sent_shapes(2 * feat),
         flops=4 * slots * grid_count * feat,
     )
     arrived = exchange(outgoing)
@@ -350,7 +425,7 @@
             dec_w2_ref,
         ) = refs[:16]
         refs = refs[16:]
-        out_refs, refs = refs[:links], refs[links:]
+        out_refs, refs = refs[:sent_count], refs[sent_count:]
         (
             mesh_out_ref,
             spot_ref,
@@ -368,7 +443,7 @@
             mesh_act_ref,
             table_ref,
         ) = refs
-        rows = stack(arrived_refs, low)
+        rows = by_slot(arrived_refs, low)
         pe = mm(rows, enc_wg_ref[low, :]).astype(BF16)
         pre = enc_part_ref[...] + mm(enc_pick_ref[:, grid_count:spots], pe)
         activate(pre, enc_act_ref, enc_slope_ref)
@@ -388,10 +463,11 @@
         norm_forward(mm(dec_act_ref[...], dec_w2_ref[...]), dec_normed_ref, dec_scale_ref)
         spot_ref[...] = mm(dec_pool_ref[:spots, :], dec_normed_ref[...])
         shared = mm(select_ref[:slots, :], spot_ref[:grid_count, :].astype(BF16)).astype(BF16)
-        for j, out_ref in enumerate(out_refs):
-            start = grid_count + reverse[j] * width
-            out_ref[:, low] = spot_ref[start : start + width, :].astype(BF16)
-            out_ref[:, high] = shared[j * width : (j + 1) * width, :]
+        slot_msg = spot_ref[grid_count:, :].astype(BF16)
+        send(
+            out_refs, lambda j: slot_msg[reverse[j] * width : (reverse[j] + 1) * width, :], low
+        )
+        send(out_refs, lambda j: shared[j * width : (j + 1) * width, :], high)
 
     edge_saved = [
         ((enc_count, feat), BF16),
@@ -426,7 +502,7 @@
             dec_first,
             dec_second,
         ],
-        [((width, 2 * feat), BF16)] * links
+        sent_shapes(2 * feat)
         + [((mesh_count, feat), BF16), ((spots, feat), F32)]
         + edge_saved,
         scratch=[
@@ -437,14 +513,14 @@
         ],
         flops=2 * feat * feat * 2 * (enc_count + dec_count),
     )
-    outgoing, results = results[:links], results[links:]
+    outgoing, results = results[:sent_count], results[sent_count:]
     mesh_out, spot_msg, *saved = results
     returned = exchange(outgoing)
 
     def node_part(*refs):
         arrived_refs, (nodes_ref, weight_ref, out_ref) = refs[:links], refs[links:]
         out_ref[:grid_count, :] = mm(nodes_ref[...], weight_ref[low, :])
-        out_ref[grid_count:, :] = mm(stack(arrived_refs, low), weight_ref[low, :])
+        out_ref[grid_count:, :] = mm(by_slot(arrived_refs, low), weight_ref[low, :])
 
     (grid_part,) = call(
         node_part,
@@ -487,8 +563,8 @@
             mesh_slope_ref,
         ) = refs[:28]
         refs = refs[28:]
+        out_refs, refs = refs[:sent_count], refs[sent_count:]
         (
-            slot_back_ref,
             grid_out_ref,
             grid_gpre_ref,
             gpe_ref,
@@ -508,12 +584,11 @@
             mesh_gout_ref,
             enc_gout_ref,
         ) = refs
-        back = [returned_refs[reverse[j]] for j in range(links)]
         agg_ref[:grid_count, :] = (
-            spot_ref[:grid_count, :] + mm(select_t_ref[:, :slots], stack(back, low))
+            spot_ref[:grid_count, :] + mm(select_t_ref[:, :slots], by_row(returned_refs, low))
         ).astype(BF16)
         agg_ref[grid_count:, :] = (
-            spot_ref[grid_count:, :] + stack(returned_refs, high).astype(F32)
+            spot_ref[grid_count:, :] + by_slot(returned_refs, high).astype(F32)
         ).astype(BF16)
         activate(
             grid_part_ref[...] + mm(agg_ref[...], grid_wa_ref[high, :]), grid_act_ref, grid_slope_ref
@@ -522,7 +597,7 @@
         grid_out_ref[...] = (
             nodes_ref[...].astype(F32) + grid_normed_ref[:grid_count, :]
         ).astype(BF16)
-        cot = jnp.concatenate([cot_ref[...], stack(arrived_refs, high)], axis=0)
+        cot = jnp.concatenate([cot_ref[...], by_slot(arrived_refs, high)], axis=0)
         norm_backward(grid_normed_ref, grid_scale_ref, cot, grid_gout_ref)
         times_slope(mm_t(grid_gout_ref[...], grid_w2_ref[...]), grid_slope_ref, grid_gall_ref)
         grid_gpre_ref[...] = grid_gall_ref[:grid_count, :]
@@ -548,7 +623,7 @@
         gpe_ref[...] = pooled[:grid_count, :]
         mesh_pool_ref[...] = pooled[mesh_rows, :]
         slot_back = (slot_back + mm_t(pooled[grid_count:spots, :], enc_wg_ref[low, :])).astype(BF16)
-        slot_back_ref[...] = slot_back
+        send(out_refs, lambda j: slot_back[reverse[j] * width : (reverse[j] + 1) * width, :])
 
     results = call(
         backward,
@@ -577,7 +652,7 @@
             dec_first,
             *saved,
         ],
-        [((slots, feat), BF16)]
+        sent_shapes(feat)
         + [((grid_count, feat), BF16)] * 4
         + [((mesh_count, feat), F32), ((mesh_count, feat), BF16), ((mesh_count, feat), BF16)],
         scratch=[
@@ -595,8 +670,9 @@
         ],
         flops=2 * feat * feat * (4 * spots + 3 * dec_count + 2 * enc_count),
     )
-    slot_back, grid_out, grid_gpre, gpe, gpd, mesh_gin, mesh_gpre, mesh_pool = results
-    final = lax.all_gather(slot_back, "tile", axis=0, tiled=True)
+    outgoing, results = results[:sent_count], results[sent_count:]
+    grid_out, grid_gpre, gpe, gpd, mesh_gin, mesh_gpre, mesh_pool = results
+    final = exchange(outgoing)
 
     def tail(
         cot_ref,
@@ -647,36 +723,17 @@
         flops=2 * feat * feat * 3 * grid_count,
     )
 
-    def finish(all_ref, base_ref, select_t_ref, out_ref, back_ref, semaphores):
-        own = lax.axis_index("tile")
-        copies = []
-        for j, offset in enumerate(offsets):
-            holder = lax.rem(own + (offset + peer_count), peer_count)
-            start = pl.multiple_of(holder * slots + j * width, width)
-            rows = pl.ds(j * width, width)
-            copies.append(
-                pltpu.make_async_copy(
-                    all_ref.at[pl.ds(start, width), :], back_ref.at[rows, :], semaphores.at[j]
-                )
-            )
-            copies[-1].start()
-        for copy in copies:
-            copy.wait()
-        out_ref[...] = base_ref[...] + mm(select_t_ref[:, :slots], back_ref[...])
-
-    grad_grid = pl.pallas_call(
+    def finish(*refs):
+        back_refs, (base_ref, select_t_ref, out_ref) = refs[:links], refs[links:]
+        out_ref[...] = base_ref[...] + mm(select_t_ref[:, :slots], by_row(back_refs))
+
+    (grad_grid,) = call(
         finish,
-        name="add_returned",
-        in_specs=[
-            pl.BlockSpec(memory_space=pl.ANY),
-            pl.BlockSpec(memory_space=pltpu.VMEM),
-            pl.BlockSpec(memory_space=pltpu.VMEM),
-        ],
-        out_specs=pl.BlockSpec(memory_space=pltpu.VMEM),
-        out_shape=jax.ShapeDtypeStruct((grid_count, feat), F32),
-        scratch_shapes=[pltpu.VMEM((slots, feat), BF16), pltpu.SemaphoreType.DMA((links,))],
-        compiler_params=pltpu.CompilerParams(vmem_limit_bytes=VMEM_LIMIT),
-    )(final, base, select_t)
+        "add_returned",
+        [*final, base, select_t],
+        [((grid_count, feat), F32)],
+        flops=2 * grid_count * slots * feat,
+    )
     return (grid_out, mesh_out, grad_grid, grad_mesh)
 
 

time: 121 us -> 62.1 us (0.51)
  local copies, waits for them, and re-layouts: 30 us -> 0.07 us
  waiting for transfers between devices: 35.3 us -> 11.3 us
  between operations: 14.3 us -> 0.91 us
  starting transfers between devices: 23.4 us -> 30.1 us
  Pallas kernels: 17.4 us -> 19.6 us
    unnamed x88 -> x24, local copies, waits for them, and re-layouts: 30 us -> 0.07 us
    all_gather x1 -> x0, waiting for transfers between devices: 29.4 us -> none  [per_device(): final = lax.all_gather(slot_back, 'tile', axis=0, tiled=True)]
    ppermute x18 -> x27, starting transfers between devices: 23.4 us -> 30.1 us  [permute(): lax.ppermute(part, 'tile', [(s, (s + steps[s % 2]) % peer_count) for s in...]
    ppermute x18 -> x27, waiting for transfers between devices: 5.91 us -> 11.3 us  [permute(): lax.ppermute(part, 'tile', [(s, (s + steps[s % 2]) % peer_count) for s in...]
    pallas_call x6 -> x7, Pallas kernels: 16.1 us -> 19.6 us  [call(): pl.pallas_call(kernel, name=name, in_specs=specs, out_specs=[pl.BlockSpec...]
    pallas_call x1 -> x0, Pallas kernels: 1.3 us -> none  [per_device(): pl.pallas_call(finish, name='add_returned', in_specs=[pl.BlockSpec(memory...]
  transfers between devices with their start and end apart: 19 -> 27, of which waited for: 5 -> 8; matrix products, arithmetic and copies ran while one was open for 0% -> 0% of each run, Pallas kernels for 5% -> 12%
where the time goes in v3:
time: 62.1 us; the launch traced here: 61.9 us
  starting transfers between devices  30.1 us (48%)
  Pallas kernels  19.6 us (32%)
  waiting for transfers between devices  11.3 us (18%)
  between operations  0.91 us (1%)
    ppermute x27, starting transfers between devices, permute(): lax.ppermute(part, 'tile', [(s, (s + steps[s % 2]) % peer_count) for s in...  30.1 us
    pallas_call x7, Pallas kernels, call(): pl.pallas_call(kernel, name=name, in_specs=specs, out_specs=[pl.BlockSpec...  19.6 us
    ppermute x27, waiting for transfers between devices, permute(): lax.ppermute(part, 'tile', [(s, (s + steps[s % 2]) % peer_count) for s in...  11.3 us
  transfers between devices with their start and end apart: 27, of which 8 were waited for; matrix products, arithmetic and copies ran while one was open for 0% of the time, Pallas kernels for 12%

profile of v3, /device:TPU:0, one launch (start us, length us, event | category | flops | bytes accessed | tf_op | source)
XLA Modules:
  0.0 61.9 jit_solution(8493517602589178857)
XLA Ops:
  0.6 1.4 %pack_rows.1 = (bf16[256,256]{1,0:T(8,128)(2,1)S(1)}, bf16[32,1024]{1,0:T(8,128)(2,1)S(1)}, bf16[32,1024]{1,0:T(8,128)(2,1)S(1)}, bf16[16,1024]{1,0:T(8,128)(2,1...) custom-call(s32[9,16]{1,0:T(8,128)} %refs_0_.2, ...), custom_call_target="tpu_custom_call" | custom-call | flops 75497472 | bytes 950884 | tf_op jit(solution)/shard_map/pack_rows/pallas_call | solution.py:157
  2.1 3.1 %collective-permute-start = (bf16[32,1024]{1,0:T(8,128)(2,1)S(1)}, bf16[32,1024]{1,0:T(8,128)(2,1)S(1)}, u32[]{:S(2)}, u32[]{:S(2)}) collective-permute-start(bf16[32,1024]{1,0:T(8,128)(2,1)S(1)} %get-tuple-element.54), channel_id=1, source_target_pairs={{0,4},{1,5},{2,6},{3,7},{4,8},{5,9},{6,10},{7,11},{8,12},{9,13},{1... | collective-permute-start | bytes 196616 | tf_op jit(solution)/shard_map/ppermute | solution.py:214
  5.1 2.1 %collective-permute-start.1 = (bf16[32,1024]{1,0:T(8,128)(2,1)S(1)}, bf16[32,1024]{1,0:T(8,128)(2,1)S(1)}, u32[]{:S(2)}, u32[]{:S(2)}) collective-permute-start(bf16[32,1024]{1,0:T(8,128)(2,1)S(1)} %get-tuple-element.55), channel_id=1, source_target_pairs={{0,12},{1,13},{2,14},{3,15},{4,0},{5,1},{6,2},{7,3},{8,4},{9,5},{1... | collective-permute-start | bytes 196616 | tf_op jit(solution)/shard_map/ppermute | solution.py:214
  7.2 1.8 %collective-permute-start.3 = (bf16[16,1024]{1,0:T(8,128)(2,1)S(1)}, bf16[16,1024]{1,0:T(8,128)(2,1)S(1)}, u32[]{:S(2)}, u32[]{:S(2)}) collective-permute-start(bf16[16,1024]{1,0:T(8,128)(2,1)S(1)} %get-tuple-element.57), channel_id=1, source_target_pairs={{0,3},{1,2},{2,5},{3,4},{4,7},{5,6},{6,9},{7,8},{8,11},{9,10},{10,... | collective-permute-start | bytes 98312 | tf_op jit(solution)/shard_map/ppermute | solution.py:214
  9.0 2.7 %collective-permute-start.4 = (bf16[16,1024]{1,0:T(8,128)(2,1)S(1)}, bf16[16,1024]{1,0:T(8,128)(2,1)S(1)}, u32[]{:S(2)}, u32[]{:S(2)}) collective-permute-start(bf16[16,1024]{1,0:T(8,128)(2,1)S(1)} %get-tuple-element.58), channel_id=1, source_target_pairs={{0,15},{1,14},{2,1},{3,0},{4,3},{5,2},{6,5},{7,4},{8,7},{9,6},{10,... | collective-permute-start | bytes 98312 | tf_op jit(solution)/shard_map/ppermute | solution.py:214
  11.7 1.6 %collective-permute-done.3.refs_3_ = bf16[16,1024]{1,0:T(8,128)(2,1)S(1)} collective-permute-done((bf16[16,1024]{1,0:T(8,128)(2,1)S(1)}, bf16[16,1024]{1,0:T(8,128)(2,1)S(1)}, u32[]{:S(2)}, u32[]{:S(2)}) %collective-permute-start.3) | collective-permute-done | bytes 32800 | tf_op jit(solution)/shard_map/ppermute | solution.py:214
  13.9 5.6 %local_products.1 = (bf16[256,256]{1,0:T(8,128)(2,1)S(1)}, f32[384,512]{1,0:T(8,128)S(1)}, f32[768,512]{1,0:T(8,128)S(1)}, f32[64,512]{1,0:T(8,128)S(1)}, bf16[3...) custom-call(bf16[256,256]{1,0:T(8,128)(2,1)S(1)} %get-tuple-element., ...), custom_call_target="tpu_custom_call" | custom-call | flops 1275068416 | bytes 9774080 | tf_op jit(solution)/shard_map/local_products/pallas_call | solution.py:157
  19.7 3.6 %edges_forward.1 = (bf16[32,1024]{1,0:T(8,128)(2,1)S(1)}, bf16[32,1024]{1,0:T(8,128)(2,1)S(1)}, bf16[16,1024]{1,0:T(8,128)(2,1)S(1)}, bf16[16,1024]{1,0:T(8,128)...) custom-call(bf16[32,1024]{1,0:T(8,128)(2,1)S(1)} %collective-permute, ...), custom_call_target="tpu_custom_call" | custom-call | flops 1207959552 | bytes 16552704 | tf_op jit(solution)/shard_map/edges_forward/pallas_call | solution.py:157
  23.4 1.2 %collective-permute-start.9 = (bf16[32,1024]{1,0:T(8,128)(2,1)S(1)}, bf16[32,1024]{1,0:T(8,128)(2,1)S(1)}, u32[]{:S(2)}, u32[]{:S(2)}) collective-permute-start(bf16[32,1024]{1,0:T(8,128)(2,1)S(1)} %get-tuple-element.69), channel_id=1, source_target_pairs={{0,4},{1,5},{2,6},{3,7},{4,8},{5,9},{6,10},{7,11},{8,12},{9,13},{1... | collective-permute-start | bytes 196616 | tf_op jit(solution)/shard_map/ppermute | solution.py:214
  24.5 2.7 %collective-permute-start.10 = (bf16[32,1024]{1,0:T(8,128)(2,1)S(1)}, bf16[32,1024]{1,0:T(8,128)(2,1)S(1)}, u32[]{:S(2)}, u32[]{:S(2)}) collective-permute-start(bf16[32,1024]{1,0:T(8,128)(2,1)S(1)} %get-tuple-element.70), channel_id=1, source_target_pairs={{0,12},{1,13},{2,14},{3,15},{4,0},{5,1},{6,2},{7,3},{8,4},{9,5},{1... | collective-permute-start | bytes 196616 | tf_op jit(solution)/shard_map/ppermute | solution.py:214
  27.2 2.2 %collective-permute-start.12 = (bf16[16,1024]{1,0:T(8,128)(2,1)S(1)}, bf16[16,1024]{1,0:T(8,128)(2,1)S(1)}, u32[]{:S(2)}, u32[]{:S(2)}) collective-permute-start(bf16[16,1024]{1,0:T(8,128)(2,1)S(1)} %get-tuple-element.72), channel_id=1, source_target_pairs={{0,3},{1,2},{2,5},{3,4},{4,7},{5,6},{6,9},{7,8},{8,11},{9,10},{10,... | collective-permute-start | bytes 98312 | tf_op jit(solution)/shard_map/ppermute | solution.py:214
  29.5 0.6 %collective-permute-done.9.refs_9_ = bf16[32,1024]{1,0:T(8,128)(2,1)S(1)} collective-permute-done((bf16[32,1024]{1,0:T(8,128)(2,1)S(1)}, bf16[32,1024]{1,0:T(8,128)(2,1)S(1)}, u32[]{:S(2)}, u32[]{:S(2)}) %collective-permute-start.9) | collective-permute-done | bytes 65568 | tf_op jit(solution)/shard_map/ppermute | solution.py:214
  30.6 4.6 %collective-permute-start.13 = (bf16[16,1024]{1,0:T(8,128)(2,1)S(1)}, bf16[16,1024]{1,0:T(8,128)(2,1)S(1)}, u32[]{:S(2)}, u32[]{:S(2)}) collective-permute-start(bf16[16,1024]{1,0:T(8,128)(2,1)S(1)} %get-tuple-element.73), channel_id=1, source_target_pairs={{0,15},{1,14},{2,1},{3,0},{4,3},{5,2},{6,5},{7,4},{8,7},{9,6},{10,... | collective-permute-start | bytes 98312 | tf_op jit(solution)/shard_map/ppermute | solution.py:214
  35.7 1.2 %collective-permute-done.13.refs_13_ = bf16[16,1024]{1,0:T(8,128)(2,1)S(1)} collective-permute-done((bf16[16,1024]{1,0:T(8,128)(2,1)S(1)}, bf16[16,1024]{1,0:T(8,128)(2,1)S(1)}, u32[]{:S(2)}, u32[]{:S(2)}) %collective-permute-start.13) | collective-permute-done | bytes 32800 | tf_op jit(solution)/shard_map/ppermute | solution.py:214
  37.0 3.5 %collective-permute-done.14.refs_14_ = bf16[16,1024]{1,0:T(8,128)(2,1)S(1)} collective-permute-done((bf16[16,1024]{1,0:T(8,128)(2,1)S(1)}, bf16[16,1024]{1,0:T(8,128)(2,1)S(1)}, u32[]{:S(2)}, u32[]{:S(2)}) %collective-permute-start.14) | collective-permute-done | bytes 32800 | tf_op jit(solution)/shard_map/ppermute | solution.py:214
  40.5 6.0 %edges_backward.1 = (bf16[32,512]{1,0:T(8,128)(2,1)S(1)}, bf16[32,512]{1,0:T(8,128)(2,1)S(1)}, bf16[16,512]{1,0:T(8,128)(2,1)S(1)}, bf16[16,512]{1,0:T(8,128)(2,...) custom-call(bf16[32,1024]{1,0:T(8,128)(2,1)S(1)} %collective-permute, ...), custom_call_target="tpu_custom_call" | custom-call | flops 2449473536 | bytes 18502400 | tf_op jit(solution)/shard_map/edges_backward/pallas_call | solution.py:157
  46.7 3.7 %collective-permute-start.19 = (bf16[32,512]{1,0:T(8,128)(2,1)S(1)}, bf16[32,512]{1,0:T(8,128)(2,1)S(1)}, u32[]{:S(2)}, u32[]{:S(2)}) collective-permute-start(bf16[32,512]{1,0:T(8,128)(2,1)S(1)} %get-tuple-element.90), channel_id=1, source_target_pairs={{0,12},{1,13},{2,14},{3,15},{4,0},{5,1},{6,2},{7,3},{8,4},{9,5},{1... | collective-permute-start | bytes 98312 | tf_op jit(solution)/shard_map/ppermute | solution.py:214
  50.8 4.0 %collective-permute-start.22 = (bf16[16,512]{1,0:T(8,128)(2,1)S(1)}, bf16[16,512]{1,0:T(8,128)(2,1)S(1)}, u32[]{:S(2)}, u32[]{:S(2)}) collective-permute-start(bf16[16,512]{1,0:T(8,128)(2,1)S(1)} %get-tuple-element.93), channel_id=1, source_target_pairs={{0,15},{1,14},{2,1},{3,0},{4,3},{5,2},{6,5},{7,4},{8,7},{9,6},{10,... | collective-permute-start | bytes 49160 | tf_op jit(solution)/shard_map/ppermute | solution.py:214
  54.8 1.4 %collective-permute-done.21.refs_3_ = bf16[16,512]{1,0:T(8,128)(2,1)S(1)} collective-permute-done((bf16[16,512]{1,0:T(8,128)(2,1)S(1)}, bf16[16,512]{1,0:T(8,128)(2,1)S(1)}, u32[]{:S(2)}, u32[]{:S(2)}) %collective-permute-start.21) | collective-permute-done | bytes 16416 | tf_op jit(solution)/shard_map/ppermute | solution.py:214
  56.3 0.5 collective-permute-start.25
  56.8 1.5 %local_gradients.1 = (f32[256,512]{1,0:T(8,128)S(1)}, f32[64,512]{1,0:T(8,128)}) custom-call(bf16[256,512]{1,0:T(8,128)(2,1)S(1)} %copy-done.5, bf16[256,512]{1,0:T(8,128)(2,1)S(1)} %get-tuple-element.96.refs_1_, bf16[256,512]{1,0:T(8,128)(2,1)S(1)} %get-tuple-element.97.refs_2_, bf16[256,512]{1,0:T(8,128)(2,1)S(1)} %get-tuple-element.98.refs_3_, ...), custom_call_target="tpu_custom_call" | custom-call | flops 402653184 | bytes 8781824 | tf_op jit(solution)/shard_map/local_gradients/pallas_call | solution.py:157
  58.4 1.4 %collective-permute-done.23.refs_5_ = bf16[16,512]{1,0:T(8,128)(2,1)S(1)} collective-permute-done((bf16[16,512]{1,0:T(8,128)(2,1)S(1)}, bf16[16,512]{1,0:T(8,128)(2,1)S(1)}, u32[]{:S(2)}, u32[]{:S(2)}) %collective-permute-start.23) | collective-permute-done | bytes 16416 | tf_op jit(solution)/shard_map/ppermute | solution.py:214
  59.8 1.1 %collective-permute-done.24.refs_6_ = bf16[16,512]{1,0:T(8,128)(2,1)S(1)} collective-permute-done((bf16[16,512]{1,0:T(8,128)(2,1)S(1)}, bf16[16,512]{1,0:T(8,128)(2,1)S(1)}, u32[]{:S(2)}, u32[]{:S(2)}) %collective-permute-start.24) | collective-permute-done | bytes 16416 | tf_op jit(solution)/shard_map/ppermute | solution.py:214
  60.9 1.0 %add_returned.1 = f32[256,512]{1,0:T(8,128)} custom-call(bf16[32,512]{1,0:T(8,128)(2,1)S(1)} %collective-permute-done.18.refs_0_, bf16[32,512]{1,0:T(8,128)(2,1)S(1)} %collective-permute-done.19.refs_1_, bf16[16,512]{1,0:T(8,128)(2,1)S(1)} %collective-permute-done.20.refs_2_, bf16[16,512]{1,0:T(8,128)(2,1)S(1)} %collective-permute-done.21.refs_3_, ...), custom_call_target="tpu_custom_call" | custom-call | flops 37748736 | bytes 1392640 | tf_op jit(solution)/shard_map/add_returned/pallas_call | solution.py:157
  (61 shorter events, 2.4 us)
Async XLA Ops:
  2.1 11.2 %collective-permute-start = (bf16[32,1024]{1,0:T(8,128)(2,1)S(1)}, bf16[32,1024]{1,0:T(8,128)(2,1)S(1)}, u32[]{:S(2)}, u32[]{:S(2)}) collective-permute-start(bf16[32,1024]{1,0:T(8,128)(2,1)S(1)} %get-tuple-element.54), channel_id=1, source_target_pairs={{0,4},{1,5},{2,6},{3,7},{4,8},{5,9},{6,10},{7,11},{8,12},{9,13},{1... | collective-permute-start | bytes 196616 | tf_op jit(solution)/shard_map/ppermute | solution.py:214
  5.1 8.7 %collective-permute-start.1 = (bf16[32,1024]{1,0:T(8,128)(2,1)S(1)}, bf16[32,1024]{1,0:T(8,128)(2,1)S(1)}, u32[]{:S(2)}, u32[]{:S(2)}) collective-permute-start(bf16[32,1024]{1,0:T(8,128)(2,1)S(1)} %get-tuple-element.55), channel_id=1, source_target_pairs={{0,12},{1,13},{2,14},{3,15},{4,0},{5,1},{6,2},{7,3},{8,4},{9,5},{1... | collective-permute-start | bytes 196616 | tf_op jit(solution)/shard_map/ppermute | solution.py:214
  7.2 6.0 %collective-permute-start.3 = (bf16[16,1024]{1,0:T(8,128)(2,1)S(1)}, bf16[16,1024]{1,0:T(8,128)(2,1)S(1)}, u32[]{:S(2)}, u32[]{:S(2)}) collective-permute-start(bf16[16,1024]{1,0:T(8,128)(2,1)S(1)} %get-tuple-element.57), channel_id=1, source_target_pairs={{0,3},{1,2},{2,5},{3,4},{4,7},{5,6},{6,9},{7,8},{8,11},{9,10},{10,... | collective-permute-start | bytes 98312 | tf_op jit(solution)/shard_map/ppermute | solution.py:214
  9.0 10.5 %collective-permute-start.4 = (bf16[16,1024]{1,0:T(8,128)(2,1)S(1)}, bf16[16,1024]{1,0:T(8,128)(2,1)S(1)}, u32[]{:S(2)}, u32[]{:S(2)}) collective-permute-start(bf16[16,1024]{1,0:T(8,128)(2,1)S(1)} %get-tuple-element.58), channel_id=1, source_target_pairs={{0,15},{1,14},{2,1},{3,0},{4,3},{5,2},{6,5},{7,4},{8,7},{9,6},{10,... | collective-permute-start | bytes 98312 | tf_op jit(solution)/shard_map/ppermute | solution.py:214
  11.7 7.9 %collective-permute-start.5 = (bf16[16,1024]{1,0:T(8,128)(2,1)S(1)}, bf16[16,1024]{1,0:T(8,128)(2,1)S(1)}, u32[]{:S(2)}, u32[]{:S(2)}) collective-permute-start(bf16[16,1024]{1,0:T(8,128)(2,1)S(1)} %get-tuple-element.59), channel_id=1, source_target_pairs={{0,11},{1,6},{2,13},{3,8},{4,15},{5,10},{6,1},{7,12},{8,3},{9,14},... | collective-permute-start | bytes 98312 | tf_op jit(solution)/shard_map/ppermute | solution.py:214
  13.3 6.3 %collective-permute-start.6 = (bf16[16,1024]{1,0:T(8,128)(2,1)S(1)}, bf16[16,1024]{1,0:T(8,128)(2,1)S(1)}, u32[]{:S(2)}, u32[]{:S(2)}) collective-permute-start(bf16[16,1024]{1,0:T(8,128)(2,1)S(1)} %get-tuple-element.60), channel_id=1, source_target_pairs={{0,8},{1,9},{2,10},{3,11},{4,12},{5,13},{6,14},{7,15},{8,0},{9,1},... | collective-permute-start | bytes 98312 | tf_op jit(solution)/shard_map/ppermute | solution.py:214
  13.3 6.3 %collective-permute-start.7 = (bf16[32,1024]{1,0:T(8,128)(2,1)S(1)}, bf16[32,1024]{1,0:T(8,128)(2,1)S(1)}, u32[]{:S(2)}, u32[]{:S(2)}) collective-permute-start(bf16[32,1024]{1,0:T(8,128)(2,1)S(1)} %collective-permute-done.refs_0_), channel_id=1, source_target_pairs={{0,1},{1,0},{2,3},{3,2},{4,5},{5,4},{6,7},{7,6},{8,9},{9,8},{10,11... | collective-permute-start | bytes 196616 | tf_op jit(solution)/shard_map/ppermute | solution.py:214
  13.8 5.8 %collective-permute-start.8 = (bf16[32,1024]{1,0:T(8,128)(2,1)S(1)}, bf16[32,1024]{1,0:T(8,128)(2,1)S(1)}, u32[]{:S(2)}, u32[]{:S(2)}) collective-permute-start(bf16[32,1024]{1,0:T(8,128)(2,1)S(1)} %collective-permute-done.1.refs_1_), channel_id=1, source_target_pairs={{0,1},{1,0},{2,3},{3,2},{4,5},{5,4},{6,7},{7,6},{8,9},{9,8},{10,11... | collective-permute-start | bytes 196616 | tf_op jit(solution)/shard_map/ppermute | solution.py:214
  23.4 6.8 %collective-permute-start.9 = (bf16[32,1024]{1,0:T(8,128)(2,1)S(1)}, bf16[32,1024]{1,0:T(8,128)(2,1)S(1)}, u32[]{:S(2)}, u32[]{:S(2)}) collective-permute-start(bf16[32,1024]{1,0:T(8,128)(2,1)S(1)} %get-tuple-element.69), channel_id=1, source_target_pairs={{0,4},{1,5},{2,6},{3,7},{4,8},{5,9},{6,10},{7,11},{8,12},{9,13},{1... | collective-permute-start | bytes 196616 | tf_op jit(solution)/shard_map/ppermute | solution.py:214
  24.5 5.9 %collective-permute-start.10 = (bf16[32,1024]{1,0:T(8,128)(2,1)S(1)}, bf16[32,1024]{1,0:T(8,128)(2,1)S(1)}, u32[]{:S(2)}, u32[]{:S(2)}) collective-permute-start(bf16[32,1024]{1,0:T(8,128)(2,1)S(1)} %get-tuple-element.70), channel_id=1, source_target_pairs={{0,12},{1,13},{2,14},{3,15},{4,0},{5,1},{6,2},{7,3},{8,4},{9,5},{1... | collective-permute-start | bytes 196616 | tf_op jit(solution)/shard_map/ppermute | solution.py:214
  27.2 8.0 %collective-permute-start.11 = (bf16[16,1024]{1,0:T(8,128)(2,1)S(1)}, bf16[16,1024]{1,0:T(8,128)(2,1)S(1)}, u32[]{:S(2)}, u32[]{:S(2)}) collective-permute-start(bf16[16,1024]{1,0:T(8,128)(2,1)S(1)} %get-tuple-element.71), channel_id=1, source_target_pairs={{0,1},{1,0},{2,3},{3,2},{4,5},{5,4},{6,7},{7,6},{8,9},{9,8},{10,11... | collective-permute-start | bytes 98312 | tf_op jit(solution)/shard_map/ppermute | solution.py:214
  27.2 8.0 %collective-permute-start.12 = (bf16[16,1024]{1,0:T(8,128)(2,1)S(1)}, bf16[16,1024]{1,0:T(8,128)(2,1)S(1)}, u32[]{:S(2)}, u32[]{:S(2)}) collective-permute-start(bf16[16,1024]{1,0:T(8,128)(2,1)S(1)} %get-tuple-element.72), channel_id=1, source_target_pairs={{0,3},{1,2},{2,5},{3,4},{4,7},{5,6},{6,9},{7,8},{8,11},{9,10},{10,... | collective-permute-start | bytes 98312 | tf_op jit(solution)/shard_map/ppermute | solution.py:214
  30.1 10.4 %collective-permute-start.16 = (bf16[32,1024]{1,0:T(8,128)(2,1)S(1)}, bf16[32,1024]{1,0:T(8,128)(2,1)S(1)}, u32[]{:S(2)}, u32[]{:S(2)}) collective-permute-start(bf16[32,1024]{1,0:T(8,128)(2,1)S(1)} %collective-permute-done.9.refs_9_), channel_id=1, source_target_pairs={{0,1},{1,0},{2,3},{3,2},{4,5},{5,4},{6,7},{7,6},{8,9},{9,8},{10,11... | collective-permute-start | bytes 196616 | tf_op jit(solution)/shard_map/ppermute | solution.py:214
  30.4 10.1 %collective-permute-start.17 = (bf16[32,1024]{1,0:T(8,128)(2,1)S(1)}, bf16[32,1024]{1,0:T(8,128)(2,1)S(1)}, u32[]{:S(2)}, u32[]{:S(2)}) collective-permute-start(bf16[32,1024]{1,0:T(8,128)(2,1)S(1)} %collective-permute-done.10.refs_10_), channel_id=1, source_target_pairs={{0,1},{1,0},{2,3},{3,2},{4,5},{5,4},{6,7},{7,6},{8,9},{9,8},{10,11... | collective-permute-start | bytes 196616 | tf_op jit(solution)/shard_map/ppermute | solution.py:214
  30.6 6.3 %collective-permute-start.13 = (bf16[16,1024]{1,0:T(8,128)(2,1)S(1)}, bf16[16,1024]{1,0:T(8,128)(2,1)S(1)}, u32[]{:S(2)}, u32[]{:S(2)}) collective-permute-start(bf16[16,1024]{1,0:T(8,128)(2,1)S(1)} %get-tuple-element.73), channel_id=1, source_target_pairs={{0,15},{1,14},{2,1},{3,0},{4,3},{5,2},{6,5},{7,4},{8,7},{9,6},{10,... | collective-permute-start | bytes 98312 | tf_op jit(solution)/shard_map/ppermute | solution.py:214
  35.2 5.2 %collective-permute-start.14 = (bf16[16,1024]{1,0:T(8,128)(2,1)S(1)}, bf16[16,1024]{1,0:T(8,128)(2,1)S(1)}, u32[]{:S(2)}, u32[]{:S(2)}) collective-permute-start(bf16[16,1024]{1,0:T(8,128)(2,1)S(1)} %get-tuple-element.74), channel_id=1, source_target_pairs={{0,11},{1,6},{2,13},{3,8},{4,15},{5,10},{6,1},{7,12},{8,3},{9,14},... | collective-permute-start | bytes 98312 | tf_op jit(solution)/shard_map/ppermute | solution.py:214
  35.2 5.2 %collective-permute-start.15 = (bf16[16,1024]{1,0:T(8,128)(2,1)S(1)}, bf16[16,1024]{1,0:T(8,128)(2,1)S(1)}, u32[]{:S(2)}, u32[]{:S(2)}) collective-permute-start(bf16[16,1024]{1,0:T(8,128)(2,1)S(1)} %get-tuple-element.75), channel_id=1, source_target_pairs={{0,8},{1,9},{2,10},{3,11},{4,12},{5,13},{6,14},{7,15},{8,0},{9,1},... | collective-permute-start | bytes 98312 | tf_op jit(solution)/shard_map/ppermute | solution.py:214
  46.5 9.7 %collective-permute-start.18 = (bf16[32,512]{1,0:T(8,128)(2,1)S(1)}, bf16[32,512]{1,0:T(8,128)(2,1)S(1)}, u32[]{:S(2)}, u32[]{:S(2)}) collective-permute-start(bf16[32,512]{1,0:T(8,128)(2,1)S(1)} %get-tuple-element.89), channel_id=1, source_target_pairs={{0,4},{1,5},{2,6},{3,7},{4,8},{5,9},{6,10},{7,11},{8,12},{9,13},{1... | collective-permute-start | bytes 98312 | tf_op jit(solution)/shard_map/ppermute | solution.py:214
  46.7 10.1 %collective-permute-start.19 = (bf16[32,512]{1,0:T(8,128)(2,1)S(1)}, bf16[32,512]{1,0:T(8,128)(2,1)S(1)}, u32[]{:S(2)}, u32[]{:S(2)}) collective-permute-start(bf16[32,512]{1,0:T(8,128)(2,1)S(1)} %get-tuple-element.90), channel_id=1, source_target_pairs={{0,12},{1,13},{2,14},{3,15},{4,0},{5,1},{6,2},{7,3},{8,4},{9,5},{1... | collective-permute-start | bytes 98312 | tf_op jit(solution)/shard_map/ppermute | solution.py:214
  50.4 5.9 %collective-permute-start.21 = (bf16[16,512]{1,0:T(8,128)(2,1)S(1)}, bf16[16,512]{1,0:T(8,128)(2,1)S(1)}, u32[]{:S(2)}, u32[]{:S(2)}) collective-permute-start(bf16[16,512]{1,0:T(8,128)(2,1)S(1)} %get-tuple-element.92), channel_id=1, source_target_pairs={{0,3},{1,2},{2,5},{3,4},{4,7},{5,6},{6,9},{7,8},{8,11},{9,10},{10,... | collective-permute-start | bytes 49160 | tf_op jit(solution)/shard_map/ppermute | solution.py:214
  50.8 7.6 %collective-permute-start.22 = (bf16[16,512]{1,0:T(8,128)(2,1)S(1)}, bf16[16,512]{1,0:T(8,128)(2,1)S(1)}, u32[]{:S(2)}, u32[]{:S(2)}) collective-permute-start(bf16[16,512]{1,0:T(8,128)(2,1)S(1)} %get-tuple-element.93), channel_id=1, source_target_pairs={{0,15},{1,14},{2,1},{3,0},{4,3},{5,2},{6,5},{7,4},{8,7},{9,6},{10,... | collective-permute-start | bytes 49160 | tf_op jit(solution)/shard_map/ppermute | solution.py:214
  54.8 5.0 %collective-permute-start.23 = (bf16[16,512]{1,0:T(8,128)(2,1)S(1)}, bf16[16,512]{1,0:T(8,128)(2,1)S(1)}, u32[]{:S(2)}, u32[]{:S(2)}) collective-permute-start(bf16[16,512]{1,0:T(8,128)(2,1)S(1)} %get-tuple-element.94), channel_id=1, source_target_pairs={{0,11},{1,6},{2,13},{3,8},{4,15},{5,10},{6,1},{7,12},{8,3},{9,14},... | collective-permute-start | bytes 49160 | tf_op jit(solution)/shard_map/ppermute | solution.py:214
  56.2 4.6 %collective-permute-start.24 = (bf16[16,512]{1,0:T(8,128)(2,1)S(1)}, bf16[16,512]{1,0:T(8,128)(2,1)S(1)}, u32[]{:S(2)}, u32[]{:S(2)}) collective-permute-start(bf16[16,512]{1,0:T(8,128)(2,1)S(1)} %get-tuple-element.95), channel_id=1, source_target_pairs={{0,8},{1,9},{2,10},{3,11},{4,12},{5,13},{6,14},{7,15},{8,0},{9,1},... | collective-permute-start | bytes 49160 | tf_op jit(solution)/shard_map/ppermute | solution.py:214
  56.3 4.6 %collective-permute-start.25 = (bf16[32,512]{1,0:T(8,128)(2,1)S(1)}, bf16[32,512]{1,0:T(8,128)(2,1)S(1)}, u32[]{:S(2)}, u32[]{:S(2)}) collective-permute-start(bf16[32,512]{1,0:T(8,128)(2,1)S(1)} %collective-permute-done.18.refs_0_), channel_id=1, source_target_pairs={{0,1},{1,0},{2,3},{3,2},{4,5},{5,4},{6,7},{7,6},{8,9},{9,8},{10,11... | collective-permute-start | bytes 98312 | tf_op jit(solution)/shard_map/ppermute | solution.py:214
  (15 other events, 136.1 us)

commit v4 on v3

--- a/solution.py
+++ b/solution.py
@@ -213,32 +213,36 @@
         steps = (even_step, odd_step)
         return lax.ppermute(part, "tile", [(s, (s + steps[s % 2]) % peer_count) for s in peers])
 
+    def lay_together(kept_ref, got_ref, next_ref, second_ref):
+        next_ref[:width, :] = kept_ref[:width, :]
+        next_ref[width:, :] = got_ref[width : 2 * width, :]
+        second_ref[:width, :] = kept_ref[width : 2 * width, :]
+        second_ref[width : 2 * width, :] = got_ref[3 * width :, :]
+        second_ref[2 * width : 3 * width, :] = kept_ref[2 * width :, :]
+        second_ref[3 * width :, :] = got_ref[2 * width : 3 * width, :]
+
     def exchange(parts):
-        plus_two, minus_two, own_chip, plus_one, minus_one, three_off, opposite = parts
-        plus_two = permute(plus_two, 4, 4)
-        minus_two = permute(minus_two, -4, -4)
-        own_chip = permute(own_chip, 1, -1)
-        plus_one = permute(plus_one, 3, 1)
-        minus_one = permute(minus_one, -1, -3)
+        for_partner, three_off, opposite, kept = parts
+        columns = kept.shape[1]
+        got = permute(for_partner, 1, -1)
+        opposite = permute(opposite, peer_count // 2, peer_count // 2)
         three_off = permute(three_off, -5, 5)
-        opposite = permute(opposite, peer_count // 2, peer_count // 2)
-        plus_passed = permute(plus_two, 1, -1)
-        minus_passed = permute(minus_two, 1, -1)
-        return [
-            plus_two,
-            minus_two,
-            own_chip,
-            plus_one,
-            minus_one,
-            three_off,
-            opposite,
-            plus_passed,
-            minus_passed,
-        ]
+        next_chip, second_chip = call(
+            lay_together,
+            "lay_together",
+            [kept, got],
+            [((2 * width, columns), BF16), ((4 * width, columns), BF16)],
+        )
+        second_chip = permute(second_chip, -4, 4)
+        next_chip = permute(next_chip, -2, 2)
+        second_passed = permute(second_chip, 1, -1)
+        next_passed = permute(next_chip, 1, -1)
+        return [got, opposite, three_off, second_chip, next_chip, second_passed, next_passed]
+
+    arrived_count = 7
 
     def sent_shapes(columns):
-        rows = (2, 2, 1, 1, 1, 1, 1)
-        return [((count * width, columns), BF16) for count in rows]
+        return [((count * width, columns), BF16) for count in (4, 1, 1, 3)]
 
     sent_count = len(sent_shapes(feat))
 
@@ -247,39 +251,38 @@
 
     def send(refs, message, columns=slice(None)):
         odd = is_odd()
-
-        def by_parity(even, odd_one):
-            return jnp.where(odd, message(odd_one), message(even))
-
-        plus_two, minus_two, own_chip, plus_one, minus_one, three_off, opposite = refs
-        plus_two[:width, columns] = message(four)
-        plus_two[width:, columns] = by_parity(five, three)
-        minus_two[:width, columns] = message(minus[four])
-        minus_two[width:, columns] = by_parity(minus[three], minus[five])
-        own_chip[:, columns] = by_parity(one, minus[one])
-        plus_one[:, columns] = by_parity(three, one)
-        minus_one[:, columns] = by_parity(minus[one], minus[three])
-        three_off[:, columns] = by_parity(minus[five], five)
+        for_partner, three_off, opposite, kept = refs
+
+        def block(place):
+            return slice(place * width, (place + 1) * width)
+
+        for place, step in enumerate((one, three, four, five)):
+            ahead, behind = message(step), message(minus[step])
+            for_partner[block(place), columns] = jnp.where(odd, behind, ahead)
+            own = jnp.where(odd, ahead, behind)
+            if step == five:
+                three_off[:, columns] = own
+            else:
+                kept[block((one, four, three).index(step)), columns] = own
         opposite[:, columns] = message(across)
 
     def receive(refs, columns=slice(None)):
         odd = is_odd()
-        plus_two, minus_two, own_chip, plus_one, minus_one, three_off, opposite = refs[:7]
-        plus_passed, minus_passed = refs[7:]
-        first, second = slice(0, width), slice(width, 2 * width)
-        own = own_chip[:, columns]
-        near_plus, near_minus = plus_one[:, columns], minus_one[:, columns]
-        far = three_off[:, columns]
-        passed_plus, passed_minus = plus_passed[second, columns], minus_passed[second, columns]
+        got, opposite, three_off, second_chip, next_chip, second_passed, next_passed = refs
+
+        def block(ref, place):
+            return ref[place * width : (place + 1) * width, columns]
+
+        pairs = {
+            one: (block(got, 0), block(next_passed, 0)),
+            three: (block(next_chip, 1), block(second_passed, 2)),
+            four: (block(second_chip, 0), block(second_passed, 3)),
+            five: (block(second_chip, 1), block(three_off, 0)),
+        }
         slot_rows = [None] * links
-        slot_rows[one] = jnp.where(odd, own, near_plus)
-        slot_rows[minus[one]] = jnp.where(odd, near_minus, own)
-        slot_rows[three] = jnp.where(odd, near_plus, passed_plus)
-        slot_rows[minus[three]] = jnp.where(odd, passed_minus, near_minus)
-        slot_rows[five] = jnp.where(odd, passed_plus, far)
-        slot_rows[minus[five]] = jnp.where(odd, far, passed_minus)
-        slot_rows[four] = plus_two[first, columns]
-        slot_rows[minus[four]] = minus_two[first, columns]
+        for step, (near, far) in pairs.items():
+            slot_rows[step] = jnp.where(odd, near, far)
+            slot_rows[minus[step]] = jnp.where(odd, far, near)
         slot_rows[across] = opposite[:, columns]
         return slot_rows
 
@@ -405,7 +408,7 @@
     )
 
     def forward(*refs):
-        arrived_refs, refs = refs[:links], refs[links:]
+        arrived_refs, refs = refs[:arrived_count], refs[arrived_count:]
         (
             select_ref,
             enc_part_ref,
@@ -518,7 +521,8 @@
     returned = exchange(outgoing)
 
     def node_part(*refs):
-        arrived_refs, (nodes_ref, weight_ref, out_ref) = refs[:links], refs[links:]
+        arrived_refs = refs[:arrived_count]
+        nodes_ref, weight_ref, out_ref = refs[arrived_count:]
         out_ref[:grid_count, :] = mm(nodes_ref[...], weight_ref[low, :])
         out_ref[grid_count:, :] = mm(by_slot(arrived_refs, low), weight_ref[low, :])
 
@@ -531,7 +535,8 @@
     )
 
     def backward(*refs):
-        arrived_refs, returned_refs, refs = refs[:links], refs[links : 2 * links], refs[2 * links :]
+        arrived_refs, refs = refs[:arrived_count], refs[arrived_count:]
+        returned_refs, refs = refs[:arrived_count], refs[arrived_count:]
         (
             spot_ref,
             grid_part_ref,
@@ -724,7 +729,8 @@
     )
 
     def finish(*refs):
-        back_refs, (base_ref, select_t_ref, out_ref) = refs[:links], refs[links:]
+        back_refs = refs[:arrived_count]
+        base_ref, select_t_ref, out_ref = refs[arrived_count:]
         out_ref[...] = base_ref[...] + mm(select_t_ref[:, :slots], by_row(back_refs))
 
     (grad_grid,) = call(

time: 62.1 us -> 62.1 us (level)
    pallas_call x7 -> x10, Pallas kernels: 19.6 us -> 19.6 us  [call(): pl.pallas_call(kernel, name=name, in_specs=specs, out_specs=[pl.BlockSpec...]
    ppermute x27 -> x21, starting transfers between devices: 30.1 us -> 30.1 us  [permute(): lax.ppermute(part, 'tile', [(s, (s + steps[s % 2]) % peer_count) for s in...]
    ppermute x27 -> x21, waiting for transfers between devices: 11.3 us -> 11.3 us  [permute(): lax.ppermute(part, 'tile', [(s, (s + steps[s % 2]) % peer_count) for s in...]
  transfers between devices with their start and end apart: 27 -> 21, of which waited for: 8 -> 9; matrix products, arithmetic and copies ran while one was open for 0% -> 0% of each run, Pallas kernels for 12% -> 12%
where the time goes in v4:
time: 62.1 us; the launch traced here: 61.9 us
  starting transfers between devices  30.1 us (48%)
  Pallas kernels  19.6 us (32%)
  waiting for transfers between devices  11.3 us (18%)
  between operations  0.87 us (1%)
    ppermute x21, starting transfers between devices, permute(): lax.ppermute(part, 'tile', [(s, (s + steps[s % 2]) % peer_count) for s in...  30.1 us
    pallas_call x10, Pallas kernels, call(): pl.pallas_call(kernel, name=name, in_specs=specs, out_specs=[pl.BlockSpec...  19.6 us
    ppermute x21, waiting for transfers between devices, permute(): lax.ppermute(part, 'tile', [(s, (s + steps[s % 2]) % peer_count) for s in...  11.3 us
  transfers between devices with their start and end apart: 21, of which 9 were waited for; matrix products, arithmetic and copies ran while one was open for 0% of the time, Pallas kernels for 12%

profile of v4, /device:TPU:0, one launch (start us, length us, event | category | flops | bytes accessed | tf_op | source)
XLA Modules:
  0.0 61.9 jit_solution(10494557741444175596)
XLA Ops:
  0.6 1.4 %pack_rows.1 = (bf16[256,256]{1,0:T(8,128)(2,1)S(1)}, bf16[64,1024]{1,0:T(8,128)(2,1)S(1)}, bf16[16,1024]{1,0:T(8,128)(2,1)S(1)}, bf16[16,1024]{1,0:T(8,128)(2,1)S(1)}, bf16[48,1024]{1,0:T(8,128)(2,1)S(1)}) custom-call(s32[9,16]{1,0:T(8,128)} %refs_0_.2, s32[9]{0:T(128)} %refs_1_.2, bf16[256,512]{1,0:T(8,128)(2,1)} %refs_17_.3, bf16[256,512]{1,0:T(8,128)(2,1)} %refs_0_.3), custom_call_target="tpu_custom_call" | custom-call | flops 75497472 | bytes 950884 | tf_op jit(solution)/shard_map/pack_rows/pallas_call | solution.py:157
  3.6 5.0 %collective-permute-start.3 = (bf16[64,1024]{1,0:T(8,128)(2,1)S(1)}, bf16[64,1024]{1,0:T(8,128)(2,1)S(1)}, u32[]{:S(2)}, u32[]{:S(2)}) collective-permute-start(bf16[64,1024]{1,0:T(8,128)(2,1)S(1)} %get-tuple-element.55), channel_id=1, source_target_pairs={{0,12},{1,5},{2,14},{3,7},{4,0},{5,9},{6,2},{7,11},{8,4},{9,13},{1... | collective-permute-start | bytes 393224 | tf_op jit(solution)/shard_map/ppermute | solution.py:214
  8.6 1.4 %collective-permute-start.4 = (bf16[32,1024]{1,0:T(8,128)(2,1)S(1)}, bf16[32,1024]{1,0:T(8,128)(2,1)S(1)}, u32[]{:S(2)}, u32[]{:S(2)}) collective-permute-start(bf16[32,1024]{1,0:T(8,128)(2,1)S(1)} %get-tuple-element.56), channel_id=1, source_target_pairs={{0,14},{1,3},{2,0},{3,5},{4,2},{5,7},{6,4},{7,9},{8,6},{9,11},{10,... | collective-permute-start | bytes 196616 | tf_op jit(solution)/shard_map/ppermute | solution.py:214
  10.0 1.1 %collective-permute-done.3.refs_3_ = bf16[64,1024]{1,0:T(8,128)(2,1)S(1)} collective-permute-done((bf16[64,1024]{1,0:T(8,128)(2,1)S(1)}, bf16[64,1024]{1,0:T(8,128)(2,1)S(1)}, u32[]{:S(2)}, u32[]{:S(2)}) %collective-permute-start.3) | collective-permute-done | bytes 131104 | tf_op jit(solution)/shard_map/ppermute | solution.py:214
  11.3 1.7 %collective-permute-start.1 = (bf16[16,1024]{1,0:T(8,128)(2,1)S(1)}, bf16[16,1024]{1,0:T(8,128)(2,1)S(1)}, u32[]{:S(2)}, u32[]{:S(2)}) collective-permute-start(bf16[16,1024]{1,0:T(8,128)(2,1)S(1)} %get-tuple-element.52), channel_id=1, source_target_pairs={{0,8},{1,9},{2,10},{3,11},{4,12},{5,13},{6,14},{7,15},{8,0},{9,1},... | collective-permute-start | bytes 98312 | tf_op jit(solution)/shard_map/ppermute | solution.py:214
  13.0 1.9 %collective-permute-start.2 = (bf16[16,1024]{1,0:T(8,128)(2,1)S(1)}, bf16[16,1024]{1,0:T(8,128)(2,1)S(1)}, u32[]{:S(2)}, u32[]{:S(2)}) collective-permute-start(bf16[16,1024]{1,0:T(8,128)(2,1)S(1)} %get-tuple-element.53), channel_id=1, source_target_pairs={{0,11},{1,6},{2,13},{3,8},{4,15},{5,10},{6,1},{7,12},{8,3},{9,14},... | collective-permute-start | bytes 98312 | tf_op jit(solution)/shard_map/ppermute | solution.py:214
  15.0 2.0 %collective-permute-start.6 = (bf16[32,1024]{1,0:T(8,128)(2,1)S(1)}, bf16[32,1024]{1,0:T(8,128)(2,1)S(1)}, u32[]{:S(2)}, u32[]{:S(2)}) collective-permute-start(bf16[32,1024]{1,0:T(8,128)(2,1)S(1)} %collective-permute-done.4.refs_4_), channel_id=1, source_target_pairs={{0,1},{1,0},{2,3},{3,2},{4,5},{5,4},{6,7},{7,6},{8,9},{9,8},{10,11... | collective-permute-start | bytes 196616 | tf_op jit(solution)/shard_map/ppermute | solution.py:214
  17.1 5.6 %local_products.1 = (bf16[256,256]{1,0:T(8,128)(2,1)S(1)}, f32[384,512]{1,0:T(8,128)S(1)}, f32[768,512]{1,0:T(8,128)S(1)}, f32[64,512]{1,0:T(8,128)S(1)}, bf16[3...) custom-call(bf16[256,256]{1,0:T(8,128)(2,1)S(1)} %get-tuple-element., ...), custom_call_target="tpu_custom_call" | custom-call | flops 1275068416 | bytes 9774080 | tf_op jit(solution)/shard_map/local_products/pallas_call | solution.py:157
  22.8 3.6 %edges_forward.1 = (bf16[64,1024]{1,0:T(8,128)(2,1)S(1)}, bf16[16,1024]{1,0:T(8,128)(2,1)S(1)}, bf16[16,1024]{1,0:T(8,128)(2,1)S(1)}, bf16[48,1024]{1,0:T(8,128)...) custom-call(bf16[64,1024]{1,0:T(8,128)(2,1)S(1)} %collective-permute, ...), custom_call_target="tpu_custom_call" | custom-call | flops 1207959552 | bytes 16716544 | tf_op jit(solution)/shard_map/edges_forward/pallas_call | solution.py:157
  26.6 1.3 %collective-permute-done.7.refs_1_.refs_7_ = bf16[64,1024]{1,0:T(8,128)(2,1)S(1)} collective-permute-done((bf16[64,1024]{1,0:T(8,128)(2,1)S(1)}, bf16[64,1024]{1,0:T(8,128)(2,1)S(1)}, u32[]{:S(2)}, u32[]{:S(2)}) %collective-permute-start.7) | collective-permute-done | bytes 131104 | tf_op jit(solution)/shard_map/ppermute | solution.py:214
  27.9 2.3 %collective-permute-start.10 = (bf16[64,1024]{1,0:T(8,128)(2,1)S(1)}, bf16[64,1024]{1,0:T(8,128)(2,1)S(1)}, u32[]{:S(2)}, u32[]{:S(2)}) collective-permute-start(bf16[64,1024]{1,0:T(8,128)(2,1)S(1)} %get-tuple-element.69), channel_id=1, source_target_pairs={{0,12},{1,5},{2,14},{3,7},{4,0},{5,9},{6,2},{7,11},{8,4},{9,13},{1... | collective-permute-start | bytes 393224 | tf_op jit(solution)/shard_map/ppermute | solution.py:214
  30.7 2.7 %collective-permute-done.10.refs_10_ = bf16[64,1024]{1,0:T(8,128)(2,1)S(1)} collective-permute-done((bf16[64,1024]{1,0:T(8,128)(2,1)S(1)}, bf16[64,1024]{1,0:T(8,128)(2,1)S(1)}, u32[]{:S(2)}, u32[]{:S(2)}) %collective-permute-start.10) | collective-permute-done | bytes 131104 | tf_op jit(solution)/shard_map/ppermute | solution.py:214
  33.4 1.7 %collective-permute-start.12 = (bf16[64,1024]{1,0:T(8,128)(2,1)S(1)}, bf16[64,1024]{1,0:T(8,128)(2,1)S(1)}, u32[]{:S(2)}, u32[]{:S(2)}) collective-permute-start(bf16[64,1024]{1,0:T(8,128)(2,1)S(1)} %collective-permute-done.10.refs_10_), channel_id=1, source_target_pairs={{0,1},{1,0},{2,3},{3,2},{4,5},{5,4},{6,7},{7,6},{8,9},{9,8},{10,11... | collective-permute-start | bytes 393224 | tf_op jit(solution)/shard_map/ppermute | solution.py:214
  36.3 2.7 %collective-permute-start.9 = (bf16[16,1024]{1,0:T(8,128)(2,1)S(1)}, bf16[16,1024]{1,0:T(8,128)(2,1)S(1)}, u32[]{:S(2)}, u32[]{:S(2)}) collective-permute-start(bf16[16,1024]{1,0:T(8,128)(2,1)S(1)} %get-tuple-element.67), channel_id=1, source_target_pairs={{0,11},{1,6},{2,13},{3,8},{4,15},{5,10},{6,1},{7,12},{8,3},{9,14},... | collective-permute-start | bytes 98312 | tf_op jit(solution)/shard_map/ppermute | solution.py:214
  39.3 1.1 %collective-permute-done.8.refs_8_ = bf16[16,1024]{1,0:T(8,128)(2,1)S(1)} collective-permute-done((bf16[16,1024]{1,0:T(8,128)(2,1)S(1)}, bf16[16,1024]{1,0:T(8,128)(2,1)S(1)}, u32[]{:S(2)}, u32[]{:S(2)}) %collective-permute-start.8) | collective-permute-done | bytes 32800 | tf_op jit(solution)/shard_map/ppermute | solution.py:214
  40.4 1.6 %collective-permute-done.9.refs_9_ = bf16[16,1024]{1,0:T(8,128)(2,1)S(1)} collective-permute-done((bf16[16,1024]{1,0:T(8,128)(2,1)S(1)}, bf16[16,1024]{1,0:T(8,128)(2,1)S(1)}, u32[]{:S(2)}, u32[]{:S(2)}) %collective-permute-start.9) | collective-permute-done | bytes 32800 | tf_op jit(solution)/shard_map/ppermute | solution.py:214
  42.0 6.0 %edges_backward.1 = (bf16[64,512]{1,0:T(8,128)(2,1)S(1)}, bf16[16,512]{1,0:T(8,128)(2,1)S(1)}, bf16[16,512]{1,0:T(8,128)(2,1)S(1)}, bf16[48,512]{1,0:T(8,128)(2,...) custom-call(bf16[64,1024]{1,0:T(8,128)(2,1)S(1)} %collective-permute, ...), custom_call_target="tpu_custom_call" | custom-call | flops 2449473536 | bytes 18830080 | tf_op jit(solution)/shard_map/edges_backward/pallas_call | solution.py:157
  48.2 1.1 %collective-permute-done.14.refs_1_.refs_0_ = bf16[64,512]{1,0:T(8,128)(2,1)S(1)} collective-permute-done((bf16[64,512]{1,0:T(8,128)(2,1)S(1)}, bf16[64,512]{1,0:T(8,128)(2,1)S(1)}, u32[]{:S(2)}, u32[]{:S(2)}) %collective-permute-start.14) | collective-permute-done | bytes 65568 | tf_op jit(solution)/shard_map/ppermute | solution.py:214
  49.3 2.0 %collective-permute-start.17 = (bf16[64,512]{1,0:T(8,128)(2,1)S(1)}, bf16[64,512]{1,0:T(8,128)(2,1)S(1)}, u32[]{:S(2)}, u32[]{:S(2)}) collective-permute-start(bf16[64,512]{1,0:T(8,128)(2,1)S(1)} %get-tuple-element.88), channel_id=1, source_target_pairs={{0,12},{1,5},{2,14},{3,7},{4,0},{5,9},{6,2},{7,11},{8,4},{9,13},{1... | collective-permute-start | bytes 196616 | tf_op jit(solution)/shard_map/ppermute | solution.py:214
  51.3 1.6 %collective-permute-start.18 = (bf16[32,512]{1,0:T(8,128)(2,1)S(1)}, bf16[32,512]{1,0:T(8,128)(2,1)S(1)}, u32[]{:S(2)}, u32[]{:S(2)}) collective-permute-start(bf16[32,512]{1,0:T(8,128)(2,1)S(1)} %get-tuple-element.89), channel_id=1, source_target_pairs={{0,14},{1,3},{2,0},{3,5},{4,2},{5,7},{6,4},{7,9},{8,6},{9,11},{10,... | collective-permute-start | bytes 98312 | tf_op jit(solution)/shard_map/ppermute | solution.py:214
  53.6 1.4 %collective-permute-start.19 = (bf16[64,512]{1,0:T(8,128)(2,1)S(1)}, bf16[64,512]{1,0:T(8,128)(2,1)S(1)}, u32[]{:S(2)}, u32[]{:S(2)}) collective-permute-start(bf16[64,512]{1,0:T(8,128)(2,1)S(1)} %collective-permute-done.17.refs_3_), channel_id=1, source_target_pairs={{0,1},{1,0},{2,3},{3,2},{4,5},{5,4},{6,7},{7,6},{8,9},{9,8},{10,11... | collective-permute-start | bytes 196616 | tf_op jit(solution)/shard_map/ppermute | solution.py:214
  55.9 2.1 %collective-permute-start.16 = (bf16[16,512]{1,0:T(8,128)(2,1)S(1)}, bf16[16,512]{1,0:T(8,128)(2,1)S(1)}, u32[]{:S(2)}, u32[]{:S(2)}) collective-permute-start(bf16[16,512]{1,0:T(8,128)(2,1)S(1)} %get-tuple-element.86), channel_id=1, source_target_pairs={{0,11},{1,6},{2,13},{3,8},{4,15},{5,10},{6,1},{7,12},{8,3},{9,14},... | collective-permute-start | bytes 49160 | tf_op jit(solution)/shard_map/ppermute | solution.py:214
  58.7 1.5 %local_gradients.1 = (f32[256,512]{1,0:T(8,128)S(1)}, f32[64,512]{1,0:T(8,128)}) custom-call(bf16[256,512]{1,0:T(8,128)(2,1)S(1)} %copy-done.5, bf16[256,512]{1,0:T(8,128)(2,1)S(1)} %get-tuple-element.90.refs_1_, bf16[256,512]{1,0:T(8,128)(2,1)S(1)} %get-tuple-element.91.refs_2_, bf16[256,512]{1,0:T(8,128)(2,1)S(1)} %get-tuple-element.92.refs_3_, ...), custom_call_target="tpu_custom_call" | custom-call | flops 402653184 | bytes 8781824 | tf_op jit(solution)/shard_map/local_gradients/pallas_call | solution.py:157
  60.9 1.0 %add_returned.1 = f32[256,512]{1,0:T(8,128)} custom-call(bf16[64,512]{1,0:T(8,128)(2,1)S(1)} %collective-permute-done.14.refs_1_.refs_0_, bf16[16,512]{1,0:T(8,128)(2,1)S(1)} %collective-permute-done.15.refs_1_, bf16[16,512]{1,0:T(8,128)(2,1)S(1)} %collective-permute-done.16.refs_2_, bf16[64,512]{1,0:T(8,128)(2,1)S(1)} %collective-permute-done.17.refs_3_, ...), custom_call_target="tpu_custom_call" | custom-call | flops 37748736 | bytes 1474560 | tf_op jit(solution)/shard_map/add_returned/pallas_call | solution.py:157
  (52 shorter events, 7.1 us)
Async XLA Ops:
  2.0 1.5 %collective-permute-start = (bf16[64,1024]{1,0:T(8,128)(2,1)S(1)}, bf16[64,1024]{1,0:T(8,128)(2,1)S(1)}, u32[]{:S(2)}, u32[]{:S(2)}) collective-permute-start(bf16[64,1024]{1,0:T(8,128)(2,1)S(1)} %get-tuple-element.51), channel_id=1, source_target_pairs={{0,1},{1,0},{2,3},{3,2},{4,5},{5,4},{6,7},{7,6},{8,9},{9,8},{10,11... | collective-permute-start | bytes 393224 | tf_op jit(solution)/shard_map/ppermute | solution.py:214
  3.6 7.5 %collective-permute-start.3 = (bf16[64,1024]{1,0:T(8,128)(2,1)S(1)}, bf16[64,1024]{1,0:T(8,128)(2,1)S(1)}, u32[]{:S(2)}, u32[]{:S(2)}) collective-permute-start(bf16[64,1024]{1,0:T(8,128)(2,1)S(1)} %get-tuple-element.55), channel_id=1, source_target_pairs={{0,12},{1,5},{2,14},{3,7},{4,0},{5,9},{6,2},{7,11},{8,4},{9,13},{1... | collective-permute-start | bytes 393224 | tf_op jit(solution)/shard_map/ppermute | solution.py:214
  8.6 6.4 %collective-permute-start.4 = (bf16[32,1024]{1,0:T(8,128)(2,1)S(1)}, bf16[32,1024]{1,0:T(8,128)(2,1)S(1)}, u32[]{:S(2)}, u32[]{:S(2)}) collective-permute-start(bf16[32,1024]{1,0:T(8,128)(2,1)S(1)} %get-tuple-element.56), channel_id=1, source_target_pairs={{0,14},{1,3},{2,0},{3,5},{4,2},{5,7},{6,4},{7,9},{8,6},{9,11},{10,... | collective-permute-start | bytes 196616 | tf_op jit(solution)/shard_map/ppermute | solution.py:214
  11.1 11.6 %collective-permute-start.5 = (bf16[64,1024]{1,0:T(8,128)(2,1)S(1)}, bf16[64,1024]{1,0:T(8,128)(2,1)S(1)}, u32[]{:S(2)}, u32[]{:S(2)}) collective-permute-start(bf16[64,1024]{1,0:T(8,128)(2,1)S(1)} %collective-permute-done.3.refs_3_), channel_id=1, source_target_pairs={{0,1},{1,0},{2,3},{3,2},{4,5},{5,4},{6,7},{7,6},{8,9},{9,8},{10,11... | collective-permute-start | bytes 393224 | tf_op jit(solution)/shard_map/ppermute | solution.py:214
  11.3 11.4 %collective-permute-start.1 = (bf16[16,1024]{1,0:T(8,128)(2,1)S(1)}, bf16[16,1024]{1,0:T(8,128)(2,1)S(1)}, u32[]{:S(2)}, u32[]{:S(2)}) collective-permute-start(bf16[16,1024]{1,0:T(8,128)(2,1)S(1)} %get-tuple-element.52), channel_id=1, source_target_pairs={{0,8},{1,9},{2,10},{3,11},{4,12},{5,13},{6,14},{7,15},{8,0},{9,1},... | collective-permute-start | bytes 98312 | tf_op jit(solution)/shard_map/ppermute | solution.py:214
  13.0 9.7 %collective-permute-start.2 = (bf16[16,1024]{1,0:T(8,128)(2,1)S(1)}, bf16[16,1024]{1,0:T(8,128)(2,1)S(1)}, u32[]{:S(2)}, u32[]{:S(2)}) collective-permute-start(bf16[16,1024]{1,0:T(8,128)(2,1)S(1)} %get-tuple-element.53), channel_id=1, source_target_pairs={{0,11},{1,6},{2,13},{3,8},{4,15},{5,10},{6,1},{7,12},{8,3},{9,14},... | collective-permute-start | bytes 98312 | tf_op jit(solution)/shard_map/ppermute | solution.py:214
  15.0 7.8 %collective-permute-start.6 = (bf16[32,1024]{1,0:T(8,128)(2,1)S(1)}, bf16[32,1024]{1,0:T(8,128)(2,1)S(1)}, u32[]{:S(2)}, u32[]{:S(2)}) collective-permute-start(bf16[32,1024]{1,0:T(8,128)(2,1)S(1)} %collective-permute-done.4.refs_4_), channel_id=1, source_target_pairs={{0,1},{1,0},{2,3},{3,2},{4,5},{5,4},{6,7},{7,6},{8,9},{9,8},{10,11... | collective-permute-start | bytes 196616 | tf_op jit(solution)/shard_map/ppermute | solution.py:214
  22.8 16.1 %copy-start.3 = (bf16[1024,512]{1,0:T(8,128)(2,1)S(1)}, bf16[1024,512]{1,0:T(8,128)(2,1)}, u32[]{:S(2)}) copy-start(bf16[1024,512]{1,0:T(8,128)(2,1)} %refs_7_.5) | copy-start | bytes 3145732
  22.8 16.1 %copy-start.4 = (bf16[256,512]{1,0:T(8,128)(2,1)S(1)}, bf16[256,512]{1,0:T(8,128)(2,1)}, u32[]{:S(2)}) copy-start(bf16[256,512]{1,0:T(8,128)(2,1)} %refs_17_.3) | copy-start | bytes 786436
  26.5 15.5 %copy-start.5 = (bf16[256,512]{1,0:T(8,128)(2,1)S(1)}, bf16[256,512]{1,0:T(8,128)(2,1)}, u32[]{:S(2)}) copy-start(bf16[256,512]{1,0:T(8,128)(2,1)} %refs_0_.3) | copy-start | bytes 786436
  26.5 1.4 %collective-permute-start.7 = (bf16[64,1024]{1,0:T(8,128)(2,1)S(1)}, bf16[64,1024]{1,0:T(8,128)(2,1)S(1)}, u32[]{:S(2)}, u32[]{:S(2)}) collective-permute-start(bf16[64,1024]{1,0:T(8,128)(2,1)S(1)} %get-tuple-element.65), channel_id=1, source_target_pairs={{0,1},{1,0},{2,3},{3,2},{4,5},{5,4},{6,7},{7,6},{8,9},{9,8},{10,11... | collective-permute-start | bytes 393224 | tf_op jit(solution)/shard_map/ppermute | solution.py:214
  27.9 5.5 %collective-permute-start.10 = (bf16[64,1024]{1,0:T(8,128)(2,1)S(1)}, bf16[64,1024]{1,0:T(8,128)(2,1)S(1)}, u32[]{:S(2)}, u32[]{:S(2)}) collective-permute-start(bf16[64,1024]{1,0:T(8,128)(2,1)S(1)} %get-tuple-element.69), channel_id=1, source_target_pairs={{0,12},{1,5},{2,14},{3,7},{4,0},{5,9},{6,2},{7,11},{8,4},{9,13},{1... | collective-permute-start | bytes 393224 | tf_op jit(solution)/shard_map/ppermute | solution.py:214
  30.2 4.9 %collective-permute-start.11 = (bf16[32,1024]{1,0:T(8,128)(2,1)S(1)}, bf16[32,1024]{1,0:T(8,128)(2,1)S(1)}, u32[]{:S(2)}, u32[]{:S(2)}) collective-permute-start(bf16[32,1024]{1,0:T(8,128)(2,1)S(1)} %get-tuple-element.70), channel_id=1, source_target_pairs={{0,14},{1,3},{2,0},{3,5},{4,2},{5,7},{6,4},{7,9},{8,6},{9,11},{10,... | collective-permute-start | bytes 196616 | tf_op jit(solution)/shard_map/ppermute | solution.py:214
  33.4 8.6 %collective-permute-start.12 = (bf16[64,1024]{1,0:T(8,128)(2,1)S(1)}, bf16[64,1024]{1,0:T(8,128)(2,1)S(1)}, u32[]{:S(2)}, u32[]{:S(2)}) collective-permute-start(bf16[64,1024]{1,0:T(8,128)(2,1)S(1)} %collective-permute-done.10.refs_10_), channel_id=1, source_target_pairs={{0,1},{1,0},{2,3},{3,2},{4,5},{5,4},{6,7},{7,6},{8,9},{9,8},{10,11... | collective-permute-start | bytes 393224 | tf_op jit(solution)/shard_map/ppermute | solution.py:214
  35.1 6.9 %collective-permute-start.13 = (bf16[32,1024]{1,0:T(8,128)(2,1)S(1)}, bf16[32,1024]{1,0:T(8,128)(2,1)S(1)}, u32[]{:S(2)}, u32[]{:S(2)}) collective-permute-start(bf16[32,1024]{1,0:T(8,128)(2,1)S(1)} %collective-permute-done.11.refs_11_), channel_id=1, source_target_pairs={{0,1},{1,0},{2,3},{3,2},{4,5},{5,4},{6,7},{7,6},{8,9},{9,8},{10,11... | collective-permute-start | bytes 196616 | tf_op jit(solution)/shard_map/ppermute | solution.py:214
  35.6 4.8 %collective-permute-start.8 = (bf16[16,1024]{1,0:T(8,128)(2,1)S(1)}, bf16[16,1024]{1,0:T(8,128)(2,1)S(1)}, u32[]{:S(2)}, u32[]{:S(2)}) collective-permute-start(bf16[16,1024]{1,0:T(8,128)(2,1)S(1)} %get-tuple-element.66), channel_id=1, source_target_pairs={{0,8},{1,9},{2,10},{3,11},{4,12},{5,13},{6,14},{7,15},{8,0},{9,1},... | collective-permute-start | bytes 98312 | tf_op jit(solution)/shard_map/ppermute | solution.py:214
  36.3 5.7 %collective-permute-start.9 = (bf16[16,1024]{1,0:T(8,128)(2,1)S(1)}, bf16[16,1024]{1,0:T(8,128)(2,1)S(1)}, u32[]{:S(2)}, u32[]{:S(2)}) collective-permute-start(bf16[16,1024]{1,0:T(8,128)(2,1)S(1)} %get-tuple-element.67), channel_id=1, source_target_pairs={{0,11},{1,6},{2,13},{3,8},{4,15},{5,10},{6,1},{7,12},{8,3},{9,14},... | collective-permute-start | bytes 98312 | tf_op jit(solution)/shard_map/ppermute | solution.py:214
  48.0 1.3 %collective-permute-start.14 = (bf16[64,512]{1,0:T(8,128)(2,1)S(1)}, bf16[64,512]{1,0:T(8,128)(2,1)S(1)}, u32[]{:S(2)}, u32[]{:S(2)}) collective-permute-start(bf16[64,512]{1,0:T(8,128)(2,1)S(1)} %get-tuple-element.84), channel_id=1, source_target_pairs={{0,1},{1,0},{2,3},{3,2},{4,5},{5,4},{6,7},{7,6},{8,9},{9,8},{10,11... | collective-permute-start | bytes 196616 | tf_op jit(solution)/shard_map/ppermute | solution.py:214
  49.3 4.3 %collective-permute-start.17 = (bf16[64,512]{1,0:T(8,128)(2,1)S(1)}, bf16[64,512]{1,0:T(8,128)(2,1)S(1)}, u32[]{:S(2)}, u32[]{:S(2)}) collective-permute-start(bf16[64,512]{1,0:T(8,128)(2,1)S(1)} %get-tuple-element.88), channel_id=1, source_target_pairs={{0,12},{1,5},{2,14},{3,7},{4,0},{5,9},{6,2},{7,11},{8,4},{9,13},{1... | collective-permute-start | bytes 196616 | tf_op jit(solution)/shard_map/ppermute | solution.py:214
  51.3 6.7 %collective-permute-start.18 = (bf16[32,512]{1,0:T(8,128)(2,1)S(1)}, bf16[32,512]{1,0:T(8,128)(2,1)S(1)}, u32[]{:S(2)}, u32[]{:S(2)}) collective-permute-start(bf16[32,512]{1,0:T(8,128)(2,1)S(1)} %get-tuple-element.89), channel_id=1, source_target_pairs={{0,14},{1,3},{2,0},{3,5},{4,2},{5,7},{6,4},{7,9},{8,6},{9,11},{10,... | collective-permute-start | bytes 98312 | tf_op jit(solution)/shard_map/ppermute | solution.py:214
  53.6 7.2 %collective-permute-start.19 = (bf16[64,512]{1,0:T(8,128)(2,1)S(1)}, bf16[64,512]{1,0:T(8,128)(2,1)S(1)}, u32[]{:S(2)}, u32[]{:S(2)}) collective-permute-start(bf16[64,512]{1,0:T(8,128)(2,1)S(1)} %collective-permute-done.17.refs_3_), channel_id=1, source_target_pairs={{0,1},{1,0},{2,3},{3,2},{4,5},{5,4},{6,7},{7,6},{8,9},{9,8},{10,11... | collective-permute-start | bytes 196616 | tf_op jit(solution)/shard_map/ppermute | solution.py:214
  55.0 5.2 %collective-permute-start.15 = (bf16[16,512]{1,0:T(8,128)(2,1)S(1)}, bf16[16,512]{1,0:T(8,128)(2,1)S(1)}, u32[]{:S(2)}, u32[]{:S(2)}) collective-permute-start(bf16[16,512]{1,0:T(8,128)(2,1)S(1)} %get-tuple-element.85), channel_id=1, source_target_pairs={{0,8},{1,9},{2,10},{3,11},{4,12},{5,13},{6,14},{7,15},{8,0},{9,1},... | collective-permute-start | bytes 49160 | tf_op jit(solution)/shard_map/ppermute | solution.py:214
  55.9 5.0 %collective-permute-start.16 = (bf16[16,512]{1,0:T(8,128)(2,1)S(1)}, bf16[16,512]{1,0:T(8,128)(2,1)S(1)}, u32[]{:S(2)}, u32[]{:S(2)}) collective-permute-start(bf16[16,512]{1,0:T(8,128)(2,1)S(1)} %get-tuple-element.86), channel_id=1, source_target_pairs={{0,11},{1,6},{2,13},{3,8},{4,15},{5,10},{6,1},{7,12},{8,3},{9,14},... | collective-permute-start | bytes 49160 | tf_op jit(solution)/shard_map/ppermute | solution.py:214
  58.0 2.9 %collective-permute-start.20 = (bf16[32,512]{1,0:T(8,128)(2,1)S(1)}, bf16[32,512]{1,0:T(8,128)(2,1)S(1)}, u32[]{:S(2)}, u32[]{:S(2)}) collective-permute-start(bf16[32,512]{1,0:T(8,128)(2,1)S(1)} %collective-permute-done.18.refs_4_), channel_id=1, source_target_pairs={{0,1},{1,0},{2,3},{3,2},{4,5},{5,4},{6,7},{7,6},{8,9},{9,8},{10,11... | collective-permute-start | bytes 98312 | tf_op jit(solution)/shard_map/ppermute | solution.py:214
  (9 other events, 71.3 us)

commit v5 on v4

--- a/solution.py
+++ b/solution.py
@@ -111,7 +111,7 @@
         return self.target[key]
 
 
-def call(body, name, inputs, outputs, scratch=(), flops=0):
+def call(body, name, inputs, outputs, scratch=(), flops=0, loads=()):
     arrays, specs, moved, fetches = [], [], 0, []
     for place, entry in enumerate(inputs):
         if isinstance(entry, tuple):
@@ -126,31 +126,49 @@
             specs.append(pl.BlockSpec(memory_space=pltpu.VMEM))
             moved += array.size * array.dtype.itemsize
         arrays.append(array)
+    for array in loads:
+        arrays.append(pltpu.with_memory_space_constraint(array, pltpu.HBM))
+        specs.append(pl.BlockSpec(memory_space=pltpu.HBM))
     shapes = [jax.ShapeDtypeStruct(shape, dtype) for shape, dtype in outputs]
+    shapes += [jax.ShapeDtypeStruct(array.shape, array.dtype) for array in loads]
     for shape in shapes:
         moved += shape.size * shape.dtype.itemsize
     buffers = [pltpu.VMEM(shape, dtype) for _, _, _, shape, dtype in fetches]
+    load_semaphores = [pltpu.SemaphoreType.DMA((len(loads),))] if loads else []
     if fetches:
         buffers.append(pltpu.SemaphoreType.DMA((len(fetches),)))
 
     def kernel(*refs):
         refs = list(refs)
-        if not fetches:
-            body(*refs)
-            return
-        refs, targets, semaphores = (
-            refs[: -len(buffers)],
-            refs[-len(buffers) : -1],
-            refs[-1],
-        )
         waiting = []
+        targets, semaphores = [], None
+        load_semaphore = refs.pop() if loads else None
+        if fetches:
+            refs, targets, semaphores = (
+                refs[: -len(buffers)],
+                refs[-len(buffers) : -1],
+                refs[-1],
+            )
         for slot, (place, first, rows, shape, _) in enumerate(fetches):
             source = refs[place]
             if source.shape != shape:
                 source = source.at[pl.ds(first, rows)]
             refs[place] = Fetched(source, targets[slot], semaphores.at[slot])
             waiting.append(refs[place])
-        body(*refs)
+        first_load, last_out = len(inputs), len(arrays) + len(shapes)
+        for slot in range(len(loads)):
+            waiting.append(
+                Fetched(
+                    refs[first_load + slot],
+                    refs[last_out - len(loads) + slot],
+                    load_semaphore.at[slot],
+                )
+            )
+        body(
+            *refs[:first_load],
+            *refs[len(arrays) : last_out - len(loads)],
+            *refs[last_out:],
+        )
         for fetched in waiting:
             fetched.land()
 
@@ -160,7 +178,9 @@
         in_specs=specs,
         out_specs=[pl.BlockSpec(memory_space=pltpu.VMEM) for _ in shapes],
         out_shape=shapes,
-        scratch_shapes=[pltpu.VMEM(shape, dtype) for shape, dtype in scratch] + buffers,
+        scratch_shapes=[pltpu.VMEM(shape, dtype) for shape, dtype in scratch]
+        + buffers
+        + load_semaphores,
         compiler_params=pltpu.CompilerParams(vmem_limit_bytes=VMEM_LIMIT),
         cost_estimate=pl.CostEstimate(flops=flops, bytes_accessed=moved, transcendentals=0),
     )(*arrays)
@@ -213,7 +233,8 @@
         steps = (even_step, odd_step)
         return lax.ppermute(part, "tile", [(s, (s + steps[s % 2]) % peer_count) for s in peers])
 
-    def lay_together(kept_ref, got_ref, next_ref, second_ref):
+    def lay_together(kept_ref, got_ref, *rest):
+        next_ref, second_ref = rest[-2:]
         next_ref[:width, :] = kept_ref[:width, :]
         next_ref[width:, :] = got_ref[width : 2 * width, :]
         second_ref[:width, :] = kept_ref[width : 2 * width, :]
@@ -221,7 +242,7 @@
         second_ref[2 * width : 3 * width, :] = kept_ref[2 * width :, :]
         second_ref[3 * width :, :] = got_ref[2 * width : 3 * width, :]
 
-    def exchange(parts):
+    def exchange(parts, first_work=(), second_work=()):
         for_partner, three_off, opposite, kept = parts
         columns = kept.shape[1]
         got = permute(for_partner, 1, -1)
@@ -230,14 +251,23 @@
         next_chip, second_chip = call(
             lay_together,
             "lay_together",
-            [kept, got],
+            [kept, got, opposite, *first_work],
             [((2 * width, columns), BF16), ((4 * width, columns), BF16)],
         )
         second_chip = permute(second_chip, -4, 4)
         next_chip = permute(next_chip, -2, 2)
+        if second_work:
+            second_chip, next_chip, *second_work = lax.optimization_barrier(
+                (second_chip, next_chip, *second_work)
+            )
+        else:
+            second_chip, next_chip, three_off = lax.optimization_barrier(
+                (second_chip, next_chip, three_off)
+            )
         second_passed = permute(second_chip, 1, -1)
         next_passed = permute(next_chip, 1, -1)
-        return [got, opposite, three_off, second_chip, next_chip, second_passed, next_passed]
+        arrived = [got, opposite, three_off, second_chip, next_chip, second_passed, next_passed]
+        return arrived, list(second_work)
 
     arrived_count = 7
 
@@ -331,81 +361,103 @@
         [((slots_pad, grid_count), BF16)] + sent_shapes(2 * feat),
         flops=4 * slots * grid_count * feat,
     )
-    arrived = exchange(outgoing)
-
-    def local(
+    def tables(
         select_ref,
-        nodes_ref,
-        mesh_ref,
-        enc_edges_ref,
-        dec_edges_ref,
-        enc_wg_ref,
-        enc_wm_ref,
-        enc_we_ref,
-        dec_wg_ref,
-        dec_we_ref,
-        mesh_wn_ref,
         enc_grid_ref,
         enc_mesh_ref,
         dec_grid_ref,
         dec_mesh_ref,
         select_t_ref,
-        enc_part_ref,
-        dec_part_ref,
-        mesh_part_ref,
         enc_pick_ref,
         enc_pool_ref,
         dec_pick_ref,
         dec_pool_ref,
-        table_ref,
     ):
+        select_t_ref[...] = select_ref[...].astype(F32).T.astype(BF16)
         onehot_pair(enc_grid_ref, enc_mesh_ref, spots, enc_pick_ref, enc_pool_ref)
         onehot_pair(dec_grid_ref, dec_mesh_ref, spots, dec_pick_ref, dec_pool_ref)
-        select_t_ref[...] = select_ref[...].astype(F32).T.astype(BF16)
-        nodes = nodes_ref[...]
-        mesh_part_ref[...] = mm(mesh_ref[...], mesh_wn_ref[...])
-        table_ref[:grid_count, :] = mm(nodes, enc_wg_ref[...]).astype(BF16)
-        table_ref[grid_count:, :] = jnp.zeros((total - grid_count, feat), BF16)
-        table_ref[mesh_rows, :] = mm(mesh_ref[...], enc_wm_ref[...]).astype(BF16)
-        enc_part_ref[...] = mm(enc_edges_ref[...], enc_we_ref[...])
-        enc_part_ref[...] += mm(enc_pick_ref[...], table_ref[...])
-        pd = mm(nodes, dec_wg_ref[...]).astype(BF16)
-        dec_part_ref[...] = mm(dec_edges_ref[...], dec_we_ref[...])
-        dec_part_ref[...] += mm(dec_pick_ref[:, :grid_count], pd)
-
-    select_t, enc_part, dec_part, mesh_part, enc_pick, enc_pool, dec_pick, dec_pool = call(
-        local,
-        "local_products",
+
+    (
+        select_t,
+        enc_pick,
+        enc_pool,
+        dec_pick,
+        dec_pool,
+        enc_first,
+        enc_edges,
+        mesh_first,
+        grid_rows,
+        mesh_nodes,
+        dec_first,
+        dec_edges,
+    ) = call(
+        tables,
+        "index_tables",
         [
             select,
-            (grid_nodes, 0, grid_count),
-            (mesh_nodes, 0, mesh_count),
-            (enc_edges, 0, enc_count),
-            (dec_edges, 0, dec_count),
-            (enc_first, 0, feat),
-            (enc_first, feat, feat),
-            (enc_first, 2 * feat, feat),
-            (dec_first, 0, feat),
-            (dec_first, 2 * feat, feat),
-            (mesh_first, 0, feat),
-            (enc_grid, 0, enc_grid.shape[0]),
-            (enc_mesh, 0, enc_mesh.shape[0]),
-            (dec_grid, 0, dec_grid.shape[0]),
-            (dec_mesh, 0, dec_mesh.shape[0]),
+            (enc_grid, 0, enc_count),
+            (enc_mesh, 0, enc_count),
+            (dec_grid, 0, dec_count),
+            (dec_mesh, 0, dec_count),
         ],
         [
             ((grid_count, slots_pad), BF16),
-            ((enc_count, feat), F32),
-            ((dec_count, feat), F32),
-            ((mesh_count, feat), F32),
             ((enc_count, total), BF16),
             ((total, enc_count), BF16),
             ((dec_count, total), BF16),
             ((total, dec_count), BF16),
         ],
+        loads=[
+            enc_first,
+            enc_edges,
+            mesh_first,
+            grid_nodes,
+            mesh_nodes,
+            dec_first,
+            dec_edges,
+        ],
+    )
+
+    def enc_local(
+        nodes_ref,
+        mesh_ref,
+        enc_edges_ref,
+        enc_first_ref,
+        mesh_first_ref,
+        enc_pick_ref,
+        enc_part_ref,
+        mesh_part_ref,
+        table_ref,
+    ):
+        table_ref[:grid_count, :] = mm(nodes_ref[...], enc_first_ref[low, :]).astype(BF16)
+        table_ref[grid_count:, :] = jnp.zeros((total - grid_count, feat), BF16)
+        table_ref[mesh_rows, :] = mm(mesh_ref[...], enc_first_ref[high, :]).astype(BF16)
+        enc_part_ref[...] = mm(enc_edges_ref[...], enc_first_ref[2 * feat :, :])
+        enc_part_ref[...] += mm(enc_pick_ref[...], table_ref[...])
+        mesh_part_ref[...] = mm(mesh_ref[...], mesh_first_ref[low, :])
+
+    enc_part, mesh_part = call(
+        enc_local,
+        "enc_local_products",
+        [grid_rows, mesh_nodes, enc_edges, enc_first, mesh_first, enc_pick],
+        [((enc_count, feat), F32), ((mesh_count, feat), F32)],
         scratch=[((total, feat), BF16)],
-        flops=2 * feat * (feat * (2 * grid_count + enc_count + dec_count) + total * dec_count),
-    )
+        flops=2 * feat * feat * (grid_count + 2 * enc_count),
+    )
+
+    def dec_local(nodes_ref, dec_edges_ref, dec_first_ref, dec_pick_ref, dec_part_ref):
+        pd = mm(nodes_ref[...], dec_first_ref[low, :]).astype(BF16)
+        dec_part_ref[...] = mm(dec_edges_ref[...], dec_first_ref[2 * feat :, :])
+        dec_part_ref[...] += mm(dec_pick_ref[:, :grid_count], pd)
+
+    (dec_part,) = call(
+        dec_local,
+        "dec_local_products",
+        [grid_rows, dec_edges, dec_first, dec_pick],
+        [((dec_count, feat), F32)],
+        flops=2 * feat * feat * (grid_count + 2 * dec_count),
+    )
+    arrived, (enc_part, mesh_part) = exchange(outgoing, [select_t], [enc_part, mesh_part])
 
     def forward(*refs):
         arrived_refs, refs = refs[:arrived_count], refs[arrived_count:]
@@ -518,7 +570,7 @@
     )
     outgoing, results = results[:sent_count], results[sent_count:]
     mesh_out, spot_msg, *saved = results
-    returned = exchange(outgoing)
+    returned, _ = exchange(outgoing)
 
     def node_part(*refs):
         arrived_refs = refs[:arrived_count]
@@ -529,7 +581,7 @@
     (grid_part,) = call(
         node_part,
         "node_products",
-        [*arrived, grid_nodes, grid_first],
+        [*arrived, grid_rows, grid_first],
         [((spots, feat), F32)],
         flops=2 * spots * feat * feat,
     )
@@ -639,7 +691,7 @@
             spot_msg,
             grid_part,
             select_t,
-            grid_nodes,
+            grid_rows,
             grid_cot,
             mesh_cot,
             enc_pick,
@@ -677,7 +729,7 @@
     )
     outgoing, results = results[:sent_count], results[sent_count:]
     grid_out, grid_gpre, gpe, gpd, mesh_gin, mesh_gpre, mesh_pool = results
-    final = exchange(outgoing)
+    final, _ = exchange(outgoing)
 
     def tail(
         cot_ref,

time: 62.1 us -> 64.5 us (1.039)
  waiting for transfers between devices: 11.3 us -> 23.6 us
  starting transfers between devices: 30.1 us -> 21.4 us
  Pallas kernels: 19.6 us -> 18.5 us
    ppermute x21, waiting for transfers between devices: 11.3 us -> 23.6 us  [permute(): lax.ppermute(part, 'tile', [(s, (s + steps[s % 2]) % peer_count) for s in...]
    ppermute x21, starting transfers between devices: 30.1 us -> 21.4 us  [permute(): lax.ppermute(part, 'tile', [(s, (s + steps[s % 2]) % peer_count) for s in...]
    pallas_call x10 -> x12, Pallas kernels: 19.6 us -> 18.5 us  [call(): pl.pallas_call(kernel, name=name, in_specs=specs, out_specs=[pl.BlockSpec...]
  transfers between devices with their start and end apart: 21 -> 21, of which waited for: 9 -> 7; matrix products, arithmetic and copies ran while one was open for 0% -> 0% of each run, Pallas kernels for 12% -> 10%
where the time goes in v5:
time: 64.5 us; the launch traced here: 64.3 us
  waiting for transfers between devices  23.6 us (37%)
  starting transfers between devices  21.4 us (33%)
  Pallas kernels  18.5 us (29%)
  between operations  0.8 us (1%)
    ppermute x21, waiting for transfers between devices, permute(): lax.ppermute(part, 'tile', [(s, (s + steps[s % 2]) % peer_count) for s in...  23.6 us
    ppermute x21, starting transfers between devices, permute(): lax.ppermute(part, 'tile', [(s, (s + steps[s % 2]) % peer_count) for s in...  21.4 us
    pallas_call x12, Pallas kernels, call(): pl.pallas_call(kernel, name=name, in_specs=specs, out_specs=[pl.BlockSpec...  18.5 us
  transfers between devices with their start and end apart: 21, of which 7 were waited for; matrix products, arithmetic and copies ran while one was open for 0% of the time, Pallas kernels for 10%

profile of v5, /device:TPU:0, one launch (start us, length us, event | category | flops | bytes accessed | tf_op | source)
XLA Modules:
  0.0 64.3 jit_solution(15689905148044960294)
XLA Ops:
  0.6 1.4 %pack_rows.1 = (bf16[256,256]{1,0:T(8,128)(2,1)S(1)}, bf16[64,1024]{1,0:T(8,128)(2,1)S(1)}, bf16[16,1024]{1,0:T(8,128)(2,1)S(1)}, bf16[16,1024]{1,0:T(8,128)(2,1)S(1)}, bf16[48,1024]{1,0:T(8,128)(2,1)S(1)}) custom-call(s32[9,16]{1,0:T(8,128)} %refs_0_.2, s32[9]{0:T(128)} %refs_1_.2, bf16[256,512]{1,0:T(8,128)(2,1)} %refs_8_.2, bf16[256,512]{1,0:T(8,128)(2,1)} %refs_0_.3), custom_call_target="tpu_custom_call" | custom-call | flops 75497472 | bytes 950884 | tf_op jit(solution)/shard_map/pack_rows/pallas_call | solution.py:175
  2.6 3.7 %collective-permute-start.1 = (bf16[16,1024]{1,0:T(8,128)(2,1)S(1)}, bf16[16,1024]{1,0:T(8,128)(2,1)S(1)}, u32[]{:S(2)}, u32[]{:S(2)}) collective-permute-start(bf16[16,1024]{1,0:T(8,128)(2,1)S(1)} %get-tuple-element.68), channel_id=1, source_target_pairs={{0,8},{1,9},{2,10},{3,11},{4,12},{5,13},{6,14},{7,15},{8,0},{9,1},... | collective-permute-start | bytes 98312 | tf_op jit(solution)/shard_map/ppermute | solution.py:234
  6.2 2.8 %index_tables.1 = (bf16[256,256]{1,0:T(8,128)(2,1)S(1)}, bf16[384,512]{1,0:T(8,128)(2,1)S(1)}, bf16[512,384]{1,0:T(8,128)(2,1)S(1)}, bf16[768,512]{1,0:T(8,128)(...) custom-call(bf16[256,256]{1,0:T(8,128)(2,1)S(1)} %get-tuple-element., ...), custom_call_target="tpu_custom_call" | custom-call | bytes 8332288 | tf_op jit(solution)/shard_map/index_tables/pallas_call | solution.py:175
  9.1 3.5 %collective-permute-start.3 = (bf16[64,1024]{1,0:T(8,128)(2,1)S(1)}, bf16[64,1024]{1,0:T(8,128)(2,1)S(1)}, u32[]{:S(2)}, u32[]{:S(2)}) collective-permute-start(bf16[64,1024]{1,0:T(8,128)(2,1)S(1)} %get-tuple-element.73), channel_id=1, source_target_pairs={{0,12},{1,5},{2,14},{3,7},{4,0},{5,9},{6,2},{7,11},{8,4},{9,13},{1... | collective-permute-start | bytes 393224 | tf_op jit(solution)/shard_map/ppermute | solution.py:234
  12.6 1.0 %collective-permute-start.4 = (bf16[32,1024]{1,0:T(8,128)(2,1)S(1)}, bf16[32,1024]{1,0:T(8,128)(2,1)S(1)}, u32[]{:S(2)}, u32[]{:S(2)}) collective-permute-start(bf16[32,1024]{1,0:T(8,128)(2,1)S(1)} %get-tuple-element.74), channel_id=1, source_target_pairs={{0,14},{1,3},{2,0},{3,5},{4,2},{5,7},{6,4},{7,9},{8,6},{9,11},{10,... | collective-permute-start | bytes 196616 | tf_op jit(solution)/shard_map/ppermute | solution.py:234
  13.6 0.9 %enc_local_products.1 = (f32[384,512]{1,0:T(8,128)S(1)}, f32[64,512]{1,0:T(8,128)S(1)}) custom-call(bf16[256,512]{1,0:T(8,128)(2,1)S(1)} %get-tuple-element.75.refs_0_.refs_7_.refs_17_, bf16[64,512]{1,0:T(8,128)(2,1)S(1)} %get-tuple-element.76.refs_1_.refs_15_, bf16[384,512]{1,0:T(8,128)(2,1)S(1)} %get-tuple-element.77.refs_2_, ...), custom_call_target="tpu_custom_call" | custom-call | flops 536870912 | bytes 4653056 | tf_op jit(solution)/shard_map/enc_local_products/pallas_call | solution.py:175
  14.4 2.4 %collective-permute-done.4.refs_4_ = bf16[32,1024]{1,0:T(8,128)(2,1)S(1)} collective-permute-done((bf16[32,1024]{1,0:T(8,128)(2,1)S(1)}, bf16[32,1024]{1,0:T(8,128)(2,1)S(1)}, u32[]{:S(2)}, u32[]{:S(2)}) %collective-permute-start.4) | collective-permute-done | bytes 65568 | tf_op jit(solution)/shard_map/ppermute | solution.py:234
  16.8 1.1 %collective-permute-start.5 = (bf16[64,1024]{1,0:T(8,128)(2,1)S(1)}, bf16[64,1024]{1,0:T(8,128)(2,1)S(1)}, u32[]{:S(2)}, u32[]{:S(2)}) collective-permute-start(bf16[64,1024]{1,0:T(8,128)(2,1)S(1)} %collective-permute-done.3.refs_3_), channel_id=1, source_target_pairs={{0,1},{1,0},{2,3},{3,2},{4,5},{5,4},{6,7},{7,6},{8,9},{9,8},{10,11... | collective-permute-start | bytes 393224 | tf_op jit(solution)/shard_map/ppermute | solution.py:234
  18.0 0.8 %collective-permute-start.2 = (bf16[16,1024]{1,0:T(8,128)(2,1)S(1)}, bf16[16,1024]{1,0:T(8,128)(2,1)S(1)}, u32[]{:S(2)}, u32[]{:S(2)}) collective-permute-start(bf16[16,1024]{1,0:T(8,128)(2,1)S(1)} %get-tuple-element.69), channel_id=1, source_target_pairs={{0,11},{1,6},{2,13},{3,8},{4,15},{5,10},{6,1},{7,12},{8,3},{9,14},... | collective-permute-start | bytes 98312 | tf_op jit(solution)/shard_map/ppermute | solution.py:234
  18.8 0.9 %dec_local_products.1.refs_9_ = f32[768,512]{1,0:T(8,128)S(1)} custom-call(bf16[256,512]{1,0:T(8,128)(2,1)S(1)} %get-tuple-element.75.refs_0_.refs_7_.refs_17_, bf16[768,512]{1,0:T(8,128)(2,1)S(1)} %get-tuple-element.86.refs_1_, bf16[1536,512]{1,0:T(8,128)(2,1)S(1)} %get-tuple-element.87.refs_2_.refs_17_.refs_21_.refs_27_.refs_32_.refs_9_, ...), custom_call_target="tpu_custom_call" | custom-call | flops 939524096 | bytes 4980736 | tf_op jit(solution)/shard_map/dec_local_products/pallas_call | solution.py:175
  19.7 3.4 %collective-permute-done.2.refs_2_ = bf16[16,1024]{1,0:T(8,128)(2,1)S(1)} collective-permute-done((bf16[16,1024]{1,0:T(8,128)(2,1)S(1)}, bf16[16,1024]{1,0:T(8,128)(2,1)S(1)}, u32[]{:S(2)}, u32[]{:S(2)}) %collective-permute-start.2) | collective-permute-done | bytes 32800 | tf_op jit(solution)/shard_map/ppermute | solution.py:234
  23.2 3.6 %edges_forward.1 = (bf16[64,1024]{1,0:T(8,128)(2,1)S(1)}, bf16[16,1024]{1,0:T(8,128)(2,1)S(1)}, bf16[16,1024]{1,0:T(8,128)(2,1)S(1)}, bf16[48,1024]{1,0:T(8,128)...) custom-call(bf16[64,1024]{1,0:T(8,128)(2,1)S(1)} %collective-permute, ...), custom_call_target="tpu_custom_call" | custom-call | flops 1207959552 | bytes 16716544 | tf_op jit(solution)/shard_map/edges_forward/pallas_call | solution.py:175
  27.3 4.7 %collective-permute-done.8.refs_2_.refs_8_ = bf16[16,1024]{1,0:T(8,128)(2,1)S(1)} collective-permute-done((bf16[16,1024]{1,0:T(8,128)(2,1)S(1)}, bf16[16,1024]{1,0:T(8,128)(2,1)S(1)}, u32[]{:S(2)}, u32[]{:S(2)}) %collective-permute-start.8) | collective-permute-done | bytes 32800 | tf_op jit(solution)/shard_map/ppermute | solution.py:234
  32.0 2.5 %collective-permute-start.9 = (bf16[64,1024]{1,0:T(8,128)(2,1)S(1)}, bf16[64,1024]{1,0:T(8,128)(2,1)S(1)}, u32[]{:S(2)}, u32[]{:S(2)}) collective-permute-start(bf16[64,1024]{1,0:T(8,128)(2,1)S(1)} %get-tuple-element.95), channel_id=1, source_target_pairs={{0,12},{1,5},{2,14},{3,7},{4,0},{5,9},{6,2},{7,11},{8,4},{9,13},{1... | collective-permute-start | bytes 393224 | tf_op jit(solution)/shard_map/ppermute | solution.py:234
  35.3 1.0 %collective-permute-start.11 = (bf16[16,1024]{1,0:T(8,128)(2,1)S(1)}, bf16[16,1024]{1,0:T(8,128)(2,1)S(1)}, u32[]{:S(2)}, u32[]{:S(2)}) collective-permute-start(bf16[16,1024]{1,0:T(8,128)(2,1)S(1)} %get-tuple-element.97), channel_id=1, source_target_pairs={{0,11},{1,6},{2,13},{3,8},{4,15},{5,10},{6,1},{7,12},{8,3},{9,14},... | collective-permute-start | bytes 98312 | tf_op jit(solution)/shard_map/ppermute | solution.py:234
  36.3 4.7 %collective-permute-done.11.refs_9_ = bf16[16,1024]{1,0:T(8,128)(2,1)S(1)} collective-permute-done((bf16[16,1024]{1,0:T(8,128)(2,1)S(1)}, bf16[16,1024]{1,0:T(8,128)(2,1)S(1)}, u32[]{:S(2)}, u32[]{:S(2)}) %collective-permute-start.11) | collective-permute-done | bytes 32800 | tf_op jit(solution)/shard_map/ppermute | solution.py:234
  42.5 6.0 %edges_backward.1 = (bf16[64,512]{1,0:T(8,128)(2,1)S(1)}, bf16[16,512]{1,0:T(8,128)(2,1)S(1)}, bf16[16,512]{1,0:T(8,128)(2,1)S(1)}, bf16[48,512]{1,0:T(8,128)(2,...) custom-call(bf16[64,1024]{1,0:T(8,128)(2,1)S(1)} %collective-permute, ...), custom_call_target="tpu_custom_call" | custom-call | flops 2449473536 | bytes 18830080 | tf_op jit(solution)/shard_map/edges_backward/pallas_call | solution.py:175
  48.8 1.4 %collective-permute-start.15 = (bf16[16,512]{1,0:T(8,128)(2,1)S(1)}, bf16[16,512]{1,0:T(8,128)(2,1)S(1)}, u32[]{:S(2)}, u32[]{:S(2)}) collective-permute-start(bf16[16,512]{1,0:T(8,128)(2,1)S(1)} %get-tuple-element.114), channel_id=1, source_target_pairs={{0,8},{1,9},{2,10},{3,11},{4,12},{5,13},{6,14},{7,15},{8,0},{9,1},... | collective-permute-start | bytes 49160 | tf_op jit(solution)/shard_map/ppermute | solution.py:234
  50.2 3.5 %collective-permute-done.15.refs_2_.refs_1_ = bf16[16,512]{1,0:T(8,128)(2,1)S(1)} collective-permute-done((bf16[16,512]{1,0:T(8,128)(2,1)S(1)}, bf16[16,512]{1,0:T(8,128)(2,1)S(1)}, u32[]{:S(2)}, u32[]{:S(2)}) %collective-permute-start.15) | collective-permute-done | bytes 16416 | tf_op jit(solution)/shard_map/ppermute | solution.py:234
  53.7 1.5 %collective-permute-start.16 = (bf16[64,512]{1,0:T(8,128)(2,1)S(1)}, bf16[64,512]{1,0:T(8,128)(2,1)S(1)}, u32[]{:S(2)}, u32[]{:S(2)}) collective-permute-start(bf16[64,512]{1,0:T(8,128)(2,1)S(1)} %get-tuple-element.116), channel_id=1, source_target_pairs={{0,12},{1,5},{2,14},{3,7},{4,0},{5,9},{6,2},{7,11},{8,4},{9,13},{1... | collective-permute-start | bytes 196616 | tf_op jit(solution)/shard_map/ppermute | solution.py:234
  55.2 1.1 %collective-permute-start.17 = (bf16[32,512]{1,0:T(8,128)(2,1)S(1)}, bf16[32,512]{1,0:T(8,128)(2,1)S(1)}, u32[]{:S(2)}, u32[]{:S(2)}) collective-permute-start(bf16[32,512]{1,0:T(8,128)(2,1)S(1)} %get-tuple-element.117), channel_id=1, source_target_pairs={{0,14},{1,3},{2,0},{3,5},{4,2},{5,7},{6,4},{7,9},{8,6},{9,11},{10,... | collective-permute-start | bytes 98312 | tf_op jit(solution)/shard_map/ppermute | solution.py:234
  56.9 4.4 %collective-permute-done.18.refs_2_ = bf16[16,512]{1,0:T(8,128)(2,1)S(1)} collective-permute-done((bf16[16,512]{1,0:T(8,128)(2,1)S(1)}, bf16[16,512]{1,0:T(8,128)(2,1)S(1)}, u32[]{:S(2)}, u32[]{:S(2)}) %collective-permute-start.18) | collective-permute-done | bytes 16416 | tf_op jit(solution)/shard_map/ppermute | solution.py:234
  61.8 1.5 %local_gradients.1 = (f32[256,512]{1,0:T(8,128)S(1)}, f32[64,512]{1,0:T(8,128)}) custom-call(bf16[256,512]{1,0:T(8,128)(2,1)S(1)} %copy-done.1, bf16[256,512]{1,0:T(8,128)(2,1)S(1)} %get-tuple-element.122.refs_1_, bf16[256,512]{1,0:T(8,128)(2,1)S(1)} %get-tuple-element.123.refs_2_, bf16[256,512]{1,0:T(8,128)(2,1)S(1)} %get-tuple-element.124.refs_3_, ...), custom_call_target="tpu_custom_call" | custom-call | flops 402653184 | bytes 8781824 | tf_op jit(solution)/shard_map/local_gradients/pallas_call | solution.py:175
  63.3 1.0 %add_returned.1 = f32[256,512]{1,0:T(8,128)} custom-call(bf16[64,512]{1,0:T(8,128)(2,1)S(1)} %collective-permute-done.14.refs_1_.refs_0_, bf16[16,512]{1,0:T(8,128)(2,1)S(1)} %collective-permute-done.15.refs_2_.refs_1_, bf16[16,512]{1,0:T(8,128)(2,1)S(1)} %collective-permute-done.18.refs_2_, bf16[64,512]{1,0:T(8,128)(2,1)S(1)} %collective-permute-done.16.refs_3_, ...), custom_call_target="tpu_custom_call" | custom-call | flops 37748736 | bytes 1474560 | tf_op jit(solution)/shard_map/add_returned/pallas_call | solution.py:175
  (44 shorter events, 4.8 us)
Async XLA Ops:
  2.0 7.0 %collective-permute-start = (bf16[64,1024]{1,0:T(8,128)(2,1)S(1)}, bf16[64,1024]{1,0:T(8,128)(2,1)S(1)}, u32[]{:S(2)}, u32[]{:S(2)}) collective-permute-start(bf16[64,1024]{1,0:T(8,128)(2,1)S(1)} %get-tuple-element.67), channel_id=1, source_target_pairs={{0,1},{1,0},{2,3},{3,2},{4,5},{5,4},{6,7},{7,6},{8,9},{9,8},{10,11... | collective-permute-start | bytes 393224 | tf_op jit(solution)/shard_map/ppermute | solution.py:234
  2.6 6.5 %collective-permute-start.1 = (bf16[16,1024]{1,0:T(8,128)(2,1)S(1)}, bf16[16,1024]{1,0:T(8,128)(2,1)S(1)}, u32[]{:S(2)}, u32[]{:S(2)}) collective-permute-start(bf16[16,1024]{1,0:T(8,128)(2,1)S(1)} %get-tuple-element.68), channel_id=1, source_target_pairs={{0,8},{1,9},{2,10},{3,11},{4,12},{5,13},{6,14},{7,15},{8,0},{9,1},... | collective-permute-start | bytes 98312 | tf_op jit(solution)/shard_map/ppermute | solution.py:234
  9.1 7.7 %collective-permute-start.3 = (bf16[64,1024]{1,0:T(8,128)(2,1)S(1)}, bf16[64,1024]{1,0:T(8,128)(2,1)S(1)}, u32[]{:S(2)}, u32[]{:S(2)}) collective-permute-start(bf16[64,1024]{1,0:T(8,128)(2,1)S(1)} %get-tuple-element.73), channel_id=1, source_target_pairs={{0,12},{1,5},{2,14},{3,7},{4,0},{5,9},{6,2},{7,11},{8,4},{9,13},{1... | collective-permute-start | bytes 393224 | tf_op jit(solution)/shard_map/ppermute | solution.py:234
  12.6 4.3 %collective-permute-start.4 = (bf16[32,1024]{1,0:T(8,128)(2,1)S(1)}, bf16[32,1024]{1,0:T(8,128)(2,1)S(1)}, u32[]{:S(2)}, u32[]{:S(2)}) collective-permute-start(bf16[32,1024]{1,0:T(8,128)(2,1)S(1)} %get-tuple-element.74), channel_id=1, source_target_pairs={{0,14},{1,3},{2,0},{3,5},{4,2},{5,7},{6,4},{7,9},{8,6},{9,11},{10,... | collective-permute-start | bytes 196616 | tf_op jit(solution)/shard_map/ppermute | solution.py:234
  16.8 6.3 %collective-permute-start.5 = (bf16[64,1024]{1,0:T(8,128)(2,1)S(1)}, bf16[64,1024]{1,0:T(8,128)(2,1)S(1)}, u32[]{:S(2)}, u32[]{:S(2)}) collective-permute-start(bf16[64,1024]{1,0:T(8,128)(2,1)S(1)} %collective-permute-done.3.refs_3_), channel_id=1, source_target_pairs={{0,1},{1,0},{2,3},{3,2},{4,5},{5,4},{6,7},{7,6},{8,9},{9,8},{10,11... | collective-permute-start | bytes 393224 | tf_op jit(solution)/shard_map/ppermute | solution.py:234
  18.0 5.2 %collective-permute-start.2 = (bf16[16,1024]{1,0:T(8,128)(2,1)S(1)}, bf16[16,1024]{1,0:T(8,128)(2,1)S(1)}, u32[]{:S(2)}, u32[]{:S(2)}) collective-permute-start(bf16[16,1024]{1,0:T(8,128)(2,1)S(1)} %get-tuple-element.69), channel_id=1, source_target_pairs={{0,11},{1,6},{2,13},{3,8},{4,15},{5,10},{6,1},{7,12},{8,3},{9,14},... | collective-permute-start | bytes 98312 | tf_op jit(solution)/shard_map/ppermute | solution.py:234
  18.8 4.4 %collective-permute-start.6 = (bf16[32,1024]{1,0:T(8,128)(2,1)S(1)}, bf16[32,1024]{1,0:T(8,128)(2,1)S(1)}, u32[]{:S(2)}, u32[]{:S(2)}) collective-permute-start(bf16[32,1024]{1,0:T(8,128)(2,1)S(1)} %collective-permute-done.4.refs_4_), channel_id=1, source_target_pairs={{0,1},{1,0},{2,3},{3,2},{4,5},{5,4},{6,7},{7,6},{8,9},{9,8},{10,11... | collective-permute-start | bytes 196616 | tf_op jit(solution)/shard_map/ppermute | solution.py:234
  23.2 18.4 %copy-start = (bf16[1024,512]{1,0:T(8,128)(2,1)S(1)}, bf16[1024,512]{1,0:T(8,128)(2,1)}, u32[]{:S(2)}) copy-start(bf16[1024,512]{1,0:T(8,128)(2,1)} %refs_7_.3) | copy-start | bytes 3145732
  26.8 15.7 %copy-start.1 = (bf16[256,512]{1,0:T(8,128)(2,1)S(1)}, bf16[256,512]{1,0:T(8,128)(2,1)}, u32[]{:S(2)}) copy-start(bf16[256,512]{1,0:T(8,128)(2,1)} %refs_0_.3) | copy-start | bytes 786436
  26.8 15.6 %copy-start.5 = (bf16[512,512]{1,0:T(8,128)(2,1)S(1)}, bf16[512,512]{1,0:T(8,128)(2,1)}, u32[]{:S(2)}) copy-start(bf16[512,512]{1,0:T(8,128)(2,1)} %refs_25_.1) | copy-start | bytes 1572868
  26.8 5.2 %collective-permute-start.7 = (bf16[64,1024]{1,0:T(8,128)(2,1)S(1)}, bf16[64,1024]{1,0:T(8,128)(2,1)S(1)}, u32[]{:S(2)}, u32[]{:S(2)}) collective-permute-start(bf16[64,1024]{1,0:T(8,128)(2,1)S(1)} %get-tuple-element.92), channel_id=1, source_target_pairs={{0,1},{1,0},{2,3},{3,2},{4,5},{5,4},{6,7},{7,6},{8,9},{9,8},{10,11... | collective-permute-start | bytes 393224 | tf_op jit(solution)/shard_map/ppermute | solution.py:234
  26.9 5.1 %collective-permute-start.8 = (bf16[16,1024]{1,0:T(8,128)(2,1)S(1)}, bf16[16,1024]{1,0:T(8,128)(2,1)S(1)}, u32[]{:S(2)}, u32[]{:S(2)}) collective-permute-start(bf16[16,1024]{1,0:T(8,128)(2,1)S(1)} %get-tuple-element.93), channel_id=1, source_target_pairs={{0,8},{1,9},{2,10},{3,11},{4,12},{5,13},{6,14},{7,15},{8,0},{9,1},... | collective-permute-start | bytes 98312 | tf_op jit(solution)/shard_map/ppermute | solution.py:234
  32.0 9.0 %collective-permute-start.9 = (bf16[64,1024]{1,0:T(8,128)(2,1)S(1)}, bf16[64,1024]{1,0:T(8,128)(2,1)S(1)}, u32[]{:S(2)}, u32[]{:S(2)}) collective-permute-start(bf16[64,1024]{1,0:T(8,128)(2,1)S(1)} %get-tuple-element.95), channel_id=1, source_target_pairs={{0,12},{1,5},{2,14},{3,7},{4,0},{5,9},{6,2},{7,11},{8,4},{9,13},{1... | collective-permute-start | bytes 393224 | tf_op jit(solution)/shard_map/ppermute | solution.py:234
  34.5 6.5 %collective-permute-start.10 = (bf16[32,1024]{1,0:T(8,128)(2,1)S(1)}, bf16[32,1024]{1,0:T(8,128)(2,1)S(1)}, u32[]{:S(2)}, u32[]{:S(2)}) collective-permute-start(bf16[32,1024]{1,0:T(8,128)(2,1)S(1)} %get-tuple-element.96), channel_id=1, source_target_pairs={{0,14},{1,3},{2,0},{3,5},{4,2},{5,7},{6,4},{7,9},{8,6},{9,11},{10,... | collective-permute-start | bytes 196616 | tf_op jit(solution)/shard_map/ppermute | solution.py:234
  35.3 5.7 %collective-permute-start.11 = (bf16[16,1024]{1,0:T(8,128)(2,1)S(1)}, bf16[16,1024]{1,0:T(8,128)(2,1)S(1)}, u32[]{:S(2)}, u32[]{:S(2)}) collective-permute-start(bf16[16,1024]{1,0:T(8,128)(2,1)S(1)} %get-tuple-element.97), channel_id=1, source_target_pairs={{0,11},{1,6},{2,13},{3,8},{4,15},{5,10},{6,1},{7,12},{8,3},{9,14},... | collective-permute-start | bytes 98312 | tf_op jit(solution)/shard_map/ppermute | solution.py:234
  41.0 1.4 %collective-permute-start.12 = (bf16[64,1024]{1,0:T(8,128)(2,1)S(1)}, bf16[64,1024]{1,0:T(8,128)(2,1)S(1)}, u32[]{:S(2)}, u32[]{:S(2)}) collective-permute-start(bf16[64,1024]{1,0:T(8,128)(2,1)S(1)} %collective-permute-done.9.refs_10_), channel_id=1, source_target_pairs={{0,1},{1,0},{2,3},{3,2},{4,5},{5,4},{6,7},{7,6},{8,9},{9,8},{10,11... | collective-permute-start | bytes 393224 | tf_op jit(solution)/shard_map/ppermute | solution.py:234
  41.2 1.3 %collective-permute-start.13 = (bf16[32,1024]{1,0:T(8,128)(2,1)S(1)}, bf16[32,1024]{1,0:T(8,128)(2,1)S(1)}, u32[]{:S(2)}, u32[]{:S(2)}) collective-permute-start(bf16[32,1024]{1,0:T(8,128)(2,1)S(1)} %collective-permute-done.10.refs_11_), channel_id=1, source_target_pairs={{0,1},{1,0},{2,3},{3,2},{4,5},{5,4},{6,7},{7,6},{8,9},{9,8},{10,11... | collective-permute-start | bytes 196616 | tf_op jit(solution)/shard_map/ppermute | solution.py:234
  48.5 5.2 %collective-permute-start.14 = (bf16[64,512]{1,0:T(8,128)(2,1)S(1)}, bf16[64,512]{1,0:T(8,128)(2,1)S(1)}, u32[]{:S(2)}, u32[]{:S(2)}) collective-permute-start(bf16[64,512]{1,0:T(8,128)(2,1)S(1)} %get-tuple-element.113), channel_id=1, source_target_pairs={{0,1},{1,0},{2,3},{3,2},{4,5},{5,4},{6,7},{7,6},{8,9},{9,8},{10,11... | collective-permute-start | bytes 196616 | tf_op jit(solution)/shard_map/ppermute | solution.py:234
  48.8 4.8 %collective-permute-start.15 = (bf16[16,512]{1,0:T(8,128)(2,1)S(1)}, bf16[16,512]{1,0:T(8,128)(2,1)S(1)}, u32[]{:S(2)}, u32[]{:S(2)}) collective-permute-start(bf16[16,512]{1,0:T(8,128)(2,1)S(1)} %get-tuple-element.114), channel_id=1, source_target_pairs={{0,8},{1,9},{2,10},{3,11},{4,12},{5,13},{6,14},{7,15},{8,0},{9,1},... | collective-permute-start | bytes 49160 | tf_op jit(solution)/shard_map/ppermute | solution.py:234
  53.7 7.6 %collective-permute-start.16 = (bf16[64,512]{1,0:T(8,128)(2,1)S(1)}, bf16[64,512]{1,0:T(8,128)(2,1)S(1)}, u32[]{:S(2)}, u32[]{:S(2)}) collective-permute-start(bf16[64,512]{1,0:T(8,128)(2,1)S(1)} %get-tuple-element.116), channel_id=1, source_target_pairs={{0,12},{1,5},{2,14},{3,7},{4,0},{5,9},{6,2},{7,11},{8,4},{9,13},{1... | collective-permute-start | bytes 196616 | tf_op jit(solution)/shard_map/ppermute | solution.py:234
  55.2 6.1 %collective-permute-start.17 = (bf16[32,512]{1,0:T(8,128)(2,1)S(1)}, bf16[32,512]{1,0:T(8,128)(2,1)S(1)}, u32[]{:S(2)}, u32[]{:S(2)}) collective-permute-start(bf16[32,512]{1,0:T(8,128)(2,1)S(1)} %get-tuple-element.117), channel_id=1, source_target_pairs={{0,14},{1,3},{2,0},{3,5},{4,2},{5,7},{6,4},{7,9},{8,6},{9,11},{10,... | collective-permute-start | bytes 98312 | tf_op jit(solution)/shard_map/ppermute | solution.py:234
  56.3 5.0 %collective-permute-start.18 = (bf16[16,512]{1,0:T(8,128)(2,1)S(1)}, bf16[16,512]{1,0:T(8,128)(2,1)S(1)}, u32[]{:S(2)}, u32[]{:S(2)}) collective-permute-start(bf16[16,512]{1,0:T(8,128)(2,1)S(1)} %get-tuple-element.118), channel_id=1, source_target_pairs={{0,11},{1,6},{2,13},{3,8},{4,15},{5,10},{6,1},{7,12},{8,3},{9,14},... | collective-permute-start | bytes 49160 | tf_op jit(solution)/shard_map/ppermute | solution.py:234
  61.3 2.0 %collective-permute-start.19 = (bf16[64,512]{1,0:T(8,128)(2,1)S(1)}, bf16[64,512]{1,0:T(8,128)(2,1)S(1)}, u32[]{:S(2)}, u32[]{:S(2)}) collective-permute-start(bf16[64,512]{1,0:T(8,128)(2,1)S(1)} %collective-permute-done.16.refs_3_), channel_id=1, source_target_pairs={{0,1},{1,0},{2,3},{3,2},{4,5},{5,4},{6,7},{7,6},{8,9},{9,8},{10,11... | collective-permute-start | bytes 196616 | tf_op jit(solution)/shard_map/ppermute | solution.py:234
  61.3 2.0 %collective-permute-start.20 = (bf16[32,512]{1,0:T(8,128)(2,1)S(1)}, bf16[32,512]{1,0:T(8,128)(2,1)S(1)}, u32[]{:S(2)}, u32[]{:S(2)}) collective-permute-start(bf16[32,512]{1,0:T(8,128)(2,1)S(1)} %collective-permute-done.17.refs_4_), channel_id=1, source_target_pairs={{0,1},{1,0},{2,3},{3,2},{4,5},{5,4},{6,7},{7,6},{8,9},{9,8},{10,11... | collective-permute-start | bytes 98312 | tf_op jit(solution)/shard_map/ppermute | solution.py:234
  (4 other events, 28.7 us)

commit v6 on v3

--- a/solution.py
+++ b/solution.py
@@ -75,23 +75,35 @@
     return forward_half + [-offset for offset in forward_half] + [peer_count // 2]
 
 
-def onehot_pair(spot_ref, mesh_ref, spots, by_edge_ref, by_spot_ref):
+def onehot_pair(spot_ref, mesh_ref, spots, mesh_count, by_edge_ref, by_spot_ref):
     edges, total = by_edge_ref.shape
     spot_row = spot_ref[...].reshape(1, -1).astype(F32)
     mesh_row = mesh_ref[...].reshape(1, -1).astype(F32) + float(spots)
-    for rows in row_chunks(total, 64):
-        ids = lax.broadcasted_iota(jnp.int32, (rows.stop - rows.start, edges), 0) + rows.start
-        ids = ids.astype(F32)
-        hit = (ids == spot_row) | (ids == mesh_row)
-        by_spot_ref[rows, :] = jnp.where(hit, 1.0, 0.0).astype(BF16)
+
+    def ids(shape, axis, start):
+        return (lax.broadcasted_iota(jnp.int32, shape, axis) + start).astype(F32)
+
+    def ones(hit):
+        return jnp.where(hit, 1.0, 0.0).astype(BF16)
+
+    for row, first, count in ((spot_row, 0, spots), (mesh_row, spots, mesh_count)):
+        for rows in row_chunks(count, 80):
+            rows = slice(rows.start + first, rows.stop + first)
+            shape = (rows.stop - rows.start, edges)
+            by_spot_ref[rows, :] = ones(ids(shape, 0, rows.start) == row)
+    by_spot_ref[spots + mesh_count :, :] = jnp.zeros((total - spots - mesh_count, edges), BF16)
     for rows in row_chunks(edges, 128):
         spot_col = jnp.broadcast_to(spot_row[:, rows], (128, 128)).T
         mesh_col = jnp.broadcast_to(mesh_row[:, rows], (128, 128)).T
         for columns in row_chunks(total, 128):
-            ids = lax.broadcasted_iota(jnp.int32, (128, 128), 1) + columns.start
-            ids = ids.astype(F32)
-            hit = (ids == spot_col) | (ids == mesh_col)
-            by_edge_ref[rows, columns] = jnp.where(hit, 1.0, 0.0).astype(BF16)
+            lane = ids((128, 128), 1, columns.start)
+            hit = None
+            if columns.start < spots:
+                hit = lane == spot_col
+            if columns.stop > spots:
+                mesh_hit = lane == mesh_col
+                hit = mesh_hit if hit is None else hit | mesh_hit
+            by_edge_ref[rows, columns] = ones(hit)
 
 
 class Fetched:
@@ -135,15 +147,10 @@
 
     def kernel(*refs):
         refs = list(refs)
-        if not fetches:
-            body(*refs)
-            return
-        refs, targets, semaphores = (
-            refs[: -len(buffers)],
-            refs[-len(buffers) : -1],
-            refs[-1],
-        )
         waiting = []
+        if fetches:
+            targets, semaphores = refs[-len(buffers) : -1], refs[-1]
+            refs = refs[: -len(buffers)]
         for slot, (place, first, rows, shape, _) in enumerate(fetches):
             source = refs[place]
             if source.shape != shape:
@@ -160,7 +167,8 @@
         in_specs=specs,
         out_specs=[pl.BlockSpec(memory_space=pltpu.VMEM) for _ in shapes],
         out_shape=shapes,
-        scratch_shapes=[pltpu.VMEM(shape, dtype) for shape, dtype in scratch] + buffers,
+        scratch_shapes=[pltpu.VMEM(shape, dtype) for shape, dtype in scratch]
+        + buffers,
         compiler_params=pltpu.CompilerParams(vmem_limit_bytes=VMEM_LIMIT),
         cost_estimate=pl.CostEstimate(flops=flops, bytes_accessed=moved, transcendentals=0),
     )(*arrays)
@@ -216,14 +224,15 @@
     def exchange(parts):
         plus_two, minus_two, own_chip, plus_one, minus_one, three_off, opposite = parts
         plus_two = permute(plus_two, 4, 4)
+        plus_one = permute(plus_one, 3, 1)
         minus_two = permute(minus_two, -4, -4)
-        own_chip = permute(own_chip, 1, -1)
-        plus_one = permute(plus_one, 3, 1)
         minus_one = permute(minus_one, -1, -3)
         three_off = permute(three_off, -5, 5)
         opposite = permute(opposite, peer_count // 2, peer_count // 2)
+        plus_two, own_chip = lax.optimization_barrier((plus_two, own_chip))
         plus_passed = permute(plus_two, 1, -1)
         minus_passed = permute(minus_two, 1, -1)
+        own_chip = permute(own_chip, 1, -1)
         return [
             plus_two,
             minus_two,
@@ -235,6 +244,8 @@
             plus_passed,
             minus_passed,
         ]
+
+    arrived_count = 9
 
     def sent_shapes(columns):
         rows = (2, 2, 1, 1, 1, 1, 1)
@@ -356,8 +367,8 @@
         dec_pool_ref,
         table_ref,
     ):
-        onehot_pair(enc_grid_ref, enc_mesh_ref, spots, enc_pick_ref, enc_pool_ref)
-        onehot_pair(dec_grid_ref, dec_mesh_ref, spots, dec_pick_ref, dec_pool_ref)
+        onehot_pair(enc_grid_ref, enc_mesh_ref, spots, mesh_count, enc_pick_ref, enc_pool_ref)
+        onehot_pair(dec_grid_ref, dec_mesh_ref, spots, mesh_count, dec_pick_ref, dec_pool_ref)
         select_t_ref[...] = select_ref[...].astype(F32).T.astype(BF16)
         nodes = nodes_ref[...]
         mesh_part_ref[...] = mm(mesh_ref[...], mesh_wn_ref[...])
@@ -405,7 +416,7 @@
     )
 
     def forward(*refs):
-        arrived_refs, refs = refs[:links], refs[links:]
+        arrived_refs, refs = refs[:arrived_count], refs[arrived_count:]
         (
             select_ref,
             enc_part_ref,
@@ -518,7 +529,8 @@
     returned = exchange(outgoing)
 
     def node_part(*refs):
-        arrived_refs, (nodes_ref, weight_ref, out_ref) = refs[:links], refs[links:]
+        arrived_refs = refs[:arrived_count]
+        nodes_ref, weight_ref, out_ref = refs[arrived_count:]
         out_ref[:grid_count, :] = mm(nodes_ref[...], weight_ref[low, :])
         out_ref[grid_count:, :] = mm(by_slot(arrived_refs, low), weight_ref[low, :])
 
@@ -527,11 +539,12 @@
         "node_products",
         [*arrived, grid_nodes, grid_first],
         [((spots, feat), F32)],
-        flops=2 * spots * feat * feat,
+        flops=16 * spots * feat * feat,
     )
 
     def backward(*refs):
-        arrived_refs, returned_refs, refs = refs[:links], refs[links : 2 * links], refs[2 * links :]
+        arrived_refs, refs = refs[:arrived_count], refs[arrived_count:]
+        returned_refs, refs = refs[:arrived_count], refs[arrived_count:]
         (
             spot_ref,
             grid_part_ref,
@@ -724,7 +737,8 @@
     )
 
     def finish(*refs):
-        back_refs, (base_ref, select_t_ref, out_ref) = refs[:links], refs[links:]
+        back_refs = refs[:arrived_count]
+        base_ref, select_t_ref, out_ref = refs[arrived_count:]
         out_ref[...] = base_ref[...] + mm(select_t_ref[:, :slots], by_row(back_refs))
 
     (grad_grid,) = call(

time: 62.1 us -> 57.5 us (0.926)
  waiting for transfers between devices: 11.3 us -> 7.44 us
    ppermute x27, waiting for transfers between devices: 11.3 us -> 7.44 us  [permute(): lax.ppermute(part, 'tile', [(s, (s + steps[s % 2]) % peer_count) for s in...]
  transfers between devices with their start and end apart: 27 -> 27, of which waited for: 8 -> 5; matrix products, arithmetic and copies ran while one was open for 0% -> 0% of each run, Pallas kernels for 12% -> 13%
where the time goes in v6:
time: 57.5 us; the launch traced here: 57.3 us
  starting transfers between devices  29.6 us (51%)
  Pallas kernels  19.3 us (34%)
  waiting for transfers between devices  7.44 us (13%)
  between operations  0.87 us (2%)
    ppermute x27, starting transfers between devices, permute(): lax.ppermute(part, 'tile', [(s, (s + steps[s % 2]) % peer_count) for s in...  29.6 us
    pallas_call x7, Pallas kernels, call(): pl.pallas_call(kernel, name=name, in_specs=specs, out_specs=[pl.BlockSpec...  19.3 us
    ppermute x27, waiting for transfers between devices, permute(): lax.ppermute(part, 'tile', [(s, (s + steps[s % 2]) % peer_count) for s in...  7.44 us
  transfers between devices with their start and end apart: 27, of which 5 were waited for; matrix products, arithmetic and copies ran while one was open for 0% of the time, Pallas kernels for 13%

profile of v6, /device:TPU:0, one launch (start us, length us, event | category | flops | bytes accessed | tf_op | source)
XLA Modules:
  0.0 57.3 jit_solution(577023944737817589)
XLA Ops:
  0.6 1.4 %pack_rows.1 = (bf16[256,256]{1,0:T(8,128)(2,1)S(1)}, bf16[32,1024]{1,0:T(8,128)(2,1)S(1)}, bf16[32,1024]{1,0:T(8,128)(2,1)S(1)}, bf16[16,1024]{1,0:T(8,128)(2,1...) custom-call(s32[9,16]{1,0:T(8,128)} %refs_0_.2, ...), custom_call_target="tpu_custom_call" | custom-call | flops 75497472 | bytes 950884 | tf_op jit(solution)/shard_map/pack_rows/pallas_call | solution.py:164
  2.1 3.1 %collective-permute-start = (bf16[32,1024]{1,0:T(8,128)(2,1)S(1)}, bf16[32,1024]{1,0:T(8,128)(2,1)S(1)}, u32[]{:S(2)}, u32[]{:S(2)}) collective-permute-start(bf16[32,1024]{1,0:T(8,128)(2,1)S(1)} %get-tuple-element.60), channel_id=1, source_target_pairs={{0,4},{1,5},{2,6},{3,7},{4,8},{5,9},{6,10},{7,11},{8,12},{9,13},{1... | collective-permute-start | bytes 196616 | tf_op jit(solution)/shard_map/ppermute | solution.py:222
  5.1 2.1 %collective-permute-start.1 = (bf16[32,1024]{1,0:T(8,128)(2,1)S(1)}, bf16[32,1024]{1,0:T(8,128)(2,1)S(1)}, u32[]{:S(2)}, u32[]{:S(2)}) collective-permute-start(bf16[32,1024]{1,0:T(8,128)(2,1)S(1)} %get-tuple-element.63), channel_id=1, source_target_pairs={{0,12},{1,13},{2,14},{3,15},{4,0},{5,1},{6,2},{7,3},{8,4},{9,5},{1... | collective-permute-start | bytes 196616 | tf_op jit(solution)/shard_map/ppermute | solution.py:222
  7.2 0.7 %collective-permute-start.3 = (bf16[16,1024]{1,0:T(8,128)(2,1)S(1)}, bf16[16,1024]{1,0:T(8,128)(2,1)S(1)}, u32[]{:S(2)}, u32[]{:S(2)}) collective-permute-start(bf16[16,1024]{1,0:T(8,128)(2,1)S(1)} %get-tuple-element.65), channel_id=1, source_target_pairs={{0,3},{1,2},{2,5},{3,4},{4,7},{5,6},{6,9},{7,8},{8,11},{9,10},{10,... | collective-permute-start | bytes 98312 | tf_op jit(solution)/shard_map/ppermute | solution.py:222
  7.9 3.8 %collective-permute-start.4 = (bf16[16,1024]{1,0:T(8,128)(2,1)S(1)}, bf16[16,1024]{1,0:T(8,128)(2,1)S(1)}, u32[]{:S(2)}, u32[]{:S(2)}) collective-permute-start(bf16[16,1024]{1,0:T(8,128)(2,1)S(1)} %get-tuple-element.66), channel_id=1, source_target_pairs={{0,15},{1,14},{2,1},{3,0},{4,3},{5,2},{6,5},{7,4},{8,7},{9,6},{10,... | collective-permute-start | bytes 98312 | tf_op jit(solution)/shard_map/ppermute | solution.py:222
  12.0 1.3 %collective-permute-done.3.refs_3_ = bf16[16,1024]{1,0:T(8,128)(2,1)S(1)} collective-permute-done((bf16[16,1024]{1,0:T(8,128)(2,1)S(1)}, bf16[16,1024]{1,0:T(8,128)(2,1)S(1)}, u32[]{:S(2)}, u32[]{:S(2)}) %collective-permute-start.3) | collective-permute-done | bytes 32800 | tf_op jit(solution)/shard_map/ppermute | solution.py:222
  13.4 0.5 collective-permute-start.2
  14.0 5.4 %local_products.1 = (bf16[256,256]{1,0:T(8,128)(2,1)S(1)}, f32[384,512]{1,0:T(8,128)S(1)}, f32[768,512]{1,0:T(8,128)S(1)}, f32[64,512]{1,0:T(8,128)S(1)}, bf16[3...) custom-call(bf16[256,256]{1,0:T(8,128)(2,1)S(1)} %get-tuple-element., ...), custom_call_target="tpu_custom_call" | custom-call | flops 1275068416 | bytes 9774080 | tf_op jit(solution)/shard_map/local_products/pallas_call | solution.py:164
  19.6 3.6 %edges_forward.1 = (bf16[32,1024]{1,0:T(8,128)(2,1)S(1)}, bf16[32,1024]{1,0:T(8,128)(2,1)S(1)}, bf16[16,1024]{1,0:T(8,128)(2,1)S(1)}, bf16[16,1024]{1,0:T(8,128)...) custom-call(bf16[32,1024]{1,0:T(8,128)(2,1)S(1)} %collective-permute, ...), custom_call_target="tpu_custom_call" | custom-call | flops 1207959552 | bytes 16552704 | tf_op jit(solution)/shard_map/edges_forward/pallas_call | solution.py:164
  23.2 0.9 %collective-permute-start.9 = (bf16[32,1024]{1,0:T(8,128)(2,1)S(1)}, bf16[32,1024]{1,0:T(8,128)(2,1)S(1)}, u32[]{:S(2)}, u32[]{:S(2)}) collective-permute-start(bf16[32,1024]{1,0:T(8,128)(2,1)S(1)} %get-tuple-element.77), channel_id=1, source_target_pairs={{0,4},{1,5},{2,6},{3,7},{4,8},{5,9},{6,10},{7,11},{8,12},{9,13},{1... | collective-permute-start | bytes 196616 | tf_op jit(solution)/shard_map/ppermute | solution.py:222
  24.1 2.9 %collective-permute-start.10 = (bf16[32,1024]{1,0:T(8,128)(2,1)S(1)}, bf16[32,1024]{1,0:T(8,128)(2,1)S(1)}, u32[]{:S(2)}, u32[]{:S(2)}) collective-permute-start(bf16[32,1024]{1,0:T(8,128)(2,1)S(1)} %get-tuple-element.80), channel_id=1, source_target_pairs={{0,12},{1,13},{2,14},{3,15},{4,0},{5,1},{6,2},{7,3},{8,4},{9,5},{1... | collective-permute-start | bytes 196616 | tf_op jit(solution)/shard_map/ppermute | solution.py:222
  27.1 1.6 %collective-permute-start.12 = (bf16[16,1024]{1,0:T(8,128)(2,1)S(1)}, bf16[16,1024]{1,0:T(8,128)(2,1)S(1)}, u32[]{:S(2)}, u32[]{:S(2)}) collective-permute-start(bf16[16,1024]{1,0:T(8,128)(2,1)S(1)} %get-tuple-element.82), channel_id=1, source_target_pairs={{0,3},{1,2},{2,5},{3,4},{4,7},{5,6},{6,9},{7,8},{8,11},{9,10},{10,... | collective-permute-start | bytes 98312 | tf_op jit(solution)/shard_map/ppermute | solution.py:222
  28.7 2.8 %collective-permute-start.13 = (bf16[16,1024]{1,0:T(8,128)(2,1)S(1)}, bf16[16,1024]{1,0:T(8,128)(2,1)S(1)}, u32[]{:S(2)}, u32[]{:S(2)}) collective-permute-start(bf16[16,1024]{1,0:T(8,128)(2,1)S(1)} %get-tuple-element.83), channel_id=1, source_target_pairs={{0,15},{1,14},{2,1},{3,0},{4,3},{5,2},{6,5},{7,4},{8,7},{9,6},{10,... | collective-permute-start | bytes 98312 | tf_op jit(solution)/shard_map/ppermute | solution.py:222
  31.5 1.3 %collective-permute-start.15 = (bf16[16,1024]{1,0:T(8,128)(2,1)S(1)}, bf16[16,1024]{1,0:T(8,128)(2,1)S(1)}, u32[]{:S(2)}, u32[]{:S(2)}) collective-permute-start(bf16[16,1024]{1,0:T(8,128)(2,1)S(1)} %get-tuple-element.85), channel_id=1, source_target_pairs={{0,8},{1,9},{2,10},{3,11},{4,12},{5,13},{6,14},{7,15},{8,0},{9,1},... | collective-permute-start | bytes 98312 | tf_op jit(solution)/shard_map/ppermute | solution.py:222
  32.8 0.7 %collective-permute-done.12.refs_12_ = bf16[16,1024]{1,0:T(8,128)(2,1)S(1)} collective-permute-done((bf16[16,1024]{1,0:T(8,128)(2,1)S(1)}, bf16[16,1024]{1,0:T(8,128)(2,1)S(1)}, u32[]{:S(2)}, u32[]{:S(2)}) %collective-permute-start.12) | collective-permute-done | bytes 32800 | tf_op jit(solution)/shard_map/ppermute | solution.py:222
  34.4 2.5 %collective-permute-done.14.refs_14_ = bf16[16,1024]{1,0:T(8,128)(2,1)S(1)} collective-permute-done((bf16[16,1024]{1,0:T(8,128)(2,1)S(1)}, bf16[16,1024]{1,0:T(8,128)(2,1)S(1)}, u32[]{:S(2)}, u32[]{:S(2)}) %collective-permute-start.14) | collective-permute-done | bytes 32800 | tf_op jit(solution)/shard_map/ppermute | solution.py:222
  37.0 6.0 %edges_backward.1 = (bf16[32,512]{1,0:T(8,128)(2,1)S(1)}, bf16[32,512]{1,0:T(8,128)(2,1)S(1)}, bf16[16,512]{1,0:T(8,128)(2,1)S(1)}, bf16[16,512]{1,0:T(8,128)(2,...) custom-call(bf16[32,1024]{1,0:T(8,128)(2,1)S(1)} %collective-permute, ...), custom_call_target="tpu_custom_call" | custom-call | flops 2449473536 | bytes 18502400 | tf_op jit(solution)/shard_map/edges_backward/pallas_call | solution.py:164
  43.3 3.6 %collective-permute-start.19 = (bf16[32,512]{1,0:T(8,128)(2,1)S(1)}, bf16[32,512]{1,0:T(8,128)(2,1)S(1)}, u32[]{:S(2)}, u32[]{:S(2)}) collective-permute-start(bf16[32,512]{1,0:T(8,128)(2,1)S(1)} %get-tuple-element.102), channel_id=1, source_target_pairs={{0,12},{1,13},{2,14},{3,15},{4,0},{5,1},{6,2},{7,3},{8,4},{9,5},{1... | collective-permute-start | bytes 98312 | tf_op jit(solution)/shard_map/ppermute | solution.py:222
  46.8 4.4 %collective-permute-start.22 = (bf16[16,512]{1,0:T(8,128)(2,1)S(1)}, bf16[16,512]{1,0:T(8,128)(2,1)S(1)}, u32[]{:S(2)}, u32[]{:S(2)}) collective-permute-start(bf16[16,512]{1,0:T(8,128)(2,1)S(1)} %get-tuple-element.105), channel_id=1, source_target_pairs={{0,15},{1,14},{2,1},{3,0},{4,3},{5,2},{6,5},{7,4},{8,7},{9,6},{10,... | collective-permute-start | bytes 49160 | tf_op jit(solution)/shard_map/ppermute | solution.py:222
  51.3 1.4 %collective-permute-done.21.refs_3_ = bf16[16,512]{1,0:T(8,128)(2,1)S(1)} collective-permute-done((bf16[16,512]{1,0:T(8,128)(2,1)S(1)}, bf16[16,512]{1,0:T(8,128)(2,1)S(1)}, u32[]{:S(2)}, u32[]{:S(2)}) %collective-permute-start.21) | collective-permute-done | bytes 16416 | tf_op jit(solution)/shard_map/ppermute | solution.py:222
  52.7 0.5 collective-permute-start.20
  53.3 1.5 %local_gradients.1 = (f32[256,512]{1,0:T(8,128)S(1)}, f32[64,512]{1,0:T(8,128)}) custom-call(bf16[256,512]{1,0:T(8,128)(2,1)S(1)} %copy-done.5, bf16[256,512]{1,0:T(8,128)(2,1)S(1)} %get-tuple-element.108.refs_1_, bf16[256,512]{1,0:T(8,128)(2,1)S(1)} %get-tuple-element.109.refs_2_, bf16[256,512]{1,0:T(8,128)(2,1)S(1)} %get-tuple-element.110.refs_3_, ...), custom_call_target="tpu_custom_call" | custom-call | flops 402653184 | bytes 8781824 | tf_op jit(solution)/shard_map/local_gradients/pallas_call | solution.py:164
  54.8 1.4 %collective-permute-done.23.refs_5_ = bf16[16,512]{1,0:T(8,128)(2,1)S(1)} collective-permute-done((bf16[16,512]{1,0:T(8,128)(2,1)S(1)}, bf16[16,512]{1,0:T(8,128)(2,1)S(1)}, u32[]{:S(2)}, u32[]{:S(2)}) %collective-permute-start.23) | collective-permute-done | bytes 16416 | tf_op jit(solution)/shard_map/ppermute | solution.py:222
  56.3 1.0 %add_returned.1 = f32[256,512]{1,0:T(8,128)} custom-call(bf16[32,512]{1,0:T(8,128)(2,1)S(1)} %collective-permute-done.18.refs_0_, bf16[32,512]{1,0:T(8,128)(2,1)S(1)} %collective-permute-done.19.refs_1_, bf16[16,512]{1,0:T(8,128)(2,1)S(1)} %collective-permute-done.20.refs_2_, bf16[16,512]{1,0:T(8,128)(2,1)S(1)} %collective-permute-done.21.refs_3_, ...), custom_call_target="tpu_custom_call" | custom-call | flops 37748736 | bytes 1392640 | tf_op jit(solution)/shard_map/add_returned/pallas_call | solution.py:164
  (61 shorter events, 2.0 us)
Async XLA Ops:
  2.1 9.6 %collective-permute-start = (bf16[32,1024]{1,0:T(8,128)(2,1)S(1)}, bf16[32,1024]{1,0:T(8,128)(2,1)S(1)}, u32[]{:S(2)}, u32[]{:S(2)}) collective-permute-start(bf16[32,1024]{1,0:T(8,128)(2,1)S(1)} %get-tuple-element.60), channel_id=1, source_target_pairs={{0,4},{1,5},{2,6},{3,7},{4,8},{5,9},{6,10},{7,11},{8,12},{9,13},{1... | collective-permute-start | bytes 196616 | tf_op jit(solution)/shard_map/ppermute | solution.py:222
  5.1 8.7 %collective-permute-start.1 = (bf16[32,1024]{1,0:T(8,128)(2,1)S(1)}, bf16[32,1024]{1,0:T(8,128)(2,1)S(1)}, u32[]{:S(2)}, u32[]{:S(2)}) collective-permute-start(bf16[32,1024]{1,0:T(8,128)(2,1)S(1)} %get-tuple-element.63), channel_id=1, source_target_pairs={{0,12},{1,13},{2,14},{3,15},{4,0},{5,1},{6,2},{7,3},{8,4},{9,5},{1... | collective-permute-start | bytes 196616 | tf_op jit(solution)/shard_map/ppermute | solution.py:222
  7.2 6.1 %collective-permute-start.3 = (bf16[16,1024]{1,0:T(8,128)(2,1)S(1)}, bf16[16,1024]{1,0:T(8,128)(2,1)S(1)}, u32[]{:S(2)}, u32[]{:S(2)}) collective-permute-start(bf16[16,1024]{1,0:T(8,128)(2,1)S(1)} %get-tuple-element.65), channel_id=1, source_target_pairs={{0,3},{1,2},{2,5},{3,4},{4,7},{5,6},{6,9},{7,8},{8,11},{9,10},{10,... | collective-permute-start | bytes 98312 | tf_op jit(solution)/shard_map/ppermute | solution.py:222
  7.9 5.5 %collective-permute-start.4 = (bf16[16,1024]{1,0:T(8,128)(2,1)S(1)}, bf16[16,1024]{1,0:T(8,128)(2,1)S(1)}, u32[]{:S(2)}, u32[]{:S(2)}) collective-permute-start(bf16[16,1024]{1,0:T(8,128)(2,1)S(1)} %get-tuple-element.66), channel_id=1, source_target_pairs={{0,15},{1,14},{2,1},{3,0},{4,3},{5,2},{6,5},{7,4},{8,7},{9,6},{10,... | collective-permute-start | bytes 98312 | tf_op jit(solution)/shard_map/ppermute | solution.py:222
  11.7 7.8 %collective-permute-start.5 = (bf16[16,1024]{1,0:T(8,128)(2,1)S(1)}, bf16[16,1024]{1,0:T(8,128)(2,1)S(1)}, u32[]{:S(2)}, u32[]{:S(2)}) collective-permute-start(bf16[16,1024]{1,0:T(8,128)(2,1)S(1)} %get-tuple-element.67), channel_id=1, source_target_pairs={{0,11},{1,6},{2,13},{3,8},{4,15},{5,10},{6,1},{7,12},{8,3},{9,14},... | collective-permute-start | bytes 98312 | tf_op jit(solution)/shard_map/ppermute | solution.py:222
  11.7 7.8 %collective-permute-start.6 = (bf16[16,1024]{1,0:T(8,128)(2,1)S(1)}, bf16[16,1024]{1,0:T(8,128)(2,1)S(1)}, u32[]{:S(2)}, u32[]{:S(2)}) collective-permute-start(bf16[16,1024]{1,0:T(8,128)(2,1)S(1)} %get-tuple-element.68), channel_id=1, source_target_pairs={{0,8},{1,9},{2,10},{3,11},{4,12},{5,13},{6,14},{7,15},{8,0},{9,1},... | collective-permute-start | bytes 98312 | tf_op jit(solution)/shard_map/ppermute | solution.py:222
  13.4 6.1 %collective-permute-start.7 = (bf16[32,1024]{1,0:T(8,128)(2,1)S(1)}, bf16[32,1024]{1,0:T(8,128)(2,1)S(1)}, u32[]{:S(2)}, u32[]{:S(2)}) collective-permute-start(bf16[32,1024]{1,0:T(8,128)(2,1)S(1)} %collective-permute-done.refs_0_), channel_id=1, source_target_pairs={{0,1},{1,0},{2,3},{3,2},{4,5},{5,4},{6,7},{7,6},{8,9},{9,8},{10,11... | collective-permute-start | bytes 196616 | tf_op jit(solution)/shard_map/ppermute | solution.py:222
  13.4 6.1 %collective-permute-start.2 = (bf16[16,1024]{1,0:T(8,128)(2,1)S(1)}, bf16[16,1024]{1,0:T(8,128)(2,1)S(1)}, u32[]{:S(2)}, u32[]{:S(2)}) collective-permute-start(bf16[16,1024]{1,0:T(8,128)(2,1)S(1)} %get-tuple-element.64), channel_id=1, source_target_pairs={{0,1},{1,0},{2,3},{3,2},{4,5},{5,4},{6,7},{7,6},{8,9},{9,8},{10,11... | collective-permute-start | bytes 98312 | tf_op jit(solution)/shard_map/ppermute | solution.py:222
  13.9 5.6 %collective-permute-start.8 = (bf16[32,1024]{1,0:T(8,128)(2,1)S(1)}, bf16[32,1024]{1,0:T(8,128)(2,1)S(1)}, u32[]{:S(2)}, u32[]{:S(2)}) collective-permute-start(bf16[32,1024]{1,0:T(8,128)(2,1)S(1)} %collective-permute-done.1.refs_1_), channel_id=1, source_target_pairs={{0,1},{1,0},{2,3},{3,2},{4,5},{5,4},{6,7},{7,6},{8,9},{9,8},{10,11... | collective-permute-start | bytes 196616 | tf_op jit(solution)/shard_map/ppermute | solution.py:222
  23.2 8.3 %collective-permute-start.9 = (bf16[32,1024]{1,0:T(8,128)(2,1)S(1)}, bf16[32,1024]{1,0:T(8,128)(2,1)S(1)}, u32[]{:S(2)}, u32[]{:S(2)}) collective-permute-start(bf16[32,1024]{1,0:T(8,128)(2,1)S(1)} %get-tuple-element.77), channel_id=1, source_target_pairs={{0,4},{1,5},{2,6},{3,7},{4,8},{5,9},{6,10},{7,11},{8,12},{9,13},{1... | collective-permute-start | bytes 196616 | tf_op jit(solution)/shard_map/ppermute | solution.py:222
  24.1 9.8 %collective-permute-start.10 = (bf16[32,1024]{1,0:T(8,128)(2,1)S(1)}, bf16[32,1024]{1,0:T(8,128)(2,1)S(1)}, u32[]{:S(2)}, u32[]{:S(2)}) collective-permute-start(bf16[32,1024]{1,0:T(8,128)(2,1)S(1)} %get-tuple-element.80), channel_id=1, source_target_pairs={{0,12},{1,13},{2,14},{3,15},{4,0},{5,1},{6,2},{7,3},{8,4},{9,5},{1... | collective-permute-start | bytes 196616 | tf_op jit(solution)/shard_map/ppermute | solution.py:222
  27.1 6.4 %collective-permute-start.12 = (bf16[16,1024]{1,0:T(8,128)(2,1)S(1)}, bf16[16,1024]{1,0:T(8,128)(2,1)S(1)}, u32[]{:S(2)}, u32[]{:S(2)}) collective-permute-start(bf16[16,1024]{1,0:T(8,128)(2,1)S(1)} %get-tuple-element.82), channel_id=1, source_target_pairs={{0,3},{1,2},{2,5},{3,4},{4,7},{5,6},{6,9},{7,8},{8,11},{9,10},{10,... | collective-permute-start | bytes 98312 | tf_op jit(solution)/shard_map/ppermute | solution.py:222
  28.7 4.8 %collective-permute-start.13 = (bf16[16,1024]{1,0:T(8,128)(2,1)S(1)}, bf16[16,1024]{1,0:T(8,128)(2,1)S(1)}, u32[]{:S(2)}, u32[]{:S(2)}) collective-permute-start(bf16[16,1024]{1,0:T(8,128)(2,1)S(1)} %get-tuple-element.83), channel_id=1, source_target_pairs={{0,15},{1,14},{2,1},{3,0},{4,3},{5,2},{6,5},{7,4},{8,7},{9,6},{10,... | collective-permute-start | bytes 98312 | tf_op jit(solution)/shard_map/ppermute | solution.py:222
  31.5 5.4 %collective-permute-start.14 = (bf16[16,1024]{1,0:T(8,128)(2,1)S(1)}, bf16[16,1024]{1,0:T(8,128)(2,1)S(1)}, u32[]{:S(2)}, u32[]{:S(2)}) collective-permute-start(bf16[16,1024]{1,0:T(8,128)(2,1)S(1)} %get-tuple-element.84), channel_id=1, source_target_pairs={{0,11},{1,6},{2,13},{3,8},{4,15},{5,10},{6,1},{7,12},{8,3},{9,14},... | collective-permute-start | bytes 98312 | tf_op jit(solution)/shard_map/ppermute | solution.py:222
  31.5 5.4 %collective-permute-start.15 = (bf16[16,1024]{1,0:T(8,128)(2,1)S(1)}, bf16[16,1024]{1,0:T(8,128)(2,1)S(1)}, u32[]{:S(2)}, u32[]{:S(2)}) collective-permute-start(bf16[16,1024]{1,0:T(8,128)(2,1)S(1)} %get-tuple-element.85), channel_id=1, source_target_pairs={{0,8},{1,9},{2,10},{3,11},{4,12},{5,13},{6,14},{7,15},{8,0},{9,1},... | collective-permute-start | bytes 98312 | tf_op jit(solution)/shard_map/ppermute | solution.py:222
  33.5 3.5 %collective-permute-start.16 = (bf16[32,1024]{1,0:T(8,128)(2,1)S(1)}, bf16[32,1024]{1,0:T(8,128)(2,1)S(1)}, u32[]{:S(2)}, u32[]{:S(2)}) collective-permute-start(bf16[32,1024]{1,0:T(8,128)(2,1)S(1)} %collective-permute-done.9.refs_9_), channel_id=1, source_target_pairs={{0,1},{1,0},{2,3},{3,2},{4,5},{5,4},{6,7},{7,6},{8,9},{9,8},{10,11... | collective-permute-start | bytes 196616 | tf_op jit(solution)/shard_map/ppermute | solution.py:222
  43.0 8.3 %collective-permute-start.18 = (bf16[32,512]{1,0:T(8,128)(2,1)S(1)}, bf16[32,512]{1,0:T(8,128)(2,1)S(1)}, u32[]{:S(2)}, u32[]{:S(2)}) collective-permute-start(bf16[32,512]{1,0:T(8,128)(2,1)S(1)} %get-tuple-element.99), channel_id=1, source_target_pairs={{0,4},{1,5},{2,6},{3,7},{4,8},{5,9},{6,10},{7,11},{8,12},{9,13},{1... | collective-permute-start | bytes 98312 | tf_op jit(solution)/shard_map/ppermute | solution.py:222
  43.3 9.9 %collective-permute-start.19 = (bf16[32,512]{1,0:T(8,128)(2,1)S(1)}, bf16[32,512]{1,0:T(8,128)(2,1)S(1)}, u32[]{:S(2)}, u32[]{:S(2)}) collective-permute-start(bf16[32,512]{1,0:T(8,128)(2,1)S(1)} %get-tuple-element.102), channel_id=1, source_target_pairs={{0,12},{1,13},{2,14},{3,15},{4,0},{5,1},{6,2},{7,3},{8,4},{9,5},{1... | collective-permute-start | bytes 98312 | tf_op jit(solution)/shard_map/ppermute | solution.py:222
  46.8 5.9 %collective-permute-start.21 = (bf16[16,512]{1,0:T(8,128)(2,1)S(1)}, bf16[16,512]{1,0:T(8,128)(2,1)S(1)}, u32[]{:S(2)}, u32[]{:S(2)}) collective-permute-start(bf16[16,512]{1,0:T(8,128)(2,1)S(1)} %get-tuple-element.104), channel_id=1, source_target_pairs={{0,3},{1,2},{2,5},{3,4},{4,7},{5,6},{6,9},{7,8},{8,11},{9,10},{10,... | collective-permute-start | bytes 49160 | tf_op jit(solution)/shard_map/ppermute | solution.py:222
  46.8 5.9 %collective-permute-start.22 = (bf16[16,512]{1,0:T(8,128)(2,1)S(1)}, bf16[16,512]{1,0:T(8,128)(2,1)S(1)}, u32[]{:S(2)}, u32[]{:S(2)}) collective-permute-start(bf16[16,512]{1,0:T(8,128)(2,1)S(1)} %get-tuple-element.105), channel_id=1, source_target_pairs={{0,15},{1,14},{2,1},{3,0},{4,3},{5,2},{6,5},{7,4},{8,7},{9,6},{10,... | collective-permute-start | bytes 49160 | tf_op jit(solution)/shard_map/ppermute | solution.py:222
  51.3 5.0 %collective-permute-start.23 = (bf16[16,512]{1,0:T(8,128)(2,1)S(1)}, bf16[16,512]{1,0:T(8,128)(2,1)S(1)}, u32[]{:S(2)}, u32[]{:S(2)}) collective-permute-start(bf16[16,512]{1,0:T(8,128)(2,1)S(1)} %get-tuple-element.106), channel_id=1, source_target_pairs={{0,11},{1,6},{2,13},{3,8},{4,15},{5,10},{6,1},{7,12},{8,3},{9,14},... | collective-permute-start | bytes 49160 | tf_op jit(solution)/shard_map/ppermute | solution.py:222
  51.3 5.0 %collective-permute-start.24 = (bf16[16,512]{1,0:T(8,128)(2,1)S(1)}, bf16[16,512]{1,0:T(8,128)(2,1)S(1)}, u32[]{:S(2)}, u32[]{:S(2)}) collective-permute-start(bf16[16,512]{1,0:T(8,128)(2,1)S(1)} %get-tuple-element.107), channel_id=1, source_target_pairs={{0,8},{1,9},{2,10},{3,11},{4,12},{5,13},{6,14},{7,15},{8,0},{9,1},... | collective-permute-start | bytes 49160 | tf_op jit(solution)/shard_map/ppermute | solution.py:222
  52.7 3.6 %collective-permute-start.25 = (bf16[32,512]{1,0:T(8,128)(2,1)S(1)}, bf16[32,512]{1,0:T(8,128)(2,1)S(1)}, u32[]{:S(2)}, u32[]{:S(2)}) collective-permute-start(bf16[32,512]{1,0:T(8,128)(2,1)S(1)} %collective-permute-done.18.refs_0_), channel_id=1, source_target_pairs={{0,1},{1,0},{2,3},{3,2},{4,5},{5,4},{6,7},{7,6},{8,9},{9,8},{10,11... | collective-permute-start | bytes 98312 | tf_op jit(solution)/shard_map/ppermute | solution.py:222
  52.7 3.5 %collective-permute-start.20 = (bf16[16,512]{1,0:T(8,128)(2,1)S(1)}, bf16[16,512]{1,0:T(8,128)(2,1)S(1)}, u32[]{:S(2)}, u32[]{:S(2)}) collective-permute-start(bf16[16,512]{1,0:T(8,128)(2,1)S(1)} %get-tuple-element.103), channel_id=1, source_target_pairs={{0,1},{1,0},{2,3},{3,2},{4,5},{5,4},{6,7},{7,6},{8,9},{9,8},{10,11... | collective-permute-start | bytes 49160 | tf_op jit(solution)/shard_map/ppermute | solution.py:222
  (15 other events, 89.9 us)

commit v7 on v6

--- a/solution.py
+++ b/solution.py
@@ -42,32 +42,44 @@
     return [slice(start, min(start + size, rows)) for start in range(0, rows, size)]
 
 
-def activate(pre, act_ref, slope_ref):
-    for rows in row_chunks(pre.shape[0]):
-        part = pre[rows, :]
+def row_blocks(rows, parts):
+    size = -(-rows // (16 * parts)) * 16
+    return row_chunks(rows, size)
+
+
+def inner_chunks(block):
+    return [
+        (slice(part.start, part.stop), slice(block.start + part.start, block.start + part.stop))
+        for part in row_chunks(block.stop - block.start)
+    ]
+
+
+def activate(pre, act_ref, slope_ref, block):
+    for inner, rows in inner_chunks(block):
+        part = pre[inner, :]
         gate = sigmoid(part)
         act = part * gate
         act_ref[rows, :] = act.astype(BF16)
         slope_ref[rows, :] = (gate + act * (1.0 - gate)).astype(BF16)
 
 
-def norm_forward(raw, normed_ref, scale_ref):
-    for rows in row_chunks(raw.shape[0]):
-        normed, scale_inv = norm_rows(raw[rows, :])
+def norm_forward(raw, normed_ref, scale_ref, block):
+    for inner, rows in inner_chunks(block):
+        normed, scale_inv = norm_rows(raw[inner, :])
         normed_ref[rows, :] = normed.astype(normed_ref.dtype)
         scale_ref[rows, :] = scale_inv
 
 
-def norm_backward(normed_ref, scale_ref, upstream, out_ref):
-    for rows in row_chunks(out_ref.shape[0]):
+def norm_backward(normed_ref, scale_ref, upstream, out_ref, block):
+    for inner, rows in inner_chunks(block):
         out_ref[rows, :] = norm_back(
-            normed_ref[rows, :].astype(F32), scale_ref[rows, :], upstream[rows, :].astype(F32)
+            normed_ref[rows, :].astype(F32), scale_ref[rows, :], upstream[inner, :].astype(F32)
         ).astype(BF16)
 
 
-def times_slope(raw, slope_ref, out_ref):
-    for rows in row_chunks(out_ref.shape[0]):
-        out_ref[rows, :] = (raw[rows, :] * slope_ref[rows, :].astype(F32)).astype(BF16)
+def times_slope(raw, slope_ref, out_ref, block):
+    for inner, rows in inner_chunks(block):
+        out_ref[rows, :] = (raw[inner, :] * slope_ref[rows, :].astype(F32)).astype(BF16)
 
 
 def neighbour_offsets(peer_count):
@@ -77,31 +89,28 @@
 
 def onehot_pair(spot_ref, mesh_ref, spots, mesh_count, by_edge_ref, by_spot_ref):
     edges, total = by_edge_ref.shape
-    spot_row = spot_ref[...].reshape(1, -1).astype(F32)
-    mesh_row = mesh_ref[...].reshape(1, -1).astype(F32) + float(spots)
-
-    def ids(shape, axis, start):
-        return (lax.broadcasted_iota(jnp.int32, shape, axis) + start).astype(F32)
+    spot_row = spot_ref[...].reshape(1, -1)
+    mesh_row = mesh_ref[...].reshape(1, -1) + spots
 
     def ones(hit):
         return jnp.where(hit, 1.0, 0.0).astype(BF16)
 
     for row, first, count in ((spot_row, 0, spots), (mesh_row, spots, mesh_count)):
-        for rows in row_chunks(count, 80):
+        for rows in row_chunks(count, 16):
+            ids = lax.broadcasted_iota(jnp.int32, (16, edges), 0)
             rows = slice(rows.start + first, rows.stop + first)
-            shape = (rows.stop - rows.start, edges)
-            by_spot_ref[rows, :] = ones(ids(shape, 0, rows.start) == row)
+            by_spot_ref[rows, :] = ones(ids == row - rows.start)
     by_spot_ref[spots + mesh_count :, :] = jnp.zeros((total - spots - mesh_count, edges), BF16)
+    lane = lax.broadcasted_iota(jnp.int32, (1, 128), 1)
     for rows in row_chunks(edges, 128):
         spot_col = jnp.broadcast_to(spot_row[:, rows], (128, 128)).T
         mesh_col = jnp.broadcast_to(mesh_row[:, rows], (128, 128)).T
         for columns in row_chunks(total, 128):
-            lane = ids((128, 128), 1, columns.start)
             hit = None
             if columns.start < spots:
-                hit = lane == spot_col
+                hit = lane + columns.start == spot_col
             if columns.stop > spots:
-                mesh_hit = lane == mesh_col
+                mesh_hit = lane + columns.start == mesh_col
                 hit = mesh_hit if hit is None else hit | mesh_hit
             by_edge_ref[rows, columns] = ones(hit)
 
@@ -217,32 +226,33 @@
     across = links - 1
     peers = range(peer_count)
 
-    def permute(part, even_step, odd_step):
-        steps = (even_step, odd_step)
-        return lax.ppermute(part, "tile", [(s, (s + steps[s % 2]) % peer_count) for s in peers])
+    def permute(part, steps, odd_row_steps=None):
+        rows = (steps, odd_row_steps or steps)
+        pairs = [(s, (s + rows[s // TW % 2][s % 2]) % peer_count) for s in peers]
+        return lax.ppermute(part, "tile", pairs)
 
     def exchange(parts):
-        plus_two, minus_two, own_chip, plus_one, minus_one, three_off, opposite = parts
-        plus_two = permute(plus_two, 4, 4)
-        plus_one = permute(plus_one, 3, 1)
-        minus_two = permute(minus_two, -4, -4)
-        minus_one = permute(minus_one, -1, -3)
-        three_off = permute(three_off, -5, 5)
-        opposite = permute(opposite, peer_count // 2, peer_count // 2)
-        plus_two, own_chip = lax.optimization_barrier((plus_two, own_chip))
-        plus_passed = permute(plus_two, 1, -1)
-        minus_passed = permute(minus_two, 1, -1)
-        own_chip = permute(own_chip, 1, -1)
+        late_pair, early_pair, behind_one, ahead_three, five_off, opposite, own_chip = parts
+        late_pair = permute(late_pair, (-4, -4), (4, 4))
+        early_pair = permute(early_pair, (4, 4), (-4, -4))
+        behind_one = permute(behind_one, (-1, 1))
+        ahead_three = permute(ahead_three, (3, -3))
+        five_off = permute(five_off, (-5, 5))
+        opposite = permute(opposite, (peer_count // 2, peer_count // 2))
+        late_pair, own_chip = lax.optimization_barrier((late_pair, own_chip))
+        late_passed = permute(late_pair, (1, -1))
+        own_chip = permute(own_chip, (1, -1))
+        early_passed = permute(early_pair, (1, -1))
         return [
-            plus_two,
-            minus_two,
+            late_pair,
+            early_pair,
+            behind_one,
+            ahead_three,
+            five_off,
+            opposite,
             own_chip,
-            plus_one,
-            minus_one,
-            three_off,
-            opposite,
-            plus_passed,
-            minus_passed,
+            late_passed,
+            early_passed,
         ]
 
     arrived_count = 9
@@ -253,44 +263,49 @@
 
     sent_count = len(sent_shapes(feat))
 
-    def is_odd():
-        return lax.rem(lax.axis_index("tile"), 2) == 1
+    def place_bits():
+        own = lax.axis_index("tile")
+        return lax.rem(own, 2) == 1, lax.rem(lax.div(own, TW), 2) == 1
 
     def send(refs, message, columns=slice(None)):
-        odd = is_odd()
+        odd, odd_row = place_bits()
 
         def by_parity(even, odd_one):
             return jnp.where(odd, message(odd_one), message(even))
 
-        plus_two, minus_two, own_chip, plus_one, minus_one, three_off, opposite = refs
-        plus_two[:width, columns] = message(four)
-        plus_two[width:, columns] = by_parity(five, three)
-        minus_two[:width, columns] = message(minus[four])
-        minus_two[width:, columns] = by_parity(minus[three], minus[five])
+        late_pair, early_pair, behind_one, ahead_three, five_off, opposite, own_chip = refs
+        first, second = slice(0, width), slice(width, 2 * width)
+        ahead = message(four), by_parity(five, three)
+        behind = message(minus[four]), by_parity(minus[three], minus[five])
+        for rows, go_ahead, go_behind in zip((first, second), ahead, behind):
+            late_pair[rows, columns] = jnp.where(odd_row, go_ahead, go_behind)
+            early_pair[rows, columns] = jnp.where(odd_row, go_behind, go_ahead)
+        behind_one[:, columns] = by_parity(minus[one], one)
+        ahead_three[:, columns] = by_parity(three, minus[three])
+        five_off[:, columns] = by_parity(minus[five], five)
+        opposite[:, columns] = message(across)
         own_chip[:, columns] = by_parity(one, minus[one])
-        plus_one[:, columns] = by_parity(three, one)
-        minus_one[:, columns] = by_parity(minus[one], minus[three])
-        three_off[:, columns] = by_parity(minus[five], five)
-        opposite[:, columns] = message(across)
 
     def receive(refs, columns=slice(None)):
-        odd = is_odd()
-        plus_two, minus_two, own_chip, plus_one, minus_one, three_off, opposite = refs[:7]
-        plus_passed, minus_passed = refs[7:]
+        odd, odd_row = place_bits()
+        late_pair, early_pair, behind_one, ahead_three, five_off, opposite, own_chip = refs[:7]
+        late_passed, early_passed = refs[7:]
         first, second = slice(0, width), slice(width, 2 * width)
-        own = own_chip[:, columns]
-        near_plus, near_minus = plus_one[:, columns], minus_one[:, columns]
-        far = three_off[:, columns]
-        passed_plus, passed_minus = plus_passed[second, columns], minus_passed[second, columns]
+        near, near_three = behind_one[:, columns], ahead_three[:, columns]
+        far, own = five_off[:, columns], own_chip[:, columns]
+        late_rows, early_rows = late_passed[second, columns], early_passed[second, columns]
+        from_behind = jnp.where(odd_row, early_rows, late_rows)
+        from_ahead = jnp.where(odd_row, late_rows, early_rows)
+        late_rows, early_rows = late_pair[first, columns], early_pair[first, columns]
         slot_rows = [None] * links
-        slot_rows[one] = jnp.where(odd, own, near_plus)
-        slot_rows[minus[one]] = jnp.where(odd, near_minus, own)
-        slot_rows[three] = jnp.where(odd, near_plus, passed_plus)
-        slot_rows[minus[three]] = jnp.where(odd, passed_minus, near_minus)
-        slot_rows[five] = jnp.where(odd, passed_plus, far)
-        slot_rows[minus[five]] = jnp.where(odd, far, passed_minus)
-        slot_rows[four] = plus_two[first, columns]
-        slot_rows[minus[four]] = minus_two[first, columns]
+        slot_rows[one] = jnp.where(odd, own, near)
+        slot_rows[minus[one]] = jnp.where(odd, near, own)
+        slot_rows[three] = jnp.where(odd, near_three, from_behind)
+        slot_rows[minus[three]] = jnp.where(odd, from_ahead, near_three)
+        slot_rows[five] = jnp.where(odd, from_behind, far)
+        slot_rows[minus[five]] = jnp.where(odd, far, from_ahead)
+        slot_rows[four] = jnp.where(odd_row, early_rows, late_rows)
+        slot_rows[minus[four]] = jnp.where(odd_row, late_rows, early_rows)
         slot_rows[across] = opposite[:, columns]
         return slot_rows
 
@@ -456,12 +471,17 @@
         ) = refs
         rows = by_slot(arrived_refs, low)
         pe = mm(rows, enc_wg_ref[low, :]).astype(BF16)
-        pre = enc_part_ref[...] + mm(enc_pick_ref[:, grid_count:spots], pe)
-        activate(pre, enc_act_ref, enc_slope_ref)
-        norm_forward(mm(enc_act_ref[...], enc_w2_ref[...]), enc_normed_ref, enc_scale_ref)
+        for block in row_blocks(enc_count, 3):
+            pre = enc_part_ref[block, :] + mm(enc_pick_ref[block, grid_count:spots], pe)
+            activate(pre, enc_act_ref, enc_slope_ref, block)
+            raw = mm(enc_act_ref[block, :], enc_w2_ref[...])
+            norm_forward(raw, enc_normed_ref, enc_scale_ref, block)
         agg = mm(enc_pool_ref[mesh_rows, :], enc_normed_ref[...]).astype(BF16)
-        activate(mesh_part_ref[...] + mm(agg, mesh_wa_ref[high, :]), mesh_act_ref, mesh_slope_ref)
-        norm_forward(mm(mesh_act_ref[...], mesh_w2_ref[...]), mesh_normed_ref, mesh_scale_ref)
+        whole = slice(0, mesh_count)
+        pre = mesh_part_ref[...] + mm(agg, mesh_wa_ref[high, :])
+        activate(pre, mesh_act_ref, mesh_slope_ref, whole)
+        raw = mm(mesh_act_ref[...], mesh_w2_ref[...])
+        norm_forward(raw, mesh_normed_ref, mesh_scale_ref, whole)
         mesh_out = (mesh_ref[...].astype(F32) + mesh_normed_ref[...]).astype(BF16)
         mesh_out_ref[...] = mesh_out
         table_ref[:slots, :] = mm(rows, dec_wg_ref[low, :]).astype(BF16)
@@ -469,9 +489,11 @@
         table_ref[slots + mesh_count :, :] = jnp.zeros(
             (total - spots - mesh_count, feat), BF16
         )
-        pre = dec_part_ref[...] + mm(dec_pick_ref[:, grid_count:], table_ref[...])
-        activate(pre, dec_act_ref, dec_slope_ref)
-        norm_forward(mm(dec_act_ref[...], dec_w2_ref[...]), dec_normed_ref, dec_scale_ref)
+        for block in row_blocks(dec_count, 3):
+            pre = dec_part_ref[block, :] + mm(dec_pick_ref[block, grid_count:], table_ref[...])
+            activate(pre, dec_act_ref, dec_slope_ref, block)
+            raw = mm(dec_act_ref[block, :], dec_w2_ref[...])
+            norm_forward(raw, dec_normed_ref, dec_scale_ref, block)
         spot_ref[...] = mm(dec_pool_ref[:spots, :], dec_normed_ref[...])
         shared = mm(select_ref[:slots, :], spot_ref[:grid_count, :].astype(BF16)).astype(BF16)
         slot_msg = spot_ref[grid_count:, :].astype(BF16)
@@ -586,6 +608,7 @@
             mesh_gpre_ref,
             mesh_pool_ref,
             agg_ref,
+            cot_rows_ref,
             grid_act_ref,
             grid_slope_ref,
             grid_normed_ref,
@@ -603,35 +626,48 @@
         agg_ref[grid_count:, :] = (
             spot_ref[grid_count:, :] + by_slot(returned_refs, high).astype(F32)
         ).astype(BF16)
-        activate(
-            grid_part_ref[...] + mm(agg_ref[...], grid_wa_ref[high, :]), grid_act_ref, grid_slope_ref
-        )
-        norm_forward(mm(grid_act_ref[...], grid_w2_ref[...]), grid_normed_ref, grid_scale_ref)
+        cot_rows_ref[:grid_count, :] = cot_ref[...]
+        cot_rows_ref[grid_count:, :] = by_slot(arrived_refs, high)
+        spot_grad_ref[spots:, :] = jnp.zeros((total - spots, feat), BF16)
+        for block in row_blocks(spots, 2):
+            pre = grid_part_ref[block, :] + mm(agg_ref[block, :], grid_wa_ref[high, :])
+            activate(pre, grid_act_ref, grid_slope_ref, block)
+            raw = mm(grid_act_ref[block, :], grid_w2_ref[...])
+            norm_forward(raw, grid_normed_ref, grid_scale_ref, block)
+            norm_backward(
+                grid_normed_ref, grid_scale_ref, cot_rows_ref[block, :], grid_gout_ref, block
+            )
+            raw = mm_t(grid_gout_ref[block, :], grid_w2_ref[...])
+            times_slope(raw, grid_slope_ref, grid_gall_ref, block)
+            spot_grad_ref[block, :] = mm_t(
+                grid_gall_ref[block, :], grid_wa_ref[high, :]
+            ).astype(BF16)
         grid_out_ref[...] = (
             nodes_ref[...].astype(F32) + grid_normed_ref[:grid_count, :]
         ).astype(BF16)
-        cot = jnp.concatenate([cot_ref[...], by_slot(arrived_refs, high)], axis=0)
-        norm_backward(grid_normed_ref, grid_scale_ref, cot, grid_gout_ref)
-        times_slope(mm_t(grid_gout_ref[...], grid_w2_ref[...]), grid_slope_ref, grid_gall_ref)
         grid_gpre_ref[...] = grid_gall_ref[:grid_count, :]
-        spot_grad_ref[:spots, :] = mm_t(grid_gall_ref[...], grid_wa_ref[high, :]).astype(BF16)
-        spot_grad_ref[spots:, :] = jnp.zeros((total - spots, feat), BF16)
-        norm_backward(
-            dec_normed_ref, dec_scale_ref, mm(dec_pick_ref[...], spot_grad_ref[...]), dec_gout_ref
-        )
-        times_slope(mm_t(dec_gout_ref[...], dec_w2_ref[...]), dec_slope_ref, dec_gout_ref)
+        for block in row_blocks(dec_count, 3):
+            upstream = mm(dec_pick_ref[block, :], spot_grad_ref[...])
+            norm_backward(dec_normed_ref, dec_scale_ref, upstream, dec_gout_ref, block)
+            raw = mm_t(dec_gout_ref[block, :], dec_w2_ref[...])
+            times_slope(raw, dec_slope_ref, dec_gout_ref, block)
         pooled = mm(dec_pool_ref[...], dec_gout_ref[...]).astype(BF16)
         gpd_ref[...] = pooled[:grid_count, :]
         slot_back = mm_t(pooled[grid_count:spots, :], dec_wg_ref[low, :])
-        mesh_gin = mesh_cot_ref[...].astype(F32) + mm_t(pooled[mesh_rows, :], dec_wm_ref[high, :])
+        mesh_gin = mesh_cot_ref[...].astype(F32) + mm_t(
+            pooled[mesh_rows, :], dec_wm_ref[high, :]
+        )
         mesh_gin_ref[...] = mesh_gin
-        norm_backward(mesh_normed_ref, mesh_scale_ref, mesh_gin, mesh_gout_ref)
-        times_slope(mm_t(mesh_gout_ref[...], mesh_w2_ref[...]), mesh_slope_ref, mesh_gpre_ref)
+        whole = slice(0, mesh_count)
+        norm_backward(mesh_normed_ref, mesh_scale_ref, mesh_gin, mesh_gout_ref, whole)
+        raw = mm_t(mesh_gout_ref[...], mesh_w2_ref[...])
+        times_slope(raw, mesh_slope_ref, mesh_gpre_ref, whole)
         gagg = mm_t(mesh_gpre_ref[...], mesh_wa_ref[high, :]).astype(BF16)
-        norm_backward(
-            enc_normed_ref, enc_scale_ref, mm(enc_pick_ref[:, mesh_rows], gagg), enc_gout_ref
-        )
-        times_slope(mm_t(enc_gout_ref[...], enc_w2_ref[...]), enc_slope_ref, enc_gout_ref)
+        for block in row_blocks(enc_count, 3):
+            upstream = mm(enc_pick_ref[block, mesh_rows], gagg)
+            norm_backward(enc_normed_ref, enc_scale_ref, upstream, enc_gout_ref, block)
+            raw = mm_t(enc_gout_ref[block, :], enc_w2_ref[...])
+            times_slope(raw, enc_slope_ref, enc_gout_ref, block)
         pooled = mm(enc_pool_ref[...], enc_gout_ref[...]).astype(BF16)
         gpe_ref[...] = pooled[:grid_count, :]
         mesh_pool_ref[...] = pooled[mesh_rows, :]
@@ -672,6 +708,7 @@
             ((spots, feat), BF16),
             ((spots, feat), BF16),
             ((spots, feat), BF16),
+            ((spots, feat), BF16),
             ((spots, feat), F32),
             ((spots, 1), F32),
             ((spots, feat), BF16),

time: 57.5 us -> 56.2 us (0.977)
  waiting for transfers between devices: 7.44 us -> 5.47 us
  Pallas kernels: 19.3 us -> 21.2 us
  starting transfers between devices: 29.6 us -> 28.5 us
    ppermute x27, waiting for transfers between devices: 7.44 us -> 5.47 us  [permute(): return lax.ppermute(part, 'tile', pairs)]
    pallas_call x7, Pallas kernels: 19.3 us -> 21.2 us  [call(): pl.pallas_call(kernel, name=name, in_specs=specs, out_specs=[pl.BlockSpec...]
    ppermute x27, starting transfers between devices: 29.6 us -> 28.5 us  [permute(): return lax.ppermute(part, 'tile', pairs)]
  transfers between devices with their start and end apart: 27 -> 27, of which waited for: 5 -> 7; matrix products, arithmetic and copies ran while one was open for 0% -> 0% of each run, Pallas kernels for 13% -> 13%
where the time goes in v7:
time: 56.2 us; the launch traced here: 56.1 us
  starting transfers between devices  28.5 us (51%)
  Pallas kernels  21.2 us (38%)
  waiting for transfers between devices  5.47 us (10%)
  between operations  0.9 us (2%)
    ppermute x27, starting transfers between devices, permute(): return lax.ppermute(part, 'tile', pairs)  28.5 us
    pallas_call x7, Pallas kernels, call(): pl.pallas_call(kernel, name=name, in_specs=specs, out_specs=[pl.BlockSpec...  21.2 us
    ppermute x27, waiting for transfers between devices, permute(): return lax.ppermute(part, 'tile', pairs)  5.47 us
  transfers between devices with their start and end apart: 27, of which 7 were waited for; matrix products, arithmetic and copies ran while one was open for 0% of the time, Pallas kernels for 13%

profile of v7, /device:TPU:0, one launch (start us, length us, event | category | flops | bytes accessed | tf_op | source)
XLA Modules:
  0.0 56.1 jit_solution(6434230126025357196)
XLA Ops:
  0.6 1.4 %pack_rows.1 = (bf16[256,256]{1,0:T(8,128)(2,1)S(1)}, bf16[32,1024]{1,0:T(8,128)(2,1)S(1)}, bf16[32,1024]{1,0:T(8,128)(2,1)S(1)}, bf16[16,1024]{1,0:T(8,128)(2,1...) custom-call(s32[9,16]{1,0:T(8,128)} %refs_0_.2, ...), custom_call_target="tpu_custom_call" | custom-call | flops 75497472 | bytes 950884 | tf_op jit(solution)/shard_map/pack_rows/pallas_call | solution.py:173
  2.1 5.1 %collective-permute-start = (bf16[32,1024]{1,0:T(8,128)(2,1)S(1)}, bf16[32,1024]{1,0:T(8,128)(2,1)S(1)}, u32[]{:S(2)}, u32[]{:S(2)}) collective-permute-start(bf16[32,1024]{1,0:T(8,128)(2,1)S(1)} %get-tuple-element.60), channel_id=1, source_target_pairs={{0,12},{1,13},{2,14},{3,15},{4,8},{5,9},{6,10},{7,11},{8,4},{9,5},... | collective-permute-start | bytes 196616 | tf_op jit(solution)/shard_map/ppermute | solution.py:232
  7.2 0.7 %collective-permute-start.2 = (bf16[16,1024]{1,0:T(8,128)(2,1)S(1)}, bf16[16,1024]{1,0:T(8,128)(2,1)S(1)}, u32[]{:S(2)}, u32[]{:S(2)}) collective-permute-start(bf16[16,1024]{1,0:T(8,128)(2,1)S(1)} %get-tuple-element.64), channel_id=1, source_target_pairs={{0,15},{1,2},{2,1},{3,4},{4,3},{5,6},{6,5},{7,8},{8,7},{9,10},{10,... | collective-permute-start | bytes 98312 | tf_op jit(solution)/shard_map/ppermute | solution.py:232
  7.9 2.5 %collective-permute-start.3 = (bf16[16,1024]{1,0:T(8,128)(2,1)S(1)}, bf16[16,1024]{1,0:T(8,128)(2,1)S(1)}, u32[]{:S(2)}, u32[]{:S(2)}) collective-permute-start(bf16[16,1024]{1,0:T(8,128)(2,1)S(1)} %get-tuple-element.65), channel_id=1, source_target_pairs={{0,3},{1,14},{2,5},{3,0},{4,7},{5,2},{6,9},{7,4},{8,11},{9,6},{10,... | collective-permute-start | bytes 98312 | tf_op jit(solution)/shard_map/ppermute | solution.py:232
  10.4 1.3 %collective-permute-start.4 = (bf16[16,1024]{1,0:T(8,128)(2,1)S(1)}, bf16[16,1024]{1,0:T(8,128)(2,1)S(1)}, u32[]{:S(2)}, u32[]{:S(2)}) collective-permute-start(bf16[16,1024]{1,0:T(8,128)(2,1)S(1)} %get-tuple-element.66), channel_id=1, source_target_pairs={{0,11},{1,6},{2,13},{3,8},{4,15},{5,10},{6,1},{7,12},{8,3},{9,14},... | collective-permute-start | bytes 98312 | tf_op jit(solution)/shard_map/ppermute | solution.py:232
  11.7 1.1 %collective-permute-start.5 = (bf16[16,1024]{1,0:T(8,128)(2,1)S(1)}, bf16[16,1024]{1,0:T(8,128)(2,1)S(1)}, u32[]{:S(2)}, u32[]{:S(2)}) collective-permute-start(bf16[16,1024]{1,0:T(8,128)(2,1)S(1)} %get-tuple-element.67), channel_id=1, source_target_pairs={{0,8},{1,9},{2,10},{3,11},{4,12},{5,13},{6,14},{7,15},{8,0},{9,1},... | collective-permute-start | bytes 98312 | tf_op jit(solution)/shard_map/ppermute | solution.py:232
  13.5 1.3 %collective-permute-start.6 = (bf16[16,1024]{1,0:T(8,128)(2,1)S(1)}, bf16[16,1024]{1,0:T(8,128)(2,1)S(1)}, u32[]{:S(2)}, u32[]{:S(2)}) collective-permute-start(bf16[16,1024]{1,0:T(8,128)(2,1)S(1)} %get-tuple-element.68), channel_id=1, source_target_pairs={{0,1},{1,0},{2,3},{3,2},{4,5},{5,4},{6,7},{7,6},{8,9},{9,8},{10,11... | collective-permute-start | bytes 98312 | tf_op jit(solution)/shard_map/ppermute | solution.py:232
  14.9 5.5 %local_products.1 = (bf16[256,256]{1,0:T(8,128)(2,1)S(1)}, f32[384,512]{1,0:T(8,128)S(1)}, f32[768,512]{1,0:T(8,128)S(1)}, f32[64,512]{1,0:T(8,128)S(1)}, bf16[3...) custom-call(bf16[256,256]{1,0:T(8,128)(2,1)S(1)} %get-tuple-element., ...), custom_call_target="tpu_custom_call" | custom-call | flops 1275068416 | bytes 9774080 | tf_op jit(solution)/shard_map/local_products/pallas_call | solution.py:173
  20.6 4.1 %edges_forward.1 = (bf16[32,1024]{1,0:T(8,128)(2,1)S(1)}, bf16[32,1024]{1,0:T(8,128)(2,1)S(1)}, bf16[16,1024]{1,0:T(8,128)(2,1)S(1)}, bf16[16,1024]{1,0:T(8,128)...) custom-call(bf16[32,1024]{1,0:T(8,128)(2,1)S(1)} %collective-permute, ...), custom_call_target="tpu_custom_call" | custom-call | flops 1207959552 | bytes 16552704 | tf_op jit(solution)/shard_map/edges_forward/pallas_call | solution.py:173
  24.7 1.0 %collective-permute-start.9 = (bf16[32,1024]{1,0:T(8,128)(2,1)S(1)}, bf16[32,1024]{1,0:T(8,128)(2,1)S(1)}, u32[]{:S(2)}, u32[]{:S(2)}) collective-permute-start(bf16[32,1024]{1,0:T(8,128)(2,1)S(1)} %get-tuple-element.77), channel_id=1, source_target_pairs={{0,12},{1,13},{2,14},{3,15},{4,8},{5,9},{6,10},{7,11},{8,4},{9,5},... | collective-permute-start | bytes 196616 | tf_op jit(solution)/shard_map/ppermute | solution.py:232
  26.0 1.9 %collective-permute-start.11 = (bf16[16,1024]{1,0:T(8,128)(2,1)S(1)}, bf16[16,1024]{1,0:T(8,128)(2,1)S(1)}, u32[]{:S(2)}, u32[]{:S(2)}) collective-permute-start(bf16[16,1024]{1,0:T(8,128)(2,1)S(1)} %get-tuple-element.81), channel_id=1, source_target_pairs={{0,15},{1,2},{2,1},{3,4},{4,3},{5,6},{6,5},{7,8},{8,7},{9,10},{10,... | collective-permute-start | bytes 98312 | tf_op jit(solution)/shard_map/ppermute | solution.py:232
  27.9 1.0 %collective-permute-start.12 = (bf16[16,1024]{1,0:T(8,128)(2,1)S(1)}, bf16[16,1024]{1,0:T(8,128)(2,1)S(1)}, u32[]{:S(2)}, u32[]{:S(2)}) collective-permute-start(bf16[16,1024]{1,0:T(8,128)(2,1)S(1)} %get-tuple-element.82), channel_id=1, source_target_pairs={{0,3},{1,14},{2,5},{3,0},{4,7},{5,2},{6,9},{7,4},{8,11},{9,6},{10,... | collective-permute-start | bytes 98312 | tf_op jit(solution)/shard_map/ppermute | solution.py:232
  28.9 1.4 %collective-permute-start.13 = (bf16[16,1024]{1,0:T(8,128)(2,1)S(1)}, bf16[16,1024]{1,0:T(8,128)(2,1)S(1)}, u32[]{:S(2)}, u32[]{:S(2)}) collective-permute-start(bf16[16,1024]{1,0:T(8,128)(2,1)S(1)} %get-tuple-element.83), channel_id=1, source_target_pairs={{0,11},{1,6},{2,13},{3,8},{4,15},{5,10},{6,1},{7,12},{8,3},{9,14},... | collective-permute-start | bytes 98312 | tf_op jit(solution)/shard_map/ppermute | solution.py:232
  30.3 1.1 %collective-permute-done.9.refs_9_ = bf16[32,1024]{1,0:T(8,128)(2,1)S(1)} collective-permute-done((bf16[32,1024]{1,0:T(8,128)(2,1)S(1)}, bf16[32,1024]{1,0:T(8,128)(2,1)S(1)}, u32[]{:S(2)}, u32[]{:S(2)}) %collective-permute-start.9) | collective-permute-done | bytes 65568 | tf_op jit(solution)/shard_map/ppermute | solution.py:232
  32.1 0.9 %collective-permute-start.15 = (bf16[16,1024]{1,0:T(8,128)(2,1)S(1)}, bf16[16,1024]{1,0:T(8,128)(2,1)S(1)}, u32[]{:S(2)}, u32[]{:S(2)}) collective-permute-start(bf16[16,1024]{1,0:T(8,128)(2,1)S(1)} %get-tuple-element.85), channel_id=1, source_target_pairs={{0,1},{1,0},{2,3},{3,2},{4,5},{5,4},{6,7},{7,6},{8,9},{9,8},{10,11... | collective-permute-start | bytes 98312 | tf_op jit(solution)/shard_map/ppermute | solution.py:232
  34.1 2.2 %collective-permute-done.14.refs_14_ = bf16[16,1024]{1,0:T(8,128)(2,1)S(1)} collective-permute-done((bf16[16,1024]{1,0:T(8,128)(2,1)S(1)}, bf16[16,1024]{1,0:T(8,128)(2,1)S(1)}, u32[]{:S(2)}, u32[]{:S(2)}) %collective-permute-start.14) | collective-permute-done | bytes 32800 | tf_op jit(solution)/shard_map/ppermute | solution.py:232
  36.3 7.2 %edges_backward.1 = (bf16[32,512]{1,0:T(8,128)(2,1)S(1)}, bf16[32,512]{1,0:T(8,128)(2,1)S(1)}, bf16[16,512]{1,0:T(8,128)(2,1)S(1)}, bf16[16,512]{1,0:T(8,128)(2,...) custom-call(bf16[32,1024]{1,0:T(8,128)(2,1)S(1)} %collective-permute, ...), custom_call_target="tpu_custom_call" | custom-call | flops 2449473536 | bytes 18502400 | tf_op jit(solution)/shard_map/edges_backward/pallas_call | solution.py:173
  43.6 1.7 %collective-permute-start.18 = (bf16[32,512]{1,0:T(8,128)(2,1)S(1)}, bf16[32,512]{1,0:T(8,128)(2,1)S(1)}, u32[]{:S(2)}, u32[]{:S(2)}) collective-permute-start(bf16[32,512]{1,0:T(8,128)(2,1)S(1)} %get-tuple-element.99), channel_id=1, source_target_pairs={{0,12},{1,13},{2,14},{3,15},{4,8},{5,9},{6,10},{7,11},{8,4},{9,5},... | collective-permute-start | bytes 98312 | tf_op jit(solution)/shard_map/ppermute | solution.py:232
  45.3 1.3 %collective-permute-start.20 = (bf16[16,512]{1,0:T(8,128)(2,1)S(1)}, bf16[16,512]{1,0:T(8,128)(2,1)S(1)}, u32[]{:S(2)}, u32[]{:S(2)}) collective-permute-start(bf16[16,512]{1,0:T(8,128)(2,1)S(1)} %get-tuple-element.103), channel_id=1, source_target_pairs={{0,15},{1,2},{2,1},{3,4},{4,3},{5,6},{6,5},{7,8},{8,7},{9,10},{10,... | collective-permute-start | bytes 49160 | tf_op jit(solution)/shard_map/ppermute | solution.py:232
  46.5 2.0 %collective-permute-start.21 = (bf16[16,512]{1,0:T(8,128)(2,1)S(1)}, bf16[16,512]{1,0:T(8,128)(2,1)S(1)}, u32[]{:S(2)}, u32[]{:S(2)}) collective-permute-start(bf16[16,512]{1,0:T(8,128)(2,1)S(1)} %get-tuple-element.104), channel_id=1, source_target_pairs={{0,3},{1,14},{2,5},{3,0},{4,7},{5,2},{6,9},{7,4},{8,11},{9,6},{10,... | collective-permute-start | bytes 49160 | tf_op jit(solution)/shard_map/ppermute | solution.py:232
  48.5 1.7 %collective-permute-start.22 = (bf16[16,512]{1,0:T(8,128)(2,1)S(1)}, bf16[16,512]{1,0:T(8,128)(2,1)S(1)}, u32[]{:S(2)}, u32[]{:S(2)}) collective-permute-start(bf16[16,512]{1,0:T(8,128)(2,1)S(1)} %get-tuple-element.105), channel_id=1, source_target_pairs={{0,11},{1,6},{2,13},{3,8},{4,15},{5,10},{6,1},{7,12},{8,3},{9,14},... | collective-permute-start | bytes 49160 | tf_op jit(solution)/shard_map/ppermute | solution.py:232
  51.8 1.1 %collective-permute-start.24 = (bf16[16,512]{1,0:T(8,128)(2,1)S(1)}, bf16[16,512]{1,0:T(8,128)(2,1)S(1)}, u32[]{:S(2)}, u32[]{:S(2)}) collective-permute-start(bf16[16,512]{1,0:T(8,128)(2,1)S(1)} %get-tuple-element.107), channel_id=1, source_target_pairs={{0,1},{1,0},{2,3},{3,2},{4,5},{5,4},{6,7},{7,6},{8,9},{9,8},{10,11... | collective-permute-start | bytes 49160 | tf_op jit(solution)/shard_map/ppermute | solution.py:232
  52.9 1.5 %local_gradients.1 = (f32[256,512]{1,0:T(8,128)S(1)}, f32[64,512]{1,0:T(8,128)}) custom-call(bf16[256,512]{1,0:T(8,128)(2,1)S(1)} %copy-done.5, bf16[256,512]{1,0:T(8,128)(2,1)S(1)} %get-tuple-element.108.refs_1_, bf16[256,512]{1,0:T(8,128)(2,1)S(1)} %get-tuple-element.109.refs_2_, bf16[256,512]{1,0:T(8,128)(2,1)S(1)} %get-tuple-element.110.refs_3_, ...), custom_call_target="tpu_custom_call" | custom-call | flops 402653184 | bytes 8781824 | tf_op jit(solution)/shard_map/local_gradients/pallas_call | solution.py:173
  55.1 1.0 %add_returned.1 = f32[256,512]{1,0:T(8,128)} custom-call(bf16[32,512]{1,0:T(8,128)(2,1)S(1)} %collective-permute-done.18.refs_0_, bf16[32,512]{1,0:T(8,128)(2,1)S(1)} %collective-permute-done.19.refs_1_, bf16[16,512]{1,0:T(8,128)(2,1)S(1)} %collective-permute-done.20.refs_2_, bf16[16,512]{1,0:T(8,128)(2,1)S(1)} %collective-permute-done.21.refs_3_, ...), custom_call_target="tpu_custom_call" | custom-call | flops 37748736 | bytes 1392640 | tf_op jit(solution)/shard_map/add_returned/pallas_call | solution.py:173
  (61 shorter events, 5.1 us)
Async XLA Ops:
  2.1 9.6 %collective-permute-start = (bf16[32,1024]{1,0:T(8,128)(2,1)S(1)}, bf16[32,1024]{1,0:T(8,128)(2,1)S(1)}, u32[]{:S(2)}, u32[]{:S(2)}) collective-permute-start(bf16[32,1024]{1,0:T(8,128)(2,1)S(1)} %get-tuple-element.60), channel_id=1, source_target_pairs={{0,12},{1,13},{2,14},{3,15},{4,8},{5,9},{6,10},{7,11},{8,4},{9,5},... | collective-permute-start | bytes 196616 | tf_op jit(solution)/shard_map/ppermute | solution.py:232
  7.2 7.7 %collective-permute-start.1 = (bf16[32,1024]{1,0:T(8,128)(2,1)S(1)}, bf16[32,1024]{1,0:T(8,128)(2,1)S(1)}, u32[]{:S(2)}, u32[]{:S(2)}) collective-permute-start(bf16[32,1024]{1,0:T(8,128)(2,1)S(1)} %get-tuple-element.63), channel_id=1, source_target_pairs={{0,4},{1,5},{2,6},{3,7},{4,0},{5,1},{6,2},{7,3},{8,12},{9,13},{10,... | collective-permute-start | bytes 196616 | tf_op jit(solution)/shard_map/ppermute | solution.py:232
  7.2 6.0 %collective-permute-start.2 = (bf16[16,1024]{1,0:T(8,128)(2,1)S(1)}, bf16[16,1024]{1,0:T(8,128)(2,1)S(1)}, u32[]{:S(2)}, u32[]{:S(2)}) collective-permute-start(bf16[16,1024]{1,0:T(8,128)(2,1)S(1)} %get-tuple-element.64), channel_id=1, source_target_pairs={{0,15},{1,2},{2,1},{3,4},{4,3},{5,6},{6,5},{7,8},{8,7},{9,10},{10,... | collective-permute-start | bytes 98312 | tf_op jit(solution)/shard_map/ppermute | solution.py:232
  7.9 5.6 %collective-permute-start.3 = (bf16[16,1024]{1,0:T(8,128)(2,1)S(1)}, bf16[16,1024]{1,0:T(8,128)(2,1)S(1)}, u32[]{:S(2)}, u32[]{:S(2)}) collective-permute-start(bf16[16,1024]{1,0:T(8,128)(2,1)S(1)} %get-tuple-element.65), channel_id=1, source_target_pairs={{0,3},{1,14},{2,5},{3,0},{4,7},{5,2},{6,9},{7,4},{8,11},{9,6},{10,... | collective-permute-start | bytes 98312 | tf_op jit(solution)/shard_map/ppermute | solution.py:232
  10.4 10.1 %collective-permute-start.4 = (bf16[16,1024]{1,0:T(8,128)(2,1)S(1)}, bf16[16,1024]{1,0:T(8,128)(2,1)S(1)}, u32[]{:S(2)}, u32[]{:S(2)}) collective-permute-start(bf16[16,1024]{1,0:T(8,128)(2,1)S(1)} %get-tuple-element.66), channel_id=1, source_target_pairs={{0,11},{1,6},{2,13},{3,8},{4,15},{5,10},{6,1},{7,12},{8,3},{9,14},... | collective-permute-start | bytes 98312 | tf_op jit(solution)/shard_map/ppermute | solution.py:232
  11.7 8.8 %collective-permute-start.5 = (bf16[16,1024]{1,0:T(8,128)(2,1)S(1)}, bf16[16,1024]{1,0:T(8,128)(2,1)S(1)}, u32[]{:S(2)}, u32[]{:S(2)}) collective-permute-start(bf16[16,1024]{1,0:T(8,128)(2,1)S(1)} %get-tuple-element.67), channel_id=1, source_target_pairs={{0,8},{1,9},{2,10},{3,11},{4,12},{5,13},{6,14},{7,15},{8,0},{9,1},... | collective-permute-start | bytes 98312 | tf_op jit(solution)/shard_map/ppermute | solution.py:232
  13.2 7.3 %collective-permute-start.7 = (bf16[32,1024]{1,0:T(8,128)(2,1)S(1)}, bf16[32,1024]{1,0:T(8,128)(2,1)S(1)}, u32[]{:S(2)}, u32[]{:S(2)}) collective-permute-start(bf16[32,1024]{1,0:T(8,128)(2,1)S(1)} %collective-permute-done.refs_0_), channel_id=1, source_target_pairs={{0,1},{1,0},{2,3},{3,2},{4,5},{5,4},{6,7},{7,6},{8,9},{9,8},{10,11... | collective-permute-start | bytes 196616 | tf_op jit(solution)/shard_map/ppermute | solution.py:232
  13.5 6.9 %collective-permute-start.6 = (bf16[16,1024]{1,0:T(8,128)(2,1)S(1)}, bf16[16,1024]{1,0:T(8,128)(2,1)S(1)}, u32[]{:S(2)}, u32[]{:S(2)}) collective-permute-start(bf16[16,1024]{1,0:T(8,128)(2,1)S(1)} %get-tuple-element.68), channel_id=1, source_target_pairs={{0,1},{1,0},{2,3},{3,2},{4,5},{5,4},{6,7},{7,6},{8,9},{9,8},{10,11... | collective-permute-start | bytes 98312 | tf_op jit(solution)/shard_map/ppermute | solution.py:232
  14.9 5.6 %collective-permute-start.8 = (bf16[32,1024]{1,0:T(8,128)(2,1)S(1)}, bf16[32,1024]{1,0:T(8,128)(2,1)S(1)}, u32[]{:S(2)}, u32[]{:S(2)}) collective-permute-start(bf16[32,1024]{1,0:T(8,128)(2,1)S(1)} %collective-permute-done.1.refs_1_), channel_id=1, source_target_pairs={{0,1},{1,0},{2,3},{3,2},{4,5},{5,4},{6,7},{7,6},{8,9},{9,8},{10,11... | collective-permute-start | bytes 196616 | tf_op jit(solution)/shard_map/ppermute | solution.py:232
  24.7 6.8 %collective-permute-start.9 = (bf16[32,1024]{1,0:T(8,128)(2,1)S(1)}, bf16[32,1024]{1,0:T(8,128)(2,1)S(1)}, u32[]{:S(2)}, u32[]{:S(2)}) collective-permute-start(bf16[32,1024]{1,0:T(8,128)(2,1)S(1)} %get-tuple-element.77), channel_id=1, source_target_pairs={{0,12},{1,13},{2,14},{3,15},{4,8},{5,9},{6,10},{7,11},{8,4},{9,5},... | collective-permute-start | bytes 196616 | tf_op jit(solution)/shard_map/ppermute | solution.py:232
  25.7 7.3 %collective-permute-start.10 = (bf16[32,1024]{1,0:T(8,128)(2,1)S(1)}, bf16[32,1024]{1,0:T(8,128)(2,1)S(1)}, u32[]{:S(2)}, u32[]{:S(2)}) collective-permute-start(bf16[32,1024]{1,0:T(8,128)(2,1)S(1)} %get-tuple-element.80), channel_id=1, source_target_pairs={{0,4},{1,5},{2,6},{3,7},{4,0},{5,1},{6,2},{7,3},{8,12},{9,13},{10,... | collective-permute-start | bytes 196616 | tf_op jit(solution)/shard_map/ppermute | solution.py:232
  26.0 6.0 %collective-permute-start.11 = (bf16[16,1024]{1,0:T(8,128)(2,1)S(1)}, bf16[16,1024]{1,0:T(8,128)(2,1)S(1)}, u32[]{:S(2)}, u32[]{:S(2)}) collective-permute-start(bf16[16,1024]{1,0:T(8,128)(2,1)S(1)} %get-tuple-element.81), channel_id=1, source_target_pairs={{0,15},{1,2},{2,1},{3,4},{4,3},{5,6},{6,5},{7,8},{8,7},{9,10},{10,... | collective-permute-start | bytes 98312 | tf_op jit(solution)/shard_map/ppermute | solution.py:232
  27.9 4.2 %collective-permute-start.12 = (bf16[16,1024]{1,0:T(8,128)(2,1)S(1)}, bf16[16,1024]{1,0:T(8,128)(2,1)S(1)}, u32[]{:S(2)}, u32[]{:S(2)}) collective-permute-start(bf16[16,1024]{1,0:T(8,128)(2,1)S(1)} %get-tuple-element.82), channel_id=1, source_target_pairs={{0,3},{1,14},{2,5},{3,0},{4,7},{5,2},{6,9},{7,4},{8,11},{9,6},{10,... | collective-permute-start | bytes 98312 | tf_op jit(solution)/shard_map/ppermute | solution.py:232
  28.9 5.1 %collective-permute-start.13 = (bf16[16,1024]{1,0:T(8,128)(2,1)S(1)}, bf16[16,1024]{1,0:T(8,128)(2,1)S(1)}, u32[]{:S(2)}, u32[]{:S(2)}) collective-permute-start(bf16[16,1024]{1,0:T(8,128)(2,1)S(1)} %get-tuple-element.83), channel_id=1, source_target_pairs={{0,11},{1,6},{2,13},{3,8},{4,15},{5,10},{6,1},{7,12},{8,3},{9,14},... | collective-permute-start | bytes 98312 | tf_op jit(solution)/shard_map/ppermute | solution.py:232
  31.4 4.8 %collective-permute-start.14 = (bf16[16,1024]{1,0:T(8,128)(2,1)S(1)}, bf16[16,1024]{1,0:T(8,128)(2,1)S(1)}, u32[]{:S(2)}, u32[]{:S(2)}) collective-permute-start(bf16[16,1024]{1,0:T(8,128)(2,1)S(1)} %get-tuple-element.84), channel_id=1, source_target_pairs={{0,8},{1,9},{2,10},{3,11},{4,12},{5,13},{6,14},{7,15},{8,0},{9,1},... | collective-permute-start | bytes 98312 | tf_op jit(solution)/shard_map/ppermute | solution.py:232
  32.1 4.2 %collective-permute-start.16 = (bf16[32,1024]{1,0:T(8,128)(2,1)S(1)}, bf16[32,1024]{1,0:T(8,128)(2,1)S(1)}, u32[]{:S(2)}, u32[]{:S(2)}) collective-permute-start(bf16[32,1024]{1,0:T(8,128)(2,1)S(1)} %collective-permute-done.9.refs_9_), channel_id=1, source_target_pairs={{0,1},{1,0},{2,3},{3,2},{4,5},{5,4},{6,7},{7,6},{8,9},{9,8},{10,11... | collective-permute-start | bytes 196616 | tf_op jit(solution)/shard_map/ppermute | solution.py:232
  32.1 4.2 %collective-permute-start.15 = (bf16[16,1024]{1,0:T(8,128)(2,1)S(1)}, bf16[16,1024]{1,0:T(8,128)(2,1)S(1)}, u32[]{:S(2)}, u32[]{:S(2)}) collective-permute-start(bf16[16,1024]{1,0:T(8,128)(2,1)S(1)} %get-tuple-element.85), channel_id=1, source_target_pairs={{0,1},{1,0},{2,3},{3,2},{4,5},{5,4},{6,7},{7,6},{8,9},{9,8},{10,11... | collective-permute-start | bytes 98312 | tf_op jit(solution)/shard_map/ppermute | solution.py:232
  43.6 6.6 %collective-permute-start.18 = (bf16[32,512]{1,0:T(8,128)(2,1)S(1)}, bf16[32,512]{1,0:T(8,128)(2,1)S(1)}, u32[]{:S(2)}, u32[]{:S(2)}) collective-permute-start(bf16[32,512]{1,0:T(8,128)(2,1)S(1)} %get-tuple-element.99), channel_id=1, source_target_pairs={{0,12},{1,13},{2,14},{3,15},{4,8},{5,9},{6,10},{7,11},{8,4},{9,5},... | collective-permute-start | bytes 98312 | tf_op jit(solution)/shard_map/ppermute | solution.py:232
  45.3 7.6 %collective-permute-start.19 = (bf16[32,512]{1,0:T(8,128)(2,1)S(1)}, bf16[32,512]{1,0:T(8,128)(2,1)S(1)}, u32[]{:S(2)}, u32[]{:S(2)}) collective-permute-start(bf16[32,512]{1,0:T(8,128)(2,1)S(1)} %get-tuple-element.102), channel_id=1, source_target_pairs={{0,4},{1,5},{2,6},{3,7},{4,0},{5,1},{6,2},{7,3},{8,12},{9,13},{10,... | collective-permute-start | bytes 98312 | tf_op jit(solution)/shard_map/ppermute | solution.py:232
  45.3 5.9 %collective-permute-start.20 = (bf16[16,512]{1,0:T(8,128)(2,1)S(1)}, bf16[16,512]{1,0:T(8,128)(2,1)S(1)}, u32[]{:S(2)}, u32[]{:S(2)}) collective-permute-start(bf16[16,512]{1,0:T(8,128)(2,1)S(1)} %get-tuple-element.103), channel_id=1, source_target_pairs={{0,15},{1,2},{2,1},{3,4},{4,3},{5,6},{6,5},{7,8},{8,7},{9,10},{10,... | collective-permute-start | bytes 49160 | tf_op jit(solution)/shard_map/ppermute | solution.py:232
  46.5 5.2 %collective-permute-start.21 = (bf16[16,512]{1,0:T(8,128)(2,1)S(1)}, bf16[16,512]{1,0:T(8,128)(2,1)S(1)}, u32[]{:S(2)}, u32[]{:S(2)}) collective-permute-start(bf16[16,512]{1,0:T(8,128)(2,1)S(1)} %get-tuple-element.104), channel_id=1, source_target_pairs={{0,3},{1,14},{2,5},{3,0},{4,7},{5,2},{6,9},{7,4},{8,11},{9,6},{10,... | collective-permute-start | bytes 49160 | tf_op jit(solution)/shard_map/ppermute | solution.py:232
  48.5 5.9 %collective-permute-start.22 = (bf16[16,512]{1,0:T(8,128)(2,1)S(1)}, bf16[16,512]{1,0:T(8,128)(2,1)S(1)}, u32[]{:S(2)}, u32[]{:S(2)}) collective-permute-start(bf16[16,512]{1,0:T(8,128)(2,1)S(1)} %get-tuple-element.105), channel_id=1, source_target_pairs={{0,11},{1,6},{2,13},{3,8},{4,15},{5,10},{6,1},{7,12},{8,3},{9,14},... | collective-permute-start | bytes 49160 | tf_op jit(solution)/shard_map/ppermute | solution.py:232
  50.2 4.9 %collective-permute-start.23 = (bf16[16,512]{1,0:T(8,128)(2,1)S(1)}, bf16[16,512]{1,0:T(8,128)(2,1)S(1)}, u32[]{:S(2)}, u32[]{:S(2)}) collective-permute-start(bf16[16,512]{1,0:T(8,128)(2,1)S(1)} %get-tuple-element.106), channel_id=1, source_target_pairs={{0,8},{1,9},{2,10},{3,11},{4,12},{5,13},{6,14},{7,15},{8,0},{9,1},... | collective-permute-start | bytes 49160 | tf_op jit(solution)/shard_map/ppermute | solution.py:232
  51.1 3.9 %collective-permute-start.25 = (bf16[32,512]{1,0:T(8,128)(2,1)S(1)}, bf16[32,512]{1,0:T(8,128)(2,1)S(1)}, u32[]{:S(2)}, u32[]{:S(2)}) collective-permute-start(bf16[32,512]{1,0:T(8,128)(2,1)S(1)} %collective-permute-done.18.refs_0_), channel_id=1, source_target_pairs={{0,1},{1,0},{2,3},{3,2},{4,5},{5,4},{6,7},{7,6},{8,9},{9,8},{10,11... | collective-permute-start | bytes 98312 | tf_op jit(solution)/shard_map/ppermute | solution.py:232
  (15 other events, 86.1 us)

commit v8 on v7

--- a/solution.py
+++ b/solution.py
@@ -91,28 +91,34 @@
     edges, total = by_edge_ref.shape
     spot_row = spot_ref[...].reshape(1, -1)
     mesh_row = mesh_ref[...].reshape(1, -1) + spots
-
-    def ones(hit):
-        return jnp.where(hit, 1.0, 0.0).astype(BF16)
+    one, zero = jnp.ones((), BF16), jnp.zeros((), BF16)
+
+    def ones(ids, index):
+        shape = jnp.broadcast_shapes(ids.shape, index.shape)
+        hit = jnp.broadcast_to(ids, shape) == jnp.broadcast_to(index, shape)
+        return jnp.where(hit, jnp.broadcast_to(one, shape), jnp.broadcast_to(zero, shape))
 
     for row, first, count in ((spot_row, 0, spots), (mesh_row, spots, mesh_count)):
+        ids = lax.broadcasted_iota(jnp.int32, (16, edges), 0).astype(jnp.int16)
+        wide = jnp.broadcast_to(row, (16, edges)).astype(jnp.int16)
         for rows in row_chunks(count, 16):
-            ids = lax.broadcasted_iota(jnp.int32, (16, edges), 0)
             rows = slice(rows.start + first, rows.stop + first)
-            by_spot_ref[rows, :] = ones(ids == row - rows.start)
+            by_spot_ref[rows, :] = ones(ids, wide - jnp.int16(rows.start))
     by_spot_ref[spots + mesh_count :, :] = jnp.zeros((total - spots - mesh_count, edges), BF16)
-    lane = lax.broadcasted_iota(jnp.int32, (1, 128), 1)
+    lane = lax.broadcasted_iota(jnp.int32, (16, 128), 1).astype(jnp.int16)
     for rows in row_chunks(edges, 128):
-        spot_col = jnp.broadcast_to(spot_row[:, rows], (128, 128)).T
-        mesh_col = jnp.broadcast_to(mesh_row[:, rows], (128, 128)).T
+        spot_col = jnp.broadcast_to(spot_row[:, rows], (128, 128)).T.astype(jnp.int16)
+        mesh_col = jnp.broadcast_to(mesh_row[:, rows], (128, 128)).T.astype(jnp.int16)
         for columns in row_chunks(total, 128):
-            hit = None
-            if columns.start < spots:
-                hit = lane + columns.start == spot_col
-            if columns.stop > spots:
-                mesh_hit = lane + columns.start == mesh_col
-                hit = mesh_hit if hit is None else hit | mesh_hit
-            by_edge_ref[rows, columns] = ones(hit)
+            for part in row_chunks(128, 16):
+                place = slice(rows.start + part.start, rows.start + part.stop)
+                ids = lane + jnp.int16(columns.start)
+                hits = []
+                if columns.start < spots:
+                    hits.append(ones(ids, spot_col[part, :]))
+                if columns.stop > spots:
+                    hits.append(ones(ids, mesh_col[part, :]))
+                by_edge_ref[place, columns] = sum(hits[1:], hits[0])
 
 
 class Fetched:
@@ -471,7 +477,7 @@
         ) = refs
         rows = by_slot(arrived_refs, low)
         pe = mm(rows, enc_wg_ref[low, :]).astype(BF16)
-        for block in row_blocks(enc_count, 3):
+        for block in row_blocks(enc_count, 1):
             pre = enc_part_ref[block, :] + mm(enc_pick_ref[block, grid_count:spots], pe)
             activate(pre, enc_act_ref, enc_slope_ref, block)
             raw = mm(enc_act_ref[block, :], enc_w2_ref[...])
@@ -489,7 +495,7 @@
         table_ref[slots + mesh_count :, :] = jnp.zeros(
             (total - spots - mesh_count, feat), BF16
         )
-        for block in row_blocks(dec_count, 3):
+        for block in row_blocks(dec_count, 1):
             pre = dec_part_ref[block, :] + mm(dec_pick_ref[block, grid_count:], table_ref[...])
             activate(pre, dec_act_ref, dec_slope_ref, block)
             raw = mm(dec_act_ref[block, :], dec_w2_ref[...])
@@ -550,17 +556,32 @@
     mesh_out, spot_msg, *saved = results
     returned = exchange(outgoing)
 
+    turned = [
+        (grid_first, feat),
+        (grid_second, 0),
+        (dec_second, 0),
+        (dec_first, feat),
+        (mesh_first, feat),
+        (mesh_second, 0),
+        (enc_second, 0),
+        (enc_first, 0),
+        (dec_first, 0),
+    ]
+
     def node_part(*refs):
-        arrived_refs = refs[:arrived_count]
-        nodes_ref, weight_ref, out_ref = refs[arrived_count:]
+        arrived_refs, refs = refs[:arrived_count], refs[arrived_count:]
+        (nodes_ref, weight_ref, _), refs = refs[:3], refs[3:]
+        weight_refs, (out_ref, *turned_refs) = refs[: len(turned)], refs[len(turned) :]
         out_ref[:grid_count, :] = mm(nodes_ref[...], weight_ref[low, :])
         out_ref[grid_count:, :] = mm(by_slot(arrived_refs, low), weight_ref[low, :])
-
-    (grid_part,) = call(
+        for ref, (_, first), turned_ref in zip(weight_refs, turned, turned_refs):
+            turned_ref[...] = ref[first : first + feat, :].T
+
+    grid_part, *turned_weights = call(
         node_part,
         "node_products",
-        [*arrived, grid_nodes, grid_first],
-        [((spots, feat), F32)],
+        [*arrived, grid_nodes, grid_first, mesh_out, *[weight for weight, _ in turned]],
+        [((spots, feat), F32)] + [((feat, feat), BF16)] * len(turned),
         flops=16 * spots * feat * feat,
     )
 
@@ -580,13 +601,15 @@
             dec_pool_ref,
             grid_wa_ref,
             grid_w2_ref,
-            dec_w2_ref,
-            dec_wm_ref,
-            mesh_wa_ref,
-            mesh_w2_ref,
-            enc_w2_ref,
-            enc_wg_ref,
-            dec_wg_ref,
+            grid_wat_ref,
+            grid_w2t_ref,
+            dec_w2t_ref,
+            dec_wmt_ref,
+            mesh_wat_ref,
+            mesh_w2t_ref,
+            enc_w2t_ref,
+            enc_wgt_ref,
+            dec_wgt_ref,
             enc_normed_ref,
             enc_scale_ref,
             enc_slope_ref,
@@ -596,8 +619,8 @@
             mesh_normed_ref,
             mesh_scale_ref,
             mesh_slope_ref,
-        ) = refs[:28]
-        refs = refs[28:]
+        ) = refs[:30]
+        refs = refs[30:]
         out_refs, refs = refs[:sent_count], refs[sent_count:]
         (
             grid_out_ref,
@@ -629,7 +652,7 @@
         cot_rows_ref[:grid_count, :] = cot_ref[...]
         cot_rows_ref[grid_count:, :] = by_slot(arrived_refs, high)
         spot_grad_ref[spots:, :] = jnp.zeros((total - spots, feat), BF16)
-        for block in row_blocks(spots, 2):
+        for block in row_blocks(spots, 1):
             pre = grid_part_ref[block, :] + mm(agg_ref[block, :], grid_wa_ref[high, :])
             activate(pre, grid_act_ref, grid_slope_ref, block)
             raw = mm(grid_act_ref[block, :], grid_w2_ref[...])
@@ -637,41 +660,37 @@
             norm_backward(
                 grid_normed_ref, grid_scale_ref, cot_rows_ref[block, :], grid_gout_ref, block
             )
-            raw = mm_t(grid_gout_ref[block, :], grid_w2_ref[...])
+            raw = mm(grid_gout_ref[block, :], grid_w2t_ref[...])
             times_slope(raw, grid_slope_ref, grid_gall_ref, block)
-            spot_grad_ref[block, :] = mm_t(
-                grid_gall_ref[block, :], grid_wa_ref[high, :]
-            ).astype(BF16)
+            spot_grad_ref[block, :] = mm(grid_gall_ref[block, :], grid_wat_ref[...]).astype(BF16)
         grid_out_ref[...] = (
             nodes_ref[...].astype(F32) + grid_normed_ref[:grid_count, :]
         ).astype(BF16)
         grid_gpre_ref[...] = grid_gall_ref[:grid_count, :]
-        for block in row_blocks(dec_count, 3):
+        for block in row_blocks(dec_count, 1):
             upstream = mm(dec_pick_ref[block, :], spot_grad_ref[...])
             norm_backward(dec_normed_ref, dec_scale_ref, upstream, dec_gout_ref, block)
-            raw = mm_t(dec_gout_ref[block, :], dec_w2_ref[...])
+            raw = mm(dec_gout_ref[block, :], dec_w2t_ref[...])
             times_slope(raw, dec_slope_ref, dec_gout_ref, block)
         pooled = mm(dec_pool_ref[...], dec_gout_ref[...]).astype(BF16)
         gpd_ref[...] = pooled[:grid_count, :]
-        slot_back = mm_t(pooled[grid_count:spots, :], dec_wg_ref[low, :])
-        mesh_gin = mesh_cot_ref[...].astype(F32) + mm_t(
-            pooled[mesh_rows, :], dec_wm_ref[high, :]
-        )
+        slot_back = mm(pooled[grid_count:spots, :], dec_wgt_ref[...])
+        mesh_gin = mesh_cot_ref[...].astype(F32) + mm(pooled[mesh_rows, :], dec_wmt_ref[...])
         mesh_gin_ref[...] = mesh_gin
         whole = slice(0, mesh_count)
         norm_backward(mesh_normed_ref, mesh_scale_ref, mesh_gin, mesh_gout_ref, whole)
-        raw = mm_t(mesh_gout_ref[...], mesh_w2_ref[...])
+        raw = mm(mesh_gout_ref[...], mesh_w2t_ref[...])
         times_slope(raw, mesh_slope_ref, mesh_gpre_ref, whole)
-        gagg = mm_t(mesh_gpre_ref[...], mesh_wa_ref[high, :]).astype(BF16)
-        for block in row_blocks(enc_count, 3):
+        gagg = mm(mesh_gpre_ref[...], mesh_wat_ref[...]).astype(BF16)
+        for block in row_blocks(enc_count, 1):
             upstream = mm(enc_pick_ref[block, mesh_rows], gagg)
             norm_backward(enc_normed_ref, enc_scale_ref, upstream, enc_gout_ref, block)
-            raw = mm_t(enc_gout_ref[block, :], enc_w2_ref[...])
+            raw = mm(enc_gout_ref[block, :], enc_w2t_ref[...])
             times_slope(raw, enc_slope_ref, enc_gout_ref, block)
         pooled = mm(enc_pool_ref[...], enc_gout_ref[...]).astype(BF16)
         gpe_ref[...] = pooled[:grid_count, :]
         mesh_pool_ref[...] = pooled[mesh_rows, :]
-        slot_back = (slot_back + mm_t(pooled[grid_count:spots, :], enc_wg_ref[low, :])).astype(BF16)
+        slot_back = (slot_back + mm(pooled[grid_count:spots, :], enc_wgt_ref[...])).astype(BF16)
         send(out_refs, lambda j: slot_back[reverse[j] * width : (reverse[j] + 1) * width, :])
 
     results = call(
@@ -692,13 +711,7 @@
             dec_pool,
             grid_first,
             grid_second,
-            dec_second,
-            dec_first,
-            mesh_first,
-            mesh_second,
-            enc_second,
-            enc_first,
-            dec_first,
+            *turned_weights,
             *saved,
         ],
         sent_shapes(feat)

time: 56.2 us -> 54.6 us (0.972)
  waiting for transfers between devices: 5.47 us -> 3.7 us
  local copies, waits for them, and re-layouts: 0.07 us -> 0.9 us
  Pallas kernels: 21.2 us -> 20.5 us
    ppermute x27, waiting for transfers between devices: 5.47 us -> 3.7 us  [permute(): return lax.ppermute(part, 'tile', pairs)]
    unnamed x24 -> x26, local copies, waits for them, and re-layouts: 0.07 us -> 0.9 us
    pallas_call x7, Pallas kernels: 21.2 us -> 20.5 us  [call(): pl.pallas_call(kernel, name=name, in_specs=specs, out_specs=[pl.BlockSpec...]
  transfers between devices with their start and end apart: 27 -> 27, of which waited for: 7 -> 6; matrix products, arithmetic and copies ran while one was open for 0% -> 0% of each run, Pallas kernels for 13% -> 15%
where the time goes in v8:
time: 54.6 us; the launch traced here: 54.4 us
  starting transfers between devices  28.4 us (52%)
  Pallas kernels  20.5 us (38%)
  waiting for transfers between devices  3.7 us (7%)
  between operations  0.91 us (2%)
  local copies, waits for them, and re-layouts  0.9 us (2%)
    ppermute x27, starting transfers between devices, permute(): return lax.ppermute(part, 'tile', pairs)  28.4 us
    pallas_call x7, Pallas kernels, call(): pl.pallas_call(kernel, name=name, in_specs=specs, out_specs=[pl.BlockSpec...  20.5 us
    ppermute x27, waiting for transfers between devices, permute(): return lax.ppermute(part, 'tile', pairs)  3.7 us
  transfers between devices with their start and end apart: 27, of which 6 were waited for; matrix products, arithmetic and copies ran while one was open for 0% of the time, Pallas kernels for 15%

profile of v8, /device:TPU:0, one launch (start us, length us, event | category | flops | bytes accessed | tf_op | source)
XLA Modules:
  0.0 54.4 jit_solution(3205092992079777906)
XLA Ops:
  0.6 1.4 %pack_rows.1 = (bf16[256,256]{1,0:T(8,128)(2,1)S(1)}, bf16[32,1024]{1,0:T(8,128)(2,1)S(1)}, bf16[32,1024]{1,0:T(8,128)(2,1)S(1)}, bf16[16,1024]{1,0:T(8,128)(2,1...) custom-call(s32[9,16]{1,0:T(8,128)} %refs_0_.2, ...), custom_call_target="tpu_custom_call" | custom-call | flops 75497472 | bytes 950884 | tf_op jit(solution)/shard_map/pack_rows/pallas_call | solution.py:179
  2.1 5.1 %collective-permute-start = (bf16[32,1024]{1,0:T(8,128)(2,1)S(1)}, bf16[32,1024]{1,0:T(8,128)(2,1)S(1)}, u32[]{:S(2)}, u32[]{:S(2)}) collective-permute-start(bf16[32,1024]{1,0:T(8,128)(2,1)S(1)} %get-tuple-element.70), channel_id=1, source_target_pairs={{0,12},{1,13},{2,14},{3,15},{4,8},{5,9},{6,10},{7,11},{8,4},{9,5},... | collective-permute-start | bytes 196616 | tf_op jit(solution)/shard_map/ppermute | solution.py:238
  7.9 2.5 %collective-permute-start.3 = (bf16[16,1024]{1,0:T(8,128)(2,1)S(1)}, bf16[16,1024]{1,0:T(8,128)(2,1)S(1)}, u32[]{:S(2)}, u32[]{:S(2)}) collective-permute-start(bf16[16,1024]{1,0:T(8,128)(2,1)S(1)} %get-tuple-element.75), channel_id=1, source_target_pairs={{0,3},{1,14},{2,5},{3,0},{4,7},{5,2},{6,9},{7,4},{8,11},{9,6},{10,... | collective-permute-start | bytes 98312 | tf_op jit(solution)/shard_map/ppermute | solution.py:238
  10.4 1.3 %collective-permute-start.4 = (bf16[16,1024]{1,0:T(8,128)(2,1)S(1)}, bf16[16,1024]{1,0:T(8,128)(2,1)S(1)}, u32[]{:S(2)}, u32[]{:S(2)}) collective-permute-start(bf16[16,1024]{1,0:T(8,128)(2,1)S(1)} %get-tuple-element.76), channel_id=1, source_target_pairs={{0,11},{1,6},{2,13},{3,8},{4,15},{5,10},{6,1},{7,12},{8,3},{9,14},... | collective-permute-start | bytes 98312 | tf_op jit(solution)/shard_map/ppermute | solution.py:238
  11.7 1.1 %collective-permute-start.5 = (bf16[16,1024]{1,0:T(8,128)(2,1)S(1)}, bf16[16,1024]{1,0:T(8,128)(2,1)S(1)}, u32[]{:S(2)}, u32[]{:S(2)}) collective-permute-start(bf16[16,1024]{1,0:T(8,128)(2,1)S(1)} %get-tuple-element.77), channel_id=1, source_target_pairs={{0,8},{1,9},{2,10},{3,11},{4,12},{5,13},{6,14},{7,15},{8,0},{9,1},... | collective-permute-start | bytes 98312 | tf_op jit(solution)/shard_map/ppermute | solution.py:238
  13.5 1.3 %collective-permute-start.7 = (bf16[32,1024]{1,0:T(8,128)(2,1)S(1)}, bf16[32,1024]{1,0:T(8,128)(2,1)S(1)}, u32[]{:S(2)}, u32[]{:S(2)}) collective-permute-start(bf16[32,1024]{1,0:T(8,128)(2,1)S(1)} %collective-permute-done.refs_0_), channel_id=1, source_target_pairs={{0,1},{1,0},{2,3},{3,2},{4,5},{5,4},{6,7},{7,6},{8,9},{9,8},{10,11... | collective-permute-start | bytes 196616 | tf_op jit(solution)/shard_map/ppermute | solution.py:238
  14.9 5.4 %local_products.1 = (bf16[256,256]{1,0:T(8,128)(2,1)S(1)}, f32[384,512]{1,0:T(8,128)S(1)}, f32[768,512]{1,0:T(8,128)S(1)}, f32[64,512]{1,0:T(8,128)S(1)}, bf16[3...) custom-call(bf16[256,256]{1,0:T(8,128)(2,1)S(1)} %get-tuple-element., ...), custom_call_target="tpu_custom_call" | custom-call | flops 1275068416 | bytes 9774080 | tf_op jit(solution)/shard_map/local_products/pallas_call | solution.py:179
  20.5 3.6 %edges_forward.1 = (bf16[32,1024]{1,0:T(8,128)(2,1)S(1)}, bf16[32,1024]{1,0:T(8,128)(2,1)S(1)}, bf16[16,1024]{1,0:T(8,128)(2,1)S(1)}, bf16[16,1024]{1,0:T(8,128)...) custom-call(bf16[32,1024]{1,0:T(8,128)(2,1)S(1)} %collective-permute, ...), custom_call_target="tpu_custom_call" | custom-call | flops 1207959552 | bytes 16552704 | tf_op jit(solution)/shard_map/edges_forward/pallas_call | solution.py:179
  24.1 1.0 %collective-permute-start.9 = (bf16[32,1024]{1,0:T(8,128)(2,1)S(1)}, bf16[32,1024]{1,0:T(8,128)(2,1)S(1)}, u32[]{:S(2)}, u32[]{:S(2)}) collective-permute-start(bf16[32,1024]{1,0:T(8,128)(2,1)S(1)} %get-tuple-element.87), channel_id=1, source_target_pairs={{0,12},{1,13},{2,14},{3,15},{4,8},{5,9},{6,10},{7,11},{8,4},{9,5},... | collective-permute-start | bytes 196616 | tf_op jit(solution)/shard_map/ppermute | solution.py:238
  25.4 1.9 %collective-permute-start.11 = (bf16[16,1024]{1,0:T(8,128)(2,1)S(1)}, bf16[16,1024]{1,0:T(8,128)(2,1)S(1)}, u32[]{:S(2)}, u32[]{:S(2)}) collective-permute-start(bf16[16,1024]{1,0:T(8,128)(2,1)S(1)} %get-tuple-element.91), channel_id=1, source_target_pairs={{0,15},{1,2},{2,1},{3,4},{4,3},{5,6},{6,5},{7,8},{8,7},{9,10},{10,... | collective-permute-start | bytes 98312 | tf_op jit(solution)/shard_map/ppermute | solution.py:238
  27.3 1.1 %collective-permute-start.12 = (bf16[16,1024]{1,0:T(8,128)(2,1)S(1)}, bf16[16,1024]{1,0:T(8,128)(2,1)S(1)}, u32[]{:S(2)}, u32[]{:S(2)}) collective-permute-start(bf16[16,1024]{1,0:T(8,128)(2,1)S(1)} %get-tuple-element.92), channel_id=1, source_target_pairs={{0,3},{1,14},{2,5},{3,0},{4,7},{5,2},{6,9},{7,4},{8,11},{9,6},{10,... | collective-permute-start | bytes 98312 | tf_op jit(solution)/shard_map/ppermute | solution.py:238
  28.3 1.4 %collective-permute-start.13 = (bf16[16,1024]{1,0:T(8,128)(2,1)S(1)}, bf16[16,1024]{1,0:T(8,128)(2,1)S(1)}, u32[]{:S(2)}, u32[]{:S(2)}) collective-permute-start(bf16[16,1024]{1,0:T(8,128)(2,1)S(1)} %get-tuple-element.93), channel_id=1, source_target_pairs={{0,11},{1,6},{2,13},{3,8},{4,15},{5,10},{6,1},{7,12},{8,3},{9,14},... | collective-permute-start | bytes 98312 | tf_op jit(solution)/shard_map/ppermute | solution.py:238
  29.7 1.1 %collective-permute-done.9.refs_9_ = bf16[32,1024]{1,0:T(8,128)(2,1)S(1)} collective-permute-done((bf16[32,1024]{1,0:T(8,128)(2,1)S(1)}, bf16[32,1024]{1,0:T(8,128)(2,1)S(1)}, u32[]{:S(2)}, u32[]{:S(2)}) %collective-permute-start.9) | collective-permute-done | bytes 65568 | tf_op jit(solution)/shard_map/ppermute | solution.py:238
  31.5 1.0 %collective-permute-start.16 = (bf16[32,1024]{1,0:T(8,128)(2,1)S(1)}, bf16[32,1024]{1,0:T(8,128)(2,1)S(1)}, u32[]{:S(2)}, u32[]{:S(2)}) collective-permute-start(bf16[32,1024]{1,0:T(8,128)(2,1)S(1)} %collective-permute-done.9.refs_9_), channel_id=1, source_target_pairs={{0,1},{1,0},{2,3},{3,2},{4,5},{5,4},{6,7},{7,6},{8,9},{9,8},{10,11... | collective-permute-start | bytes 196616 | tf_op jit(solution)/shard_map/ppermute | solution.py:238
  33.3 1.3 %node_products.1 = (f32[400,512]{1,0:T(8,128)S(1)}, bf16[512,512]{1,0:T(8,128)(2,1)S(1)}, bf16[512,512]{1,0:T(8,128)(2,1)S(1)}, bf16[512,512]{1,0:T(8,128)(2,1)S...) custom-call(bf16[32,1024]{1,0:T(8,128)(2,1)S(1)} %collective-permute, ...), custom_call_target="tpu_custom_call" | custom-call | flops 1677721600 | bytes 16252928 | tf_op jit(solution)/shard_map/node_products/pallas_call | solution.py:179
  34.7 1.1 %collective-permute-done.14.refs_14_ = bf16[16,1024]{1,0:T(8,128)(2,1)S(1)} collective-permute-done((bf16[16,1024]{1,0:T(8,128)(2,1)S(1)}, bf16[16,1024]{1,0:T(8,128)(2,1)S(1)}, u32[]{:S(2)}, u32[]{:S(2)}) %collective-permute-start.14) | collective-permute-done | bytes 32800 | tf_op jit(solution)/shard_map/ppermute | solution.py:238
  35.8 6.3 %edges_backward.1 = (bf16[32,512]{1,0:T(8,128)(2,1)S(1)}, bf16[32,512]{1,0:T(8,128)(2,1)S(1)}, bf16[16,512]{1,0:T(8,128)(2,1)S(1)}, bf16[16,512]{1,0:T(8,128)(2,...) custom-call(bf16[32,1024]{1,0:T(8,128)(2,1)S(1)} %collective-permute, ...), custom_call_target="tpu_custom_call" | custom-call | flops 2449473536 | bytes 15880960 | tf_op jit(solution)/shard_map/edges_backward/pallas_call | solution.py:179
  42.0 1.6 %collective-permute-start.18 = (bf16[32,512]{1,0:T(8,128)(2,1)S(1)}, bf16[32,512]{1,0:T(8,128)(2,1)S(1)}, u32[]{:S(2)}, u32[]{:S(2)}) collective-permute-start(bf16[32,512]{1,0:T(8,128)(2,1)S(1)} %get-tuple-element.119), channel_id=1, source_target_pairs={{0,12},{1,13},{2,14},{3,15},{4,8},{5,9},{6,10},{7,11},{8,4},{9,5},... | collective-permute-start | bytes 98312 | tf_op jit(solution)/shard_map/ppermute | solution.py:238
  43.6 1.4 %collective-permute-start.20 = (bf16[16,512]{1,0:T(8,128)(2,1)S(1)}, bf16[16,512]{1,0:T(8,128)(2,1)S(1)}, u32[]{:S(2)}, u32[]{:S(2)}) collective-permute-start(bf16[16,512]{1,0:T(8,128)(2,1)S(1)} %get-tuple-element.123), channel_id=1, source_target_pairs={{0,15},{1,2},{2,1},{3,4},{4,3},{5,6},{6,5},{7,8},{8,7},{9,10},{10,... | collective-permute-start | bytes 49160 | tf_op jit(solution)/shard_map/ppermute | solution.py:238
  45.0 1.8 %collective-permute-start.21 = (bf16[16,512]{1,0:T(8,128)(2,1)S(1)}, bf16[16,512]{1,0:T(8,128)(2,1)S(1)}, u32[]{:S(2)}, u32[]{:S(2)}) collective-permute-start(bf16[16,512]{1,0:T(8,128)(2,1)S(1)} %get-tuple-element.124), channel_id=1, source_target_pairs={{0,3},{1,14},{2,5},{3,0},{4,7},{5,2},{6,9},{7,4},{8,11},{9,6},{10,... | collective-permute-start | bytes 49160 | tf_op jit(solution)/shard_map/ppermute | solution.py:238
  46.8 1.7 %collective-permute-start.22 = (bf16[16,512]{1,0:T(8,128)(2,1)S(1)}, bf16[16,512]{1,0:T(8,128)(2,1)S(1)}, u32[]{:S(2)}, u32[]{:S(2)}) collective-permute-start(bf16[16,512]{1,0:T(8,128)(2,1)S(1)} %get-tuple-element.125), channel_id=1, source_target_pairs={{0,11},{1,6},{2,13},{3,8},{4,15},{5,10},{6,1},{7,12},{8,3},{9,14},... | collective-permute-start | bytes 49160 | tf_op jit(solution)/shard_map/ppermute | solution.py:238
  50.1 1.1 %collective-permute-start.25 = (bf16[32,512]{1,0:T(8,128)(2,1)S(1)}, bf16[32,512]{1,0:T(8,128)(2,1)S(1)}, u32[]{:S(2)}, u32[]{:S(2)}) collective-permute-start(bf16[32,512]{1,0:T(8,128)(2,1)S(1)} %collective-permute-done.18.refs_0_), channel_id=1, source_target_pairs={{0,1},{1,0},{2,3},{3,2},{4,5},{5,4},{6,7},{7,6},{8,9},{9,8},{10,11... | collective-permute-start | bytes 98312 | tf_op jit(solution)/shard_map/ppermute | solution.py:238
  51.2 1.5 %local_gradients.1 = (f32[256,512]{1,0:T(8,128)S(1)}, f32[64,512]{1,0:T(8,128)}) custom-call(bf16[256,512]{1,0:T(8,128)(2,1)S(1)} %copy-done.5, bf16[256,512]{1,0:T(8,128)(2,1)S(1)} %get-tuple-element.128.refs_1_, bf16[256,512]{1,0:T(8,128)(2,1)S(1)} %get-tuple-element.129.refs_2_, bf16[256,512]{1,0:T(8,128)(2,1)S(1)} %get-tuple-element.130.refs_3_, ...), custom_call_target="tpu_custom_call" | custom-call | flops 402653184 | bytes 8781824 | tf_op jit(solution)/shard_map/local_gradients/pallas_call | solution.py:179
  53.4 1.0 %add_returned.1 = f32[256,512]{1,0:T(8,128)} custom-call(bf16[32,512]{1,0:T(8,128)(2,1)S(1)} %collective-permute-done.18.refs_0_, bf16[32,512]{1,0:T(8,128)(2,1)S(1)} %collective-permute-done.19.refs_1_, bf16[16,512]{1,0:T(8,128)(2,1)S(1)} %collective-permute-done.20.refs_2_, bf16[16,512]{1,0:T(8,128)(2,1)S(1)} %collective-permute-done.21.refs_3_, ...), custom_call_target="tpu_custom_call" | custom-call | flops 37748736 | bytes 1392640 | tf_op jit(solution)/shard_map/add_returned/pallas_call | solution.py:179
  (63 shorter events, 5.6 us)
Async XLA Ops:
  2.1 9.6 %collective-permute-start = (bf16[32,1024]{1,0:T(8,128)(2,1)S(1)}, bf16[32,1024]{1,0:T(8,128)(2,1)S(1)}, u32[]{:S(2)}, u32[]{:S(2)}) collective-permute-start(bf16[32,1024]{1,0:T(8,128)(2,1)S(1)} %get-tuple-element.70), channel_id=1, source_target_pairs={{0,12},{1,13},{2,14},{3,15},{4,8},{5,9},{6,10},{7,11},{8,4},{9,5},... | collective-permute-start | bytes 196616 | tf_op jit(solution)/shard_map/ppermute | solution.py:238
  7.2 7.7 %collective-permute-start.1 = (bf16[32,1024]{1,0:T(8,128)(2,1)S(1)}, bf16[32,1024]{1,0:T(8,128)(2,1)S(1)}, u32[]{:S(2)}, u32[]{:S(2)}) collective-permute-start(bf16[32,1024]{1,0:T(8,128)(2,1)S(1)} %get-tuple-element.73), channel_id=1, source_target_pairs={{0,4},{1,5},{2,6},{3,7},{4,0},{5,1},{6,2},{7,3},{8,12},{9,13},{10,... | collective-permute-start | bytes 196616 | tf_op jit(solution)/shard_map/ppermute | solution.py:238
  7.2 6.0 %collective-permute-start.2 = (bf16[16,1024]{1,0:T(8,128)(2,1)S(1)}, bf16[16,1024]{1,0:T(8,128)(2,1)S(1)}, u32[]{:S(2)}, u32[]{:S(2)}) collective-permute-start(bf16[16,1024]{1,0:T(8,128)(2,1)S(1)} %get-tuple-element.74), channel_id=1, source_target_pairs={{0,15},{1,2},{2,1},{3,4},{4,3},{5,6},{6,5},{7,8},{8,7},{9,10},{10,... | collective-permute-start | bytes 98312 | tf_op jit(solution)/shard_map/ppermute | solution.py:238
  7.9 5.6 %collective-permute-start.3 = (bf16[16,1024]{1,0:T(8,128)(2,1)S(1)}, bf16[16,1024]{1,0:T(8,128)(2,1)S(1)}, u32[]{:S(2)}, u32[]{:S(2)}) collective-permute-start(bf16[16,1024]{1,0:T(8,128)(2,1)S(1)} %get-tuple-element.75), channel_id=1, source_target_pairs={{0,3},{1,14},{2,5},{3,0},{4,7},{5,2},{6,9},{7,4},{8,11},{9,6},{10,... | collective-permute-start | bytes 98312 | tf_op jit(solution)/shard_map/ppermute | solution.py:238
  10.4 9.9 %collective-permute-start.4 = (bf16[16,1024]{1,0:T(8,128)(2,1)S(1)}, bf16[16,1024]{1,0:T(8,128)(2,1)S(1)}, u32[]{:S(2)}, u32[]{:S(2)}) collective-permute-start(bf16[16,1024]{1,0:T(8,128)(2,1)S(1)} %get-tuple-element.76), channel_id=1, source_target_pairs={{0,11},{1,6},{2,13},{3,8},{4,15},{5,10},{6,1},{7,12},{8,3},{9,14},... | collective-permute-start | bytes 98312 | tf_op jit(solution)/shard_map/ppermute | solution.py:238
  11.7 8.6 %collective-permute-start.5 = (bf16[16,1024]{1,0:T(8,128)(2,1)S(1)}, bf16[16,1024]{1,0:T(8,128)(2,1)S(1)}, u32[]{:S(2)}, u32[]{:S(2)}) collective-permute-start(bf16[16,1024]{1,0:T(8,128)(2,1)S(1)} %get-tuple-element.77), channel_id=1, source_target_pairs={{0,8},{1,9},{2,10},{3,11},{4,12},{5,13},{6,14},{7,15},{8,0},{9,1},... | collective-permute-start | bytes 98312 | tf_op jit(solution)/shard_map/ppermute | solution.py:238
  13.2 7.1 %collective-permute-start.6 = (bf16[16,1024]{1,0:T(8,128)(2,1)S(1)}, bf16[16,1024]{1,0:T(8,128)(2,1)S(1)}, u32[]{:S(2)}, u32[]{:S(2)}) collective-permute-start(bf16[16,1024]{1,0:T(8,128)(2,1)S(1)} %get-tuple-element.78), channel_id=1, source_target_pairs={{0,1},{1,0},{2,3},{3,2},{4,5},{5,4},{6,7},{7,6},{8,9},{9,8},{10,11... | collective-permute-start | bytes 98312 | tf_op jit(solution)/shard_map/ppermute | solution.py:238
  13.5 6.8 %collective-permute-start.7 = (bf16[32,1024]{1,0:T(8,128)(2,1)S(1)}, bf16[32,1024]{1,0:T(8,128)(2,1)S(1)}, u32[]{:S(2)}, u32[]{:S(2)}) collective-permute-start(bf16[32,1024]{1,0:T(8,128)(2,1)S(1)} %collective-permute-done.refs_0_), channel_id=1, source_target_pairs={{0,1},{1,0},{2,3},{3,2},{4,5},{5,4},{6,7},{7,6},{8,9},{9,8},{10,11... | collective-permute-start | bytes 196616 | tf_op jit(solution)/shard_map/ppermute | solution.py:238
  14.9 5.5 %collective-permute-start.8 = (bf16[32,1024]{1,0:T(8,128)(2,1)S(1)}, bf16[32,1024]{1,0:T(8,128)(2,1)S(1)}, u32[]{:S(2)}, u32[]{:S(2)}) collective-permute-start(bf16[32,1024]{1,0:T(8,128)(2,1)S(1)} %collective-permute-done.1.refs_1_), channel_id=1, source_target_pairs={{0,1},{1,0},{2,3},{3,2},{4,5},{5,4},{6,7},{7,6},{8,9},{9,8},{10,11... | collective-permute-start | bytes 196616 | tf_op jit(solution)/shard_map/ppermute | solution.py:238
  24.1 6.8 %collective-permute-start.9 = (bf16[32,1024]{1,0:T(8,128)(2,1)S(1)}, bf16[32,1024]{1,0:T(8,128)(2,1)S(1)}, u32[]{:S(2)}, u32[]{:S(2)}) collective-permute-start(bf16[32,1024]{1,0:T(8,128)(2,1)S(1)} %get-tuple-element.87), channel_id=1, source_target_pairs={{0,12},{1,13},{2,14},{3,15},{4,8},{5,9},{6,10},{7,11},{8,4},{9,5},... | collective-permute-start | bytes 196616 | tf_op jit(solution)/shard_map/ppermute | solution.py:238
  25.1 7.3 %collective-permute-start.10 = (bf16[32,1024]{1,0:T(8,128)(2,1)S(1)}, bf16[32,1024]{1,0:T(8,128)(2,1)S(1)}, u32[]{:S(2)}, u32[]{:S(2)}) collective-permute-start(bf16[32,1024]{1,0:T(8,128)(2,1)S(1)} %get-tuple-element.90), channel_id=1, source_target_pairs={{0,4},{1,5},{2,6},{3,7},{4,0},{5,1},{6,2},{7,3},{8,12},{9,13},{10,... | collective-permute-start | bytes 196616 | tf_op jit(solution)/shard_map/ppermute | solution.py:238
  25.4 6.0 %collective-permute-start.11 = (bf16[16,1024]{1,0:T(8,128)(2,1)S(1)}, bf16[16,1024]{1,0:T(8,128)(2,1)S(1)}, u32[]{:S(2)}, u32[]{:S(2)}) collective-permute-start(bf16[16,1024]{1,0:T(8,128)(2,1)S(1)} %get-tuple-element.91), channel_id=1, source_target_pairs={{0,15},{1,2},{2,1},{3,4},{4,3},{5,6},{6,5},{7,8},{8,7},{9,10},{10,... | collective-permute-start | bytes 98312 | tf_op jit(solution)/shard_map/ppermute | solution.py:238
  27.3 4.2 %collective-permute-start.12 = (bf16[16,1024]{1,0:T(8,128)(2,1)S(1)}, bf16[16,1024]{1,0:T(8,128)(2,1)S(1)}, u32[]{:S(2)}, u32[]{:S(2)}) collective-permute-start(bf16[16,1024]{1,0:T(8,128)(2,1)S(1)} %get-tuple-element.92), channel_id=1, source_target_pairs={{0,3},{1,14},{2,5},{3,0},{4,7},{5,2},{6,9},{7,4},{8,11},{9,6},{10,... | collective-permute-start | bytes 98312 | tf_op jit(solution)/shard_map/ppermute | solution.py:238
  28.3 6.3 %collective-permute-start.13 = (bf16[16,1024]{1,0:T(8,128)(2,1)S(1)}, bf16[16,1024]{1,0:T(8,128)(2,1)S(1)}, u32[]{:S(2)}, u32[]{:S(2)}) collective-permute-start(bf16[16,1024]{1,0:T(8,128)(2,1)S(1)} %get-tuple-element.93), channel_id=1, source_target_pairs={{0,11},{1,6},{2,13},{3,8},{4,15},{5,10},{6,1},{7,12},{8,3},{9,14},... | collective-permute-start | bytes 98312 | tf_op jit(solution)/shard_map/ppermute | solution.py:238
  30.8 4.9 %collective-permute-start.14 = (bf16[16,1024]{1,0:T(8,128)(2,1)S(1)}, bf16[16,1024]{1,0:T(8,128)(2,1)S(1)}, u32[]{:S(2)}, u32[]{:S(2)}) collective-permute-start(bf16[16,1024]{1,0:T(8,128)(2,1)S(1)} %get-tuple-element.94), channel_id=1, source_target_pairs={{0,8},{1,9},{2,10},{3,11},{4,12},{5,13},{6,14},{7,15},{8,0},{9,1},... | collective-permute-start | bytes 98312 | tf_op jit(solution)/shard_map/ppermute | solution.py:238
  31.5 4.3 %collective-permute-start.15 = (bf16[16,1024]{1,0:T(8,128)(2,1)S(1)}, bf16[16,1024]{1,0:T(8,128)(2,1)S(1)}, u32[]{:S(2)}, u32[]{:S(2)}) collective-permute-start(bf16[16,1024]{1,0:T(8,128)(2,1)S(1)} %get-tuple-element.95), channel_id=1, source_target_pairs={{0,1},{1,0},{2,3},{3,2},{4,5},{5,4},{6,7},{7,6},{8,9},{9,8},{10,11... | collective-permute-start | bytes 98312 | tf_op jit(solution)/shard_map/ppermute | solution.py:238
  31.5 4.3 %collective-permute-start.16 = (bf16[32,1024]{1,0:T(8,128)(2,1)S(1)}, bf16[32,1024]{1,0:T(8,128)(2,1)S(1)}, u32[]{:S(2)}, u32[]{:S(2)}) collective-permute-start(bf16[32,1024]{1,0:T(8,128)(2,1)S(1)} %collective-permute-done.9.refs_9_), channel_id=1, source_target_pairs={{0,1},{1,0},{2,3},{3,2},{4,5},{5,4},{6,7},{7,6},{8,9},{9,8},{10,11... | collective-permute-start | bytes 196616 | tf_op jit(solution)/shard_map/ppermute | solution.py:238
  42.0 6.5 %collective-permute-start.18 = (bf16[32,512]{1,0:T(8,128)(2,1)S(1)}, bf16[32,512]{1,0:T(8,128)(2,1)S(1)}, u32[]{:S(2)}, u32[]{:S(2)}) collective-permute-start(bf16[32,512]{1,0:T(8,128)(2,1)S(1)} %get-tuple-element.119), channel_id=1, source_target_pairs={{0,12},{1,13},{2,14},{3,15},{4,8},{5,9},{6,10},{7,11},{8,4},{9,5},... | collective-permute-start | bytes 98312 | tf_op jit(solution)/shard_map/ppermute | solution.py:238
  43.6 7.6 %collective-permute-start.19 = (bf16[32,512]{1,0:T(8,128)(2,1)S(1)}, bf16[32,512]{1,0:T(8,128)(2,1)S(1)}, u32[]{:S(2)}, u32[]{:S(2)}) collective-permute-start(bf16[32,512]{1,0:T(8,128)(2,1)S(1)} %get-tuple-element.122), channel_id=1, source_target_pairs={{0,4},{1,5},{2,6},{3,7},{4,0},{5,1},{6,2},{7,3},{8,12},{9,13},{10,... | collective-permute-start | bytes 98312 | tf_op jit(solution)/shard_map/ppermute | solution.py:238
  43.6 5.9 %collective-permute-start.20 = (bf16[16,512]{1,0:T(8,128)(2,1)S(1)}, bf16[16,512]{1,0:T(8,128)(2,1)S(1)}, u32[]{:S(2)}, u32[]{:S(2)}) collective-permute-start(bf16[16,512]{1,0:T(8,128)(2,1)S(1)} %get-tuple-element.123), channel_id=1, source_target_pairs={{0,15},{1,2},{2,1},{3,4},{4,3},{5,6},{6,5},{7,8},{8,7},{9,10},{10,... | collective-permute-start | bytes 49160 | tf_op jit(solution)/shard_map/ppermute | solution.py:238
  45.0 5.1 %collective-permute-start.21 = (bf16[16,512]{1,0:T(8,128)(2,1)S(1)}, bf16[16,512]{1,0:T(8,128)(2,1)S(1)}, u32[]{:S(2)}, u32[]{:S(2)}) collective-permute-start(bf16[16,512]{1,0:T(8,128)(2,1)S(1)} %get-tuple-element.124), channel_id=1, source_target_pairs={{0,3},{1,14},{2,5},{3,0},{4,7},{5,2},{6,9},{7,4},{8,11},{9,6},{10,... | collective-permute-start | bytes 49160 | tf_op jit(solution)/shard_map/ppermute | solution.py:238
  46.8 5.9 %collective-permute-start.22 = (bf16[16,512]{1,0:T(8,128)(2,1)S(1)}, bf16[16,512]{1,0:T(8,128)(2,1)S(1)}, u32[]{:S(2)}, u32[]{:S(2)}) collective-permute-start(bf16[16,512]{1,0:T(8,128)(2,1)S(1)} %get-tuple-element.125), channel_id=1, source_target_pairs={{0,11},{1,6},{2,13},{3,8},{4,15},{5,10},{6,1},{7,12},{8,3},{9,14},... | collective-permute-start | bytes 49160 | tf_op jit(solution)/shard_map/ppermute | solution.py:238
  48.5 4.9 %collective-permute-start.23 = (bf16[16,512]{1,0:T(8,128)(2,1)S(1)}, bf16[16,512]{1,0:T(8,128)(2,1)S(1)}, u32[]{:S(2)}, u32[]{:S(2)}) collective-permute-start(bf16[16,512]{1,0:T(8,128)(2,1)S(1)} %get-tuple-element.126), channel_id=1, source_target_pairs={{0,8},{1,9},{2,10},{3,11},{4,12},{5,13},{6,14},{7,15},{8,0},{9,1},... | collective-permute-start | bytes 49160 | tf_op jit(solution)/shard_map/ppermute | solution.py:238
  49.5 3.9 %collective-permute-start.24 = (bf16[16,512]{1,0:T(8,128)(2,1)S(1)}, bf16[16,512]{1,0:T(8,128)(2,1)S(1)}, u32[]{:S(2)}, u32[]{:S(2)}) collective-permute-start(bf16[16,512]{1,0:T(8,128)(2,1)S(1)} %get-tuple-element.127), channel_id=1, source_target_pairs={{0,1},{1,0},{2,3},{3,2},{4,5},{5,4},{6,7},{7,6},{8,9},{9,8},{10,11... | collective-permute-start | bytes 49160 | tf_op jit(solution)/shard_map/ppermute | solution.py:238
  (16 other events, 89.0 us)

commit v9 on v7

--- a/solution.py
+++ b/solution.py
@@ -7,6 +7,7 @@
 
 TW = 4
 CHUNK = 32
+ROUND_FLOPS = 2 * 10**10
 F32 = jnp.float32
 BF16 = jnp.bfloat16
 VMEM_LIMIT = 30 * 1024 * 1024
@@ -91,28 +92,34 @@
     edges, total = by_edge_ref.shape
     spot_row = spot_ref[...].reshape(1, -1)
     mesh_row = mesh_ref[...].reshape(1, -1) + spots
-
-    def ones(hit):
-        return jnp.where(hit, 1.0, 0.0).astype(BF16)
+    one, zero = jnp.ones((), BF16), jnp.zeros((), BF16)
+
+    def ones(ids, index):
+        shape = jnp.broadcast_shapes(ids.shape, index.shape)
+        hit = jnp.broadcast_to(ids, shape) == jnp.broadcast_to(index, shape)
+        return jnp.where(hit, jnp.broadcast_to(one, shape), jnp.broadcast_to(zero, shape))
 
     for row, first, count in ((spot_row, 0, spots), (mesh_row, spots, mesh_count)):
+        ids = lax.broadcasted_iota(jnp.int32, (16, edges), 0).astype(jnp.int16)
+        wide = jnp.broadcast_to(row, (16, edges)).astype(jnp.int16)
         for rows in row_chunks(count, 16):
-            ids = lax.broadcasted_iota(jnp.int32, (16, edges), 0)
             rows = slice(rows.start + first, rows.stop + first)
-            by_spot_ref[rows, :] = ones(ids == row - rows.start)
+            by_spot_ref[rows, :] = ones(ids, wide - jnp.int16(rows.start))
     by_spot_ref[spots + mesh_count :, :] = jnp.zeros((total - spots - mesh_count, edges), BF16)
-    lane = lax.broadcasted_iota(jnp.int32, (1, 128), 1)
+    lane = lax.broadcasted_iota(jnp.int32, (16, 128), 1).astype(jnp.int16)
     for rows in row_chunks(edges, 128):
-        spot_col = jnp.broadcast_to(spot_row[:, rows], (128, 128)).T
-        mesh_col = jnp.broadcast_to(mesh_row[:, rows], (128, 128)).T
+        spot_col = jnp.broadcast_to(spot_row[:, rows], (128, 128)).T.astype(jnp.int16)
+        mesh_col = jnp.broadcast_to(mesh_row[:, rows], (128, 128)).T.astype(jnp.int16)
         for columns in row_chunks(total, 128):
-            hit = None
-            if columns.start < spots:
-                hit = lane + columns.start == spot_col
-            if columns.stop > spots:
-                mesh_hit = lane + columns.start == mesh_col
-                hit = mesh_hit if hit is None else hit | mesh_hit
-            by_edge_ref[rows, columns] = ones(hit)
+            for part in row_chunks(128, 16):
+                place = slice(rows.start + part.start, rows.start + part.stop)
+                ids = lane + jnp.int16(columns.start)
+                hits = []
+                if columns.start < spots:
+                    hits.append(ones(ids, spot_col[part, :]))
+                if columns.stop > spots:
+                    hits.append(ones(ids, mesh_col[part, :]))
+                by_edge_ref[place, columns] = sum(hits[1:], hits[0])
 
 
 class Fetched:
@@ -354,25 +361,27 @@
         [((slots_pad, grid_count), BF16)] + sent_shapes(2 * feat),
         flops=4 * slots * grid_count * feat,
     )
+    def turn(select_ref, select_t_ref):
+        select_t_ref[...] = select_ref[...].astype(F32).T.astype(BF16)
+
+    (select_t,) = call(
+        turn, "turn_select", [select], [((grid_count, slots_pad), BF16)], flops=ROUND_FLOPS
+    )
+    *outgoing, select_t = lax.optimization_barrier((*outgoing, select_t))
     arrived = exchange(outgoing)
 
     def local(
-        select_ref,
         nodes_ref,
         mesh_ref,
         enc_edges_ref,
         dec_edges_ref,
-        enc_wg_ref,
-        enc_wm_ref,
-        enc_we_ref,
-        dec_wg_ref,
-        dec_we_ref,
-        mesh_wn_ref,
+        enc_first_ref,
+        dec_first_ref,
+        mesh_first_ref,
         enc_grid_ref,
         enc_mesh_ref,
         dec_grid_ref,
         dec_mesh_ref,
-        select_t_ref,
         enc_part_ref,
         dec_part_ref,
         mesh_part_ref,
@@ -384,40 +393,34 @@
     ):
         onehot_pair(enc_grid_ref, enc_mesh_ref, spots, mesh_count, enc_pick_ref, enc_pool_ref)
         onehot_pair(dec_grid_ref, dec_mesh_ref, spots, mesh_count, dec_pick_ref, dec_pool_ref)
-        select_t_ref[...] = select_ref[...].astype(F32).T.astype(BF16)
         nodes = nodes_ref[...]
-        mesh_part_ref[...] = mm(mesh_ref[...], mesh_wn_ref[...])
-        table_ref[:grid_count, :] = mm(nodes, enc_wg_ref[...]).astype(BF16)
+        mesh_part_ref[...] = mm(mesh_ref[...], mesh_first_ref[low, :])
+        table_ref[:grid_count, :] = mm(nodes, enc_first_ref[low, :]).astype(BF16)
         table_ref[grid_count:, :] = jnp.zeros((total - grid_count, feat), BF16)
-        table_ref[mesh_rows, :] = mm(mesh_ref[...], enc_wm_ref[...]).astype(BF16)
-        enc_part_ref[...] = mm(enc_edges_ref[...], enc_we_ref[...])
+        table_ref[mesh_rows, :] = mm(mesh_ref[...], enc_first_ref[high, :]).astype(BF16)
+        enc_part_ref[...] = mm(enc_edges_ref[...], enc_first_ref[2 * feat :, :])
         enc_part_ref[...] += mm(enc_pick_ref[...], table_ref[...])
-        pd = mm(nodes, dec_wg_ref[...]).astype(BF16)
-        dec_part_ref[...] = mm(dec_edges_ref[...], dec_we_ref[...])
+        pd = mm(nodes, dec_first_ref[low, :]).astype(BF16)
+        dec_part_ref[...] = mm(dec_edges_ref[...], dec_first_ref[2 * feat :, :])
         dec_part_ref[...] += mm(dec_pick_ref[:, :grid_count], pd)
 
-    select_t, enc_part, dec_part, mesh_part, enc_pick, enc_pool, dec_pick, dec_pool = call(
+    enc_part, dec_part, mesh_part, enc_pick, enc_pool, dec_pick, dec_pool = call(
         local,
         "local_products",
         [
-            select,
-            (grid_nodes, 0, grid_count),
-            (mesh_nodes, 0, mesh_count),
-            (enc_edges, 0, enc_count),
-            (dec_edges, 0, dec_count),
-            (enc_first, 0, feat),
-            (enc_first, feat, feat),
-            (enc_first, 2 * feat, feat),
-            (dec_first, 0, feat),
-            (dec_first, 2 * feat, feat),
-            (mesh_first, 0, feat),
-            (enc_grid, 0, enc_grid.shape[0]),
-            (enc_mesh, 0, enc_mesh.shape[0]),
-            (dec_grid, 0, dec_grid.shape[0]),
-            (dec_mesh, 0, dec_mesh.shape[0]),
+            grid_nodes,
+            mesh_nodes,
+            enc_edges,
+            dec_edges,
+            enc_first,
+            dec_first,
+            mesh_first,
+            enc_grid,
+            enc_mesh,
+            dec_grid,
+            dec_mesh,
         ],
         [
-            ((grid_count, slots_pad), BF16),
             ((enc_count, feat), F32),
             ((dec_count, feat), F32),
             ((mesh_count, feat), F32),
@@ -471,7 +474,7 @@
         ) = refs
         rows = by_slot(arrived_refs, low)
         pe = mm(rows, enc_wg_ref[low, :]).astype(BF16)
-        for block in row_blocks(enc_count, 3):
+        for block in row_blocks(enc_count, 1):
             pre = enc_part_ref[block, :] + mm(enc_pick_ref[block, grid_count:spots], pe)
             activate(pre, enc_act_ref, enc_slope_ref, block)
             raw = mm(enc_act_ref[block, :], enc_w2_ref[...])
@@ -489,7 +492,7 @@
         table_ref[slots + mesh_count :, :] = jnp.zeros(
             (total - spots - mesh_count, feat), BF16
         )
-        for block in row_blocks(dec_count, 3):
+        for block in row_blocks(dec_count, 1):
             pre = dec_part_ref[block, :] + mm(dec_pick_ref[block, grid_count:], table_ref[...])
             activate(pre, dec_act_ref, dec_slope_ref, block)
             raw = mm(dec_act_ref[block, :], dec_w2_ref[...])
@@ -629,7 +632,7 @@
         cot_rows_ref[:grid_count, :] = cot_ref[...]
         cot_rows_ref[grid_count:, :] = by_slot(arrived_refs, high)
         spot_grad_ref[spots:, :] = jnp.zeros((total - spots, feat), BF16)
-        for block in row_blocks(spots, 2):
+        for block in row_blocks(spots, 1):
             pre = grid_part_ref[block, :] + mm(agg_ref[block, :], grid_wa_ref[high, :])
             activate(pre, grid_act_ref, grid_slope_ref, block)
             raw = mm(grid_act_ref[block, :], grid_w2_ref[...])
@@ -646,7 +649,7 @@
             nodes_ref[...].astype(F32) + grid_normed_ref[:grid_count, :]
         ).astype(BF16)
         grid_gpre_ref[...] = grid_gall_ref[:grid_count, :]
-        for block in row_blocks(dec_count, 3):
+        for block in row_blocks(dec_count, 1):
             upstream = mm(dec_pick_ref[block, :], spot_grad_ref[...])
             norm_backward(dec_normed_ref, dec_scale_ref, upstream, dec_gout_ref, block)
             raw = mm_t(dec_gout_ref[block, :], dec_w2_ref[...])
@@ -654,16 +657,14 @@
         pooled = mm(dec_pool_ref[...], dec_gout_ref[...]).astype(BF16)
         gpd_ref[...] = pooled[:grid_count, :]
         slot_back = mm_t(pooled[grid_count:spots, :], dec_wg_ref[low, :])
-        mesh_gin = mesh_cot_ref[...].astype(F32) + mm_t(
-            pooled[mesh_rows, :], dec_wm_ref[high, :]
-        )
+        mesh_gin = mesh_cot_ref[...].astype(F32) + mm_t(pooled[mesh_rows, :], dec_wm_ref[high, :])
         mesh_gin_ref[...] = mesh_gin
         whole = slice(0, mesh_count)
         norm_backward(mesh_normed_ref, mesh_scale_ref, mesh_gin, mesh_gout_ref, whole)
         raw = mm_t(mesh_gout_ref[...], mesh_w2_ref[...])
         times_slope(raw, mesh_slope_ref, mesh_gpre_ref, whole)
         gagg = mm_t(mesh_gpre_ref[...], mesh_wa_ref[high, :]).astype(BF16)
-        for block in row_blocks(enc_count, 3):
+        for block in row_blocks(enc_count, 1):
             upstream = mm(enc_pick_ref[block, mesh_rows], gagg)
             norm_backward(enc_normed_ref, enc_scale_ref, upstream, enc_gout_ref, block)
             raw = mm_t(enc_gout_ref[block, :], enc_w2_ref[...])

time: 56.2 us -> 51.2 us (0.911)
  Pallas kernels: 21.2 us -> 15.7 us
    pallas_call x7 -> x8, Pallas kernels: 21.2 us -> 15.7 us  [call(): pl.pallas_call(kernel, name=name, in_specs=specs, out_specs=[pl.BlockSpec...]
  transfers between devices with their start and end apart: 27 -> 27, of which waited for: 7 -> 8; matrix products, arithmetic and copies ran while one was open for 0% -> 0% of each run, Pallas kernels for 13% -> 7%
where the time goes in v9:
time: 51.2 us; the launch traced here: 51 us
  starting transfers between devices  28.4 us (55%)
  Pallas kernels  15.7 us (31%)
  waiting for transfers between devices  5.87 us (11%)
  between operations  0.97 us (2%)
    ppermute x27, starting transfers between devices, permute(): return lax.ppermute(part, 'tile', pairs)  28.4 us
    pallas_call x8, Pallas kernels, call(): pl.pallas_call(kernel, name=name, in_specs=specs, out_specs=[pl.BlockSpec...  15.7 us
    ppermute x27, waiting for transfers between devices, permute(): return lax.ppermute(part, 'tile', pairs)  5.87 us
  transfers between devices with their start and end apart: 27, of which 8 were waited for; matrix products, arithmetic and copies ran while one was open for 0% of the time, Pallas kernels for 7%

profile of v9, /device:TPU:0, one launch (start us, length us, event | category | flops | bytes accessed | tf_op | source)
XLA Modules:
  0.0 51.0 jit_solution(293834159114695017)
XLA Ops:
  0.6 1.4 %pack_rows.1 = (bf16[256,256]{1,0:T(8,128)(2,1)S(1)}, bf16[32,1024]{1,0:T(8,128)(2,1)S(1)}, bf16[32,1024]{1,0:T(8,128)(2,1)S(1)}, bf16[16,1024]{1,0:T(8,128)(2,1...) custom-call(s32[9,16]{1,0:T(8,128)} %refs_0_.3, ...), custom_call_target="tpu_custom_call" | custom-call | flops 75497472 | bytes 950884 | tf_op jit(solution)/shard_map/pack_rows/pallas_call | solution.py:180
  2.3 5.1 %collective-permute-start = (bf16[32,1024]{1,0:T(8,128)(2,1)S(1)}, bf16[32,1024]{1,0:T(8,128)(2,1)S(1)}, u32[]{:S(2)}, u32[]{:S(2)}) collective-permute-start(bf16[32,1024]{1,0:T(8,128)(2,1)S(1)} %get-tuple-element.75), channel_id=1, source_target_pairs={{0,12},{1,13},{2,14},{3,15},{4,8},{5,9},{6,10},{7,11},{8,4},{9,5},... | collective-permute-start | bytes 196616 | tf_op jit(solution)/shard_map/ppermute | solution.py:239
  7.4 0.7 %collective-permute-start.2 = (bf16[16,1024]{1,0:T(8,128)(2,1)S(1)}, bf16[16,1024]{1,0:T(8,128)(2,1)S(1)}, u32[]{:S(2)}, u32[]{:S(2)}) collective-permute-start(bf16[16,1024]{1,0:T(8,128)(2,1)S(1)} %get-tuple-element.79), channel_id=1, source_target_pairs={{0,15},{1,2},{2,1},{3,4},{4,3},{5,6},{6,5},{7,8},{8,7},{9,10},{10,... | collective-permute-start | bytes 98312 | tf_op jit(solution)/shard_map/ppermute | solution.py:239
  8.2 2.5 %collective-permute-start.3 = (bf16[16,1024]{1,0:T(8,128)(2,1)S(1)}, bf16[16,1024]{1,0:T(8,128)(2,1)S(1)}, u32[]{:S(2)}, u32[]{:S(2)}) collective-permute-start(bf16[16,1024]{1,0:T(8,128)(2,1)S(1)} %get-tuple-element.80), channel_id=1, source_target_pairs={{0,3},{1,14},{2,5},{3,0},{4,7},{5,2},{6,9},{7,4},{8,11},{9,6},{10,... | collective-permute-start | bytes 98312 | tf_op jit(solution)/shard_map/ppermute | solution.py:239
  10.7 1.3 %collective-permute-start.4 = (bf16[16,1024]{1,0:T(8,128)(2,1)S(1)}, bf16[16,1024]{1,0:T(8,128)(2,1)S(1)}, u32[]{:S(2)}, u32[]{:S(2)}) collective-permute-start(bf16[16,1024]{1,0:T(8,128)(2,1)S(1)} %get-tuple-element.81), channel_id=1, source_target_pairs={{0,11},{1,6},{2,13},{3,8},{4,15},{5,10},{6,1},{7,12},{8,3},{9,14},... | collective-permute-start | bytes 98312 | tf_op jit(solution)/shard_map/ppermute | solution.py:239
  12.0 1.1 %collective-permute-start.5 = (bf16[16,1024]{1,0:T(8,128)(2,1)S(1)}, bf16[16,1024]{1,0:T(8,128)(2,1)S(1)}, u32[]{:S(2)}, u32[]{:S(2)}) collective-permute-start(bf16[16,1024]{1,0:T(8,128)(2,1)S(1)} %get-tuple-element.82), channel_id=1, source_target_pairs={{0,8},{1,9},{2,10},{3,11},{4,12},{5,13},{6,14},{7,15},{8,0},{9,1},... | collective-permute-start | bytes 98312 | tf_op jit(solution)/shard_map/ppermute | solution.py:239
  13.8 1.3 %collective-permute-start.6 = (bf16[16,1024]{1,0:T(8,128)(2,1)S(1)}, bf16[16,1024]{1,0:T(8,128)(2,1)S(1)}, u32[]{:S(2)}, u32[]{:S(2)}) collective-permute-start(bf16[16,1024]{1,0:T(8,128)(2,1)S(1)} %get-tuple-element.83), channel_id=1, source_target_pairs={{0,1},{1,0},{2,3},{3,2},{4,5},{5,4},{6,7},{7,6},{8,9},{9,8},{10,11... | collective-permute-start | bytes 98312 | tf_op jit(solution)/shard_map/ppermute | solution.py:239
  15.2 1.7 %local_products.1 = (f32[384,512]{1,0:T(8,128)S(1)}, f32[768,512]{1,0:T(8,128)S(1)}, f32[64,512]{1,0:T(8,128)S(1)}, bf16[384,512]{1,0:T(8,128)(2,1)S(1)}, bf16[5...) custom-call(bf16[256,512]{1,0:T(8,128)(2,1)S(1)} %copy-done.4, ...), custom_call_target="tpu_custom_call" | custom-call | flops 1275068416 | bytes 10560512 | tf_op jit(solution)/shard_map/local_products/pallas_call | solution.py:180
  16.9 0.8 %collective-permute-done.5.refs_5_ = bf16[16,1024]{1,0:T(8,128)(2,1)S(1)} collective-permute-done((bf16[16,1024]{1,0:T(8,128)(2,1)S(1)}, bf16[16,1024]{1,0:T(8,128)(2,1)S(1)}, u32[]{:S(2)}, u32[]{:S(2)}) %collective-permute-start.5) | collective-permute-done | bytes 32800 | tf_op jit(solution)/shard_map/ppermute | solution.py:239
  17.8 3.6 %edges_forward.1 = (bf16[32,1024]{1,0:T(8,128)(2,1)S(1)}, bf16[32,1024]{1,0:T(8,128)(2,1)S(1)}, bf16[16,1024]{1,0:T(8,128)(2,1)S(1)}, bf16[16,1024]{1,0:T(8,128)...) custom-call(bf16[32,1024]{1,0:T(8,128)(2,1)S(1)} %collective-permute, ...), custom_call_target="tpu_custom_call" | custom-call | flops 1207959552 | bytes 16552704 | tf_op jit(solution)/shard_map/edges_forward/pallas_call | solution.py:180
  21.4 1.7 %collective-permute-start.9 = (bf16[32,1024]{1,0:T(8,128)(2,1)S(1)}, bf16[32,1024]{1,0:T(8,128)(2,1)S(1)}, u32[]{:S(2)}, u32[]{:S(2)}) collective-permute-start(bf16[32,1024]{1,0:T(8,128)(2,1)S(1)} %get-tuple-element.91), channel_id=1, source_target_pairs={{0,12},{1,13},{2,14},{3,15},{4,8},{5,9},{6,10},{7,11},{8,4},{9,5},... | collective-permute-start | bytes 196616 | tf_op jit(solution)/shard_map/ppermute | solution.py:239
  23.9 2.5 %collective-permute-start.12 = (bf16[16,1024]{1,0:T(8,128)(2,1)S(1)}, bf16[16,1024]{1,0:T(8,128)(2,1)S(1)}, u32[]{:S(2)}, u32[]{:S(2)}) collective-permute-start(bf16[16,1024]{1,0:T(8,128)(2,1)S(1)} %get-tuple-element.96), channel_id=1, source_target_pairs={{0,3},{1,14},{2,5},{3,0},{4,7},{5,2},{6,9},{7,4},{8,11},{9,6},{10,... | collective-permute-start | bytes 98312 | tf_op jit(solution)/shard_map/ppermute | solution.py:239
  26.4 0.7 %collective-permute-start.13 = (bf16[16,1024]{1,0:T(8,128)(2,1)S(1)}, bf16[16,1024]{1,0:T(8,128)(2,1)S(1)}, u32[]{:S(2)}, u32[]{:S(2)}) collective-permute-start(bf16[16,1024]{1,0:T(8,128)(2,1)S(1)} %get-tuple-element.97), channel_id=1, source_target_pairs={{0,11},{1,6},{2,13},{3,8},{4,15},{5,10},{6,1},{7,12},{8,3},{9,14},... | collective-permute-start | bytes 98312 | tf_op jit(solution)/shard_map/ppermute | solution.py:239
  27.8 0.9 %collective-permute-start.14 = (bf16[16,1024]{1,0:T(8,128)(2,1)S(1)}, bf16[16,1024]{1,0:T(8,128)(2,1)S(1)}, u32[]{:S(2)}, u32[]{:S(2)}) collective-permute-start(bf16[16,1024]{1,0:T(8,128)(2,1)S(1)} %get-tuple-element.98), channel_id=1, source_target_pairs={{0,8},{1,9},{2,10},{3,11},{4,12},{5,13},{6,14},{7,15},{8,0},{9,1},... | collective-permute-start | bytes 98312 | tf_op jit(solution)/shard_map/ppermute | solution.py:239
  29.2 1.1 %collective-permute-start.15 = (bf16[16,1024]{1,0:T(8,128)(2,1)S(1)}, bf16[16,1024]{1,0:T(8,128)(2,1)S(1)}, u32[]{:S(2)}, u32[]{:S(2)}) collective-permute-start(bf16[16,1024]{1,0:T(8,128)(2,1)S(1)} %get-tuple-element.99), channel_id=1, source_target_pairs={{0,1},{1,0},{2,3},{3,2},{4,5},{5,4},{6,7},{7,6},{8,9},{9,8},{10,11... | collective-permute-start | bytes 98312 | tf_op jit(solution)/shard_map/ppermute | solution.py:239
  30.7 0.8 %collective-permute-done.13.refs_13_ = bf16[16,1024]{1,0:T(8,128)(2,1)S(1)} collective-permute-done((bf16[16,1024]{1,0:T(8,128)(2,1)S(1)}, bf16[16,1024]{1,0:T(8,128)(2,1)S(1)}, u32[]{:S(2)}, u32[]{:S(2)}) %collective-permute-start.13) | collective-permute-done | bytes 32800 | tf_op jit(solution)/shard_map/ppermute | solution.py:239
  31.5 1.7 %collective-permute-done.14.refs_14_ = bf16[16,1024]{1,0:T(8,128)(2,1)S(1)} collective-permute-done((bf16[16,1024]{1,0:T(8,128)(2,1)S(1)}, bf16[16,1024]{1,0:T(8,128)(2,1)S(1)}, u32[]{:S(2)}, u32[]{:S(2)}) %collective-permute-start.14) | collective-permute-done | bytes 32800 | tf_op jit(solution)/shard_map/ppermute | solution.py:239
  33.2 6.0 %edges_backward.1 = (bf16[32,512]{1,0:T(8,128)(2,1)S(1)}, bf16[32,512]{1,0:T(8,128)(2,1)S(1)}, bf16[16,512]{1,0:T(8,128)(2,1)S(1)}, bf16[16,512]{1,0:T(8,128)(2,...) custom-call(bf16[32,1024]{1,0:T(8,128)(2,1)S(1)} %collective-permute, ...), custom_call_target="tpu_custom_call" | custom-call | flops 2449473536 | bytes 18502400 | tf_op jit(solution)/shard_map/edges_backward/pallas_call | solution.py:180
  39.2 2.0 %collective-permute-start.18 = (bf16[32,512]{1,0:T(8,128)(2,1)S(1)}, bf16[32,512]{1,0:T(8,128)(2,1)S(1)}, u32[]{:S(2)}, u32[]{:S(2)}) collective-permute-start(bf16[32,512]{1,0:T(8,128)(2,1)S(1)} %get-tuple-element.113), channel_id=1, source_target_pairs={{0,12},{1,13},{2,14},{3,15},{4,8},{5,9},{6,10},{7,11},{8,4},{9,5},... | collective-permute-start | bytes 98312 | tf_op jit(solution)/shard_map/ppermute | solution.py:239
  41.5 2.9 %collective-permute-start.21 = (bf16[16,512]{1,0:T(8,128)(2,1)S(1)}, bf16[16,512]{1,0:T(8,128)(2,1)S(1)}, u32[]{:S(2)}, u32[]{:S(2)}) collective-permute-start(bf16[16,512]{1,0:T(8,128)(2,1)S(1)} %get-tuple-element.118), channel_id=1, source_target_pairs={{0,3},{1,14},{2,5},{3,0},{4,7},{5,2},{6,9},{7,4},{8,11},{9,6},{10,... | collective-permute-start | bytes 49160 | tf_op jit(solution)/shard_map/ppermute | solution.py:239
  45.1 1.7 %collective-permute-start.23 = (bf16[16,512]{1,0:T(8,128)(2,1)S(1)}, bf16[16,512]{1,0:T(8,128)(2,1)S(1)}, u32[]{:S(2)}, u32[]{:S(2)}) collective-permute-start(bf16[16,512]{1,0:T(8,128)(2,1)S(1)} %get-tuple-element.120), channel_id=1, source_target_pairs={{0,8},{1,9},{2,10},{3,11},{4,12},{5,13},{6,14},{7,15},{8,0},{9,1},... | collective-permute-start | bytes 49160 | tf_op jit(solution)/shard_map/ppermute | solution.py:239
  47.1 0.8 %collective-permute-start.24 = (bf16[16,512]{1,0:T(8,128)(2,1)S(1)}, bf16[16,512]{1,0:T(8,128)(2,1)S(1)}, u32[]{:S(2)}, u32[]{:S(2)}) collective-permute-start(bf16[16,512]{1,0:T(8,128)(2,1)S(1)} %get-tuple-element.121), channel_id=1, source_target_pairs={{0,1},{1,0},{2,3},{3,2},{4,5},{5,4},{6,7},{7,6},{8,9},{9,8},{10,11... | collective-permute-start | bytes 49160 | tf_op jit(solution)/shard_map/ppermute | solution.py:239
  47.9 1.5 %local_gradients.1 = (f32[256,512]{1,0:T(8,128)S(1)}, f32[64,512]{1,0:T(8,128)}) custom-call(bf16[256,512]{1,0:T(8,128)(2,1)S(1)} %copy-done.5, bf16[256,512]{1,0:T(8,128)(2,1)S(1)} %get-tuple-element.122.refs_1_, bf16[256,512]{1,0:T(8,128)(2,1)S(1)} %get-tuple-element.123.refs_2_, bf16[256,512]{1,0:T(8,128)(2,1)S(1)} %get-tuple-element.124.refs_3_, ...), custom_call_target="tpu_custom_call" | custom-call | flops 402653184 | bytes 8781824 | tf_op jit(solution)/shard_map/local_gradients/pallas_call | solution.py:180
  50.0 1.0 %add_returned.1 = f32[256,512]{1,0:T(8,128)} custom-call(bf16[32,512]{1,0:T(8,128)(2,1)S(1)} %collective-permute-done.18.refs_0_, bf16[32,512]{1,0:T(8,128)(2,1)S(1)} %collective-permute-done.19.refs_1_, bf16[16,512]{1,0:T(8,128)(2,1)S(1)} %collective-permute-done.20.refs_2_, bf16[16,512]{1,0:T(8,128)(2,1)S(1)} %collective-permute-done.21.refs_3_, ...), custom_call_target="tpu_custom_call" | custom-call | flops 37748736 | bytes 1392640 | tf_op jit(solution)/shard_map/add_returned/pallas_call | solution.py:180
  (74 shorter events, 5.2 us)
Async XLA Ops:
  2.3 9.6 %collective-permute-start = (bf16[32,1024]{1,0:T(8,128)(2,1)S(1)}, bf16[32,1024]{1,0:T(8,128)(2,1)S(1)}, u32[]{:S(2)}, u32[]{:S(2)}) collective-permute-start(bf16[32,1024]{1,0:T(8,128)(2,1)S(1)} %get-tuple-element.75), channel_id=1, source_target_pairs={{0,12},{1,13},{2,14},{3,15},{4,8},{5,9},{6,10},{7,11},{8,4},{9,5},... | collective-permute-start | bytes 196616 | tf_op jit(solution)/shard_map/ppermute | solution.py:239
  7.4 7.7 %collective-permute-start.1 = (bf16[32,1024]{1,0:T(8,128)(2,1)S(1)}, bf16[32,1024]{1,0:T(8,128)(2,1)S(1)}, u32[]{:S(2)}, u32[]{:S(2)}) collective-permute-start(bf16[32,1024]{1,0:T(8,128)(2,1)S(1)} %get-tuple-element.78), channel_id=1, source_target_pairs={{0,4},{1,5},{2,6},{3,7},{4,0},{5,1},{6,2},{7,3},{8,12},{9,13},{10,... | collective-permute-start | bytes 196616 | tf_op jit(solution)/shard_map/ppermute | solution.py:239
  7.4 6.0 %collective-permute-start.2 = (bf16[16,1024]{1,0:T(8,128)(2,1)S(1)}, bf16[16,1024]{1,0:T(8,128)(2,1)S(1)}, u32[]{:S(2)}, u32[]{:S(2)}) collective-permute-start(bf16[16,1024]{1,0:T(8,128)(2,1)S(1)} %get-tuple-element.79), channel_id=1, source_target_pairs={{0,15},{1,2},{2,1},{3,4},{4,3},{5,6},{6,5},{7,8},{8,7},{9,10},{10,... | collective-permute-start | bytes 98312 | tf_op jit(solution)/shard_map/ppermute | solution.py:239
  8.2 5.6 %collective-permute-start.3 = (bf16[16,1024]{1,0:T(8,128)(2,1)S(1)}, bf16[16,1024]{1,0:T(8,128)(2,1)S(1)}, u32[]{:S(2)}, u32[]{:S(2)}) collective-permute-start(bf16[16,1024]{1,0:T(8,128)(2,1)S(1)} %get-tuple-element.80), channel_id=1, source_target_pairs={{0,3},{1,14},{2,5},{3,0},{4,7},{5,2},{6,9},{7,4},{8,11},{9,6},{10,... | collective-permute-start | bytes 98312 | tf_op jit(solution)/shard_map/ppermute | solution.py:239
  10.7 6.3 %collective-permute-start.4 = (bf16[16,1024]{1,0:T(8,128)(2,1)S(1)}, bf16[16,1024]{1,0:T(8,128)(2,1)S(1)}, u32[]{:S(2)}, u32[]{:S(2)}) collective-permute-start(bf16[16,1024]{1,0:T(8,128)(2,1)S(1)} %get-tuple-element.81), channel_id=1, source_target_pairs={{0,11},{1,6},{2,13},{3,8},{4,15},{5,10},{6,1},{7,12},{8,3},{9,14},... | collective-permute-start | bytes 98312 | tf_op jit(solution)/shard_map/ppermute | solution.py:239
  12.0 5.8 %collective-permute-start.5 = (bf16[16,1024]{1,0:T(8,128)(2,1)S(1)}, bf16[16,1024]{1,0:T(8,128)(2,1)S(1)}, u32[]{:S(2)}, u32[]{:S(2)}) collective-permute-start(bf16[16,1024]{1,0:T(8,128)(2,1)S(1)} %get-tuple-element.82), channel_id=1, source_target_pairs={{0,8},{1,9},{2,10},{3,11},{4,12},{5,13},{6,14},{7,15},{8,0},{9,1},... | collective-permute-start | bytes 98312 | tf_op jit(solution)/shard_map/ppermute | solution.py:239
  13.5 4.3 %collective-permute-start.7 = (bf16[32,1024]{1,0:T(8,128)(2,1)S(1)}, bf16[32,1024]{1,0:T(8,128)(2,1)S(1)}, u32[]{:S(2)}, u32[]{:S(2)}) collective-permute-start(bf16[32,1024]{1,0:T(8,128)(2,1)S(1)} %collective-permute-done.refs_0_), channel_id=1, source_target_pairs={{0,1},{1,0},{2,3},{3,2},{4,5},{5,4},{6,7},{7,6},{8,9},{9,8},{10,11... | collective-permute-start | bytes 196616 | tf_op jit(solution)/shard_map/ppermute | solution.py:239
  13.8 3.9 %collective-permute-start.6 = (bf16[16,1024]{1,0:T(8,128)(2,1)S(1)}, bf16[16,1024]{1,0:T(8,128)(2,1)S(1)}, u32[]{:S(2)}, u32[]{:S(2)}) collective-permute-start(bf16[16,1024]{1,0:T(8,128)(2,1)S(1)} %get-tuple-element.83), channel_id=1, source_target_pairs={{0,1},{1,0},{2,3},{3,2},{4,5},{5,4},{6,7},{7,6},{8,9},{9,8},{10,11... | collective-permute-start | bytes 98312 | tf_op jit(solution)/shard_map/ppermute | solution.py:239
  21.4 6.4 %collective-permute-start.9 = (bf16[32,1024]{1,0:T(8,128)(2,1)S(1)}, bf16[32,1024]{1,0:T(8,128)(2,1)S(1)}, u32[]{:S(2)}, u32[]{:S(2)}) collective-permute-start(bf16[32,1024]{1,0:T(8,128)(2,1)S(1)} %get-tuple-element.91), channel_id=1, source_target_pairs={{0,12},{1,13},{2,14},{3,15},{4,8},{5,9},{6,10},{7,11},{8,4},{9,5},... | collective-permute-start | bytes 196616 | tf_op jit(solution)/shard_map/ppermute | solution.py:239
  23.1 7.2 %collective-permute-start.10 = (bf16[32,1024]{1,0:T(8,128)(2,1)S(1)}, bf16[32,1024]{1,0:T(8,128)(2,1)S(1)}, u32[]{:S(2)}, u32[]{:S(2)}) collective-permute-start(bf16[32,1024]{1,0:T(8,128)(2,1)S(1)} %get-tuple-element.94), channel_id=1, source_target_pairs={{0,4},{1,5},{2,6},{3,7},{4,0},{5,1},{6,2},{7,3},{8,12},{9,13},{10,... | collective-permute-start | bytes 196616 | tf_op jit(solution)/shard_map/ppermute | solution.py:239
  23.1 6.0 %collective-permute-start.11 = (bf16[16,1024]{1,0:T(8,128)(2,1)S(1)}, bf16[16,1024]{1,0:T(8,128)(2,1)S(1)}, u32[]{:S(2)}, u32[]{:S(2)}) collective-permute-start(bf16[16,1024]{1,0:T(8,128)(2,1)S(1)} %get-tuple-element.95), channel_id=1, source_target_pairs={{0,15},{1,2},{2,1},{3,4},{4,3},{5,6},{6,5},{7,8},{8,7},{9,10},{10,... | collective-permute-start | bytes 98312 | tf_op jit(solution)/shard_map/ppermute | solution.py:239
  23.9 5.3 %collective-permute-start.12 = (bf16[16,1024]{1,0:T(8,128)(2,1)S(1)}, bf16[16,1024]{1,0:T(8,128)(2,1)S(1)}, u32[]{:S(2)}, u32[]{:S(2)}) collective-permute-start(bf16[16,1024]{1,0:T(8,128)(2,1)S(1)} %get-tuple-element.96), channel_id=1, source_target_pairs={{0,3},{1,14},{2,5},{3,0},{4,7},{5,2},{6,9},{7,4},{8,11},{9,6},{10,... | collective-permute-start | bytes 98312 | tf_op jit(solution)/shard_map/ppermute | solution.py:239
  26.4 5.1 %collective-permute-start.13 = (bf16[16,1024]{1,0:T(8,128)(2,1)S(1)}, bf16[16,1024]{1,0:T(8,128)(2,1)S(1)}, u32[]{:S(2)}, u32[]{:S(2)}) collective-permute-start(bf16[16,1024]{1,0:T(8,128)(2,1)S(1)} %get-tuple-element.97), channel_id=1, source_target_pairs={{0,11},{1,6},{2,13},{3,8},{4,15},{5,10},{6,1},{7,12},{8,3},{9,14},... | collective-permute-start | bytes 98312 | tf_op jit(solution)/shard_map/ppermute | solution.py:239
  27.8 5.4 %collective-permute-start.14 = (bf16[16,1024]{1,0:T(8,128)(2,1)S(1)}, bf16[16,1024]{1,0:T(8,128)(2,1)S(1)}, u32[]{:S(2)}, u32[]{:S(2)}) collective-permute-start(bf16[16,1024]{1,0:T(8,128)(2,1)S(1)} %get-tuple-element.98), channel_id=1, source_target_pairs={{0,8},{1,9},{2,10},{3,11},{4,12},{5,13},{6,14},{7,15},{8,0},{9,1},... | collective-permute-start | bytes 98312 | tf_op jit(solution)/shard_map/ppermute | solution.py:239
  29.2 4.0 %collective-permute-start.16 = (bf16[32,1024]{1,0:T(8,128)(2,1)S(1)}, bf16[32,1024]{1,0:T(8,128)(2,1)S(1)}, u32[]{:S(2)}, u32[]{:S(2)}) collective-permute-start(bf16[32,1024]{1,0:T(8,128)(2,1)S(1)} %collective-permute-done.9.refs_9_), channel_id=1, source_target_pairs={{0,1},{1,0},{2,3},{3,2},{4,5},{5,4},{6,7},{7,6},{8,9},{9,8},{10,11... | collective-permute-start | bytes 196616 | tf_op jit(solution)/shard_map/ppermute | solution.py:239
  29.2 4.0 %collective-permute-start.15 = (bf16[16,1024]{1,0:T(8,128)(2,1)S(1)}, bf16[16,1024]{1,0:T(8,128)(2,1)S(1)}, u32[]{:S(2)}, u32[]{:S(2)}) collective-permute-start(bf16[16,1024]{1,0:T(8,128)(2,1)S(1)} %get-tuple-element.99), channel_id=1, source_target_pairs={{0,1},{1,0},{2,3},{3,2},{4,5},{5,4},{6,7},{7,6},{8,9},{9,8},{10,11... | collective-permute-start | bytes 98312 | tf_op jit(solution)/shard_map/ppermute | solution.py:239
  30.3 2.9 %collective-permute-start.17 = (bf16[32,1024]{1,0:T(8,128)(2,1)S(1)}, bf16[32,1024]{1,0:T(8,128)(2,1)S(1)}, u32[]{:S(2)}, u32[]{:S(2)}) collective-permute-start(bf16[32,1024]{1,0:T(8,128)(2,1)S(1)} %collective-permute-done.10.refs_10_), channel_id=1, source_target_pairs={{0,1},{1,0},{2,3},{3,2},{4,5},{5,4},{6,7},{7,6},{8,9},{9,8},{10,11... | collective-permute-start | bytes 196616 | tf_op jit(solution)/shard_map/ppermute | solution.py:239
  39.2 5.9 %collective-permute-start.18 = (bf16[32,512]{1,0:T(8,128)(2,1)S(1)}, bf16[32,512]{1,0:T(8,128)(2,1)S(1)}, u32[]{:S(2)}, u32[]{:S(2)}) collective-permute-start(bf16[32,512]{1,0:T(8,128)(2,1)S(1)} %get-tuple-element.113), channel_id=1, source_target_pairs={{0,12},{1,13},{2,14},{3,15},{4,8},{5,9},{6,10},{7,11},{8,4},{9,5},... | collective-permute-start | bytes 98312 | tf_op jit(solution)/shard_map/ppermute | solution.py:239
  41.2 6.6 %collective-permute-start.19 = (bf16[32,512]{1,0:T(8,128)(2,1)S(1)}, bf16[32,512]{1,0:T(8,128)(2,1)S(1)}, u32[]{:S(2)}, u32[]{:S(2)}) collective-permute-start(bf16[32,512]{1,0:T(8,128)(2,1)S(1)} %get-tuple-element.116), channel_id=1, source_target_pairs={{0,4},{1,5},{2,6},{3,7},{4,0},{5,1},{6,2},{7,3},{8,12},{9,13},{10,... | collective-permute-start | bytes 98312 | tf_op jit(solution)/shard_map/ppermute | solution.py:239
  41.2 5.9 %collective-permute-start.20 = (bf16[16,512]{1,0:T(8,128)(2,1)S(1)}, bf16[16,512]{1,0:T(8,128)(2,1)S(1)}, u32[]{:S(2)}, u32[]{:S(2)}) collective-permute-start(bf16[16,512]{1,0:T(8,128)(2,1)S(1)} %get-tuple-element.117), channel_id=1, source_target_pairs={{0,15},{1,2},{2,1},{3,4},{4,3},{5,6},{6,5},{7,8},{8,7},{9,10},{10,... | collective-permute-start | bytes 49160 | tf_op jit(solution)/shard_map/ppermute | solution.py:239
  41.5 5.6 %collective-permute-start.21 = (bf16[16,512]{1,0:T(8,128)(2,1)S(1)}, bf16[16,512]{1,0:T(8,128)(2,1)S(1)}, u32[]{:S(2)}, u32[]{:S(2)}) collective-permute-start(bf16[16,512]{1,0:T(8,128)(2,1)S(1)} %get-tuple-element.118), channel_id=1, source_target_pairs={{0,3},{1,14},{2,5},{3,0},{4,7},{5,2},{6,9},{7,4},{8,11},{9,6},{10,... | collective-permute-start | bytes 49160 | tf_op jit(solution)/shard_map/ppermute | solution.py:239
  44.4 5.0 %collective-permute-start.22 = (bf16[16,512]{1,0:T(8,128)(2,1)S(1)}, bf16[16,512]{1,0:T(8,128)(2,1)S(1)}, u32[]{:S(2)}, u32[]{:S(2)}) collective-permute-start(bf16[16,512]{1,0:T(8,128)(2,1)S(1)} %get-tuple-element.119), channel_id=1, source_target_pairs={{0,11},{1,6},{2,13},{3,8},{4,15},{5,10},{6,1},{7,12},{8,3},{9,14},... | collective-permute-start | bytes 49160 | tf_op jit(solution)/shard_map/ppermute | solution.py:239
  45.1 4.9 %collective-permute-start.23 = (bf16[16,512]{1,0:T(8,128)(2,1)S(1)}, bf16[16,512]{1,0:T(8,128)(2,1)S(1)}, u32[]{:S(2)}, u32[]{:S(2)}) collective-permute-start(bf16[16,512]{1,0:T(8,128)(2,1)S(1)} %get-tuple-element.120), channel_id=1, source_target_pairs={{0,8},{1,9},{2,10},{3,11},{4,12},{5,13},{6,14},{7,15},{8,0},{9,1},... | collective-permute-start | bytes 49160 | tf_op jit(solution)/shard_map/ppermute | solution.py:239
  47.1 2.9 %collective-permute-start.25 = (bf16[32,512]{1,0:T(8,128)(2,1)S(1)}, bf16[32,512]{1,0:T(8,128)(2,1)S(1)}, u32[]{:S(2)}, u32[]{:S(2)}) collective-permute-start(bf16[32,512]{1,0:T(8,128)(2,1)S(1)} %collective-permute-done.18.refs_0_), channel_id=1, source_target_pairs={{0,1},{1,0},{2,3},{3,2},{4,5},{5,4},{6,7},{7,6},{8,9},{9,8},{10,11... | collective-permute-start | bytes 98312 | tf_op jit(solution)/shard_map/ppermute | solution.py:239
  (21 other events, 223.9 us)

commit v10 on v9

--- a/solution.py
+++ b/solution.py
@@ -21,66 +21,74 @@
     return lax.dot_general(left, right, (((1,), (1,)), ((), ())), preferred_element_type=F32)
 
 
-def sigmoid(values):
-    return 0.5 * jnp.tanh(0.5 * values) + 0.5
-
-
-def norm_rows(values):
-    centre = values - jnp.mean(values, axis=-1, keepdims=True)
-    scale_inv = lax.rsqrt(jnp.mean(centre * centre, axis=-1, keepdims=True) + 1e-05)
-    return centre * scale_inv, scale_inv
+def centred(values, axis):
+    values = values.astype(F32)
+    return values - jnp.mean(values, axis=axis, keepdims=True)
+
+
+def silu_and_slope(pre):
+    half = 0.5 * pre
+    lifted = 1.0 + jnp.tanh(half)
+    return half * lifted, lifted * (0.5 + 0.5 * half * (2.0 - lifted))
+
+
+def silu(pre):
+    half = 0.5 * pre
+    return half * (1.0 + jnp.tanh(half))
+
+
+def scale_rows(raw):
+    return lax.rsqrt(jnp.mean(raw * raw, axis=-1, keepdims=True) + 1e-05)
 
 
 def norm_back(normed, scale_inv, upstream):
-    return scale_inv * (
-        upstream
-        - jnp.mean(upstream, axis=-1, keepdims=True)
-        - normed * jnp.mean(upstream * normed, axis=-1, keepdims=True)
-    )
+    return scale_inv * (upstream - normed * jnp.mean(upstream * normed, axis=-1, keepdims=True))
 
 
 def row_chunks(rows, size=CHUNK):
     return [slice(start, min(start + size, rows)) for start in range(0, rows, size)]
 
 
-def row_blocks(rows, parts):
-    size = -(-rows // (16 * parts)) * 16
-    return row_chunks(rows, size)
-
-
-def inner_chunks(block):
-    return [
-        (slice(part.start, part.stop), slice(block.start + part.start, block.start + part.stop))
-        for part in row_chunks(block.stop - block.start)
-    ]
-
-
-def activate(pre, act_ref, slope_ref, block):
-    for inner, rows in inner_chunks(block):
-        part = pre[inner, :]
-        gate = sigmoid(part)
-        act = part * gate
-        act_ref[rows, :] = act.astype(BF16)
-        slope_ref[rows, :] = (gate + act * (1.0 - gate)).astype(BF16)
-
-
-def norm_forward(raw, normed_ref, scale_ref, block):
-    for inner, rows in inner_chunks(block):
-        normed, scale_inv = norm_rows(raw[inner, :])
-        normed_ref[rows, :] = normed.astype(normed_ref.dtype)
-        scale_ref[rows, :] = scale_inv
-
-
-def norm_backward(normed_ref, scale_ref, upstream, out_ref, block):
-    for inner, rows in inner_chunks(block):
-        out_ref[rows, :] = norm_back(
-            normed_ref[rows, :].astype(F32), scale_ref[rows, :], upstream[inner, :].astype(F32)
-        ).astype(BF16)
-
-
-def times_slope(raw, slope_ref, out_ref, block):
-    for inner, rows in inner_chunks(block):
-        out_ref[rows, :] = (raw[inner, :] * slope_ref[rows, :].astype(F32)).astype(BF16)
+def write_silu(pre, act_ref):
+    for rows in row_chunks(pre.shape[0]):
+        act_ref[rows, :] = silu(pre[rows, :]).astype(BF16)
+
+
+def write_norm(raw, normed_ref, scale_ref):
+    for rows in row_chunks(raw.shape[0]):
+        part = raw[rows, :]
+        scale_inv = scale_rows(part)
+        normed_ref[rows, :] = (part * scale_inv).astype(normed_ref.dtype)
+        scale_ref[rows, :] = jnp.broadcast_to(
+            scale_inv, (part.shape[0], scale_ref.shape[1])
+        ).astype(scale_ref.dtype)
+
+
+def write_slope(pre_ref, slope_ref):
+    for rows in row_chunks(pre_ref.shape[0]):
+        slope_ref[rows, :] = silu_and_slope(pre_ref[rows, :])[1].astype(BF16)
+
+
+def edge_back(upstream, normed_ref, scale_ref, upstream_ref, product_ref, out_ref):
+    edges, features = normed_ref.shape
+    lanes = scale_ref.shape[1]
+    for rows in row_chunks(edges):
+        part = upstream[rows, :].astype(BF16)
+        upstream_ref[rows, :] = part
+        product_ref[rows, :] = part * normed_ref[rows, :]
+    ones = jnp.full((features, lanes), 1.0 / features, BF16)
+    means = mm(product_ref[...], ones).astype(BF16)
+    for rows in row_chunks(edges):
+        mean, scale_inv = means[rows, :], scale_ref[rows, :]
+        for columns in row_chunks(features, lanes):
+            out_ref[rows, columns] = scale_inv * (
+                upstream_ref[rows, columns] - normed_ref[rows, columns] * mean
+            )
+
+
+def times_slope(raw, slope_ref, out_ref):
+    for rows in row_chunks(out_ref.shape[0]):
+        out_ref[rows, :] = raw[rows, :].astype(BF16) * slope_ref[rows, :]
 
 
 def neighbour_offsets(peer_count):
@@ -382,6 +390,9 @@
         enc_mesh_ref,
         dec_grid_ref,
         dec_mesh_ref,
+        enc_second_ref,
+        mesh_second_ref,
+        dec_second_ref,
         enc_part_ref,
         dec_part_ref,
         mesh_part_ref,
@@ -389,10 +400,16 @@
         enc_pool_ref,
         dec_pick_ref,
         dec_pool_ref,
+        enc_centred_ref,
+        mesh_centred_ref,
+        dec_centred_ref,
         table_ref,
     ):
         onehot_pair(enc_grid_ref, enc_mesh_ref, spots, mesh_count, enc_pick_ref, enc_pool_ref)
         onehot_pair(dec_grid_ref, dec_mesh_ref, spots, mesh_count, dec_pick_ref, dec_pool_ref)
+        enc_centred_ref[...] = centred(enc_second_ref[...], 1).astype(BF16)
+        mesh_centred_ref[...] = centred(mesh_second_ref[...], 1).astype(BF16)
+        dec_centred_ref[...] = centred(dec_second_ref[...], 1).astype(BF16)
         nodes = nodes_ref[...]
         mesh_part_ref[...] = mm(mesh_ref[...], mesh_first_ref[low, :])
         table_ref[:grid_count, :] = mm(nodes, enc_first_ref[low, :]).astype(BF16)
@@ -404,7 +421,18 @@
         dec_part_ref[...] = mm(dec_edges_ref[...], dec_first_ref[2 * feat :, :])
         dec_part_ref[...] += mm(dec_pick_ref[:, :grid_count], pd)
 
-    enc_part, dec_part, mesh_part, enc_pick, enc_pool, dec_pick, dec_pool = call(
+    (
+        enc_part,
+        dec_part,
+        mesh_part,
+        enc_pick,
+        enc_pool,
+        dec_pick,
+        dec_pool,
+        enc_centred,
+        mesh_centred,
+        dec_centred,
+    ) = call(
         local,
         "local_products",
         [
@@ -419,6 +447,9 @@
             enc_mesh,
             dec_grid,
             dec_mesh,
+            enc_second,
+            mesh_second,
+            dec_second,
         ],
         [
             ((enc_count, feat), F32),
@@ -428,7 +459,8 @@
             ((total, enc_count), BF16),
             ((dec_count, total), BF16),
             ((total, dec_count), BF16),
-        ],
+        ]
+        + [((feat, feat), BF16)] * 3,
         scratch=[((total, feat), BF16)],
         flops=2 * feat * (feat * (2 * grid_count + enc_count + dec_count) + total * dec_count),
     )
@@ -456,17 +488,16 @@
         refs = refs[16:]
         out_refs, refs = refs[:sent_count], refs[sent_count:]
         (
-            mesh_out_ref,
             spot_ref,
             enc_normed_ref,
             enc_scale_ref,
-            enc_slope_ref,
+            enc_pre_ref,
             dec_normed_ref,
             dec_scale_ref,
-            dec_slope_ref,
+            dec_pre_ref,
             mesh_normed_ref,
             mesh_scale_ref,
-            mesh_slope_ref,
+            mesh_pre_ref,
             enc_act_ref,
             dec_act_ref,
             mesh_act_ref,
@@ -474,29 +505,22 @@
         ) = refs
         rows = by_slot(arrived_refs, low)
         pe = mm(rows, enc_wg_ref[low, :]).astype(BF16)
-        for block in row_blocks(enc_count, 1):
-            pre = enc_part_ref[block, :] + mm(enc_pick_ref[block, grid_count:spots], pe)
-            activate(pre, enc_act_ref, enc_slope_ref, block)
-            raw = mm(enc_act_ref[block, :], enc_w2_ref[...])
-            norm_forward(raw, enc_normed_ref, enc_scale_ref, block)
+        enc_pre_ref[...] = enc_part_ref[...] + mm(enc_pick_ref[:, grid_count:spots], pe)
+        write_silu(enc_pre_ref, enc_act_ref)
+        write_norm(mm(enc_act_ref[...], enc_w2_ref[...]), enc_normed_ref, enc_scale_ref)
         agg = mm(enc_pool_ref[mesh_rows, :], enc_normed_ref[...]).astype(BF16)
-        whole = slice(0, mesh_count)
-        pre = mesh_part_ref[...] + mm(agg, mesh_wa_ref[high, :])
-        activate(pre, mesh_act_ref, mesh_slope_ref, whole)
-        raw = mm(mesh_act_ref[...], mesh_w2_ref[...])
-        norm_forward(raw, mesh_normed_ref, mesh_scale_ref, whole)
+        mesh_pre_ref[...] = mesh_part_ref[...] + mm(agg, mesh_wa_ref[high, :])
+        write_silu(mesh_pre_ref, mesh_act_ref)
+        write_norm(mm(mesh_act_ref[...], mesh_w2_ref[...]), mesh_normed_ref, mesh_scale_ref)
         mesh_out = (mesh_ref[...].astype(F32) + mesh_normed_ref[...]).astype(BF16)
-        mesh_out_ref[...] = mesh_out
         table_ref[:slots, :] = mm(rows, dec_wg_ref[low, :]).astype(BF16)
         table_ref[slots : slots + mesh_count, :] = mm(mesh_out, dec_wm_ref[high, :]).astype(BF16)
         table_ref[slots + mesh_count :, :] = jnp.zeros(
             (total - spots - mesh_count, feat), BF16
         )
-        for block in row_blocks(dec_count, 1):
-            pre = dec_part_ref[block, :] + mm(dec_pick_ref[block, grid_count:], table_ref[...])
-            activate(pre, dec_act_ref, dec_slope_ref, block)
-            raw = mm(dec_act_ref[block, :], dec_w2_ref[...])
-            norm_forward(raw, dec_normed_ref, dec_scale_ref, block)
+        dec_pre_ref[...] = dec_part_ref[...] + mm(dec_pick_ref[:, grid_count:], table_ref[...])
+        write_silu(dec_pre_ref, dec_act_ref)
+        write_norm(mm(dec_act_ref[...], dec_w2_ref[...]), dec_normed_ref, dec_scale_ref)
         spot_ref[...] = mm(dec_pool_ref[:spots, :], dec_normed_ref[...])
         shared = mm(select_ref[:slots, :], spot_ref[:grid_count, :].astype(BF16)).astype(BF16)
         slot_msg = spot_ref[grid_count:, :].astype(BF16)
@@ -505,16 +529,17 @@
         )
         send(out_refs, lambda j: shared[j * width : (j + 1) * width, :], high)
 
-    edge_saved = [
+    lanes = 128
+    saved_shapes = [
         ((enc_count, feat), BF16),
-        ((enc_count, 1), F32),
-        ((enc_count, feat), BF16),
+        ((enc_count, lanes), BF16),
+        ((enc_count, feat), F32),
         ((dec_count, feat), BF16),
-        ((dec_count, 1), F32),
-        ((dec_count, feat), BF16),
+        ((dec_count, lanes), BF16),
+        ((dec_count, feat), F32),
         ((mesh_count, feat), F32),
         ((mesh_count, 1), F32),
-        ((mesh_count, feat), BF16),
+        ((mesh_count, feat), F32),
     ]
     results = call(
         forward,
@@ -532,15 +557,15 @@
             mesh_nodes,
             enc_first,
             dec_first,
-            enc_second,
+            enc_centred,
             mesh_first,
-            mesh_second,
+            mesh_centred,
             dec_first,
-            dec_second,
+            dec_centred,
         ],
         sent_shapes(2 * feat)
-        + [((mesh_count, feat), BF16), ((spots, feat), F32)]
-        + edge_saved,
+        + [((spots, feat), F32)]
+        + saved_shapes,
         scratch=[
             ((enc_count, feat), BF16),
             ((dec_count, feat), BF16),
@@ -550,42 +575,102 @@
         flops=2 * feat * feat * 2 * (enc_count + dec_count),
     )
     outgoing, results = results[:sent_count], results[sent_count:]
-    mesh_out, spot_msg, *saved = results
+    spot_msg, *saved = results
+    enc_normed, enc_scale, enc_pre, dec_normed, dec_scale, dec_pre = saved[:6]
+    mesh_normed, mesh_scale, mesh_pre = saved[6:]
     returned = exchange(outgoing)
 
-    def node_part(*refs):
-        arrived_refs = refs[:arrived_count]
-        nodes_ref, weight_ref, out_ref = refs[arrived_count:]
-        out_ref[:grid_count, :] = mm(nodes_ref[...], weight_ref[low, :])
-        out_ref[grid_count:, :] = mm(by_slot(arrived_refs, low), weight_ref[low, :])
-
-    (grid_part,) = call(
-        node_part,
-        "node_products",
-        [*arrived, grid_nodes, grid_first],
-        [((spots, feat), F32)],
+    def between(*refs):
+        arrived_refs, refs = refs[:arrived_count], refs[arrived_count:]
+        (
+            nodes_ref,
+            grid_first_ref,
+            grid_second_ref,
+            cot_ref,
+            mesh_first_ref,
+            mesh_ref,
+            mesh_normed_ref,
+            enc_pre_ref,
+            dec_pre_ref,
+            mesh_pre_ref,
+            part_ref,
+            cot_rows_ref,
+            grid_w2_ref,
+            grid_wa_ref,
+            mesh_wa_ref,
+            mesh_out_ref,
+            enc_slope_ref,
+            dec_slope_ref,
+            mesh_slope_ref,
+        ) = refs
+        part_ref[:grid_count, :] = mm(nodes_ref[...], grid_first_ref[low, :])
+        part_ref[grid_count:, :] = mm(by_slot(arrived_refs, low), grid_first_ref[low, :])
+        mesh_out_ref[...] = (mesh_ref[...].astype(F32) + mesh_normed_ref[...]).astype(BF16)
+        cot_rows_ref[:grid_count, :] = centred(cot_ref[...], 1)
+        cot_rows_ref[grid_count:, :] = centred(by_slot(arrived_refs, high), 1)
+        grid_w2_ref[...] = centred(grid_second_ref[...], 1).astype(BF16)
+        grid_wa_ref[...] = centred(grid_first_ref[high, :], 0).astype(BF16)
+        mesh_wa_ref[...] = centred(mesh_first_ref[high, :], 0).astype(BF16)
+        write_slope(enc_pre_ref, enc_slope_ref)
+        write_slope(dec_pre_ref, dec_slope_ref)
+        write_slope(mesh_pre_ref, mesh_slope_ref)
+
+    (
+        grid_part,
+        cot_rows,
+        grid_w2_centred,
+        grid_wa_centred,
+        mesh_wa_centred,
+        mesh_out,
+        enc_slope,
+        dec_slope,
+        mesh_slope,
+    ) = call(
+        between,
+        "slopes_and_nodes",
+        [
+            *arrived,
+            grid_nodes,
+            grid_first,
+            grid_second,
+            grid_cot,
+            mesh_first,
+            mesh_nodes,
+            mesh_normed,
+            enc_pre,
+            dec_pre,
+            mesh_pre,
+        ],
+        [((spots, feat), F32)] * 2
+        + [((feat, feat), BF16)] * 3
+        + [
+            ((mesh_count, feat), BF16),
+            ((enc_count, feat), BF16),
+            ((dec_count, feat), BF16),
+            ((mesh_count, feat), BF16),
+        ],
         flops=16 * spots * feat * feat,
     )
 
     def backward(*refs):
-        arrived_refs, refs = refs[:arrived_count], refs[arrived_count:]
         returned_refs, refs = refs[:arrived_count], refs[arrived_count:]
         (
             spot_ref,
             grid_part_ref,
             select_t_ref,
-            nodes_ref,
-            cot_ref,
+            cot_rows_ref,
             mesh_cot_ref,
             enc_pick_ref,
             enc_pool_ref,
             dec_pick_ref,
             dec_pool_ref,
             grid_wa_ref,
+            grid_wac_ref,
             grid_w2_ref,
+            grid_w2c_ref,
             dec_w2_ref,
             dec_wm_ref,
-            mesh_wa_ref,
+            mesh_wac_ref,
             mesh_w2_ref,
             enc_w2_ref,
             enc_wg_ref,
@@ -599,11 +684,11 @@
             mesh_normed_ref,
             mesh_scale_ref,
             mesh_slope_ref,
-        ) = refs[:28]
-        refs = refs[28:]
+        ) = refs[:29]
+        refs = refs[29:]
         out_refs, refs = refs[:sent_count], refs[sent_count:]
         (
-            grid_out_ref,
+            grid_normed_ref,
             grid_gpre_ref,
             gpe_ref,
             gpd_ref,
@@ -611,16 +696,16 @@
             mesh_gpre_ref,
             mesh_pool_ref,
             agg_ref,
-            cot_rows_ref,
             grid_act_ref,
             grid_slope_ref,
-            grid_normed_ref,
-            grid_scale_ref,
             grid_gout_ref,
-            grid_gall_ref,
             spot_grad_ref,
+            dec_up_ref,
+            dec_product_ref,
             dec_gout_ref,
             mesh_gout_ref,
+            enc_up_ref,
+            enc_product_ref,
             enc_gout_ref,
         ) = refs
         agg_ref[:grid_count, :] = (
@@ -629,103 +714,118 @@
         agg_ref[grid_count:, :] = (
             spot_ref[grid_count:, :] + by_slot(returned_refs, high).astype(F32)
         ).astype(BF16)
-        cot_rows_ref[:grid_count, :] = cot_ref[...]
-        cot_rows_ref[grid_count:, :] = by_slot(arrived_refs, high)
+        pre = grid_part_ref[...] + mm(agg_ref[...], grid_wa_ref[high, :])
+        for rows in row_chunks(spots):
+            act, slope = silu_and_slope(pre[rows, :])
+            grid_act_ref[rows, :] = act.astype(BF16)
+            grid_slope_ref[rows, :] = slope.astype(BF16)
+        raw = mm(grid_act_ref[...], grid_w2c_ref[...])
+        for rows in row_chunks(spots):
+            part = raw[rows, :]
+            scale_inv = scale_rows(part)
+            normed = part * scale_inv
+            grid_normed_ref[rows, :] = normed
+            grid_gout_ref[rows, :] = norm_back(normed, scale_inv, cot_rows_ref[rows, :]).astype(
+                BF16
+            )
+        times_slope(mm_t(grid_gout_ref[...], grid_w2_ref[...]), grid_slope_ref, grid_gpre_ref)
+        spot_grad_ref[:spots, :] = mm_t(grid_gpre_ref[...], grid_wac_ref[...]).astype(BF16)
         spot_grad_ref[spots:, :] = jnp.zeros((total - spots, feat), BF16)
-        for block in row_blocks(spots, 1):
-            pre = grid_part_ref[block, :] + mm(agg_ref[block, :], grid_wa_ref[high, :])
-            activate(pre, grid_act_ref, grid_slope_ref, block)
-            raw = mm(grid_act_ref[block, :], grid_w2_ref[...])
-            norm_forward(raw, grid_normed_ref, grid_scale_ref, block)
-            norm_backward(
-                grid_normed_ref, grid_scale_ref, cot_rows_ref[block, :], grid_gout_ref, block
-            )
-            raw = mm_t(grid_gout_ref[block, :], grid_w2_ref[...])
-            times_slope(raw, grid_slope_ref, grid_gall_ref, block)
-            spot_grad_ref[block, :] = mm_t(
-                grid_gall_ref[block, :], grid_wa_ref[high, :]
-            ).astype(BF16)
-        grid_out_ref[...] = (
-            nodes_ref[...].astype(F32) + grid_normed_ref[:grid_count, :]
-        ).astype(BF16)
-        grid_gpre_ref[...] = grid_gall_ref[:grid_count, :]
-        for block in row_blocks(dec_count, 1):
-            upstream = mm(dec_pick_ref[block, :], spot_grad_ref[...])
-            norm_backward(dec_normed_ref, dec_scale_ref, upstream, dec_gout_ref, block)
-            raw = mm_t(dec_gout_ref[block, :], dec_w2_ref[...])
-            times_slope(raw, dec_slope_ref, dec_gout_ref, block)
+        edge_back(
+            mm(dec_pick_ref[...], spot_grad_ref[...]),
+            dec_normed_ref,
+            dec_scale_ref,
+            dec_up_ref,
+            dec_product_ref,
+            dec_gout_ref,
+        )
+        times_slope(mm_t(dec_gout_ref[...], dec_w2_ref[...]), dec_slope_ref, dec_gout_ref)
         pooled = mm(dec_pool_ref[...], dec_gout_ref[...]).astype(BF16)
         gpd_ref[...] = pooled[:grid_count, :]
         slot_back = mm_t(pooled[grid_count:spots, :], dec_wg_ref[low, :])
         mesh_gin = mesh_cot_ref[...].astype(F32) + mm_t(pooled[mesh_rows, :], dec_wm_ref[high, :])
         mesh_gin_ref[...] = mesh_gin
-        whole = slice(0, mesh_count)
-        norm_backward(mesh_normed_ref, mesh_scale_ref, mesh_gin, mesh_gout_ref, whole)
-        raw = mm_t(mesh_gout_ref[...], mesh_w2_ref[...])
-        times_slope(raw, mesh_slope_ref, mesh_gpre_ref, whole)
-        gagg = mm_t(mesh_gpre_ref[...], mesh_wa_ref[high, :]).astype(BF16)
-        for block in row_blocks(enc_count, 1):
-            upstream = mm(enc_pick_ref[block, mesh_rows], gagg)
-            norm_backward(enc_normed_ref, enc_scale_ref, upstream, enc_gout_ref, block)
-            raw = mm_t(enc_gout_ref[block, :], enc_w2_ref[...])
-            times_slope(raw, enc_slope_ref, enc_gout_ref, block)
+        mesh_gout_ref[...] = norm_back(
+            mesh_normed_ref[...], mesh_scale_ref[...], centred(mesh_gin, 1)
+        ).astype(BF16)
+        times_slope(mm_t(mesh_gout_ref[...], mesh_w2_ref[...]), mesh_slope_ref, mesh_gpre_ref)
+        gagg = mm_t(mesh_gpre_ref[...], mesh_wac_ref[...]).astype(BF16)
+        edge_back(
+            mm(enc_pick_ref[:, mesh_rows], gagg),
+            enc_normed_ref,
+            enc_scale_ref,
+            enc_up_ref,
+            enc_product_ref,
+            enc_gout_ref,
+        )
+        times_slope(mm_t(enc_gout_ref[...], enc_w2_ref[...]), enc_slope_ref, enc_gout_ref)
         pooled = mm(enc_pool_ref[...], enc_gout_ref[...]).astype(BF16)
         gpe_ref[...] = pooled[:grid_count, :]
         mesh_pool_ref[...] = pooled[mesh_rows, :]
-        slot_back = (slot_back + mm_t(pooled[grid_count:spots, :], enc_wg_ref[low, :])).astype(BF16)
+        slot_back = (
+            slot_back + mm_t(pooled[grid_count:spots, :], enc_wg_ref[low, :])
+        ).astype(BF16)
         send(out_refs, lambda j: slot_back[reverse[j] * width : (reverse[j] + 1) * width, :])
 
     results = call(
         backward,
         "edges_backward",
         [
-            *arrived,
             *returned,
             spot_msg,
             grid_part,
             select_t,
-            grid_nodes,
-            grid_cot,
+            cot_rows,
             mesh_cot,
             enc_pick,
             enc_pool,
             dec_pick,
             dec_pool,
             grid_first,
+            grid_wa_centred,
             grid_second,
+            grid_w2_centred,
             dec_second,
             dec_first,
-            mesh_first,
+            mesh_wa_centred,
             mesh_second,
             enc_second,
             enc_first,
             dec_first,
-            *saved,
+            enc_normed,
+            enc_scale,
+            enc_slope,
+            dec_normed,
+            dec_scale,
+            dec_slope,
+            mesh_normed,
+            mesh_scale,
+            mesh_slope,
         ],
         sent_shapes(feat)
-        + [((grid_count, feat), BF16)] * 4
-        + [((mesh_count, feat), F32), ((mesh_count, feat), BF16), ((mesh_count, feat), BF16)],
-        scratch=[
+        + [
+            ((spots, feat), F32),
             ((spots, feat), BF16),
-            ((spots, feat), BF16),
-            ((spots, feat), BF16),
-            ((spots, feat), BF16),
-            ((spots, feat), F32),
-            ((spots, 1), F32),
-            ((spots, feat), BF16),
-            ((spots, feat), BF16),
-            ((total, feat), BF16),
-            ((dec_count, feat), BF16),
+            ((grid_count, feat), BF16),
+            ((grid_count, feat), BF16),
+            ((mesh_count, feat), F32),
             ((mesh_count, feat), BF16),
-            ((enc_count, feat), BF16),
+            ((mesh_count, feat), BF16),
         ],
+        scratch=[((spots, feat), BF16)] * 4
+        + [((total, feat), BF16)]
+        + [((dec_count, feat), BF16)] * 3
+        + [((mesh_count, feat), BF16)]
+        + [((enc_count, feat), BF16)] * 3,
         flops=2 * feat * feat * (4 * spots + 3 * dec_count + 2 * enc_count),
     )
     outgoing, results = results[:sent_count], results[sent_count:]
-    grid_out, grid_gpre, gpe, gpd, mesh_gin, mesh_gpre, mesh_pool = results
+    grid_normed, grid_gpre, gpe, gpd, mesh_gin, mesh_gpre, mesh_pool = results
     final = exchange(outgoing)
 
     def tail(
+        nodes_ref,
+        grid_normed_ref,
         cot_ref,
         grid_gpre_ref,
         gpe_ref,
@@ -740,10 +840,14 @@
         enc_wm_ref,
         base_ref,
         grad_mesh_ref,
+        grid_out_ref,
     ):
+        grid_out_ref[...] = (
+            nodes_ref[...].astype(F32) + grid_normed_ref[:grid_count, :]
+        ).astype(BF16)
         base_ref[...] = (
             cot_ref[...].astype(F32)
-            + mm_t(grid_gpre_ref[...], grid_wn_ref[low, :])
+            + mm_t(grid_gpre_ref[:grid_count, :], grid_wn_ref[low, :])
             + mm_t(gpe_ref[...], enc_wg_ref[low, :])
             + mm_t(gpd_ref[...], dec_wg_ref[low, :])
         )
@@ -753,10 +857,12 @@
             + mm_t(mesh_pool_ref[...], enc_wm_ref[high, :])
         )
 
-    base, grad_mesh = call(
+    base, grad_mesh, grid_out = call(
         tail,
         "local_gradients",
         [
+            grid_nodes,
+            grid_normed,
             grid_cot,
             grid_gpre,
             gpe,
@@ -770,7 +876,7 @@
             mesh_first,
             enc_first,
         ],
-        [((grid_count, feat), F32), ((mesh_count, feat), F32)],
+        [((grid_count, feat), F32), ((mesh_count, feat), F32), ((grid_count, feat), BF16)],
         flops=2 * feat * feat * 3 * grid_count,
     )
 

time: 51.2 us -> 51.2 us (level)
  waiting for transfers between devices: 5.87 us -> 4.55 us
  Pallas kernels: 15.7 us -> 16.9 us
    ppermute x27, waiting for transfers between devices: 5.87 us -> 4.55 us  [permute(): return lax.ppermute(part, 'tile', pairs)]
    pallas_call x8, Pallas kernels: 15.7 us -> 16.9 us  [call(): pl.pallas_call(kernel, name=name, in_specs=specs, out_specs=[pl.BlockSpec...]
  transfers between devices with their start and end apart: 27 -> 27, of which waited for: 8 -> 7; matrix products, arithmetic and copies ran while one was open for 0% -> 0% of each run, Pallas kernels for 7% -> 10%
where the time goes in v10:
time: 51.2 us; the launch traced here: 51 us
  starting transfers between devices  28.4 us (55%)
  Pallas kernels  16.9 us (33%)
  waiting for transfers between devices  4.55 us (9%)
  between operations  0.99 us (2%)
    ppermute x27, starting transfers between devices, permute(): return lax.ppermute(part, 'tile', pairs)  28.4 us
    pallas_call x8, Pallas kernels, call(): pl.pallas_call(kernel, name=name, in_specs=specs, out_specs=[pl.BlockSpec...  16.9 us
    ppermute x27, waiting for transfers between devices, permute(): return lax.ppermute(part, 'tile', pairs)  4.55 us
  transfers between devices with their start and end apart: 27, of which 7 were waited for; matrix products, arithmetic and copies ran while one was open for 0% of the time, Pallas kernels for 10%

profile of v10, /device:TPU:0, one launch (start us, length us, event | category | flops | bytes accessed | tf_op | source)
XLA Modules:
  0.0 51.0 jit_solution(1733066617558144898)
XLA Ops:
  0.6 1.4 %pack_rows.1 = (bf16[256,256]{1,0:T(8,128)(2,1)S(1)}, bf16[32,1024]{1,0:T(8,128)(2,1)S(1)}, bf16[32,1024]{1,0:T(8,128)(2,1)S(1)}, bf16[16,1024]{1,0:T(8,128)(2,1...) custom-call(s32[9,16]{1,0:T(8,128)} %refs_0_.3, ...), custom_call_target="tpu_custom_call" | custom-call | flops 75497472 | bytes 950884 | tf_op jit(solution)/shard_map/pack_rows/pallas_call | solution.py:188
  2.3 5.1 %collective-permute-start = (bf16[32,1024]{1,0:T(8,128)(2,1)S(1)}, bf16[32,1024]{1,0:T(8,128)(2,1)S(1)}, u32[]{:S(2)}, u32[]{:S(2)}) collective-permute-start(bf16[32,1024]{1,0:T(8,128)(2,1)S(1)} %get-tuple-element.87), channel_id=1, source_target_pairs={{0,12},{1,13},{2,14},{3,15},{4,8},{5,9},{6,10},{7,11},{8,4},{9,5},... | collective-permute-start | bytes 196616 | tf_op jit(solution)/shard_map/ppermute | solution.py:247
  8.2 2.5 %collective-permute-start.3 = (bf16[16,1024]{1,0:T(8,128)(2,1)S(1)}, bf16[16,1024]{1,0:T(8,128)(2,1)S(1)}, u32[]{:S(2)}, u32[]{:S(2)}) collective-permute-start(bf16[16,1024]{1,0:T(8,128)(2,1)S(1)} %get-tuple-element.92), channel_id=1, source_target_pairs={{0,3},{1,14},{2,5},{3,0},{4,7},{5,2},{6,9},{7,4},{8,11},{9,6},{10,... | collective-permute-start | bytes 98312 | tf_op jit(solution)/shard_map/ppermute | solution.py:247
  10.7 1.3 %collective-permute-start.4 = (bf16[16,1024]{1,0:T(8,128)(2,1)S(1)}, bf16[16,1024]{1,0:T(8,128)(2,1)S(1)}, u32[]{:S(2)}, u32[]{:S(2)}) collective-permute-start(bf16[16,1024]{1,0:T(8,128)(2,1)S(1)} %get-tuple-element.93), channel_id=1, source_target_pairs={{0,11},{1,6},{2,13},{3,8},{4,15},{5,10},{6,1},{7,12},{8,3},{9,14},... | collective-permute-start | bytes 98312 | tf_op jit(solution)/shard_map/ppermute | solution.py:247
  12.0 1.1 %collective-permute-start.5 = (bf16[16,1024]{1,0:T(8,128)(2,1)S(1)}, bf16[16,1024]{1,0:T(8,128)(2,1)S(1)}, u32[]{:S(2)}, u32[]{:S(2)}) collective-permute-start(bf16[16,1024]{1,0:T(8,128)(2,1)S(1)} %get-tuple-element.94), channel_id=1, source_target_pairs={{0,8},{1,9},{2,10},{3,11},{4,12},{5,13},{6,14},{7,15},{8,0},{9,1},... | collective-permute-start | bytes 98312 | tf_op jit(solution)/shard_map/ppermute | solution.py:247
  13.8 1.3 %collective-permute-start.6 = (bf16[16,1024]{1,0:T(8,128)(2,1)S(1)}, bf16[16,1024]{1,0:T(8,128)(2,1)S(1)}, u32[]{:S(2)}, u32[]{:S(2)}) collective-permute-start(bf16[16,1024]{1,0:T(8,128)(2,1)S(1)} %get-tuple-element.95), channel_id=1, source_target_pairs={{0,1},{1,0},{2,3},{3,2},{4,5},{5,4},{6,7},{7,6},{8,9},{9,8},{10,11... | collective-permute-start | bytes 98312 | tf_op jit(solution)/shard_map/ppermute | solution.py:247
  15.3 1.9 %local_products.1 = (f32[384,512]{1,0:T(8,128)S(1)}, f32[768,512]{1,0:T(8,128)S(1)}, f32[64,512]{1,0:T(8,128)S(1)}, bf16[384,512]{1,0:T(8,128)(2,1)S(1)}, bf16[5...) custom-call(bf16[256,512]{1,0:T(8,128)(2,1)S(1)} %copy-done.4, ...), custom_call_target="tpu_custom_call" | custom-call | flops 1275068416 | bytes 13706240 | tf_op jit(solution)/shard_map/local_products/pallas_call | solution.py:188
  17.8 3.0 %edges_forward.1 = (bf16[32,1024]{1,0:T(8,128)(2,1)S(1)}, bf16[32,1024]{1,0:T(8,128)(2,1)S(1)}, bf16[16,1024]{1,0:T(8,128)(2,1)S(1)}, bf16[16,1024]{1,0:T(8,128)...) custom-call(bf16[32,1024]{1,0:T(8,128)(2,1)S(1)} %collective-permute, ...), custom_call_target="tpu_custom_call" | custom-call | flops 1207959552 | bytes 18022656 | tf_op jit(solution)/shard_map/edges_forward/pallas_call | solution.py:188
  20.8 1.7 %collective-permute-start.9 = (bf16[32,1024]{1,0:T(8,128)(2,1)S(1)}, bf16[32,1024]{1,0:T(8,128)(2,1)S(1)}, u32[]{:S(2)}, u32[]{:S(2)}) collective-permute-start(bf16[32,1024]{1,0:T(8,128)(2,1)S(1)} %get-tuple-element.106), channel_id=1, source_target_pairs={{0,12},{1,13},{2,14},{3,15},{4,8},{5,9},{6,10},{7,11},{8,4},{9,5},... | collective-permute-start | bytes 196616 | tf_op jit(solution)/shard_map/ppermute | solution.py:247
  22.5 1.0 %collective-permute-start.11 = (bf16[16,1024]{1,0:T(8,128)(2,1)S(1)}, bf16[16,1024]{1,0:T(8,128)(2,1)S(1)}, u32[]{:S(2)}, u32[]{:S(2)}) collective-permute-start(bf16[16,1024]{1,0:T(8,128)(2,1)S(1)} %get-tuple-element.110), channel_id=1, source_target_pairs={{0,15},{1,2},{2,1},{3,4},{4,3},{5,6},{6,5},{7,8},{8,7},{9,10},{10,... | collective-permute-start | bytes 98312 | tf_op jit(solution)/shard_map/ppermute | solution.py:247
  23.4 2.2 %collective-permute-start.12 = (bf16[16,1024]{1,0:T(8,128)(2,1)S(1)}, bf16[16,1024]{1,0:T(8,128)(2,1)S(1)}, u32[]{:S(2)}, u32[]{:S(2)}) collective-permute-start(bf16[16,1024]{1,0:T(8,128)(2,1)S(1)} %get-tuple-element.111), channel_id=1, source_target_pairs={{0,3},{1,14},{2,5},{3,0},{4,7},{5,2},{6,9},{7,4},{8,11},{9,6},{10,... | collective-permute-start | bytes 98312 | tf_op jit(solution)/shard_map/ppermute | solution.py:247
  26.4 1.0 %collective-permute-done.9.refs_0_ = bf16[32,1024]{1,0:T(8,128)(2,1)S(1)} collective-permute-done((bf16[32,1024]{1,0:T(8,128)(2,1)S(1)}, bf16[32,1024]{1,0:T(8,128)(2,1)S(1)}, u32[]{:S(2)}, u32[]{:S(2)}) %collective-permute-start.9) | collective-permute-done | bytes 65568 | tf_op jit(solution)/shard_map/ppermute | solution.py:247
  28.5 1.0 %collective-permute-start.15 = (bf16[16,1024]{1,0:T(8,128)(2,1)S(1)}, bf16[16,1024]{1,0:T(8,128)(2,1)S(1)}, u32[]{:S(2)}, u32[]{:S(2)}) collective-permute-start(bf16[16,1024]{1,0:T(8,128)(2,1)S(1)} %get-tuple-element.114), channel_id=1, source_target_pairs={{0,1},{1,0},{2,3},{3,2},{4,5},{5,4},{6,7},{7,6},{8,9},{9,8},{10,11... | collective-permute-start | bytes 98312 | tf_op jit(solution)/shard_map/ppermute | solution.py:247
  29.6 1.7 %slopes_and_nodes.1 = (f32[400,512]{1,0:T(8,128)S(1)}, f32[400,512]{1,0:T(8,128)S(1)}, bf16[512,512]{1,0:T(8,128)(2,1)S(1)}, bf16[512,512]{1,0:T(8,128)(2,1)S(1)...) custom-call(bf16[32,1024]{1,0:T(8,128)(2,1)S(1)} %collective-permute, ...), custom_call_target="tpu_custom_call" | custom-call | flops 1677721600 | bytes 10780672 | tf_op jit(solution)/shard_map/slopes_and_nodes/pallas_call | solution.py:188
  31.3 1.2 %collective-permute-done.14.refs_5_ = bf16[16,1024]{1,0:T(8,128)(2,1)S(1)} collective-permute-done((bf16[16,1024]{1,0:T(8,128)(2,1)S(1)}, bf16[16,1024]{1,0:T(8,128)(2,1)S(1)}, u32[]{:S(2)}, u32[]{:S(2)}) %collective-permute-start.14) | collective-permute-done | bytes 32800 | tf_op jit(solution)/shard_map/ppermute | solution.py:247
  32.5 6.2 %edges_backward.1 = (bf16[32,512]{1,0:T(8,128)(2,1)S(1)}, bf16[32,512]{1,0:T(8,128)(2,1)S(1)}, bf16[16,512]{1,0:T(8,128)(2,1)S(1)}, bf16[16,512]{1,0:T(8,128)(2,...) custom-call(bf16[32,1024]{1,0:T(8,128)(2,1)S(1)} %collective-permute, ...), custom_call_target="tpu_custom_call" | custom-call | flops 2449473536 | bytes 19890432 | tf_op jit(solution)/shard_map/edges_backward/pallas_call | solution.py:188
  38.8 2.0 %collective-permute-start.18 = (bf16[32,512]{1,0:T(8,128)(2,1)S(1)}, bf16[32,512]{1,0:T(8,128)(2,1)S(1)}, u32[]{:S(2)}, u32[]{:S(2)}) collective-permute-start(bf16[32,512]{1,0:T(8,128)(2,1)S(1)} %get-tuple-element.143), channel_id=1, source_target_pairs={{0,12},{1,13},{2,14},{3,15},{4,8},{5,9},{6,10},{7,11},{8,4},{9,5},... | collective-permute-start | bytes 98312 | tf_op jit(solution)/shard_map/ppermute | solution.py:247
  40.8 0.8 %collective-permute-start.20 = (bf16[16,512]{1,0:T(8,128)(2,1)S(1)}, bf16[16,512]{1,0:T(8,128)(2,1)S(1)}, u32[]{:S(2)}, u32[]{:S(2)}) collective-permute-start(bf16[16,512]{1,0:T(8,128)(2,1)S(1)} %get-tuple-element.147), channel_id=1, source_target_pairs={{0,15},{1,2},{2,1},{3,4},{4,3},{5,6},{6,5},{7,8},{8,7},{9,10},{10,... | collective-permute-start | bytes 49160 | tf_op jit(solution)/shard_map/ppermute | solution.py:247
  41.6 2.4 %collective-permute-start.21 = (bf16[16,512]{1,0:T(8,128)(2,1)S(1)}, bf16[16,512]{1,0:T(8,128)(2,1)S(1)}, u32[]{:S(2)}, u32[]{:S(2)}) collective-permute-start(bf16[16,512]{1,0:T(8,128)(2,1)S(1)} %get-tuple-element.148), channel_id=1, source_target_pairs={{0,3},{1,14},{2,5},{3,0},{4,7},{5,2},{6,9},{7,4},{8,11},{9,6},{10,... | collective-permute-start | bytes 49160 | tf_op jit(solution)/shard_map/ppermute | solution.py:247
  44.0 1.0 %collective-permute-start.22 = (bf16[16,512]{1,0:T(8,128)(2,1)S(1)}, bf16[16,512]{1,0:T(8,128)(2,1)S(1)}, u32[]{:S(2)}, u32[]{:S(2)}) collective-permute-start(bf16[16,512]{1,0:T(8,128)(2,1)S(1)} %get-tuple-element.149), channel_id=1, source_target_pairs={{0,11},{1,6},{2,13},{3,8},{4,15},{5,10},{6,1},{7,12},{8,3},{9,14},... | collective-permute-start | bytes 49160 | tf_op jit(solution)/shard_map/ppermute | solution.py:247
  45.0 1.4 %collective-permute-start.23 = (bf16[16,512]{1,0:T(8,128)(2,1)S(1)}, bf16[16,512]{1,0:T(8,128)(2,1)S(1)}, u32[]{:S(2)}, u32[]{:S(2)}) collective-permute-start(bf16[16,512]{1,0:T(8,128)(2,1)S(1)} %get-tuple-element.150), channel_id=1, source_target_pairs={{0,8},{1,9},{2,10},{3,11},{4,12},{5,13},{6,14},{7,15},{8,0},{9,1},... | collective-permute-start | bytes 49160 | tf_op jit(solution)/shard_map/ppermute | solution.py:247
  46.6 1.2 %collective-permute-start.24 = (bf16[16,512]{1,0:T(8,128)(2,1)S(1)}, bf16[16,512]{1,0:T(8,128)(2,1)S(1)}, u32[]{:S(2)}, u32[]{:S(2)}) collective-permute-start(bf16[16,512]{1,0:T(8,128)(2,1)S(1)} %get-tuple-element.151), channel_id=1, source_target_pairs={{0,1},{1,0},{2,3},{3,2},{4,5},{5,4},{6,7},{7,6},{8,9},{9,8},{10,11... | collective-permute-start | bytes 49160 | tf_op jit(solution)/shard_map/ppermute | solution.py:247
  47.8 1.6 %local_gradients.1 = (f32[256,512]{1,0:T(8,128)S(1)}, f32[64,512]{1,0:T(8,128)}, bf16[256,512]{1,0:T(8,128)(2,1)}) custom-call(bf16[256,512]{1,0:T(8,128)(2,1)S(1)} %copy-done.4, f32[400,512]{1,0:T(8,128)S(1)} %get-tuple-element.134.refs_1_, bf16[256,512]{1,0:T(8,128)(2,1)S(1)} %copy-done.5, bf16[400,512]{1,0:T(8,128)(2,1)S(1)} %get-tuple-element.135.refs_3_, ...), custom_call_target="tpu_custom_call" | custom-call | flops 402653184 | bytes 10272768 | tf_op jit(solution)/shard_map/local_gradients/pallas_call | solution.py:188
  50.0 1.0 %add_returned.1 = f32[256,512]{1,0:T(8,128)} custom-call(bf16[32,512]{1,0:T(8,128)(2,1)S(1)} %collective-permute-done.18.refs_0_, bf16[32,512]{1,0:T(8,128)(2,1)S(1)} %collective-permute-done.19.refs_1_, bf16[16,512]{1,0:T(8,128)(2,1)S(1)} %collective-permute-done.20.refs_2_, bf16[16,512]{1,0:T(8,128)(2,1)S(1)} %collective-permute-done.21.refs_3_, ...), custom_call_target="tpu_custom_call" | custom-call | flops 37748736 | bytes 1392640 | tf_op jit(solution)/shard_map/add_returned/pallas_call | solution.py:188
  (74 shorter events, 5.1 us)
Async XLA Ops:
  2.3 9.6 %collective-permute-start = (bf16[32,1024]{1,0:T(8,128)(2,1)S(1)}, bf16[32,1024]{1,0:T(8,128)(2,1)S(1)}, u32[]{:S(2)}, u32[]{:S(2)}) collective-permute-start(bf16[32,1024]{1,0:T(8,128)(2,1)S(1)} %get-tuple-element.87), channel_id=1, source_target_pairs={{0,12},{1,13},{2,14},{3,15},{4,8},{5,9},{6,10},{7,11},{8,4},{9,5},... | collective-permute-start | bytes 196616 | tf_op jit(solution)/shard_map/ppermute | solution.py:247
  7.4 7.7 %collective-permute-start.1 = (bf16[32,1024]{1,0:T(8,128)(2,1)S(1)}, bf16[32,1024]{1,0:T(8,128)(2,1)S(1)}, u32[]{:S(2)}, u32[]{:S(2)}) collective-permute-start(bf16[32,1024]{1,0:T(8,128)(2,1)S(1)} %get-tuple-element.90), channel_id=1, source_target_pairs={{0,4},{1,5},{2,6},{3,7},{4,0},{5,1},{6,2},{7,3},{8,12},{9,13},{10,... | collective-permute-start | bytes 196616 | tf_op jit(solution)/shard_map/ppermute | solution.py:247
  7.4 6.0 %collective-permute-start.2 = (bf16[16,1024]{1,0:T(8,128)(2,1)S(1)}, bf16[16,1024]{1,0:T(8,128)(2,1)S(1)}, u32[]{:S(2)}, u32[]{:S(2)}) collective-permute-start(bf16[16,1024]{1,0:T(8,128)(2,1)S(1)} %get-tuple-element.91), channel_id=1, source_target_pairs={{0,15},{1,2},{2,1},{3,4},{4,3},{5,6},{6,5},{7,8},{8,7},{9,10},{10,... | collective-permute-start | bytes 98312 | tf_op jit(solution)/shard_map/ppermute | solution.py:247
  8.2 5.6 %collective-permute-start.3 = (bf16[16,1024]{1,0:T(8,128)(2,1)S(1)}, bf16[16,1024]{1,0:T(8,128)(2,1)S(1)}, u32[]{:S(2)}, u32[]{:S(2)}) collective-permute-start(bf16[16,1024]{1,0:T(8,128)(2,1)S(1)} %get-tuple-element.92), channel_id=1, source_target_pairs={{0,3},{1,14},{2,5},{3,0},{4,7},{5,2},{6,9},{7,4},{8,11},{9,6},{10,... | collective-permute-start | bytes 98312 | tf_op jit(solution)/shard_map/ppermute | solution.py:247
  10.7 6.5 %collective-permute-start.4 = (bf16[16,1024]{1,0:T(8,128)(2,1)S(1)}, bf16[16,1024]{1,0:T(8,128)(2,1)S(1)}, u32[]{:S(2)}, u32[]{:S(2)}) collective-permute-start(bf16[16,1024]{1,0:T(8,128)(2,1)S(1)} %get-tuple-element.93), channel_id=1, source_target_pairs={{0,11},{1,6},{2,13},{3,8},{4,15},{5,10},{6,1},{7,12},{8,3},{9,14},... | collective-permute-start | bytes 98312 | tf_op jit(solution)/shard_map/ppermute | solution.py:247
  12.0 5.8 %collective-permute-start.5 = (bf16[16,1024]{1,0:T(8,128)(2,1)S(1)}, bf16[16,1024]{1,0:T(8,128)(2,1)S(1)}, u32[]{:S(2)}, u32[]{:S(2)}) collective-permute-start(bf16[16,1024]{1,0:T(8,128)(2,1)S(1)} %get-tuple-element.94), channel_id=1, source_target_pairs={{0,8},{1,9},{2,10},{3,11},{4,12},{5,13},{6,14},{7,15},{8,0},{9,1},... | collective-permute-start | bytes 98312 | tf_op jit(solution)/shard_map/ppermute | solution.py:247
  13.5 4.3 %collective-permute-start.7 = (bf16[32,1024]{1,0:T(8,128)(2,1)S(1)}, bf16[32,1024]{1,0:T(8,128)(2,1)S(1)}, u32[]{:S(2)}, u32[]{:S(2)}) collective-permute-start(bf16[32,1024]{1,0:T(8,128)(2,1)S(1)} %collective-permute-done.refs_0_), channel_id=1, source_target_pairs={{0,1},{1,0},{2,3},{3,2},{4,5},{5,4},{6,7},{7,6},{8,9},{9,8},{10,11... | collective-permute-start | bytes 196616 | tf_op jit(solution)/shard_map/ppermute | solution.py:247
  13.8 3.9 %collective-permute-start.6 = (bf16[16,1024]{1,0:T(8,128)(2,1)S(1)}, bf16[16,1024]{1,0:T(8,128)(2,1)S(1)}, u32[]{:S(2)}, u32[]{:S(2)}) collective-permute-start(bf16[16,1024]{1,0:T(8,128)(2,1)S(1)} %get-tuple-element.95), channel_id=1, source_target_pairs={{0,1},{1,0},{2,3},{3,2},{4,5},{5,4},{6,7},{7,6},{8,9},{9,8},{10,11... | collective-permute-start | bytes 98312 | tf_op jit(solution)/shard_map/ppermute | solution.py:247
  20.8 6.6 %collective-permute-start.9 = (bf16[32,1024]{1,0:T(8,128)(2,1)S(1)}, bf16[32,1024]{1,0:T(8,128)(2,1)S(1)}, u32[]{:S(2)}, u32[]{:S(2)}) collective-permute-start(bf16[32,1024]{1,0:T(8,128)(2,1)S(1)} %get-tuple-element.106), channel_id=1, source_target_pairs={{0,12},{1,13},{2,14},{3,15},{4,8},{5,9},{6,10},{7,11},{8,4},{9,5},... | collective-permute-start | bytes 196616 | tf_op jit(solution)/shard_map/ppermute | solution.py:247
  22.5 7.1 %collective-permute-start.10 = (bf16[32,1024]{1,0:T(8,128)(2,1)S(1)}, bf16[32,1024]{1,0:T(8,128)(2,1)S(1)}, u32[]{:S(2)}, u32[]{:S(2)}) collective-permute-start(bf16[32,1024]{1,0:T(8,128)(2,1)S(1)} %get-tuple-element.109), channel_id=1, source_target_pairs={{0,4},{1,5},{2,6},{3,7},{4,0},{5,1},{6,2},{7,3},{8,12},{9,13},{10,... | collective-permute-start | bytes 196616 | tf_op jit(solution)/shard_map/ppermute | solution.py:247
  22.5 6.0 %collective-permute-start.11 = (bf16[16,1024]{1,0:T(8,128)(2,1)S(1)}, bf16[16,1024]{1,0:T(8,128)(2,1)S(1)}, u32[]{:S(2)}, u32[]{:S(2)}) collective-permute-start(bf16[16,1024]{1,0:T(8,128)(2,1)S(1)} %get-tuple-element.110), channel_id=1, source_target_pairs={{0,15},{1,2},{2,1},{3,4},{4,3},{5,6},{6,5},{7,8},{8,7},{9,10},{10,... | collective-permute-start | bytes 98312 | tf_op jit(solution)/shard_map/ppermute | solution.py:247
  23.4 5.1 %collective-permute-start.12 = (bf16[16,1024]{1,0:T(8,128)(2,1)S(1)}, bf16[16,1024]{1,0:T(8,128)(2,1)S(1)}, u32[]{:S(2)}, u32[]{:S(2)}) collective-permute-start(bf16[16,1024]{1,0:T(8,128)(2,1)S(1)} %get-tuple-element.111), channel_id=1, source_target_pairs={{0,3},{1,14},{2,5},{3,0},{4,7},{5,2},{6,9},{7,4},{8,11},{9,6},{10,... | collective-permute-start | bytes 98312 | tf_op jit(solution)/shard_map/ppermute | solution.py:247
  25.7 5.7 %collective-permute-start.13 = (bf16[16,1024]{1,0:T(8,128)(2,1)S(1)}, bf16[16,1024]{1,0:T(8,128)(2,1)S(1)}, u32[]{:S(2)}, u32[]{:S(2)}) collective-permute-start(bf16[16,1024]{1,0:T(8,128)(2,1)S(1)} %get-tuple-element.112), channel_id=1, source_target_pairs={{0,11},{1,6},{2,13},{3,8},{4,15},{5,10},{6,1},{7,12},{8,3},{9,14},... | collective-permute-start | bytes 98312 | tf_op jit(solution)/shard_map/ppermute | solution.py:247
  27.4 5.1 %collective-permute-start.14 = (bf16[16,1024]{1,0:T(8,128)(2,1)S(1)}, bf16[16,1024]{1,0:T(8,128)(2,1)S(1)}, u32[]{:S(2)}, u32[]{:S(2)}) collective-permute-start(bf16[16,1024]{1,0:T(8,128)(2,1)S(1)} %get-tuple-element.113), channel_id=1, source_target_pairs={{0,8},{1,9},{2,10},{3,11},{4,12},{5,13},{6,14},{7,15},{8,0},{9,1},... | collective-permute-start | bytes 98312 | tf_op jit(solution)/shard_map/ppermute | solution.py:247
  28.5 4.0 %collective-permute-start.16 = (bf16[32,1024]{1,0:T(8,128)(2,1)S(1)}, bf16[32,1024]{1,0:T(8,128)(2,1)S(1)}, u32[]{:S(2)}, u32[]{:S(2)}) collective-permute-start(bf16[32,1024]{1,0:T(8,128)(2,1)S(1)} %collective-permute-done.9.refs_0_), channel_id=1, source_target_pairs={{0,1},{1,0},{2,3},{3,2},{4,5},{5,4},{6,7},{7,6},{8,9},{9,8},{10,11... | collective-permute-start | bytes 196616 | tf_op jit(solution)/shard_map/ppermute | solution.py:247
  28.5 4.0 %collective-permute-start.15 = (bf16[16,1024]{1,0:T(8,128)(2,1)S(1)}, bf16[16,1024]{1,0:T(8,128)(2,1)S(1)}, u32[]{:S(2)}, u32[]{:S(2)}) collective-permute-start(bf16[16,1024]{1,0:T(8,128)(2,1)S(1)} %get-tuple-element.114), channel_id=1, source_target_pairs={{0,1},{1,0},{2,3},{3,2},{4,5},{5,4},{6,7},{7,6},{8,9},{9,8},{10,11... | collective-permute-start | bytes 98312 | tf_op jit(solution)/shard_map/ppermute | solution.py:247
  38.8 6.2 %collective-permute-start.18 = (bf16[32,512]{1,0:T(8,128)(2,1)S(1)}, bf16[32,512]{1,0:T(8,128)(2,1)S(1)}, u32[]{:S(2)}, u32[]{:S(2)}) collective-permute-start(bf16[32,512]{1,0:T(8,128)(2,1)S(1)} %get-tuple-element.143), channel_id=1, source_target_pairs={{0,12},{1,13},{2,14},{3,15},{4,8},{5,9},{6,10},{7,11},{8,4},{9,5},... | collective-permute-start | bytes 98312 | tf_op jit(solution)/shard_map/ppermute | solution.py:247
  40.8 7.0 %collective-permute-start.19 = (bf16[32,512]{1,0:T(8,128)(2,1)S(1)}, bf16[32,512]{1,0:T(8,128)(2,1)S(1)}, u32[]{:S(2)}, u32[]{:S(2)}) collective-permute-start(bf16[32,512]{1,0:T(8,128)(2,1)S(1)} %get-tuple-element.146), channel_id=1, source_target_pairs={{0,4},{1,5},{2,6},{3,7},{4,0},{5,1},{6,2},{7,3},{8,12},{9,13},{10,... | collective-permute-start | bytes 98312 | tf_op jit(solution)/shard_map/ppermute | solution.py:247
  40.8 5.9 %collective-permute-start.20 = (bf16[16,512]{1,0:T(8,128)(2,1)S(1)}, bf16[16,512]{1,0:T(8,128)(2,1)S(1)}, u32[]{:S(2)}, u32[]{:S(2)}) collective-permute-start(bf16[16,512]{1,0:T(8,128)(2,1)S(1)} %get-tuple-element.147), channel_id=1, source_target_pairs={{0,15},{1,2},{2,1},{3,4},{4,3},{5,6},{6,5},{7,8},{8,7},{9,10},{10,... | collective-permute-start | bytes 49160 | tf_op jit(solution)/shard_map/ppermute | solution.py:247
  41.6 5.1 %collective-permute-start.21 = (bf16[16,512]{1,0:T(8,128)(2,1)S(1)}, bf16[16,512]{1,0:T(8,128)(2,1)S(1)}, u32[]{:S(2)}, u32[]{:S(2)}) collective-permute-start(bf16[16,512]{1,0:T(8,128)(2,1)S(1)} %get-tuple-element.148), channel_id=1, source_target_pairs={{0,3},{1,14},{2,5},{3,0},{4,7},{5,2},{6,9},{7,4},{8,11},{9,6},{10,... | collective-permute-start | bytes 49160 | tf_op jit(solution)/shard_map/ppermute | solution.py:247
  44.0 5.4 %collective-permute-start.22 = (bf16[16,512]{1,0:T(8,128)(2,1)S(1)}, bf16[16,512]{1,0:T(8,128)(2,1)S(1)}, u32[]{:S(2)}, u32[]{:S(2)}) collective-permute-start(bf16[16,512]{1,0:T(8,128)(2,1)S(1)} %get-tuple-element.149), channel_id=1, source_target_pairs={{0,11},{1,6},{2,13},{3,8},{4,15},{5,10},{6,1},{7,12},{8,3},{9,14},... | collective-permute-start | bytes 49160 | tf_op jit(solution)/shard_map/ppermute | solution.py:247
  45.0 5.0 %collective-permute-start.23 = (bf16[16,512]{1,0:T(8,128)(2,1)S(1)}, bf16[16,512]{1,0:T(8,128)(2,1)S(1)}, u32[]{:S(2)}, u32[]{:S(2)}) collective-permute-start(bf16[16,512]{1,0:T(8,128)(2,1)S(1)} %get-tuple-element.150), channel_id=1, source_target_pairs={{0,8},{1,9},{2,10},{3,11},{4,12},{5,13},{6,14},{7,15},{8,0},{9,1},... | collective-permute-start | bytes 49160 | tf_op jit(solution)/shard_map/ppermute | solution.py:247
  46.6 3.3 %collective-permute-start.25 = (bf16[32,512]{1,0:T(8,128)(2,1)S(1)}, bf16[32,512]{1,0:T(8,128)(2,1)S(1)}, u32[]{:S(2)}, u32[]{:S(2)}) collective-permute-start(bf16[32,512]{1,0:T(8,128)(2,1)S(1)} %collective-permute-done.18.refs_0_), channel_id=1, source_target_pairs={{0,1},{1,0},{2,3},{3,2},{4,5},{5,4},{6,7},{7,6},{8,9},{9,8},{10,11... | collective-permute-start | bytes 98312 | tf_op jit(solution)/shard_map/ppermute | solution.py:247
  46.6 3.3 %collective-permute-start.24 = (bf16[16,512]{1,0:T(8,128)(2,1)S(1)}, bf16[16,512]{1,0:T(8,128)(2,1)S(1)}, u32[]{:S(2)}, u32[]{:S(2)}) collective-permute-start(bf16[16,512]{1,0:T(8,128)(2,1)S(1)} %get-tuple-element.151), channel_id=1, source_target_pairs={{0,1},{1,0},{2,3},{3,2},{4,5},{5,4},{6,7},{7,6},{8,9},{9,8},{10,11... | collective-permute-start | bytes 49160 | tf_op jit(solution)/shard_map/ppermute | solution.py:247
  (21 other events, 229.0 us)

commit v11 on v10

--- a/solution.py
+++ b/solution.py
@@ -41,10 +41,6 @@
     return lax.rsqrt(jnp.mean(raw * raw, axis=-1, keepdims=True) + 1e-05)
 
 
-def norm_back(normed, scale_inv, upstream):
-    return scale_inv * (upstream - normed * jnp.mean(upstream * normed, axis=-1, keepdims=True))
-
-
 def row_chunks(rows, size=CHUNK):
     return [slice(start, min(start + size, rows)) for start in range(0, rows, size)]
 
@@ -59,36 +55,27 @@
         part = raw[rows, :]
         scale_inv = scale_rows(part)
         normed_ref[rows, :] = (part * scale_inv).astype(normed_ref.dtype)
-        scale_ref[rows, :] = jnp.broadcast_to(
-            scale_inv, (part.shape[0], scale_ref.shape[1])
-        ).astype(scale_ref.dtype)
-
-
-def write_slope(pre_ref, slope_ref):
+        scale_ref[rows, :] = scale_inv
+
+
+def write_slopes(pre_ref, normed_ref, scale_ref, second_ref, gain_ref, turned_ref):
+    raw = mm_t(normed_ref[...], second_ref[...])
     for rows in row_chunks(pre_ref.shape[0]):
-        slope_ref[rows, :] = silu_and_slope(pre_ref[rows, :])[1].astype(BF16)
-
-
-def edge_back(upstream, normed_ref, scale_ref, upstream_ref, product_ref, out_ref):
+        gain = silu_and_slope(pre_ref[rows, :])[1] * scale_ref[rows, :]
+        gain_ref[rows, :] = gain.astype(BF16)
+        turned_ref[rows, :] = (gain * raw[rows, :]).astype(BF16)
+
+
+def edge_back(both, normed_ref, gain_ref, turned_ref, out_ref):
     edges, features = normed_ref.shape
-    lanes = scale_ref.shape[1]
     for rows in row_chunks(edges):
-        part = upstream[rows, :].astype(BF16)
-        upstream_ref[rows, :] = part
-        product_ref[rows, :] = part * normed_ref[rows, :]
-    ones = jnp.full((features, lanes), 1.0 / features, BF16)
-    means = mm(product_ref[...], ones).astype(BF16)
-    for rows in row_chunks(edges):
-        mean, scale_inv = means[rows, :], scale_ref[rows, :]
-        for columns in row_chunks(features, lanes):
-            out_ref[rows, columns] = scale_inv * (
-                upstream_ref[rows, columns] - normed_ref[rows, columns] * mean
-            )
-
-
-def times_slope(raw, slope_ref, out_ref):
-    for rows in row_chunks(out_ref.shape[0]):
-        out_ref[rows, :] = raw[rows, :].astype(BF16) * slope_ref[rows, :]
+        mean = jnp.mean(
+            both[rows, :features] * normed_ref[rows, :].astype(F32), axis=-1, keepdims=True
+        )
+        out_ref[rows, :] = (
+            gain_ref[rows, :] * both[rows, features:].astype(BF16)
+            - turned_ref[rows, :] * mean.astype(BF16)
+        )
 
 
 def neighbour_offsets(peer_count):
@@ -379,6 +366,7 @@
     arrived = exchange(outgoing)
 
     def local(
+        select_ref,
         nodes_ref,
         mesh_ref,
         enc_edges_ref,
@@ -401,14 +389,22 @@
         dec_pick_ref,
         dec_pool_ref,
         enc_centred_ref,
-        mesh_centred_ref,
         dec_centred_ref,
+        mesh_wide_ref,
+        mesh_base_ref,
+        shared_pool_ref,
         table_ref,
     ):
         onehot_pair(enc_grid_ref, enc_mesh_ref, spots, mesh_count, enc_pick_ref, enc_pool_ref)
         onehot_pair(dec_grid_ref, dec_mesh_ref, spots, mesh_count, dec_pick_ref, dec_pool_ref)
         enc_centred_ref[...] = centred(enc_second_ref[...], 1).astype(BF16)
-        mesh_centred_ref[...] = centred(mesh_second_ref[...], 1).astype(BF16)
+        mesh_centred = centred(mesh_second_ref[...], 1).astype(BF16)
+        mesh_wide_ref[:, low] = mesh_centred
+        mesh_wide_ref[:, high] = mm(mesh_centred, dec_first_ref[high, :]).astype(BF16)
+        mesh_base_ref[...] = mm(mesh_ref[...], dec_first_ref[high, :])
+        shared_pool_ref[...] = mm(
+            select_ref[:slots, :], dec_pool_ref[:grid_count, :]
+        ).astype(BF16)
         dec_centred_ref[...] = centred(dec_second_ref[...], 1).astype(BF16)
         nodes = nodes_ref[...]
         mesh_part_ref[...] = mm(mesh_ref[...], mesh_first_ref[low, :])
@@ -430,12 +426,15 @@
         dec_pick,
         dec_pool,
         enc_centred,
-        mesh_centred,
         dec_centred,
+        mesh_wide,
+        mesh_base,
+        shared_pool,
     ) = call(
         local,
         "local_products",
         [
+            select,
             grid_nodes,
             mesh_nodes,
             enc_edges,
@@ -460,7 +459,13 @@
             ((dec_count, total), BF16),
             ((total, dec_count), BF16),
         ]
-        + [((feat, feat), BF16)] * 3,
+        + [
+            ((feat, feat), BF16),
+            ((feat, feat), BF16),
+            ((feat, 2 * feat), BF16),
+            ((mesh_count, feat), F32),
+            ((slots, dec_count), BF16),
+        ],
         scratch=[((total, feat), BF16)],
         flops=2 * feat * (feat * (2 * grid_count + enc_count + dec_count) + total * dec_count),
     )
@@ -468,7 +473,7 @@
     def forward(*refs):
         arrived_refs, refs = refs[:arrived_count], refs[arrived_count:]
         (
-            select_ref,
+            shared_pool_ref,
             enc_part_ref,
             dec_part_ref,
             mesh_part_ref,
@@ -476,16 +481,15 @@
             enc_pool_ref,
             dec_pick_ref,
             dec_pool_ref,
-            mesh_ref,
             enc_wg_ref,
             dec_wg_ref,
             enc_w2_ref,
             mesh_wa_ref,
             mesh_w2_ref,
-            dec_wm_ref,
+            mesh_base_ref,
             dec_w2_ref,
-        ) = refs[:16]
-        refs = refs[16:]
+        ) = refs[:15]
+        refs = refs[15:]
         out_refs, refs = refs[:sent_count], refs[sent_count:]
         (
             spot_ref,
@@ -511,10 +515,11 @@
         agg = mm(enc_pool_ref[mesh_rows, :], enc_normed_ref[...]).astype(BF16)
         mesh_pre_ref[...] = mesh_part_ref[...] + mm(agg, mesh_wa_ref[high, :])
         write_silu(mesh_pre_ref, mesh_act_ref)
-        write_norm(mm(mesh_act_ref[...], mesh_w2_ref[...]), mesh_normed_ref, mesh_scale_ref)
-        mesh_out = (mesh_ref[...].astype(F32) + mesh_normed_ref[...]).astype(BF16)
+        both = mm(mesh_act_ref[...], mesh_w2_ref[...])
+        write_norm(both[:, low], mesh_normed_ref, mesh_scale_ref)
+        mesh_sent = mesh_base_ref[...] + mesh_scale_ref[...] * both[:, high]
         table_ref[:slots, :] = mm(rows, dec_wg_ref[low, :]).astype(BF16)
-        table_ref[slots : slots + mesh_count, :] = mm(mesh_out, dec_wm_ref[high, :]).astype(BF16)
+        table_ref[slots : slots + mesh_count, :] = mesh_sent.astype(BF16)
         table_ref[slots + mesh_count :, :] = jnp.zeros(
             (total - spots - mesh_count, feat), BF16
         )
@@ -522,20 +527,19 @@
         write_silu(dec_pre_ref, dec_act_ref)
         write_norm(mm(dec_act_ref[...], dec_w2_ref[...]), dec_normed_ref, dec_scale_ref)
         spot_ref[...] = mm(dec_pool_ref[:spots, :], dec_normed_ref[...])
-        shared = mm(select_ref[:slots, :], spot_ref[:grid_count, :].astype(BF16)).astype(BF16)
+        shared = mm(shared_pool_ref[...], dec_normed_ref[...]).astype(BF16)
         slot_msg = spot_ref[grid_count:, :].astype(BF16)
         send(
             out_refs, lambda j: slot_msg[reverse[j] * width : (reverse[j] + 1) * width, :], low
         )
         send(out_refs, lambda j: shared[j * width : (j + 1) * width, :], high)
 
-    lanes = 128
     saved_shapes = [
         ((enc_count, feat), BF16),
-        ((enc_count, lanes), BF16),
+        ((enc_count, 1), F32),
         ((enc_count, feat), F32),
         ((dec_count, feat), BF16),
-        ((dec_count, lanes), BF16),
+        ((dec_count, 1), F32),
         ((dec_count, feat), F32),
         ((mesh_count, feat), F32),
         ((mesh_count, 1), F32),
@@ -546,7 +550,7 @@
         "edges_forward",
         [
             *arrived,
-            select,
+            shared_pool,
             enc_part,
             dec_part,
             mesh_part,
@@ -554,13 +558,12 @@
             enc_pool,
             dec_pick,
             dec_pool,
-            mesh_nodes,
             enc_first,
             dec_first,
             enc_centred,
             mesh_first,
-            mesh_centred,
-            dec_first,
+            mesh_wide,
+            mesh_base,
             dec_centred,
         ],
         sent_shapes(2 * feat)
@@ -588,43 +591,88 @@
             grid_second_ref,
             cot_ref,
             mesh_first_ref,
+            mesh_second_ref,
+            dec_first_ref,
+            dec_second_ref,
+            enc_second_ref,
             mesh_ref,
+            mesh_cot_ref,
+            enc_normed_ref,
+            enc_scale_ref,
+            enc_pre_ref,
+            dec_normed_ref,
+            dec_scale_ref,
+            dec_pre_ref,
             mesh_normed_ref,
-            enc_pre_ref,
-            dec_pre_ref,
             mesh_pre_ref,
+            mesh_wide_ref,
             part_ref,
             cot_rows_ref,
-            grid_w2_ref,
-            grid_wa_ref,
-            mesh_wa_ref,
+            cot_turned_ref,
+            grid_wide_ref,
+            grid_back_ref,
+            mesh_in_ref,
+            mesh_back_ref,
             mesh_out_ref,
-            enc_slope_ref,
-            dec_slope_ref,
+            mesh_cot_turned_ref,
             mesh_slope_ref,
+            mesh_turned_ref,
+            enc_gain_ref,
+            enc_turned_ref,
+            dec_gain_ref,
+            dec_turned_ref,
         ) = refs
         part_ref[:grid_count, :] = mm(nodes_ref[...], grid_first_ref[low, :])
         part_ref[grid_count:, :] = mm(by_slot(arrived_refs, low), grid_first_ref[low, :])
         mesh_out_ref[...] = (mesh_ref[...].astype(F32) + mesh_normed_ref[...]).astype(BF16)
-        cot_rows_ref[:grid_count, :] = centred(cot_ref[...], 1)
-        cot_rows_ref[grid_count:, :] = centred(by_slot(arrived_refs, high), 1)
-        grid_w2_ref[...] = centred(grid_second_ref[...], 1).astype(BF16)
-        grid_wa_ref[...] = centred(grid_first_ref[high, :], 0).astype(BF16)
-        mesh_wa_ref[...] = centred(mesh_first_ref[high, :], 0).astype(BF16)
-        write_slope(enc_pre_ref, enc_slope_ref)
-        write_slope(dec_pre_ref, dec_slope_ref)
-        write_slope(mesh_pre_ref, mesh_slope_ref)
+        cot_rows_ref[:grid_count, :] = cot_ref[...]
+        cot_rows_ref[grid_count:, :] = by_slot(arrived_refs, high)
+        second = centred(grid_second_ref[...], 1).astype(BF16)
+        grid_wide_ref[:, low] = second
+        grid_wide_ref[:, high] = mm_t(second, grid_second_ref[...]).astype(BF16)
+        cot_turned_ref[...] = mm_t(cot_rows_ref[...], second)
+        grid_back_ref[low, :] = centred(grid_first_ref[high, :], 0).astype(BF16)
+        grid_back_ref[high, :] = mm(dec_second_ref[...], grid_back_ref[low, :]).astype(BF16)
+        mesh_back_ref[low, :] = centred(mesh_first_ref[high, :], 0).astype(BF16)
+        mesh_back_ref[high, :] = mm(enc_second_ref[...], mesh_back_ref[low, :]).astype(BF16)
+        mesh_in_ref[low, :] = dec_first_ref[high, :]
+        mesh_in_ref[high, :] = mm(mesh_wide_ref[:, low], dec_first_ref[high, :]).astype(BF16)
+        mesh_cot_turned_ref[...] = mm_t(mesh_cot_ref[...], mesh_wide_ref[:, low])
+        mesh_turned_ref[...] = mm_t(mesh_normed_ref[...].astype(BF16), mesh_second_ref[...])
+        mesh_slope_ref[...] = silu_and_slope(mesh_pre_ref[...])[1]
+        write_slopes(
+            enc_pre_ref,
+            enc_normed_ref,
+            enc_scale_ref,
+            enc_second_ref,
+            enc_gain_ref,
+            enc_turned_ref,
+        )
+        write_slopes(
+            dec_pre_ref,
+            dec_normed_ref,
+            dec_scale_ref,
+            dec_second_ref,
+            dec_gain_ref,
+            dec_turned_ref,
+        )
 
     (
         grid_part,
         cot_rows,
-        grid_w2_centred,
-        grid_wa_centred,
-        mesh_wa_centred,
+        cot_turned,
+        grid_wide,
+        grid_back,
+        mesh_in,
+        mesh_back,
         mesh_out,
-        enc_slope,
-        dec_slope,
+        mesh_cot_turned,
         mesh_slope,
+        mesh_turned,
+        enc_gain,
+        enc_turned,
+        dec_gain,
+        dec_turned,
     ) = call(
         between,
         "slopes_and_nodes",
@@ -635,19 +683,38 @@
             grid_second,
             grid_cot,
             mesh_first,
+            mesh_second,
+            dec_first,
+            dec_second,
+            enc_second,
             mesh_nodes,
+            mesh_cot,
+            enc_normed,
+            enc_scale,
+            enc_pre,
+            dec_normed,
+            dec_scale,
+            dec_pre,
             mesh_normed,
-            enc_pre,
-            dec_pre,
             mesh_pre,
-        ],
-        [((spots, feat), F32)] * 2
-        + [((feat, feat), BF16)] * 3
-        + [
+            mesh_wide,
+        ],
+        [
+            ((spots, feat), F32),
+            ((spots, feat), BF16),
+            ((spots, feat), F32),
+            ((feat, 2 * feat), BF16),
+            ((2 * feat, feat), BF16),
+            ((2 * feat, feat), BF16),
+            ((2 * feat, feat), BF16),
             ((mesh_count, feat), BF16),
+            ((mesh_count, feat), F32),
+            ((mesh_count, feat), F32),
+            ((mesh_count, feat), F32),
+            ((enc_count, feat), BF16),
             ((enc_count, feat), BF16),
             ((dec_count, feat), BF16),
-            ((mesh_count, feat), BF16),
+            ((dec_count, feat), BF16),
         ],
         flops=16 * spots * feat * feat,
     )
@@ -659,33 +726,32 @@
             grid_part_ref,
             select_t_ref,
             cot_rows_ref,
+            cot_turned_ref,
             mesh_cot_ref,
+            mesh_cot_turned_ref,
             enc_pick_ref,
             enc_pool_ref,
             dec_pick_ref,
             dec_pool_ref,
-            grid_wa_ref,
-            grid_wac_ref,
-            grid_w2_ref,
-            grid_w2c_ref,
-            dec_w2_ref,
-            dec_wm_ref,
-            mesh_wac_ref,
-            mesh_w2_ref,
-            enc_w2_ref,
-            enc_wg_ref,
-            dec_wg_ref,
+            grid_first_ref,
+            grid_wide_ref,
+            grid_back_ref,
+            mesh_in_ref,
+            mesh_back_ref,
+            enc_first_ref,
+            dec_first_ref,
             enc_normed_ref,
-            enc_scale_ref,
-            enc_slope_ref,
+            enc_gain_ref,
+            enc_turned_ref,
             dec_normed_ref,
-            dec_scale_ref,
-            dec_slope_ref,
+            dec_gain_ref,
+            dec_turned_ref,
             mesh_normed_ref,
             mesh_scale_ref,
             mesh_slope_ref,
-        ) = refs[:29]
-        refs = refs[29:]
+            mesh_turned_ref,
+        ) = refs[:28]
+        refs = refs[28:]
         out_refs, refs = refs[:sent_count], refs[sent_count:]
         (
             grid_normed_ref,
@@ -698,15 +764,9 @@
             agg_ref,
             grid_act_ref,
             grid_slope_ref,
-            grid_gout_ref,
             spot_grad_ref,
-            dec_up_ref,
-            dec_product_ref,
-            dec_gout_ref,
-            mesh_gout_ref,
-            enc_up_ref,
-            enc_product_ref,
-            enc_gout_ref,
+            dec_gpre_ref,
+            enc_gpre_ref,
         ) = refs
         agg_ref[:grid_count, :] = (
             spot_ref[:grid_count, :] + mm(select_t_ref[:, :slots], by_row(returned_refs, low))
@@ -714,56 +774,52 @@
         agg_ref[grid_count:, :] = (
             spot_ref[grid_count:, :] + by_slot(returned_refs, high).astype(F32)
         ).astype(BF16)
-        pre = grid_part_ref[...] + mm(agg_ref[...], grid_wa_ref[high, :])
+        pre = grid_part_ref[...] + mm(agg_ref[...], grid_first_ref[high, :])
         for rows in row_chunks(spots):
             act, slope = silu_and_slope(pre[rows, :])
             grid_act_ref[rows, :] = act.astype(BF16)
-            grid_slope_ref[rows, :] = slope.astype(BF16)
-        raw = mm(grid_act_ref[...], grid_w2c_ref[...])
+            grid_slope_ref[rows, :] = slope
+        both = mm(grid_act_ref[...], grid_wide_ref[...])
         for rows in row_chunks(spots):
-            part = raw[rows, :]
+            part = both[rows, low]
             scale_inv = scale_rows(part)
             normed = part * scale_inv
             grid_normed_ref[rows, :] = normed
-            grid_gout_ref[rows, :] = norm_back(normed, scale_inv, cot_rows_ref[rows, :]).astype(
-                BF16
-            )
-        times_slope(mm_t(grid_gout_ref[...], grid_w2_ref[...]), grid_slope_ref, grid_gpre_ref)
-        spot_grad_ref[:spots, :] = mm_t(grid_gpre_ref[...], grid_wac_ref[...]).astype(BF16)
-        spot_grad_ref[spots:, :] = jnp.zeros((total - spots, feat), BF16)
+            mean = jnp.mean(cot_rows_ref[rows, :].astype(F32) * normed, axis=-1, keepdims=True)
+            raw = scale_inv * (cot_turned_ref[rows, :] - (mean * scale_inv) * both[rows, high])
+            grid_gpre_ref[rows, :] = (raw * grid_slope_ref[rows, :]).astype(BF16)
+        spot_grad_ref[:spots, :] = mm_t(grid_gpre_ref[...], grid_back_ref[...]).astype(BF16)
+        spot_grad_ref[spots:, :] = jnp.zeros((total - spots, 2 * feat), BF16)
         edge_back(
             mm(dec_pick_ref[...], spot_grad_ref[...]),
             dec_normed_ref,
-            dec_scale_ref,
-            dec_up_ref,
-            dec_product_ref,
-            dec_gout_ref,
+            dec_gain_ref,
+            dec_turned_ref,
+            dec_gpre_ref,
         )
-        times_slope(mm_t(dec_gout_ref[...], dec_w2_ref[...]), dec_slope_ref, dec_gout_ref)
-        pooled = mm(dec_pool_ref[...], dec_gout_ref[...]).astype(BF16)
+        mesh_sum = mm(dec_pool_ref[mesh_rows, :], dec_gpre_ref[...]).astype(BF16)
+        both = mm_t(mesh_sum, mesh_in_ref[...])
+        mesh_gin = mesh_cot_ref[...].astype(F32) + both[:, low]
+        mesh_gin_ref[...] = mesh_gin
+        mean = jnp.mean(mesh_gin * mesh_normed_ref[...], axis=-1, keepdims=True)
+        raw = mesh_cot_turned_ref[...] + both[:, high] - mean * mesh_turned_ref[...]
+        mesh_gpre_ref[...] = (mesh_scale_ref[...] * raw * mesh_slope_ref[...]).astype(BF16)
+        mesh_gagg = mm_t(mesh_gpre_ref[...], mesh_back_ref[...]).astype(BF16)
+        pooled = mm(dec_pool_ref[:spots, :], dec_gpre_ref[...]).astype(BF16)
         gpd_ref[...] = pooled[:grid_count, :]
-        slot_back = mm_t(pooled[grid_count:spots, :], dec_wg_ref[low, :])
-        mesh_gin = mesh_cot_ref[...].astype(F32) + mm_t(pooled[mesh_rows, :], dec_wm_ref[high, :])
-        mesh_gin_ref[...] = mesh_gin
-        mesh_gout_ref[...] = norm_back(
-            mesh_normed_ref[...], mesh_scale_ref[...], centred(mesh_gin, 1)
-        ).astype(BF16)
-        times_slope(mm_t(mesh_gout_ref[...], mesh_w2_ref[...]), mesh_slope_ref, mesh_gpre_ref)
-        gagg = mm_t(mesh_gpre_ref[...], mesh_wac_ref[...]).astype(BF16)
+        slot_back = mm_t(pooled[grid_count:, :], dec_first_ref[low, :])
         edge_back(
-            mm(enc_pick_ref[:, mesh_rows], gagg),
+            mm(enc_pick_ref[:, mesh_rows], mesh_gagg),
             enc_normed_ref,
-            enc_scale_ref,
-            enc_up_ref,
-            enc_product_ref,
-            enc_gout_ref,
+            enc_gain_ref,
+            enc_turned_ref,
+            enc_gpre_ref,
         )
-        times_slope(mm_t(enc_gout_ref[...], enc_w2_ref[...]), enc_slope_ref, enc_gout_ref)
-        pooled = mm(enc_pool_ref[...], enc_gout_ref[...]).astype(BF16)
+        pooled = mm(enc_pool_ref[...], enc_gpre_ref[...]).astype(BF16)
         gpe_ref[...] = pooled[:grid_count, :]
         mesh_pool_ref[...] = pooled[mesh_rows, :]
         slot_back = (
-            slot_back + mm_t(pooled[grid_count:spots, :], enc_wg_ref[low, :])
+            slot_back + mm_t(pooled[grid_count:spots, :], enc_first_ref[low, :])
         ).astype(BF16)
         send(out_refs, lambda j: slot_back[reverse[j] * width : (reverse[j] + 1) * width, :])
 
@@ -776,31 +832,30 @@
             grid_part,
             select_t,
             cot_rows,
+            cot_turned,
             mesh_cot,
+            mesh_cot_turned,
             enc_pick,
             enc_pool,
             dec_pick,
             dec_pool,
             grid_first,
-            grid_wa_centred,
-            grid_second,
-            grid_w2_centred,
-            dec_second,
-            dec_first,
-            mesh_wa_centred,
-            mesh_second,
-            enc_second,
+            grid_wide,
+            grid_back,
+            mesh_in,
+            mesh_back,
             enc_first,
             dec_first,
             enc_normed,
-            enc_scale,
-            enc_slope,
+            enc_gain,
+            enc_turned,
             dec_normed,
-            dec_scale,
-            dec_slope,
+            dec_gain,
+            dec_turned,
             mesh_normed,
             mesh_scale,
             mesh_slope,
+            mesh_turned,
         ],
         sent_shapes(feat)
         + [
@@ -812,11 +867,14 @@
             ((mesh_count, feat), BF16),
             ((mesh_count, feat), BF16),
         ],
-        scratch=[((spots, feat), BF16)] * 4
-        + [((total, feat), BF16)]
-        + [((dec_count, feat), BF16)] * 3
-        + [((mesh_count, feat), BF16)]
-        + [((enc_count, feat), BF16)] * 3,
+        scratch=[
+            ((spots, feat), BF16),
+            ((spots, feat), BF16),
+            ((spots, feat), F32),
+            ((total, 2 * feat), BF16),
+            ((dec_count, feat), BF16),
+            ((enc_count, feat), BF16),
+        ],
         flops=2 * feat * feat * (4 * spots + 3 * dec_count + 2 * enc_count),
     )
     outgoing, results = results[:sent_count], results[sent_count:]

time: 51.2 us -> 51.1 us (level)
  waiting for transfers between devices: 4.55 us -> 3.06 us
  Pallas kernels: 16.9 us -> 17.9 us
    ppermute x27, waiting for transfers between devices: 4.55 us -> 3.06 us  [permute(): return lax.ppermute(part, 'tile', pairs)]
    pallas_call x8, Pallas kernels: 16.9 us -> 17.9 us  [call(): pl.pallas_call(kernel, name=name, in_specs=specs, out_specs=[pl.BlockSpec...]
  transfers between devices with their start and end apart: 27 -> 27, of which waited for: 7 -> 6; matrix products, arithmetic and copies ran while one was open for 0% -> 0% of each run, Pallas kernels for 10% -> 15%
where the time goes in v11:
time: 51.1 us; the launch traced here: 51 us
  starting transfers between devices  28.9 us (57%)
  Pallas kernels  17.9 us (35%)
  waiting for transfers between devices  3.06 us (6%)
  between operations  1 us (2%)
    ppermute x27, starting transfers between devices, permute(): return lax.ppermute(part, 'tile', pairs)  28.9 us
    pallas_call x8, Pallas kernels, call(): pl.pallas_call(kernel, name=name, in_specs=specs, out_specs=[pl.BlockSpec...  17.9 us
    ppermute x27, waiting for transfers between devices, permute(): return lax.ppermute(part, 'tile', pairs)  3.06 us
  transfers between devices with their start and end apart: 27, of which 6 were waited for; matrix products, arithmetic and copies ran while one was open for 0% of the time, Pallas kernels for 15%

profile of v11, /device:TPU:0, one launch (start us, length us, event | category | flops | bytes accessed | tf_op | source)
XLA Modules:
  0.0 51.0 jit_solution(3754550731496810929)
XLA Ops:
  0.6 1.4 %pack_rows.1 = (bf16[256,256]{1,0:T(8,128)(2,1)S(1)}, bf16[32,1024]{1,0:T(8,128)(2,1)S(1)}, bf16[32,1024]{1,0:T(8,128)(2,1)S(1)}, bf16[16,1024]{1,0:T(8,128)(2,1...) custom-call(s32[9,16]{1,0:T(8,128)} %refs_0_.2, ...), custom_call_target="tpu_custom_call" | custom-call | flops 75497472 | bytes 950884 | tf_op jit(solution)/shard_map/pack_rows/pallas_call | solution.py:175
  2.3 5.1 %collective-permute-start = (bf16[32,1024]{1,0:T(8,128)(2,1)S(1)}, bf16[32,1024]{1,0:T(8,128)(2,1)S(1)}, u32[]{:S(2)}, u32[]{:S(2)}) collective-permute-start(bf16[32,1024]{1,0:T(8,128)(2,1)S(1)} %get-tuple-element.95), channel_id=1, source_target_pairs={{0,12},{1,13},{2,14},{3,15},{4,8},{5,9},{6,10},{7,11},{8,4},{9,5},... | collective-permute-start | bytes 196616 | tf_op jit(solution)/shard_map/ppermute | solution.py:234
  8.2 2.5 %collective-permute-start.3 = (bf16[16,1024]{1,0:T(8,128)(2,1)S(1)}, bf16[16,1024]{1,0:T(8,128)(2,1)S(1)}, u32[]{:S(2)}, u32[]{:S(2)}) collective-permute-start(bf16[16,1024]{1,0:T(8,128)(2,1)S(1)} %get-tuple-element.100), channel_id=1, source_target_pairs={{0,3},{1,14},{2,5},{3,0},{4,7},{5,2},{6,9},{7,4},{8,11},{9,6},{10,... | collective-permute-start | bytes 98312 | tf_op jit(solution)/shard_map/ppermute | solution.py:234
  10.7 1.3 %collective-permute-start.4 = (bf16[16,1024]{1,0:T(8,128)(2,1)S(1)}, bf16[16,1024]{1,0:T(8,128)(2,1)S(1)}, u32[]{:S(2)}, u32[]{:S(2)}) collective-permute-start(bf16[16,1024]{1,0:T(8,128)(2,1)S(1)} %get-tuple-element.101), channel_id=1, source_target_pairs={{0,11},{1,6},{2,13},{3,8},{4,15},{5,10},{6,1},{7,12},{8,3},{9,14},... | collective-permute-start | bytes 98312 | tf_op jit(solution)/shard_map/ppermute | solution.py:234
  12.0 1.1 %collective-permute-start.5 = (bf16[16,1024]{1,0:T(8,128)(2,1)S(1)}, bf16[16,1024]{1,0:T(8,128)(2,1)S(1)}, u32[]{:S(2)}, u32[]{:S(2)}) collective-permute-start(bf16[16,1024]{1,0:T(8,128)(2,1)S(1)} %get-tuple-element.102), channel_id=1, source_target_pairs={{0,8},{1,9},{2,10},{3,11},{4,12},{5,13},{6,14},{7,15},{8,0},{9,1},... | collective-permute-start | bytes 98312 | tf_op jit(solution)/shard_map/ppermute | solution.py:234
  13.8 1.3 %collective-permute-start.6 = (bf16[16,1024]{1,0:T(8,128)(2,1)S(1)}, bf16[16,1024]{1,0:T(8,128)(2,1)S(1)}, u32[]{:S(2)}, u32[]{:S(2)}) collective-permute-start(bf16[16,1024]{1,0:T(8,128)(2,1)S(1)} %get-tuple-element.103), channel_id=1, source_target_pairs={{0,1},{1,0},{2,3},{3,2},{4,5},{5,4},{6,7},{7,6},{8,9},{9,8},{10,11... | collective-permute-start | bytes 98312 | tf_op jit(solution)/shard_map/ppermute | solution.py:234
  15.3 2.3 %local_products.1 = (f32[384,512]{1,0:T(8,128)S(1)}, f32[768,512]{1,0:T(8,128)S(1)}, f32[64,512]{1,0:T(8,128)S(1)}, bf16[384,512]{1,0:T(8,128)(2,1)S(1)}, bf16[5...) custom-call(bf16[256,256]{1,0:T(8,128)(2,1)S(1)} %get-tuple-element., ...), custom_call_target="tpu_custom_call" | custom-call | flops 1275068416 | bytes 14713856 | tf_op jit(solution)/shard_map/local_products/pallas_call | solution.py:175
  17.8 2.9 %edges_forward.1 = (bf16[32,1024]{1,0:T(8,128)(2,1)S(1)}, bf16[32,1024]{1,0:T(8,128)(2,1)S(1)}, bf16[16,1024]{1,0:T(8,128)(2,1)S(1)}, bf16[16,1024]{1,0:T(8,128)...) custom-call(bf16[32,1024]{1,0:T(8,128)(2,1)S(1)} %collective-permute, ...), custom_call_target="tpu_custom_call" | custom-call | flops 1207959552 | bytes 16839424 | tf_op jit(solution)/shard_map/edges_forward/pallas_call | solution.py:175
  20.7 1.7 %collective-permute-start.9 = (bf16[32,1024]{1,0:T(8,128)(2,1)S(1)}, bf16[32,1024]{1,0:T(8,128)(2,1)S(1)}, u32[]{:S(2)}, u32[]{:S(2)}) collective-permute-start(bf16[32,1024]{1,0:T(8,128)(2,1)S(1)} %get-tuple-element.116), channel_id=1, source_target_pairs={{0,12},{1,13},{2,14},{3,15},{4,8},{5,9},{6,10},{7,11},{8,4},{9,5},... | collective-permute-start | bytes 196616 | tf_op jit(solution)/shard_map/ppermute | solution.py:234
  22.4 1.4 %collective-permute-start.11 = (bf16[16,1024]{1,0:T(8,128)(2,1)S(1)}, bf16[16,1024]{1,0:T(8,128)(2,1)S(1)}, u32[]{:S(2)}, u32[]{:S(2)}) collective-permute-start(bf16[16,1024]{1,0:T(8,128)(2,1)S(1)} %get-tuple-element.120), channel_id=1, source_target_pairs={{0,15},{1,2},{2,1},{3,4},{4,3},{5,6},{6,5},{7,8},{8,7},{9,10},{10,... | collective-permute-start | bytes 98312 | tf_op jit(solution)/shard_map/ppermute | solution.py:234
  23.8 1.9 %collective-permute-start.12 = (bf16[16,1024]{1,0:T(8,128)(2,1)S(1)}, bf16[16,1024]{1,0:T(8,128)(2,1)S(1)}, u32[]{:S(2)}, u32[]{:S(2)}) collective-permute-start(bf16[16,1024]{1,0:T(8,128)(2,1)S(1)} %get-tuple-element.121), channel_id=1, source_target_pairs={{0,3},{1,14},{2,5},{3,0},{4,7},{5,2},{6,9},{7,4},{8,11},{9,6},{10,... | collective-permute-start | bytes 98312 | tf_op jit(solution)/shard_map/ppermute | solution.py:234
  25.6 0.7 %collective-permute-start.13 = (bf16[16,1024]{1,0:T(8,128)(2,1)S(1)}, bf16[16,1024]{1,0:T(8,128)(2,1)S(1)}, u32[]{:S(2)}, u32[]{:S(2)}) collective-permute-start(bf16[16,1024]{1,0:T(8,128)(2,1)S(1)} %get-tuple-element.122), channel_id=1, source_target_pairs={{0,11},{1,6},{2,13},{3,8},{4,15},{5,10},{6,1},{7,12},{8,3},{9,14},... | collective-permute-start | bytes 98312 | tf_op jit(solution)/shard_map/ppermute | solution.py:234
  26.4 1.1 %collective-permute-done.9.refs_0_ = bf16[32,1024]{1,0:T(8,128)(2,1)S(1)} collective-permute-done((bf16[32,1024]{1,0:T(8,128)(2,1)S(1)}, bf16[32,1024]{1,0:T(8,128)(2,1)S(1)}, u32[]{:S(2)}, u32[]{:S(2)}) %collective-permute-start.9) | collective-permute-done | bytes 65568 | tf_op jit(solution)/shard_map/ppermute | solution.py:234
  28.5 1.0 %collective-permute-start.15 = (bf16[16,1024]{1,0:T(8,128)(2,1)S(1)}, bf16[16,1024]{1,0:T(8,128)(2,1)S(1)}, u32[]{:S(2)}, u32[]{:S(2)}) collective-permute-start(bf16[16,1024]{1,0:T(8,128)(2,1)S(1)} %get-tuple-element.124), channel_id=1, source_target_pairs={{0,1},{1,0},{2,3},{3,2},{4,5},{5,4},{6,7},{7,6},{8,9},{9,8},{10,11... | collective-permute-start | bytes 98312 | tf_op jit(solution)/shard_map/ppermute | solution.py:234
  29.5 3.9 %slopes_and_nodes.1 = (f32[400,512]{1,0:T(8,128)S(1)}, bf16[400,512]{1,0:T(8,128)(2,1)S(1)}, f32[400,512]{1,0:T(8,128)S(1)}, bf16[512,1024]{1,0:T(8,128)(2,1)S(1...) custom-call(bf16[32,1024]{1,0:T(8,128)(2,1)S(1)} %collective-permute, ...), custom_call_target="tpu_custom_call" | custom-call | flops 1677721600 | bytes 20763136 | tf_op jit(solution)/shard_map/slopes_and_nodes/pallas_call | solution.py:175
  33.4 4.8 %edges_backward.1 = (bf16[32,512]{1,0:T(8,128)(2,1)S(1)}, bf16[32,512]{1,0:T(8,128)(2,1)S(1)}, bf16[16,512]{1,0:T(8,128)(2,1)S(1)}, bf16[16,512]{1,0:T(8,128)(2,...) custom-call(bf16[32,1024]{1,0:T(8,128)(2,1)S(1)} %collective-permute, ...), custom_call_target="tpu_custom_call" | custom-call | flops 2449473536 | bytes 20463872 | tf_op jit(solution)/shard_map/edges_backward/pallas_call | solution.py:175
  38.2 1.1 %collective-permute-start.18 = (bf16[32,512]{1,0:T(8,128)(2,1)S(1)}, bf16[32,512]{1,0:T(8,128)(2,1)S(1)}, u32[]{:S(2)}, u32[]{:S(2)}) collective-permute-start(bf16[32,512]{1,0:T(8,128)(2,1)S(1)} %get-tuple-element.159), channel_id=1, source_target_pairs={{0,12},{1,13},{2,14},{3,15},{4,8},{5,9},{6,10},{7,11},{8,4},{9,5},... | collective-permute-start | bytes 98312 | tf_op jit(solution)/shard_map/ppermute | solution.py:234
  39.3 1.1 %collective-permute-start.19 = (bf16[32,512]{1,0:T(8,128)(2,1)S(1)}, bf16[32,512]{1,0:T(8,128)(2,1)S(1)}, u32[]{:S(2)}, u32[]{:S(2)}) collective-permute-start(bf16[32,512]{1,0:T(8,128)(2,1)S(1)} %get-tuple-element.162), channel_id=1, source_target_pairs={{0,4},{1,5},{2,6},{3,7},{4,0},{5,1},{6,2},{7,3},{8,12},{9,13},{10,... | collective-permute-start | bytes 98312 | tf_op jit(solution)/shard_map/ppermute | solution.py:234
  40.4 1.6 %collective-permute-start.20 = (bf16[16,512]{1,0:T(8,128)(2,1)S(1)}, bf16[16,512]{1,0:T(8,128)(2,1)S(1)}, u32[]{:S(2)}, u32[]{:S(2)}) collective-permute-start(bf16[16,512]{1,0:T(8,128)(2,1)S(1)} %get-tuple-element.163), channel_id=1, source_target_pairs={{0,15},{1,2},{2,1},{3,4},{4,3},{5,6},{6,5},{7,8},{8,7},{9,10},{10,... | collective-permute-start | bytes 49160 | tf_op jit(solution)/shard_map/ppermute | solution.py:234
  42.5 2.5 %collective-permute-start.22 = (bf16[16,512]{1,0:T(8,128)(2,1)S(1)}, bf16[16,512]{1,0:T(8,128)(2,1)S(1)}, u32[]{:S(2)}, u32[]{:S(2)}) collective-permute-start(bf16[16,512]{1,0:T(8,128)(2,1)S(1)} %get-tuple-element.165), channel_id=1, source_target_pairs={{0,11},{1,6},{2,13},{3,8},{4,15},{5,10},{6,1},{7,12},{8,3},{9,14},... | collective-permute-start | bytes 49160 | tf_op jit(solution)/shard_map/ppermute | solution.py:234
  45.0 1.1 %collective-permute-start.23 = (bf16[16,512]{1,0:T(8,128)(2,1)S(1)}, bf16[16,512]{1,0:T(8,128)(2,1)S(1)}, u32[]{:S(2)}, u32[]{:S(2)}) collective-permute-start(bf16[16,512]{1,0:T(8,128)(2,1)S(1)} %get-tuple-element.166), channel_id=1, source_target_pairs={{0,8},{1,9},{2,10},{3,11},{4,12},{5,13},{6,14},{7,15},{8,0},{9,1},... | collective-permute-start | bytes 49160 | tf_op jit(solution)/shard_map/ppermute | solution.py:234
  46.7 1.1 %collective-permute-start.24 = (bf16[16,512]{1,0:T(8,128)(2,1)S(1)}, bf16[16,512]{1,0:T(8,128)(2,1)S(1)}, u32[]{:S(2)}, u32[]{:S(2)}) collective-permute-start(bf16[16,512]{1,0:T(8,128)(2,1)S(1)} %get-tuple-element.167), channel_id=1, source_target_pairs={{0,1},{1,0},{2,3},{3,2},{4,5},{5,4},{6,7},{7,6},{8,9},{9,8},{10,11... | collective-permute-start | bytes 49160 | tf_op jit(solution)/shard_map/ppermute | solution.py:234
  47.8 1.6 %local_gradients.1 = (f32[256,512]{1,0:T(8,128)S(1)}, f32[64,512]{1,0:T(8,128)}, bf16[256,512]{1,0:T(8,128)(2,1)}) custom-call(bf16[256,512]{1,0:T(8,128)(2,1)S(1)} %copy-done.4, f32[400,512]{1,0:T(8,128)S(1)} %get-tuple-element.150.refs_1_, bf16[256,512]{1,0:T(8,128)(2,1)S(1)} %copy-done.5, bf16[400,512]{1,0:T(8,128)(2,1)S(1)} %get-tuple-element.151.refs_3_, ...), custom_call_target="tpu_custom_call" | custom-call | flops 402653184 | bytes 10272768 | tf_op jit(solution)/shard_map/local_gradients/pallas_call | solution.py:175
  49.9 1.0 %add_returned.1 = f32[256,512]{1,0:T(8,128)} custom-call(bf16[32,512]{1,0:T(8,128)(2,1)S(1)} %collective-permute-done.18.refs_0_, bf16[32,512]{1,0:T(8,128)(2,1)S(1)} %collective-permute-done.19.refs_1_, bf16[16,512]{1,0:T(8,128)(2,1)S(1)} %collective-permute-done.20.refs_2_, bf16[16,512]{1,0:T(8,128)(2,1)S(1)} %collective-permute-done.21.refs_3_, ...), custom_call_target="tpu_custom_call" | custom-call | flops 37748736 | bytes 1392640 | tf_op jit(solution)/shard_map/add_returned/pallas_call | solution.py:175
  (74 shorter events, 4.7 us)
Async XLA Ops:
  2.3 9.6 %collective-permute-start = (bf16[32,1024]{1,0:T(8,128)(2,1)S(1)}, bf16[32,1024]{1,0:T(8,128)(2,1)S(1)}, u32[]{:S(2)}, u32[]{:S(2)}) collective-permute-start(bf16[32,1024]{1,0:T(8,128)(2,1)S(1)} %get-tuple-element.95), channel_id=1, source_target_pairs={{0,12},{1,13},{2,14},{3,15},{4,8},{5,9},{6,10},{7,11},{8,4},{9,5},... | collective-permute-start | bytes 196616 | tf_op jit(solution)/shard_map/ppermute | solution.py:234
  7.4 7.7 %collective-permute-start.1 = (bf16[32,1024]{1,0:T(8,128)(2,1)S(1)}, bf16[32,1024]{1,0:T(8,128)(2,1)S(1)}, u32[]{:S(2)}, u32[]{:S(2)}) collective-permute-start(bf16[32,1024]{1,0:T(8,128)(2,1)S(1)} %get-tuple-element.98), channel_id=1, source_target_pairs={{0,4},{1,5},{2,6},{3,7},{4,0},{5,1},{6,2},{7,3},{8,12},{9,13},{10,... | collective-permute-start | bytes 196616 | tf_op jit(solution)/shard_map/ppermute | solution.py:234
  7.4 6.0 %collective-permute-start.2 = (bf16[16,1024]{1,0:T(8,128)(2,1)S(1)}, bf16[16,1024]{1,0:T(8,128)(2,1)S(1)}, u32[]{:S(2)}, u32[]{:S(2)}) collective-permute-start(bf16[16,1024]{1,0:T(8,128)(2,1)S(1)} %get-tuple-element.99), channel_id=1, source_target_pairs={{0,15},{1,2},{2,1},{3,4},{4,3},{5,6},{6,5},{7,8},{8,7},{9,10},{10,... | collective-permute-start | bytes 98312 | tf_op jit(solution)/shard_map/ppermute | solution.py:234
  8.2 5.6 %collective-permute-start.3 = (bf16[16,1024]{1,0:T(8,128)(2,1)S(1)}, bf16[16,1024]{1,0:T(8,128)(2,1)S(1)}, u32[]{:S(2)}, u32[]{:S(2)}) collective-permute-start(bf16[16,1024]{1,0:T(8,128)(2,1)S(1)} %get-tuple-element.100), channel_id=1, source_target_pairs={{0,3},{1,14},{2,5},{3,0},{4,7},{5,2},{6,9},{7,4},{8,11},{9,6},{10,... | collective-permute-start | bytes 98312 | tf_op jit(solution)/shard_map/ppermute | solution.py:234
  10.7 6.9 %collective-permute-start.4 = (bf16[16,1024]{1,0:T(8,128)(2,1)S(1)}, bf16[16,1024]{1,0:T(8,128)(2,1)S(1)}, u32[]{:S(2)}, u32[]{:S(2)}) collective-permute-start(bf16[16,1024]{1,0:T(8,128)(2,1)S(1)} %get-tuple-element.101), channel_id=1, source_target_pairs={{0,11},{1,6},{2,13},{3,8},{4,15},{5,10},{6,1},{7,12},{8,3},{9,14},... | collective-permute-start | bytes 98312 | tf_op jit(solution)/shard_map/ppermute | solution.py:234
  12.0 5.8 %collective-permute-start.5 = (bf16[16,1024]{1,0:T(8,128)(2,1)S(1)}, bf16[16,1024]{1,0:T(8,128)(2,1)S(1)}, u32[]{:S(2)}, u32[]{:S(2)}) collective-permute-start(bf16[16,1024]{1,0:T(8,128)(2,1)S(1)} %get-tuple-element.102), channel_id=1, source_target_pairs={{0,8},{1,9},{2,10},{3,11},{4,12},{5,13},{6,14},{7,15},{8,0},{9,1},... | collective-permute-start | bytes 98312 | tf_op jit(solution)/shard_map/ppermute | solution.py:234
  13.5 4.3 %collective-permute-start.7 = (bf16[32,1024]{1,0:T(8,128)(2,1)S(1)}, bf16[32,1024]{1,0:T(8,128)(2,1)S(1)}, u32[]{:S(2)}, u32[]{:S(2)}) collective-permute-start(bf16[32,1024]{1,0:T(8,128)(2,1)S(1)} %collective-permute-done.refs_0_), channel_id=1, source_target_pairs={{0,1},{1,0},{2,3},{3,2},{4,5},{5,4},{6,7},{7,6},{8,9},{9,8},{10,11... | collective-permute-start | bytes 196616 | tf_op jit(solution)/shard_map/ppermute | solution.py:234
  13.8 3.9 %collective-permute-start.6 = (bf16[16,1024]{1,0:T(8,128)(2,1)S(1)}, bf16[16,1024]{1,0:T(8,128)(2,1)S(1)}, u32[]{:S(2)}, u32[]{:S(2)}) collective-permute-start(bf16[16,1024]{1,0:T(8,128)(2,1)S(1)} %get-tuple-element.103), channel_id=1, source_target_pairs={{0,1},{1,0},{2,3},{3,2},{4,5},{5,4},{6,7},{7,6},{8,9},{9,8},{10,11... | collective-permute-start | bytes 98312 | tf_op jit(solution)/shard_map/ppermute | solution.py:234
  20.7 6.8 %collective-permute-start.9 = (bf16[32,1024]{1,0:T(8,128)(2,1)S(1)}, bf16[32,1024]{1,0:T(8,128)(2,1)S(1)}, u32[]{:S(2)}, u32[]{:S(2)}) collective-permute-start(bf16[32,1024]{1,0:T(8,128)(2,1)S(1)} %get-tuple-element.116), channel_id=1, source_target_pairs={{0,12},{1,13},{2,14},{3,15},{4,8},{5,9},{6,10},{7,11},{8,4},{9,5},... | collective-permute-start | bytes 196616 | tf_op jit(solution)/shard_map/ppermute | solution.py:234
  22.4 7.1 %collective-permute-start.10 = (bf16[32,1024]{1,0:T(8,128)(2,1)S(1)}, bf16[32,1024]{1,0:T(8,128)(2,1)S(1)}, u32[]{:S(2)}, u32[]{:S(2)}) collective-permute-start(bf16[32,1024]{1,0:T(8,128)(2,1)S(1)} %get-tuple-element.119), channel_id=1, source_target_pairs={{0,4},{1,5},{2,6},{3,7},{4,0},{5,1},{6,2},{7,3},{8,12},{9,13},{10,... | collective-permute-start | bytes 196616 | tf_op jit(solution)/shard_map/ppermute | solution.py:234
  22.4 6.0 %collective-permute-start.11 = (bf16[16,1024]{1,0:T(8,128)(2,1)S(1)}, bf16[16,1024]{1,0:T(8,128)(2,1)S(1)}, u32[]{:S(2)}, u32[]{:S(2)}) collective-permute-start(bf16[16,1024]{1,0:T(8,128)(2,1)S(1)} %get-tuple-element.120), channel_id=1, source_target_pairs={{0,15},{1,2},{2,1},{3,4},{4,3},{5,6},{6,5},{7,8},{8,7},{9,10},{10,... | collective-permute-start | bytes 98312 | tf_op jit(solution)/shard_map/ppermute | solution.py:234
  23.8 4.7 %collective-permute-start.12 = (bf16[16,1024]{1,0:T(8,128)(2,1)S(1)}, bf16[16,1024]{1,0:T(8,128)(2,1)S(1)}, u32[]{:S(2)}, u32[]{:S(2)}) collective-permute-start(bf16[16,1024]{1,0:T(8,128)(2,1)S(1)} %get-tuple-element.121), channel_id=1, source_target_pairs={{0,3},{1,14},{2,5},{3,0},{4,7},{5,2},{6,9},{7,4},{8,11},{9,6},{10,... | collective-permute-start | bytes 98312 | tf_op jit(solution)/shard_map/ppermute | solution.py:234
  25.6 7.8 %collective-permute-start.13 = (bf16[16,1024]{1,0:T(8,128)(2,1)S(1)}, bf16[16,1024]{1,0:T(8,128)(2,1)S(1)}, u32[]{:S(2)}, u32[]{:S(2)}) collective-permute-start(bf16[16,1024]{1,0:T(8,128)(2,1)S(1)} %get-tuple-element.122), channel_id=1, source_target_pairs={{0,11},{1,6},{2,13},{3,8},{4,15},{5,10},{6,1},{7,12},{8,3},{9,14},... | collective-permute-start | bytes 98312 | tf_op jit(solution)/shard_map/ppermute | solution.py:234
  27.5 5.9 %collective-permute-start.14 = (bf16[16,1024]{1,0:T(8,128)(2,1)S(1)}, bf16[16,1024]{1,0:T(8,128)(2,1)S(1)}, u32[]{:S(2)}, u32[]{:S(2)}) collective-permute-start(bf16[16,1024]{1,0:T(8,128)(2,1)S(1)} %get-tuple-element.123), channel_id=1, source_target_pairs={{0,8},{1,9},{2,10},{3,11},{4,12},{5,13},{6,14},{7,15},{8,0},{9,1},... | collective-permute-start | bytes 98312 | tf_op jit(solution)/shard_map/ppermute | solution.py:234
  28.5 5.0 %collective-permute-start.16 = (bf16[32,1024]{1,0:T(8,128)(2,1)S(1)}, bf16[32,1024]{1,0:T(8,128)(2,1)S(1)}, u32[]{:S(2)}, u32[]{:S(2)}) collective-permute-start(bf16[32,1024]{1,0:T(8,128)(2,1)S(1)} %collective-permute-done.9.refs_0_), channel_id=1, source_target_pairs={{0,1},{1,0},{2,3},{3,2},{4,5},{5,4},{6,7},{7,6},{8,9},{9,8},{10,11... | collective-permute-start | bytes 196616 | tf_op jit(solution)/shard_map/ppermute | solution.py:234
  28.5 4.9 %collective-permute-start.15 = (bf16[16,1024]{1,0:T(8,128)(2,1)S(1)}, bf16[16,1024]{1,0:T(8,128)(2,1)S(1)}, u32[]{:S(2)}, u32[]{:S(2)}) collective-permute-start(bf16[16,1024]{1,0:T(8,128)(2,1)S(1)} %get-tuple-element.124), channel_id=1, source_target_pairs={{0,1},{1,0},{2,3},{3,2},{4,5},{5,4},{6,7},{7,6},{8,9},{9,8},{10,11... | collective-permute-start | bytes 98312 | tf_op jit(solution)/shard_map/ppermute | solution.py:234
  29.5 3.9 %collective-permute-start.17 = (bf16[32,1024]{1,0:T(8,128)(2,1)S(1)}, bf16[32,1024]{1,0:T(8,128)(2,1)S(1)}, u32[]{:S(2)}, u32[]{:S(2)}) collective-permute-start(bf16[32,1024]{1,0:T(8,128)(2,1)S(1)} %collective-permute-done.10.refs_1_), channel_id=1, source_target_pairs={{0,1},{1,0},{2,3},{3,2},{4,5},{5,4},{6,7},{7,6},{8,9},{9,8},{10,11... | collective-permute-start | bytes 196616 | tf_op jit(solution)/shard_map/ppermute | solution.py:234
  38.2 6.7 %collective-permute-start.18 = (bf16[32,512]{1,0:T(8,128)(2,1)S(1)}, bf16[32,512]{1,0:T(8,128)(2,1)S(1)}, u32[]{:S(2)}, u32[]{:S(2)}) collective-permute-start(bf16[32,512]{1,0:T(8,128)(2,1)S(1)} %get-tuple-element.159), channel_id=1, source_target_pairs={{0,12},{1,13},{2,14},{3,15},{4,8},{5,9},{6,10},{7,11},{8,4},{9,5},... | collective-permute-start | bytes 98312 | tf_op jit(solution)/shard_map/ppermute | solution.py:234
  39.3 8.5 %collective-permute-start.19 = (bf16[32,512]{1,0:T(8,128)(2,1)S(1)}, bf16[32,512]{1,0:T(8,128)(2,1)S(1)}, u32[]{:S(2)}, u32[]{:S(2)}) collective-permute-start(bf16[32,512]{1,0:T(8,128)(2,1)S(1)} %get-tuple-element.162), channel_id=1, source_target_pairs={{0,4},{1,5},{2,6},{3,7},{4,0},{5,1},{6,2},{7,3},{8,12},{9,13},{10,... | collective-permute-start | bytes 98312 | tf_op jit(solution)/shard_map/ppermute | solution.py:234
  40.4 5.9 %collective-permute-start.20 = (bf16[16,512]{1,0:T(8,128)(2,1)S(1)}, bf16[16,512]{1,0:T(8,128)(2,1)S(1)}, u32[]{:S(2)}, u32[]{:S(2)}) collective-permute-start(bf16[16,512]{1,0:T(8,128)(2,1)S(1)} %get-tuple-element.163), channel_id=1, source_target_pairs={{0,15},{1,2},{2,1},{3,4},{4,3},{5,6},{6,5},{7,8},{8,7},{9,10},{10,... | collective-permute-start | bytes 49160 | tf_op jit(solution)/shard_map/ppermute | solution.py:234
  42.0 4.7 %collective-permute-start.21 = (bf16[16,512]{1,0:T(8,128)(2,1)S(1)}, bf16[16,512]{1,0:T(8,128)(2,1)S(1)}, u32[]{:S(2)}, u32[]{:S(2)}) collective-permute-start(bf16[16,512]{1,0:T(8,128)(2,1)S(1)} %get-tuple-element.164), channel_id=1, source_target_pairs={{0,3},{1,14},{2,5},{3,0},{4,7},{5,2},{6,9},{7,4},{8,11},{9,6},{10,... | collective-permute-start | bytes 49160 | tf_op jit(solution)/shard_map/ppermute | solution.py:234
  42.5 6.8 %collective-permute-start.22 = (bf16[16,512]{1,0:T(8,128)(2,1)S(1)}, bf16[16,512]{1,0:T(8,128)(2,1)S(1)}, u32[]{:S(2)}, u32[]{:S(2)}) collective-permute-start(bf16[16,512]{1,0:T(8,128)(2,1)S(1)} %get-tuple-element.165), channel_id=1, source_target_pairs={{0,11},{1,6},{2,13},{3,8},{4,15},{5,10},{6,1},{7,12},{8,3},{9,14},... | collective-permute-start | bytes 49160 | tf_op jit(solution)/shard_map/ppermute | solution.py:234
  45.0 5.0 %collective-permute-start.23 = (bf16[16,512]{1,0:T(8,128)(2,1)S(1)}, bf16[16,512]{1,0:T(8,128)(2,1)S(1)}, u32[]{:S(2)}, u32[]{:S(2)}) collective-permute-start(bf16[16,512]{1,0:T(8,128)(2,1)S(1)} %get-tuple-element.166), channel_id=1, source_target_pairs={{0,8},{1,9},{2,10},{3,11},{4,12},{5,13},{6,14},{7,15},{8,0},{9,1},... | collective-permute-start | bytes 49160 | tf_op jit(solution)/shard_map/ppermute | solution.py:234
  46.2 3.7 %collective-permute-start.25 = (bf16[32,512]{1,0:T(8,128)(2,1)S(1)}, bf16[32,512]{1,0:T(8,128)(2,1)S(1)}, u32[]{:S(2)}, u32[]{:S(2)}) collective-permute-start(bf16[32,512]{1,0:T(8,128)(2,1)S(1)} %collective-permute-done.18.refs_0_), channel_id=1, source_target_pairs={{0,1},{1,0},{2,3},{3,2},{4,5},{5,4},{6,7},{7,6},{8,9},{9,8},{10,11... | collective-permute-start | bytes 98312 | tf_op jit(solution)/shard_map/ppermute | solution.py:234
  (21 other events, 237.8 us)

commit v12 on v11

--- a/solution.py
+++ b/solution.py
@@ -590,16 +590,10 @@
             grid_first_ref,
             grid_second_ref,
             cot_ref,
-            mesh_first_ref,
             mesh_second_ref,
-            dec_first_ref,
             dec_second_ref,
-            enc_second_ref,
             mesh_ref,
             mesh_cot_ref,
-            enc_normed_ref,
-            enc_scale_ref,
-            enc_pre_ref,
             dec_normed_ref,
             dec_scale_ref,
             dec_pre_ref,
@@ -611,14 +605,10 @@
             cot_turned_ref,
             grid_wide_ref,
             grid_back_ref,
-            mesh_in_ref,
-            mesh_back_ref,
             mesh_out_ref,
             mesh_cot_turned_ref,
             mesh_slope_ref,
             mesh_turned_ref,
-            enc_gain_ref,
-            enc_turned_ref,
             dec_gain_ref,
             dec_turned_ref,
         ) = refs
@@ -633,21 +623,9 @@
         cot_turned_ref[...] = mm_t(cot_rows_ref[...], second)
         grid_back_ref[low, :] = centred(grid_first_ref[high, :], 0).astype(BF16)
         grid_back_ref[high, :] = mm(dec_second_ref[...], grid_back_ref[low, :]).astype(BF16)
-        mesh_back_ref[low, :] = centred(mesh_first_ref[high, :], 0).astype(BF16)
-        mesh_back_ref[high, :] = mm(enc_second_ref[...], mesh_back_ref[low, :]).astype(BF16)
-        mesh_in_ref[low, :] = dec_first_ref[high, :]
-        mesh_in_ref[high, :] = mm(mesh_wide_ref[:, low], dec_first_ref[high, :]).astype(BF16)
         mesh_cot_turned_ref[...] = mm_t(mesh_cot_ref[...], mesh_wide_ref[:, low])
         mesh_turned_ref[...] = mm_t(mesh_normed_ref[...].astype(BF16), mesh_second_ref[...])
         mesh_slope_ref[...] = silu_and_slope(mesh_pre_ref[...])[1]
-        write_slopes(
-            enc_pre_ref,
-            enc_normed_ref,
-            enc_scale_ref,
-            enc_second_ref,
-            enc_gain_ref,
-            enc_turned_ref,
-        )
         write_slopes(
             dec_pre_ref,
             dec_normed_ref,
@@ -663,14 +641,10 @@
         cot_turned,
         grid_wide,
         grid_back,
-        mesh_in,
-        mesh_back,
         mesh_out,
         mesh_cot_turned,
         mesh_slope,
         mesh_turned,
-        enc_gain,
-        enc_turned,
         dec_gain,
         dec_turned,
     ) = call(
@@ -682,16 +656,10 @@
             grid_first,
             grid_second,
             grid_cot,
-            mesh_first,
             mesh_second,
-            dec_first,
             dec_second,
-            enc_second,
             mesh_nodes,
             mesh_cot,
-            enc_normed,
-            enc_scale,
-            enc_pre,
             dec_normed,
             dec_scale,
             dec_pre,
@@ -705,14 +673,10 @@
             ((spots, feat), F32),
             ((feat, 2 * feat), BF16),
             ((2 * feat, feat), BF16),
-            ((2 * feat, feat), BF16),
-            ((2 * feat, feat), BF16),
             ((mesh_count, feat), BF16),
             ((mesh_count, feat), F32),
             ((mesh_count, feat), F32),
             ((mesh_count, feat), F32),
-            ((enc_count, feat), BF16),
-            ((enc_count, feat), BF16),
             ((dec_count, feat), BF16),
             ((dec_count, feat), BF16),
         ],
@@ -736,13 +700,14 @@
             grid_first_ref,
             grid_wide_ref,
             grid_back_ref,
-            mesh_in_ref,
-            mesh_back_ref,
+            mesh_first_ref,
+            mesh_wide_ref,
             enc_first_ref,
+            enc_second_ref,
             dec_first_ref,
             enc_normed_ref,
-            enc_gain_ref,
-            enc_turned_ref,
+            enc_scale_ref,
+            enc_pre_ref,
             dec_normed_ref,
             dec_gain_ref,
             dec_turned_ref,
@@ -750,23 +715,24 @@
             mesh_scale_ref,
             mesh_slope_ref,
             mesh_turned_ref,
-        ) = refs[:28]
-        refs = refs[28:]
+        ) = refs[:29]
+        refs = refs[29:]
         out_refs, refs = refs[:sent_count], refs[sent_count:]
         (
             grid_normed_ref,
             grid_gpre_ref,
-            gpe_ref,
-            gpd_ref,
+            dec_gpre_ref,
+            enc_gpre_ref,
             mesh_gin_ref,
             mesh_gpre_ref,
-            mesh_pool_ref,
             agg_ref,
             grid_act_ref,
             grid_slope_ref,
             spot_grad_ref,
-            dec_gpre_ref,
-            enc_gpre_ref,
+            mesh_in_ref,
+            mesh_back_ref,
+            enc_gain_ref,
+            enc_turned_ref,
         ) = refs
         agg_ref[:grid_count, :] = (
             spot_ref[:grid_count, :] + mm(select_t_ref[:, :slots], by_row(returned_refs, low))
@@ -775,11 +741,15 @@
             spot_ref[grid_count:, :] + by_slot(returned_refs, high).astype(F32)
         ).astype(BF16)
         pre = grid_part_ref[...] + mm(agg_ref[...], grid_first_ref[high, :])
+        mesh_in_ref[low, :] = dec_first_ref[high, :]
+        mesh_in_ref[high, :] = mm(mesh_wide_ref[:, low], dec_first_ref[high, :]).astype(BF16)
         for rows in row_chunks(spots):
             act, slope = silu_and_slope(pre[rows, :])
             grid_act_ref[rows, :] = act.astype(BF16)
             grid_slope_ref[rows, :] = slope
         both = mm(grid_act_ref[...], grid_wide_ref[...])
+        mesh_back_ref[low, :] = centred(mesh_first_ref[high, :], 0).astype(BF16)
+        mesh_back_ref[high, :] = mm(enc_second_ref[...], mesh_back_ref[low, :]).astype(BF16)
         for rows in row_chunks(spots):
             part = both[rows, low]
             scale_inv = scale_rows(part)
@@ -790,6 +760,14 @@
             grid_gpre_ref[rows, :] = (raw * grid_slope_ref[rows, :]).astype(BF16)
         spot_grad_ref[:spots, :] = mm_t(grid_gpre_ref[...], grid_back_ref[...]).astype(BF16)
         spot_grad_ref[spots:, :] = jnp.zeros((total - spots, 2 * feat), BF16)
+        write_slopes(
+            enc_pre_ref,
+            enc_normed_ref,
+            enc_scale_ref,
+            enc_second_ref,
+            enc_gain_ref,
+            enc_turned_ref,
+        )
         edge_back(
             mm(dec_pick_ref[...], spot_grad_ref[...]),
             dec_normed_ref,
@@ -805,9 +783,8 @@
         raw = mesh_cot_turned_ref[...] + both[:, high] - mean * mesh_turned_ref[...]
         mesh_gpre_ref[...] = (mesh_scale_ref[...] * raw * mesh_slope_ref[...]).astype(BF16)
         mesh_gagg = mm_t(mesh_gpre_ref[...], mesh_back_ref[...]).astype(BF16)
-        pooled = mm(dec_pool_ref[:spots, :], dec_gpre_ref[...]).astype(BF16)
-        gpd_ref[...] = pooled[:grid_count, :]
-        slot_back = mm_t(pooled[grid_count:, :], dec_first_ref[low, :])
+        pooled = mm(dec_pool_ref[grid_count:spots, :], dec_gpre_ref[...]).astype(BF16)
+        slot_back = mm_t(pooled, dec_first_ref[low, :])
         edge_back(
             mm(enc_pick_ref[:, mesh_rows], mesh_gagg),
             enc_normed_ref,
@@ -815,12 +792,8 @@
             enc_turned_ref,
             enc_gpre_ref,
         )
-        pooled = mm(enc_pool_ref[...], enc_gpre_ref[...]).astype(BF16)
-        gpe_ref[...] = pooled[:grid_count, :]
-        mesh_pool_ref[...] = pooled[mesh_rows, :]
-        slot_back = (
-            slot_back + mm_t(pooled[grid_count:spots, :], enc_first_ref[low, :])
-        ).astype(BF16)
+        pooled = mm(enc_pool_ref[grid_count:spots, :], enc_gpre_ref[...]).astype(BF16)
+        slot_back = (slot_back + mm_t(pooled, enc_first_ref[low, :])).astype(BF16)
         send(out_refs, lambda j: slot_back[reverse[j] * width : (reverse[j] + 1) * width, :])
 
     results = call(
@@ -842,13 +815,14 @@
             grid_first,
             grid_wide,
             grid_back,
-            mesh_in,
-            mesh_back,
+            mesh_first,
+            mesh_wide,
             enc_first,
+            enc_second,
             dec_first,
             enc_normed,
-            enc_gain,
-            enc_turned,
+            enc_scale,
+            enc_pre,
             dec_normed,
             dec_gain,
             dec_turned,
@@ -861,10 +835,9 @@
         + [
             ((spots, feat), F32),
             ((spots, feat), BF16),
-            ((grid_count, feat), BF16),
-            ((grid_count, feat), BF16),
+            ((dec_count, feat), BF16),
+            ((enc_count, feat), BF16),
             ((mesh_count, feat), F32),
-            ((mesh_count, feat), BF16),
             ((mesh_count, feat), BF16),
         ],
         scratch=[
@@ -872,13 +845,15 @@
             ((spots, feat), BF16),
             ((spots, feat), F32),
             ((total, 2 * feat), BF16),
-            ((dec_count, feat), BF16),
+            ((2 * feat, feat), BF16),
+            ((2 * feat, feat), BF16),
+            ((enc_count, feat), BF16),
             ((enc_count, feat), BF16),
         ],
         flops=2 * feat * feat * (4 * spots + 3 * dec_count + 2 * enc_count),
     )
     outgoing, results = results[:sent_count], results[sent_count:]
-    grid_normed, grid_gpre, gpe, gpd, mesh_gin, mesh_gpre, mesh_pool = results
+    grid_normed, grid_gpre, dec_gpre, enc_gpre, mesh_gin, mesh_gpre = results
     final = exchange(outgoing)
 
     def tail(
@@ -886,11 +861,12 @@
         grid_normed_ref,
         cot_ref,
         grid_gpre_ref,
-        gpe_ref,
-        gpd_ref,
+        enc_pool_ref,
+        enc_gpre_ref,
+        dec_pool_ref,
+        dec_gpre_ref,
         mesh_gin_ref,
         mesh_gpre_ref,
-        mesh_pool_ref,
         grid_wn_ref,
         enc_wg_ref,
         dec_wg_ref,
@@ -903,16 +879,18 @@
         grid_out_ref[...] = (
             nodes_ref[...].astype(F32) + grid_normed_ref[:grid_count, :]
         ).astype(BF16)
+        enc_sums = mm(enc_pool_ref[...], enc_gpre_ref[...]).astype(BF16)
+        dec_sums = mm(dec_pool_ref[:grid_count, :], dec_gpre_ref[...]).astype(BF16)
         base_ref[...] = (
             cot_ref[...].astype(F32)
             + mm_t(grid_gpre_ref[:grid_count, :], grid_wn_ref[low, :])
-            + mm_t(gpe_ref[...], enc_wg_ref[low, :])
-            + mm_t(gpd_ref[...], dec_wg_ref[low, :])
+            + mm_t(enc_sums[:grid_count, :], enc_wg_ref[low, :])
+            + mm_t(dec_sums, dec_wg_ref[low, :])
         )
         grad_mesh_ref[...] = (
             mesh_gin_ref[...]
             + mm_t(mesh_gpre_ref[...], mesh_wn_ref[low, :])
-            + mm_t(mesh_pool_ref[...], enc_wm_ref[high, :])
+            + mm_t(enc_sums[mesh_rows, :], enc_wm_ref[high, :])
         )
 
     base, grad_mesh, grid_out = call(
@@ -923,11 +901,12 @@
             grid_normed,
             grid_cot,
             grid_gpre,
-            gpe,
-            gpd,
+            enc_pool,
+            enc_gpre,
+            dec_pool,
+            dec_gpre,
             mesh_gin,
             mesh_gpre,
-            mesh_pool,
             grid_first,
             enc_first,
             dec_first,

time: 51.1 us -> 50.8 us (level)
  transfers between devices with their start and end apart: 27 -> 27, of which waited for: 6 -> 6; matrix products, arithmetic and copies ran while one was open for 0% -> 0% of each run, Pallas kernels for 15% -> 14%
where the time goes in v12:
time: 50.8 us; the launch traced here: 50.6 us
  starting transfers between devices  28.9 us (57%)
  Pallas kernels  18 us (35%)
  waiting for transfers between devices  2.62 us (5%)
  between operations  1 us (2%)
    ppermute x27, starting transfers between devices, permute(): return lax.ppermute(part, 'tile', pairs)  28.9 us
    pallas_call x8, Pallas kernels, call(): pl.pallas_call(kernel, name=name, in_specs=specs, out_specs=[pl.BlockSpec...  18 us
    ppermute x27, waiting for transfers between devices, permute(): return lax.ppermute(part, 'tile', pairs)  2.62 us
  transfers between devices with their start and end apart: 27, of which 6 were waited for; matrix products, arithmetic and copies ran while one was open for 0% of the time, Pallas kernels for 14%

profile of v12, /device:TPU:0, one launch (start us, length us, event | category | flops | bytes accessed | tf_op | source)
XLA Modules:
  0.0 50.6 jit_solution(10444175372957453960)
XLA Ops:
  0.6 1.4 %pack_rows.1 = (bf16[256,256]{1,0:T(8,128)(2,1)S(1)}, bf16[32,1024]{1,0:T(8,128)(2,1)S(1)}, bf16[32,1024]{1,0:T(8,128)(2,1)S(1)}, bf16[16,1024]{1,0:T(8,128)(2,1...) custom-call(s32[9,16]{1,0:T(8,128)} %refs_0_.2, ...), custom_call_target="tpu_custom_call" | custom-call | flops 75497472 | bytes 950884 | tf_op jit(solution)/shard_map/pack_rows/pallas_call | solution.py:175
  2.3 5.1 %collective-permute-start = (bf16[32,1024]{1,0:T(8,128)(2,1)S(1)}, bf16[32,1024]{1,0:T(8,128)(2,1)S(1)}, u32[]{:S(2)}, u32[]{:S(2)}) collective-permute-start(bf16[32,1024]{1,0:T(8,128)(2,1)S(1)} %get-tuple-element.90), channel_id=1, source_target_pairs={{0,12},{1,13},{2,14},{3,15},{4,8},{5,9},{6,10},{7,11},{8,4},{9,5},... | collective-permute-start | bytes 196616 | tf_op jit(solution)/shard_map/ppermute | solution.py:234
  7.4 0.7 %collective-permute-start.2 = (bf16[16,1024]{1,0:T(8,128)(2,1)S(1)}, bf16[16,1024]{1,0:T(8,128)(2,1)S(1)}, u32[]{:S(2)}, u32[]{:S(2)}) collective-permute-start(bf16[16,1024]{1,0:T(8,128)(2,1)S(1)} %get-tuple-element.94), channel_id=1, source_target_pairs={{0,15},{1,2},{2,1},{3,4},{4,3},{5,6},{6,5},{7,8},{8,7},{9,10},{10,... | collective-permute-start | bytes 98312 | tf_op jit(solution)/shard_map/ppermute | solution.py:234
  8.2 2.5 %collective-permute-start.3 = (bf16[16,1024]{1,0:T(8,128)(2,1)S(1)}, bf16[16,1024]{1,0:T(8,128)(2,1)S(1)}, u32[]{:S(2)}, u32[]{:S(2)}) collective-permute-start(bf16[16,1024]{1,0:T(8,128)(2,1)S(1)} %get-tuple-element.95), channel_id=1, source_target_pairs={{0,3},{1,14},{2,5},{3,0},{4,7},{5,2},{6,9},{7,4},{8,11},{9,6},{10,... | collective-permute-start | bytes 98312 | tf_op jit(solution)/shard_map/ppermute | solution.py:234
  10.7 1.3 %collective-permute-start.4 = (bf16[16,1024]{1,0:T(8,128)(2,1)S(1)}, bf16[16,1024]{1,0:T(8,128)(2,1)S(1)}, u32[]{:S(2)}, u32[]{:S(2)}) collective-permute-start(bf16[16,1024]{1,0:T(8,128)(2,1)S(1)} %get-tuple-element.96), channel_id=1, source_target_pairs={{0,11},{1,6},{2,13},{3,8},{4,15},{5,10},{6,1},{7,12},{8,3},{9,14},... | collective-permute-start | bytes 98312 | tf_op jit(solution)/shard_map/ppermute | solution.py:234
  12.0 1.1 %collective-permute-start.5 = (bf16[16,1024]{1,0:T(8,128)(2,1)S(1)}, bf16[16,1024]{1,0:T(8,128)(2,1)S(1)}, u32[]{:S(2)}, u32[]{:S(2)}) collective-permute-start(bf16[16,1024]{1,0:T(8,128)(2,1)S(1)} %get-tuple-element.97), channel_id=1, source_target_pairs={{0,8},{1,9},{2,10},{3,11},{4,12},{5,13},{6,14},{7,15},{8,0},{9,1},... | collective-permute-start | bytes 98312 | tf_op jit(solution)/shard_map/ppermute | solution.py:234
  13.8 1.3 %collective-permute-start.7 = (bf16[32,1024]{1,0:T(8,128)(2,1)S(1)}, bf16[32,1024]{1,0:T(8,128)(2,1)S(1)}, u32[]{:S(2)}, u32[]{:S(2)}) collective-permute-start(bf16[32,1024]{1,0:T(8,128)(2,1)S(1)} %collective-permute-done.refs_0_), channel_id=1, source_target_pairs={{0,1},{1,0},{2,3},{3,2},{4,5},{5,4},{6,7},{7,6},{8,9},{9,8},{10,11... | collective-permute-start | bytes 196616 | tf_op jit(solution)/shard_map/ppermute | solution.py:234
  15.3 2.3 %local_products.1 = (f32[384,512]{1,0:T(8,128)S(1)}, f32[768,512]{1,0:T(8,128)S(1)}, f32[64,512]{1,0:T(8,128)S(1)}, bf16[384,512]{1,0:T(8,128)(2,1)S(1)}, bf16[5...) custom-call(bf16[256,256]{1,0:T(8,128)(2,1)S(1)} %get-tuple-element., ...), custom_call_target="tpu_custom_call" | custom-call | flops 1275068416 | bytes 14713856 | tf_op jit(solution)/shard_map/local_products/pallas_call | solution.py:175
  17.8 2.8 %edges_forward.1 = (bf16[32,1024]{1,0:T(8,128)(2,1)S(1)}, bf16[32,1024]{1,0:T(8,128)(2,1)S(1)}, bf16[16,1024]{1,0:T(8,128)(2,1)S(1)}, bf16[16,1024]{1,0:T(8,128)...) custom-call(bf16[32,1024]{1,0:T(8,128)(2,1)S(1)} %collective-permute, ...), custom_call_target="tpu_custom_call" | custom-call | flops 1207959552 | bytes 16839424 | tf_op jit(solution)/shard_map/edges_forward/pallas_call | solution.py:175
  20.7 1.7 %collective-permute-start.9 = (bf16[32,1024]{1,0:T(8,128)(2,1)S(1)}, bf16[32,1024]{1,0:T(8,128)(2,1)S(1)}, u32[]{:S(2)}, u32[]{:S(2)}) collective-permute-start(bf16[32,1024]{1,0:T(8,128)(2,1)S(1)} %get-tuple-element.111), channel_id=1, source_target_pairs={{0,12},{1,13},{2,14},{3,15},{4,8},{5,9},{6,10},{7,11},{8,4},{9,5},... | collective-permute-start | bytes 196616 | tf_op jit(solution)/shard_map/ppermute | solution.py:234
  22.4 1.3 %collective-permute-start.11 = (bf16[16,1024]{1,0:T(8,128)(2,1)S(1)}, bf16[16,1024]{1,0:T(8,128)(2,1)S(1)}, u32[]{:S(2)}, u32[]{:S(2)}) collective-permute-start(bf16[16,1024]{1,0:T(8,128)(2,1)S(1)} %get-tuple-element.115), channel_id=1, source_target_pairs={{0,15},{1,2},{2,1},{3,4},{4,3},{5,6},{6,5},{7,8},{8,7},{9,10},{10,... | collective-permute-start | bytes 98312 | tf_op jit(solution)/shard_map/ppermute | solution.py:234
  23.8 1.9 %collective-permute-start.12 = (bf16[16,1024]{1,0:T(8,128)(2,1)S(1)}, bf16[16,1024]{1,0:T(8,128)(2,1)S(1)}, u32[]{:S(2)}, u32[]{:S(2)}) collective-permute-start(bf16[16,1024]{1,0:T(8,128)(2,1)S(1)} %get-tuple-element.116), channel_id=1, source_target_pairs={{0,3},{1,14},{2,5},{3,0},{4,7},{5,2},{6,9},{7,4},{8,11},{9,6},{10,... | collective-permute-start | bytes 98312 | tf_op jit(solution)/shard_map/ppermute | solution.py:234
  26.3 1.1 %collective-permute-done.9.refs_0_ = bf16[32,1024]{1,0:T(8,128)(2,1)S(1)} collective-permute-done((bf16[32,1024]{1,0:T(8,128)(2,1)S(1)}, bf16[32,1024]{1,0:T(8,128)(2,1)S(1)}, u32[]{:S(2)}, u32[]{:S(2)}) %collective-permute-start.9) | collective-permute-done | bytes 65568 | tf_op jit(solution)/shard_map/ppermute | solution.py:234
  28.5 1.0 %collective-permute-start.16 = (bf16[32,1024]{1,0:T(8,128)(2,1)S(1)}, bf16[32,1024]{1,0:T(8,128)(2,1)S(1)}, u32[]{:S(2)}, u32[]{:S(2)}) collective-permute-start(bf16[32,1024]{1,0:T(8,128)(2,1)S(1)} %collective-permute-done.9.refs_0_), channel_id=1, source_target_pairs={{0,1},{1,0},{2,3},{3,2},{4,5},{5,4},{6,7},{7,6},{8,9},{9,8},{10,11... | collective-permute-start | bytes 196616 | tf_op jit(solution)/shard_map/ppermute | solution.py:234
  29.5 3.0 %slopes_and_nodes.1 = (f32[400,512]{1,0:T(8,128)S(1)}, bf16[400,512]{1,0:T(8,128)(2,1)S(1)}, f32[400,512]{1,0:T(8,128)S(1)}, bf16[512,1024]{1,0:T(8,128)(2,1)S(1...) custom-call(bf16[32,1024]{1,0:T(8,128)(2,1)S(1)} %collective-permute, ...), custom_call_target="tpu_custom_call" | custom-call | flops 1677721600 | bytes 13552640 | tf_op jit(solution)/shard_map/slopes_and_nodes/pallas_call | solution.py:175
  32.6 5.3 %edges_backward.1 = (bf16[32,512]{1,0:T(8,128)(2,1)S(1)}, bf16[32,512]{1,0:T(8,128)(2,1)S(1)}, bf16[16,512]{1,0:T(8,128)(2,1)S(1)}, bf16[16,512]{1,0:T(8,128)(2,...) custom-call(bf16[32,1024]{1,0:T(8,128)(2,1)S(1)} %collective-permute, ...), custom_call_target="tpu_custom_call" | custom-call | flops 2449473536 | bytes 21579520 | tf_op jit(solution)/shard_map/edges_backward/pallas_call | solution.py:175
  37.9 1.9 %collective-permute-start.18 = (bf16[32,512]{1,0:T(8,128)(2,1)S(1)}, bf16[32,512]{1,0:T(8,128)(2,1)S(1)}, u32[]{:S(2)}, u32[]{:S(2)}) collective-permute-start(bf16[32,512]{1,0:T(8,128)(2,1)S(1)} %get-tuple-element.149), channel_id=1, source_target_pairs={{0,12},{1,13},{2,14},{3,15},{4,8},{5,9},{6,10},{7,11},{8,4},{9,5},... | collective-permute-start | bytes 98312 | tf_op jit(solution)/shard_map/ppermute | solution.py:234
  40.0 1.6 %collective-permute-start.20 = (bf16[16,512]{1,0:T(8,128)(2,1)S(1)}, bf16[16,512]{1,0:T(8,128)(2,1)S(1)}, u32[]{:S(2)}, u32[]{:S(2)}) collective-permute-start(bf16[16,512]{1,0:T(8,128)(2,1)S(1)} %get-tuple-element.153), channel_id=1, source_target_pairs={{0,15},{1,2},{2,1},{3,4},{4,3},{5,6},{6,5},{7,8},{8,7},{9,10},{10,... | collective-permute-start | bytes 49160 | tf_op jit(solution)/shard_map/ppermute | solution.py:234
  41.6 1.4 %collective-permute-start.21 = (bf16[16,512]{1,0:T(8,128)(2,1)S(1)}, bf16[16,512]{1,0:T(8,128)(2,1)S(1)}, u32[]{:S(2)}, u32[]{:S(2)}) collective-permute-start(bf16[16,512]{1,0:T(8,128)(2,1)S(1)} %get-tuple-element.154), channel_id=1, source_target_pairs={{0,3},{1,14},{2,5},{3,0},{4,7},{5,2},{6,9},{7,4},{8,11},{9,6},{10,... | collective-permute-start | bytes 49160 | tf_op jit(solution)/shard_map/ppermute | solution.py:234
  43.0 1.6 %collective-permute-start.22 = (bf16[16,512]{1,0:T(8,128)(2,1)S(1)}, bf16[16,512]{1,0:T(8,128)(2,1)S(1)}, u32[]{:S(2)}, u32[]{:S(2)}) collective-permute-start(bf16[16,512]{1,0:T(8,128)(2,1)S(1)} %get-tuple-element.155), channel_id=1, source_target_pairs={{0,11},{1,6},{2,13},{3,8},{4,15},{5,10},{6,1},{7,12},{8,3},{9,14},... | collective-permute-start | bytes 49160 | tf_op jit(solution)/shard_map/ppermute | solution.py:234
  44.6 1.1 %collective-permute-start.23 = (bf16[16,512]{1,0:T(8,128)(2,1)S(1)}, bf16[16,512]{1,0:T(8,128)(2,1)S(1)}, u32[]{:S(2)}, u32[]{:S(2)}) collective-permute-start(bf16[16,512]{1,0:T(8,128)(2,1)S(1)} %get-tuple-element.156), channel_id=1, source_target_pairs={{0,8},{1,9},{2,10},{3,11},{4,12},{5,13},{6,14},{7,15},{8,0},{9,1},... | collective-permute-start | bytes 49160 | tf_op jit(solution)/shard_map/ppermute | solution.py:234
  46.3 1.1 %collective-permute-start.25 = (bf16[32,512]{1,0:T(8,128)(2,1)S(1)}, bf16[32,512]{1,0:T(8,128)(2,1)S(1)}, u32[]{:S(2)}, u32[]{:S(2)}) collective-permute-start(bf16[32,512]{1,0:T(8,128)(2,1)S(1)} %collective-permute-done.18.refs_0_), channel_id=1, source_target_pairs={{0,1},{1,0},{2,3},{3,2},{4,5},{5,4},{6,7},{7,6},{8,9},{9,8},{10,11... | collective-permute-start | bytes 98312 | tf_op jit(solution)/shard_map/ppermute | solution.py:234
  47.5 2.0 %local_gradients.1 = (f32[256,512]{1,0:T(8,128)S(1)}, f32[64,512]{1,0:T(8,128)}, bf16[256,512]{1,0:T(8,128)(2,1)}) custom-call(bf16[256,512]{1,0:T(8,128)(2,1)S(1)} %copy-done.4, f32[400,512]{1,0:T(8,128)S(1)} %get-tuple-element.141.refs_1_, bf16[256,512]{1,0:T(8,128)(2,1)S(1)} %copy-done.5, bf16[400,512]{1,0:T(8,128)(2,1)S(1)} %get-tuple-element.142.refs_3_, ...), custom_call_target="tpu_custom_call" | custom-call | flops 402653184 | bytes 12042240 | tf_op jit(solution)/shard_map/local_gradients/pallas_call | solution.py:175
  49.6 1.0 %add_returned.1 = f32[256,512]{1,0:T(8,128)} custom-call(bf16[32,512]{1,0:T(8,128)(2,1)S(1)} %collective-permute-done.18.refs_0_, bf16[32,512]{1,0:T(8,128)(2,1)S(1)} %collective-permute-done.19.refs_1_, bf16[16,512]{1,0:T(8,128)(2,1)S(1)} %collective-permute-done.20.refs_2_, bf16[16,512]{1,0:T(8,128)(2,1)S(1)} %collective-permute-done.21.refs_3_, ...), custom_call_target="tpu_custom_call" | custom-call | flops 37748736 | bytes 1392640 | tf_op jit(solution)/shard_map/add_returned/pallas_call | solution.py:175
  (74 shorter events, 3.9 us)
Async XLA Ops:
  2.3 9.6 %collective-permute-start = (bf16[32,1024]{1,0:T(8,128)(2,1)S(1)}, bf16[32,1024]{1,0:T(8,128)(2,1)S(1)}, u32[]{:S(2)}, u32[]{:S(2)}) collective-permute-start(bf16[32,1024]{1,0:T(8,128)(2,1)S(1)} %get-tuple-element.90), channel_id=1, source_target_pairs={{0,12},{1,13},{2,14},{3,15},{4,8},{5,9},{6,10},{7,11},{8,4},{9,5},... | collective-permute-start | bytes 196616 | tf_op jit(solution)/shard_map/ppermute | solution.py:234
  7.4 7.7 %collective-permute-start.1 = (bf16[32,1024]{1,0:T(8,128)(2,1)S(1)}, bf16[32,1024]{1,0:T(8,128)(2,1)S(1)}, u32[]{:S(2)}, u32[]{:S(2)}) collective-permute-start(bf16[32,1024]{1,0:T(8,128)(2,1)S(1)} %get-tuple-element.93), channel_id=1, source_target_pairs={{0,4},{1,5},{2,6},{3,7},{4,0},{5,1},{6,2},{7,3},{8,12},{9,13},{10,... | collective-permute-start | bytes 196616 | tf_op jit(solution)/shard_map/ppermute | solution.py:234
  7.4 6.0 %collective-permute-start.2 = (bf16[16,1024]{1,0:T(8,128)(2,1)S(1)}, bf16[16,1024]{1,0:T(8,128)(2,1)S(1)}, u32[]{:S(2)}, u32[]{:S(2)}) collective-permute-start(bf16[16,1024]{1,0:T(8,128)(2,1)S(1)} %get-tuple-element.94), channel_id=1, source_target_pairs={{0,15},{1,2},{2,1},{3,4},{4,3},{5,6},{6,5},{7,8},{8,7},{9,10},{10,... | collective-permute-start | bytes 98312 | tf_op jit(solution)/shard_map/ppermute | solution.py:234
  8.2 5.6 %collective-permute-start.3 = (bf16[16,1024]{1,0:T(8,128)(2,1)S(1)}, bf16[16,1024]{1,0:T(8,128)(2,1)S(1)}, u32[]{:S(2)}, u32[]{:S(2)}) collective-permute-start(bf16[16,1024]{1,0:T(8,128)(2,1)S(1)} %get-tuple-element.95), channel_id=1, source_target_pairs={{0,3},{1,14},{2,5},{3,0},{4,7},{5,2},{6,9},{7,4},{8,11},{9,6},{10,... | collective-permute-start | bytes 98312 | tf_op jit(solution)/shard_map/ppermute | solution.py:234
  10.7 6.9 %collective-permute-start.4 = (bf16[16,1024]{1,0:T(8,128)(2,1)S(1)}, bf16[16,1024]{1,0:T(8,128)(2,1)S(1)}, u32[]{:S(2)}, u32[]{:S(2)}) collective-permute-start(bf16[16,1024]{1,0:T(8,128)(2,1)S(1)} %get-tuple-element.96), channel_id=1, source_target_pairs={{0,11},{1,6},{2,13},{3,8},{4,15},{5,10},{6,1},{7,12},{8,3},{9,14},... | collective-permute-start | bytes 98312 | tf_op jit(solution)/shard_map/ppermute | solution.py:234
  12.0 5.8 %collective-permute-start.5 = (bf16[16,1024]{1,0:T(8,128)(2,1)S(1)}, bf16[16,1024]{1,0:T(8,128)(2,1)S(1)}, u32[]{:S(2)}, u32[]{:S(2)}) collective-permute-start(bf16[16,1024]{1,0:T(8,128)(2,1)S(1)} %get-tuple-element.97), channel_id=1, source_target_pairs={{0,8},{1,9},{2,10},{3,11},{4,12},{5,13},{6,14},{7,15},{8,0},{9,1},... | collective-permute-start | bytes 98312 | tf_op jit(solution)/shard_map/ppermute | solution.py:234
  13.5 4.3 %collective-permute-start.6 = (bf16[16,1024]{1,0:T(8,128)(2,1)S(1)}, bf16[16,1024]{1,0:T(8,128)(2,1)S(1)}, u32[]{:S(2)}, u32[]{:S(2)}) collective-permute-start(bf16[16,1024]{1,0:T(8,128)(2,1)S(1)} %get-tuple-element.98), channel_id=1, source_target_pairs={{0,1},{1,0},{2,3},{3,2},{4,5},{5,4},{6,7},{7,6},{8,9},{9,8},{10,11... | collective-permute-start | bytes 98312 | tf_op jit(solution)/shard_map/ppermute | solution.py:234
  13.8 4.0 %collective-permute-start.7 = (bf16[32,1024]{1,0:T(8,128)(2,1)S(1)}, bf16[32,1024]{1,0:T(8,128)(2,1)S(1)}, u32[]{:S(2)}, u32[]{:S(2)}) collective-permute-start(bf16[32,1024]{1,0:T(8,128)(2,1)S(1)} %collective-permute-done.refs_0_), channel_id=1, source_target_pairs={{0,1},{1,0},{2,3},{3,2},{4,5},{5,4},{6,7},{7,6},{8,9},{9,8},{10,11... | collective-permute-start | bytes 196616 | tf_op jit(solution)/shard_map/ppermute | solution.py:234
  20.7 6.8 %collective-permute-start.9 = (bf16[32,1024]{1,0:T(8,128)(2,1)S(1)}, bf16[32,1024]{1,0:T(8,128)(2,1)S(1)}, u32[]{:S(2)}, u32[]{:S(2)}) collective-permute-start(bf16[32,1024]{1,0:T(8,128)(2,1)S(1)} %get-tuple-element.111), channel_id=1, source_target_pairs={{0,12},{1,13},{2,14},{3,15},{4,8},{5,9},{6,10},{7,11},{8,4},{9,5},... | collective-permute-start | bytes 196616 | tf_op jit(solution)/shard_map/ppermute | solution.py:234
  22.4 7.1 %collective-permute-start.10 = (bf16[32,1024]{1,0:T(8,128)(2,1)S(1)}, bf16[32,1024]{1,0:T(8,128)(2,1)S(1)}, u32[]{:S(2)}, u32[]{:S(2)}) collective-permute-start(bf16[32,1024]{1,0:T(8,128)(2,1)S(1)} %get-tuple-element.114), channel_id=1, source_target_pairs={{0,4},{1,5},{2,6},{3,7},{4,0},{5,1},{6,2},{7,3},{8,12},{9,13},{10,... | collective-permute-start | bytes 196616 | tf_op jit(solution)/shard_map/ppermute | solution.py:234
  22.4 6.0 %collective-permute-start.11 = (bf16[16,1024]{1,0:T(8,128)(2,1)S(1)}, bf16[16,1024]{1,0:T(8,128)(2,1)S(1)}, u32[]{:S(2)}, u32[]{:S(2)}) collective-permute-start(bf16[16,1024]{1,0:T(8,128)(2,1)S(1)} %get-tuple-element.115), channel_id=1, source_target_pairs={{0,15},{1,2},{2,1},{3,4},{4,3},{5,6},{6,5},{7,8},{8,7},{9,10},{10,... | collective-permute-start | bytes 98312 | tf_op jit(solution)/shard_map/ppermute | solution.py:234
  23.8 4.7 %collective-permute-start.12 = (bf16[16,1024]{1,0:T(8,128)(2,1)S(1)}, bf16[16,1024]{1,0:T(8,128)(2,1)S(1)}, u32[]{:S(2)}, u32[]{:S(2)}) collective-permute-start(bf16[16,1024]{1,0:T(8,128)(2,1)S(1)} %get-tuple-element.116), channel_id=1, source_target_pairs={{0,3},{1,14},{2,5},{3,0},{4,7},{5,2},{6,9},{7,4},{8,11},{9,6},{10,... | collective-permute-start | bytes 98312 | tf_op jit(solution)/shard_map/ppermute | solution.py:234
  25.6 6.9 %collective-permute-start.13 = (bf16[16,1024]{1,0:T(8,128)(2,1)S(1)}, bf16[16,1024]{1,0:T(8,128)(2,1)S(1)}, u32[]{:S(2)}, u32[]{:S(2)}) collective-permute-start(bf16[16,1024]{1,0:T(8,128)(2,1)S(1)} %get-tuple-element.117), channel_id=1, source_target_pairs={{0,11},{1,6},{2,13},{3,8},{4,15},{5,10},{6,1},{7,12},{8,3},{9,14},... | collective-permute-start | bytes 98312 | tf_op jit(solution)/shard_map/ppermute | solution.py:234
  27.5 5.1 %collective-permute-start.14 = (bf16[16,1024]{1,0:T(8,128)(2,1)S(1)}, bf16[16,1024]{1,0:T(8,128)(2,1)S(1)}, u32[]{:S(2)}, u32[]{:S(2)}) collective-permute-start(bf16[16,1024]{1,0:T(8,128)(2,1)S(1)} %get-tuple-element.118), channel_id=1, source_target_pairs={{0,8},{1,9},{2,10},{3,11},{4,12},{5,13},{6,14},{7,15},{8,0},{9,1},... | collective-permute-start | bytes 98312 | tf_op jit(solution)/shard_map/ppermute | solution.py:234
  28.5 4.1 %collective-permute-start.15 = (bf16[16,1024]{1,0:T(8,128)(2,1)S(1)}, bf16[16,1024]{1,0:T(8,128)(2,1)S(1)}, u32[]{:S(2)}, u32[]{:S(2)}) collective-permute-start(bf16[16,1024]{1,0:T(8,128)(2,1)S(1)} %get-tuple-element.119), channel_id=1, source_target_pairs={{0,1},{1,0},{2,3},{3,2},{4,5},{5,4},{6,7},{7,6},{8,9},{9,8},{10,11... | collective-permute-start | bytes 98312 | tf_op jit(solution)/shard_map/ppermute | solution.py:234
  28.5 4.1 %collective-permute-start.16 = (bf16[32,1024]{1,0:T(8,128)(2,1)S(1)}, bf16[32,1024]{1,0:T(8,128)(2,1)S(1)}, u32[]{:S(2)}, u32[]{:S(2)}) collective-permute-start(bf16[32,1024]{1,0:T(8,128)(2,1)S(1)} %collective-permute-done.9.refs_0_), channel_id=1, source_target_pairs={{0,1},{1,0},{2,3},{3,2},{4,5},{5,4},{6,7},{7,6},{8,9},{9,8},{10,11... | collective-permute-start | bytes 196616 | tf_op jit(solution)/shard_map/ppermute | solution.py:234
  37.9 6.7 %collective-permute-start.18 = (bf16[32,512]{1,0:T(8,128)(2,1)S(1)}, bf16[32,512]{1,0:T(8,128)(2,1)S(1)}, u32[]{:S(2)}, u32[]{:S(2)}) collective-permute-start(bf16[32,512]{1,0:T(8,128)(2,1)S(1)} %get-tuple-element.149), channel_id=1, source_target_pairs={{0,12},{1,13},{2,14},{3,15},{4,8},{5,9},{6,10},{7,11},{8,4},{9,5},... | collective-permute-start | bytes 98312 | tf_op jit(solution)/shard_map/ppermute | solution.py:234
  39.8 7.6 %collective-permute-start.19 = (bf16[32,512]{1,0:T(8,128)(2,1)S(1)}, bf16[32,512]{1,0:T(8,128)(2,1)S(1)}, u32[]{:S(2)}, u32[]{:S(2)}) collective-permute-start(bf16[32,512]{1,0:T(8,128)(2,1)S(1)} %get-tuple-element.152), channel_id=1, source_target_pairs={{0,4},{1,5},{2,6},{3,7},{4,0},{5,1},{6,2},{7,3},{8,12},{9,13},{10,... | collective-permute-start | bytes 98312 | tf_op jit(solution)/shard_map/ppermute | solution.py:234
  40.0 5.9 %collective-permute-start.20 = (bf16[16,512]{1,0:T(8,128)(2,1)S(1)}, bf16[16,512]{1,0:T(8,128)(2,1)S(1)}, u32[]{:S(2)}, u32[]{:S(2)}) collective-permute-start(bf16[16,512]{1,0:T(8,128)(2,1)S(1)} %get-tuple-element.153), channel_id=1, source_target_pairs={{0,15},{1,2},{2,1},{3,4},{4,3},{5,6},{6,5},{7,8},{8,7},{9,10},{10,... | collective-permute-start | bytes 49160 | tf_op jit(solution)/shard_map/ppermute | solution.py:234
  41.6 4.7 %collective-permute-start.21 = (bf16[16,512]{1,0:T(8,128)(2,1)S(1)}, bf16[16,512]{1,0:T(8,128)(2,1)S(1)}, u32[]{:S(2)}, u32[]{:S(2)}) collective-permute-start(bf16[16,512]{1,0:T(8,128)(2,1)S(1)} %get-tuple-element.154), channel_id=1, source_target_pairs={{0,3},{1,14},{2,5},{3,0},{4,7},{5,2},{6,9},{7,4},{8,11},{9,6},{10,... | collective-permute-start | bytes 49160 | tf_op jit(solution)/shard_map/ppermute | solution.py:234
  43.0 6.4 %collective-permute-start.22 = (bf16[16,512]{1,0:T(8,128)(2,1)S(1)}, bf16[16,512]{1,0:T(8,128)(2,1)S(1)}, u32[]{:S(2)}, u32[]{:S(2)}) collective-permute-start(bf16[16,512]{1,0:T(8,128)(2,1)S(1)} %get-tuple-element.155), channel_id=1, source_target_pairs={{0,11},{1,6},{2,13},{3,8},{4,15},{5,10},{6,1},{7,12},{8,3},{9,14},... | collective-permute-start | bytes 49160 | tf_op jit(solution)/shard_map/ppermute | solution.py:234
  44.6 5.0 %collective-permute-start.23 = (bf16[16,512]{1,0:T(8,128)(2,1)S(1)}, bf16[16,512]{1,0:T(8,128)(2,1)S(1)}, u32[]{:S(2)}, u32[]{:S(2)}) collective-permute-start(bf16[16,512]{1,0:T(8,128)(2,1)S(1)} %get-tuple-element.156), channel_id=1, source_target_pairs={{0,8},{1,9},{2,10},{3,11},{4,12},{5,13},{6,14},{7,15},{8,0},{9,1},... | collective-permute-start | bytes 49160 | tf_op jit(solution)/shard_map/ppermute | solution.py:234
  45.9 3.7 %collective-permute-start.24 = (bf16[16,512]{1,0:T(8,128)(2,1)S(1)}, bf16[16,512]{1,0:T(8,128)(2,1)S(1)}, u32[]{:S(2)}, u32[]{:S(2)}) collective-permute-start(bf16[16,512]{1,0:T(8,128)(2,1)S(1)} %get-tuple-element.157), channel_id=1, source_target_pairs={{0,1},{1,0},{2,3},{3,2},{4,5},{5,4},{6,7},{7,6},{8,9},{9,8},{10,11... | collective-permute-start | bytes 49160 | tf_op jit(solution)/shard_map/ppermute | solution.py:234
  46.3 3.3 %collective-permute-start.25 = (bf16[32,512]{1,0:T(8,128)(2,1)S(1)}, bf16[32,512]{1,0:T(8,128)(2,1)S(1)}, u32[]{:S(2)}, u32[]{:S(2)}) collective-permute-start(bf16[32,512]{1,0:T(8,128)(2,1)S(1)} %collective-permute-done.18.refs_0_), channel_id=1, source_target_pairs={{0,1},{1,0},{2,3},{3,2},{4,5},{5,4},{6,7},{7,6},{8,9},{9,8},{10,11... | collective-permute-start | bytes 98312 | tf_op jit(solution)/shard_map/ppermute | solution.py:234
  (21 other events, 237.6 us)

commit v13 on v12

--- a/solution.py
+++ b/solution.py
@@ -45,17 +45,53 @@
     return [slice(start, min(start + size, rows)) for start in range(0, rows, size)]
 
 
-def write_silu(pre, act_ref):
-    for rows in row_chunks(pre.shape[0]):
-        act_ref[rows, :] = silu(pre[rows, :]).astype(BF16)
-
-
-def write_norm(raw, normed_ref, scale_ref):
-    for rows in row_chunks(raw.shape[0]):
-        part = raw[rows, :]
-        scale_inv = scale_rows(part)
-        normed_ref[rows, :] = (part * scale_inv).astype(normed_ref.dtype)
+def row_halves(rows):
+    size = -(-rows // 32) * 16
+    return row_chunks(rows, size)
+
+
+def in_step(chains):
+    chains = list(chains)
+    while chains:
+        left = []
+        for chain in chains:
+            try:
+                next(chain)
+                left.append(chain)
+            except StopIteration:
+                pass
+        chains = left
+
+
+def parts_of(block):
+    return [
+        (part, slice(block.start + part.start, block.start + part.stop))
+        for part in row_chunks(block.stop - block.start)
+    ]
+
+
+def write_silu(pre, act_ref, block):
+    for part, rows in parts_of(block):
+        act_ref[rows, :] = silu(pre[part, :]).astype(BF16)
+
+
+def write_norm(raw, normed_ref, scale_ref, block):
+    for part, rows in parts_of(block):
+        values = raw[part, :]
+        scale_inv = scale_rows(values)
+        normed_ref[rows, :] = (values * scale_inv).astype(normed_ref.dtype)
         scale_ref[rows, :] = scale_inv
+
+
+def forward_chain(make_pre, pre_ref, act_ref, second_ref, normed_ref, scale_ref, block):
+    pre = make_pre(block)
+    pre_ref[block, :] = pre
+    yield
+    write_silu(pre, act_ref, block)
+    yield
+    raw = mm(act_ref[block, :], second_ref[...])
+    yield
+    write_norm(raw, normed_ref, scale_ref, block)
 
 
 def write_slopes(pre_ref, normed_ref, scale_ref, second_ref, gain_ref, turned_ref):
@@ -66,14 +102,16 @@
         turned_ref[rows, :] = (gain * raw[rows, :]).astype(BF16)
 
 
-def edge_back(both, normed_ref, gain_ref, turned_ref, out_ref):
-    edges, features = normed_ref.shape
-    for rows in row_chunks(edges):
+def edge_back(make_both, normed_ref, gain_ref, turned_ref, out_ref, block):
+    features = normed_ref.shape[1]
+    both = make_both(block)
+    yield
+    for part, rows in parts_of(block):
         mean = jnp.mean(
-            both[rows, :features] * normed_ref[rows, :].astype(F32), axis=-1, keepdims=True
+            both[part, :features] * normed_ref[rows, :].astype(F32), axis=-1, keepdims=True
         )
         out_ref[rows, :] = (
-            gain_ref[rows, :] * both[rows, features:].astype(BF16)
+            gain_ref[rows, :] * both[part, features:].astype(BF16)
             - turned_ref[rows, :] * mean.astype(BF16)
         )
 
@@ -509,23 +547,50 @@
         ) = refs
         rows = by_slot(arrived_refs, low)
         pe = mm(rows, enc_wg_ref[low, :]).astype(BF16)
-        enc_pre_ref[...] = enc_part_ref[...] + mm(enc_pick_ref[:, grid_count:spots], pe)
-        write_silu(enc_pre_ref, enc_act_ref)
-        write_norm(mm(enc_act_ref[...], enc_w2_ref[...]), enc_normed_ref, enc_scale_ref)
+
+        def enc_pre(block):
+            return enc_part_ref[block, :] + mm(enc_pick_ref[block, grid_count:spots], pe)
+
+        in_step(
+            forward_chain(
+                enc_pre,
+                enc_pre_ref,
+                enc_act_ref,
+                enc_w2_ref,
+                enc_normed_ref,
+                enc_scale_ref,
+                block,
+            )
+            for block in row_halves(enc_count)
+        )
         agg = mm(enc_pool_ref[mesh_rows, :], enc_normed_ref[...]).astype(BF16)
         mesh_pre_ref[...] = mesh_part_ref[...] + mm(agg, mesh_wa_ref[high, :])
-        write_silu(mesh_pre_ref, mesh_act_ref)
+        whole = slice(0, mesh_count)
+        write_silu(mesh_pre_ref[...], mesh_act_ref, whole)
         both = mm(mesh_act_ref[...], mesh_w2_ref[...])
-        write_norm(both[:, low], mesh_normed_ref, mesh_scale_ref)
+        write_norm(both[:, low], mesh_normed_ref, mesh_scale_ref, whole)
         mesh_sent = mesh_base_ref[...] + mesh_scale_ref[...] * both[:, high]
         table_ref[:slots, :] = mm(rows, dec_wg_ref[low, :]).astype(BF16)
         table_ref[slots : slots + mesh_count, :] = mesh_sent.astype(BF16)
         table_ref[slots + mesh_count :, :] = jnp.zeros(
             (total - spots - mesh_count, feat), BF16
         )
-        dec_pre_ref[...] = dec_part_ref[...] + mm(dec_pick_ref[:, grid_count:], table_ref[...])
-        write_silu(dec_pre_ref, dec_act_ref)
-        write_norm(mm(dec_act_ref[...], dec_w2_ref[...]), dec_normed_ref, dec_scale_ref)
+
+        def dec_pre(block):
+            return dec_part_ref[block, :] + mm(dec_pick_ref[block, grid_count:], table_ref[...])
+
+        in_step(
+            forward_chain(
+                dec_pre,
+                dec_pre_ref,
+                dec_act_ref,
+                dec_w2_ref,
+                dec_normed_ref,
+                dec_scale_ref,
+                block,
+            )
+            for block in row_halves(dec_count)
+        )
         spot_ref[...] = mm(dec_pool_ref[:spots, :], dec_normed_ref[...])
         shared = mm(shared_pool_ref[...], dec_normed_ref[...]).astype(BF16)
         slot_msg = spot_ref[grid_count:, :].astype(BF16)
@@ -740,25 +805,33 @@
         agg_ref[grid_count:, :] = (
             spot_ref[grid_count:, :] + by_slot(returned_refs, high).astype(F32)
         ).astype(BF16)
-        pre = grid_part_ref[...] + mm(agg_ref[...], grid_first_ref[high, :])
         mesh_in_ref[low, :] = dec_first_ref[high, :]
         mesh_in_ref[high, :] = mm(mesh_wide_ref[:, low], dec_first_ref[high, :]).astype(BF16)
-        for rows in row_chunks(spots):
-            act, slope = silu_and_slope(pre[rows, :])
-            grid_act_ref[rows, :] = act.astype(BF16)
-            grid_slope_ref[rows, :] = slope
-        both = mm(grid_act_ref[...], grid_wide_ref[...])
+
+        def grid_chain(block):
+            pre = grid_part_ref[block, :] + mm(agg_ref[block, :], grid_first_ref[high, :])
+            yield
+            for part, rows in parts_of(block):
+                act, slope = silu_and_slope(pre[part, :])
+                grid_act_ref[rows, :] = act.astype(BF16)
+                grid_slope_ref[rows, :] = slope
+            yield
+            both = mm(grid_act_ref[block, :], grid_wide_ref[...])
+            yield
+            for part, rows in parts_of(block):
+                raw = both[part, low]
+                scale_inv = scale_rows(raw)
+                normed = raw * scale_inv
+                grid_normed_ref[rows, :] = normed
+                mean = jnp.mean(cot_rows_ref[rows, :].astype(F32) * normed, axis=-1, keepdims=True)
+                raw = scale_inv * (cot_turned_ref[rows, :] - (mean * scale_inv) * both[part, high])
+                grid_gpre_ref[rows, :] = (raw * grid_slope_ref[rows, :]).astype(BF16)
+            yield
+            spot_grad_ref[block, :] = mm_t(grid_gpre_ref[block, :], grid_back_ref[...]).astype(BF16)
+
+        in_step(grid_chain(block) for block in row_halves(spots))
         mesh_back_ref[low, :] = centred(mesh_first_ref[high, :], 0).astype(BF16)
         mesh_back_ref[high, :] = mm(enc_second_ref[...], mesh_back_ref[low, :]).astype(BF16)
-        for rows in row_chunks(spots):
-            part = both[rows, low]
-            scale_inv = scale_rows(part)
-            normed = part * scale_inv
-            grid_normed_ref[rows, :] = normed
-            mean = jnp.mean(cot_rows_ref[rows, :].astype(F32) * normed, axis=-1, keepdims=True)
-            raw = scale_inv * (cot_turned_ref[rows, :] - (mean * scale_inv) * both[rows, high])
-            grid_gpre_ref[rows, :] = (raw * grid_slope_ref[rows, :]).astype(BF16)
-        spot_grad_ref[:spots, :] = mm_t(grid_gpre_ref[...], grid_back_ref[...]).astype(BF16)
         spot_grad_ref[spots:, :] = jnp.zeros((total - spots, 2 * feat), BF16)
         write_slopes(
             enc_pre_ref,
@@ -768,12 +841,16 @@
             enc_gain_ref,
             enc_turned_ref,
         )
-        edge_back(
-            mm(dec_pick_ref[...], spot_grad_ref[...]),
-            dec_normed_ref,
-            dec_gain_ref,
-            dec_turned_ref,
-            dec_gpre_ref,
+        in_step(
+            edge_back(
+                lambda rows: mm(dec_pick_ref[rows, :], spot_grad_ref[...]),
+                dec_normed_ref,
+                dec_gain_ref,
+                dec_turned_ref,
+                dec_gpre_ref,
+                block,
+            )
+            for block in row_halves(dec_count)
         )
         mesh_sum = mm(dec_pool_ref[mesh_rows, :], dec_gpre_ref[...]).astype(BF16)
         both = mm_t(mesh_sum, mesh_in_ref[...])
@@ -785,12 +862,16 @@
         mesh_gagg = mm_t(mesh_gpre_ref[...], mesh_back_ref[...]).astype(BF16)
         pooled = mm(dec_pool_ref[grid_count:spots, :], dec_gpre_ref[...]).astype(BF16)
         slot_back = mm_t(pooled, dec_first_ref[low, :])
-        edge_back(
-            mm(enc_pick_ref[:, mesh_rows], mesh_gagg),
-            enc_normed_ref,
-            enc_gain_ref,
-            enc_turned_ref,
-            enc_gpre_ref,
+        in_step(
+            edge_back(
+                lambda rows: mm(enc_pick_ref[rows, mesh_rows], mesh_gagg),
+                enc_normed_ref,
+                enc_gain_ref,
+                enc_turned_ref,
+                enc_gpre_ref,
+                block,
+            )
+            for block in row_halves(enc_count)
         )
         pooled = mm(enc_pool_ref[grid_count:spots, :], enc_gpre_ref[...]).astype(BF16)
         slot_back = (slot_back + mm_t(pooled, enc_first_ref[low, :])).astype(BF16)

time: 50.8 us -> 50.8 us (level)
  transfers between devices with their start and end apart: 27 -> 27, of which waited for: 6 -> 5; matrix products, arithmetic and copies ran while one was open for 0% -> 0% of each run, Pallas kernels for 14% -> 14%
where the time goes in v13:
time: 50.8 us; the launch traced here: 50.6 us
  starting transfers between devices  28.8 us (57%)
  Pallas kernels  18.2 us (36%)
  waiting for transfers between devices  2.53 us (5%)
  between operations  1 us (2%)
    ppermute x27, starting transfers between devices, permute(): return lax.ppermute(part, 'tile', pairs)  28.8 us
    pallas_call x8, Pallas kernels, call(): pl.pallas_call(kernel, name=name, in_specs=specs, out_specs=[pl.BlockSpec...  18.2 us
    ppermute x27, waiting for transfers between devices, permute(): return lax.ppermute(part, 'tile', pairs)  2.53 us
  transfers between devices with their start and end apart: 27, of which 5 were waited for; matrix products, arithmetic and copies ran while one was open for 0% of the time, Pallas kernels for 14%

profile of v13, /device:TPU:0, one launch (start us, length us, event | category | flops | bytes accessed | tf_op | source)
XLA Modules:
  0.0 50.6 jit_solution(6052775490470581780)
XLA Ops:
  0.6 1.4 %pack_rows.1 = (bf16[256,256]{1,0:T(8,128)(2,1)S(1)}, bf16[32,1024]{1,0:T(8,128)(2,1)S(1)}, bf16[32,1024]{1,0:T(8,128)(2,1)S(1)}, bf16[16,1024]{1,0:T(8,128)(2,1...) custom-call(s32[9,16]{1,0:T(8,128)} %refs_0_.2, ...), custom_call_target="tpu_custom_call" | custom-call | flops 75497472 | bytes 950884 | tf_op jit(solution)/shard_map/pack_rows/pallas_call | solution.py:213
  2.3 5.1 %collective-permute-start = (bf16[32,1024]{1,0:T(8,128)(2,1)S(1)}, bf16[32,1024]{1,0:T(8,128)(2,1)S(1)}, u32[]{:S(2)}, u32[]{:S(2)}) collective-permute-start(bf16[32,1024]{1,0:T(8,128)(2,1)S(1)} %get-tuple-element.90), channel_id=1, source_target_pairs={{0,12},{1,13},{2,14},{3,15},{4,8},{5,9},{6,10},{7,11},{8,4},{9,5},... | collective-permute-start | bytes 196616 | tf_op jit(solution)/shard_map/ppermute | solution.py:272
  8.2 2.5 %collective-permute-start.3 = (bf16[16,1024]{1,0:T(8,128)(2,1)S(1)}, bf16[16,1024]{1,0:T(8,128)(2,1)S(1)}, u32[]{:S(2)}, u32[]{:S(2)}) collective-permute-start(bf16[16,1024]{1,0:T(8,128)(2,1)S(1)} %get-tuple-element.95), channel_id=1, source_target_pairs={{0,3},{1,14},{2,5},{3,0},{4,7},{5,2},{6,9},{7,4},{8,11},{9,6},{10,... | collective-permute-start | bytes 98312 | tf_op jit(solution)/shard_map/ppermute | solution.py:272
  10.7 1.3 %collective-permute-start.4 = (bf16[16,1024]{1,0:T(8,128)(2,1)S(1)}, bf16[16,1024]{1,0:T(8,128)(2,1)S(1)}, u32[]{:S(2)}, u32[]{:S(2)}) collective-permute-start(bf16[16,1024]{1,0:T(8,128)(2,1)S(1)} %get-tuple-element.96), channel_id=1, source_target_pairs={{0,11},{1,6},{2,13},{3,8},{4,15},{5,10},{6,1},{7,12},{8,3},{9,14},... | collective-permute-start | bytes 98312 | tf_op jit(solution)/shard_map/ppermute | solution.py:272
  12.0 1.1 %collective-permute-start.5 = (bf16[16,1024]{1,0:T(8,128)(2,1)S(1)}, bf16[16,1024]{1,0:T(8,128)(2,1)S(1)}, u32[]{:S(2)}, u32[]{:S(2)}) collective-permute-start(bf16[16,1024]{1,0:T(8,128)(2,1)S(1)} %get-tuple-element.97), channel_id=1, source_target_pairs={{0,8},{1,9},{2,10},{3,11},{4,12},{5,13},{6,14},{7,15},{8,0},{9,1},... | collective-permute-start | bytes 98312 | tf_op jit(solution)/shard_map/ppermute | solution.py:272
  13.8 1.3 %collective-permute-start.7 = (bf16[32,1024]{1,0:T(8,128)(2,1)S(1)}, bf16[32,1024]{1,0:T(8,128)(2,1)S(1)}, u32[]{:S(2)}, u32[]{:S(2)}) collective-permute-start(bf16[32,1024]{1,0:T(8,128)(2,1)S(1)} %collective-permute-done.refs_0_), channel_id=1, source_target_pairs={{0,1},{1,0},{2,3},{3,2},{4,5},{5,4},{6,7},{7,6},{8,9},{9,8},{10,11... | collective-permute-start | bytes 196616 | tf_op jit(solution)/shard_map/ppermute | solution.py:272
  15.3 2.3 %local_products.1 = (f32[384,512]{1,0:T(8,128)S(1)}, f32[768,512]{1,0:T(8,128)S(1)}, f32[64,512]{1,0:T(8,128)S(1)}, bf16[384,512]{1,0:T(8,128)(2,1)S(1)}, bf16[5...) custom-call(bf16[256,256]{1,0:T(8,128)(2,1)S(1)} %get-tuple-element., ...), custom_call_target="tpu_custom_call" | custom-call | flops 1275068416 | bytes 14713856 | tf_op jit(solution)/shard_map/local_products/pallas_call | solution.py:213
  17.8 3.0 %edges_forward.1 = (bf16[32,1024]{1,0:T(8,128)(2,1)S(1)}, bf16[32,1024]{1,0:T(8,128)(2,1)S(1)}, bf16[16,1024]{1,0:T(8,128)(2,1)S(1)}, bf16[16,1024]{1,0:T(8,128)...) custom-call(bf16[32,1024]{1,0:T(8,128)(2,1)S(1)} %collective-permute, ...), custom_call_target="tpu_custom_call" | custom-call | flops 1207959552 | bytes 16839424 | tf_op jit(solution)/shard_map/edges_forward/pallas_call | solution.py:213
  20.8 1.7 %collective-permute-start.9 = (bf16[32,1024]{1,0:T(8,128)(2,1)S(1)}, bf16[32,1024]{1,0:T(8,128)(2,1)S(1)}, u32[]{:S(2)}, u32[]{:S(2)}) collective-permute-start(bf16[32,1024]{1,0:T(8,128)(2,1)S(1)} %get-tuple-element.111), channel_id=1, source_target_pairs={{0,12},{1,13},{2,14},{3,15},{4,8},{5,9},{6,10},{7,11},{8,4},{9,5},... | collective-permute-start | bytes 196616 | tf_op jit(solution)/shard_map/ppermute | solution.py:272
  22.5 1.4 %collective-permute-start.11 = (bf16[16,1024]{1,0:T(8,128)(2,1)S(1)}, bf16[16,1024]{1,0:T(8,128)(2,1)S(1)}, u32[]{:S(2)}, u32[]{:S(2)}) collective-permute-start(bf16[16,1024]{1,0:T(8,128)(2,1)S(1)} %get-tuple-element.115), channel_id=1, source_target_pairs={{0,15},{1,2},{2,1},{3,4},{4,3},{5,6},{6,5},{7,8},{8,7},{9,10},{10,... | collective-permute-start | bytes 98312 | tf_op jit(solution)/shard_map/ppermute | solution.py:272
  23.8 1.8 %collective-permute-start.12 = (bf16[16,1024]{1,0:T(8,128)(2,1)S(1)}, bf16[16,1024]{1,0:T(8,128)(2,1)S(1)}, u32[]{:S(2)}, u32[]{:S(2)}) collective-permute-start(bf16[16,1024]{1,0:T(8,128)(2,1)S(1)} %get-tuple-element.116), channel_id=1, source_target_pairs={{0,3},{1,14},{2,5},{3,0},{4,7},{5,2},{6,9},{7,4},{8,11},{9,6},{10,... | collective-permute-start | bytes 98312 | tf_op jit(solution)/shard_map/ppermute | solution.py:272
  25.7 0.8 %collective-permute-start.13 = (bf16[16,1024]{1,0:T(8,128)(2,1)S(1)}, bf16[16,1024]{1,0:T(8,128)(2,1)S(1)}, u32[]{:S(2)}, u32[]{:S(2)}) collective-permute-start(bf16[16,1024]{1,0:T(8,128)(2,1)S(1)} %get-tuple-element.117), channel_id=1, source_target_pairs={{0,11},{1,6},{2,13},{3,8},{4,15},{5,10},{6,1},{7,12},{8,3},{9,14},... | collective-permute-start | bytes 98312 | tf_op jit(solution)/shard_map/ppermute | solution.py:272
  26.4 1.1 %collective-permute-done.9.refs_0_ = bf16[32,1024]{1,0:T(8,128)(2,1)S(1)} collective-permute-done((bf16[32,1024]{1,0:T(8,128)(2,1)S(1)}, bf16[32,1024]{1,0:T(8,128)(2,1)S(1)}, u32[]{:S(2)}, u32[]{:S(2)}) %collective-permute-start.9) | collective-permute-done | bytes 65568 | tf_op jit(solution)/shard_map/ppermute | solution.py:272
  28.5 1.0 %collective-permute-start.16 = (bf16[32,1024]{1,0:T(8,128)(2,1)S(1)}, bf16[32,1024]{1,0:T(8,128)(2,1)S(1)}, u32[]{:S(2)}, u32[]{:S(2)}) collective-permute-start(bf16[32,1024]{1,0:T(8,128)(2,1)S(1)} %collective-permute-done.9.refs_0_), channel_id=1, source_target_pairs={{0,1},{1,0},{2,3},{3,2},{4,5},{5,4},{6,7},{7,6},{8,9},{9,8},{10,11... | collective-permute-start | bytes 196616 | tf_op jit(solution)/shard_map/ppermute | solution.py:272
  29.6 3.0 %slopes_and_nodes.1 = (f32[400,512]{1,0:T(8,128)S(1)}, bf16[400,512]{1,0:T(8,128)(2,1)S(1)}, f32[400,512]{1,0:T(8,128)S(1)}, bf16[512,1024]{1,0:T(8,128)(2,1)S(1...) custom-call(bf16[32,1024]{1,0:T(8,128)(2,1)S(1)} %collective-permute, ...), custom_call_target="tpu_custom_call" | custom-call | flops 1677721600 | bytes 13552640 | tf_op jit(solution)/shard_map/slopes_and_nodes/pallas_call | solution.py:213
  32.6 5.4 %edges_backward.1 = (bf16[32,512]{1,0:T(8,128)(2,1)S(1)}, bf16[32,512]{1,0:T(8,128)(2,1)S(1)}, bf16[16,512]{1,0:T(8,128)(2,1)S(1)}, bf16[16,512]{1,0:T(8,128)(2,...) custom-call(bf16[32,1024]{1,0:T(8,128)(2,1)S(1)} %collective-permute, ...), custom_call_target="tpu_custom_call" | custom-call | flops 2449473536 | bytes 21579520 | tf_op jit(solution)/shard_map/edges_backward/pallas_call | solution.py:213
  38.0 1.9 %collective-permute-start.18 = (bf16[32,512]{1,0:T(8,128)(2,1)S(1)}, bf16[32,512]{1,0:T(8,128)(2,1)S(1)}, u32[]{:S(2)}, u32[]{:S(2)}) collective-permute-start(bf16[32,512]{1,0:T(8,128)(2,1)S(1)} %get-tuple-element.149), channel_id=1, source_target_pairs={{0,12},{1,13},{2,14},{3,15},{4,8},{5,9},{6,10},{7,11},{8,4},{9,5},... | collective-permute-start | bytes 98312 | tf_op jit(solution)/shard_map/ppermute | solution.py:272
  40.2 1.6 %collective-permute-start.20 = (bf16[16,512]{1,0:T(8,128)(2,1)S(1)}, bf16[16,512]{1,0:T(8,128)(2,1)S(1)}, u32[]{:S(2)}, u32[]{:S(2)}) collective-permute-start(bf16[16,512]{1,0:T(8,128)(2,1)S(1)} %get-tuple-element.153), channel_id=1, source_target_pairs={{0,15},{1,2},{2,1},{3,4},{4,3},{5,6},{6,5},{7,8},{8,7},{9,10},{10,... | collective-permute-start | bytes 49160 | tf_op jit(solution)/shard_map/ppermute | solution.py:272
  41.7 1.4 %collective-permute-start.21 = (bf16[16,512]{1,0:T(8,128)(2,1)S(1)}, bf16[16,512]{1,0:T(8,128)(2,1)S(1)}, u32[]{:S(2)}, u32[]{:S(2)}) collective-permute-start(bf16[16,512]{1,0:T(8,128)(2,1)S(1)} %get-tuple-element.154), channel_id=1, source_target_pairs={{0,3},{1,14},{2,5},{3,0},{4,7},{5,2},{6,9},{7,4},{8,11},{9,6},{10,... | collective-permute-start | bytes 49160 | tf_op jit(solution)/shard_map/ppermute | solution.py:272
  43.1 1.5 %collective-permute-start.22 = (bf16[16,512]{1,0:T(8,128)(2,1)S(1)}, bf16[16,512]{1,0:T(8,128)(2,1)S(1)}, u32[]{:S(2)}, u32[]{:S(2)}) collective-permute-start(bf16[16,512]{1,0:T(8,128)(2,1)S(1)} %get-tuple-element.155), channel_id=1, source_target_pairs={{0,11},{1,6},{2,13},{3,8},{4,15},{5,10},{6,1},{7,12},{8,3},{9,14},... | collective-permute-start | bytes 49160 | tf_op jit(solution)/shard_map/ppermute | solution.py:272
  44.6 1.2 %collective-permute-start.23 = (bf16[16,512]{1,0:T(8,128)(2,1)S(1)}, bf16[16,512]{1,0:T(8,128)(2,1)S(1)}, u32[]{:S(2)}, u32[]{:S(2)}) collective-permute-start(bf16[16,512]{1,0:T(8,128)(2,1)S(1)} %get-tuple-element.156), channel_id=1, source_target_pairs={{0,8},{1,9},{2,10},{3,11},{4,12},{5,13},{6,14},{7,15},{8,0},{9,1},... | collective-permute-start | bytes 49160 | tf_op jit(solution)/shard_map/ppermute | solution.py:272
  46.3 1.2 %collective-permute-start.25 = (bf16[32,512]{1,0:T(8,128)(2,1)S(1)}, bf16[32,512]{1,0:T(8,128)(2,1)S(1)}, u32[]{:S(2)}, u32[]{:S(2)}) collective-permute-start(bf16[32,512]{1,0:T(8,128)(2,1)S(1)} %collective-permute-done.18.refs_0_), channel_id=1, source_target_pairs={{0,1},{1,0},{2,3},{3,2},{4,5},{5,4},{6,7},{7,6},{8,9},{9,8},{10,11... | collective-permute-start | bytes 98312 | tf_op jit(solution)/shard_map/ppermute | solution.py:272
  47.5 2.0 %local_gradients.1 = (f32[256,512]{1,0:T(8,128)S(1)}, f32[64,512]{1,0:T(8,128)}, bf16[256,512]{1,0:T(8,128)(2,1)}) custom-call(bf16[256,512]{1,0:T(8,128)(2,1)S(1)} %copy-done.4, f32[400,512]{1,0:T(8,128)S(1)} %get-tuple-element.141.refs_1_, bf16[256,512]{1,0:T(8,128)(2,1)S(1)} %copy-done.5, bf16[400,512]{1,0:T(8,128)(2,1)S(1)} %get-tuple-element.142.refs_3_, ...), custom_call_target="tpu_custom_call" | custom-call | flops 402653184 | bytes 12042240 | tf_op jit(solution)/shard_map/local_gradients/pallas_call | solution.py:213
  49.6 1.0 %add_returned.1 = f32[256,512]{1,0:T(8,128)} custom-call(bf16[32,512]{1,0:T(8,128)(2,1)S(1)} %collective-permute-done.18.refs_0_, bf16[32,512]{1,0:T(8,128)(2,1)S(1)} %collective-permute-done.19.refs_1_, bf16[16,512]{1,0:T(8,128)(2,1)S(1)} %collective-permute-done.20.refs_2_, bf16[16,512]{1,0:T(8,128)(2,1)S(1)} %collective-permute-done.21.refs_3_, ...), custom_call_target="tpu_custom_call" | custom-call | flops 37748736 | bytes 1392640 | tf_op jit(solution)/shard_map/add_returned/pallas_call | solution.py:213
  (74 shorter events, 3.7 us)
Async XLA Ops:
  2.3 9.6 %collective-permute-start = (bf16[32,1024]{1,0:T(8,128)(2,1)S(1)}, bf16[32,1024]{1,0:T(8,128)(2,1)S(1)}, u32[]{:S(2)}, u32[]{:S(2)}) collective-permute-start(bf16[32,1024]{1,0:T(8,128)(2,1)S(1)} %get-tuple-element.90), channel_id=1, source_target_pairs={{0,12},{1,13},{2,14},{3,15},{4,8},{5,9},{6,10},{7,11},{8,4},{9,5},... | collective-permute-start | bytes 196616 | tf_op jit(solution)/shard_map/ppermute | solution.py:272
  7.4 7.7 %collective-permute-start.1 = (bf16[32,1024]{1,0:T(8,128)(2,1)S(1)}, bf16[32,1024]{1,0:T(8,128)(2,1)S(1)}, u32[]{:S(2)}, u32[]{:S(2)}) collective-permute-start(bf16[32,1024]{1,0:T(8,128)(2,1)S(1)} %get-tuple-element.93), channel_id=1, source_target_pairs={{0,4},{1,5},{2,6},{3,7},{4,0},{5,1},{6,2},{7,3},{8,12},{9,13},{10,... | collective-permute-start | bytes 196616 | tf_op jit(solution)/shard_map/ppermute | solution.py:272
  7.4 6.0 %collective-permute-start.2 = (bf16[16,1024]{1,0:T(8,128)(2,1)S(1)}, bf16[16,1024]{1,0:T(8,128)(2,1)S(1)}, u32[]{:S(2)}, u32[]{:S(2)}) collective-permute-start(bf16[16,1024]{1,0:T(8,128)(2,1)S(1)} %get-tuple-element.94), channel_id=1, source_target_pairs={{0,15},{1,2},{2,1},{3,4},{4,3},{5,6},{6,5},{7,8},{8,7},{9,10},{10,... | collective-permute-start | bytes 98312 | tf_op jit(solution)/shard_map/ppermute | solution.py:272
  8.2 5.6 %collective-permute-start.3 = (bf16[16,1024]{1,0:T(8,128)(2,1)S(1)}, bf16[16,1024]{1,0:T(8,128)(2,1)S(1)}, u32[]{:S(2)}, u32[]{:S(2)}) collective-permute-start(bf16[16,1024]{1,0:T(8,128)(2,1)S(1)} %get-tuple-element.95), channel_id=1, source_target_pairs={{0,3},{1,14},{2,5},{3,0},{4,7},{5,2},{6,9},{7,4},{8,11},{9,6},{10,... | collective-permute-start | bytes 98312 | tf_op jit(solution)/shard_map/ppermute | solution.py:272
  10.7 6.9 %collective-permute-start.4 = (bf16[16,1024]{1,0:T(8,128)(2,1)S(1)}, bf16[16,1024]{1,0:T(8,128)(2,1)S(1)}, u32[]{:S(2)}, u32[]{:S(2)}) collective-permute-start(bf16[16,1024]{1,0:T(8,128)(2,1)S(1)} %get-tuple-element.96), channel_id=1, source_target_pairs={{0,11},{1,6},{2,13},{3,8},{4,15},{5,10},{6,1},{7,12},{8,3},{9,14},... | collective-permute-start | bytes 98312 | tf_op jit(solution)/shard_map/ppermute | solution.py:272
  12.0 5.8 %collective-permute-start.5 = (bf16[16,1024]{1,0:T(8,128)(2,1)S(1)}, bf16[16,1024]{1,0:T(8,128)(2,1)S(1)}, u32[]{:S(2)}, u32[]{:S(2)}) collective-permute-start(bf16[16,1024]{1,0:T(8,128)(2,1)S(1)} %get-tuple-element.97), channel_id=1, source_target_pairs={{0,8},{1,9},{2,10},{3,11},{4,12},{5,13},{6,14},{7,15},{8,0},{9,1},... | collective-permute-start | bytes 98312 | tf_op jit(solution)/shard_map/ppermute | solution.py:272
  13.5 4.3 %collective-permute-start.6 = (bf16[16,1024]{1,0:T(8,128)(2,1)S(1)}, bf16[16,1024]{1,0:T(8,128)(2,1)S(1)}, u32[]{:S(2)}, u32[]{:S(2)}) collective-permute-start(bf16[16,1024]{1,0:T(8,128)(2,1)S(1)} %get-tuple-element.98), channel_id=1, source_target_pairs={{0,1},{1,0},{2,3},{3,2},{4,5},{5,4},{6,7},{7,6},{8,9},{9,8},{10,11... | collective-permute-start | bytes 98312 | tf_op jit(solution)/shard_map/ppermute | solution.py:272
  13.8 4.0 %collective-permute-start.7 = (bf16[32,1024]{1,0:T(8,128)(2,1)S(1)}, bf16[32,1024]{1,0:T(8,128)(2,1)S(1)}, u32[]{:S(2)}, u32[]{:S(2)}) collective-permute-start(bf16[32,1024]{1,0:T(8,128)(2,1)S(1)} %collective-permute-done.refs_0_), channel_id=1, source_target_pairs={{0,1},{1,0},{2,3},{3,2},{4,5},{5,4},{6,7},{7,6},{8,9},{9,8},{10,11... | collective-permute-start | bytes 196616 | tf_op jit(solution)/shard_map/ppermute | solution.py:272
  20.8 6.8 %collective-permute-start.9 = (bf16[32,1024]{1,0:T(8,128)(2,1)S(1)}, bf16[32,1024]{1,0:T(8,128)(2,1)S(1)}, u32[]{:S(2)}, u32[]{:S(2)}) collective-permute-start(bf16[32,1024]{1,0:T(8,128)(2,1)S(1)} %get-tuple-element.111), channel_id=1, source_target_pairs={{0,12},{1,13},{2,14},{3,15},{4,8},{5,9},{6,10},{7,11},{8,4},{9,5},... | collective-permute-start | bytes 196616 | tf_op jit(solution)/shard_map/ppermute | solution.py:272
  22.5 7.1 %collective-permute-start.10 = (bf16[32,1024]{1,0:T(8,128)(2,1)S(1)}, bf16[32,1024]{1,0:T(8,128)(2,1)S(1)}, u32[]{:S(2)}, u32[]{:S(2)}) collective-permute-start(bf16[32,1024]{1,0:T(8,128)(2,1)S(1)} %get-tuple-element.114), channel_id=1, source_target_pairs={{0,4},{1,5},{2,6},{3,7},{4,0},{5,1},{6,2},{7,3},{8,12},{9,13},{10,... | collective-permute-start | bytes 196616 | tf_op jit(solution)/shard_map/ppermute | solution.py:272
  22.5 6.0 %collective-permute-start.11 = (bf16[16,1024]{1,0:T(8,128)(2,1)S(1)}, bf16[16,1024]{1,0:T(8,128)(2,1)S(1)}, u32[]{:S(2)}, u32[]{:S(2)}) collective-permute-start(bf16[16,1024]{1,0:T(8,128)(2,1)S(1)} %get-tuple-element.115), channel_id=1, source_target_pairs={{0,15},{1,2},{2,1},{3,4},{4,3},{5,6},{6,5},{7,8},{8,7},{9,10},{10,... | collective-permute-start | bytes 98312 | tf_op jit(solution)/shard_map/ppermute | solution.py:272
  23.8 4.7 %collective-permute-start.12 = (bf16[16,1024]{1,0:T(8,128)(2,1)S(1)}, bf16[16,1024]{1,0:T(8,128)(2,1)S(1)}, u32[]{:S(2)}, u32[]{:S(2)}) collective-permute-start(bf16[16,1024]{1,0:T(8,128)(2,1)S(1)} %get-tuple-element.116), channel_id=1, source_target_pairs={{0,3},{1,14},{2,5},{3,0},{4,7},{5,2},{6,9},{7,4},{8,11},{9,6},{10,... | collective-permute-start | bytes 98312 | tf_op jit(solution)/shard_map/ppermute | solution.py:272
  25.7 6.9 %collective-permute-start.13 = (bf16[16,1024]{1,0:T(8,128)(2,1)S(1)}, bf16[16,1024]{1,0:T(8,128)(2,1)S(1)}, u32[]{:S(2)}, u32[]{:S(2)}) collective-permute-start(bf16[16,1024]{1,0:T(8,128)(2,1)S(1)} %get-tuple-element.117), channel_id=1, source_target_pairs={{0,11},{1,6},{2,13},{3,8},{4,15},{5,10},{6,1},{7,12},{8,3},{9,14},... | collective-permute-start | bytes 98312 | tf_op jit(solution)/shard_map/ppermute | solution.py:272
  27.6 5.0 %collective-permute-start.14 = (bf16[16,1024]{1,0:T(8,128)(2,1)S(1)}, bf16[16,1024]{1,0:T(8,128)(2,1)S(1)}, u32[]{:S(2)}, u32[]{:S(2)}) collective-permute-start(bf16[16,1024]{1,0:T(8,128)(2,1)S(1)} %get-tuple-element.118), channel_id=1, source_target_pairs={{0,8},{1,9},{2,10},{3,11},{4,12},{5,13},{6,14},{7,15},{8,0},{9,1},... | collective-permute-start | bytes 98312 | tf_op jit(solution)/shard_map/ppermute | solution.py:272
  28.5 4.1 %collective-permute-start.15 = (bf16[16,1024]{1,0:T(8,128)(2,1)S(1)}, bf16[16,1024]{1,0:T(8,128)(2,1)S(1)}, u32[]{:S(2)}, u32[]{:S(2)}) collective-permute-start(bf16[16,1024]{1,0:T(8,128)(2,1)S(1)} %get-tuple-element.119), channel_id=1, source_target_pairs={{0,1},{1,0},{2,3},{3,2},{4,5},{5,4},{6,7},{7,6},{8,9},{9,8},{10,11... | collective-permute-start | bytes 98312 | tf_op jit(solution)/shard_map/ppermute | solution.py:272
  28.5 4.1 %collective-permute-start.16 = (bf16[32,1024]{1,0:T(8,128)(2,1)S(1)}, bf16[32,1024]{1,0:T(8,128)(2,1)S(1)}, u32[]{:S(2)}, u32[]{:S(2)}) collective-permute-start(bf16[32,1024]{1,0:T(8,128)(2,1)S(1)} %collective-permute-done.9.refs_0_), channel_id=1, source_target_pairs={{0,1},{1,0},{2,3},{3,2},{4,5},{5,4},{6,7},{7,6},{8,9},{9,8},{10,11... | collective-permute-start | bytes 196616 | tf_op jit(solution)/shard_map/ppermute | solution.py:272
  38.0 6.6 %collective-permute-start.18 = (bf16[32,512]{1,0:T(8,128)(2,1)S(1)}, bf16[32,512]{1,0:T(8,128)(2,1)S(1)}, u32[]{:S(2)}, u32[]{:S(2)}) collective-permute-start(bf16[32,512]{1,0:T(8,128)(2,1)S(1)} %get-tuple-element.149), channel_id=1, source_target_pairs={{0,12},{1,13},{2,14},{3,15},{4,8},{5,9},{6,10},{7,11},{8,4},{9,5},... | collective-permute-start | bytes 98312 | tf_op jit(solution)/shard_map/ppermute | solution.py:272
  39.9 7.6 %collective-permute-start.19 = (bf16[32,512]{1,0:T(8,128)(2,1)S(1)}, bf16[32,512]{1,0:T(8,128)(2,1)S(1)}, u32[]{:S(2)}, u32[]{:S(2)}) collective-permute-start(bf16[32,512]{1,0:T(8,128)(2,1)S(1)} %get-tuple-element.152), channel_id=1, source_target_pairs={{0,4},{1,5},{2,6},{3,7},{4,0},{5,1},{6,2},{7,3},{8,12},{9,13},{10,... | collective-permute-start | bytes 98312 | tf_op jit(solution)/shard_map/ppermute | solution.py:272
  40.2 5.9 %collective-permute-start.20 = (bf16[16,512]{1,0:T(8,128)(2,1)S(1)}, bf16[16,512]{1,0:T(8,128)(2,1)S(1)}, u32[]{:S(2)}, u32[]{:S(2)}) collective-permute-start(bf16[16,512]{1,0:T(8,128)(2,1)S(1)} %get-tuple-element.153), channel_id=1, source_target_pairs={{0,15},{1,2},{2,1},{3,4},{4,3},{5,6},{6,5},{7,8},{8,7},{9,10},{10,... | collective-permute-start | bytes 49160 | tf_op jit(solution)/shard_map/ppermute | solution.py:272
  41.7 4.6 %collective-permute-start.21 = (bf16[16,512]{1,0:T(8,128)(2,1)S(1)}, bf16[16,512]{1,0:T(8,128)(2,1)S(1)}, u32[]{:S(2)}, u32[]{:S(2)}) collective-permute-start(bf16[16,512]{1,0:T(8,128)(2,1)S(1)} %get-tuple-element.154), channel_id=1, source_target_pairs={{0,3},{1,14},{2,5},{3,0},{4,7},{5,2},{6,9},{7,4},{8,11},{9,6},{10,... | collective-permute-start | bytes 49160 | tf_op jit(solution)/shard_map/ppermute | solution.py:272
  43.1 6.4 %collective-permute-start.22 = (bf16[16,512]{1,0:T(8,128)(2,1)S(1)}, bf16[16,512]{1,0:T(8,128)(2,1)S(1)}, u32[]{:S(2)}, u32[]{:S(2)}) collective-permute-start(bf16[16,512]{1,0:T(8,128)(2,1)S(1)} %get-tuple-element.155), channel_id=1, source_target_pairs={{0,11},{1,6},{2,13},{3,8},{4,15},{5,10},{6,1},{7,12},{8,3},{9,14},... | collective-permute-start | bytes 49160 | tf_op jit(solution)/shard_map/ppermute | solution.py:272
  44.6 5.0 %collective-permute-start.23 = (bf16[16,512]{1,0:T(8,128)(2,1)S(1)}, bf16[16,512]{1,0:T(8,128)(2,1)S(1)}, u32[]{:S(2)}, u32[]{:S(2)}) collective-permute-start(bf16[16,512]{1,0:T(8,128)(2,1)S(1)} %get-tuple-element.156), channel_id=1, source_target_pairs={{0,8},{1,9},{2,10},{3,11},{4,12},{5,13},{6,14},{7,15},{8,0},{9,1},... | collective-permute-start | bytes 49160 | tf_op jit(solution)/shard_map/ppermute | solution.py:272
  46.0 3.5 %collective-permute-start.24 = (bf16[16,512]{1,0:T(8,128)(2,1)S(1)}, bf16[16,512]{1,0:T(8,128)(2,1)S(1)}, u32[]{:S(2)}, u32[]{:S(2)}) collective-permute-start(bf16[16,512]{1,0:T(8,128)(2,1)S(1)} %get-tuple-element.157), channel_id=1, source_target_pairs={{0,1},{1,0},{2,3},{3,2},{4,5},{5,4},{6,7},{7,6},{8,9},{9,8},{10,11... | collective-permute-start | bytes 49160 | tf_op jit(solution)/shard_map/ppermute | solution.py:272
  46.3 3.3 %collective-permute-start.25 = (bf16[32,512]{1,0:T(8,128)(2,1)S(1)}, bf16[32,512]{1,0:T(8,128)(2,1)S(1)}, u32[]{:S(2)}, u32[]{:S(2)}) collective-permute-start(bf16[32,512]{1,0:T(8,128)(2,1)S(1)} %collective-permute-done.18.refs_0_), channel_id=1, source_target_pairs={{0,1},{1,0},{2,3},{3,2},{4,5},{5,4},{6,7},{7,6},{8,9},{9,8},{10,11... | collective-permute-start | bytes 98312 | tf_op jit(solution)/shard_map/ppermute | solution.py:272
  (21 other events, 237.8 us)

commit v14 on v12

--- a/solution.py
+++ b/solution.py
@@ -233,72 +233,68 @@
         pairs = [(s, (s + rows[s // TW % 2][s % 2]) % peer_count) for s in peers]
         return lax.ppermute(part, "tile", pairs)
 
+    planes = peer_count // TW
+
+    def plane(step):
+        return lax.rem(lax.div(lax.axis_index("tile"), TW) + (planes + step), planes)
+
+    def pass_rows(planes_ref, passed_ref):
+        passed_ref[:width, :] = planes_ref[plane(-1), width:, :]
+        passed_ref[width:, :] = planes_ref[plane(1), width:, :]
+
     def exchange(parts):
-        late_pair, early_pair, behind_one, ahead_three, five_off, opposite, own_chip = parts
-        late_pair = permute(late_pair, (-4, -4), (4, 4))
-        early_pair = permute(early_pair, (4, 4), (-4, -4))
+        to_planes, behind_one, ahead_three, five_off, own_chip = parts
+        columns = to_planes.shape[2]
+        to_planes = lax.all_to_all(
+            to_planes,
+            "tile",
+            split_axis=0,
+            concat_axis=0,
+            tiled=True,
+            axis_index_groups=[[z * TW + row for z in range(planes)] for row in range(TW)],
+        )
         behind_one = permute(behind_one, (-1, 1))
         ahead_three = permute(ahead_three, (3, -3))
         five_off = permute(five_off, (-5, 5))
-        opposite = permute(opposite, (peer_count // 2, peer_count // 2))
-        late_pair, own_chip = lax.optimization_barrier((late_pair, own_chip))
-        late_passed = permute(late_pair, (1, -1))
         own_chip = permute(own_chip, (1, -1))
-        early_passed = permute(early_pair, (1, -1))
-        return [
-            late_pair,
-            early_pair,
-            behind_one,
-            ahead_three,
-            five_off,
-            opposite,
-            own_chip,
-            late_passed,
-            early_passed,
-        ]
-
-    arrived_count = 9
+        (passed,) = call(pass_rows, "pass_rows", [to_planes], [((2 * width, columns), BF16)])
+        passed = permute(passed, (1, -1))
+        return [to_planes, behind_one, ahead_three, five_off, own_chip, passed]
+
+    arrived_count = 6
 
     def sent_shapes(columns):
-        rows = (2, 2, 1, 1, 1, 1, 1)
-        return [((count * width, columns), BF16) for count in rows]
+        return [((planes, 2 * width, columns), BF16)] + [((width, columns), BF16)] * 4
 
     sent_count = len(sent_shapes(feat))
 
-    def place_bits():
-        own = lax.axis_index("tile")
-        return lax.rem(own, 2) == 1, lax.rem(lax.div(own, TW), 2) == 1
-
     def send(refs, message, columns=slice(None)):
-        odd, odd_row = place_bits()
+        odd = lax.rem(lax.axis_index("tile"), 2) == 1
 
         def by_parity(even, odd_one):
             return jnp.where(odd, message(odd_one), message(even))
 
-        late_pair, early_pair, behind_one, ahead_three, five_off, opposite, own_chip = refs
+        to_planes, behind_one, ahead_three, five_off, own_chip = refs
         first, second = slice(0, width), slice(width, 2 * width)
-        ahead = message(four), by_parity(five, three)
-        behind = message(minus[four]), by_parity(minus[three], minus[five])
-        for rows, go_ahead, go_behind in zip((first, second), ahead, behind):
-            late_pair[rows, columns] = jnp.where(odd_row, go_ahead, go_behind)
-            early_pair[rows, columns] = jnp.where(odd_row, go_behind, go_ahead)
+        if columns.start in (None, 0):
+            to_planes[...] = jnp.zeros(to_planes.shape, BF16)
+        to_planes[plane(1), first, columns] = message(four)
+        to_planes[plane(1), second, columns] = by_parity(five, three)
+        to_planes[plane(-1), first, columns] = message(minus[four])
+        to_planes[plane(-1), second, columns] = by_parity(minus[three], minus[five])
+        to_planes[plane(planes // 2), first, columns] = message(across)
         behind_one[:, columns] = by_parity(minus[one], one)
         ahead_three[:, columns] = by_parity(three, minus[three])
         five_off[:, columns] = by_parity(minus[five], five)
-        opposite[:, columns] = message(across)
         own_chip[:, columns] = by_parity(one, minus[one])
 
     def receive(refs, columns=slice(None)):
-        odd, odd_row = place_bits()
-        late_pair, early_pair, behind_one, ahead_three, five_off, opposite, own_chip = refs[:7]
-        late_passed, early_passed = refs[7:]
+        odd = lax.rem(lax.axis_index("tile"), 2) == 1
+        from_planes, behind_one, ahead_three, five_off, own_chip, passed = refs
         first, second = slice(0, width), slice(width, 2 * width)
         near, near_three = behind_one[:, columns], ahead_three[:, columns]
         far, own = five_off[:, columns], own_chip[:, columns]
-        late_rows, early_rows = late_passed[second, columns], early_passed[second, columns]
-        from_behind = jnp.where(odd_row, early_rows, late_rows)
-        from_ahead = jnp.where(odd_row, late_rows, early_rows)
-        late_rows, early_rows = late_pair[first, columns], early_pair[first, columns]
+        from_behind, from_ahead = passed[first, columns], passed[second, columns]
         slot_rows = [None] * links
         slot_rows[one] = jnp.where(odd, own, near)
         slot_rows[minus[one]] = jnp.where(odd, near, own)
@@ -306,9 +302,9 @@
         slot_rows[minus[three]] = jnp.where(odd, from_ahead, near_three)
         slot_rows[five] = jnp.where(odd, from_behind, far)
         slot_rows[minus[five]] = jnp.where(odd, far, from_ahead)
-        slot_rows[four] = jnp.where(odd_row, early_rows, late_rows)
-        slot_rows[minus[four]] = jnp.where(odd_row, late_rows, early_rows)
-        slot_rows[across] = opposite[:, columns]
+        slot_rows[four] = from_planes[plane(-1), first, columns]
+        slot_rows[minus[four]] = from_planes[plane(1), first, columns]
+        slot_rows[across] = from_planes[plane(planes // 2), first, columns]
         return slot_rows
 
     def by_slot(refs, columns=slice(None)):

time: 50.8 us -> 128 us (2.52); the launches traced: 50.6 us -> 126 us
  local copies, waits for them, and re-layouts: 0.11 us -> 58.9 us
  waiting for transfers between devices: 2.62 us -> 9.47 us
  Pallas kernels: 18 us -> 24.4 us
  starting transfers between devices: 28.9 us -> 31.8 us
    unnamed x36 -> x192, local copies, waits for them, and re-layouts: 0.11 us -> 58.9 us
    all_to_all x0 -> x3, starting transfers between devices: none -> 13.9 us  [exchange(): lax.all_to_all(to_planes, 'tile', split_axis=0, concat_axis=0, tiled=True...]
    ppermute x27 -> x15, starting transfers between devices: 28.9 us -> 18 us  [permute(): return lax.ppermute(part, 'tile', pairs)]
    all_to_all x0 -> x3, waiting for transfers between devices: none -> 9.43 us  [exchange(): lax.all_to_all(to_planes, 'tile', split_axis=0, concat_axis=0, tiled=True...]
    pallas_call x8 -> x11, Pallas kernels: 18 us -> 24.4 us  [call(): pl.pallas_call(kernel, name=name, in_specs=specs, out_specs=[pl.BlockSpec...]
    ppermute x27 -> x15, waiting for transfers between devices: 2.62 us -> 0.04 us  [permute(): return lax.ppermute(part, 'tile', pairs)]
  transfers between devices with their start and end apart: 27 -> 18, of which waited for: 6 -> 3; matrix products, arithmetic and copies ran while one was open for 0% -> 0% of each run, Pallas kernels for 14% -> 8%
where the time goes in v14:
time: 128 us; the launch traced here: 126 us
  local copies, waits for them, and re-layouts  58.9 us (46%)
  starting transfers between devices  31.8 us (25%)
  Pallas kernels  24.4 us (19%)
  waiting for transfers between devices  9.47 us (7%)
    unnamed x192, local copies, waits for them, and re-layouts  58.9 us
    pallas_call x11, Pallas kernels, call(): pl.pallas_call(kernel, name=name, in_specs=specs, out_specs=[pl.BlockSpec...  24.4 us
    ppermute x15, starting transfers between devices, permute(): return lax.ppermute(part, 'tile', pairs)  18 us
    all_to_all x3, starting transfers between devices, exchange(): lax.all_to_all(to_planes, 'tile', split_axis=0, concat_axis=0, tiled=True...  13.9 us
    all_to_all x3, waiting for transfers between devices, exchange(): lax.all_to_all(to_planes, 'tile', split_axis=0, concat_axis=0, tiled=True...  9.43 us
  transfers between devices with their start and end apart: 18, of which 3 were waited for; matrix products, arithmetic and copies ran while one was open for 0% of the time, Pallas kernels for 8%

profile of v14, /device:TPU:0, one launch (start us, length us, event | category | flops | bytes accessed | tf_op | source)
XLA Modules:
  0.0 125.9 jit_solution(11209440430589884148)
XLA Ops:
  0.6 2.0 %pack_rows.1 = (bf16[256,256]{1,0:T(8,128)(2,1)S(1)}, bf16[4,32,1024]{2,1,0:T(8,128)(2,1)S(1)}, bf16[16,1024]{1,0:T(8,128)(2,1)}, bf16[16,1024]{1,0:T(8,128)(2,1...) custom-call(s32[9,16]{1,0:T(8,128)} %refs_0_.2, s32[9]{0:T(128)} %refs_1_.2, bf16[256,512]{1,0:T(8,128)(2,1)} %refs_0_.3, ...), custom_call_target="tpu_custom_call" | custom-call | flops 75497472 | bytes 1049188 | tf_op jit(solution)/shard_map/pack_rows/pallas_call | solution.py:175
  6.5 6.3 %all-to-all-start = ((bf16[4,32,1024]{2,1,0:T(8,128)(2,1)}), bf16[4,32,1024]{2,1,0:T(8,128)(2,1)}, u32[]{:S(2)}, u32[]{:S(2)}) async-start(bf16[4,32,1024]{2,1,0:T(8,128)(2,1)} %copy-done.61), calls=%async_computation | async-start | bytes 524288 | tf_op jit(solution)/shard_map/all_to_all | solution.py:248
  12.8 3.7 %collective-permute-start = (bf16[16,1024]{1,0:T(8,128)(2,1)}, bf16[16,1024]{1,0:T(8,128)(2,1)S(1)}, u32[]{:S(2)}, u32[]{:S(2)}) collective-permute-start(bf16[16,1024]{1,0:T(8,128)(2,1)} %get-tuple-element.75), channel_id=1, source_target_pairs={{0,15},{1,2},{2,1},{3,4},{4,3},{5,6},{6,5},{7,8},{8,7},{9,10},{10,... | collective-permute-start | bytes 98312 | tf_op jit(solution)/shard_map/ppermute | solution.py:234
  16.5 1.3 %collective-permute-start.2 = (bf16[16,1024]{1,0:T(8,128)(2,1)}, bf16[16,1024]{1,0:T(8,128)(2,1)}, u32[]{:S(2)}, u32[]{:S(2)}) collective-permute-start(bf16[16,1024]{1,0:T(8,128)(2,1)} %copy-done.90), channel_id=1, source_target_pairs={{0,11},{1,6},{2,13},{3,8},{4,15},{5,10},{6,1},{7,12},{8,3},{9,14},... | collective-permute-start | bytes 98312 | tf_op jit(solution)/shard_map/ppermute | solution.py:234
  18.6 4.3 %all-to-all-done.refs_0_ = bf16[4,32,1024]{2,1,0:T(8,128)(2,1)} async-done(((bf16[4,32,1024]{2,1,0:T(8,128)(2,1)}), bf16[4,32,1024]{2,1,0:T(8,128)(2,1)}, u32[]{:S(2)}, u32[]{:S(2)}) %all-to-all-start) | async-done | bytes 262176 | tf_op jit(solution)/shard_map/all_to_all | solution.py:248
  24.0 1.2 copy-done.2
  31.3 2.3 %local_products.1 = (f32[384,512]{1,0:T(8,128)S(1)}, f32[768,512]{1,0:T(8,128)S(1)}, f32[64,512]{1,0:T(8,128)S(1)}, bf16[384,512]{1,0:T(8,128)(2,1)S(1)}, bf16[5...) custom-call(bf16[256,256]{1,0:T(8,128)(2,1)S(1)} %copy-done.69, ...), custom_call_target="tpu_custom_call" | custom-call | flops 1275068416 | bytes 14713856 | tf_op jit(solution)/shard_map/local_products/pallas_call | solution.py:175
  37.0 3.8 %edges_forward.1 = (bf16[4,32,1024]{2,1,0:T(8,128)(2,1)S(1)}, bf16[16,1024]{1,0:T(8,128)(2,1)S(1)}, bf16[16,1024]{1,0:T(8,128)(2,1)S(1)}, bf16[16,1024]{1,0:T(8,...) custom-call(bf16[4,32,1024]{2,1,0:T(8,128)(2,1)} %all-to-all-done.re, ...), custom_call_target="tpu_custom_call" | custom-call | flops 1207959552 | bytes 16970496 | tf_op jit(solution)/shard_map/edges_forward/pallas_call | solution.py:175
  41.8 1.1 copy-done.31
  51.3 4.2 %all-to-all-start.1 = ((bf16[4,32,1024]{2,1,0:T(8,128)(2,1)}), bf16[4,32,1024]{2,1,0:T(8,128)(2,1)}, u32[]{:S(2)}, u32[]{:S(2)}) async-start(bf16[4,32,1024]{2,1,0:T(8,128)(2,1)} %copy-done.60), calls=%async_computation.1 | async-start | bytes 524288 | tf_op jit(solution)/shard_map/all_to_all | solution.py:248
  55.5 4.7 %collective-permute-start.5 = (bf16[16,1024]{1,0:T(8,128)(2,1)}, bf16[16,1024]{1,0:T(8,128)(2,1)}, u32[]{:S(2)}, u32[]{:S(2)}) collective-permute-start(bf16[16,1024]{1,0:T(8,128)(2,1)} %copy-done.88), channel_id=1, source_target_pairs={{0,15},{1,2},{2,1},{3,4},{4,3},{5,6},{6,5},{7,8},{8,7},{9,10},{10,... | collective-permute-start | bytes 98312 | tf_op jit(solution)/shard_map/ppermute | solution.py:234
  61.4 4.9 %all-to-all-done.1.refs_0_ = bf16[4,32,1024]{2,1,0:T(8,128)(2,1)} async-done(((bf16[4,32,1024]{2,1,0:T(8,128)(2,1)}), bf16[4,32,1024]{2,1,0:T(8,128)(2,1)}, u32[]{:S(2)}, u32[]{:S(2)}) %all-to-all-start.1) | async-done | bytes 262176 | tf_op jit(solution)/shard_map/all_to_all | solution.py:248
  67.2 1.2 copy-done.6
  68.4 1.2 copy-done.7
  73.8 1.4 %copy-done.32 = f32[768,512]{1,0:T(8,128)S(1)} copy-done((f32[768,512]{1,0:T(8,128)S(1)}, f32[768,512]{1,0:T(8,128)}, u32[]{:S(2)}) %copy-start.32) | copy-done | bytes 1572888
  82.3 4.1 %slopes_and_nodes.1 = (f32[400,512]{1,0:T(8,128)S(1)}, bf16[400,512]{1,0:T(8,128)(2,1)S(1)}, f32[400,512]{1,0:T(8,128)S(1)}, bf16[512,1024]{1,0:T(8,128)(2,1)S(1...) custom-call(bf16[4,32,1024]{2,1,0:T(8,128)(2,1)} %all-to-all-done.re, ...), custom_call_target="tpu_custom_call" | custom-call | flops 1677721600 | bytes 13585408 | tf_op jit(solution)/shard_map/slopes_and_nodes/pallas_call | solution.py:175
  86.6 6.4 %edges_backward.1 = (bf16[4,32,512]{2,1,0:T(8,128)(2,1)S(1)}, bf16[16,512]{1,0:T(8,128)(2,1)S(1)}, bf16[16,512]{1,0:T(8,128)(2,1)S(1)}, bf16[16,512]{1,0:T(8,128...) custom-call(bf16[4,32,1024]{2,1,0:T(8,128)(2,1)} %all-to-all-done.1., ...), custom_call_target="tpu_custom_call" | custom-call | flops 2449473536 | bytes 21661440 | tf_op jit(solution)/shard_map/edges_backward/pallas_call | solution.py:175
  100.6 3.3 %all-to-all-start.2 = ((bf16[4,32,512]{2,1,0:T(8,128)(2,1)}), bf16[4,32,512]{2,1,0:T(8,128)(2,1)S(1)}, u32[]{:S(2)}, u32[]{:S(2)}) async-start(bf16[4,32,512]{2,1,0:T(8,128)(2,1)} %copy-done.76), calls=%async_computation.2 | async-start | bytes 262144 | tf_op jit(solution)/shard_map/all_to_all | solution.py:248
  104.0 5.2 %collective-permute-start.10 = (bf16[16,512]{1,0:T(8,128)(2,1)}, bf16[16,512]{1,0:T(8,128)(2,1)S(1)}, u32[]{:S(2)}, u32[]{:S(2)}) collective-permute-start(bf16[16,512]{1,0:T(8,128)(2,1)} %copy-done.95), channel_id=1, source_target_pairs={{0,15},{1,2},{2,1},{3,4},{4,3},{5,6},{6,5},{7,8},{8,7},{9,10},{10,... | collective-permute-start | bytes 49160 | tf_op jit(solution)/shard_map/ppermute | solution.py:234
  110.6 1.2 copy-done.4
  111.8 1.2 copy-done.9
  116.1 1.1 copy-done.36
  122.1 2.0 %local_gradients.1 = (f32[256,512]{1,0:T(8,128)S(1)}, f32[64,512]{1,0:T(8,128)}, bf16[256,512]{1,0:T(8,128)(2,1)}) custom-call(bf16[256,512]{1,0:T(8,128)(2,1)S(1)} %copy-done.13, f32[400,512]{1,0:T(8,128)S(1)} %copy-done.36, bf16[256,512]{1,0:T(8,128)(2,1)S(1)} %copy-done.22, bf16[400,512]{1,0:T(8,128)(2,1)S(1)} %copy-done.47, ...), custom_call_target="tpu_custom_call" | custom-call | flops 402653184 | bytes 12042240 | tf_op jit(solution)/shard_map/local_gradients/pallas_call | solution.py:175
  124.1 1.8 %add_returned.1 = f32[256,512]{1,0:T(8,128)} custom-call(bf16[4,32,512]{2,1,0:T(8,128)(2,1)S(1)} %all-to-all-done.2.refs_0_, bf16[16,512]{1,0:T(8,128)(2,1)S(1)} %collective-permute-done.10.refs_1_, bf16[16,512]{1,0:T(8,128)(2,1)} %collective-permute-done.11.refs_2_, bf16[16,512]{1,0:T(8,128)(2,1)} %collective-permute-done.12.refs_3_, ...), custom_call_target="tpu_custom_call" | custom-call | flops 37748736 | bytes 1409024 | tf_op jit(solution)/shard_map/add_returned/pallas_call | solution.py:175
  (215 shorter events, 54.4 us)
Async XLA Ops:
  5.2 18.7 %copy-start.13 = (bf16[256,512]{1,0:T(8,128)(2,1)S(1)}, bf16[256,512]{1,0:T(8,128)(2,1)}, u32[]{:S(2)}) copy-start(bf16[256,512]{1,0:T(8,128)(2,1)} %refs_0_.3) | copy-start | bytes 786436
  5.2 18.7 %copy-start.55 = (bf16[64,512]{1,0:T(8,128)(2,1)S(1)}, bf16[64,512]{1,0:T(8,128)(2,1)}, u32[]{:S(2)}) copy-start(bf16[64,512]{1,0:T(8,128)(2,1)} %refs_12_.4) | copy-start | bytes 196612
  5.2 18.7 %copy-start.81 = (s32[768]{0:T(1024)S(1)}, s32[768]{0:T(1024)}, u32[]{:S(2)}) copy-start(s32[768]{0:T(1024)} %refs_10_.3) | copy-start | bytes 9220
  5.2 18.7 %copy-start.82 = (s32[768]{0:T(1024)S(1)}, s32[768]{0:T(1024)}, u32[]{:S(2)}) copy-start(s32[768]{0:T(1024)} %refs_11_.4) | copy-start | bytes 9220
  5.3 18.7 %copy-start.83 = (s32[384]{0:T(512)S(1)}, s32[384]{0:T(512)}, u32[]{:S(2)}) copy-start(s32[384]{0:T(512)} %refs_8_.2) | copy-start | bytes 4612
  5.3 18.7 %copy-start.84 = (s32[384]{0:T(512)S(1)}, s32[384]{0:T(512)}, u32[]{:S(2)}) copy-start(s32[384]{0:T(512)} %refs_9_.2) | copy-start | bytes 4612
  6.5 16.4 %all-to-all-start = ((bf16[4,32,1024]{2,1,0:T(8,128)(2,1)}), bf16[4,32,1024]{2,1,0:T(8,128)(2,1)}, u32[]{:S(2)}, u32[]{:S(2)}) async-start(bf16[4,32,1024]{2,1,0:T(8,128)(2,1)} %copy-done.61), calls=%async_computation | async-start | bytes 524288 | tf_op jit(solution)/shard_map/all_to_all | solution.py:248
  12.8 20.8 %collective-permute-start = (bf16[16,1024]{1,0:T(8,128)(2,1)}, bf16[16,1024]{1,0:T(8,128)(2,1)S(1)}, u32[]{:S(2)}, u32[]{:S(2)}) collective-permute-start(bf16[16,1024]{1,0:T(8,128)(2,1)} %get-tuple-element.75), channel_id=1, source_target_pairs={{0,15},{1,2},{2,1},{3,4},{4,3},{5,6},{6,5},{7,8},{8,7},{9,10},{10,... | collective-permute-start | bytes 98312 | tf_op jit(solution)/shard_map/ppermute | solution.py:234
  16.5 17.9 %collective-permute-start.1 = (bf16[16,1024]{1,0:T(8,128)(2,1)}, bf16[16,1024]{1,0:T(8,128)(2,1)S(1)}, u32[]{:S(2)}, u32[]{:S(2)}) collective-permute-start(bf16[16,1024]{1,0:T(8,128)(2,1)} %copy-done.91), channel_id=1, source_target_pairs={{0,3},{1,14},{2,5},{3,0},{4,7},{5,2},{6,9},{7,4},{8,11},{9,6},{10,... | collective-permute-start | bytes 98312 | tf_op jit(solution)/shard_map/ppermute | solution.py:234
  16.5 18.9 %collective-permute-start.2 = (bf16[16,1024]{1,0:T(8,128)(2,1)}, bf16[16,1024]{1,0:T(8,128)(2,1)}, u32[]{:S(2)}, u32[]{:S(2)}) collective-permute-start(bf16[16,1024]{1,0:T(8,128)(2,1)} %copy-done.90), channel_id=1, source_target_pairs={{0,11},{1,6},{2,13},{3,8},{4,15},{5,10},{6,1},{7,12},{8,3},{9,14},... | collective-permute-start | bytes 98312 | tf_op jit(solution)/shard_map/ppermute | solution.py:234
  17.8 17.5 %collective-permute-start.3 = (bf16[16,1024]{1,0:T(8,128)(2,1)}, bf16[16,1024]{1,0:T(8,128)(2,1)}, u32[]{:S(2)}, u32[]{:S(2)}) collective-permute-start(bf16[16,1024]{1,0:T(8,128)(2,1)} %copy-done.89), channel_id=1, source_target_pairs={{0,1},{1,0},{2,3},{3,2},{4,5},{5,4},{6,7},{7,6},{8,9},{9,8},{10,11... | collective-permute-start | bytes 98312 | tf_op jit(solution)/shard_map/ppermute | solution.py:234
  23.9 11.5 %collective-permute-start.4 = (bf16[32,1024]{1,0:T(8,128)(2,1)S(1)}, bf16[32,1024]{1,0:T(8,128)(2,1)S(1)}, u32[]{:S(2)}, u32[]{:S(2)}) collective-permute-start(bf16[32,1024]{1,0:T(8,128)(2,1)S(1)} %pass_rows.3), channel_id=1, source_target_pairs={{0,1},{1,0},{2,3},{3,2},{4,5},{5,4},{6,7},{7,6},{8,9},{9,8},{10,11... | collective-permute-start | bytes 196616 | tf_op jit(solution)/shard_map/ppermute | solution.py:234
  51.3 15.0 %all-to-all-start.1 = ((bf16[4,32,1024]{2,1,0:T(8,128)(2,1)}), bf16[4,32,1024]{2,1,0:T(8,128)(2,1)}, u32[]{:S(2)}, u32[]{:S(2)}) async-start(bf16[4,32,1024]{2,1,0:T(8,128)(2,1)} %copy-done.60), calls=%async_computation.1 | async-start | bytes 524288 | tf_op jit(solution)/shard_map/all_to_all | solution.py:248
  55.5 30.9 %collective-permute-start.5 = (bf16[16,1024]{1,0:T(8,128)(2,1)}, bf16[16,1024]{1,0:T(8,128)(2,1)}, u32[]{:S(2)}, u32[]{:S(2)}) collective-permute-start(bf16[16,1024]{1,0:T(8,128)(2,1)} %copy-done.88), channel_id=1, source_target_pairs={{0,15},{1,2},{2,1},{3,4},{4,3},{5,6},{6,5},{7,8},{8,7},{9,10},{10,... | collective-permute-start | bytes 98312 | tf_op jit(solution)/shard_map/ppermute | solution.py:234
  60.2 26.2 %collective-permute-start.6 = (bf16[16,1024]{1,0:T(8,128)(2,1)}, bf16[16,1024]{1,0:T(8,128)(2,1)}, u32[]{:S(2)}, u32[]{:S(2)}) collective-permute-start(bf16[16,1024]{1,0:T(8,128)(2,1)} %copy-done.87), channel_id=1, source_target_pairs={{0,3},{1,14},{2,5},{3,0},{4,7},{5,2},{6,9},{7,4},{8,11},{9,6},{10,... | collective-permute-start | bytes 98312 | tf_op jit(solution)/shard_map/ppermute | solution.py:234
  60.2 26.2 %collective-permute-start.7 = (bf16[16,1024]{1,0:T(8,128)(2,1)}, bf16[16,1024]{1,0:T(8,128)(2,1)}, u32[]{:S(2)}, u32[]{:S(2)}) collective-permute-start(bf16[16,1024]{1,0:T(8,128)(2,1)} %copy-done.86), channel_id=1, source_target_pairs={{0,11},{1,6},{2,13},{3,8},{4,15},{5,10},{6,1},{7,12},{8,3},{9,14},... | collective-permute-start | bytes 98312 | tf_op jit(solution)/shard_map/ppermute | solution.py:234
  61.1 25.4 %collective-permute-start.8 = (bf16[16,1024]{1,0:T(8,128)(2,1)}, bf16[16,1024]{1,0:T(8,128)(2,1)}, u32[]{:S(2)}, u32[]{:S(2)}) collective-permute-start(bf16[16,1024]{1,0:T(8,128)(2,1)} %copy-done.85), channel_id=1, source_target_pairs={{0,1},{1,0},{2,3},{3,2},{4,5},{5,4},{6,7},{7,6},{8,9},{9,8},{10,11... | collective-permute-start | bytes 98312 | tf_op jit(solution)/shard_map/ppermute | solution.py:234
  67.2 19.3 %collective-permute-start.9 = (bf16[32,1024]{1,0:T(8,128)(2,1)S(1)}, bf16[32,1024]{1,0:T(8,128)(2,1)S(1)}, u32[]{:S(2)}, u32[]{:S(2)}) collective-permute-start(bf16[32,1024]{1,0:T(8,128)(2,1)S(1)} %pass_rows.4), channel_id=1, source_target_pairs={{0,1},{1,0},{2,3},{3,2},{4,5},{5,4},{6,7},{7,6},{8,9},{9,8},{10,11... | collective-permute-start | bytes 196616 | tf_op jit(solution)/shard_map/ppermute | solution.py:234
  100.6 9.9 %all-to-all-start.2 = ((bf16[4,32,512]{2,1,0:T(8,128)(2,1)}), bf16[4,32,512]{2,1,0:T(8,128)(2,1)S(1)}, u32[]{:S(2)}, u32[]{:S(2)}) async-start(bf16[4,32,512]{2,1,0:T(8,128)(2,1)} %copy-done.76), calls=%async_computation.2 | async-start | bytes 262144 | tf_op jit(solution)/shard_map/all_to_all | solution.py:248
  104.0 20.1 %collective-permute-start.10 = (bf16[16,512]{1,0:T(8,128)(2,1)}, bf16[16,512]{1,0:T(8,128)(2,1)S(1)}, u32[]{:S(2)}, u32[]{:S(2)}) collective-permute-start(bf16[16,512]{1,0:T(8,128)(2,1)} %copy-done.95), channel_id=1, source_target_pairs={{0,15},{1,2},{2,1},{3,4},{4,3},{5,6},{6,5},{7,8},{8,7},{9,10},{10,... | collective-permute-start | bytes 49160 | tf_op jit(solution)/shard_map/ppermute | solution.py:234
  109.2 14.9 %collective-permute-start.11 = (bf16[16,512]{1,0:T(8,128)(2,1)}, bf16[16,512]{1,0:T(8,128)(2,1)}, u32[]{:S(2)}, u32[]{:S(2)}) collective-permute-start(bf16[16,512]{1,0:T(8,128)(2,1)} %copy-done.94), channel_id=1, source_target_pairs={{0,3},{1,14},{2,5},{3,0},{4,7},{5,2},{6,9},{7,4},{8,11},{9,6},{10,... | collective-permute-start | bytes 49160 | tf_op jit(solution)/shard_map/ppermute | solution.py:234
  109.2 14.9 %collective-permute-start.12 = (bf16[16,512]{1,0:T(8,128)(2,1)}, bf16[16,512]{1,0:T(8,128)(2,1)}, u32[]{:S(2)}, u32[]{:S(2)}) collective-permute-start(bf16[16,512]{1,0:T(8,128)(2,1)} %copy-done.93), channel_id=1, source_target_pairs={{0,11},{1,6},{2,13},{3,8},{4,15},{5,10},{6,1},{7,12},{8,3},{9,14},... | collective-permute-start | bytes 49160 | tf_op jit(solution)/shard_map/ppermute | solution.py:234
  110.0 14.1 %collective-permute-start.13 = (bf16[16,512]{1,0:T(8,128)(2,1)}, bf16[16,512]{1,0:T(8,128)(2,1)}, u32[]{:S(2)}, u32[]{:S(2)}) collective-permute-start(bf16[16,512]{1,0:T(8,128)(2,1)} %copy-done.92), channel_id=1, source_target_pairs={{0,1},{1,0},{2,3},{3,2},{4,5},{5,4},{6,7},{7,6},{8,9},{9,8},{10,11... | collective-permute-start | bytes 49160 | tf_op jit(solution)/shard_map/ppermute | solution.py:234
  110.5 13.6 %collective-permute-start.14 = (bf16[32,512]{1,0:T(8,128)(2,1)S(1)}, bf16[32,512]{1,0:T(8,128)(2,1)S(1)}, u32[]{:S(2)}, u32[]{:S(2)}) collective-permute-start(bf16[32,512]{1,0:T(8,128)(2,1)S(1)} %pass_rows.5), channel_id=1, source_target_pairs={{0,1},{1,0},{2,3},{3,2},{4,5},{5,4},{6,7},{7,6},{8,9},{9,8},{10,11... | collective-permute-start | bytes 98312 | tf_op jit(solution)/shard_map/ppermute | solution.py:234
  (90 other events, 195.3 us)

commit v15 on v12

--- a/solution.py
+++ b/solution.py
@@ -233,49 +233,50 @@
         pairs = [(s, (s + rows[s // TW % 2][s % 2]) % peer_count) for s in peers]
         return lax.ppermute(part, "tile", pairs)
 
-    def exchange(parts):
-        late_pair, early_pair, behind_one, ahead_three, five_off, opposite, own_chip = parts
-        late_pair = permute(late_pair, (-4, -4), (4, 4))
-        early_pair = permute(early_pair, (4, 4), (-4, -4))
-        behind_one = permute(behind_one, (-1, 1))
-        ahead_three = permute(ahead_three, (3, -3))
-        five_off = permute(five_off, (-5, 5))
-        opposite = permute(opposite, (peer_count // 2, peer_count // 2))
-        late_pair, own_chip = lax.optimization_barrier((late_pair, own_chip))
-        late_passed = permute(late_pair, (1, -1))
-        own_chip = permute(own_chip, (1, -1))
-        early_passed = permute(early_pair, (1, -1))
-        return [
-            late_pair,
-            early_pair,
-            behind_one,
-            ahead_three,
-            five_off,
-            opposite,
-            own_chip,
-            late_passed,
-            early_passed,
-        ]
-
+    steady = ("late", "early", "behind", "ahead", "five", "opposite", "own")
+    staggered = ("early", "late", "ahead", "five", "behind", "opposite", "own")
     arrived_count = 9
 
-    def sent_shapes(columns):
-        rows = (2, 2, 1, 1, 1, 1, 1)
-        return [((count * width, columns), BF16) for count in rows]
-
-    sent_count = len(sent_shapes(feat))
+    def exchange(parts, order):
+        moves = {
+            "late": ((-4, -4), (4, 4)),
+            "early": ((4, 4), (-4, -4)),
+            "behind": ((-1, 1),),
+            "ahead": ((3, -3),),
+            "five": ((-5, 5),),
+            "opposite": ((peer_count // 2, peer_count // 2),),
+            "own": ((1, -1),),
+        }
+        parts = dict(zip(order, parts))
+        own_chip = parts.pop("own")
+        got = {name: permute(part, *moves[name]) for name, part in parts.items()}
+        first = order[0]
+        got[first], own_chip = lax.optimization_barrier((got[first], own_chip))
+        late_passed = permute(got["late"], (1, -1))
+        got["own"] = permute(own_chip, (1, -1))
+        early_passed = permute(got["early"], (1, -1))
+        return [got[name] for name in order] + [late_passed, early_passed]
+
+    def sent_shapes(columns, order=steady):
+        double = ("late", "early")
+        return [((width * (1 + (name in double)), columns), BF16) for name in order]
+
+    sent_count = len(steady)
 
     def place_bits():
         own = lax.axis_index("tile")
         return lax.rem(own, 2) == 1, lax.rem(lax.div(own, TW), 2) == 1
 
-    def send(refs, message, columns=slice(None)):
+    def send(refs, message, columns=slice(None), order=steady):
         odd, odd_row = place_bits()
+        refs = dict(zip(order, refs))
 
         def by_parity(even, odd_one):
             return jnp.where(odd, message(odd_one), message(even))
 
-        late_pair, early_pair, behind_one, ahead_three, five_off, opposite, own_chip = refs
+        late_pair, early_pair, behind_one, ahead_three, five_off, opposite, own_chip = [
+            refs[name] for name in steady
+        ]
         first, second = slice(0, width), slice(width, 2 * width)
         ahead = message(four), by_parity(five, three)
         behind = message(minus[four]), by_parity(minus[three], minus[five])
@@ -288,10 +289,13 @@
         opposite[:, columns] = message(across)
         own_chip[:, columns] = by_parity(one, minus[one])
 
-    def receive(refs, columns=slice(None)):
+    def receive(refs, columns=slice(None), order=steady):
         odd, odd_row = place_bits()
-        late_pair, early_pair, behind_one, ahead_three, five_off, opposite, own_chip = refs[:7]
-        late_passed, early_passed = refs[7:]
+        late_passed, early_passed = refs[sent_count:]
+        refs = dict(zip(order, refs))
+        late_pair, early_pair, behind_one, ahead_three, five_off, opposite, own_chip = [
+            refs[name] for name in steady
+        ]
         first, second = slice(0, width), slice(width, 2 * width)
         near, near_three = behind_one[:, columns], ahead_three[:, columns]
         far, own = five_off[:, columns], own_chip[:, columns]
@@ -311,8 +315,8 @@
         slot_rows[across] = opposite[:, columns]
         return slot_rows
 
-    def by_slot(refs, columns=slice(None)):
-        return jnp.concatenate(receive(refs, columns), axis=0)
+    def by_slot(refs, columns=slice(None), order=steady):
+        return jnp.concatenate(receive(refs, columns, order), axis=0)
 
     def by_row(refs, columns=slice(None)):
         slot_rows = receive(refs, columns)
@@ -341,8 +345,10 @@
         select_ref[slots:, :] = jnp.zeros((slots_pad - slots, grid_count), BF16)
         sent_nodes = mm(select, nodes_ref[...]).astype(BF16)
         sent_cot = mm(select, cot_ref[...]).astype(BF16)
-        send(out_refs, lambda j: sent_nodes[j * width : (j + 1) * width, :], low)
-        send(out_refs, lambda j: sent_cot[j * width : (j + 1) * width, :], high)
+        send(
+            out_refs, lambda j: sent_nodes[j * width : (j + 1) * width, :], low, staggered
+        )
+        send(out_refs, lambda j: sent_cot[j * width : (j + 1) * width, :], high, staggered)
 
     select, *outgoing = call(
         pack,
@@ -353,7 +359,7 @@
             (grid_nodes, 0, grid_count),
             (grid_cot, 0, grid_count),
         ],
-        [((slots_pad, grid_count), BF16)] + sent_shapes(2 * feat),
+        [((slots_pad, grid_count), BF16)] + sent_shapes(2 * feat, staggered),
         flops=4 * slots * grid_count * feat,
     )
     def turn(select_ref, select_t_ref):
@@ -363,7 +369,7 @@
         turn, "turn_select", [select], [((grid_count, slots_pad), BF16)], flops=ROUND_FLOPS
     )
     *outgoing, select_t = lax.optimization_barrier((*outgoing, select_t))
-    arrived = exchange(outgoing)
+    arrived = exchange(outgoing, staggered)
 
     def local(
         select_ref,
@@ -507,7 +513,7 @@
             mesh_act_ref,
             table_ref,
         ) = refs
-        rows = by_slot(arrived_refs, low)
+        rows = by_slot(arrived_refs, low, staggered)
         pe = mm(rows, enc_wg_ref[low, :]).astype(BF16)
         enc_pre_ref[...] = enc_part_ref[...] + mm(enc_pick_ref[:, grid_count:spots], pe)
         write_silu(enc_pre_ref, enc_act_ref)
@@ -581,7 +587,7 @@
     spot_msg, *saved = results
     enc_normed, enc_scale, enc_pre, dec_normed, dec_scale, dec_pre = saved[:6]
     mesh_normed, mesh_scale, mesh_pre = saved[6:]
-    returned = exchange(outgoing)
+    returned = exchange(outgoing, steady)
 
     def between(*refs):
         arrived_refs, refs = refs[:arrived_count], refs[arrived_count:]
@@ -613,10 +619,10 @@
             dec_turned_ref,
         ) = refs
         part_ref[:grid_count, :] = mm(nodes_ref[...], grid_first_ref[low, :])
-        part_ref[grid_count:, :] = mm(by_slot(arrived_refs, low), grid_first_ref[low, :])
+        part_ref[grid_count:, :] = mm(by_slot(arrived_refs, low, staggered), grid_first_ref[low, :])
         mesh_out_ref[...] = (mesh_ref[...].astype(F32) + mesh_normed_ref[...]).astype(BF16)
         cot_rows_ref[:grid_count, :] = cot_ref[...]
-        cot_rows_ref[grid_count:, :] = by_slot(arrived_refs, high)
+        cot_rows_ref[grid_count:, :] = by_slot(arrived_refs, high, staggered)
         second = centred(grid_second_ref[...], 1).astype(BF16)
         grid_wide_ref[:, low] = second
         grid_wide_ref[:, high] = mm_t(second, grid_second_ref[...]).astype(BF16)
@@ -854,7 +860,7 @@
     )
     outgoing, results = results[:sent_count], results[sent_count:]
     grid_normed, grid_gpre, dec_gpre, enc_gpre, mesh_gin, mesh_gpre = results
-    final = exchange(outgoing)
+    final = exchange(outgoing, steady)
 
     def tail(
         nodes_ref,
@@ -917,18 +923,36 @@
         flops=2 * feat * feat * 3 * grid_count,
     )
 
+    pieces = row_chunks(grid_count, 64)
+
     def finish(*refs):
         back_refs = refs[:arrived_count]
-        base_ref, select_t_ref, out_ref = refs[arrived_count:]
-        out_ref[...] = base_ref[...] + mm(select_t_ref[:, :slots], by_row(back_refs))
-
-    (grad_grid,) = call(
+        base_ref, select_t_ref, out_ref, piece_ref, semaphores = refs[arrived_count:]
+        back = by_row(back_refs)
+        copies = []
+        for place, rows in enumerate(pieces):
+            piece_ref[rows, :] = base_ref[rows, :] + mm(select_t_ref[rows, :slots], back)
+            copies.append(
+                pltpu.make_async_copy(
+                    piece_ref.at[rows, :], out_ref.at[rows, :], semaphores.at[place]
+                )
+            )
+            copies[-1].start()
+        for copy in copies:
+            copy.wait()
+
+    grad_grid = pl.pallas_call(
         finish,
-        "add_returned",
-        [*final, base, select_t],
-        [((grid_count, feat), F32)],
-        flops=2 * grid_count * slots * feat,
-    )
+        name="add_returned",
+        in_specs=[pl.BlockSpec(memory_space=pltpu.VMEM)] * (arrived_count + 2),
+        out_specs=pl.BlockSpec(memory_space=pltpu.HBM),
+        out_shape=jax.ShapeDtypeStruct((grid_count, feat), F32),
+        scratch_shapes=[
+            pltpu.VMEM((grid_count, feat), F32),
+            pltpu.SemaphoreType.DMA((len(pieces),)),
+        ],
+        compiler_params=pltpu.CompilerParams(vmem_limit_bytes=VMEM_LIMIT),
+    )(*final, base, select_t)
     return (grid_out, mesh_out, grad_grid, grad_mesh)
 
 

time: 50.8 us -> 50.4 us (level)
  waiting for transfers between devices: 2.62 us -> 1.57 us
  starting transfers between devices: 28.9 us -> 29.5 us
    ppermute x27, waiting for transfers between devices: 2.62 us -> 1.57 us  [permute(): return lax.ppermute(part, 'tile', pairs)]
    pallas_call x0 -> x1, Pallas kernels: none -> 1 us  [per_device(): pl.pallas_call(finish, name='add_returned', in_specs=[pl.BlockSpec(memory...]
    pallas_call x8 -> x7, Pallas kernels: 18 us -> 17.1 us  [call(): pl.pallas_call(kernel, name=name, in_specs=specs, out_specs=[pl.BlockSpec...]
    ppermute x27, starting transfers between devices: 28.9 us -> 29.5 us  [permute(): return lax.ppermute(part, 'tile', pairs)]
  transfers between devices with their start and end apart: 27 -> 27, of which waited for: 6 -> 4; matrix products, arithmetic and copies ran while one was open for 0% -> 0% of each run, Pallas kernels for 14% -> 15%
where the time goes in v15:
time: 50.4 us; the launch traced here: 50.2 us
  starting transfers between devices  29.5 us (59%)
  Pallas kernels  18.1 us (36%)
  waiting for transfers between devices  1.57 us (3%)
  between operations  1.01 us (2%)
    ppermute x27, starting transfers between devices, permute(): return lax.ppermute(part, 'tile', pairs)  29.5 us
    pallas_call x7, Pallas kernels, call(): pl.pallas_call(kernel, name=name, in_specs=specs, out_specs=[pl.BlockSpec...  17.1 us
    ppermute x27, waiting for transfers between devices, permute(): return lax.ppermute(part, 'tile', pairs)  1.57 us
  transfers between devices with their start and end apart: 27, of which 4 were waited for; matrix products, arithmetic and copies ran while one was open for 0% of the time, Pallas kernels for 15%

profile of v15, /device:TPU:0, one launch (start us, length us, event | category | flops | bytes accessed | tf_op | source)
XLA Modules:
  0.0 50.2 jit_solution(7428518699450949358)
XLA Ops:
  0.6 1.4 %pack_rows.1 = (bf16[256,256]{1,0:T(8,128)(2,1)S(1)}, bf16[32,1024]{1,0:T(8,128)(2,1)S(1)}, bf16[32,1024]{1,0:T(8,128)(2,1)S(1)}, bf16[16,1024]{1,0:T(8,128)(2,1...) custom-call(s32[9,16]{1,0:T(8,128)} %refs_0_.2, ...), custom_call_target="tpu_custom_call" | custom-call | flops 75497472 | bytes 950884 | tf_op jit(solution)/shard_map/pack_rows/pallas_call | solution.py:175
  2.3 3.1 %collective-permute-start = (bf16[32,1024]{1,0:T(8,128)(2,1)S(1)}, bf16[32,1024]{1,0:T(8,128)(2,1)S(1)}, u32[]{:S(2)}, u32[]{:S(2)}) collective-permute-start(bf16[32,1024]{1,0:T(8,128)(2,1)S(1)} %get-tuple-element.90), channel_id=1, source_target_pairs={{0,4},{1,5},{2,6},{3,7},{4,0},{5,1},{6,2},{7,3},{8,12},{9,13},{10,... | collective-permute-start | bytes 196616 | tf_op jit(solution)/shard_map/ppermute | solution.py:234
  5.4 2.5 %collective-permute-start.1 = (bf16[32,1024]{1,0:T(8,128)(2,1)S(1)}, bf16[32,1024]{1,0:T(8,128)(2,1)S(1)}, u32[]{:S(2)}, u32[]{:S(2)}) collective-permute-start(bf16[32,1024]{1,0:T(8,128)(2,1)S(1)} %get-tuple-element.93), channel_id=1, source_target_pairs={{0,12},{1,13},{2,14},{3,15},{4,8},{5,9},{6,10},{7,11},{8,4},{9,5},... | collective-permute-start | bytes 196616 | tf_op jit(solution)/shard_map/ppermute | solution.py:234
  8.3 0.9 %collective-permute-start.3 = (bf16[16,1024]{1,0:T(8,128)(2,1)S(1)}, bf16[16,1024]{1,0:T(8,128)(2,1)S(1)}, u32[]{:S(2)}, u32[]{:S(2)}) collective-permute-start(bf16[16,1024]{1,0:T(8,128)(2,1)S(1)} %get-tuple-element.95), channel_id=1, source_target_pairs={{0,11},{1,6},{2,13},{3,8},{4,15},{5,10},{6,1},{7,12},{8,3},{9,14},... | collective-permute-start | bytes 98312 | tf_op jit(solution)/shard_map/ppermute | solution.py:234
  9.2 2.8 %collective-permute-start.4 = (bf16[16,1024]{1,0:T(8,128)(2,1)S(1)}, bf16[16,1024]{1,0:T(8,128)(2,1)S(1)}, u32[]{:S(2)}, u32[]{:S(2)}) collective-permute-start(bf16[16,1024]{1,0:T(8,128)(2,1)S(1)} %get-tuple-element.96), channel_id=1, source_target_pairs={{0,15},{1,2},{2,1},{3,4},{4,3},{5,6},{6,5},{7,8},{8,7},{9,10},{10,... | collective-permute-start | bytes 98312 | tf_op jit(solution)/shard_map/ppermute | solution.py:234
  12.3 1.2 %collective-permute-start.6 = (bf16[16,1024]{1,0:T(8,128)(2,1)S(1)}, bf16[16,1024]{1,0:T(8,128)(2,1)S(1)}, u32[]{:S(2)}, u32[]{:S(2)}) collective-permute-start(bf16[16,1024]{1,0:T(8,128)(2,1)S(1)} %get-tuple-element.98), channel_id=1, source_target_pairs={{0,1},{1,0},{2,3},{3,2},{4,5},{5,4},{6,7},{7,6},{8,9},{9,8},{10,11... | collective-permute-start | bytes 98312 | tf_op jit(solution)/shard_map/ppermute | solution.py:234
  14.1 0.7 %collective-permute-start.8 = (bf16[32,1024]{1,0:T(8,128)(2,1)S(1)}, bf16[32,1024]{1,0:T(8,128)(2,1)S(1)}, u32[]{:S(2)}, u32[]{:S(2)}) collective-permute-start(bf16[32,1024]{1,0:T(8,128)(2,1)S(1)} %collective-permute-done.refs_0_), channel_id=1, source_target_pairs={{0,1},{1,0},{2,3},{3,2},{4,5},{5,4},{6,7},{7,6},{8,9},{9,8},{10,11... | collective-permute-start | bytes 196616 | tf_op jit(solution)/shard_map/ppermute | solution.py:234
  15.0 2.3 %local_products.1 = (f32[384,512]{1,0:T(8,128)S(1)}, f32[768,512]{1,0:T(8,128)S(1)}, f32[64,512]{1,0:T(8,128)S(1)}, bf16[384,512]{1,0:T(8,128)(2,1)S(1)}, bf16[5...) custom-call(bf16[256,256]{1,0:T(8,128)(2,1)S(1)} %get-tuple-element., ...), custom_call_target="tpu_custom_call" | custom-call | flops 1275068416 | bytes 14713856 | tf_op jit(solution)/shard_map/local_products/pallas_call | solution.py:175
  17.4 2.9 %edges_forward.1 = (bf16[32,1024]{1,0:T(8,128)(2,1)S(1)}, bf16[32,1024]{1,0:T(8,128)(2,1)S(1)}, bf16[16,1024]{1,0:T(8,128)(2,1)S(1)}, bf16[16,1024]{1,0:T(8,128)...) custom-call(bf16[32,1024]{1,0:T(8,128)(2,1)S(1)} %collective-permute, ...), custom_call_target="tpu_custom_call" | custom-call | flops 1207959552 | bytes 16839424 | tf_op jit(solution)/shard_map/edges_forward/pallas_call | solution.py:175
  20.3 1.9 %collective-permute-start.9 = (bf16[32,1024]{1,0:T(8,128)(2,1)S(1)}, bf16[32,1024]{1,0:T(8,128)(2,1)S(1)}, u32[]{:S(2)}, u32[]{:S(2)}) collective-permute-start(bf16[32,1024]{1,0:T(8,128)(2,1)S(1)} %get-tuple-element.111), channel_id=1, source_target_pairs={{0,12},{1,13},{2,14},{3,15},{4,8},{5,9},{6,10},{7,11},{8,4},{9,5},... | collective-permute-start | bytes 196616 | tf_op jit(solution)/shard_map/ppermute | solution.py:234
  22.2 2.3 %collective-permute-start.11 = (bf16[16,1024]{1,0:T(8,128)(2,1)S(1)}, bf16[16,1024]{1,0:T(8,128)(2,1)S(1)}, u32[]{:S(2)}, u32[]{:S(2)}) collective-permute-start(bf16[16,1024]{1,0:T(8,128)(2,1)S(1)} %get-tuple-element.115), channel_id=1, source_target_pairs={{0,15},{1,2},{2,1},{3,4},{4,3},{5,6},{6,5},{7,8},{8,7},{9,10},{10,... | collective-permute-start | bytes 98312 | tf_op jit(solution)/shard_map/ppermute | solution.py:234
  24.5 0.9 %collective-permute-start.12 = (bf16[16,1024]{1,0:T(8,128)(2,1)S(1)}, bf16[16,1024]{1,0:T(8,128)(2,1)S(1)}, u32[]{:S(2)}, u32[]{:S(2)}) collective-permute-start(bf16[16,1024]{1,0:T(8,128)(2,1)S(1)} %get-tuple-element.116), channel_id=1, source_target_pairs={{0,3},{1,14},{2,5},{3,0},{4,7},{5,2},{6,9},{7,4},{8,11},{9,6},{10,... | collective-permute-start | bytes 98312 | tf_op jit(solution)/shard_map/ppermute | solution.py:234
  25.4 1.1 %collective-permute-start.13 = (bf16[16,1024]{1,0:T(8,128)(2,1)S(1)}, bf16[16,1024]{1,0:T(8,128)(2,1)S(1)}, u32[]{:S(2)}, u32[]{:S(2)}) collective-permute-start(bf16[16,1024]{1,0:T(8,128)(2,1)S(1)} %get-tuple-element.117), channel_id=1, source_target_pairs={{0,11},{1,6},{2,13},{3,8},{4,15},{5,10},{6,1},{7,12},{8,3},{9,14},... | collective-permute-start | bytes 98312 | tf_op jit(solution)/shard_map/ppermute | solution.py:234
  27.0 1.6 %collective-permute-start.14 = (bf16[16,1024]{1,0:T(8,128)(2,1)S(1)}, bf16[16,1024]{1,0:T(8,128)(2,1)S(1)}, u32[]{:S(2)}, u32[]{:S(2)}) collective-permute-start(bf16[16,1024]{1,0:T(8,128)(2,1)S(1)} %get-tuple-element.118), channel_id=1, source_target_pairs={{0,8},{1,9},{2,10},{3,11},{4,12},{5,13},{6,14},{7,15},{8,0},{9,1},... | collective-permute-start | bytes 98312 | tf_op jit(solution)/shard_map/ppermute | solution.py:234
  29.2 3.0 %slopes_and_nodes.1 = (f32[400,512]{1,0:T(8,128)S(1)}, bf16[400,512]{1,0:T(8,128)(2,1)S(1)}, f32[400,512]{1,0:T(8,128)S(1)}, bf16[512,1024]{1,0:T(8,128)(2,1)S(1...) custom-call(bf16[32,1024]{1,0:T(8,128)(2,1)S(1)} %collective-permute, ...), custom_call_target="tpu_custom_call" | custom-call | flops 1677721600 | bytes 13552640 | tf_op jit(solution)/shard_map/slopes_and_nodes/pallas_call | solution.py:175
  32.3 5.4 %edges_backward.1 = (bf16[32,512]{1,0:T(8,128)(2,1)S(1)}, bf16[32,512]{1,0:T(8,128)(2,1)S(1)}, bf16[16,512]{1,0:T(8,128)(2,1)S(1)}, bf16[16,512]{1,0:T(8,128)(2,...) custom-call(bf16[32,1024]{1,0:T(8,128)(2,1)S(1)} %collective-permute, ...), custom_call_target="tpu_custom_call" | custom-call | flops 2449473536 | bytes 21579520 | tf_op jit(solution)/shard_map/edges_backward/pallas_call | solution.py:175
  37.6 1.9 %collective-permute-start.18 = (bf16[32,512]{1,0:T(8,128)(2,1)S(1)}, bf16[32,512]{1,0:T(8,128)(2,1)S(1)}, u32[]{:S(2)}, u32[]{:S(2)}) collective-permute-start(bf16[32,512]{1,0:T(8,128)(2,1)S(1)} %get-tuple-element.149), channel_id=1, source_target_pairs={{0,12},{1,13},{2,14},{3,15},{4,8},{5,9},{6,10},{7,11},{8,4},{9,5},... | collective-permute-start | bytes 98312 | tf_op jit(solution)/shard_map/ppermute | solution.py:234
  40.0 1.5 %collective-permute-start.20 = (bf16[16,512]{1,0:T(8,128)(2,1)S(1)}, bf16[16,512]{1,0:T(8,128)(2,1)S(1)}, u32[]{:S(2)}, u32[]{:S(2)}) collective-permute-start(bf16[16,512]{1,0:T(8,128)(2,1)S(1)} %get-tuple-element.153), channel_id=1, source_target_pairs={{0,15},{1,2},{2,1},{3,4},{4,3},{5,6},{6,5},{7,8},{8,7},{9,10},{10,... | collective-permute-start | bytes 49160 | tf_op jit(solution)/shard_map/ppermute | solution.py:234
  41.5 1.2 %collective-permute-start.21 = (bf16[16,512]{1,0:T(8,128)(2,1)S(1)}, bf16[16,512]{1,0:T(8,128)(2,1)S(1)}, u32[]{:S(2)}, u32[]{:S(2)}) collective-permute-start(bf16[16,512]{1,0:T(8,128)(2,1)S(1)} %get-tuple-element.154), channel_id=1, source_target_pairs={{0,3},{1,14},{2,5},{3,0},{4,7},{5,2},{6,9},{7,4},{8,11},{9,6},{10,... | collective-permute-start | bytes 49160 | tf_op jit(solution)/shard_map/ppermute | solution.py:234
  42.7 1.5 %collective-permute-start.22 = (bf16[16,512]{1,0:T(8,128)(2,1)S(1)}, bf16[16,512]{1,0:T(8,128)(2,1)S(1)}, u32[]{:S(2)}, u32[]{:S(2)}) collective-permute-start(bf16[16,512]{1,0:T(8,128)(2,1)S(1)} %get-tuple-element.155), channel_id=1, source_target_pairs={{0,11},{1,6},{2,13},{3,8},{4,15},{5,10},{6,1},{7,12},{8,3},{9,14},... | collective-permute-start | bytes 49160 | tf_op jit(solution)/shard_map/ppermute | solution.py:234
  44.2 1.3 %collective-permute-start.23 = (bf16[16,512]{1,0:T(8,128)(2,1)S(1)}, bf16[16,512]{1,0:T(8,128)(2,1)S(1)}, u32[]{:S(2)}, u32[]{:S(2)}) collective-permute-start(bf16[16,512]{1,0:T(8,128)(2,1)S(1)} %get-tuple-element.156), channel_id=1, source_target_pairs={{0,8},{1,9},{2,10},{3,11},{4,12},{5,13},{6,14},{7,15},{8,0},{9,1},... | collective-permute-start | bytes 49160 | tf_op jit(solution)/shard_map/ppermute | solution.py:234
  45.9 1.2 %collective-permute-start.25 = (bf16[32,512]{1,0:T(8,128)(2,1)S(1)}, bf16[32,512]{1,0:T(8,128)(2,1)S(1)}, u32[]{:S(2)}, u32[]{:S(2)}) collective-permute-start(bf16[32,512]{1,0:T(8,128)(2,1)S(1)} %collective-permute-done.18.refs_0_), channel_id=1, source_target_pairs={{0,1},{1,0},{2,3},{3,2},{4,5},{5,4},{6,7},{7,6},{8,9},{9,8},{10,11... | collective-permute-start | bytes 98312 | tf_op jit(solution)/shard_map/ppermute | solution.py:234
  47.1 2.0 %local_gradients.1 = (f32[256,512]{1,0:T(8,128)S(1)}, f32[64,512]{1,0:T(8,128)}, bf16[256,512]{1,0:T(8,128)(2,1)}) custom-call(bf16[256,512]{1,0:T(8,128)(2,1)S(1)} %copy-done.4, f32[400,512]{1,0:T(8,128)S(1)} %get-tuple-element.141.refs_1_, bf16[256,512]{1,0:T(8,128)(2,1)S(1)} %copy-done.5, bf16[400,512]{1,0:T(8,128)(2,1)S(1)} %get-tuple-element.142.refs_3_, ...), custom_call_target="tpu_custom_call" | custom-call | flops 402653184 | bytes 12042240 | tf_op jit(solution)/shard_map/local_gradients/pallas_call | solution.py:175
  49.2 1.0 %add_returned.1 = f32[256,512]{1,0:T(8,128)} custom-call(bf16[32,512]{1,0:T(8,128)(2,1)S(1)} %collective-permute-done.18.refs_0_, bf16[32,512]{1,0:T(8,128)(2,1)S(1)} %collective-permute-done.19.refs_1_, bf16[16,512]{1,0:T(8,128)(2,1)S(1)} %collective-permute-done.20.refs_2_, bf16[16,512]{1,0:T(8,128)(2,1)S(1)} %collective-permute-done.21.refs_3_, ...), custom_call_target="tpu_custom_call" | custom-call | tf_op jit(solution)/shard_map/add_returned/pallas_call | solution.py:944
  (74 shorter events, 3.7 us)
Async XLA Ops:
  2.3 9.6 %collective-permute-start = (bf16[32,1024]{1,0:T(8,128)(2,1)S(1)}, bf16[32,1024]{1,0:T(8,128)(2,1)S(1)}, u32[]{:S(2)}, u32[]{:S(2)}) collective-permute-start(bf16[32,1024]{1,0:T(8,128)(2,1)S(1)} %get-tuple-element.90), channel_id=1, source_target_pairs={{0,4},{1,5},{2,6},{3,7},{4,0},{5,1},{6,2},{7,3},{8,12},{9,13},{10,... | collective-permute-start | bytes 196616 | tf_op jit(solution)/shard_map/ppermute | solution.py:234
  5.4 9.4 %collective-permute-start.1 = (bf16[32,1024]{1,0:T(8,128)(2,1)S(1)}, bf16[32,1024]{1,0:T(8,128)(2,1)S(1)}, u32[]{:S(2)}, u32[]{:S(2)}) collective-permute-start(bf16[32,1024]{1,0:T(8,128)(2,1)S(1)} %get-tuple-element.93), channel_id=1, source_target_pairs={{0,12},{1,13},{2,14},{3,15},{4,8},{5,9},{6,10},{7,11},{8,4},{9,5},... | collective-permute-start | bytes 196616 | tf_op jit(solution)/shard_map/ppermute | solution.py:234
  7.9 4.4 %collective-permute-start.2 = (bf16[16,1024]{1,0:T(8,128)(2,1)S(1)}, bf16[16,1024]{1,0:T(8,128)(2,1)S(1)}, u32[]{:S(2)}, u32[]{:S(2)}) collective-permute-start(bf16[16,1024]{1,0:T(8,128)(2,1)S(1)} %get-tuple-element.94), channel_id=1, source_target_pairs={{0,3},{1,14},{2,5},{3,0},{4,7},{5,2},{6,9},{7,4},{8,11},{9,6},{10,... | collective-permute-start | bytes 98312 | tf_op jit(solution)/shard_map/ppermute | solution.py:234
  8.3 5.8 %collective-permute-start.3 = (bf16[16,1024]{1,0:T(8,128)(2,1)S(1)}, bf16[16,1024]{1,0:T(8,128)(2,1)S(1)}, u32[]{:S(2)}, u32[]{:S(2)}) collective-permute-start(bf16[16,1024]{1,0:T(8,128)(2,1)S(1)} %get-tuple-element.95), channel_id=1, source_target_pairs={{0,11},{1,6},{2,13},{3,8},{4,15},{5,10},{6,1},{7,12},{8,3},{9,14},... | collective-permute-start | bytes 98312 | tf_op jit(solution)/shard_map/ppermute | solution.py:234
  9.2 8.1 %collective-permute-start.4 = (bf16[16,1024]{1,0:T(8,128)(2,1)S(1)}, bf16[16,1024]{1,0:T(8,128)(2,1)S(1)}, u32[]{:S(2)}, u32[]{:S(2)}) collective-permute-start(bf16[16,1024]{1,0:T(8,128)(2,1)S(1)} %get-tuple-element.96), channel_id=1, source_target_pairs={{0,15},{1,2},{2,1},{3,4},{4,3},{5,6},{6,5},{7,8},{8,7},{9,10},{10,... | collective-permute-start | bytes 98312 | tf_op jit(solution)/shard_map/ppermute | solution.py:234
  12.0 5.3 %collective-permute-start.5 = (bf16[16,1024]{1,0:T(8,128)(2,1)S(1)}, bf16[16,1024]{1,0:T(8,128)(2,1)S(1)}, u32[]{:S(2)}, u32[]{:S(2)}) collective-permute-start(bf16[16,1024]{1,0:T(8,128)(2,1)S(1)} %get-tuple-element.97), channel_id=1, source_target_pairs={{0,8},{1,9},{2,10},{3,11},{4,12},{5,13},{6,14},{7,15},{8,0},{9,1},... | collective-permute-start | bytes 98312 | tf_op jit(solution)/shard_map/ppermute | solution.py:234
  12.3 5.0 %collective-permute-start.6 = (bf16[16,1024]{1,0:T(8,128)(2,1)S(1)}, bf16[16,1024]{1,0:T(8,128)(2,1)S(1)}, u32[]{:S(2)}, u32[]{:S(2)}) collective-permute-start(bf16[16,1024]{1,0:T(8,128)(2,1)S(1)} %get-tuple-element.98), channel_id=1, source_target_pairs={{0,1},{1,0},{2,3},{3,2},{4,5},{5,4},{6,7},{7,6},{8,9},{9,8},{10,11... | collective-permute-start | bytes 98312 | tf_op jit(solution)/shard_map/ppermute | solution.py:234
  14.1 3.2 %collective-permute-start.8 = (bf16[32,1024]{1,0:T(8,128)(2,1)S(1)}, bf16[32,1024]{1,0:T(8,128)(2,1)S(1)}, u32[]{:S(2)}, u32[]{:S(2)}) collective-permute-start(bf16[32,1024]{1,0:T(8,128)(2,1)S(1)} %collective-permute-done.refs_0_), channel_id=1, source_target_pairs={{0,1},{1,0},{2,3},{3,2},{4,5},{5,4},{6,7},{7,6},{8,9},{9,8},{10,11... | collective-permute-start | bytes 196616 | tf_op jit(solution)/shard_map/ppermute | solution.py:234
  20.3 6.8 %collective-permute-start.9 = (bf16[32,1024]{1,0:T(8,128)(2,1)S(1)}, bf16[32,1024]{1,0:T(8,128)(2,1)S(1)}, u32[]{:S(2)}, u32[]{:S(2)}) collective-permute-start(bf16[32,1024]{1,0:T(8,128)(2,1)S(1)} %get-tuple-element.111), channel_id=1, source_target_pairs={{0,12},{1,13},{2,14},{3,15},{4,8},{5,9},{6,10},{7,11},{8,4},{9,5},... | collective-permute-start | bytes 196616 | tf_op jit(solution)/shard_map/ppermute | solution.py:234
  22.2 6.9 %collective-permute-start.10 = (bf16[32,1024]{1,0:T(8,128)(2,1)S(1)}, bf16[32,1024]{1,0:T(8,128)(2,1)S(1)}, u32[]{:S(2)}, u32[]{:S(2)}) collective-permute-start(bf16[32,1024]{1,0:T(8,128)(2,1)S(1)} %get-tuple-element.114), channel_id=1, source_target_pairs={{0,4},{1,5},{2,6},{3,7},{4,0},{5,1},{6,2},{7,3},{8,12},{9,13},{10,... | collective-permute-start | bytes 196616 | tf_op jit(solution)/shard_map/ppermute | solution.py:234
  22.2 6.4 %collective-permute-start.11 = (bf16[16,1024]{1,0:T(8,128)(2,1)S(1)}, bf16[16,1024]{1,0:T(8,128)(2,1)S(1)}, u32[]{:S(2)}, u32[]{:S(2)}) collective-permute-start(bf16[16,1024]{1,0:T(8,128)(2,1)S(1)} %get-tuple-element.115), channel_id=1, source_target_pairs={{0,15},{1,2},{2,1},{3,4},{4,3},{5,6},{6,5},{7,8},{8,7},{9,10},{10,... | collective-permute-start | bytes 98312 | tf_op jit(solution)/shard_map/ppermute | solution.py:234
  24.5 4.1 %collective-permute-start.12 = (bf16[16,1024]{1,0:T(8,128)(2,1)S(1)}, bf16[16,1024]{1,0:T(8,128)(2,1)S(1)}, u32[]{:S(2)}, u32[]{:S(2)}) collective-permute-start(bf16[16,1024]{1,0:T(8,128)(2,1)S(1)} %get-tuple-element.116), channel_id=1, source_target_pairs={{0,3},{1,14},{2,5},{3,0},{4,7},{5,2},{6,9},{7,4},{8,11},{9,6},{10,... | collective-permute-start | bytes 98312 | tf_op jit(solution)/shard_map/ppermute | solution.py:234
  25.4 6.8 %collective-permute-start.13 = (bf16[16,1024]{1,0:T(8,128)(2,1)S(1)}, bf16[16,1024]{1,0:T(8,128)(2,1)S(1)}, u32[]{:S(2)}, u32[]{:S(2)}) collective-permute-start(bf16[16,1024]{1,0:T(8,128)(2,1)S(1)} %get-tuple-element.117), channel_id=1, source_target_pairs={{0,11},{1,6},{2,13},{3,8},{4,15},{5,10},{6,1},{7,12},{8,3},{9,14},... | collective-permute-start | bytes 98312 | tf_op jit(solution)/shard_map/ppermute | solution.py:234
  27.0 5.2 %collective-permute-start.14 = (bf16[16,1024]{1,0:T(8,128)(2,1)S(1)}, bf16[16,1024]{1,0:T(8,128)(2,1)S(1)}, u32[]{:S(2)}, u32[]{:S(2)}) collective-permute-start(bf16[16,1024]{1,0:T(8,128)(2,1)S(1)} %get-tuple-element.118), channel_id=1, source_target_pairs={{0,8},{1,9},{2,10},{3,11},{4,12},{5,13},{6,14},{7,15},{8,0},{9,1},... | collective-permute-start | bytes 98312 | tf_op jit(solution)/shard_map/ppermute | solution.py:234
  28.6 3.6 %collective-permute-start.15 = (bf16[16,1024]{1,0:T(8,128)(2,1)S(1)}, bf16[16,1024]{1,0:T(8,128)(2,1)S(1)}, u32[]{:S(2)}, u32[]{:S(2)}) collective-permute-start(bf16[16,1024]{1,0:T(8,128)(2,1)S(1)} %get-tuple-element.119), channel_id=1, source_target_pairs={{0,1},{1,0},{2,3},{3,2},{4,5},{5,4},{6,7},{7,6},{8,9},{9,8},{10,11... | collective-permute-start | bytes 98312 | tf_op jit(solution)/shard_map/ppermute | solution.py:234
  28.6 3.6 %collective-permute-start.16 = (bf16[32,1024]{1,0:T(8,128)(2,1)S(1)}, bf16[32,1024]{1,0:T(8,128)(2,1)S(1)}, u32[]{:S(2)}, u32[]{:S(2)}) collective-permute-start(bf16[32,1024]{1,0:T(8,128)(2,1)S(1)} %collective-permute-done.9.refs_0_), channel_id=1, source_target_pairs={{0,1},{1,0},{2,3},{3,2},{4,5},{5,4},{6,7},{7,6},{8,9},{9,8},{10,11... | collective-permute-start | bytes 196616 | tf_op jit(solution)/shard_map/ppermute | solution.py:234
  37.6 6.6 %collective-permute-start.18 = (bf16[32,512]{1,0:T(8,128)(2,1)S(1)}, bf16[32,512]{1,0:T(8,128)(2,1)S(1)}, u32[]{:S(2)}, u32[]{:S(2)}) collective-permute-start(bf16[32,512]{1,0:T(8,128)(2,1)S(1)} %get-tuple-element.149), channel_id=1, source_target_pairs={{0,12},{1,13},{2,14},{3,15},{4,8},{5,9},{6,10},{7,11},{8,4},{9,5},... | collective-permute-start | bytes 98312 | tf_op jit(solution)/shard_map/ppermute | solution.py:234
  39.5 7.6 %collective-permute-start.19 = (bf16[32,512]{1,0:T(8,128)(2,1)S(1)}, bf16[32,512]{1,0:T(8,128)(2,1)S(1)}, u32[]{:S(2)}, u32[]{:S(2)}) collective-permute-start(bf16[32,512]{1,0:T(8,128)(2,1)S(1)} %get-tuple-element.152), channel_id=1, source_target_pairs={{0,4},{1,5},{2,6},{3,7},{4,0},{5,1},{6,2},{7,3},{8,12},{9,13},{10,... | collective-permute-start | bytes 98312 | tf_op jit(solution)/shard_map/ppermute | solution.py:234
  40.0 5.9 %collective-permute-start.20 = (bf16[16,512]{1,0:T(8,128)(2,1)S(1)}, bf16[16,512]{1,0:T(8,128)(2,1)S(1)}, u32[]{:S(2)}, u32[]{:S(2)}) collective-permute-start(bf16[16,512]{1,0:T(8,128)(2,1)S(1)} %get-tuple-element.153), channel_id=1, source_target_pairs={{0,15},{1,2},{2,1},{3,4},{4,3},{5,6},{6,5},{7,8},{8,7},{9,10},{10,... | collective-permute-start | bytes 49160 | tf_op jit(solution)/shard_map/ppermute | solution.py:234
  41.5 4.5 %collective-permute-start.21 = (bf16[16,512]{1,0:T(8,128)(2,1)S(1)}, bf16[16,512]{1,0:T(8,128)(2,1)S(1)}, u32[]{:S(2)}, u32[]{:S(2)}) collective-permute-start(bf16[16,512]{1,0:T(8,128)(2,1)S(1)} %get-tuple-element.154), channel_id=1, source_target_pairs={{0,3},{1,14},{2,5},{3,0},{4,7},{5,2},{6,9},{7,4},{8,11},{9,6},{10,... | collective-permute-start | bytes 49160 | tf_op jit(solution)/shard_map/ppermute | solution.py:234
  42.7 6.4 %collective-permute-start.22 = (bf16[16,512]{1,0:T(8,128)(2,1)S(1)}, bf16[16,512]{1,0:T(8,128)(2,1)S(1)}, u32[]{:S(2)}, u32[]{:S(2)}) collective-permute-start(bf16[16,512]{1,0:T(8,128)(2,1)S(1)} %get-tuple-element.155), channel_id=1, source_target_pairs={{0,11},{1,6},{2,13},{3,8},{4,15},{5,10},{6,1},{7,12},{8,3},{9,14},... | collective-permute-start | bytes 49160 | tf_op jit(solution)/shard_map/ppermute | solution.py:234
  44.2 5.0 %collective-permute-start.23 = (bf16[16,512]{1,0:T(8,128)(2,1)S(1)}, bf16[16,512]{1,0:T(8,128)(2,1)S(1)}, u32[]{:S(2)}, u32[]{:S(2)}) collective-permute-start(bf16[16,512]{1,0:T(8,128)(2,1)S(1)} %get-tuple-element.156), channel_id=1, source_target_pairs={{0,8},{1,9},{2,10},{3,11},{4,12},{5,13},{6,14},{7,15},{8,0},{9,1},... | collective-permute-start | bytes 49160 | tf_op jit(solution)/shard_map/ppermute | solution.py:234
  45.8 3.4 %collective-permute-start.24 = (bf16[16,512]{1,0:T(8,128)(2,1)S(1)}, bf16[16,512]{1,0:T(8,128)(2,1)S(1)}, u32[]{:S(2)}, u32[]{:S(2)}) collective-permute-start(bf16[16,512]{1,0:T(8,128)(2,1)S(1)} %get-tuple-element.157), channel_id=1, source_target_pairs={{0,1},{1,0},{2,3},{3,2},{4,5},{5,4},{6,7},{7,6},{8,9},{9,8},{10,11... | collective-permute-start | bytes 49160 | tf_op jit(solution)/shard_map/ppermute | solution.py:234
  45.9 3.3 %collective-permute-start.25 = (bf16[32,512]{1,0:T(8,128)(2,1)S(1)}, bf16[32,512]{1,0:T(8,128)(2,1)S(1)}, u32[]{:S(2)}, u32[]{:S(2)}) collective-permute-start(bf16[32,512]{1,0:T(8,128)(2,1)S(1)} %collective-permute-done.18.refs_0_), channel_id=1, source_target_pairs={{0,1},{1,0},{2,3},{3,2},{4,5},{5,4},{6,7},{7,6},{8,9},{9,8},{10,11... | collective-permute-start | bytes 98312 | tf_op jit(solution)/shard_map/ppermute | solution.py:234
  (21 other events, 234.0 us)

commit v16 on v15

--- a/solution.py
+++ b/solution.py
@@ -58,24 +58,21 @@
         scale_ref[rows, :] = scale_inv
 
 
-def write_slopes(pre_ref, normed_ref, scale_ref, second_ref, gain_ref, turned_ref):
-    raw = mm_t(normed_ref[...], second_ref[...])
+def write_slope(pre_ref, slope_ref):
     for rows in row_chunks(pre_ref.shape[0]):
-        gain = silu_and_slope(pre_ref[rows, :])[1] * scale_ref[rows, :]
-        gain_ref[rows, :] = gain.astype(BF16)
-        turned_ref[rows, :] = (gain * raw[rows, :]).astype(BF16)
-
-
-def edge_back(both, normed_ref, gain_ref, turned_ref, out_ref):
-    edges, features = normed_ref.shape
-    for rows in row_chunks(edges):
-        mean = jnp.mean(
-            both[rows, :features] * normed_ref[rows, :].astype(F32), axis=-1, keepdims=True
+        slope_ref[rows, :] = silu_and_slope(pre_ref[rows, :])[1].astype(BF16)
+
+
+def edge_back(upstream, normed_ref, scale_ref, second_ref, slope_ref, out_ref):
+    for rows in row_chunks(upstream.shape[0]):
+        part, normed = upstream[rows, :], normed_ref[rows, :]
+        mean = jnp.mean(part * normed.astype(F32), axis=-1, keepdims=True)
+        out_ref[rows, :] = scale_ref[rows, :].astype(BF16) * (
+            part.astype(BF16) - normed * mean.astype(BF16)
         )
-        out_ref[rows, :] = (
-            gain_ref[rows, :] * both[rows, features:].astype(BF16)
-            - turned_ref[rows, :] * mean.astype(BF16)
-        )
+    raw = mm_t(out_ref[...], second_ref[...])
+    for rows in row_chunks(upstream.shape[0]):
+        out_ref[rows, :] = raw[rows, :].astype(BF16) * slope_ref[rows, :]
 
 
 def neighbour_offsets(peer_count):
@@ -596,12 +593,12 @@
             grid_first_ref,
             grid_second_ref,
             cot_ref,
+            mesh_first_ref,
             mesh_second_ref,
-            dec_second_ref,
+            dec_first_ref,
             mesh_ref,
             mesh_cot_ref,
-            dec_normed_ref,
-            dec_scale_ref,
+            enc_pre_ref,
             dec_pre_ref,
             mesh_normed_ref,
             mesh_pre_ref,
@@ -611,12 +608,14 @@
             cot_turned_ref,
             grid_wide_ref,
             grid_back_ref,
+            mesh_back_ref,
+            mesh_in_ref,
             mesh_out_ref,
             mesh_cot_turned_ref,
             mesh_slope_ref,
             mesh_turned_ref,
-            dec_gain_ref,
-            dec_turned_ref,
+            enc_slope_ref,
+            dec_slope_ref,
         ) = refs
         part_ref[:grid_count, :] = mm(nodes_ref[...], grid_first_ref[low, :])
         part_ref[grid_count:, :] = mm(by_slot(arrived_refs, low, staggered), grid_first_ref[low, :])
@@ -627,19 +626,15 @@
         grid_wide_ref[:, low] = second
         grid_wide_ref[:, high] = mm_t(second, grid_second_ref[...]).astype(BF16)
         cot_turned_ref[...] = mm_t(cot_rows_ref[...], second)
-        grid_back_ref[low, :] = centred(grid_first_ref[high, :], 0).astype(BF16)
-        grid_back_ref[high, :] = mm(dec_second_ref[...], grid_back_ref[low, :]).astype(BF16)
+        grid_back_ref[...] = centred(grid_first_ref[high, :], 0).astype(BF16)
+        mesh_back_ref[...] = centred(mesh_first_ref[high, :], 0).astype(BF16)
+        mesh_in_ref[low, :] = dec_first_ref[high, :]
+        mesh_in_ref[high, :] = mm(mesh_wide_ref[:, low], dec_first_ref[high, :]).astype(BF16)
         mesh_cot_turned_ref[...] = mm_t(mesh_cot_ref[...], mesh_wide_ref[:, low])
         mesh_turned_ref[...] = mm_t(mesh_normed_ref[...].astype(BF16), mesh_second_ref[...])
         mesh_slope_ref[...] = silu_and_slope(mesh_pre_ref[...])[1]
-        write_slopes(
-            dec_pre_ref,
-            dec_normed_ref,
-            dec_scale_ref,
-            dec_second_ref,
-            dec_gain_ref,
-            dec_turned_ref,
-        )
+        write_slope(enc_pre_ref, enc_slope_ref)
+        write_slope(dec_pre_ref, dec_slope_ref)
 
     (
         grid_part,
@@ -647,12 +642,14 @@
         cot_turned,
         grid_wide,
         grid_back,
+        mesh_back,
+        mesh_in,
         mesh_out,
         mesh_cot_turned,
         mesh_slope,
         mesh_turned,
-        dec_gain,
-        dec_turned,
+        enc_slope,
+        dec_slope,
     ) = call(
         between,
         "slopes_and_nodes",
@@ -662,12 +659,12 @@
             grid_first,
             grid_second,
             grid_cot,
+            mesh_first,
             mesh_second,
-            dec_second,
+            dec_first,
             mesh_nodes,
             mesh_cot,
-            dec_normed,
-            dec_scale,
+            enc_pre,
             dec_pre,
             mesh_normed,
             mesh_pre,
@@ -678,12 +675,14 @@
             ((spots, feat), BF16),
             ((spots, feat), F32),
             ((feat, 2 * feat), BF16),
+            ((feat, feat), BF16),
+            ((feat, feat), BF16),
             ((2 * feat, feat), BF16),
             ((mesh_count, feat), BF16),
             ((mesh_count, feat), F32),
             ((mesh_count, feat), F32),
             ((mesh_count, feat), F32),
-            ((dec_count, feat), BF16),
+            ((enc_count, feat), BF16),
             ((dec_count, feat), BF16),
         ],
         flops=16 * spots * feat * feat,
@@ -706,23 +705,24 @@
             grid_first_ref,
             grid_wide_ref,
             grid_back_ref,
-            mesh_first_ref,
-            mesh_wide_ref,
+            mesh_back_ref,
+            mesh_in_ref,
             enc_first_ref,
             enc_second_ref,
             dec_first_ref,
+            dec_second_ref,
             enc_normed_ref,
             enc_scale_ref,
-            enc_pre_ref,
+            enc_slope_ref,
             dec_normed_ref,
-            dec_gain_ref,
-            dec_turned_ref,
+            dec_scale_ref,
+            dec_slope_ref,
             mesh_normed_ref,
             mesh_scale_ref,
             mesh_slope_ref,
             mesh_turned_ref,
-        ) = refs[:29]
-        refs = refs[29:]
+        ) = refs[:30]
+        refs = refs[30:]
         out_refs, refs = refs[:sent_count], refs[sent_count:]
         (
             grid_normed_ref,
@@ -735,10 +735,6 @@
             grid_act_ref,
             grid_slope_ref,
             spot_grad_ref,
-            mesh_in_ref,
-            mesh_back_ref,
-            enc_gain_ref,
-            enc_turned_ref,
         ) = refs
         agg_ref[:grid_count, :] = (
             spot_ref[:grid_count, :] + mm(select_t_ref[:, :slots], by_row(returned_refs, low))
@@ -747,15 +743,11 @@
             spot_ref[grid_count:, :] + by_slot(returned_refs, high).astype(F32)
         ).astype(BF16)
         pre = grid_part_ref[...] + mm(agg_ref[...], grid_first_ref[high, :])
-        mesh_in_ref[low, :] = dec_first_ref[high, :]
-        mesh_in_ref[high, :] = mm(mesh_wide_ref[:, low], dec_first_ref[high, :]).astype(BF16)
         for rows in row_chunks(spots):
             act, slope = silu_and_slope(pre[rows, :])
             grid_act_ref[rows, :] = act.astype(BF16)
             grid_slope_ref[rows, :] = slope
         both = mm(grid_act_ref[...], grid_wide_ref[...])
-        mesh_back_ref[low, :] = centred(mesh_first_ref[high, :], 0).astype(BF16)
-        mesh_back_ref[high, :] = mm(enc_second_ref[...], mesh_back_ref[low, :]).astype(BF16)
         for rows in row_chunks(spots):
             part = both[rows, low]
             scale_inv = scale_rows(part)
@@ -765,20 +757,13 @@
             raw = scale_inv * (cot_turned_ref[rows, :] - (mean * scale_inv) * both[rows, high])
             grid_gpre_ref[rows, :] = (raw * grid_slope_ref[rows, :]).astype(BF16)
         spot_grad_ref[:spots, :] = mm_t(grid_gpre_ref[...], grid_back_ref[...]).astype(BF16)
-        spot_grad_ref[spots:, :] = jnp.zeros((total - spots, 2 * feat), BF16)
-        write_slopes(
-            enc_pre_ref,
-            enc_normed_ref,
-            enc_scale_ref,
-            enc_second_ref,
-            enc_gain_ref,
-            enc_turned_ref,
-        )
+        spot_grad_ref[spots:, :] = jnp.zeros((total - spots, feat), BF16)
         edge_back(
             mm(dec_pick_ref[...], spot_grad_ref[...]),
             dec_normed_ref,
-            dec_gain_ref,
-            dec_turned_ref,
+            dec_scale_ref,
+            dec_second_ref,
+            dec_slope_ref,
             dec_gpre_ref,
         )
         mesh_sum = mm(dec_pool_ref[mesh_rows, :], dec_gpre_ref[...]).astype(BF16)
@@ -794,8 +779,9 @@
         edge_back(
             mm(enc_pick_ref[:, mesh_rows], mesh_gagg),
             enc_normed_ref,
-            enc_gain_ref,
-            enc_turned_ref,
+            enc_scale_ref,
+            enc_second_ref,
+            enc_slope_ref,
             enc_gpre_ref,
         )
         pooled = mm(enc_pool_ref[grid_count:spots, :], enc_gpre_ref[...]).astype(BF16)
@@ -821,17 +807,18 @@
             grid_first,
             grid_wide,
             grid_back,
-            mesh_first,
-            mesh_wide,
+            mesh_back,
+            mesh_in,
             enc_first,
             enc_second,
             dec_first,
+            dec_second,
             enc_normed,
             enc_scale,
-            enc_pre,
+            enc_slope,
             dec_normed,
-            dec_gain,
-            dec_turned,
+            dec_scale,
+            dec_slope,
             mesh_normed,
             mesh_scale,
             mesh_slope,
@@ -850,11 +837,7 @@
             ((spots, feat), BF16),
             ((spots, feat), BF16),
             ((spots, feat), F32),
-            ((total, 2 * feat), BF16),
-            ((2 * feat, feat), BF16),
-            ((2 * feat, feat), BF16),
-            ((enc_count, feat), BF16),
-            ((enc_count, feat), BF16),
+            ((total, feat), BF16),
         ],
         flops=2 * feat * feat * (4 * spots + 3 * dec_count + 2 * enc_count),
     )

time: 50.4 us -> 49.5 us (0.982)
  Pallas kernels: 18.1 us -> 17 us
    pallas_call x7, Pallas kernels: 17.1 us -> 16 us  [call(): pl.pallas_call(kernel, name=name, in_specs=specs, out_specs=[pl.BlockSpec...]
  transfers between devices with their start and end apart: 27 -> 27, of which waited for: 4 -> 5; matrix products, arithmetic and copies ran while one was open for 0% -> 0% of each run, Pallas kernels for 15% -> 14%
where the time goes in v16:
time: 49.5 us; the launch traced here: 49.3 us
  starting transfers between devices  29.6 us (60%)
  Pallas kernels  17 us (34%)
  waiting for transfers between devices  1.65 us (3%)
  between operations  1 us (2%)
    ppermute x27, starting transfers between devices, permute(): return lax.ppermute(part, 'tile', pairs)  29.6 us
    pallas_call x7, Pallas kernels, call(): pl.pallas_call(kernel, name=name, in_specs=specs, out_specs=[pl.BlockSpec...  16 us
    ppermute x27, waiting for transfers between devices, permute(): return lax.ppermute(part, 'tile', pairs)  1.65 us
    pallas_call x1, Pallas kernels, per_device(): pl.pallas_call(finish, name='add_returned', in_specs=[pl.BlockSpec(memory...  1 us
  transfers between devices with their start and end apart: 27, of which 5 were waited for; matrix products, arithmetic and copies ran while one was open for 0% of the time, Pallas kernels for 14%

profile of v16, /device:TPU:0, one launch (start us, length us, event | category | flops | bytes accessed | tf_op | source)
XLA Modules:
  0.0 49.3 jit_solution(14796957555519537686)
XLA Ops:
  0.6 1.4 %pack_rows.1 = (bf16[256,256]{1,0:T(8,128)(2,1)S(1)}, bf16[32,1024]{1,0:T(8,128)(2,1)S(1)}, bf16[32,1024]{1,0:T(8,128)(2,1)S(1)}, bf16[16,1024]{1,0:T(8,128)(2,1...) custom-call(s32[9,16]{1,0:T(8,128)} %refs_0_.2, ...), custom_call_target="tpu_custom_call" | custom-call | flops 75497472 | bytes 950884 | tf_op jit(solution)/shard_map/pack_rows/pallas_call | solution.py:172
  2.3 3.1 %collective-permute-start = (bf16[32,1024]{1,0:T(8,128)(2,1)S(1)}, bf16[32,1024]{1,0:T(8,128)(2,1)S(1)}, u32[]{:S(2)}, u32[]{:S(2)}) collective-permute-start(bf16[32,1024]{1,0:T(8,128)(2,1)S(1)} %get-tuple-element.92), channel_id=1, source_target_pairs={{0,4},{1,5},{2,6},{3,7},{4,0},{5,1},{6,2},{7,3},{8,12},{9,13},{10,... | collective-permute-start | bytes 196616 | tf_op jit(solution)/shard_map/ppermute | solution.py:231
  5.4 2.5 %collective-permute-start.1 = (bf16[32,1024]{1,0:T(8,128)(2,1)S(1)}, bf16[32,1024]{1,0:T(8,128)(2,1)S(1)}, u32[]{:S(2)}, u32[]{:S(2)}) collective-permute-start(bf16[32,1024]{1,0:T(8,128)(2,1)S(1)} %get-tuple-element.95), channel_id=1, source_target_pairs={{0,12},{1,13},{2,14},{3,15},{4,8},{5,9},{6,10},{7,11},{8,4},{9,5},... | collective-permute-start | bytes 196616 | tf_op jit(solution)/shard_map/ppermute | solution.py:231
  8.3 0.9 %collective-permute-start.3 = (bf16[16,1024]{1,0:T(8,128)(2,1)S(1)}, bf16[16,1024]{1,0:T(8,128)(2,1)S(1)}, u32[]{:S(2)}, u32[]{:S(2)}) collective-permute-start(bf16[16,1024]{1,0:T(8,128)(2,1)S(1)} %get-tuple-element.97), channel_id=1, source_target_pairs={{0,11},{1,6},{2,13},{3,8},{4,15},{5,10},{6,1},{7,12},{8,3},{9,14},... | collective-permute-start | bytes 98312 | tf_op jit(solution)/shard_map/ppermute | solution.py:231
  9.2 2.8 %collective-permute-start.4 = (bf16[16,1024]{1,0:T(8,128)(2,1)S(1)}, bf16[16,1024]{1,0:T(8,128)(2,1)S(1)}, u32[]{:S(2)}, u32[]{:S(2)}) collective-permute-start(bf16[16,1024]{1,0:T(8,128)(2,1)S(1)} %get-tuple-element.98), channel_id=1, source_target_pairs={{0,15},{1,2},{2,1},{3,4},{4,3},{5,6},{6,5},{7,8},{8,7},{9,10},{10,... | collective-permute-start | bytes 98312 | tf_op jit(solution)/shard_map/ppermute | solution.py:231
  12.3 1.2 %collective-permute-start.8 = (bf16[32,1024]{1,0:T(8,128)(2,1)S(1)}, bf16[32,1024]{1,0:T(8,128)(2,1)S(1)}, u32[]{:S(2)}, u32[]{:S(2)}) collective-permute-start(bf16[32,1024]{1,0:T(8,128)(2,1)S(1)} %collective-permute-done.refs_0_), channel_id=1, source_target_pairs={{0,1},{1,0},{2,3},{3,2},{4,5},{5,4},{6,7},{7,6},{8,9},{9,8},{10,11... | collective-permute-start | bytes 196616 | tf_op jit(solution)/shard_map/ppermute | solution.py:231
  14.1 0.7 %collective-permute-start.6 = (bf16[16,1024]{1,0:T(8,128)(2,1)S(1)}, bf16[16,1024]{1,0:T(8,128)(2,1)S(1)}, u32[]{:S(2)}, u32[]{:S(2)}) collective-permute-start(bf16[16,1024]{1,0:T(8,128)(2,1)S(1)} %get-tuple-element.100), channel_id=1, source_target_pairs={{0,1},{1,0},{2,3},{3,2},{4,5},{5,4},{6,7},{7,6},{8,9},{9,8},{10,11... | collective-permute-start | bytes 98312 | tf_op jit(solution)/shard_map/ppermute | solution.py:231
  15.0 2.3 %local_products.1 = (f32[384,512]{1,0:T(8,128)S(1)}, f32[768,512]{1,0:T(8,128)S(1)}, f32[64,512]{1,0:T(8,128)S(1)}, bf16[384,512]{1,0:T(8,128)(2,1)S(1)}, bf16[5...) custom-call(bf16[256,256]{1,0:T(8,128)(2,1)S(1)} %get-tuple-element., ...), custom_call_target="tpu_custom_call" | custom-call | flops 1275068416 | bytes 14713856 | tf_op jit(solution)/shard_map/local_products/pallas_call | solution.py:172
  17.4 2.9 %edges_forward.1 = (bf16[32,1024]{1,0:T(8,128)(2,1)S(1)}, bf16[32,1024]{1,0:T(8,128)(2,1)S(1)}, bf16[16,1024]{1,0:T(8,128)(2,1)S(1)}, bf16[16,1024]{1,0:T(8,128)...) custom-call(bf16[32,1024]{1,0:T(8,128)(2,1)S(1)} %collective-permute, ...), custom_call_target="tpu_custom_call" | custom-call | flops 1207959552 | bytes 16839424 | tf_op jit(solution)/shard_map/edges_forward/pallas_call | solution.py:172
  20.3 1.9 %collective-permute-start.9 = (bf16[32,1024]{1,0:T(8,128)(2,1)S(1)}, bf16[32,1024]{1,0:T(8,128)(2,1)S(1)}, u32[]{:S(2)}, u32[]{:S(2)}) collective-permute-start(bf16[32,1024]{1,0:T(8,128)(2,1)S(1)} %get-tuple-element.113), channel_id=1, source_target_pairs={{0,12},{1,13},{2,14},{3,15},{4,8},{5,9},{6,10},{7,11},{8,4},{9,5},... | collective-permute-start | bytes 196616 | tf_op jit(solution)/shard_map/ppermute | solution.py:231
  22.2 2.3 %collective-permute-start.11 = (bf16[16,1024]{1,0:T(8,128)(2,1)S(1)}, bf16[16,1024]{1,0:T(8,128)(2,1)S(1)}, u32[]{:S(2)}, u32[]{:S(2)}) collective-permute-start(bf16[16,1024]{1,0:T(8,128)(2,1)S(1)} %get-tuple-element.117), channel_id=1, source_target_pairs={{0,15},{1,2},{2,1},{3,4},{4,3},{5,6},{6,5},{7,8},{8,7},{9,10},{10,... | collective-permute-start | bytes 98312 | tf_op jit(solution)/shard_map/ppermute | solution.py:231
  24.5 0.9 %collective-permute-start.12 = (bf16[16,1024]{1,0:T(8,128)(2,1)S(1)}, bf16[16,1024]{1,0:T(8,128)(2,1)S(1)}, u32[]{:S(2)}, u32[]{:S(2)}) collective-permute-start(bf16[16,1024]{1,0:T(8,128)(2,1)S(1)} %get-tuple-element.118), channel_id=1, source_target_pairs={{0,3},{1,14},{2,5},{3,0},{4,7},{5,2},{6,9},{7,4},{8,11},{9,6},{10,... | collective-permute-start | bytes 98312 | tf_op jit(solution)/shard_map/ppermute | solution.py:231
  25.4 1.1 %collective-permute-start.13 = (bf16[16,1024]{1,0:T(8,128)(2,1)S(1)}, bf16[16,1024]{1,0:T(8,128)(2,1)S(1)}, u32[]{:S(2)}, u32[]{:S(2)}) collective-permute-start(bf16[16,1024]{1,0:T(8,128)(2,1)S(1)} %get-tuple-element.119), channel_id=1, source_target_pairs={{0,11},{1,6},{2,13},{3,8},{4,15},{5,10},{6,1},{7,12},{8,3},{9,14},... | collective-permute-start | bytes 98312 | tf_op jit(solution)/shard_map/ppermute | solution.py:231
  27.1 1.6 %collective-permute-start.14 = (bf16[16,1024]{1,0:T(8,128)(2,1)S(1)}, bf16[16,1024]{1,0:T(8,128)(2,1)S(1)}, u32[]{:S(2)}, u32[]{:S(2)}) collective-permute-start(bf16[16,1024]{1,0:T(8,128)(2,1)S(1)} %get-tuple-element.120), channel_id=1, source_target_pairs={{0,8},{1,9},{2,10},{3,11},{4,12},{5,13},{6,14},{7,15},{8,0},{9,1},... | collective-permute-start | bytes 98312 | tf_op jit(solution)/shard_map/ppermute | solution.py:231
  29.2 2.7 %slopes_and_nodes.1 = (f32[400,512]{1,0:T(8,128)S(1)}, bf16[400,512]{1,0:T(8,128)(2,1)S(1)}, f32[400,512]{1,0:T(8,128)S(1)}, bf16[512,1024]{1,0:T(8,128)(2,1)S(1...) custom-call(bf16[32,1024]{1,0:T(8,128)(2,1)S(1)} %collective-permute, ...), custom_call_target="tpu_custom_call" | custom-call | flops 1677721600 | bytes 16302080 | tf_op jit(solution)/shard_map/slopes_and_nodes/pallas_call | solution.py:172
  32.0 4.6 %edges_backward.1 = (bf16[32,512]{1,0:T(8,128)(2,1)S(1)}, bf16[32,512]{1,0:T(8,128)(2,1)S(1)}, bf16[16,512]{1,0:T(8,128)(2,1)S(1)}, bf16[16,512]{1,0:T(8,128)(2,...) custom-call(bf16[32,1024]{1,0:T(8,128)(2,1)S(1)} %collective-permute, ...), custom_call_target="tpu_custom_call" | custom-call | flops 2449473536 | bytes 19878656 | tf_op jit(solution)/shard_map/edges_backward/pallas_call | solution.py:172
  36.6 1.9 %collective-permute-start.18 = (bf16[32,512]{1,0:T(8,128)(2,1)S(1)}, bf16[32,512]{1,0:T(8,128)(2,1)S(1)}, u32[]{:S(2)}, u32[]{:S(2)}) collective-permute-start(bf16[32,512]{1,0:T(8,128)(2,1)S(1)} %get-tuple-element.153), channel_id=1, source_target_pairs={{0,12},{1,13},{2,14},{3,15},{4,8},{5,9},{6,10},{7,11},{8,4},{9,5},... | collective-permute-start | bytes 98312 | tf_op jit(solution)/shard_map/ppermute | solution.py:231
  38.9 1.5 %collective-permute-start.20 = (bf16[16,512]{1,0:T(8,128)(2,1)S(1)}, bf16[16,512]{1,0:T(8,128)(2,1)S(1)}, u32[]{:S(2)}, u32[]{:S(2)}) collective-permute-start(bf16[16,512]{1,0:T(8,128)(2,1)S(1)} %get-tuple-element.157), channel_id=1, source_target_pairs={{0,15},{1,2},{2,1},{3,4},{4,3},{5,6},{6,5},{7,8},{8,7},{9,10},{10,... | collective-permute-start | bytes 49160 | tf_op jit(solution)/shard_map/ppermute | solution.py:231
  40.4 1.2 %collective-permute-start.21 = (bf16[16,512]{1,0:T(8,128)(2,1)S(1)}, bf16[16,512]{1,0:T(8,128)(2,1)S(1)}, u32[]{:S(2)}, u32[]{:S(2)}) collective-permute-start(bf16[16,512]{1,0:T(8,128)(2,1)S(1)} %get-tuple-element.158), channel_id=1, source_target_pairs={{0,3},{1,14},{2,5},{3,0},{4,7},{5,2},{6,9},{7,4},{8,11},{9,6},{10,... | collective-permute-start | bytes 49160 | tf_op jit(solution)/shard_map/ppermute | solution.py:231
  41.6 1.8 %collective-permute-start.22 = (bf16[16,512]{1,0:T(8,128)(2,1)S(1)}, bf16[16,512]{1,0:T(8,128)(2,1)S(1)}, u32[]{:S(2)}, u32[]{:S(2)}) collective-permute-start(bf16[16,512]{1,0:T(8,128)(2,1)S(1)} %get-tuple-element.159), channel_id=1, source_target_pairs={{0,11},{1,6},{2,13},{3,8},{4,15},{5,10},{6,1},{7,12},{8,3},{9,14},... | collective-permute-start | bytes 49160 | tf_op jit(solution)/shard_map/ppermute | solution.py:231
  43.4 1.1 %collective-permute-start.23 = (bf16[16,512]{1,0:T(8,128)(2,1)S(1)}, bf16[16,512]{1,0:T(8,128)(2,1)S(1)}, u32[]{:S(2)}, u32[]{:S(2)}) collective-permute-start(bf16[16,512]{1,0:T(8,128)(2,1)S(1)} %get-tuple-element.160), channel_id=1, source_target_pairs={{0,8},{1,9},{2,10},{3,11},{4,12},{5,13},{6,14},{7,15},{8,0},{9,1},... | collective-permute-start | bytes 49160 | tf_op jit(solution)/shard_map/ppermute | solution.py:231
  45.0 1.1 %collective-permute-start.24 = (bf16[16,512]{1,0:T(8,128)(2,1)S(1)}, bf16[16,512]{1,0:T(8,128)(2,1)S(1)}, u32[]{:S(2)}, u32[]{:S(2)}) collective-permute-start(bf16[16,512]{1,0:T(8,128)(2,1)S(1)} %get-tuple-element.161), channel_id=1, source_target_pairs={{0,1},{1,0},{2,3},{3,2},{4,5},{5,4},{6,7},{7,6},{8,9},{9,8},{10,11... | collective-permute-start | bytes 49160 | tf_op jit(solution)/shard_map/ppermute | solution.py:231
  46.1 2.0 %local_gradients.1 = (f32[256,512]{1,0:T(8,128)S(1)}, f32[64,512]{1,0:T(8,128)}, bf16[256,512]{1,0:T(8,128)(2,1)}) custom-call(bf16[256,512]{1,0:T(8,128)(2,1)S(1)} %copy-done.4, f32[400,512]{1,0:T(8,128)S(1)} %get-tuple-element.145.refs_1_, bf16[256,512]{1,0:T(8,128)(2,1)S(1)} %copy-done.5, bf16[400,512]{1,0:T(8,128)(2,1)S(1)} %get-tuple-element.146.refs_3_, ...), custom_call_target="tpu_custom_call" | custom-call | flops 402653184 | bytes 12042240 | tf_op jit(solution)/shard_map/local_gradients/pallas_call | solution.py:172
  48.3 1.0 %add_returned.1 = f32[256,512]{1,0:T(8,128)} custom-call(bf16[32,512]{1,0:T(8,128)(2,1)S(1)} %collective-permute-done.18.refs_0_, bf16[32,512]{1,0:T(8,128)(2,1)S(1)} %collective-permute-done.19.refs_1_, bf16[16,512]{1,0:T(8,128)(2,1)S(1)} %collective-permute-done.20.refs_2_, bf16[16,512]{1,0:T(8,128)(2,1)S(1)} %collective-permute-done.21.refs_3_, ...), custom_call_target="tpu_custom_call" | custom-call | tf_op jit(solution)/shard_map/add_returned/pallas_call | solution.py:927
  (74 shorter events, 3.9 us)
Async XLA Ops:
  2.3 9.6 %collective-permute-start = (bf16[32,1024]{1,0:T(8,128)(2,1)S(1)}, bf16[32,1024]{1,0:T(8,128)(2,1)S(1)}, u32[]{:S(2)}, u32[]{:S(2)}) collective-permute-start(bf16[32,1024]{1,0:T(8,128)(2,1)S(1)} %get-tuple-element.92), channel_id=1, source_target_pairs={{0,4},{1,5},{2,6},{3,7},{4,0},{5,1},{6,2},{7,3},{8,12},{9,13},{10,... | collective-permute-start | bytes 196616 | tf_op jit(solution)/shard_map/ppermute | solution.py:231
  5.4 9.4 %collective-permute-start.1 = (bf16[32,1024]{1,0:T(8,128)(2,1)S(1)}, bf16[32,1024]{1,0:T(8,128)(2,1)S(1)}, u32[]{:S(2)}, u32[]{:S(2)}) collective-permute-start(bf16[32,1024]{1,0:T(8,128)(2,1)S(1)} %get-tuple-element.95), channel_id=1, source_target_pairs={{0,12},{1,13},{2,14},{3,15},{4,8},{5,9},{6,10},{7,11},{8,4},{9,5},... | collective-permute-start | bytes 196616 | tf_op jit(solution)/shard_map/ppermute | solution.py:231
  7.9 4.4 %collective-permute-start.2 = (bf16[16,1024]{1,0:T(8,128)(2,1)S(1)}, bf16[16,1024]{1,0:T(8,128)(2,1)S(1)}, u32[]{:S(2)}, u32[]{:S(2)}) collective-permute-start(bf16[16,1024]{1,0:T(8,128)(2,1)S(1)} %get-tuple-element.96), channel_id=1, source_target_pairs={{0,3},{1,14},{2,5},{3,0},{4,7},{5,2},{6,9},{7,4},{8,11},{9,6},{10,... | collective-permute-start | bytes 98312 | tf_op jit(solution)/shard_map/ppermute | solution.py:231
  8.3 5.8 %collective-permute-start.3 = (bf16[16,1024]{1,0:T(8,128)(2,1)S(1)}, bf16[16,1024]{1,0:T(8,128)(2,1)S(1)}, u32[]{:S(2)}, u32[]{:S(2)}) collective-permute-start(bf16[16,1024]{1,0:T(8,128)(2,1)S(1)} %get-tuple-element.97), channel_id=1, source_target_pairs={{0,11},{1,6},{2,13},{3,8},{4,15},{5,10},{6,1},{7,12},{8,3},{9,14},... | collective-permute-start | bytes 98312 | tf_op jit(solution)/shard_map/ppermute | solution.py:231
  9.2 8.1 %collective-permute-start.4 = (bf16[16,1024]{1,0:T(8,128)(2,1)S(1)}, bf16[16,1024]{1,0:T(8,128)(2,1)S(1)}, u32[]{:S(2)}, u32[]{:S(2)}) collective-permute-start(bf16[16,1024]{1,0:T(8,128)(2,1)S(1)} %get-tuple-element.98), channel_id=1, source_target_pairs={{0,15},{1,2},{2,1},{3,4},{4,3},{5,6},{6,5},{7,8},{8,7},{9,10},{10,... | collective-permute-start | bytes 98312 | tf_op jit(solution)/shard_map/ppermute | solution.py:231
  12.0 5.3 %collective-permute-start.5 = (bf16[16,1024]{1,0:T(8,128)(2,1)S(1)}, bf16[16,1024]{1,0:T(8,128)(2,1)S(1)}, u32[]{:S(2)}, u32[]{:S(2)}) collective-permute-start(bf16[16,1024]{1,0:T(8,128)(2,1)S(1)} %get-tuple-element.99), channel_id=1, source_target_pairs={{0,8},{1,9},{2,10},{3,11},{4,12},{5,13},{6,14},{7,15},{8,0},{9,1},... | collective-permute-start | bytes 98312 | tf_op jit(solution)/shard_map/ppermute | solution.py:231
  12.3 5.0 %collective-permute-start.8 = (bf16[32,1024]{1,0:T(8,128)(2,1)S(1)}, bf16[32,1024]{1,0:T(8,128)(2,1)S(1)}, u32[]{:S(2)}, u32[]{:S(2)}) collective-permute-start(bf16[32,1024]{1,0:T(8,128)(2,1)S(1)} %collective-permute-done.refs_0_), channel_id=1, source_target_pairs={{0,1},{1,0},{2,3},{3,2},{4,5},{5,4},{6,7},{7,6},{8,9},{9,8},{10,11... | collective-permute-start | bytes 196616 | tf_op jit(solution)/shard_map/ppermute | solution.py:231
  14.1 3.2 %collective-permute-start.6 = (bf16[16,1024]{1,0:T(8,128)(2,1)S(1)}, bf16[16,1024]{1,0:T(8,128)(2,1)S(1)}, u32[]{:S(2)}, u32[]{:S(2)}) collective-permute-start(bf16[16,1024]{1,0:T(8,128)(2,1)S(1)} %get-tuple-element.100), channel_id=1, source_target_pairs={{0,1},{1,0},{2,3},{3,2},{4,5},{5,4},{6,7},{7,6},{8,9},{9,8},{10,11... | collective-permute-start | bytes 98312 | tf_op jit(solution)/shard_map/ppermute | solution.py:231
  20.3 6.8 %collective-permute-start.9 = (bf16[32,1024]{1,0:T(8,128)(2,1)S(1)}, bf16[32,1024]{1,0:T(8,128)(2,1)S(1)}, u32[]{:S(2)}, u32[]{:S(2)}) collective-permute-start(bf16[32,1024]{1,0:T(8,128)(2,1)S(1)} %get-tuple-element.113), channel_id=1, source_target_pairs={{0,12},{1,13},{2,14},{3,15},{4,8},{5,9},{6,10},{7,11},{8,4},{9,5},... | collective-permute-start | bytes 196616 | tf_op jit(solution)/shard_map/ppermute | solution.py:231
  22.2 6.9 %collective-permute-start.10 = (bf16[32,1024]{1,0:T(8,128)(2,1)S(1)}, bf16[32,1024]{1,0:T(8,128)(2,1)S(1)}, u32[]{:S(2)}, u32[]{:S(2)}) collective-permute-start(bf16[32,1024]{1,0:T(8,128)(2,1)S(1)} %get-tuple-element.116), channel_id=1, source_target_pairs={{0,4},{1,5},{2,6},{3,7},{4,0},{5,1},{6,2},{7,3},{8,12},{9,13},{10,... | collective-permute-start | bytes 196616 | tf_op jit(solution)/shard_map/ppermute | solution.py:231
  22.2 6.4 %collective-permute-start.11 = (bf16[16,1024]{1,0:T(8,128)(2,1)S(1)}, bf16[16,1024]{1,0:T(8,128)(2,1)S(1)}, u32[]{:S(2)}, u32[]{:S(2)}) collective-permute-start(bf16[16,1024]{1,0:T(8,128)(2,1)S(1)} %get-tuple-element.117), channel_id=1, source_target_pairs={{0,15},{1,2},{2,1},{3,4},{4,3},{5,6},{6,5},{7,8},{8,7},{9,10},{10,... | collective-permute-start | bytes 98312 | tf_op jit(solution)/shard_map/ppermute | solution.py:231
  24.5 4.1 %collective-permute-start.12 = (bf16[16,1024]{1,0:T(8,128)(2,1)S(1)}, bf16[16,1024]{1,0:T(8,128)(2,1)S(1)}, u32[]{:S(2)}, u32[]{:S(2)}) collective-permute-start(bf16[16,1024]{1,0:T(8,128)(2,1)S(1)} %get-tuple-element.118), channel_id=1, source_target_pairs={{0,3},{1,14},{2,5},{3,0},{4,7},{5,2},{6,9},{7,4},{8,11},{9,6},{10,... | collective-permute-start | bytes 98312 | tf_op jit(solution)/shard_map/ppermute | solution.py:231
  25.4 6.5 %collective-permute-start.13 = (bf16[16,1024]{1,0:T(8,128)(2,1)S(1)}, bf16[16,1024]{1,0:T(8,128)(2,1)S(1)}, u32[]{:S(2)}, u32[]{:S(2)}) collective-permute-start(bf16[16,1024]{1,0:T(8,128)(2,1)S(1)} %get-tuple-element.119), channel_id=1, source_target_pairs={{0,11},{1,6},{2,13},{3,8},{4,15},{5,10},{6,1},{7,12},{8,3},{9,14},... | collective-permute-start | bytes 98312 | tf_op jit(solution)/shard_map/ppermute | solution.py:231
  27.1 4.9 %collective-permute-start.14 = (bf16[16,1024]{1,0:T(8,128)(2,1)S(1)}, bf16[16,1024]{1,0:T(8,128)(2,1)S(1)}, u32[]{:S(2)}, u32[]{:S(2)}) collective-permute-start(bf16[16,1024]{1,0:T(8,128)(2,1)S(1)} %get-tuple-element.120), channel_id=1, source_target_pairs={{0,8},{1,9},{2,10},{3,11},{4,12},{5,13},{6,14},{7,15},{8,0},{9,1},... | collective-permute-start | bytes 98312 | tf_op jit(solution)/shard_map/ppermute | solution.py:231
  28.6 3.3 %collective-permute-start.16 = (bf16[32,1024]{1,0:T(8,128)(2,1)S(1)}, bf16[32,1024]{1,0:T(8,128)(2,1)S(1)}, u32[]{:S(2)}, u32[]{:S(2)}) collective-permute-start(bf16[32,1024]{1,0:T(8,128)(2,1)S(1)} %collective-permute-done.9.refs_0_), channel_id=1, source_target_pairs={{0,1},{1,0},{2,3},{3,2},{4,5},{5,4},{6,7},{7,6},{8,9},{9,8},{10,11... | collective-permute-start | bytes 196616 | tf_op jit(solution)/shard_map/ppermute | solution.py:231
  28.6 3.3 %collective-permute-start.15 = (bf16[16,1024]{1,0:T(8,128)(2,1)S(1)}, bf16[16,1024]{1,0:T(8,128)(2,1)S(1)}, u32[]{:S(2)}, u32[]{:S(2)}) collective-permute-start(bf16[16,1024]{1,0:T(8,128)(2,1)S(1)} %get-tuple-element.121), channel_id=1, source_target_pairs={{0,1},{1,0},{2,3},{3,2},{4,5},{5,4},{6,7},{7,6},{8,9},{9,8},{10,11... | collective-permute-start | bytes 98312 | tf_op jit(solution)/shard_map/ppermute | solution.py:231
  36.6 6.9 %collective-permute-start.18 = (bf16[32,512]{1,0:T(8,128)(2,1)S(1)}, bf16[32,512]{1,0:T(8,128)(2,1)S(1)}, u32[]{:S(2)}, u32[]{:S(2)}) collective-permute-start(bf16[32,512]{1,0:T(8,128)(2,1)S(1)} %get-tuple-element.153), channel_id=1, source_target_pairs={{0,12},{1,13},{2,14},{3,15},{4,8},{5,9},{6,10},{7,11},{8,4},{9,5},... | collective-permute-start | bytes 98312 | tf_op jit(solution)/shard_map/ppermute | solution.py:231
  38.4 7.7 %collective-permute-start.19 = (bf16[32,512]{1,0:T(8,128)(2,1)S(1)}, bf16[32,512]{1,0:T(8,128)(2,1)S(1)}, u32[]{:S(2)}, u32[]{:S(2)}) collective-permute-start(bf16[32,512]{1,0:T(8,128)(2,1)S(1)} %get-tuple-element.156), channel_id=1, source_target_pairs={{0,4},{1,5},{2,6},{3,7},{4,0},{5,1},{6,2},{7,3},{8,12},{9,13},{10,... | collective-permute-start | bytes 98312 | tf_op jit(solution)/shard_map/ppermute | solution.py:231
  38.9 5.9 %collective-permute-start.20 = (bf16[16,512]{1,0:T(8,128)(2,1)S(1)}, bf16[16,512]{1,0:T(8,128)(2,1)S(1)}, u32[]{:S(2)}, u32[]{:S(2)}) collective-permute-start(bf16[16,512]{1,0:T(8,128)(2,1)S(1)} %get-tuple-element.157), channel_id=1, source_target_pairs={{0,15},{1,2},{2,1},{3,4},{4,3},{5,6},{6,5},{7,8},{8,7},{9,10},{10,... | collective-permute-start | bytes 49160 | tf_op jit(solution)/shard_map/ppermute | solution.py:231
  40.4 4.6 %collective-permute-start.21 = (bf16[16,512]{1,0:T(8,128)(2,1)S(1)}, bf16[16,512]{1,0:T(8,128)(2,1)S(1)}, u32[]{:S(2)}, u32[]{:S(2)}) collective-permute-start(bf16[16,512]{1,0:T(8,128)(2,1)S(1)} %get-tuple-element.158), channel_id=1, source_target_pairs={{0,3},{1,14},{2,5},{3,0},{4,7},{5,2},{6,9},{7,4},{8,11},{9,6},{10,... | collective-permute-start | bytes 49160 | tf_op jit(solution)/shard_map/ppermute | solution.py:231
  41.6 6.5 %collective-permute-start.22 = (bf16[16,512]{1,0:T(8,128)(2,1)S(1)}, bf16[16,512]{1,0:T(8,128)(2,1)S(1)}, u32[]{:S(2)}, u32[]{:S(2)}) collective-permute-start(bf16[16,512]{1,0:T(8,128)(2,1)S(1)} %get-tuple-element.159), channel_id=1, source_target_pairs={{0,11},{1,6},{2,13},{3,8},{4,15},{5,10},{6,1},{7,12},{8,3},{9,14},... | collective-permute-start | bytes 49160 | tf_op jit(solution)/shard_map/ppermute | solution.py:231
  43.4 4.9 %collective-permute-start.23 = (bf16[16,512]{1,0:T(8,128)(2,1)S(1)}, bf16[16,512]{1,0:T(8,128)(2,1)S(1)}, u32[]{:S(2)}, u32[]{:S(2)}) collective-permute-start(bf16[16,512]{1,0:T(8,128)(2,1)S(1)} %get-tuple-element.160), channel_id=1, source_target_pairs={{0,8},{1,9},{2,10},{3,11},{4,12},{5,13},{6,14},{7,15},{8,0},{9,1},... | collective-permute-start | bytes 49160 | tf_op jit(solution)/shard_map/ppermute | solution.py:231
  44.7 3.6 %collective-permute-start.25 = (bf16[32,512]{1,0:T(8,128)(2,1)S(1)}, bf16[32,512]{1,0:T(8,128)(2,1)S(1)}, u32[]{:S(2)}, u32[]{:S(2)}) collective-permute-start(bf16[32,512]{1,0:T(8,128)(2,1)S(1)} %collective-permute-done.18.refs_0_), channel_id=1, source_target_pairs={{0,1},{1,0},{2,3},{3,2},{4,5},{5,4},{6,7},{7,6},{8,9},{9,8},{10,11... | collective-permute-start | bytes 98312 | tf_op jit(solution)/shard_map/ppermute | solution.py:231
  45.0 3.3 %collective-permute-start.24 = (bf16[16,512]{1,0:T(8,128)(2,1)S(1)}, bf16[16,512]{1,0:T(8,128)(2,1)S(1)}, u32[]{:S(2)}, u32[]{:S(2)}) collective-permute-start(bf16[16,512]{1,0:T(8,128)(2,1)S(1)} %get-tuple-element.161), channel_id=1, source_target_pairs={{0,1},{1,0},{2,3},{3,2},{4,5},{5,4},{6,7},{7,6},{8,9},{9,8},{10,11... | collective-permute-start | bytes 49160 | tf_op jit(solution)/shard_map/ppermute | solution.py:231
  (21 other events, 233.8 us)

commit v17 on v16

--- a/solution.py
+++ b/solution.py
@@ -393,18 +393,14 @@
         dec_pool_ref,
         enc_centred_ref,
         dec_centred_ref,
-        mesh_wide_ref,
-        mesh_base_ref,
+        mesh_centred_ref,
         shared_pool_ref,
         table_ref,
     ):
         onehot_pair(enc_grid_ref, enc_mesh_ref, spots, mesh_count, enc_pick_ref, enc_pool_ref)
         onehot_pair(dec_grid_ref, dec_mesh_ref, spots, mesh_count, dec_pick_ref, dec_pool_ref)
         enc_centred_ref[...] = centred(enc_second_ref[...], 1).astype(BF16)
-        mesh_centred = centred(mesh_second_ref[...], 1).astype(BF16)
-        mesh_wide_ref[:, low] = mesh_centred
-        mesh_wide_ref[:, high] = mm(mesh_centred, dec_first_ref[high, :]).astype(BF16)
-        mesh_base_ref[...] = mm(mesh_ref[...], dec_first_ref[high, :])
+        mesh_centred_ref[...] = centred(mesh_second_ref[...], 1).astype(BF16)
         shared_pool_ref[...] = mm(
             select_ref[:slots, :], dec_pool_ref[:grid_count, :]
         ).astype(BF16)
@@ -430,8 +426,7 @@
         dec_pool,
         enc_centred,
         dec_centred,
-        mesh_wide,
-        mesh_base,
+        mesh_centred,
         shared_pool,
     ) = call(
         local,
@@ -465,8 +460,7 @@
         + [
             ((feat, feat), BF16),
             ((feat, feat), BF16),
-            ((feat, 2 * feat), BF16),
-            ((mesh_count, feat), F32),
+            ((feat, feat), BF16),
             ((slots, dec_count), BF16),
         ],
         scratch=[((total, feat), BF16)],
@@ -489,13 +483,14 @@
             enc_w2_ref,
             mesh_wa_ref,
             mesh_w2_ref,
-            mesh_base_ref,
+            mesh_ref,
+            dec_wm_ref,
             dec_w2_ref,
-        ) = refs[:15]
-        refs = refs[15:]
+        ) = refs[:16]
+        refs = refs[16:]
         out_refs, refs = refs[:sent_count], refs[sent_count:]
         (
-            spot_ref,
+            slot_ref,
             enc_normed_ref,
             enc_scale_ref,
             enc_pre_ref,
@@ -518,20 +513,20 @@
         agg = mm(enc_pool_ref[mesh_rows, :], enc_normed_ref[...]).astype(BF16)
         mesh_pre_ref[...] = mesh_part_ref[...] + mm(agg, mesh_wa_ref[high, :])
         write_silu(mesh_pre_ref, mesh_act_ref)
-        both = mm(mesh_act_ref[...], mesh_w2_ref[...])
-        write_norm(both[:, low], mesh_normed_ref, mesh_scale_ref)
-        mesh_sent = mesh_base_ref[...] + mesh_scale_ref[...] * both[:, high]
+        write_norm(mm(mesh_act_ref[...], mesh_w2_ref[...]), mesh_normed_ref, mesh_scale_ref)
+        mesh_out = (mesh_ref[...].astype(F32) + mesh_normed_ref[...]).astype(BF16)
         table_ref[:slots, :] = mm(rows, dec_wg_ref[low, :]).astype(BF16)
-        table_ref[slots : slots + mesh_count, :] = mesh_sent.astype(BF16)
+        table_ref[slots : slots + mesh_count, :] = mm(mesh_out, dec_wm_ref[high, :]).astype(BF16)
         table_ref[slots + mesh_count :, :] = jnp.zeros(
             (total - spots - mesh_count, feat), BF16
         )
         dec_pre_ref[...] = dec_part_ref[...] + mm(dec_pick_ref[:, grid_count:], table_ref[...])
         write_silu(dec_pre_ref, dec_act_ref)
         write_norm(mm(dec_act_ref[...], dec_w2_ref[...]), dec_normed_ref, dec_scale_ref)
-        spot_ref[...] = mm(dec_pool_ref[:spots, :], dec_normed_ref[...])
+        slot_sums = mm(dec_pool_ref[grid_count:spots, :], dec_normed_ref[...])
+        slot_ref[...] = slot_sums
         shared = mm(shared_pool_ref[...], dec_normed_ref[...]).astype(BF16)
-        slot_msg = spot_ref[grid_count:, :].astype(BF16)
+        slot_msg = slot_sums.astype(BF16)
         send(
             out_refs, lambda j: slot_msg[reverse[j] * width : (reverse[j] + 1) * width, :], low
         )
@@ -565,12 +560,13 @@
             dec_first,
             enc_centred,
             mesh_first,
-            mesh_wide,
-            mesh_base,
+            mesh_centred,
+            mesh_nodes,
+            dec_first,
             dec_centred,
         ],
         sent_shapes(2 * feat)
-        + [((spots, feat), F32)]
+        + [((slots, feat), F32)]
         + saved_shapes,
         scratch=[
             ((enc_count, feat), BF16),
@@ -581,7 +577,7 @@
         flops=2 * feat * feat * 2 * (enc_count + dec_count),
     )
     outgoing, results = results[:sent_count], results[sent_count:]
-    spot_msg, *saved = results
+    slot_sums, *saved = results
     enc_normed, enc_scale, enc_pre, dec_normed, dec_scale, dec_pre = saved[:6]
     mesh_normed, mesh_scale, mesh_pre = saved[6:]
     returned = exchange(outgoing, steady)
@@ -594,26 +590,22 @@
             grid_second_ref,
             cot_ref,
             mesh_first_ref,
-            mesh_second_ref,
-            dec_first_ref,
+            dec_pool_ref,
+            dec_normed_ref,
             mesh_ref,
-            mesh_cot_ref,
             enc_pre_ref,
             dec_pre_ref,
             mesh_normed_ref,
             mesh_pre_ref,
-            mesh_wide_ref,
+            local_sums_ref,
             part_ref,
             cot_rows_ref,
             cot_turned_ref,
             grid_wide_ref,
             grid_back_ref,
             mesh_back_ref,
-            mesh_in_ref,
             mesh_out_ref,
-            mesh_cot_turned_ref,
             mesh_slope_ref,
-            mesh_turned_ref,
             enc_slope_ref,
             dec_slope_ref,
         ) = refs
@@ -628,26 +620,21 @@
         cot_turned_ref[...] = mm_t(cot_rows_ref[...], second)
         grid_back_ref[...] = centred(grid_first_ref[high, :], 0).astype(BF16)
         mesh_back_ref[...] = centred(mesh_first_ref[high, :], 0).astype(BF16)
-        mesh_in_ref[low, :] = dec_first_ref[high, :]
-        mesh_in_ref[high, :] = mm(mesh_wide_ref[:, low], dec_first_ref[high, :]).astype(BF16)
-        mesh_cot_turned_ref[...] = mm_t(mesh_cot_ref[...], mesh_wide_ref[:, low])
-        mesh_turned_ref[...] = mm_t(mesh_normed_ref[...].astype(BF16), mesh_second_ref[...])
+        local_sums_ref[...] = mm(dec_pool_ref[:grid_count, :], dec_normed_ref[...])
         mesh_slope_ref[...] = silu_and_slope(mesh_pre_ref[...])[1]
         write_slope(enc_pre_ref, enc_slope_ref)
         write_slope(dec_pre_ref, dec_slope_ref)
 
     (
+        local_sums,
         grid_part,
         cot_rows,
         cot_turned,
         grid_wide,
         grid_back,
         mesh_back,
-        mesh_in,
         mesh_out,
-        mesh_cot_turned,
         mesh_slope,
-        mesh_turned,
         enc_slope,
         dec_slope,
     ) = call(
@@ -660,27 +647,23 @@
             grid_second,
             grid_cot,
             mesh_first,
-            mesh_second,
-            dec_first,
+            dec_pool,
+            dec_normed,
             mesh_nodes,
-            mesh_cot,
             enc_pre,
             dec_pre,
             mesh_normed,
             mesh_pre,
-            mesh_wide,
         ],
         [
+            ((grid_count, feat), F32),
             ((spots, feat), F32),
             ((spots, feat), BF16),
             ((spots, feat), F32),
             ((feat, 2 * feat), BF16),
             ((feat, feat), BF16),
             ((feat, feat), BF16),
-            ((2 * feat, feat), BF16),
             ((mesh_count, feat), BF16),
-            ((mesh_count, feat), F32),
-            ((mesh_count, feat), F32),
             ((mesh_count, feat), F32),
             ((enc_count, feat), BF16),
             ((dec_count, feat), BF16),
@@ -691,13 +674,13 @@
     def backward(*refs):
         returned_refs, refs = refs[:arrived_count], refs[arrived_count:]
         (
-            spot_ref,
+            local_sums_ref,
+            slot_sums_ref,
             grid_part_ref,
             select_t_ref,
             cot_rows_ref,
             cot_turned_ref,
             mesh_cot_ref,
-            mesh_cot_turned_ref,
             enc_pick_ref,
             enc_pool_ref,
             dec_pick_ref,
@@ -706,7 +689,7 @@
             grid_wide_ref,
             grid_back_ref,
             mesh_back_ref,
-            mesh_in_ref,
+            mesh_second_ref,
             enc_first_ref,
             enc_second_ref,
             dec_first_ref,
@@ -720,9 +703,8 @@
             mesh_normed_ref,
             mesh_scale_ref,
             mesh_slope_ref,
-            mesh_turned_ref,
-        ) = refs[:30]
-        refs = refs[30:]
+        ) = refs[:29]
+        refs = refs[29:]
         out_refs, refs = refs[:sent_count], refs[sent_count:]
         (
             grid_normed_ref,
@@ -737,10 +719,10 @@
             spot_grad_ref,
         ) = refs
         agg_ref[:grid_count, :] = (
-            spot_ref[:grid_count, :] + mm(select_t_ref[:, :slots], by_row(returned_refs, low))
+            local_sums_ref[...] + mm(select_t_ref[:, :slots], by_row(returned_refs, low))
         ).astype(BF16)
         agg_ref[grid_count:, :] = (
-            spot_ref[grid_count:, :] + by_slot(returned_refs, high).astype(F32)
+            slot_sums_ref[...] + by_slot(returned_refs, high).astype(F32)
         ).astype(BF16)
         pre = grid_part_ref[...] + mm(agg_ref[...], grid_first_ref[high, :])
         for rows in row_chunks(spots):
@@ -767,12 +749,14 @@
             dec_gpre_ref,
         )
         mesh_sum = mm(dec_pool_ref[mesh_rows, :], dec_gpre_ref[...]).astype(BF16)
-        both = mm_t(mesh_sum, mesh_in_ref[...])
-        mesh_gin = mesh_cot_ref[...].astype(F32) + both[:, low]
+        mesh_gin = mesh_cot_ref[...].astype(F32) + mm_t(mesh_sum, dec_first_ref[high, :])
         mesh_gin_ref[...] = mesh_gin
-        mean = jnp.mean(mesh_gin * mesh_normed_ref[...], axis=-1, keepdims=True)
-        raw = mesh_cot_turned_ref[...] + both[:, high] - mean * mesh_turned_ref[...]
-        mesh_gpre_ref[...] = (mesh_scale_ref[...] * raw * mesh_slope_ref[...]).astype(BF16)
+        normed = mesh_normed_ref[...]
+        upstream = centred(mesh_gin, 1)
+        mean = jnp.mean(upstream * normed, axis=-1, keepdims=True)
+        mesh_gout = (mesh_scale_ref[...] * (upstream - normed * mean)).astype(BF16)
+        raw = mm_t(mesh_gout, mesh_second_ref[...])
+        mesh_gpre_ref[...] = (raw * mesh_slope_ref[...]).astype(BF16)
         mesh_gagg = mm_t(mesh_gpre_ref[...], mesh_back_ref[...]).astype(BF16)
         pooled = mm(dec_pool_ref[grid_count:spots, :], dec_gpre_ref[...]).astype(BF16)
         slot_back = mm_t(pooled, dec_first_ref[low, :])
@@ -793,13 +777,13 @@
         "edges_backward",
         [
             *returned,
-            spot_msg,
+            local_sums,
+            slot_sums,
             grid_part,
             select_t,
             cot_rows,
             cot_turned,
             mesh_cot,
-            mesh_cot_turned,
             enc_pick,
             enc_pool,
             dec_pick,
@@ -808,7 +792,7 @@
             grid_wide,
             grid_back,
             mesh_back,
-            mesh_in,
+            mesh_second,
             enc_first,
             enc_second,
             dec_first,
@@ -822,7 +806,6 @@
             mesh_normed,
             mesh_scale,
             mesh_slope,
-            mesh_turned,
         ],
         sent_shapes(feat)
         + [
@@ -868,18 +851,19 @@
         grid_out_ref[...] = (
             nodes_ref[...].astype(F32) + grid_normed_ref[:grid_count, :]
         ).astype(BF16)
-        enc_sums = mm(enc_pool_ref[...], enc_gpre_ref[...]).astype(BF16)
+        enc_sums = mm(enc_pool_ref[:grid_count, :], enc_gpre_ref[...]).astype(BF16)
+        mesh_sums = mm(enc_pool_ref[mesh_rows, :], enc_gpre_ref[...]).astype(BF16)
         dec_sums = mm(dec_pool_ref[:grid_count, :], dec_gpre_ref[...]).astype(BF16)
         base_ref[...] = (
             cot_ref[...].astype(F32)
             + mm_t(grid_gpre_ref[:grid_count, :], grid_wn_ref[low, :])
-            + mm_t(enc_sums[:grid_count, :], enc_wg_ref[low, :])
+            + mm_t(enc_sums, enc_wg_ref[low, :])
             + mm_t(dec_sums, dec_wg_ref[low, :])
         )
         grad_mesh_ref[...] = (
             mesh_gin_ref[...]
             + mm_t(mesh_gpre_ref[...], mesh_wn_ref[low, :])
-            + mm_t(enc_sums[mesh_rows, :], enc_wm_ref[high, :])
+            + mm_t(mesh_sums, enc_wm_ref[high, :])
         )
 
     base, grad_mesh, grid_out = call(

time: 49.5 us -> 49.3 us (level)
  waiting for transfers between devices: 1.65 us -> 2.7 us
  Pallas kernels: 17 us -> 16.4 us
  starting transfers between devices: 29.6 us -> 29 us
    ppermute x27, waiting for transfers between devices: 1.65 us -> 2.7 us  [permute(): return lax.ppermute(part, 'tile', pairs)]
    ppermute x27, starting transfers between devices: 29.6 us -> 29 us  [permute(): return lax.ppermute(part, 'tile', pairs)]
    pallas_call x7, Pallas kernels: 16 us -> 15.4 us  [call(): pl.pallas_call(kernel, name=name, in_specs=specs, out_specs=[pl.BlockSpec...]
  transfers between devices with their start and end apart: 27 -> 27, of which waited for: 5 -> 7; matrix products, arithmetic and copies ran while one was open for 0% -> 0% of each run, Pallas kernels for 14% -> 13%
where the time goes in v17:
time: 49.3 us; the launch traced here: 49.2 us
  starting transfers between devices  29 us (59%)
  Pallas kernels  16.4 us (33%)
  waiting for transfers between devices  2.7 us (5%)
  between operations  0.97 us (2%)
    ppermute x27, starting transfers between devices, permute(): return lax.ppermute(part, 'tile', pairs)  29 us
    pallas_call x7, Pallas kernels, call(): pl.pallas_call(kernel, name=name, in_specs=specs, out_specs=[pl.BlockSpec...  15.4 us
    ppermute x27, waiting for transfers between devices, permute(): return lax.ppermute(part, 'tile', pairs)  2.7 us
    pallas_call x1, Pallas kernels, per_device(): pl.pallas_call(finish, name='add_returned', in_specs=[pl.BlockSpec(memory...  1 us
  transfers between devices with their start and end apart: 27, of which 7 were waited for; matrix products, arithmetic and copies ran while one was open for 0% of the time, Pallas kernels for 13%

profile of v17, /device:TPU:0, one launch (start us, length us, event | category | flops | bytes accessed | tf_op | source)
XLA Modules:
  0.0 49.2 jit_solution(11938479242017739694)
XLA Ops:
  0.6 1.4 %pack_rows.1 = (bf16[256,256]{1,0:T(8,128)(2,1)S(1)}, bf16[32,1024]{1,0:T(8,128)(2,1)S(1)}, bf16[32,1024]{1,0:T(8,128)(2,1)S(1)}, bf16[16,1024]{1,0:T(8,128)(2,1...) custom-call(s32[9,16]{1,0:T(8,128)} %refs_0_.2, ...), custom_call_target="tpu_custom_call" | custom-call | flops 75497472 | bytes 950884 | tf_op jit(solution)/shard_map/pack_rows/pallas_call | solution.py:172
  2.3 3.1 %collective-permute-start = (bf16[32,1024]{1,0:T(8,128)(2,1)S(1)}, bf16[32,1024]{1,0:T(8,128)(2,1)S(1)}, u32[]{:S(2)}, u32[]{:S(2)}) collective-permute-start(bf16[32,1024]{1,0:T(8,128)(2,1)S(1)} %get-tuple-element.89), channel_id=1, source_target_pairs={{0,4},{1,5},{2,6},{3,7},{4,0},{5,1},{6,2},{7,3},{8,12},{9,13},{10,... | collective-permute-start | bytes 196616 | tf_op jit(solution)/shard_map/ppermute | solution.py:231
  5.4 2.5 %collective-permute-start.1 = (bf16[32,1024]{1,0:T(8,128)(2,1)S(1)}, bf16[32,1024]{1,0:T(8,128)(2,1)S(1)}, u32[]{:S(2)}, u32[]{:S(2)}) collective-permute-start(bf16[32,1024]{1,0:T(8,128)(2,1)S(1)} %get-tuple-element.92), channel_id=1, source_target_pairs={{0,12},{1,13},{2,14},{3,15},{4,8},{5,9},{6,10},{7,11},{8,4},{9,5},... | collective-permute-start | bytes 196616 | tf_op jit(solution)/shard_map/ppermute | solution.py:231
  8.3 0.9 %collective-permute-start.3 = (bf16[16,1024]{1,0:T(8,128)(2,1)S(1)}, bf16[16,1024]{1,0:T(8,128)(2,1)S(1)}, u32[]{:S(2)}, u32[]{:S(2)}) collective-permute-start(bf16[16,1024]{1,0:T(8,128)(2,1)S(1)} %get-tuple-element.94), channel_id=1, source_target_pairs={{0,11},{1,6},{2,13},{3,8},{4,15},{5,10},{6,1},{7,12},{8,3},{9,14},... | collective-permute-start | bytes 98312 | tf_op jit(solution)/shard_map/ppermute | solution.py:231
  9.2 2.8 %collective-permute-start.4 = (bf16[16,1024]{1,0:T(8,128)(2,1)S(1)}, bf16[16,1024]{1,0:T(8,128)(2,1)S(1)}, u32[]{:S(2)}, u32[]{:S(2)}) collective-permute-start(bf16[16,1024]{1,0:T(8,128)(2,1)S(1)} %get-tuple-element.95), channel_id=1, source_target_pairs={{0,15},{1,2},{2,1},{3,4},{4,3},{5,6},{6,5},{7,8},{8,7},{9,10},{10,... | collective-permute-start | bytes 98312 | tf_op jit(solution)/shard_map/ppermute | solution.py:231
  12.3 1.2 %collective-permute-start.8 = (bf16[32,1024]{1,0:T(8,128)(2,1)S(1)}, bf16[32,1024]{1,0:T(8,128)(2,1)S(1)}, u32[]{:S(2)}, u32[]{:S(2)}) collective-permute-start(bf16[32,1024]{1,0:T(8,128)(2,1)S(1)} %collective-permute-done.refs_0_), channel_id=1, source_target_pairs={{0,1},{1,0},{2,3},{3,2},{4,5},{5,4},{6,7},{7,6},{8,9},{9,8},{10,11... | collective-permute-start | bytes 196616 | tf_op jit(solution)/shard_map/ppermute | solution.py:231
  14.1 0.7 %collective-permute-start.6 = (bf16[16,1024]{1,0:T(8,128)(2,1)S(1)}, bf16[16,1024]{1,0:T(8,128)(2,1)S(1)}, u32[]{:S(2)}, u32[]{:S(2)}) collective-permute-start(bf16[16,1024]{1,0:T(8,128)(2,1)S(1)} %get-tuple-element.97), channel_id=1, source_target_pairs={{0,1},{1,0},{2,3},{3,2},{4,5},{5,4},{6,7},{7,6},{8,9},{9,8},{10,11... | collective-permute-start | bytes 98312 | tf_op jit(solution)/shard_map/ppermute | solution.py:231
  15.0 2.0 %local_products.1 = (f32[384,512]{1,0:T(8,128)S(1)}, f32[768,512]{1,0:T(8,128)S(1)}, f32[64,512]{1,0:T(8,128)S(1)}, bf16[384,512]{1,0:T(8,128)(2,1)S(1)}, bf16[5...) custom-call(bf16[256,256]{1,0:T(8,128)(2,1)S(1)} %get-tuple-element., ...), custom_call_target="tpu_custom_call" | custom-call | flops 1275068416 | bytes 14058496 | tf_op jit(solution)/shard_map/local_products/pallas_call | solution.py:172
  17.2 2.8 %edges_forward.1 = (bf16[32,1024]{1,0:T(8,128)(2,1)S(1)}, bf16[32,1024]{1,0:T(8,128)(2,1)S(1)}, bf16[16,1024]{1,0:T(8,128)(2,1)S(1)}, bf16[16,1024]{1,0:T(8,128)...) custom-call(bf16[32,1024]{1,0:T(8,128)(2,1)S(1)} %collective-permute, ...), custom_call_target="tpu_custom_call" | custom-call | flops 1207959552 | bytes 17298176 | tf_op jit(solution)/shard_map/edges_forward/pallas_call | solution.py:172
  20.0 2.0 %collective-permute-start.9 = (bf16[32,1024]{1,0:T(8,128)(2,1)S(1)}, bf16[32,1024]{1,0:T(8,128)(2,1)S(1)}, u32[]{:S(2)}, u32[]{:S(2)}) collective-permute-start(bf16[32,1024]{1,0:T(8,128)(2,1)S(1)} %get-tuple-element.109), channel_id=1, source_target_pairs={{0,12},{1,13},{2,14},{3,15},{4,8},{5,9},{6,10},{7,11},{8,4},{9,5},... | collective-permute-start | bytes 196616 | tf_op jit(solution)/shard_map/ppermute | solution.py:231
  22.0 2.2 %collective-permute-start.11 = (bf16[16,1024]{1,0:T(8,128)(2,1)S(1)}, bf16[16,1024]{1,0:T(8,128)(2,1)S(1)}, u32[]{:S(2)}, u32[]{:S(2)}) collective-permute-start(bf16[16,1024]{1,0:T(8,128)(2,1)S(1)} %get-tuple-element.113), channel_id=1, source_target_pairs={{0,15},{1,2},{2,1},{3,4},{4,3},{5,6},{6,5},{7,8},{8,7},{9,10},{10,... | collective-permute-start | bytes 98312 | tf_op jit(solution)/shard_map/ppermute | solution.py:231
  24.1 1.0 %collective-permute-start.12 = (bf16[16,1024]{1,0:T(8,128)(2,1)S(1)}, bf16[16,1024]{1,0:T(8,128)(2,1)S(1)}, u32[]{:S(2)}, u32[]{:S(2)}) collective-permute-start(bf16[16,1024]{1,0:T(8,128)(2,1)S(1)} %get-tuple-element.114), channel_id=1, source_target_pairs={{0,3},{1,14},{2,5},{3,0},{4,7},{5,2},{6,9},{7,4},{8,11},{9,6},{10,... | collective-permute-start | bytes 98312 | tf_op jit(solution)/shard_map/ppermute | solution.py:231
  25.2 1.0 %collective-permute-start.13 = (bf16[16,1024]{1,0:T(8,128)(2,1)S(1)}, bf16[16,1024]{1,0:T(8,128)(2,1)S(1)}, u32[]{:S(2)}, u32[]{:S(2)}) collective-permute-start(bf16[16,1024]{1,0:T(8,128)(2,1)S(1)} %get-tuple-element.115), channel_id=1, source_target_pairs={{0,11},{1,6},{2,13},{3,8},{4,15},{5,10},{6,1},{7,12},{8,3},{9,14},... | collective-permute-start | bytes 98312 | tf_op jit(solution)/shard_map/ppermute | solution.py:231
  26.8 1.5 %collective-permute-start.14 = (bf16[16,1024]{1,0:T(8,128)(2,1)S(1)}, bf16[16,1024]{1,0:T(8,128)(2,1)S(1)}, u32[]{:S(2)}, u32[]{:S(2)}) collective-permute-start(bf16[16,1024]{1,0:T(8,128)(2,1)S(1)} %get-tuple-element.116), channel_id=1, source_target_pairs={{0,8},{1,9},{2,10},{3,11},{4,12},{5,13},{6,14},{7,15},{8,0},{9,1},... | collective-permute-start | bytes 98312 | tf_op jit(solution)/shard_map/ppermute | solution.py:231
  29.0 2.3 %slopes_and_nodes.1 = (f32[256,512]{1,0:T(8,128)S(1)}, f32[400,512]{1,0:T(8,128)S(1)}, bf16[400,512]{1,0:T(8,128)(2,1)S(1)}, f32[400,512]{1,0:T(8,128)S(1)}, bf1...) custom-call(bf16[32,1024]{1,0:T(8,128)(2,1)S(1)} %collective-permute, ...), custom_call_target="tpu_custom_call" | custom-call | flops 1677721600 | bytes 13877248 | tf_op jit(solution)/shard_map/slopes_and_nodes/pallas_call | solution.py:172
  32.0 4.8 %edges_backward.1 = (bf16[32,512]{1,0:T(8,128)(2,1)S(1)}, bf16[32,512]{1,0:T(8,128)(2,1)S(1)}, bf16[16,512]{1,0:T(8,128)(2,1)S(1)}, bf16[16,512]{1,0:T(8,128)(2,...) custom-call(bf16[32,1024]{1,0:T(8,128)(2,1)S(1)} %collective-permute, ...), custom_call_target="tpu_custom_call" | custom-call | flops 2449473536 | bytes 19092224 | tf_op jit(solution)/shard_map/edges_backward/pallas_call | solution.py:172
  36.8 1.6 %collective-permute-start.18 = (bf16[32,512]{1,0:T(8,128)(2,1)S(1)}, bf16[32,512]{1,0:T(8,128)(2,1)S(1)}, u32[]{:S(2)}, u32[]{:S(2)}) collective-permute-start(bf16[32,512]{1,0:T(8,128)(2,1)S(1)} %get-tuple-element.147), channel_id=1, source_target_pairs={{0,12},{1,13},{2,14},{3,15},{4,8},{5,9},{6,10},{7,11},{8,4},{9,5},... | collective-permute-start | bytes 98312 | tf_op jit(solution)/shard_map/ppermute | solution.py:231
  38.5 1.4 %collective-permute-start.20 = (bf16[16,512]{1,0:T(8,128)(2,1)S(1)}, bf16[16,512]{1,0:T(8,128)(2,1)S(1)}, u32[]{:S(2)}, u32[]{:S(2)}) collective-permute-start(bf16[16,512]{1,0:T(8,128)(2,1)S(1)} %get-tuple-element.151), channel_id=1, source_target_pairs={{0,15},{1,2},{2,1},{3,4},{4,3},{5,6},{6,5},{7,8},{8,7},{9,10},{10,... | collective-permute-start | bytes 49160 | tf_op jit(solution)/shard_map/ppermute | solution.py:231
  40.0 1.7 %collective-permute-start.21 = (bf16[16,512]{1,0:T(8,128)(2,1)S(1)}, bf16[16,512]{1,0:T(8,128)(2,1)S(1)}, u32[]{:S(2)}, u32[]{:S(2)}) collective-permute-start(bf16[16,512]{1,0:T(8,128)(2,1)S(1)} %get-tuple-element.152), channel_id=1, source_target_pairs={{0,3},{1,14},{2,5},{3,0},{4,7},{5,2},{6,9},{7,4},{8,11},{9,6},{10,... | collective-permute-start | bytes 49160 | tf_op jit(solution)/shard_map/ppermute | solution.py:231
  41.6 1.7 %collective-permute-start.22 = (bf16[16,512]{1,0:T(8,128)(2,1)S(1)}, bf16[16,512]{1,0:T(8,128)(2,1)S(1)}, u32[]{:S(2)}, u32[]{:S(2)}) collective-permute-start(bf16[16,512]{1,0:T(8,128)(2,1)S(1)} %get-tuple-element.153), channel_id=1, source_target_pairs={{0,11},{1,6},{2,13},{3,8},{4,15},{5,10},{6,1},{7,12},{8,3},{9,14},... | collective-permute-start | bytes 49160 | tf_op jit(solution)/shard_map/ppermute | solution.py:231
  43.3 0.7 %collective-permute-start.23 = (bf16[16,512]{1,0:T(8,128)(2,1)S(1)}, bf16[16,512]{1,0:T(8,128)(2,1)S(1)}, u32[]{:S(2)}, u32[]{:S(2)}) collective-permute-start(bf16[16,512]{1,0:T(8,128)(2,1)S(1)} %get-tuple-element.154), channel_id=1, source_target_pairs={{0,8},{1,9},{2,10},{3,11},{4,12},{5,13},{6,14},{7,15},{8,0},{9,1},... | collective-permute-start | bytes 49160 | tf_op jit(solution)/shard_map/ppermute | solution.py:231
  44.9 1.1 %collective-permute-start.24 = (bf16[16,512]{1,0:T(8,128)(2,1)S(1)}, bf16[16,512]{1,0:T(8,128)(2,1)S(1)}, u32[]{:S(2)}, u32[]{:S(2)}) collective-permute-start(bf16[16,512]{1,0:T(8,128)(2,1)S(1)} %get-tuple-element.155), channel_id=1, source_target_pairs={{0,1},{1,0},{2,3},{3,2},{4,5},{5,4},{6,7},{7,6},{8,9},{9,8},{10,11... | collective-permute-start | bytes 49160 | tf_op jit(solution)/shard_map/ppermute | solution.py:231
  46.0 1.9 %local_gradients.1 = (f32[256,512]{1,0:T(8,128)S(1)}, f32[64,512]{1,0:T(8,128)}, bf16[256,512]{1,0:T(8,128)(2,1)}) custom-call(bf16[256,512]{1,0:T(8,128)(2,1)S(1)} %copy-done.4, f32[400,512]{1,0:T(8,128)S(1)} %get-tuple-element.139.refs_1_, bf16[256,512]{1,0:T(8,128)(2,1)S(1)} %copy-done.5, bf16[400,512]{1,0:T(8,128)(2,1)S(1)} %get-tuple-element.140.refs_3_, ...), custom_call_target="tpu_custom_call" | custom-call | flops 402653184 | bytes 12042240 | tf_op jit(solution)/shard_map/local_gradients/pallas_call | solution.py:172
  48.2 1.0 %add_returned.1 = f32[256,512]{1,0:T(8,128)} custom-call(bf16[32,512]{1,0:T(8,128)(2,1)S(1)} %collective-permute-done.18.refs_0_, bf16[32,512]{1,0:T(8,128)(2,1)S(1)} %collective-permute-done.19.refs_1_, bf16[16,512]{1,0:T(8,128)(2,1)S(1)} %collective-permute-done.20.refs_2_, bf16[16,512]{1,0:T(8,128)(2,1)S(1)} %collective-permute-done.21.refs_3_, ...), custom_call_target="tpu_custom_call" | custom-call | tf_op jit(solution)/shard_map/add_returned/pallas_call | solution.py:911
  (74 shorter events, 4.9 us)
Async XLA Ops:
  2.3 9.6 %collective-permute-start = (bf16[32,1024]{1,0:T(8,128)(2,1)S(1)}, bf16[32,1024]{1,0:T(8,128)(2,1)S(1)}, u32[]{:S(2)}, u32[]{:S(2)}) collective-permute-start(bf16[32,1024]{1,0:T(8,128)(2,1)S(1)} %get-tuple-element.89), channel_id=1, source_target_pairs={{0,4},{1,5},{2,6},{3,7},{4,0},{5,1},{6,2},{7,3},{8,12},{9,13},{10,... | collective-permute-start | bytes 196616 | tf_op jit(solution)/shard_map/ppermute | solution.py:231
  5.4 9.4 %collective-permute-start.1 = (bf16[32,1024]{1,0:T(8,128)(2,1)S(1)}, bf16[32,1024]{1,0:T(8,128)(2,1)S(1)}, u32[]{:S(2)}, u32[]{:S(2)}) collective-permute-start(bf16[32,1024]{1,0:T(8,128)(2,1)S(1)} %get-tuple-element.92), channel_id=1, source_target_pairs={{0,12},{1,13},{2,14},{3,15},{4,8},{5,9},{6,10},{7,11},{8,4},{9,5},... | collective-permute-start | bytes 196616 | tf_op jit(solution)/shard_map/ppermute | solution.py:231
  7.9 4.4 %collective-permute-start.2 = (bf16[16,1024]{1,0:T(8,128)(2,1)S(1)}, bf16[16,1024]{1,0:T(8,128)(2,1)S(1)}, u32[]{:S(2)}, u32[]{:S(2)}) collective-permute-start(bf16[16,1024]{1,0:T(8,128)(2,1)S(1)} %get-tuple-element.93), channel_id=1, source_target_pairs={{0,3},{1,14},{2,5},{3,0},{4,7},{5,2},{6,9},{7,4},{8,11},{9,6},{10,... | collective-permute-start | bytes 98312 | tf_op jit(solution)/shard_map/ppermute | solution.py:231
  8.3 5.8 %collective-permute-start.3 = (bf16[16,1024]{1,0:T(8,128)(2,1)S(1)}, bf16[16,1024]{1,0:T(8,128)(2,1)S(1)}, u32[]{:S(2)}, u32[]{:S(2)}) collective-permute-start(bf16[16,1024]{1,0:T(8,128)(2,1)S(1)} %get-tuple-element.94), channel_id=1, source_target_pairs={{0,11},{1,6},{2,13},{3,8},{4,15},{5,10},{6,1},{7,12},{8,3},{9,14},... | collective-permute-start | bytes 98312 | tf_op jit(solution)/shard_map/ppermute | solution.py:231
  9.2 7.8 %collective-permute-start.4 = (bf16[16,1024]{1,0:T(8,128)(2,1)S(1)}, bf16[16,1024]{1,0:T(8,128)(2,1)S(1)}, u32[]{:S(2)}, u32[]{:S(2)}) collective-permute-start(bf16[16,1024]{1,0:T(8,128)(2,1)S(1)} %get-tuple-element.95), channel_id=1, source_target_pairs={{0,15},{1,2},{2,1},{3,4},{4,3},{5,6},{6,5},{7,8},{8,7},{9,10},{10,... | collective-permute-start | bytes 98312 | tf_op jit(solution)/shard_map/ppermute | solution.py:231
  12.0 5.2 %collective-permute-start.5 = (bf16[16,1024]{1,0:T(8,128)(2,1)S(1)}, bf16[16,1024]{1,0:T(8,128)(2,1)S(1)}, u32[]{:S(2)}, u32[]{:S(2)}) collective-permute-start(bf16[16,1024]{1,0:T(8,128)(2,1)S(1)} %get-tuple-element.96), channel_id=1, source_target_pairs={{0,8},{1,9},{2,10},{3,11},{4,12},{5,13},{6,14},{7,15},{8,0},{9,1},... | collective-permute-start | bytes 98312 | tf_op jit(solution)/shard_map/ppermute | solution.py:231
  12.3 4.8 %collective-permute-start.8 = (bf16[32,1024]{1,0:T(8,128)(2,1)S(1)}, bf16[32,1024]{1,0:T(8,128)(2,1)S(1)}, u32[]{:S(2)}, u32[]{:S(2)}) collective-permute-start(bf16[32,1024]{1,0:T(8,128)(2,1)S(1)} %collective-permute-done.refs_0_), channel_id=1, source_target_pairs={{0,1},{1,0},{2,3},{3,2},{4,5},{5,4},{6,7},{7,6},{8,9},{9,8},{10,11... | collective-permute-start | bytes 196616 | tf_op jit(solution)/shard_map/ppermute | solution.py:231
  20.0 6.8 %collective-permute-start.9 = (bf16[32,1024]{1,0:T(8,128)(2,1)S(1)}, bf16[32,1024]{1,0:T(8,128)(2,1)S(1)}, u32[]{:S(2)}, u32[]{:S(2)}) collective-permute-start(bf16[32,1024]{1,0:T(8,128)(2,1)S(1)} %get-tuple-element.109), channel_id=1, source_target_pairs={{0,12},{1,13},{2,14},{3,15},{4,8},{5,9},{6,10},{7,11},{8,4},{9,5},... | collective-permute-start | bytes 196616 | tf_op jit(solution)/shard_map/ppermute | solution.py:231
  21.9 7.0 %collective-permute-start.10 = (bf16[32,1024]{1,0:T(8,128)(2,1)S(1)}, bf16[32,1024]{1,0:T(8,128)(2,1)S(1)}, u32[]{:S(2)}, u32[]{:S(2)}) collective-permute-start(bf16[32,1024]{1,0:T(8,128)(2,1)S(1)} %get-tuple-element.112), channel_id=1, source_target_pairs={{0,4},{1,5},{2,6},{3,7},{4,0},{5,1},{6,2},{7,3},{8,12},{9,13},{10,... | collective-permute-start | bytes 196616 | tf_op jit(solution)/shard_map/ppermute | solution.py:231
  22.0 6.4 %collective-permute-start.11 = (bf16[16,1024]{1,0:T(8,128)(2,1)S(1)}, bf16[16,1024]{1,0:T(8,128)(2,1)S(1)}, u32[]{:S(2)}, u32[]{:S(2)}) collective-permute-start(bf16[16,1024]{1,0:T(8,128)(2,1)S(1)} %get-tuple-element.113), channel_id=1, source_target_pairs={{0,15},{1,2},{2,1},{3,4},{4,3},{5,6},{6,5},{7,8},{8,7},{9,10},{10,... | collective-permute-start | bytes 98312 | tf_op jit(solution)/shard_map/ppermute | solution.py:231
  24.1 4.3 %collective-permute-start.12 = (bf16[16,1024]{1,0:T(8,128)(2,1)S(1)}, bf16[16,1024]{1,0:T(8,128)(2,1)S(1)}, u32[]{:S(2)}, u32[]{:S(2)}) collective-permute-start(bf16[16,1024]{1,0:T(8,128)(2,1)S(1)} %get-tuple-element.114), channel_id=1, source_target_pairs={{0,3},{1,14},{2,5},{3,0},{4,7},{5,2},{6,9},{7,4},{8,11},{9,6},{10,... | collective-permute-start | bytes 98312 | tf_op jit(solution)/shard_map/ppermute | solution.py:231
  25.2 6.2 %collective-permute-start.13 = (bf16[16,1024]{1,0:T(8,128)(2,1)S(1)}, bf16[16,1024]{1,0:T(8,128)(2,1)S(1)}, u32[]{:S(2)}, u32[]{:S(2)}) collective-permute-start(bf16[16,1024]{1,0:T(8,128)(2,1)S(1)} %get-tuple-element.115), channel_id=1, source_target_pairs={{0,11},{1,6},{2,13},{3,8},{4,15},{5,10},{6,1},{7,12},{8,3},{9,14},... | collective-permute-start | bytes 98312 | tf_op jit(solution)/shard_map/ppermute | solution.py:231
  26.8 5.2 %collective-permute-start.14 = (bf16[16,1024]{1,0:T(8,128)(2,1)S(1)}, bf16[16,1024]{1,0:T(8,128)(2,1)S(1)}, u32[]{:S(2)}, u32[]{:S(2)}) collective-permute-start(bf16[16,1024]{1,0:T(8,128)(2,1)S(1)} %get-tuple-element.116), channel_id=1, source_target_pairs={{0,8},{1,9},{2,10},{3,11},{4,12},{5,13},{6,14},{7,15},{8,0},{9,1},... | collective-permute-start | bytes 98312 | tf_op jit(solution)/shard_map/ppermute | solution.py:231
  28.4 3.6 %collective-permute-start.16 = (bf16[32,1024]{1,0:T(8,128)(2,1)S(1)}, bf16[32,1024]{1,0:T(8,128)(2,1)S(1)}, u32[]{:S(2)}, u32[]{:S(2)}) collective-permute-start(bf16[32,1024]{1,0:T(8,128)(2,1)S(1)} %collective-permute-done.9.refs_0_), channel_id=1, source_target_pairs={{0,1},{1,0},{2,3},{3,2},{4,5},{5,4},{6,7},{7,6},{8,9},{9,8},{10,11... | collective-permute-start | bytes 196616 | tf_op jit(solution)/shard_map/ppermute | solution.py:231
  28.4 3.6 %collective-permute-start.15 = (bf16[16,1024]{1,0:T(8,128)(2,1)S(1)}, bf16[16,1024]{1,0:T(8,128)(2,1)S(1)}, u32[]{:S(2)}, u32[]{:S(2)}) collective-permute-start(bf16[16,1024]{1,0:T(8,128)(2,1)S(1)} %get-tuple-element.117), channel_id=1, source_target_pairs={{0,1},{1,0},{2,3},{3,2},{4,5},{5,4},{6,7},{7,6},{8,9},{9,8},{10,11... | collective-permute-start | bytes 98312 | tf_op jit(solution)/shard_map/ppermute | solution.py:231
  28.9 3.1 %collective-permute-start.17 = (bf16[32,1024]{1,0:T(8,128)(2,1)S(1)}, bf16[32,1024]{1,0:T(8,128)(2,1)S(1)}, u32[]{:S(2)}, u32[]{:S(2)}) collective-permute-start(bf16[32,1024]{1,0:T(8,128)(2,1)S(1)} %collective-permute-done.10.refs_1_), channel_id=1, source_target_pairs={{0,1},{1,0},{2,3},{3,2},{4,5},{5,4},{6,7},{7,6},{8,9},{9,8},{10,11... | collective-permute-start | bytes 196616 | tf_op jit(solution)/shard_map/ppermute | solution.py:231
  36.8 6.5 %collective-permute-start.18 = (bf16[32,512]{1,0:T(8,128)(2,1)S(1)}, bf16[32,512]{1,0:T(8,128)(2,1)S(1)}, u32[]{:S(2)}, u32[]{:S(2)}) collective-permute-start(bf16[32,512]{1,0:T(8,128)(2,1)S(1)} %get-tuple-element.147), channel_id=1, source_target_pairs={{0,12},{1,13},{2,14},{3,15},{4,8},{5,9},{6,10},{7,11},{8,4},{9,5},... | collective-permute-start | bytes 98312 | tf_op jit(solution)/shard_map/ppermute | solution.py:231
  38.4 7.6 %collective-permute-start.19 = (bf16[32,512]{1,0:T(8,128)(2,1)S(1)}, bf16[32,512]{1,0:T(8,128)(2,1)S(1)}, u32[]{:S(2)}, u32[]{:S(2)}) collective-permute-start(bf16[32,512]{1,0:T(8,128)(2,1)S(1)} %get-tuple-element.150), channel_id=1, source_target_pairs={{0,4},{1,5},{2,6},{3,7},{4,0},{5,1},{6,2},{7,3},{8,12},{9,13},{10,... | collective-permute-start | bytes 98312 | tf_op jit(solution)/shard_map/ppermute | solution.py:231
  38.5 5.9 %collective-permute-start.20 = (bf16[16,512]{1,0:T(8,128)(2,1)S(1)}, bf16[16,512]{1,0:T(8,128)(2,1)S(1)}, u32[]{:S(2)}, u32[]{:S(2)}) collective-permute-start(bf16[16,512]{1,0:T(8,128)(2,1)S(1)} %get-tuple-element.151), channel_id=1, source_target_pairs={{0,15},{1,2},{2,1},{3,4},{4,3},{5,6},{6,5},{7,8},{8,7},{9,10},{10,... | collective-permute-start | bytes 49160 | tf_op jit(solution)/shard_map/ppermute | solution.py:231
  40.0 5.0 %collective-permute-start.21 = (bf16[16,512]{1,0:T(8,128)(2,1)S(1)}, bf16[16,512]{1,0:T(8,128)(2,1)S(1)}, u32[]{:S(2)}, u32[]{:S(2)}) collective-permute-start(bf16[16,512]{1,0:T(8,128)(2,1)S(1)} %get-tuple-element.152), channel_id=1, source_target_pairs={{0,3},{1,14},{2,5},{3,0},{4,7},{5,2},{6,9},{7,4},{8,11},{9,6},{10,... | collective-permute-start | bytes 49160 | tf_op jit(solution)/shard_map/ppermute | solution.py:231
  41.6 6.4 %collective-permute-start.22 = (bf16[16,512]{1,0:T(8,128)(2,1)S(1)}, bf16[16,512]{1,0:T(8,128)(2,1)S(1)}, u32[]{:S(2)}, u32[]{:S(2)}) collective-permute-start(bf16[16,512]{1,0:T(8,128)(2,1)S(1)} %get-tuple-element.153), channel_id=1, source_target_pairs={{0,11},{1,6},{2,13},{3,8},{4,15},{5,10},{6,1},{7,12},{8,3},{9,14},... | collective-permute-start | bytes 49160 | tf_op jit(solution)/shard_map/ppermute | solution.py:231
  43.3 4.8 %collective-permute-start.23 = (bf16[16,512]{1,0:T(8,128)(2,1)S(1)}, bf16[16,512]{1,0:T(8,128)(2,1)S(1)}, u32[]{:S(2)}, u32[]{:S(2)}) collective-permute-start(bf16[16,512]{1,0:T(8,128)(2,1)S(1)} %get-tuple-element.154), channel_id=1, source_target_pairs={{0,8},{1,9},{2,10},{3,11},{4,12},{5,13},{6,14},{7,15},{8,0},{9,1},... | collective-permute-start | bytes 49160 | tf_op jit(solution)/shard_map/ppermute | solution.py:231
  44.4 3.8 %collective-permute-start.25 = (bf16[32,512]{1,0:T(8,128)(2,1)S(1)}, bf16[32,512]{1,0:T(8,128)(2,1)S(1)}, u32[]{:S(2)}, u32[]{:S(2)}) collective-permute-start(bf16[32,512]{1,0:T(8,128)(2,1)S(1)} %collective-permute-done.18.refs_0_), channel_id=1, source_target_pairs={{0,1},{1,0},{2,3},{3,2},{4,5},{5,4},{6,7},{7,6},{8,9},{9,8},{10,11... | collective-permute-start | bytes 98312 | tf_op jit(solution)/shard_map/ppermute | solution.py:231
  44.9 3.2 %collective-permute-start.24 = (bf16[16,512]{1,0:T(8,128)(2,1)S(1)}, bf16[16,512]{1,0:T(8,128)(2,1)S(1)}, u32[]{:S(2)}, u32[]{:S(2)}) collective-permute-start(bf16[16,512]{1,0:T(8,128)(2,1)S(1)} %get-tuple-element.155), channel_id=1, source_target_pairs={{0,1},{1,0},{2,3},{3,2},{4,5},{5,4},{6,7},{7,6},{8,9},{9,8},{10,11... | collective-permute-start | bytes 49160 | tf_op jit(solution)/shard_map/ppermute | solution.py:231
  (21 other events, 224.9 us)

commit v18 on v17

--- a/solution.py
+++ b/solution.py
@@ -592,6 +592,10 @@
             mesh_first_ref,
             dec_pool_ref,
             dec_normed_ref,
+            mesh_second_ref,
+            mesh_centred_ref,
+            dec_first_ref,
+            mesh_cot_ref,
             mesh_ref,
             enc_pre_ref,
             dec_pre_ref,
@@ -604,6 +608,9 @@
             grid_wide_ref,
             grid_back_ref,
             mesh_back_ref,
+            mesh_in_ref,
+            mesh_cot_turned_ref,
+            mesh_turned_ref,
             mesh_out_ref,
             mesh_slope_ref,
             enc_slope_ref,
@@ -620,6 +627,10 @@
         cot_turned_ref[...] = mm_t(cot_rows_ref[...], second)
         grid_back_ref[...] = centred(grid_first_ref[high, :], 0).astype(BF16)
         mesh_back_ref[...] = centred(mesh_first_ref[high, :], 0).astype(BF16)
+        mesh_in_ref[low, :] = dec_first_ref[high, :]
+        mesh_in_ref[high, :] = mm(mesh_centred_ref[...], dec_first_ref[high, :]).astype(BF16)
+        mesh_cot_turned_ref[...] = mm_t(mesh_cot_ref[...], mesh_centred_ref[...])
+        mesh_turned_ref[...] = mm_t(mesh_normed_ref[...].astype(BF16), mesh_second_ref[...])
         local_sums_ref[...] = mm(dec_pool_ref[:grid_count, :], dec_normed_ref[...])
         mesh_slope_ref[...] = silu_and_slope(mesh_pre_ref[...])[1]
         write_slope(enc_pre_ref, enc_slope_ref)
@@ -633,6 +644,9 @@
         grid_wide,
         grid_back,
         mesh_back,
+        mesh_in,
+        mesh_cot_turned,
+        mesh_turned,
         mesh_out,
         mesh_slope,
         enc_slope,
@@ -649,6 +663,10 @@
             mesh_first,
             dec_pool,
             dec_normed,
+            mesh_second,
+            mesh_centred,
+            dec_first,
+            mesh_cot,
             mesh_nodes,
             enc_pre,
             dec_pre,
@@ -663,6 +681,9 @@
             ((feat, 2 * feat), BF16),
             ((feat, feat), BF16),
             ((feat, feat), BF16),
+            ((2 * feat, feat), BF16),
+            ((mesh_count, feat), F32),
+            ((mesh_count, feat), F32),
             ((mesh_count, feat), BF16),
             ((mesh_count, feat), F32),
             ((enc_count, feat), BF16),
@@ -681,6 +702,7 @@
             cot_rows_ref,
             cot_turned_ref,
             mesh_cot_ref,
+            mesh_cot_turned_ref,
             enc_pick_ref,
             enc_pool_ref,
             dec_pick_ref,
@@ -689,7 +711,7 @@
             grid_wide_ref,
             grid_back_ref,
             mesh_back_ref,
-            mesh_second_ref,
+            mesh_in_ref,
             enc_first_ref,
             enc_second_ref,
             dec_first_ref,
@@ -703,8 +725,9 @@
             mesh_normed_ref,
             mesh_scale_ref,
             mesh_slope_ref,
-        ) = refs[:29]
-        refs = refs[29:]
+            mesh_turned_ref,
+        ) = refs[:31]
+        refs = refs[31:]
         out_refs, refs = refs[:sent_count], refs[sent_count:]
         (
             grid_normed_ref,
@@ -749,14 +772,12 @@
             dec_gpre_ref,
         )
         mesh_sum = mm(dec_pool_ref[mesh_rows, :], dec_gpre_ref[...]).astype(BF16)
-        mesh_gin = mesh_cot_ref[...].astype(F32) + mm_t(mesh_sum, dec_first_ref[high, :])
+        both = mm_t(mesh_sum, mesh_in_ref[...])
+        mesh_gin = mesh_cot_ref[...].astype(F32) + both[:, low]
         mesh_gin_ref[...] = mesh_gin
-        normed = mesh_normed_ref[...]
-        upstream = centred(mesh_gin, 1)
-        mean = jnp.mean(upstream * normed, axis=-1, keepdims=True)
-        mesh_gout = (mesh_scale_ref[...] * (upstream - normed * mean)).astype(BF16)
-        raw = mm_t(mesh_gout, mesh_second_ref[...])
-        mesh_gpre_ref[...] = (raw * mesh_slope_ref[...]).astype(BF16)
+        mean = jnp.mean(mesh_gin * mesh_normed_ref[...], axis=-1, keepdims=True)
+        raw = mesh_cot_turned_ref[...] + both[:, high] - mean * mesh_turned_ref[...]
+        mesh_gpre_ref[...] = (mesh_scale_ref[...] * raw * mesh_slope_ref[...]).astype(BF16)
         mesh_gagg = mm_t(mesh_gpre_ref[...], mesh_back_ref[...]).astype(BF16)
         pooled = mm(dec_pool_ref[grid_count:spots, :], dec_gpre_ref[...]).astype(BF16)
         slot_back = mm_t(pooled, dec_first_ref[low, :])
@@ -784,6 +805,7 @@
             cot_rows,
             cot_turned,
             mesh_cot,
+            mesh_cot_turned,
             enc_pick,
             enc_pool,
             dec_pick,
@@ -792,7 +814,7 @@
             grid_wide,
             grid_back,
             mesh_back,
-            mesh_second,
+            mesh_in,
             enc_first,
             enc_second,
             dec_first,
@@ -806,6 +828,7 @@
             mesh_normed,
             mesh_scale,
             mesh_slope,
+            mesh_turned,
         ],
         sent_shapes(feat)
         + [

time: 49.3 us -> 49.2 us (level)
  waiting for transfers between devices: 2.7 us -> 2.06 us
    ppermute x27, waiting for transfers between devices: 2.7 us -> 2.06 us  [permute(): return lax.ppermute(part, 'tile', pairs)]
  transfers between devices with their start and end apart: 27 -> 27, of which waited for: 7 -> 7; matrix products, arithmetic and copies ran while one was open for 0% -> 0% of each run, Pallas kernels for 13% -> 14%
where the time goes in v18:
time: 49.2 us; the launch traced here: 49 us
  starting transfers between devices  29.1 us (59%)
  Pallas kernels  16.8 us (34%)
  waiting for transfers between devices  2.06 us (4%)
  between operations  0.97 us (2%)
    ppermute x27, starting transfers between devices, permute(): return lax.ppermute(part, 'tile', pairs)  29.1 us
    pallas_call x7, Pallas kernels, call(): pl.pallas_call(kernel, name=name, in_specs=specs, out_specs=[pl.BlockSpec...  15.8 us
    ppermute x27, waiting for transfers between devices, permute(): return lax.ppermute(part, 'tile', pairs)  2.06 us
    pallas_call x1, Pallas kernels, per_device(): pl.pallas_call(finish, name='add_returned', in_specs=[pl.BlockSpec(memory...  1 us
  transfers between devices with their start and end apart: 27, of which 7 were waited for; matrix products, arithmetic and copies ran while one was open for 0% of the time, Pallas kernels for 14%

profile of v18, /device:TPU:0, one launch (start us, length us, event | category | flops | bytes accessed | tf_op | source)
XLA Modules:
  0.0 49.0 jit_solution(16513416701481341985)
XLA Ops:
  0.6 1.4 %pack_rows.1 = (bf16[256,256]{1,0:T(8,128)(2,1)S(1)}, bf16[32,1024]{1,0:T(8,128)(2,1)S(1)}, bf16[32,1024]{1,0:T(8,128)(2,1)S(1)}, bf16[16,1024]{1,0:T(8,128)(2,1...) custom-call(s32[9,16]{1,0:T(8,128)} %refs_0_.2, ...), custom_call_target="tpu_custom_call" | custom-call | flops 75497472 | bytes 950884 | tf_op jit(solution)/shard_map/pack_rows/pallas_call | solution.py:172
  2.3 3.1 %collective-permute-start = (bf16[32,1024]{1,0:T(8,128)(2,1)S(1)}, bf16[32,1024]{1,0:T(8,128)(2,1)S(1)}, u32[]{:S(2)}, u32[]{:S(2)}) collective-permute-start(bf16[32,1024]{1,0:T(8,128)(2,1)S(1)} %get-tuple-element.92), channel_id=1, source_target_pairs={{0,4},{1,5},{2,6},{3,7},{4,0},{5,1},{6,2},{7,3},{8,12},{9,13},{10,... | collective-permute-start | bytes 196616 | tf_op jit(solution)/shard_map/ppermute | solution.py:231
  5.4 2.5 %collective-permute-start.1 = (bf16[32,1024]{1,0:T(8,128)(2,1)S(1)}, bf16[32,1024]{1,0:T(8,128)(2,1)S(1)}, u32[]{:S(2)}, u32[]{:S(2)}) collective-permute-start(bf16[32,1024]{1,0:T(8,128)(2,1)S(1)} %get-tuple-element.95), channel_id=1, source_target_pairs={{0,12},{1,13},{2,14},{3,15},{4,8},{5,9},{6,10},{7,11},{8,4},{9,5},... | collective-permute-start | bytes 196616 | tf_op jit(solution)/shard_map/ppermute | solution.py:231
  8.3 0.9 %collective-permute-start.3 = (bf16[16,1024]{1,0:T(8,128)(2,1)S(1)}, bf16[16,1024]{1,0:T(8,128)(2,1)S(1)}, u32[]{:S(2)}, u32[]{:S(2)}) collective-permute-start(bf16[16,1024]{1,0:T(8,128)(2,1)S(1)} %get-tuple-element.97), channel_id=1, source_target_pairs={{0,11},{1,6},{2,13},{3,8},{4,15},{5,10},{6,1},{7,12},{8,3},{9,14},... | collective-permute-start | bytes 98312 | tf_op jit(solution)/shard_map/ppermute | solution.py:231
  9.2 2.8 %collective-permute-start.4 = (bf16[16,1024]{1,0:T(8,128)(2,1)S(1)}, bf16[16,1024]{1,0:T(8,128)(2,1)S(1)}, u32[]{:S(2)}, u32[]{:S(2)}) collective-permute-start(bf16[16,1024]{1,0:T(8,128)(2,1)S(1)} %get-tuple-element.98), channel_id=1, source_target_pairs={{0,15},{1,2},{2,1},{3,4},{4,3},{5,6},{6,5},{7,8},{8,7},{9,10},{10,... | collective-permute-start | bytes 98312 | tf_op jit(solution)/shard_map/ppermute | solution.py:231
  12.3 1.2 %collective-permute-start.8 = (bf16[32,1024]{1,0:T(8,128)(2,1)S(1)}, bf16[32,1024]{1,0:T(8,128)(2,1)S(1)}, u32[]{:S(2)}, u32[]{:S(2)}) collective-permute-start(bf16[32,1024]{1,0:T(8,128)(2,1)S(1)} %collective-permute-done.refs_0_), channel_id=1, source_target_pairs={{0,1},{1,0},{2,3},{3,2},{4,5},{5,4},{6,7},{7,6},{8,9},{9,8},{10,11... | collective-permute-start | bytes 196616 | tf_op jit(solution)/shard_map/ppermute | solution.py:231
  14.1 0.7 %collective-permute-start.6 = (bf16[16,1024]{1,0:T(8,128)(2,1)S(1)}, bf16[16,1024]{1,0:T(8,128)(2,1)S(1)}, u32[]{:S(2)}, u32[]{:S(2)}) collective-permute-start(bf16[16,1024]{1,0:T(8,128)(2,1)S(1)} %get-tuple-element.100), channel_id=1, source_target_pairs={{0,1},{1,0},{2,3},{3,2},{4,5},{5,4},{6,7},{7,6},{8,9},{9,8},{10,11... | collective-permute-start | bytes 98312 | tf_op jit(solution)/shard_map/ppermute | solution.py:231
  15.0 2.0 %local_products.1 = (f32[384,512]{1,0:T(8,128)S(1)}, f32[768,512]{1,0:T(8,128)S(1)}, f32[64,512]{1,0:T(8,128)S(1)}, bf16[384,512]{1,0:T(8,128)(2,1)S(1)}, bf16[5...) custom-call(bf16[256,256]{1,0:T(8,128)(2,1)S(1)} %get-tuple-element., ...), custom_call_target="tpu_custom_call" | custom-call | flops 1275068416 | bytes 14058496 | tf_op jit(solution)/shard_map/local_products/pallas_call | solution.py:172
  17.2 2.8 %edges_forward.1 = (bf16[32,1024]{1,0:T(8,128)(2,1)S(1)}, bf16[32,1024]{1,0:T(8,128)(2,1)S(1)}, bf16[16,1024]{1,0:T(8,128)(2,1)S(1)}, bf16[16,1024]{1,0:T(8,128)...) custom-call(bf16[32,1024]{1,0:T(8,128)(2,1)S(1)} %collective-permute, ...), custom_call_target="tpu_custom_call" | custom-call | flops 1207959552 | bytes 17298176 | tf_op jit(solution)/shard_map/edges_forward/pallas_call | solution.py:172
  20.0 2.0 %collective-permute-start.9 = (bf16[32,1024]{1,0:T(8,128)(2,1)S(1)}, bf16[32,1024]{1,0:T(8,128)(2,1)S(1)}, u32[]{:S(2)}, u32[]{:S(2)}) collective-permute-start(bf16[32,1024]{1,0:T(8,128)(2,1)S(1)} %get-tuple-element.112), channel_id=1, source_target_pairs={{0,12},{1,13},{2,14},{3,15},{4,8},{5,9},{6,10},{7,11},{8,4},{9,5},... | collective-permute-start | bytes 196616 | tf_op jit(solution)/shard_map/ppermute | solution.py:231
  22.0 2.2 %collective-permute-start.11 = (bf16[16,1024]{1,0:T(8,128)(2,1)S(1)}, bf16[16,1024]{1,0:T(8,128)(2,1)S(1)}, u32[]{:S(2)}, u32[]{:S(2)}) collective-permute-start(bf16[16,1024]{1,0:T(8,128)(2,1)S(1)} %get-tuple-element.116), channel_id=1, source_target_pairs={{0,15},{1,2},{2,1},{3,4},{4,3},{5,6},{6,5},{7,8},{8,7},{9,10},{10,... | collective-permute-start | bytes 98312 | tf_op jit(solution)/shard_map/ppermute | solution.py:231
  24.1 1.0 %collective-permute-start.12 = (bf16[16,1024]{1,0:T(8,128)(2,1)S(1)}, bf16[16,1024]{1,0:T(8,128)(2,1)S(1)}, u32[]{:S(2)}, u32[]{:S(2)}) collective-permute-start(bf16[16,1024]{1,0:T(8,128)(2,1)S(1)} %get-tuple-element.117), channel_id=1, source_target_pairs={{0,3},{1,14},{2,5},{3,0},{4,7},{5,2},{6,9},{7,4},{8,11},{9,6},{10,... | collective-permute-start | bytes 98312 | tf_op jit(solution)/shard_map/ppermute | solution.py:231
  25.2 1.0 %collective-permute-start.13 = (bf16[16,1024]{1,0:T(8,128)(2,1)S(1)}, bf16[16,1024]{1,0:T(8,128)(2,1)S(1)}, u32[]{:S(2)}, u32[]{:S(2)}) collective-permute-start(bf16[16,1024]{1,0:T(8,128)(2,1)S(1)} %get-tuple-element.118), channel_id=1, source_target_pairs={{0,11},{1,6},{2,13},{3,8},{4,15},{5,10},{6,1},{7,12},{8,3},{9,14},... | collective-permute-start | bytes 98312 | tf_op jit(solution)/shard_map/ppermute | solution.py:231
  26.8 1.5 %collective-permute-start.14 = (bf16[16,1024]{1,0:T(8,128)(2,1)S(1)}, bf16[16,1024]{1,0:T(8,128)(2,1)S(1)}, u32[]{:S(2)}, u32[]{:S(2)}) collective-permute-start(bf16[16,1024]{1,0:T(8,128)(2,1)S(1)} %get-tuple-element.119), channel_id=1, source_target_pairs={{0,8},{1,9},{2,10},{3,11},{4,12},{5,13},{6,14},{7,15},{8,0},{9,1},... | collective-permute-start | bytes 98312 | tf_op jit(solution)/shard_map/ppermute | solution.py:231
  29.0 2.9 %slopes_and_nodes.1 = (f32[256,512]{1,0:T(8,128)S(1)}, f32[400,512]{1,0:T(8,128)S(1)}, bf16[400,512]{1,0:T(8,128)(2,1)S(1)}, f32[400,512]{1,0:T(8,128)S(1)}, bf1...) custom-call(bf16[32,1024]{1,0:T(8,128)(2,1)S(1)} %collective-permute, ...), custom_call_target="tpu_custom_call" | custom-call | flops 1677721600 | bytes 17874944 | tf_op jit(solution)/shard_map/slopes_and_nodes/pallas_call | solution.py:172
  32.0 4.6 %edges_backward.1 = (bf16[32,512]{1,0:T(8,128)(2,1)S(1)}, bf16[32,512]{1,0:T(8,128)(2,1)S(1)}, bf16[16,512]{1,0:T(8,128)(2,1)S(1)}, bf16[16,512]{1,0:T(8,128)(2,...) custom-call(bf16[32,1024]{1,0:T(8,128)(2,1)S(1)} %collective-permute, ...), custom_call_target="tpu_custom_call" | custom-call | flops 2449473536 | bytes 19878656 | tf_op jit(solution)/shard_map/edges_backward/pallas_call | solution.py:172
  36.6 1.6 %collective-permute-start.18 = (bf16[32,512]{1,0:T(8,128)(2,1)S(1)}, bf16[32,512]{1,0:T(8,128)(2,1)S(1)}, u32[]{:S(2)}, u32[]{:S(2)}) collective-permute-start(bf16[32,512]{1,0:T(8,128)(2,1)S(1)} %get-tuple-element.153), channel_id=1, source_target_pairs={{0,12},{1,13},{2,14},{3,15},{4,8},{5,9},{6,10},{7,11},{8,4},{9,5},... | collective-permute-start | bytes 98312 | tf_op jit(solution)/shard_map/ppermute | solution.py:231
  38.8 1.5 %collective-permute-start.20 = (bf16[16,512]{1,0:T(8,128)(2,1)S(1)}, bf16[16,512]{1,0:T(8,128)(2,1)S(1)}, u32[]{:S(2)}, u32[]{:S(2)}) collective-permute-start(bf16[16,512]{1,0:T(8,128)(2,1)S(1)} %get-tuple-element.157), channel_id=1, source_target_pairs={{0,15},{1,2},{2,1},{3,4},{4,3},{5,6},{6,5},{7,8},{8,7},{9,10},{10,... | collective-permute-start | bytes 49160 | tf_op jit(solution)/shard_map/ppermute | solution.py:231
  40.3 1.1 %collective-permute-start.21 = (bf16[16,512]{1,0:T(8,128)(2,1)S(1)}, bf16[16,512]{1,0:T(8,128)(2,1)S(1)}, u32[]{:S(2)}, u32[]{:S(2)}) collective-permute-start(bf16[16,512]{1,0:T(8,128)(2,1)S(1)} %get-tuple-element.158), channel_id=1, source_target_pairs={{0,3},{1,14},{2,5},{3,0},{4,7},{5,2},{6,9},{7,4},{8,11},{9,6},{10,... | collective-permute-start | bytes 49160 | tf_op jit(solution)/shard_map/ppermute | solution.py:231
  41.4 1.7 %collective-permute-start.22 = (bf16[16,512]{1,0:T(8,128)(2,1)S(1)}, bf16[16,512]{1,0:T(8,128)(2,1)S(1)}, u32[]{:S(2)}, u32[]{:S(2)}) collective-permute-start(bf16[16,512]{1,0:T(8,128)(2,1)S(1)} %get-tuple-element.159), channel_id=1, source_target_pairs={{0,11},{1,6},{2,13},{3,8},{4,15},{5,10},{6,1},{7,12},{8,3},{9,14},... | collective-permute-start | bytes 49160 | tf_op jit(solution)/shard_map/ppermute | solution.py:231
  43.1 1.3 %collective-permute-start.23 = (bf16[16,512]{1,0:T(8,128)(2,1)S(1)}, bf16[16,512]{1,0:T(8,128)(2,1)S(1)}, u32[]{:S(2)}, u32[]{:S(2)}) collective-permute-start(bf16[16,512]{1,0:T(8,128)(2,1)S(1)} %get-tuple-element.160), channel_id=1, source_target_pairs={{0,8},{1,9},{2,10},{3,11},{4,12},{5,13},{6,14},{7,15},{8,0},{9,1},... | collective-permute-start | bytes 49160 | tf_op jit(solution)/shard_map/ppermute | solution.py:231
  44.7 1.1 %collective-permute-start.24 = (bf16[16,512]{1,0:T(8,128)(2,1)S(1)}, bf16[16,512]{1,0:T(8,128)(2,1)S(1)}, u32[]{:S(2)}, u32[]{:S(2)}) collective-permute-start(bf16[16,512]{1,0:T(8,128)(2,1)S(1)} %get-tuple-element.161), channel_id=1, source_target_pairs={{0,1},{1,0},{2,3},{3,2},{4,5},{5,4},{6,7},{7,6},{8,9},{9,8},{10,11... | collective-permute-start | bytes 49160 | tf_op jit(solution)/shard_map/ppermute | solution.py:231
  45.9 1.9 %local_gradients.1 = (f32[256,512]{1,0:T(8,128)S(1)}, f32[64,512]{1,0:T(8,128)}, bf16[256,512]{1,0:T(8,128)(2,1)}) custom-call(bf16[256,512]{1,0:T(8,128)(2,1)S(1)} %copy-done.4, f32[400,512]{1,0:T(8,128)S(1)} %get-tuple-element.145.refs_1_, bf16[256,512]{1,0:T(8,128)(2,1)S(1)} %copy-done.5, bf16[400,512]{1,0:T(8,128)(2,1)S(1)} %get-tuple-element.146.refs_3_, ...), custom_call_target="tpu_custom_call" | custom-call | flops 402653184 | bytes 12042240 | tf_op jit(solution)/shard_map/local_gradients/pallas_call | solution.py:172
  48.0 1.0 %add_returned.1 = f32[256,512]{1,0:T(8,128)} custom-call(bf16[32,512]{1,0:T(8,128)(2,1)S(1)} %collective-permute-done.18.refs_0_, bf16[32,512]{1,0:T(8,128)(2,1)S(1)} %collective-permute-done.19.refs_1_, bf16[16,512]{1,0:T(8,128)(2,1)S(1)} %collective-permute-done.20.refs_2_, bf16[16,512]{1,0:T(8,128)(2,1)S(1)} %collective-permute-done.21.refs_3_, ...), custom_call_target="tpu_custom_call" | custom-call | tf_op jit(solution)/shard_map/add_returned/pallas_call | solution.py:934
  (74 shorter events, 4.2 us)
Async XLA Ops:
  2.3 9.6 %collective-permute-start = (bf16[32,1024]{1,0:T(8,128)(2,1)S(1)}, bf16[32,1024]{1,0:T(8,128)(2,1)S(1)}, u32[]{:S(2)}, u32[]{:S(2)}) collective-permute-start(bf16[32,1024]{1,0:T(8,128)(2,1)S(1)} %get-tuple-element.92), channel_id=1, source_target_pairs={{0,4},{1,5},{2,6},{3,7},{4,0},{5,1},{6,2},{7,3},{8,12},{9,13},{10,... | collective-permute-start | bytes 196616 | tf_op jit(solution)/shard_map/ppermute | solution.py:231
  5.4 9.4 %collective-permute-start.1 = (bf16[32,1024]{1,0:T(8,128)(2,1)S(1)}, bf16[32,1024]{1,0:T(8,128)(2,1)S(1)}, u32[]{:S(2)}, u32[]{:S(2)}) collective-permute-start(bf16[32,1024]{1,0:T(8,128)(2,1)S(1)} %get-tuple-element.95), channel_id=1, source_target_pairs={{0,12},{1,13},{2,14},{3,15},{4,8},{5,9},{6,10},{7,11},{8,4},{9,5},... | collective-permute-start | bytes 196616 | tf_op jit(solution)/shard_map/ppermute | solution.py:231
  7.9 4.4 %collective-permute-start.2 = (bf16[16,1024]{1,0:T(8,128)(2,1)S(1)}, bf16[16,1024]{1,0:T(8,128)(2,1)S(1)}, u32[]{:S(2)}, u32[]{:S(2)}) collective-permute-start(bf16[16,1024]{1,0:T(8,128)(2,1)S(1)} %get-tuple-element.96), channel_id=1, source_target_pairs={{0,3},{1,14},{2,5},{3,0},{4,7},{5,2},{6,9},{7,4},{8,11},{9,6},{10,... | collective-permute-start | bytes 98312 | tf_op jit(solution)/shard_map/ppermute | solution.py:231
  8.3 5.8 %collective-permute-start.3 = (bf16[16,1024]{1,0:T(8,128)(2,1)S(1)}, bf16[16,1024]{1,0:T(8,128)(2,1)S(1)}, u32[]{:S(2)}, u32[]{:S(2)}) collective-permute-start(bf16[16,1024]{1,0:T(8,128)(2,1)S(1)} %get-tuple-element.97), channel_id=1, source_target_pairs={{0,11},{1,6},{2,13},{3,8},{4,15},{5,10},{6,1},{7,12},{8,3},{9,14},... | collective-permute-start | bytes 98312 | tf_op jit(solution)/shard_map/ppermute | solution.py:231
  9.2 7.8 %collective-permute-start.4 = (bf16[16,1024]{1,0:T(8,128)(2,1)S(1)}, bf16[16,1024]{1,0:T(8,128)(2,1)S(1)}, u32[]{:S(2)}, u32[]{:S(2)}) collective-permute-start(bf16[16,1024]{1,0:T(8,128)(2,1)S(1)} %get-tuple-element.98), channel_id=1, source_target_pairs={{0,15},{1,2},{2,1},{3,4},{4,3},{5,6},{6,5},{7,8},{8,7},{9,10},{10,... | collective-permute-start | bytes 98312 | tf_op jit(solution)/shard_map/ppermute | solution.py:231
  12.0 5.2 %collective-permute-start.5 = (bf16[16,1024]{1,0:T(8,128)(2,1)S(1)}, bf16[16,1024]{1,0:T(8,128)(2,1)S(1)}, u32[]{:S(2)}, u32[]{:S(2)}) collective-permute-start(bf16[16,1024]{1,0:T(8,128)(2,1)S(1)} %get-tuple-element.99), channel_id=1, source_target_pairs={{0,8},{1,9},{2,10},{3,11},{4,12},{5,13},{6,14},{7,15},{8,0},{9,1},... | collective-permute-start | bytes 98312 | tf_op jit(solution)/shard_map/ppermute | solution.py:231
  12.3 4.8 %collective-permute-start.8 = (bf16[32,1024]{1,0:T(8,128)(2,1)S(1)}, bf16[32,1024]{1,0:T(8,128)(2,1)S(1)}, u32[]{:S(2)}, u32[]{:S(2)}) collective-permute-start(bf16[32,1024]{1,0:T(8,128)(2,1)S(1)} %collective-permute-done.refs_0_), channel_id=1, source_target_pairs={{0,1},{1,0},{2,3},{3,2},{4,5},{5,4},{6,7},{7,6},{8,9},{9,8},{10,11... | collective-permute-start | bytes 196616 | tf_op jit(solution)/shard_map/ppermute | solution.py:231
  20.0 6.8 %collective-permute-start.9 = (bf16[32,1024]{1,0:T(8,128)(2,1)S(1)}, bf16[32,1024]{1,0:T(8,128)(2,1)S(1)}, u32[]{:S(2)}, u32[]{:S(2)}) collective-permute-start(bf16[32,1024]{1,0:T(8,128)(2,1)S(1)} %get-tuple-element.112), channel_id=1, source_target_pairs={{0,12},{1,13},{2,14},{3,15},{4,8},{5,9},{6,10},{7,11},{8,4},{9,5},... | collective-permute-start | bytes 196616 | tf_op jit(solution)/shard_map/ppermute | solution.py:231
  22.0 7.0 %collective-permute-start.10 = (bf16[32,1024]{1,0:T(8,128)(2,1)S(1)}, bf16[32,1024]{1,0:T(8,128)(2,1)S(1)}, u32[]{:S(2)}, u32[]{:S(2)}) collective-permute-start(bf16[32,1024]{1,0:T(8,128)(2,1)S(1)} %get-tuple-element.115), channel_id=1, source_target_pairs={{0,4},{1,5},{2,6},{3,7},{4,0},{5,1},{6,2},{7,3},{8,12},{9,13},{10,... | collective-permute-start | bytes 196616 | tf_op jit(solution)/shard_map/ppermute | solution.py:231
  22.0 6.4 %collective-permute-start.11 = (bf16[16,1024]{1,0:T(8,128)(2,1)S(1)}, bf16[16,1024]{1,0:T(8,128)(2,1)S(1)}, u32[]{:S(2)}, u32[]{:S(2)}) collective-permute-start(bf16[16,1024]{1,0:T(8,128)(2,1)S(1)} %get-tuple-element.116), channel_id=1, source_target_pairs={{0,15},{1,2},{2,1},{3,4},{4,3},{5,6},{6,5},{7,8},{8,7},{9,10},{10,... | collective-permute-start | bytes 98312 | tf_op jit(solution)/shard_map/ppermute | solution.py:231
  24.1 4.3 %collective-permute-start.12 = (bf16[16,1024]{1,0:T(8,128)(2,1)S(1)}, bf16[16,1024]{1,0:T(8,128)(2,1)S(1)}, u32[]{:S(2)}, u32[]{:S(2)}) collective-permute-start(bf16[16,1024]{1,0:T(8,128)(2,1)S(1)} %get-tuple-element.117), channel_id=1, source_target_pairs={{0,3},{1,14},{2,5},{3,0},{4,7},{5,2},{6,9},{7,4},{8,11},{9,6},{10,... | collective-permute-start | bytes 98312 | tf_op jit(solution)/shard_map/ppermute | solution.py:231
  25.2 6.7 %collective-permute-start.13 = (bf16[16,1024]{1,0:T(8,128)(2,1)S(1)}, bf16[16,1024]{1,0:T(8,128)(2,1)S(1)}, u32[]{:S(2)}, u32[]{:S(2)}) collective-permute-start(bf16[16,1024]{1,0:T(8,128)(2,1)S(1)} %get-tuple-element.118), channel_id=1, source_target_pairs={{0,11},{1,6},{2,13},{3,8},{4,15},{5,10},{6,1},{7,12},{8,3},{9,14},... | collective-permute-start | bytes 98312 | tf_op jit(solution)/shard_map/ppermute | solution.py:231
  26.8 5.2 %collective-permute-start.14 = (bf16[16,1024]{1,0:T(8,128)(2,1)S(1)}, bf16[16,1024]{1,0:T(8,128)(2,1)S(1)}, u32[]{:S(2)}, u32[]{:S(2)}) collective-permute-start(bf16[16,1024]{1,0:T(8,128)(2,1)S(1)} %get-tuple-element.119), channel_id=1, source_target_pairs={{0,8},{1,9},{2,10},{3,11},{4,12},{5,13},{6,14},{7,15},{8,0},{9,1},... | collective-permute-start | bytes 98312 | tf_op jit(solution)/shard_map/ppermute | solution.py:231
  28.4 3.6 %collective-permute-start.16 = (bf16[32,1024]{1,0:T(8,128)(2,1)S(1)}, bf16[32,1024]{1,0:T(8,128)(2,1)S(1)}, u32[]{:S(2)}, u32[]{:S(2)}) collective-permute-start(bf16[32,1024]{1,0:T(8,128)(2,1)S(1)} %collective-permute-done.9.refs_0_), channel_id=1, source_target_pairs={{0,1},{1,0},{2,3},{3,2},{4,5},{5,4},{6,7},{7,6},{8,9},{9,8},{10,11... | collective-permute-start | bytes 196616 | tf_op jit(solution)/shard_map/ppermute | solution.py:231
  28.4 3.6 %collective-permute-start.15 = (bf16[16,1024]{1,0:T(8,128)(2,1)S(1)}, bf16[16,1024]{1,0:T(8,128)(2,1)S(1)}, u32[]{:S(2)}, u32[]{:S(2)}) collective-permute-start(bf16[16,1024]{1,0:T(8,128)(2,1)S(1)} %get-tuple-element.120), channel_id=1, source_target_pairs={{0,1},{1,0},{2,3},{3,2},{4,5},{5,4},{6,7},{7,6},{8,9},{9,8},{10,11... | collective-permute-start | bytes 98312 | tf_op jit(solution)/shard_map/ppermute | solution.py:231
  28.9 3.1 %collective-permute-start.17 = (bf16[32,1024]{1,0:T(8,128)(2,1)S(1)}, bf16[32,1024]{1,0:T(8,128)(2,1)S(1)}, u32[]{:S(2)}, u32[]{:S(2)}) collective-permute-start(bf16[32,1024]{1,0:T(8,128)(2,1)S(1)} %collective-permute-done.10.refs_1_), channel_id=1, source_target_pairs={{0,1},{1,0},{2,3},{3,2},{4,5},{5,4},{6,7},{7,6},{8,9},{9,8},{10,11... | collective-permute-start | bytes 196616 | tf_op jit(solution)/shard_map/ppermute | solution.py:231
  36.6 6.5 %collective-permute-start.18 = (bf16[32,512]{1,0:T(8,128)(2,1)S(1)}, bf16[32,512]{1,0:T(8,128)(2,1)S(1)}, u32[]{:S(2)}, u32[]{:S(2)}) collective-permute-start(bf16[32,512]{1,0:T(8,128)(2,1)S(1)} %get-tuple-element.153), channel_id=1, source_target_pairs={{0,12},{1,13},{2,14},{3,15},{4,8},{5,9},{6,10},{7,11},{8,4},{9,5},... | collective-permute-start | bytes 98312 | tf_op jit(solution)/shard_map/ppermute | solution.py:231
  38.2 7.7 %collective-permute-start.19 = (bf16[32,512]{1,0:T(8,128)(2,1)S(1)}, bf16[32,512]{1,0:T(8,128)(2,1)S(1)}, u32[]{:S(2)}, u32[]{:S(2)}) collective-permute-start(bf16[32,512]{1,0:T(8,128)(2,1)S(1)} %get-tuple-element.156), channel_id=1, source_target_pairs={{0,4},{1,5},{2,6},{3,7},{4,0},{5,1},{6,2},{7,3},{8,12},{9,13},{10,... | collective-permute-start | bytes 98312 | tf_op jit(solution)/shard_map/ppermute | solution.py:231
  38.8 5.9 %collective-permute-start.20 = (bf16[16,512]{1,0:T(8,128)(2,1)S(1)}, bf16[16,512]{1,0:T(8,128)(2,1)S(1)}, u32[]{:S(2)}, u32[]{:S(2)}) collective-permute-start(bf16[16,512]{1,0:T(8,128)(2,1)S(1)} %get-tuple-element.157), channel_id=1, source_target_pairs={{0,15},{1,2},{2,1},{3,4},{4,3},{5,6},{6,5},{7,8},{8,7},{9,10},{10,... | collective-permute-start | bytes 49160 | tf_op jit(solution)/shard_map/ppermute | solution.py:231
  40.3 4.4 %collective-permute-start.21 = (bf16[16,512]{1,0:T(8,128)(2,1)S(1)}, bf16[16,512]{1,0:T(8,128)(2,1)S(1)}, u32[]{:S(2)}, u32[]{:S(2)}) collective-permute-start(bf16[16,512]{1,0:T(8,128)(2,1)S(1)} %get-tuple-element.158), channel_id=1, source_target_pairs={{0,3},{1,14},{2,5},{3,0},{4,7},{5,2},{6,9},{7,4},{8,11},{9,6},{10,... | collective-permute-start | bytes 49160 | tf_op jit(solution)/shard_map/ppermute | solution.py:231
  41.4 6.4 %collective-permute-start.22 = (bf16[16,512]{1,0:T(8,128)(2,1)S(1)}, bf16[16,512]{1,0:T(8,128)(2,1)S(1)}, u32[]{:S(2)}, u32[]{:S(2)}) collective-permute-start(bf16[16,512]{1,0:T(8,128)(2,1)S(1)} %get-tuple-element.159), channel_id=1, source_target_pairs={{0,11},{1,6},{2,13},{3,8},{4,15},{5,10},{6,1},{7,12},{8,3},{9,14},... | collective-permute-start | bytes 49160 | tf_op jit(solution)/shard_map/ppermute | solution.py:231
  43.1 4.9 %collective-permute-start.23 = (bf16[16,512]{1,0:T(8,128)(2,1)S(1)}, bf16[16,512]{1,0:T(8,128)(2,1)S(1)}, u32[]{:S(2)}, u32[]{:S(2)}) collective-permute-start(bf16[16,512]{1,0:T(8,128)(2,1)S(1)} %get-tuple-element.160), channel_id=1, source_target_pairs={{0,8},{1,9},{2,10},{3,11},{4,12},{5,13},{6,14},{7,15},{8,0},{9,1},... | collective-permute-start | bytes 49160 | tf_op jit(solution)/shard_map/ppermute | solution.py:231
  44.7 3.3 %collective-permute-start.25 = (bf16[32,512]{1,0:T(8,128)(2,1)S(1)}, bf16[32,512]{1,0:T(8,128)(2,1)S(1)}, u32[]{:S(2)}, u32[]{:S(2)}) collective-permute-start(bf16[32,512]{1,0:T(8,128)(2,1)S(1)} %collective-permute-done.18.refs_0_), channel_id=1, source_target_pairs={{0,1},{1,0},{2,3},{3,2},{4,5},{5,4},{6,7},{7,6},{8,9},{9,8},{10,11... | collective-permute-start | bytes 98312 | tf_op jit(solution)/shard_map/ppermute | solution.py:231
  44.7 3.3 %collective-permute-start.24 = (bf16[16,512]{1,0:T(8,128)(2,1)S(1)}, bf16[16,512]{1,0:T(8,128)(2,1)S(1)}, u32[]{:S(2)}, u32[]{:S(2)}) collective-permute-start(bf16[16,512]{1,0:T(8,128)(2,1)S(1)} %get-tuple-element.161), channel_id=1, source_target_pairs={{0,1},{1,0},{2,3},{3,2},{4,5},{5,4},{6,7},{7,6},{8,9},{9,8},{10,11... | collective-permute-start | bytes 49160 | tf_op jit(solution)/shard_map/ppermute | solution.py:231
  (21 other events, 233.8 us)

commit v19 on v18

--- a/solution.py
+++ b/solution.py
@@ -6,7 +6,7 @@
 from jax.sharding import PartitionSpec as P
 
 TW = 4
-CHUNK = 32
+CHUNK = 128
 ROUND_FLOPS = 2 * 10**10
 F32 = jnp.float32
 BF16 = jnp.bfloat16

time: 49.2 us -> 49.3 us (level)
  transfers between devices with their start and end apart: 27 -> 27, of which waited for: 7 -> 6; matrix products, arithmetic and copies ran while one was open for 0% -> 0% of each run, Pallas kernels for 14% -> 14%
where the time goes in v19:
time: 49.3 us; the launch traced here: 49.1 us
  starting transfers between devices  29.2 us (59%)
  Pallas kernels  16.9 us (34%)
  waiting for transfers between devices  1.98 us (4%)
  between operations  1.01 us (2%)
    ppermute x27, starting transfers between devices, permute(): return lax.ppermute(part, 'tile', pairs)  29.2 us
    pallas_call x7, Pallas kernels, call(): pl.pallas_call(kernel, name=name, in_specs=specs, out_specs=[pl.BlockSpec...  15.9 us
    ppermute x27, waiting for transfers between devices, permute(): return lax.ppermute(part, 'tile', pairs)  1.98 us
    pallas_call x1, Pallas kernels, per_device(): pl.pallas_call(finish, name='add_returned', in_specs=[pl.BlockSpec(memory...  1 us
  transfers between devices with their start and end apart: 27, of which 6 were waited for; matrix products, arithmetic and copies ran while one was open for 0% of the time, Pallas kernels for 14%

profile of v19, /device:TPU:0, one launch (start us, length us, event | category | flops | bytes accessed | tf_op | source)
XLA Modules:
  0.0 49.1 jit_solution(4043199483536596182)
XLA Ops:
  0.6 1.4 %pack_rows.1 = (bf16[256,256]{1,0:T(8,128)(2,1)S(1)}, bf16[32,1024]{1,0:T(8,128)(2,1)S(1)}, bf16[32,1024]{1,0:T(8,128)(2,1)S(1)}, bf16[16,1024]{1,0:T(8,128)(2,1...) custom-call(s32[9,16]{1,0:T(8,128)} %refs_0_.2, ...), custom_call_target="tpu_custom_call" | custom-call | flops 75497472 | bytes 950884 | tf_op jit(solution)/shard_map/pack_rows/pallas_call | solution.py:172
  2.3 3.1 %collective-permute-start = (bf16[32,1024]{1,0:T(8,128)(2,1)S(1)}, bf16[32,1024]{1,0:T(8,128)(2,1)S(1)}, u32[]{:S(2)}, u32[]{:S(2)}) collective-permute-start(bf16[32,1024]{1,0:T(8,128)(2,1)S(1)} %get-tuple-element.92), channel_id=1, source_target_pairs={{0,4},{1,5},{2,6},{3,7},{4,0},{5,1},{6,2},{7,3},{8,12},{9,13},{10,... | collective-permute-start | bytes 196616 | tf_op jit(solution)/shard_map/ppermute | solution.py:231
  5.4 2.5 %collective-permute-start.1 = (bf16[32,1024]{1,0:T(8,128)(2,1)S(1)}, bf16[32,1024]{1,0:T(8,128)(2,1)S(1)}, u32[]{:S(2)}, u32[]{:S(2)}) collective-permute-start(bf16[32,1024]{1,0:T(8,128)(2,1)S(1)} %get-tuple-element.95), channel_id=1, source_target_pairs={{0,12},{1,13},{2,14},{3,15},{4,8},{5,9},{6,10},{7,11},{8,4},{9,5},... | collective-permute-start | bytes 196616 | tf_op jit(solution)/shard_map/ppermute | solution.py:231
  8.3 0.9 %collective-permute-start.3 = (bf16[16,1024]{1,0:T(8,128)(2,1)S(1)}, bf16[16,1024]{1,0:T(8,128)(2,1)S(1)}, u32[]{:S(2)}, u32[]{:S(2)}) collective-permute-start(bf16[16,1024]{1,0:T(8,128)(2,1)S(1)} %get-tuple-element.97), channel_id=1, source_target_pairs={{0,11},{1,6},{2,13},{3,8},{4,15},{5,10},{6,1},{7,12},{8,3},{9,14},... | collective-permute-start | bytes 98312 | tf_op jit(solution)/shard_map/ppermute | solution.py:231
  9.2 2.8 %collective-permute-start.4 = (bf16[16,1024]{1,0:T(8,128)(2,1)S(1)}, bf16[16,1024]{1,0:T(8,128)(2,1)S(1)}, u32[]{:S(2)}, u32[]{:S(2)}) collective-permute-start(bf16[16,1024]{1,0:T(8,128)(2,1)S(1)} %get-tuple-element.98), channel_id=1, source_target_pairs={{0,15},{1,2},{2,1},{3,4},{4,3},{5,6},{6,5},{7,8},{8,7},{9,10},{10,... | collective-permute-start | bytes 98312 | tf_op jit(solution)/shard_map/ppermute | solution.py:231
  12.3 1.2 %collective-permute-start.8 = (bf16[32,1024]{1,0:T(8,128)(2,1)S(1)}, bf16[32,1024]{1,0:T(8,128)(2,1)S(1)}, u32[]{:S(2)}, u32[]{:S(2)}) collective-permute-start(bf16[32,1024]{1,0:T(8,128)(2,1)S(1)} %collective-permute-done.refs_0_), channel_id=1, source_target_pairs={{0,1},{1,0},{2,3},{3,2},{4,5},{5,4},{6,7},{7,6},{8,9},{9,8},{10,11... | collective-permute-start | bytes 196616 | tf_op jit(solution)/shard_map/ppermute | solution.py:231
  14.1 0.7 %collective-permute-start.6 = (bf16[16,1024]{1,0:T(8,128)(2,1)S(1)}, bf16[16,1024]{1,0:T(8,128)(2,1)S(1)}, u32[]{:S(2)}, u32[]{:S(2)}) collective-permute-start(bf16[16,1024]{1,0:T(8,128)(2,1)S(1)} %get-tuple-element.100), channel_id=1, source_target_pairs={{0,1},{1,0},{2,3},{3,2},{4,5},{5,4},{6,7},{7,6},{8,9},{9,8},{10,11... | collective-permute-start | bytes 98312 | tf_op jit(solution)/shard_map/ppermute | solution.py:231
  15.0 2.0 %local_products.1 = (f32[384,512]{1,0:T(8,128)S(1)}, f32[768,512]{1,0:T(8,128)S(1)}, f32[64,512]{1,0:T(8,128)S(1)}, bf16[384,512]{1,0:T(8,128)(2,1)S(1)}, bf16[5...) custom-call(bf16[256,256]{1,0:T(8,128)(2,1)S(1)} %get-tuple-element., ...), custom_call_target="tpu_custom_call" | custom-call | flops 1275068416 | bytes 14058496 | tf_op jit(solution)/shard_map/local_products/pallas_call | solution.py:172
  17.2 2.8 %edges_forward.1 = (bf16[32,1024]{1,0:T(8,128)(2,1)S(1)}, bf16[32,1024]{1,0:T(8,128)(2,1)S(1)}, bf16[16,1024]{1,0:T(8,128)(2,1)S(1)}, bf16[16,1024]{1,0:T(8,128)...) custom-call(bf16[32,1024]{1,0:T(8,128)(2,1)S(1)} %collective-permute, ...), custom_call_target="tpu_custom_call" | custom-call | flops 1207959552 | bytes 17298176 | tf_op jit(solution)/shard_map/edges_forward/pallas_call | solution.py:172
  20.0 2.0 %collective-permute-start.9 = (bf16[32,1024]{1,0:T(8,128)(2,1)S(1)}, bf16[32,1024]{1,0:T(8,128)(2,1)S(1)}, u32[]{:S(2)}, u32[]{:S(2)}) collective-permute-start(bf16[32,1024]{1,0:T(8,128)(2,1)S(1)} %get-tuple-element.112), channel_id=1, source_target_pairs={{0,12},{1,13},{2,14},{3,15},{4,8},{5,9},{6,10},{7,11},{8,4},{9,5},... | collective-permute-start | bytes 196616 | tf_op jit(solution)/shard_map/ppermute | solution.py:231
  22.0 2.2 %collective-permute-start.11 = (bf16[16,1024]{1,0:T(8,128)(2,1)S(1)}, bf16[16,1024]{1,0:T(8,128)(2,1)S(1)}, u32[]{:S(2)}, u32[]{:S(2)}) collective-permute-start(bf16[16,1024]{1,0:T(8,128)(2,1)S(1)} %get-tuple-element.116), channel_id=1, source_target_pairs={{0,15},{1,2},{2,1},{3,4},{4,3},{5,6},{6,5},{7,8},{8,7},{9,10},{10,... | collective-permute-start | bytes 98312 | tf_op jit(solution)/shard_map/ppermute | solution.py:231
  24.1 1.0 %collective-permute-start.12 = (bf16[16,1024]{1,0:T(8,128)(2,1)S(1)}, bf16[16,1024]{1,0:T(8,128)(2,1)S(1)}, u32[]{:S(2)}, u32[]{:S(2)}) collective-permute-start(bf16[16,1024]{1,0:T(8,128)(2,1)S(1)} %get-tuple-element.117), channel_id=1, source_target_pairs={{0,3},{1,14},{2,5},{3,0},{4,7},{5,2},{6,9},{7,4},{8,11},{9,6},{10,... | collective-permute-start | bytes 98312 | tf_op jit(solution)/shard_map/ppermute | solution.py:231
  25.2 1.0 %collective-permute-start.13 = (bf16[16,1024]{1,0:T(8,128)(2,1)S(1)}, bf16[16,1024]{1,0:T(8,128)(2,1)S(1)}, u32[]{:S(2)}, u32[]{:S(2)}) collective-permute-start(bf16[16,1024]{1,0:T(8,128)(2,1)S(1)} %get-tuple-element.118), channel_id=1, source_target_pairs={{0,11},{1,6},{2,13},{3,8},{4,15},{5,10},{6,1},{7,12},{8,3},{9,14},... | collective-permute-start | bytes 98312 | tf_op jit(solution)/shard_map/ppermute | solution.py:231
  26.8 1.5 %collective-permute-start.14 = (bf16[16,1024]{1,0:T(8,128)(2,1)S(1)}, bf16[16,1024]{1,0:T(8,128)(2,1)S(1)}, u32[]{:S(2)}, u32[]{:S(2)}) collective-permute-start(bf16[16,1024]{1,0:T(8,128)(2,1)S(1)} %get-tuple-element.119), channel_id=1, source_target_pairs={{0,8},{1,9},{2,10},{3,11},{4,12},{5,13},{6,14},{7,15},{8,0},{9,1},... | collective-permute-start | bytes 98312 | tf_op jit(solution)/shard_map/ppermute | solution.py:231
  29.0 3.0 %slopes_and_nodes.1 = (f32[256,512]{1,0:T(8,128)S(1)}, f32[400,512]{1,0:T(8,128)S(1)}, bf16[400,512]{1,0:T(8,128)(2,1)S(1)}, f32[400,512]{1,0:T(8,128)S(1)}, bf1...) custom-call(bf16[32,1024]{1,0:T(8,128)(2,1)S(1)} %collective-permute, ...), custom_call_target="tpu_custom_call" | custom-call | flops 1677721600 | bytes 17874944 | tf_op jit(solution)/shard_map/slopes_and_nodes/pallas_call | solution.py:172
  32.1 4.6 %edges_backward.1 = (bf16[32,512]{1,0:T(8,128)(2,1)S(1)}, bf16[32,512]{1,0:T(8,128)(2,1)S(1)}, bf16[16,512]{1,0:T(8,128)(2,1)S(1)}, bf16[16,512]{1,0:T(8,128)(2,...) custom-call(bf16[32,1024]{1,0:T(8,128)(2,1)S(1)} %collective-permute, ...), custom_call_target="tpu_custom_call" | custom-call | flops 2449473536 | bytes 19878656 | tf_op jit(solution)/shard_map/edges_backward/pallas_call | solution.py:172
  36.7 1.7 %collective-permute-start.18 = (bf16[32,512]{1,0:T(8,128)(2,1)S(1)}, bf16[32,512]{1,0:T(8,128)(2,1)S(1)}, u32[]{:S(2)}, u32[]{:S(2)}) collective-permute-start(bf16[32,512]{1,0:T(8,128)(2,1)S(1)} %get-tuple-element.153), channel_id=1, source_target_pairs={{0,12},{1,13},{2,14},{3,15},{4,8},{5,9},{6,10},{7,11},{8,4},{9,5},... | collective-permute-start | bytes 98312 | tf_op jit(solution)/shard_map/ppermute | solution.py:231
  38.9 1.5 %collective-permute-start.20 = (bf16[16,512]{1,0:T(8,128)(2,1)S(1)}, bf16[16,512]{1,0:T(8,128)(2,1)S(1)}, u32[]{:S(2)}, u32[]{:S(2)}) collective-permute-start(bf16[16,512]{1,0:T(8,128)(2,1)S(1)} %get-tuple-element.157), channel_id=1, source_target_pairs={{0,15},{1,2},{2,1},{3,4},{4,3},{5,6},{6,5},{7,8},{8,7},{9,10},{10,... | collective-permute-start | bytes 49160 | tf_op jit(solution)/shard_map/ppermute | solution.py:231
  40.5 1.1 %collective-permute-start.21 = (bf16[16,512]{1,0:T(8,128)(2,1)S(1)}, bf16[16,512]{1,0:T(8,128)(2,1)S(1)}, u32[]{:S(2)}, u32[]{:S(2)}) collective-permute-start(bf16[16,512]{1,0:T(8,128)(2,1)S(1)} %get-tuple-element.158), channel_id=1, source_target_pairs={{0,3},{1,14},{2,5},{3,0},{4,7},{5,2},{6,9},{7,4},{8,11},{9,6},{10,... | collective-permute-start | bytes 49160 | tf_op jit(solution)/shard_map/ppermute | solution.py:231
  41.6 1.6 %collective-permute-start.22 = (bf16[16,512]{1,0:T(8,128)(2,1)S(1)}, bf16[16,512]{1,0:T(8,128)(2,1)S(1)}, u32[]{:S(2)}, u32[]{:S(2)}) collective-permute-start(bf16[16,512]{1,0:T(8,128)(2,1)S(1)} %get-tuple-element.159), channel_id=1, source_target_pairs={{0,11},{1,6},{2,13},{3,8},{4,15},{5,10},{6,1},{7,12},{8,3},{9,14},... | collective-permute-start | bytes 49160 | tf_op jit(solution)/shard_map/ppermute | solution.py:231
  43.2 1.4 %collective-permute-start.23 = (bf16[16,512]{1,0:T(8,128)(2,1)S(1)}, bf16[16,512]{1,0:T(8,128)(2,1)S(1)}, u32[]{:S(2)}, u32[]{:S(2)}) collective-permute-start(bf16[16,512]{1,0:T(8,128)(2,1)S(1)} %get-tuple-element.160), channel_id=1, source_target_pairs={{0,8},{1,9},{2,10},{3,11},{4,12},{5,13},{6,14},{7,15},{8,0},{9,1},... | collective-permute-start | bytes 49160 | tf_op jit(solution)/shard_map/ppermute | solution.py:231
  44.9 1.1 %collective-permute-start.24 = (bf16[16,512]{1,0:T(8,128)(2,1)S(1)}, bf16[16,512]{1,0:T(8,128)(2,1)S(1)}, u32[]{:S(2)}, u32[]{:S(2)}) collective-permute-start(bf16[16,512]{1,0:T(8,128)(2,1)S(1)} %get-tuple-element.161), channel_id=1, source_target_pairs={{0,1},{1,0},{2,3},{3,2},{4,5},{5,4},{6,7},{7,6},{8,9},{9,8},{10,11... | collective-permute-start | bytes 49160 | tf_op jit(solution)/shard_map/ppermute | solution.py:231
  46.0 1.9 %local_gradients.1 = (f32[256,512]{1,0:T(8,128)S(1)}, f32[64,512]{1,0:T(8,128)}, bf16[256,512]{1,0:T(8,128)(2,1)}) custom-call(bf16[256,512]{1,0:T(8,128)(2,1)S(1)} %copy-done.4, f32[400,512]{1,0:T(8,128)S(1)} %get-tuple-element.145.refs_1_, bf16[256,512]{1,0:T(8,128)(2,1)S(1)} %copy-done.5, bf16[400,512]{1,0:T(8,128)(2,1)S(1)} %get-tuple-element.146.refs_3_, ...), custom_call_target="tpu_custom_call" | custom-call | flops 402653184 | bytes 12042240 | tf_op jit(solution)/shard_map/local_gradients/pallas_call | solution.py:172
  48.2 1.0 %add_returned.1 = f32[256,512]{1,0:T(8,128)} custom-call(bf16[32,512]{1,0:T(8,128)(2,1)S(1)} %collective-permute-done.18.refs_0_, bf16[32,512]{1,0:T(8,128)(2,1)S(1)} %collective-permute-done.19.refs_1_, bf16[16,512]{1,0:T(8,128)(2,1)S(1)} %collective-permute-done.20.refs_2_, bf16[16,512]{1,0:T(8,128)(2,1)S(1)} %collective-permute-done.21.refs_3_, ...), custom_call_target="tpu_custom_call" | custom-call | tf_op jit(solution)/shard_map/add_returned/pallas_call | solution.py:934
  (74 shorter events, 4.2 us)
Async XLA Ops:
  2.3 9.6 %collective-permute-start = (bf16[32,1024]{1,0:T(8,128)(2,1)S(1)}, bf16[32,1024]{1,0:T(8,128)(2,1)S(1)}, u32[]{:S(2)}, u32[]{:S(2)}) collective-permute-start(bf16[32,1024]{1,0:T(8,128)(2,1)S(1)} %get-tuple-element.92), channel_id=1, source_target_pairs={{0,4},{1,5},{2,6},{3,7},{4,0},{5,1},{6,2},{7,3},{8,12},{9,13},{10,... | collective-permute-start | bytes 196616 | tf_op jit(solution)/shard_map/ppermute | solution.py:231
  5.4 9.4 %collective-permute-start.1 = (bf16[32,1024]{1,0:T(8,128)(2,1)S(1)}, bf16[32,1024]{1,0:T(8,128)(2,1)S(1)}, u32[]{:S(2)}, u32[]{:S(2)}) collective-permute-start(bf16[32,1024]{1,0:T(8,128)(2,1)S(1)} %get-tuple-element.95), channel_id=1, source_target_pairs={{0,12},{1,13},{2,14},{3,15},{4,8},{5,9},{6,10},{7,11},{8,4},{9,5},... | collective-permute-start | bytes 196616 | tf_op jit(solution)/shard_map/ppermute | solution.py:231
  7.9 4.4 %collective-permute-start.2 = (bf16[16,1024]{1,0:T(8,128)(2,1)S(1)}, bf16[16,1024]{1,0:T(8,128)(2,1)S(1)}, u32[]{:S(2)}, u32[]{:S(2)}) collective-permute-start(bf16[16,1024]{1,0:T(8,128)(2,1)S(1)} %get-tuple-element.96), channel_id=1, source_target_pairs={{0,3},{1,14},{2,5},{3,0},{4,7},{5,2},{6,9},{7,4},{8,11},{9,6},{10,... | collective-permute-start | bytes 98312 | tf_op jit(solution)/shard_map/ppermute | solution.py:231
  8.3 5.8 %collective-permute-start.3 = (bf16[16,1024]{1,0:T(8,128)(2,1)S(1)}, bf16[16,1024]{1,0:T(8,128)(2,1)S(1)}, u32[]{:S(2)}, u32[]{:S(2)}) collective-permute-start(bf16[16,1024]{1,0:T(8,128)(2,1)S(1)} %get-tuple-element.97), channel_id=1, source_target_pairs={{0,11},{1,6},{2,13},{3,8},{4,15},{5,10},{6,1},{7,12},{8,3},{9,14},... | collective-permute-start | bytes 98312 | tf_op jit(solution)/shard_map/ppermute | solution.py:231
  9.2 7.8 %collective-permute-start.4 = (bf16[16,1024]{1,0:T(8,128)(2,1)S(1)}, bf16[16,1024]{1,0:T(8,128)(2,1)S(1)}, u32[]{:S(2)}, u32[]{:S(2)}) collective-permute-start(bf16[16,1024]{1,0:T(8,128)(2,1)S(1)} %get-tuple-element.98), channel_id=1, source_target_pairs={{0,15},{1,2},{2,1},{3,4},{4,3},{5,6},{6,5},{7,8},{8,7},{9,10},{10,... | collective-permute-start | bytes 98312 | tf_op jit(solution)/shard_map/ppermute | solution.py:231
  12.0 5.2 %collective-permute-start.5 = (bf16[16,1024]{1,0:T(8,128)(2,1)S(1)}, bf16[16,1024]{1,0:T(8,128)(2,1)S(1)}, u32[]{:S(2)}, u32[]{:S(2)}) collective-permute-start(bf16[16,1024]{1,0:T(8,128)(2,1)S(1)} %get-tuple-element.99), channel_id=1, source_target_pairs={{0,8},{1,9},{2,10},{3,11},{4,12},{5,13},{6,14},{7,15},{8,0},{9,1},... | collective-permute-start | bytes 98312 | tf_op jit(solution)/shard_map/ppermute | solution.py:231
  12.3 4.8 %collective-permute-start.8 = (bf16[32,1024]{1,0:T(8,128)(2,1)S(1)}, bf16[32,1024]{1,0:T(8,128)(2,1)S(1)}, u32[]{:S(2)}, u32[]{:S(2)}) collective-permute-start(bf16[32,1024]{1,0:T(8,128)(2,1)S(1)} %collective-permute-done.refs_0_), channel_id=1, source_target_pairs={{0,1},{1,0},{2,3},{3,2},{4,5},{5,4},{6,7},{7,6},{8,9},{9,8},{10,11... | collective-permute-start | bytes 196616 | tf_op jit(solution)/shard_map/ppermute | solution.py:231
  20.0 6.8 %collective-permute-start.9 = (bf16[32,1024]{1,0:T(8,128)(2,1)S(1)}, bf16[32,1024]{1,0:T(8,128)(2,1)S(1)}, u32[]{:S(2)}, u32[]{:S(2)}) collective-permute-start(bf16[32,1024]{1,0:T(8,128)(2,1)S(1)} %get-tuple-element.112), channel_id=1, source_target_pairs={{0,12},{1,13},{2,14},{3,15},{4,8},{5,9},{6,10},{7,11},{8,4},{9,5},... | collective-permute-start | bytes 196616 | tf_op jit(solution)/shard_map/ppermute | solution.py:231
  22.0 7.0 %collective-permute-start.10 = (bf16[32,1024]{1,0:T(8,128)(2,1)S(1)}, bf16[32,1024]{1,0:T(8,128)(2,1)S(1)}, u32[]{:S(2)}, u32[]{:S(2)}) collective-permute-start(bf16[32,1024]{1,0:T(8,128)(2,1)S(1)} %get-tuple-element.115), channel_id=1, source_target_pairs={{0,4},{1,5},{2,6},{3,7},{4,0},{5,1},{6,2},{7,3},{8,12},{9,13},{10,... | collective-permute-start | bytes 196616 | tf_op jit(solution)/shard_map/ppermute | solution.py:231
  22.0 6.4 %collective-permute-start.11 = (bf16[16,1024]{1,0:T(8,128)(2,1)S(1)}, bf16[16,1024]{1,0:T(8,128)(2,1)S(1)}, u32[]{:S(2)}, u32[]{:S(2)}) collective-permute-start(bf16[16,1024]{1,0:T(8,128)(2,1)S(1)} %get-tuple-element.116), channel_id=1, source_target_pairs={{0,15},{1,2},{2,1},{3,4},{4,3},{5,6},{6,5},{7,8},{8,7},{9,10},{10,... | collective-permute-start | bytes 98312 | tf_op jit(solution)/shard_map/ppermute | solution.py:231
  24.1 4.3 %collective-permute-start.12 = (bf16[16,1024]{1,0:T(8,128)(2,1)S(1)}, bf16[16,1024]{1,0:T(8,128)(2,1)S(1)}, u32[]{:S(2)}, u32[]{:S(2)}) collective-permute-start(bf16[16,1024]{1,0:T(8,128)(2,1)S(1)} %get-tuple-element.117), channel_id=1, source_target_pairs={{0,3},{1,14},{2,5},{3,0},{4,7},{5,2},{6,9},{7,4},{8,11},{9,6},{10,... | collective-permute-start | bytes 98312 | tf_op jit(solution)/shard_map/ppermute | solution.py:231
  25.2 6.8 %collective-permute-start.13 = (bf16[16,1024]{1,0:T(8,128)(2,1)S(1)}, bf16[16,1024]{1,0:T(8,128)(2,1)S(1)}, u32[]{:S(2)}, u32[]{:S(2)}) collective-permute-start(bf16[16,1024]{1,0:T(8,128)(2,1)S(1)} %get-tuple-element.118), channel_id=1, source_target_pairs={{0,11},{1,6},{2,13},{3,8},{4,15},{5,10},{6,1},{7,12},{8,3},{9,14},... | collective-permute-start | bytes 98312 | tf_op jit(solution)/shard_map/ppermute | solution.py:231
  26.8 5.3 %collective-permute-start.14 = (bf16[16,1024]{1,0:T(8,128)(2,1)S(1)}, bf16[16,1024]{1,0:T(8,128)(2,1)S(1)}, u32[]{:S(2)}, u32[]{:S(2)}) collective-permute-start(bf16[16,1024]{1,0:T(8,128)(2,1)S(1)} %get-tuple-element.119), channel_id=1, source_target_pairs={{0,8},{1,9},{2,10},{3,11},{4,12},{5,13},{6,14},{7,15},{8,0},{9,1},... | collective-permute-start | bytes 98312 | tf_op jit(solution)/shard_map/ppermute | solution.py:231
  28.4 3.7 %collective-permute-start.16 = (bf16[32,1024]{1,0:T(8,128)(2,1)S(1)}, bf16[32,1024]{1,0:T(8,128)(2,1)S(1)}, u32[]{:S(2)}, u32[]{:S(2)}) collective-permute-start(bf16[32,1024]{1,0:T(8,128)(2,1)S(1)} %collective-permute-done.9.refs_0_), channel_id=1, source_target_pairs={{0,1},{1,0},{2,3},{3,2},{4,5},{5,4},{6,7},{7,6},{8,9},{9,8},{10,11... | collective-permute-start | bytes 196616 | tf_op jit(solution)/shard_map/ppermute | solution.py:231
  28.4 3.6 %collective-permute-start.15 = (bf16[16,1024]{1,0:T(8,128)(2,1)S(1)}, bf16[16,1024]{1,0:T(8,128)(2,1)S(1)}, u32[]{:S(2)}, u32[]{:S(2)}) collective-permute-start(bf16[16,1024]{1,0:T(8,128)(2,1)S(1)} %get-tuple-element.120), channel_id=1, source_target_pairs={{0,1},{1,0},{2,3},{3,2},{4,5},{5,4},{6,7},{7,6},{8,9},{9,8},{10,11... | collective-permute-start | bytes 98312 | tf_op jit(solution)/shard_map/ppermute | solution.py:231
  28.9 3.1 %collective-permute-start.17 = (bf16[32,1024]{1,0:T(8,128)(2,1)S(1)}, bf16[32,1024]{1,0:T(8,128)(2,1)S(1)}, u32[]{:S(2)}, u32[]{:S(2)}) collective-permute-start(bf16[32,1024]{1,0:T(8,128)(2,1)S(1)} %collective-permute-done.10.refs_1_), channel_id=1, source_target_pairs={{0,1},{1,0},{2,3},{3,2},{4,5},{5,4},{6,7},{7,6},{8,9},{9,8},{10,11... | collective-permute-start | bytes 196616 | tf_op jit(solution)/shard_map/ppermute | solution.py:231
  36.7 6.5 %collective-permute-start.18 = (bf16[32,512]{1,0:T(8,128)(2,1)S(1)}, bf16[32,512]{1,0:T(8,128)(2,1)S(1)}, u32[]{:S(2)}, u32[]{:S(2)}) collective-permute-start(bf16[32,512]{1,0:T(8,128)(2,1)S(1)} %get-tuple-element.153), channel_id=1, source_target_pairs={{0,12},{1,13},{2,14},{3,15},{4,8},{5,9},{6,10},{7,11},{8,4},{9,5},... | collective-permute-start | bytes 98312 | tf_op jit(solution)/shard_map/ppermute | solution.py:231
  38.4 7.7 %collective-permute-start.19 = (bf16[32,512]{1,0:T(8,128)(2,1)S(1)}, bf16[32,512]{1,0:T(8,128)(2,1)S(1)}, u32[]{:S(2)}, u32[]{:S(2)}) collective-permute-start(bf16[32,512]{1,0:T(8,128)(2,1)S(1)} %get-tuple-element.156), channel_id=1, source_target_pairs={{0,4},{1,5},{2,6},{3,7},{4,0},{5,1},{6,2},{7,3},{8,12},{9,13},{10,... | collective-permute-start | bytes 98312 | tf_op jit(solution)/shard_map/ppermute | solution.py:231
  38.9 5.9 %collective-permute-start.20 = (bf16[16,512]{1,0:T(8,128)(2,1)S(1)}, bf16[16,512]{1,0:T(8,128)(2,1)S(1)}, u32[]{:S(2)}, u32[]{:S(2)}) collective-permute-start(bf16[16,512]{1,0:T(8,128)(2,1)S(1)} %get-tuple-element.157), channel_id=1, source_target_pairs={{0,15},{1,2},{2,1},{3,4},{4,3},{5,6},{6,5},{7,8},{8,7},{9,10},{10,... | collective-permute-start | bytes 49160 | tf_op jit(solution)/shard_map/ppermute | solution.py:231
  40.5 4.4 %collective-permute-start.21 = (bf16[16,512]{1,0:T(8,128)(2,1)S(1)}, bf16[16,512]{1,0:T(8,128)(2,1)S(1)}, u32[]{:S(2)}, u32[]{:S(2)}) collective-permute-start(bf16[16,512]{1,0:T(8,128)(2,1)S(1)} %get-tuple-element.158), channel_id=1, source_target_pairs={{0,3},{1,14},{2,5},{3,0},{4,7},{5,2},{6,9},{7,4},{8,11},{9,6},{10,... | collective-permute-start | bytes 49160 | tf_op jit(solution)/shard_map/ppermute | solution.py:231
  41.6 6.4 %collective-permute-start.22 = (bf16[16,512]{1,0:T(8,128)(2,1)S(1)}, bf16[16,512]{1,0:T(8,128)(2,1)S(1)}, u32[]{:S(2)}, u32[]{:S(2)}) collective-permute-start(bf16[16,512]{1,0:T(8,128)(2,1)S(1)} %get-tuple-element.159), channel_id=1, source_target_pairs={{0,11},{1,6},{2,13},{3,8},{4,15},{5,10},{6,1},{7,12},{8,3},{9,14},... | collective-permute-start | bytes 49160 | tf_op jit(solution)/shard_map/ppermute | solution.py:231
  43.2 5.0 %collective-permute-start.23 = (bf16[16,512]{1,0:T(8,128)(2,1)S(1)}, bf16[16,512]{1,0:T(8,128)(2,1)S(1)}, u32[]{:S(2)}, u32[]{:S(2)}) collective-permute-start(bf16[16,512]{1,0:T(8,128)(2,1)S(1)} %get-tuple-element.160), channel_id=1, source_target_pairs={{0,8},{1,9},{2,10},{3,11},{4,12},{5,13},{6,14},{7,15},{8,0},{9,1},... | collective-permute-start | bytes 49160 | tf_op jit(solution)/shard_map/ppermute | solution.py:231
  44.8 3.3 %collective-permute-start.25 = (bf16[32,512]{1,0:T(8,128)(2,1)S(1)}, bf16[32,512]{1,0:T(8,128)(2,1)S(1)}, u32[]{:S(2)}, u32[]{:S(2)}) collective-permute-start(bf16[32,512]{1,0:T(8,128)(2,1)S(1)} %collective-permute-done.18.refs_0_), channel_id=1, source_target_pairs={{0,1},{1,0},{2,3},{3,2},{4,5},{5,4},{6,7},{7,6},{8,9},{9,8},{10,11... | collective-permute-start | bytes 98312 | tf_op jit(solution)/shard_map/ppermute | solution.py:231
  44.9 3.3 %collective-permute-start.24 = (bf16[16,512]{1,0:T(8,128)(2,1)S(1)}, bf16[16,512]{1,0:T(8,128)(2,1)S(1)}, u32[]{:S(2)}, u32[]{:S(2)}) collective-permute-start(bf16[16,512]{1,0:T(8,128)(2,1)S(1)} %get-tuple-element.161), channel_id=1, source_target_pairs={{0,1},{1,0},{2,3},{3,2},{4,5},{5,4},{6,7},{7,6},{8,9},{9,8},{10,11... | collective-permute-start | bytes 49160 | tf_op jit(solution)/shard_map/ppermute | solution.py:231
  (21 other events, 233.8 us)

commit v20 on v18

--- a/solution.py
+++ b/solution.py
@@ -394,14 +394,15 @@
         enc_centred_ref,
         dec_centred_ref,
         mesh_centred_ref,
-        shared_pool_ref,
+        sent_pool_ref,
         table_ref,
     ):
         onehot_pair(enc_grid_ref, enc_mesh_ref, spots, mesh_count, enc_pick_ref, enc_pool_ref)
         onehot_pair(dec_grid_ref, dec_mesh_ref, spots, mesh_count, dec_pick_ref, dec_pool_ref)
         enc_centred_ref[...] = centred(enc_second_ref[...], 1).astype(BF16)
         mesh_centred_ref[...] = centred(mesh_second_ref[...], 1).astype(BF16)
-        shared_pool_ref[...] = mm(
+        sent_pool_ref[:slots, :] = dec_pool_ref[grid_count:spots, :]
+        sent_pool_ref[slots:, :] = mm(
             select_ref[:slots, :], dec_pool_ref[:grid_count, :]
         ).astype(BF16)
         dec_centred_ref[...] = centred(dec_second_ref[...], 1).astype(BF16)
@@ -427,7 +428,7 @@
         enc_centred,
         dec_centred,
         mesh_centred,
-        shared_pool,
+        sent_pool,
     ) = call(
         local,
         "local_products",
@@ -461,7 +462,7 @@
             ((feat, feat), BF16),
             ((feat, feat), BF16),
             ((feat, feat), BF16),
-            ((slots, dec_count), BF16),
+            ((2 * slots, dec_count), BF16),
         ],
         scratch=[((total, feat), BF16)],
         flops=2 * feat * (feat * (2 * grid_count + enc_count + dec_count) + total * dec_count),
@@ -470,14 +471,13 @@
     def forward(*refs):
         arrived_refs, refs = refs[:arrived_count], refs[arrived_count:]
         (
-            shared_pool_ref,
+            sent_pool_ref,
             enc_part_ref,
             dec_part_ref,
             mesh_part_ref,
             enc_pick_ref,
             enc_pool_ref,
             dec_pick_ref,
-            dec_pool_ref,
             enc_wg_ref,
             dec_wg_ref,
             enc_w2_ref,
@@ -486,8 +486,8 @@
             mesh_ref,
             dec_wm_ref,
             dec_w2_ref,
-        ) = refs[:16]
-        refs = refs[16:]
+        ) = refs[:15]
+        refs = refs[15:]
         out_refs, refs = refs[:sent_count], refs[sent_count:]
         (
             slot_ref,
@@ -523,10 +523,10 @@
         dec_pre_ref[...] = dec_part_ref[...] + mm(dec_pick_ref[:, grid_count:], table_ref[...])
         write_silu(dec_pre_ref, dec_act_ref)
         write_norm(mm(dec_act_ref[...], dec_w2_ref[...]), dec_normed_ref, dec_scale_ref)
-        slot_sums = mm(dec_pool_ref[grid_count:spots, :], dec_normed_ref[...])
-        slot_ref[...] = slot_sums
-        shared = mm(shared_pool_ref[...], dec_normed_ref[...]).astype(BF16)
-        slot_msg = slot_sums.astype(BF16)
+        sums = mm(sent_pool_ref[...], dec_normed_ref[...])
+        slot_ref[...] = sums[:slots, :]
+        shared = sums[slots:, :].astype(BF16)
+        slot_msg = sums[:slots, :].astype(BF16)
         send(
             out_refs, lambda j: slot_msg[reverse[j] * width : (reverse[j] + 1) * width, :], low
         )
@@ -548,14 +548,13 @@
         "edges_forward",
         [
             *arrived,
-            shared_pool,
+            sent_pool,
             enc_part,
             dec_part,
             mesh_part,
             enc_pick,
             enc_pool,
             dec_pick,
-            dec_pool,
             enc_first,
             dec_first,
             enc_centred,
@@ -771,16 +770,17 @@
             dec_slope_ref,
             dec_gpre_ref,
         )
-        mesh_sum = mm(dec_pool_ref[mesh_rows, :], dec_gpre_ref[...]).astype(BF16)
-        both = mm_t(mesh_sum, mesh_in_ref[...])
+        sums = mm(
+            dec_pool_ref[grid_count : spots + mesh_count, :], dec_gpre_ref[...]
+        ).astype(BF16)
+        both = mm_t(sums[slots:, :], mesh_in_ref[...])
         mesh_gin = mesh_cot_ref[...].astype(F32) + both[:, low]
         mesh_gin_ref[...] = mesh_gin
         mean = jnp.mean(mesh_gin * mesh_normed_ref[...], axis=-1, keepdims=True)
         raw = mesh_cot_turned_ref[...] + both[:, high] - mean * mesh_turned_ref[...]
         mesh_gpre_ref[...] = (mesh_scale_ref[...] * raw * mesh_slope_ref[...]).astype(BF16)
         mesh_gagg = mm_t(mesh_gpre_ref[...], mesh_back_ref[...]).astype(BF16)
-        pooled = mm(dec_pool_ref[grid_count:spots, :], dec_gpre_ref[...]).astype(BF16)
-        slot_back = mm_t(pooled, dec_first_ref[low, :])
+        slot_back = mm_t(sums[:slots, :], dec_first_ref[low, :])
         edge_back(
             mm(enc_pick_ref[:, mesh_rows], mesh_gagg),
             enc_normed_ref,

time: 49.2 us -> 49.1 us (level)
  no operation moved by 1% of the time
where the time goes in v20:
time: 49.1 us; the launch traced here: 48.9 us
  starting transfers between devices  29.2 us (59%)
  Pallas kernels  16.7 us (34%)
  waiting for transfers between devices  1.93 us (4%)
  between operations  0.97 us (2%)
    ppermute x27, starting transfers between devices, permute(): return lax.ppermute(part, 'tile', pairs)  29.2 us
    pallas_call x7, Pallas kernels, call(): pl.pallas_call(kernel, name=name, in_specs=specs, out_specs=[pl.BlockSpec...  15.7 us
    ppermute x27, waiting for transfers between devices, permute(): return lax.ppermute(part, 'tile', pairs)  1.93 us
    pallas_call x1, Pallas kernels, per_device(): pl.pallas_call(finish, name='add_returned', in_specs=[pl.BlockSpec(memory...  1 us
  transfers between devices with their start and end apart: 27, of which 7 were waited for; matrix products, arithmetic and copies ran while one was open for 0% of the time, Pallas kernels for 14%

profile of v20, /device:TPU:0, one launch (start us, length us, event | category | flops | bytes accessed | tf_op | source)
XLA Modules:
  0.0 48.9 jit_solution(14080521002469147484)
XLA Ops:
  0.6 1.4 %pack_rows.1 = (bf16[256,256]{1,0:T(8,128)(2,1)S(1)}, bf16[32,1024]{1,0:T(8,128)(2,1)S(1)}, bf16[32,1024]{1,0:T(8,128)(2,1)S(1)}, bf16[16,1024]{1,0:T(8,128)(2,1...) custom-call(s32[9,16]{1,0:T(8,128)} %refs_0_.2, ...), custom_call_target="tpu_custom_call" | custom-call | flops 75497472 | bytes 950884 | tf_op jit(solution)/shard_map/pack_rows/pallas_call | solution.py:172
  2.3 3.1 %collective-permute-start = (bf16[32,1024]{1,0:T(8,128)(2,1)S(1)}, bf16[32,1024]{1,0:T(8,128)(2,1)S(1)}, u32[]{:S(2)}, u32[]{:S(2)}) collective-permute-start(bf16[32,1024]{1,0:T(8,128)(2,1)S(1)} %get-tuple-element.92), channel_id=1, source_target_pairs={{0,4},{1,5},{2,6},{3,7},{4,0},{5,1},{6,2},{7,3},{8,12},{9,13},{10,... | collective-permute-start | bytes 196616 | tf_op jit(solution)/shard_map/ppermute | solution.py:231
  5.4 2.5 %collective-permute-start.1 = (bf16[32,1024]{1,0:T(8,128)(2,1)S(1)}, bf16[32,1024]{1,0:T(8,128)(2,1)S(1)}, u32[]{:S(2)}, u32[]{:S(2)}) collective-permute-start(bf16[32,1024]{1,0:T(8,128)(2,1)S(1)} %get-tuple-element.95), channel_id=1, source_target_pairs={{0,12},{1,13},{2,14},{3,15},{4,8},{5,9},{6,10},{7,11},{8,4},{9,5},... | collective-permute-start | bytes 196616 | tf_op jit(solution)/shard_map/ppermute | solution.py:231
  8.3 0.9 %collective-permute-start.3 = (bf16[16,1024]{1,0:T(8,128)(2,1)S(1)}, bf16[16,1024]{1,0:T(8,128)(2,1)S(1)}, u32[]{:S(2)}, u32[]{:S(2)}) collective-permute-start(bf16[16,1024]{1,0:T(8,128)(2,1)S(1)} %get-tuple-element.97), channel_id=1, source_target_pairs={{0,11},{1,6},{2,13},{3,8},{4,15},{5,10},{6,1},{7,12},{8,3},{9,14},... | collective-permute-start | bytes 98312 | tf_op jit(solution)/shard_map/ppermute | solution.py:231
  9.2 2.8 %collective-permute-start.4 = (bf16[16,1024]{1,0:T(8,128)(2,1)S(1)}, bf16[16,1024]{1,0:T(8,128)(2,1)S(1)}, u32[]{:S(2)}, u32[]{:S(2)}) collective-permute-start(bf16[16,1024]{1,0:T(8,128)(2,1)S(1)} %get-tuple-element.98), channel_id=1, source_target_pairs={{0,15},{1,2},{2,1},{3,4},{4,3},{5,6},{6,5},{7,8},{8,7},{9,10},{10,... | collective-permute-start | bytes 98312 | tf_op jit(solution)/shard_map/ppermute | solution.py:231
  12.3 1.2 %collective-permute-start.8 = (bf16[32,1024]{1,0:T(8,128)(2,1)S(1)}, bf16[32,1024]{1,0:T(8,128)(2,1)S(1)}, u32[]{:S(2)}, u32[]{:S(2)}) collective-permute-start(bf16[32,1024]{1,0:T(8,128)(2,1)S(1)} %collective-permute-done.refs_0_), channel_id=1, source_target_pairs={{0,1},{1,0},{2,3},{3,2},{4,5},{5,4},{6,7},{7,6},{8,9},{9,8},{10,11... | collective-permute-start | bytes 196616 | tf_op jit(solution)/shard_map/ppermute | solution.py:231
  14.1 0.7 %collective-permute-start.6 = (bf16[16,1024]{1,0:T(8,128)(2,1)S(1)}, bf16[16,1024]{1,0:T(8,128)(2,1)S(1)}, u32[]{:S(2)}, u32[]{:S(2)}) collective-permute-start(bf16[16,1024]{1,0:T(8,128)(2,1)S(1)} %get-tuple-element.100), channel_id=1, source_target_pairs={{0,1},{1,0},{2,3},{3,2},{4,5},{5,4},{6,7},{7,6},{8,9},{9,8},{10,11... | collective-permute-start | bytes 98312 | tf_op jit(solution)/shard_map/ppermute | solution.py:231
  15.0 2.0 %local_products.1 = (f32[384,512]{1,0:T(8,128)S(1)}, f32[768,512]{1,0:T(8,128)S(1)}, f32[64,512]{1,0:T(8,128)S(1)}, bf16[384,512]{1,0:T(8,128)(2,1)S(1)}, bf16[5...) custom-call(bf16[256,256]{1,0:T(8,128)(2,1)S(1)} %get-tuple-element., ...), custom_call_target="tpu_custom_call" | custom-call | flops 1275068416 | bytes 14279680 | tf_op jit(solution)/shard_map/local_products/pallas_call | solution.py:172
  17.2 2.7 %edges_forward.1 = (bf16[32,1024]{1,0:T(8,128)(2,1)S(1)}, bf16[32,1024]{1,0:T(8,128)(2,1)S(1)}, bf16[16,1024]{1,0:T(8,128)(2,1)S(1)}, bf16[16,1024]{1,0:T(8,128)...) custom-call(bf16[32,1024]{1,0:T(8,128)(2,1)S(1)} %collective-permute, ...), custom_call_target="tpu_custom_call" | custom-call | flops 1207959552 | bytes 16732928 | tf_op jit(solution)/shard_map/edges_forward/pallas_call | solution.py:172
  19.9 2.0 %collective-permute-start.9 = (bf16[32,1024]{1,0:T(8,128)(2,1)S(1)}, bf16[32,1024]{1,0:T(8,128)(2,1)S(1)}, u32[]{:S(2)}, u32[]{:S(2)}) collective-permute-start(bf16[32,1024]{1,0:T(8,128)(2,1)S(1)} %get-tuple-element.111), channel_id=1, source_target_pairs={{0,12},{1,13},{2,14},{3,15},{4,8},{5,9},{6,10},{7,11},{8,4},{9,5},... | collective-permute-start | bytes 196616 | tf_op jit(solution)/shard_map/ppermute | solution.py:231
  21.9 2.2 %collective-permute-start.11 = (bf16[16,1024]{1,0:T(8,128)(2,1)S(1)}, bf16[16,1024]{1,0:T(8,128)(2,1)S(1)}, u32[]{:S(2)}, u32[]{:S(2)}) collective-permute-start(bf16[16,1024]{1,0:T(8,128)(2,1)S(1)} %get-tuple-element.115), channel_id=1, source_target_pairs={{0,15},{1,2},{2,1},{3,4},{4,3},{5,6},{6,5},{7,8},{8,7},{9,10},{10,... | collective-permute-start | bytes 98312 | tf_op jit(solution)/shard_map/ppermute | solution.py:231
  24.0 1.0 %collective-permute-start.12 = (bf16[16,1024]{1,0:T(8,128)(2,1)S(1)}, bf16[16,1024]{1,0:T(8,128)(2,1)S(1)}, u32[]{:S(2)}, u32[]{:S(2)}) collective-permute-start(bf16[16,1024]{1,0:T(8,128)(2,1)S(1)} %get-tuple-element.116), channel_id=1, source_target_pairs={{0,3},{1,14},{2,5},{3,0},{4,7},{5,2},{6,9},{7,4},{8,11},{9,6},{10,... | collective-permute-start | bytes 98312 | tf_op jit(solution)/shard_map/ppermute | solution.py:231
  25.1 1.0 %collective-permute-start.13 = (bf16[16,1024]{1,0:T(8,128)(2,1)S(1)}, bf16[16,1024]{1,0:T(8,128)(2,1)S(1)}, u32[]{:S(2)}, u32[]{:S(2)}) collective-permute-start(bf16[16,1024]{1,0:T(8,128)(2,1)S(1)} %get-tuple-element.117), channel_id=1, source_target_pairs={{0,11},{1,6},{2,13},{3,8},{4,15},{5,10},{6,1},{7,12},{8,3},{9,14},... | collective-permute-start | bytes 98312 | tf_op jit(solution)/shard_map/ppermute | solution.py:231
  26.7 1.5 %collective-permute-start.14 = (bf16[16,1024]{1,0:T(8,128)(2,1)S(1)}, bf16[16,1024]{1,0:T(8,128)(2,1)S(1)}, u32[]{:S(2)}, u32[]{:S(2)}) collective-permute-start(bf16[16,1024]{1,0:T(8,128)(2,1)S(1)} %get-tuple-element.118), channel_id=1, source_target_pairs={{0,8},{1,9},{2,10},{3,11},{4,12},{5,13},{6,14},{7,15},{8,0},{9,1},... | collective-permute-start | bytes 98312 | tf_op jit(solution)/shard_map/ppermute | solution.py:231
  28.9 2.9 %slopes_and_nodes.1 = (f32[256,512]{1,0:T(8,128)S(1)}, f32[400,512]{1,0:T(8,128)S(1)}, bf16[400,512]{1,0:T(8,128)(2,1)S(1)}, f32[400,512]{1,0:T(8,128)S(1)}, bf1...) custom-call(bf16[32,1024]{1,0:T(8,128)(2,1)S(1)} %collective-permute, ...), custom_call_target="tpu_custom_call" | custom-call | flops 1677721600 | bytes 17874944 | tf_op jit(solution)/shard_map/slopes_and_nodes/pallas_call | solution.py:172
  31.9 4.6 %edges_backward.1 = (bf16[32,512]{1,0:T(8,128)(2,1)S(1)}, bf16[32,512]{1,0:T(8,128)(2,1)S(1)}, bf16[16,512]{1,0:T(8,128)(2,1)S(1)}, bf16[16,512]{1,0:T(8,128)(2,...) custom-call(bf16[32,1024]{1,0:T(8,128)(2,1)S(1)} %collective-permute, ...), custom_call_target="tpu_custom_call" | custom-call | flops 2449473536 | bytes 19878656 | tf_op jit(solution)/shard_map/edges_backward/pallas_call | solution.py:172
  36.5 1.6 %collective-permute-start.18 = (bf16[32,512]{1,0:T(8,128)(2,1)S(1)}, bf16[32,512]{1,0:T(8,128)(2,1)S(1)}, u32[]{:S(2)}, u32[]{:S(2)}) collective-permute-start(bf16[32,512]{1,0:T(8,128)(2,1)S(1)} %get-tuple-element.153), channel_id=1, source_target_pairs={{0,12},{1,13},{2,14},{3,15},{4,8},{5,9},{6,10},{7,11},{8,4},{9,5},... | collective-permute-start | bytes 98312 | tf_op jit(solution)/shard_map/ppermute | solution.py:231
  38.7 1.5 %collective-permute-start.20 = (bf16[16,512]{1,0:T(8,128)(2,1)S(1)}, bf16[16,512]{1,0:T(8,128)(2,1)S(1)}, u32[]{:S(2)}, u32[]{:S(2)}) collective-permute-start(bf16[16,512]{1,0:T(8,128)(2,1)S(1)} %get-tuple-element.157), channel_id=1, source_target_pairs={{0,15},{1,2},{2,1},{3,4},{4,3},{5,6},{6,5},{7,8},{8,7},{9,10},{10,... | collective-permute-start | bytes 49160 | tf_op jit(solution)/shard_map/ppermute | solution.py:231
  40.2 1.1 %collective-permute-start.21 = (bf16[16,512]{1,0:T(8,128)(2,1)S(1)}, bf16[16,512]{1,0:T(8,128)(2,1)S(1)}, u32[]{:S(2)}, u32[]{:S(2)}) collective-permute-start(bf16[16,512]{1,0:T(8,128)(2,1)S(1)} %get-tuple-element.158), channel_id=1, source_target_pairs={{0,3},{1,14},{2,5},{3,0},{4,7},{5,2},{6,9},{7,4},{8,11},{9,6},{10,... | collective-permute-start | bytes 49160 | tf_op jit(solution)/shard_map/ppermute | solution.py:231
  41.3 1.7 %collective-permute-start.22 = (bf16[16,512]{1,0:T(8,128)(2,1)S(1)}, bf16[16,512]{1,0:T(8,128)(2,1)S(1)}, u32[]{:S(2)}, u32[]{:S(2)}) collective-permute-start(bf16[16,512]{1,0:T(8,128)(2,1)S(1)} %get-tuple-element.159), channel_id=1, source_target_pairs={{0,11},{1,6},{2,13},{3,8},{4,15},{5,10},{6,1},{7,12},{8,3},{9,14},... | collective-permute-start | bytes 49160 | tf_op jit(solution)/shard_map/ppermute | solution.py:231
  43.0 1.3 %collective-permute-start.23 = (bf16[16,512]{1,0:T(8,128)(2,1)S(1)}, bf16[16,512]{1,0:T(8,128)(2,1)S(1)}, u32[]{:S(2)}, u32[]{:S(2)}) collective-permute-start(bf16[16,512]{1,0:T(8,128)(2,1)S(1)} %get-tuple-element.160), channel_id=1, source_target_pairs={{0,8},{1,9},{2,10},{3,11},{4,12},{5,13},{6,14},{7,15},{8,0},{9,1},... | collective-permute-start | bytes 49160 | tf_op jit(solution)/shard_map/ppermute | solution.py:231
  44.6 1.2 %collective-permute-start.24 = (bf16[16,512]{1,0:T(8,128)(2,1)S(1)}, bf16[16,512]{1,0:T(8,128)(2,1)S(1)}, u32[]{:S(2)}, u32[]{:S(2)}) collective-permute-start(bf16[16,512]{1,0:T(8,128)(2,1)S(1)} %get-tuple-element.161), channel_id=1, source_target_pairs={{0,1},{1,0},{2,3},{3,2},{4,5},{5,4},{6,7},{7,6},{8,9},{9,8},{10,11... | collective-permute-start | bytes 49160 | tf_op jit(solution)/shard_map/ppermute | solution.py:231
  45.9 1.9 %local_gradients.1 = (f32[256,512]{1,0:T(8,128)S(1)}, f32[64,512]{1,0:T(8,128)}, bf16[256,512]{1,0:T(8,128)(2,1)}) custom-call(bf16[256,512]{1,0:T(8,128)(2,1)S(1)} %copy-done.4, f32[400,512]{1,0:T(8,128)S(1)} %get-tuple-element.145.refs_1_, bf16[256,512]{1,0:T(8,128)(2,1)S(1)} %copy-done.5, bf16[400,512]{1,0:T(8,128)(2,1)S(1)} %get-tuple-element.146.refs_3_, ...), custom_call_target="tpu_custom_call" | custom-call | flops 402653184 | bytes 12042240 | tf_op jit(solution)/shard_map/local_gradients/pallas_call | solution.py:172
  47.9 1.0 %add_returned.1 = f32[256,512]{1,0:T(8,128)} custom-call(bf16[32,512]{1,0:T(8,128)(2,1)S(1)} %collective-permute-done.18.refs_0_, bf16[32,512]{1,0:T(8,128)(2,1)S(1)} %collective-permute-done.19.refs_1_, bf16[16,512]{1,0:T(8,128)(2,1)S(1)} %collective-permute-done.20.refs_2_, bf16[16,512]{1,0:T(8,128)(2,1)S(1)} %collective-permute-done.21.refs_3_, ...), custom_call_target="tpu_custom_call" | custom-call | tf_op jit(solution)/shard_map/add_returned/pallas_call | solution.py:934
  (74 shorter events, 4.1 us)
Async XLA Ops:
  2.3 9.6 %collective-permute-start = (bf16[32,1024]{1,0:T(8,128)(2,1)S(1)}, bf16[32,1024]{1,0:T(8,128)(2,1)S(1)}, u32[]{:S(2)}, u32[]{:S(2)}) collective-permute-start(bf16[32,1024]{1,0:T(8,128)(2,1)S(1)} %get-tuple-element.92), channel_id=1, source_target_pairs={{0,4},{1,5},{2,6},{3,7},{4,0},{5,1},{6,2},{7,3},{8,12},{9,13},{10,... | collective-permute-start | bytes 196616 | tf_op jit(solution)/shard_map/ppermute | solution.py:231
  5.4 9.4 %collective-permute-start.1 = (bf16[32,1024]{1,0:T(8,128)(2,1)S(1)}, bf16[32,1024]{1,0:T(8,128)(2,1)S(1)}, u32[]{:S(2)}, u32[]{:S(2)}) collective-permute-start(bf16[32,1024]{1,0:T(8,128)(2,1)S(1)} %get-tuple-element.95), channel_id=1, source_target_pairs={{0,12},{1,13},{2,14},{3,15},{4,8},{5,9},{6,10},{7,11},{8,4},{9,5},... | collective-permute-start | bytes 196616 | tf_op jit(solution)/shard_map/ppermute | solution.py:231
  7.9 4.4 %collective-permute-start.2 = (bf16[16,1024]{1,0:T(8,128)(2,1)S(1)}, bf16[16,1024]{1,0:T(8,128)(2,1)S(1)}, u32[]{:S(2)}, u32[]{:S(2)}) collective-permute-start(bf16[16,1024]{1,0:T(8,128)(2,1)S(1)} %get-tuple-element.96), channel_id=1, source_target_pairs={{0,3},{1,14},{2,5},{3,0},{4,7},{5,2},{6,9},{7,4},{8,11},{9,6},{10,... | collective-permute-start | bytes 98312 | tf_op jit(solution)/shard_map/ppermute | solution.py:231
  8.3 5.8 %collective-permute-start.3 = (bf16[16,1024]{1,0:T(8,128)(2,1)S(1)}, bf16[16,1024]{1,0:T(8,128)(2,1)S(1)}, u32[]{:S(2)}, u32[]{:S(2)}) collective-permute-start(bf16[16,1024]{1,0:T(8,128)(2,1)S(1)} %get-tuple-element.97), channel_id=1, source_target_pairs={{0,11},{1,6},{2,13},{3,8},{4,15},{5,10},{6,1},{7,12},{8,3},{9,14},... | collective-permute-start | bytes 98312 | tf_op jit(solution)/shard_map/ppermute | solution.py:231
  9.2 7.8 %collective-permute-start.4 = (bf16[16,1024]{1,0:T(8,128)(2,1)S(1)}, bf16[16,1024]{1,0:T(8,128)(2,1)S(1)}, u32[]{:S(2)}, u32[]{:S(2)}) collective-permute-start(bf16[16,1024]{1,0:T(8,128)(2,1)S(1)} %get-tuple-element.98), channel_id=1, source_target_pairs={{0,15},{1,2},{2,1},{3,4},{4,3},{5,6},{6,5},{7,8},{8,7},{9,10},{10,... | collective-permute-start | bytes 98312 | tf_op jit(solution)/shard_map/ppermute | solution.py:231
  12.0 5.2 %collective-permute-start.5 = (bf16[16,1024]{1,0:T(8,128)(2,1)S(1)}, bf16[16,1024]{1,0:T(8,128)(2,1)S(1)}, u32[]{:S(2)}, u32[]{:S(2)}) collective-permute-start(bf16[16,1024]{1,0:T(8,128)(2,1)S(1)} %get-tuple-element.99), channel_id=1, source_target_pairs={{0,8},{1,9},{2,10},{3,11},{4,12},{5,13},{6,14},{7,15},{8,0},{9,1},... | collective-permute-start | bytes 98312 | tf_op jit(solution)/shard_map/ppermute | solution.py:231
  12.3 4.8 %collective-permute-start.8 = (bf16[32,1024]{1,0:T(8,128)(2,1)S(1)}, bf16[32,1024]{1,0:T(8,128)(2,1)S(1)}, u32[]{:S(2)}, u32[]{:S(2)}) collective-permute-start(bf16[32,1024]{1,0:T(8,128)(2,1)S(1)} %collective-permute-done.refs_0_), channel_id=1, source_target_pairs={{0,1},{1,0},{2,3},{3,2},{4,5},{5,4},{6,7},{7,6},{8,9},{9,8},{10,11... | collective-permute-start | bytes 196616 | tf_op jit(solution)/shard_map/ppermute | solution.py:231
  19.9 6.8 %collective-permute-start.9 = (bf16[32,1024]{1,0:T(8,128)(2,1)S(1)}, bf16[32,1024]{1,0:T(8,128)(2,1)S(1)}, u32[]{:S(2)}, u32[]{:S(2)}) collective-permute-start(bf16[32,1024]{1,0:T(8,128)(2,1)S(1)} %get-tuple-element.111), channel_id=1, source_target_pairs={{0,12},{1,13},{2,14},{3,15},{4,8},{5,9},{6,10},{7,11},{8,4},{9,5},... | collective-permute-start | bytes 196616 | tf_op jit(solution)/shard_map/ppermute | solution.py:231
  21.9 7.0 %collective-permute-start.10 = (bf16[32,1024]{1,0:T(8,128)(2,1)S(1)}, bf16[32,1024]{1,0:T(8,128)(2,1)S(1)}, u32[]{:S(2)}, u32[]{:S(2)}) collective-permute-start(bf16[32,1024]{1,0:T(8,128)(2,1)S(1)} %get-tuple-element.114), channel_id=1, source_target_pairs={{0,4},{1,5},{2,6},{3,7},{4,0},{5,1},{6,2},{7,3},{8,12},{9,13},{10,... | collective-permute-start | bytes 196616 | tf_op jit(solution)/shard_map/ppermute | solution.py:231
  21.9 6.4 %collective-permute-start.11 = (bf16[16,1024]{1,0:T(8,128)(2,1)S(1)}, bf16[16,1024]{1,0:T(8,128)(2,1)S(1)}, u32[]{:S(2)}, u32[]{:S(2)}) collective-permute-start(bf16[16,1024]{1,0:T(8,128)(2,1)S(1)} %get-tuple-element.115), channel_id=1, source_target_pairs={{0,15},{1,2},{2,1},{3,4},{4,3},{5,6},{6,5},{7,8},{8,7},{9,10},{10,... | collective-permute-start | bytes 98312 | tf_op jit(solution)/shard_map/ppermute | solution.py:231
  24.0 4.3 %collective-permute-start.12 = (bf16[16,1024]{1,0:T(8,128)(2,1)S(1)}, bf16[16,1024]{1,0:T(8,128)(2,1)S(1)}, u32[]{:S(2)}, u32[]{:S(2)}) collective-permute-start(bf16[16,1024]{1,0:T(8,128)(2,1)S(1)} %get-tuple-element.116), channel_id=1, source_target_pairs={{0,3},{1,14},{2,5},{3,0},{4,7},{5,2},{6,9},{7,4},{8,11},{9,6},{10,... | collective-permute-start | bytes 98312 | tf_op jit(solution)/shard_map/ppermute | solution.py:231
  25.1 6.7 %collective-permute-start.13 = (bf16[16,1024]{1,0:T(8,128)(2,1)S(1)}, bf16[16,1024]{1,0:T(8,128)(2,1)S(1)}, u32[]{:S(2)}, u32[]{:S(2)}) collective-permute-start(bf16[16,1024]{1,0:T(8,128)(2,1)S(1)} %get-tuple-element.117), channel_id=1, source_target_pairs={{0,11},{1,6},{2,13},{3,8},{4,15},{5,10},{6,1},{7,12},{8,3},{9,14},... | collective-permute-start | bytes 98312 | tf_op jit(solution)/shard_map/ppermute | solution.py:231
  26.7 5.2 %collective-permute-start.14 = (bf16[16,1024]{1,0:T(8,128)(2,1)S(1)}, bf16[16,1024]{1,0:T(8,128)(2,1)S(1)}, u32[]{:S(2)}, u32[]{:S(2)}) collective-permute-start(bf16[16,1024]{1,0:T(8,128)(2,1)S(1)} %get-tuple-element.118), channel_id=1, source_target_pairs={{0,8},{1,9},{2,10},{3,11},{4,12},{5,13},{6,14},{7,15},{8,0},{9,1},... | collective-permute-start | bytes 98312 | tf_op jit(solution)/shard_map/ppermute | solution.py:231
  28.3 3.6 %collective-permute-start.16 = (bf16[32,1024]{1,0:T(8,128)(2,1)S(1)}, bf16[32,1024]{1,0:T(8,128)(2,1)S(1)}, u32[]{:S(2)}, u32[]{:S(2)}) collective-permute-start(bf16[32,1024]{1,0:T(8,128)(2,1)S(1)} %collective-permute-done.9.refs_0_), channel_id=1, source_target_pairs={{0,1},{1,0},{2,3},{3,2},{4,5},{5,4},{6,7},{7,6},{8,9},{9,8},{10,11... | collective-permute-start | bytes 196616 | tf_op jit(solution)/shard_map/ppermute | solution.py:231
  28.3 3.6 %collective-permute-start.15 = (bf16[16,1024]{1,0:T(8,128)(2,1)S(1)}, bf16[16,1024]{1,0:T(8,128)(2,1)S(1)}, u32[]{:S(2)}, u32[]{:S(2)}) collective-permute-start(bf16[16,1024]{1,0:T(8,128)(2,1)S(1)} %get-tuple-element.119), channel_id=1, source_target_pairs={{0,1},{1,0},{2,3},{3,2},{4,5},{5,4},{6,7},{7,6},{8,9},{9,8},{10,11... | collective-permute-start | bytes 98312 | tf_op jit(solution)/shard_map/ppermute | solution.py:231
  28.8 3.1 %collective-permute-start.17 = (bf16[32,1024]{1,0:T(8,128)(2,1)S(1)}, bf16[32,1024]{1,0:T(8,128)(2,1)S(1)}, u32[]{:S(2)}, u32[]{:S(2)}) collective-permute-start(bf16[32,1024]{1,0:T(8,128)(2,1)S(1)} %collective-permute-done.10.refs_1_), channel_id=1, source_target_pairs={{0,1},{1,0},{2,3},{3,2},{4,5},{5,4},{6,7},{7,6},{8,9},{9,8},{10,11... | collective-permute-start | bytes 196616 | tf_op jit(solution)/shard_map/ppermute | solution.py:231
  36.5 6.5 %collective-permute-start.18 = (bf16[32,512]{1,0:T(8,128)(2,1)S(1)}, bf16[32,512]{1,0:T(8,128)(2,1)S(1)}, u32[]{:S(2)}, u32[]{:S(2)}) collective-permute-start(bf16[32,512]{1,0:T(8,128)(2,1)S(1)} %get-tuple-element.153), channel_id=1, source_target_pairs={{0,12},{1,13},{2,14},{3,15},{4,8},{5,9},{6,10},{7,11},{8,4},{9,5},... | collective-permute-start | bytes 98312 | tf_op jit(solution)/shard_map/ppermute | solution.py:231
  38.1 7.8 %collective-permute-start.19 = (bf16[32,512]{1,0:T(8,128)(2,1)S(1)}, bf16[32,512]{1,0:T(8,128)(2,1)S(1)}, u32[]{:S(2)}, u32[]{:S(2)}) collective-permute-start(bf16[32,512]{1,0:T(8,128)(2,1)S(1)} %get-tuple-element.156), channel_id=1, source_target_pairs={{0,4},{1,5},{2,6},{3,7},{4,0},{5,1},{6,2},{7,3},{8,12},{9,13},{10,... | collective-permute-start | bytes 98312 | tf_op jit(solution)/shard_map/ppermute | solution.py:231
  38.7 5.9 %collective-permute-start.20 = (bf16[16,512]{1,0:T(8,128)(2,1)S(1)}, bf16[16,512]{1,0:T(8,128)(2,1)S(1)}, u32[]{:S(2)}, u32[]{:S(2)}) collective-permute-start(bf16[16,512]{1,0:T(8,128)(2,1)S(1)} %get-tuple-element.157), channel_id=1, source_target_pairs={{0,15},{1,2},{2,1},{3,4},{4,3},{5,6},{6,5},{7,8},{8,7},{9,10},{10,... | collective-permute-start | bytes 49160 | tf_op jit(solution)/shard_map/ppermute | solution.py:231
  40.2 4.4 %collective-permute-start.21 = (bf16[16,512]{1,0:T(8,128)(2,1)S(1)}, bf16[16,512]{1,0:T(8,128)(2,1)S(1)}, u32[]{:S(2)}, u32[]{:S(2)}) collective-permute-start(bf16[16,512]{1,0:T(8,128)(2,1)S(1)} %get-tuple-element.158), channel_id=1, source_target_pairs={{0,3},{1,14},{2,5},{3,0},{4,7},{5,2},{6,9},{7,4},{8,11},{9,6},{10,... | collective-permute-start | bytes 49160 | tf_op jit(solution)/shard_map/ppermute | solution.py:231
  41.3 6.5 %collective-permute-start.22 = (bf16[16,512]{1,0:T(8,128)(2,1)S(1)}, bf16[16,512]{1,0:T(8,128)(2,1)S(1)}, u32[]{:S(2)}, u32[]{:S(2)}) collective-permute-start(bf16[16,512]{1,0:T(8,128)(2,1)S(1)} %get-tuple-element.159), channel_id=1, source_target_pairs={{0,11},{1,6},{2,13},{3,8},{4,15},{5,10},{6,1},{7,12},{8,3},{9,14},... | collective-permute-start | bytes 49160 | tf_op jit(solution)/shard_map/ppermute | solution.py:231
  43.0 4.9 %collective-permute-start.23 = (bf16[16,512]{1,0:T(8,128)(2,1)S(1)}, bf16[16,512]{1,0:T(8,128)(2,1)S(1)}, u32[]{:S(2)}, u32[]{:S(2)}) collective-permute-start(bf16[16,512]{1,0:T(8,128)(2,1)S(1)} %get-tuple-element.160), channel_id=1, source_target_pairs={{0,8},{1,9},{2,10},{3,11},{4,12},{5,13},{6,14},{7,15},{8,0},{9,1},... | collective-permute-start | bytes 49160 | tf_op jit(solution)/shard_map/ppermute | solution.py:231
  44.6 3.4 %collective-permute-start.25 = (bf16[32,512]{1,0:T(8,128)(2,1)S(1)}, bf16[32,512]{1,0:T(8,128)(2,1)S(1)}, u32[]{:S(2)}, u32[]{:S(2)}) collective-permute-start(bf16[32,512]{1,0:T(8,128)(2,1)S(1)} %collective-permute-done.18.refs_0_), channel_id=1, source_target_pairs={{0,1},{1,0},{2,3},{3,2},{4,5},{5,4},{6,7},{7,6},{8,9},{9,8},{10,11... | collective-permute-start | bytes 98312 | tf_op jit(solution)/shard_map/ppermute | solution.py:231
  44.6 3.3 %collective-permute-start.24 = (bf16[16,512]{1,0:T(8,128)(2,1)S(1)}, bf16[16,512]{1,0:T(8,128)(2,1)S(1)}, u32[]{:S(2)}, u32[]{:S(2)}) collective-permute-start(bf16[16,512]{1,0:T(8,128)(2,1)S(1)} %get-tuple-element.161), channel_id=1, source_target_pairs={{0,1},{1,0},{2,3},{3,2},{4,5},{5,4},{6,7},{7,6},{8,9},{9,8},{10,11... | collective-permute-start | bytes 49160 | tf_op jit(solution)/shard_map/ppermute | solution.py:231
  (21 other events, 233.3 us)

commit v21 on v20

--- a/solution.py
+++ b/solution.py
@@ -230,9 +230,10 @@
         pairs = [(s, (s + rows[s // TW % 2][s % 2]) % peer_count) for s in peers]
         return lax.ppermute(part, "tile", pairs)
 
-    steady = ("late", "early", "behind", "ahead", "five", "opposite", "own")
+    steady = ("late", "early", "opposite", "ahead", "five", "behind", "own")
+    closing = ("late", "early", "behind", "ahead", "five", "opposite", "own")
     staggered = ("early", "late", "ahead", "five", "behind", "opposite", "own")
-    arrived_count = 9
+    arrived_count = 7
 
     def exchange(parts, order):
         moves = {
@@ -242,17 +243,23 @@
             "ahead": ((3, -3),),
             "five": ((-5, 5),),
             "opposite": ((peer_count // 2, peer_count // 2),),
-            "own": ((1, -1),),
         }
         parts = dict(zip(order, parts))
         own_chip = parts.pop("own")
         got = {name: permute(part, *moves[name]) for name, part in parts.items()}
-        first = order[0]
-        got[first], own_chip = lax.optimization_barrier((got[first], own_chip))
-        late_passed = permute(got["late"], (1, -1))
-        got["own"] = permute(own_chip, (1, -1))
-        early_passed = permute(got["early"], (1, -1))
-        return [got[name] for name in order] + [late_passed, early_passed]
+
+        def lay_together(own_ref, late_ref, early_ref, passed_ref):
+            passed_ref[:width, :] = own_ref[...]
+            passed_ref[width : 2 * width, :] = late_ref[width:, :]
+            passed_ref[2 * width :, :] = early_ref[width:, :]
+
+        (passed,) = call(
+            lay_together,
+            "lay_together",
+            [own_chip, got["late"], got["early"]],
+            [((3 * width, own_chip.shape[1]), BF16)],
+        )
+        return [got[name] for name in order if name in got] + [permute(passed, (1, -1))]
 
     def sent_shapes(columns, order=steady):
         double = ("late", "early")
@@ -271,7 +278,7 @@
         def by_parity(even, odd_one):
             return jnp.where(odd, message(odd_one), message(even))
 
-        late_pair, early_pair, behind_one, ahead_three, five_off, opposite, own_chip = [
+        late_pair, early_pair, opposite, ahead_three, five_off, behind_one, own_chip = [
             refs[name] for name in steady
         ]
         first, second = slice(0, width), slice(width, 2 * width)
@@ -288,15 +295,16 @@
 
     def receive(refs, columns=slice(None), order=steady):
         odd, odd_row = place_bits()
-        late_passed, early_passed = refs[sent_count:]
-        refs = dict(zip(order, refs))
-        late_pair, early_pair, behind_one, ahead_three, five_off, opposite, own_chip = [
-            refs[name] for name in steady
+        passed = refs[-1]
+        refs = dict(zip([name for name in order if name != "own"], refs))
+        late_pair, early_pair, opposite, ahead_three, five_off, behind_one = [
+            refs[name] for name in steady if name != "own"
         ]
         first, second = slice(0, width), slice(width, 2 * width)
         near, near_three = behind_one[:, columns], ahead_three[:, columns]
-        far, own = five_off[:, columns], own_chip[:, columns]
-        late_rows, early_rows = late_passed[second, columns], early_passed[second, columns]
+        far, own = five_off[:, columns], passed[first, columns]
+        late_rows = passed[second, columns]
+        early_rows = passed[2 * width :, columns]
         from_behind = jnp.where(odd_row, early_rows, late_rows)
         from_ahead = jnp.where(odd_row, late_rows, early_rows)
         late_rows, early_rows = late_pair[first, columns], early_pair[first, columns]
@@ -315,8 +323,8 @@
     def by_slot(refs, columns=slice(None), order=steady):
         return jnp.concatenate(receive(refs, columns, order), axis=0)
 
-    def by_row(refs, columns=slice(None)):
-        slot_rows = receive(refs, columns)
+    def by_row(refs, columns=slice(None), order=steady):
+        slot_rows = receive(refs, columns, order)
         return jnp.concatenate([slot_rows[reverse[j]] for j in range(links)], axis=0)
 
     def pack(index_ref, count_ref, nodes_ref, cot_ref, select_ref, *out_refs):
@@ -791,7 +799,11 @@
         )
         pooled = mm(enc_pool_ref[grid_count:spots, :], enc_gpre_ref[...]).astype(BF16)
         slot_back = (slot_back + mm_t(pooled, enc_first_ref[low, :])).astype(BF16)
-        send(out_refs, lambda j: slot_back[reverse[j] * width : (reverse[j] + 1) * width, :])
+        send(
+            out_refs,
+            lambda j: slot_back[reverse[j] * width : (reverse[j] + 1) * width, :],
+            order=closing,
+        )
 
     results = call(
         backward,
@@ -830,7 +842,7 @@
             mesh_slope,
             mesh_turned,
         ],
-        sent_shapes(feat)
+        sent_shapes(feat, closing)
         + [
             ((spots, feat), F32),
             ((spots, feat), BF16),
@@ -849,7 +861,7 @@
     )
     outgoing, results = results[:sent_count], results[sent_count:]
     grid_normed, grid_gpre, dec_gpre, enc_gpre, mesh_gin, mesh_gpre = results
-    final = exchange(outgoing, steady)
+    final = exchange(outgoing, closing)
 
     def tail(
         nodes_ref,
@@ -910,7 +922,7 @@
             enc_first,
         ],
         [((grid_count, feat), F32), ((mesh_count, feat), F32), ((grid_count, feat), BF16)],
-        flops=2 * feat * feat * 3 * grid_count,
+        flops=16 * spots * feat * feat,
     )
 
     pieces = row_chunks(grid_count, 64)
@@ -918,7 +930,7 @@
     def finish(*refs):
         back_refs = refs[:arrived_count]
         base_ref, select_t_ref, out_ref, piece_ref, semaphores = refs[arrived_count:]
-        back = by_row(back_refs)
+        back = by_row(back_refs, order=closing)
         copies = []
         for place, rows in enumerate(pieces):
             piece_ref[rows, :] = base_ref[rows, :] + mm(select_t_ref[rows, :slots], back)

time: 49.1 us -> 48.6 us (0.990)
  starting transfers between devices: 29.2 us -> 26.4 us
  waiting for transfers between devices: 1.93 us -> 4.24 us
    ppermute x27 -> x21, starting transfers between devices: 29.2 us -> 26.4 us  [permute(): return lax.ppermute(part, 'tile', pairs)]
    ppermute x27 -> x21, waiting for transfers between devices: 1.93 us -> 4.24 us  [permute(): return lax.ppermute(part, 'tile', pairs)]
    pallas_call x7 -> x10, Pallas kernels: 15.7 us -> 15.7 us  [call(): pl.pallas_call(kernel, name=name, in_specs=specs, out_specs=[pl.BlockSpec...]
  transfers between devices with their start and end apart: 27 -> 21, of which waited for: 7 -> 4; matrix products, arithmetic and copies ran while one was open for 0% -> 0% of each run, Pallas kernels for 14% -> 14%
where the time goes in v21:
time: 48.6 us; the launch traced here: 48.4 us
  starting transfers between devices  26.4 us (54%)
  Pallas kernels  16.7 us (34%)
  waiting for transfers between devices  4.24 us (9%)
  between operations  0.99 us (2%)
    ppermute x21, starting transfers between devices, permute(): return lax.ppermute(part, 'tile', pairs)  26.4 us
    pallas_call x10, Pallas kernels, call(): pl.pallas_call(kernel, name=name, in_specs=specs, out_specs=[pl.BlockSpec...  15.7 us
    ppermute x21, waiting for transfers between devices, permute(): return lax.ppermute(part, 'tile', pairs)  4.24 us
    pallas_call x1, Pallas kernels, per_device(): pl.pallas_call(finish, name='add_returned', in_specs=[pl.BlockSpec(memory...  0.99 us
  transfers between devices with their start and end apart: 21, of which 4 were waited for; matrix products, arithmetic and copies ran while one was open for 0% of the time, Pallas kernels for 14%

profile of v21, /device:TPU:0, one launch (start us, length us, event | category | flops | bytes accessed | tf_op | source)
XLA Modules:
  0.0 48.4 jit_solution(7928737886402073477)
XLA Ops:
  0.6 1.4 %pack_rows.1 = (bf16[256,256]{1,0:T(8,128)(2,1)S(1)}, bf16[32,1024]{1,0:T(8,128)(2,1)S(1)}, bf16[32,1024]{1,0:T(8,128)(2,1)S(1)}, bf16[16,1024]{1,0:T(8,128)(2,1...) custom-call(s32[9,16]{1,0:T(8,128)} %refs_0_.2, ...), custom_call_target="tpu_custom_call" | custom-call | flops 75497472 | bytes 950884 | tf_op jit(solution)/shard_map/pack_rows/pallas_call | solution.py:172
  2.3 3.1 %collective-permute-start = (bf16[32,1024]{1,0:T(8,128)(2,1)S(1)}, bf16[32,1024]{1,0:T(8,128)(2,1)S(1)}, u32[]{:S(2)}, u32[]{:S(2)}) collective-permute-start(bf16[32,1024]{1,0:T(8,128)(2,1)S(1)} %get-tuple-element.86), channel_id=1, source_target_pairs={{0,4},{1,5},{2,6},{3,7},{4,0},{5,1},{6,2},{7,3},{8,12},{9,13},{10,... | collective-permute-start | bytes 196616 | tf_op jit(solution)/shard_map/ppermute | solution.py:231
  5.4 2.5 %collective-permute-start.1 = (bf16[32,1024]{1,0:T(8,128)(2,1)S(1)}, bf16[32,1024]{1,0:T(8,128)(2,1)S(1)}, u32[]{:S(2)}, u32[]{:S(2)}) collective-permute-start(bf16[32,1024]{1,0:T(8,128)(2,1)S(1)} %get-tuple-element.87), channel_id=1, source_target_pairs={{0,12},{1,13},{2,14},{3,15},{4,8},{5,9},{6,10},{7,11},{8,4},{9,5},... | collective-permute-start | bytes 196616 | tf_op jit(solution)/shard_map/ppermute | solution.py:231
  7.9 0.4 collective-permute-start.2
  8.3 0.9 %collective-permute-start.3 = (bf16[16,1024]{1,0:T(8,128)(2,1)S(1)}, bf16[16,1024]{1,0:T(8,128)(2,1)S(1)}, u32[]{:S(2)}, u32[]{:S(2)}) collective-permute-start(bf16[16,1024]{1,0:T(8,128)(2,1)S(1)} %get-tuple-element.89), channel_id=1, source_target_pairs={{0,11},{1,6},{2,13},{3,8},{4,15},{5,10},{6,1},{7,12},{8,3},{9,14},... | collective-permute-start | bytes 98312 | tf_op jit(solution)/shard_map/ppermute | solution.py:231
  9.2 2.8 %collective-permute-start.4 = (bf16[16,1024]{1,0:T(8,128)(2,1)S(1)}, bf16[16,1024]{1,0:T(8,128)(2,1)S(1)}, u32[]{:S(2)}, u32[]{:S(2)}) collective-permute-start(bf16[16,1024]{1,0:T(8,128)(2,1)S(1)} %get-tuple-element.90), channel_id=1, source_target_pairs={{0,15},{1,2},{2,1},{3,4},{4,3},{5,6},{6,5},{7,8},{8,7},{9,10},{10,... | collective-permute-start | bytes 98312 | tf_op jit(solution)/shard_map/ppermute | solution.py:231
  12.3 1.1 %collective-permute-start.6 = (bf16[48,1024]{1,0:T(8,128)(2,1)S(1)}, bf16[48,1024]{1,0:T(8,128)(2,1)S(1)}, u32[]{:S(2)}, u32[]{:S(2)}) collective-permute-start(bf16[48,1024]{1,0:T(8,128)(2,1)S(1)} %lay_together.3), channel_id=1, source_target_pairs={{0,1},{1,0},{2,3},{3,2},{4,5},{5,4},{6,7},{7,6},{8,9},{9,8},{10,11... | collective-permute-start | bytes 294920 | tf_op jit(solution)/shard_map/ppermute | solution.py:231
  13.6 2.0 %local_products.1 = (f32[384,512]{1,0:T(8,128)S(1)}, f32[768,512]{1,0:T(8,128)S(1)}, f32[64,512]{1,0:T(8,128)S(1)}, bf16[384,512]{1,0:T(8,128)(2,1)S(1)}, bf16[5...) custom-call(bf16[256,256]{1,0:T(8,128)(2,1)S(1)} %get-tuple-element., ...), custom_call_target="tpu_custom_call" | custom-call | flops 1275068416 | bytes 14279680 | tf_op jit(solution)/shard_map/local_products/pallas_call | solution.py:172
  15.6 1.5 %collective-permute-done.5.refs_5_ = bf16[16,1024]{1,0:T(8,128)(2,1)S(1)} collective-permute-done((bf16[16,1024]{1,0:T(8,128)(2,1)S(1)}, bf16[16,1024]{1,0:T(8,128)(2,1)S(1)}, u32[]{:S(2)}, u32[]{:S(2)}) %collective-permute-start.5) | collective-permute-done | bytes 32800 | tf_op jit(solution)/shard_map/ppermute | solution.py:231
  17.1 2.7 %edges_forward.1 = (bf16[32,1024]{1,0:T(8,128)(2,1)S(1)}, bf16[32,1024]{1,0:T(8,128)(2,1)S(1)}, bf16[16,1024]{1,0:T(8,128)(2,1)S(1)}, bf16[16,1024]{1,0:T(8,128)...) custom-call(bf16[32,1024]{1,0:T(8,128)(2,1)S(1)} %collective-permute, ...), custom_call_target="tpu_custom_call" | custom-call | flops 1207959552 | bytes 16667392 | tf_op jit(solution)/shard_map/edges_forward/pallas_call | solution.py:172
  19.9 1.9 %collective-permute-start.7 = (bf16[32,1024]{1,0:T(8,128)(2,1)S(1)}, bf16[32,1024]{1,0:T(8,128)(2,1)S(1)}, u32[]{:S(2)}, u32[]{:S(2)}) collective-permute-start(bf16[32,1024]{1,0:T(8,128)(2,1)S(1)} %get-tuple-element.103), channel_id=1, source_target_pairs={{0,12},{1,13},{2,14},{3,15},{4,8},{5,9},{6,10},{7,11},{8,4},{9,5},... | collective-permute-start | bytes 196616 | tf_op jit(solution)/shard_map/ppermute | solution.py:231
  21.8 3.7 %collective-permute-start.11 = (bf16[16,1024]{1,0:T(8,128)(2,1)S(1)}, bf16[16,1024]{1,0:T(8,128)(2,1)S(1)}, u32[]{:S(2)}, u32[]{:S(2)}) collective-permute-start(bf16[16,1024]{1,0:T(8,128)(2,1)S(1)} %get-tuple-element.107), channel_id=1, source_target_pairs={{0,11},{1,6},{2,13},{3,8},{4,15},{5,10},{6,1},{7,12},{8,3},{9,14},... | collective-permute-start | bytes 98312 | tf_op jit(solution)/shard_map/ppermute | solution.py:231
  25.5 1.3 %collective-permute-start.12 = (bf16[16,1024]{1,0:T(8,128)(2,1)S(1)}, bf16[16,1024]{1,0:T(8,128)(2,1)S(1)}, u32[]{:S(2)}, u32[]{:S(2)}) collective-permute-start(bf16[16,1024]{1,0:T(8,128)(2,1)S(1)} %get-tuple-element.108), channel_id=1, source_target_pairs={{0,15},{1,2},{2,1},{3,4},{4,3},{5,6},{6,5},{7,8},{8,7},{9,10},{10,... | collective-permute-start | bytes 98312 | tf_op jit(solution)/shard_map/ppermute | solution.py:231
  27.0 2.9 %slopes_and_nodes.1 = (f32[256,512]{1,0:T(8,128)S(1)}, f32[400,512]{1,0:T(8,128)S(1)}, bf16[400,512]{1,0:T(8,128)(2,1)S(1)}, f32[400,512]{1,0:T(8,128)S(1)}, bf1...) custom-call(bf16[32,1024]{1,0:T(8,128)(2,1)S(1)} %collective-permute, ...), custom_call_target="tpu_custom_call" | custom-call | flops 1677721600 | bytes 17809408 | tf_op jit(solution)/shard_map/slopes_and_nodes/pallas_call | solution.py:172
  29.9 1.7 %collective-permute-done.12.refs_5_ = bf16[16,1024]{1,0:T(8,128)(2,1)S(1)} collective-permute-done((bf16[16,1024]{1,0:T(8,128)(2,1)S(1)}, bf16[16,1024]{1,0:T(8,128)(2,1)S(1)}, u32[]{:S(2)}, u32[]{:S(2)}) %collective-permute-start.12) | collective-permute-done | bytes 32800 | tf_op jit(solution)/shard_map/ppermute | solution.py:231
  31.6 4.6 %edges_backward.1 = (bf16[32,512]{1,0:T(8,128)(2,1)S(1)}, bf16[32,512]{1,0:T(8,128)(2,1)S(1)}, bf16[16,512]{1,0:T(8,128)(2,1)S(1)}, bf16[16,512]{1,0:T(8,128)(2,...) custom-call(bf16[32,1024]{1,0:T(8,128)(2,1)S(1)} %collective-permute, ...), custom_call_target="tpu_custom_call" | custom-call | flops 2449473536 | bytes 19813120 | tf_op jit(solution)/shard_map/edges_backward/pallas_call | solution.py:172
  36.2 1.6 %collective-permute-start.14 = (bf16[32,512]{1,0:T(8,128)(2,1)S(1)}, bf16[32,512]{1,0:T(8,128)(2,1)S(1)}, u32[]{:S(2)}, u32[]{:S(2)}) collective-permute-start(bf16[32,512]{1,0:T(8,128)(2,1)S(1)} %get-tuple-element.143), channel_id=1, source_target_pairs={{0,12},{1,13},{2,14},{3,15},{4,8},{5,9},{6,10},{7,11},{8,4},{9,5},... | collective-permute-start | bytes 98312 | tf_op jit(solution)/shard_map/ppermute | solution.py:231
  38.0 2.3 %collective-permute-start.16 = (bf16[16,512]{1,0:T(8,128)(2,1)S(1)}, bf16[16,512]{1,0:T(8,128)(2,1)S(1)}, u32[]{:S(2)}, u32[]{:S(2)}) collective-permute-start(bf16[16,512]{1,0:T(8,128)(2,1)S(1)} %get-tuple-element.145), channel_id=1, source_target_pairs={{0,15},{1,2},{2,1},{3,4},{4,3},{5,6},{6,5},{7,8},{8,7},{9,10},{10,... | collective-permute-start | bytes 49160 | tf_op jit(solution)/shard_map/ppermute | solution.py:231
  40.3 0.7 %collective-permute-start.17 = (bf16[16,512]{1,0:T(8,128)(2,1)S(1)}, bf16[16,512]{1,0:T(8,128)(2,1)S(1)}, u32[]{:S(2)}, u32[]{:S(2)}) collective-permute-start(bf16[16,512]{1,0:T(8,128)(2,1)S(1)} %get-tuple-element.146), channel_id=1, source_target_pairs={{0,3},{1,14},{2,5},{3,0},{4,7},{5,2},{6,9},{7,4},{8,11},{9,6},{10,... | collective-permute-start | bytes 49160 | tf_op jit(solution)/shard_map/ppermute | solution.py:231
  41.1 1.5 %collective-permute-start.18 = (bf16[16,512]{1,0:T(8,128)(2,1)S(1)}, bf16[16,512]{1,0:T(8,128)(2,1)S(1)}, u32[]{:S(2)}, u32[]{:S(2)}) collective-permute-start(bf16[16,512]{1,0:T(8,128)(2,1)S(1)} %get-tuple-element.147), channel_id=1, source_target_pairs={{0,11},{1,6},{2,13},{3,8},{4,15},{5,10},{6,1},{7,12},{8,3},{9,14},... | collective-permute-start | bytes 49160 | tf_op jit(solution)/shard_map/ppermute | solution.py:231
  42.6 1.9 %collective-permute-start.19 = (bf16[16,512]{1,0:T(8,128)(2,1)S(1)}, bf16[16,512]{1,0:T(8,128)(2,1)S(1)}, u32[]{:S(2)}, u32[]{:S(2)}) collective-permute-start(bf16[16,512]{1,0:T(8,128)(2,1)S(1)} %get-tuple-element.148), channel_id=1, source_target_pairs={{0,8},{1,9},{2,10},{3,11},{4,12},{5,13},{6,14},{7,15},{8,0},{9,1},... | collective-permute-start | bytes 49160 | tf_op jit(solution)/shard_map/ppermute | solution.py:231
  44.5 1.9 %local_gradients.1 = (f32[256,512]{1,0:T(8,128)S(1)}, f32[64,512]{1,0:T(8,128)}, bf16[256,512]{1,0:T(8,128)(2,1)}) custom-call(bf16[256,512]{1,0:T(8,128)(2,1)S(1)} %copy-done.4, f32[400,512]{1,0:T(8,128)S(1)} %get-tuple-element.135.refs_1_, bf16[256,512]{1,0:T(8,128)(2,1)S(1)} %copy-done.5, bf16[400,512]{1,0:T(8,128)(2,1)S(1)} %get-tuple-element.136.refs_3_, ...), custom_call_target="tpu_custom_call" | custom-call | flops 1677721600 | bytes 12042240 | tf_op jit(solution)/shard_map/local_gradients/pallas_call | solution.py:172
  46.5 0.9 %collective-permute-done.19.refs_5_ = bf16[16,512]{1,0:T(8,128)(2,1)S(1)} collective-permute-done((bf16[16,512]{1,0:T(8,128)(2,1)S(1)}, bf16[16,512]{1,0:T(8,128)(2,1)S(1)}, u32[]{:S(2)}, u32[]{:S(2)}) %collective-permute-start.19) | collective-permute-done | bytes 16416 | tf_op jit(solution)/shard_map/ppermute | solution.py:231
  47.4 1.0 %add_returned.1 = f32[256,512]{1,0:T(8,128)} custom-call(bf16[32,512]{1,0:T(8,128)(2,1)S(1)} %collective-permute-done.14.refs_1_.refs_0_, bf16[32,512]{1,0:T(8,128)(2,1)S(1)} %collective-permute-done.15.refs_2_.refs_1_, bf16[16,512]{1,0:T(8,128)(2,1)S(1)} %collective-permute-done.16.refs_2_, bf16[16,512]{1,0:T(8,128)(2,1)S(1)} %collective-permute-done.17.refs_3_, ...), custom_call_target="tpu_custom_call" | custom-call | tf_op jit(solution)/shard_map/add_returned/pallas_call | solution.py:946
  (65 shorter events, 1.0 us)
Async XLA Ops:
  2.1 11.4 %copy-start = (bf16[1536,512]{1,0:T(8,128)(2,1)S(1)}, bf16[1536,512]{1,0:T(8,128)(2,1)}, u32[]{:S(2)}) copy-start(bf16[1536,512]{1,0:T(8,128)(2,1)} %refs_12_.3) | copy-start | bytes 4718596
  2.1 11.4 %copy-start.1 = (bf16[1536,512]{1,0:T(8,128)(2,1)S(1)}, bf16[1536,512]{1,0:T(8,128)(2,1)}, u32[]{:S(2)}) copy-start(bf16[1536,512]{1,0:T(8,128)(2,1)} %refs_14_.7) | copy-start | bytes 4718596
  2.1 11.4 %copy-start.2 = (bf16[1024,512]{1,0:T(8,128)(2,1)S(1)}, bf16[1024,512]{1,0:T(8,128)(2,1)}, u32[]{:S(2)}) copy-start(bf16[1024,512]{1,0:T(8,128)(2,1)} %refs_13_.5) | copy-start | bytes 3145732
  2.3 9.6 %collective-permute-start = (bf16[32,1024]{1,0:T(8,128)(2,1)S(1)}, bf16[32,1024]{1,0:T(8,128)(2,1)S(1)}, u32[]{:S(2)}, u32[]{:S(2)}) collective-permute-start(bf16[32,1024]{1,0:T(8,128)(2,1)S(1)} %get-tuple-element.86), channel_id=1, source_target_pairs={{0,4},{1,5},{2,6},{3,7},{4,0},{5,1},{6,2},{7,3},{8,12},{9,13},{10,... | collective-permute-start | bytes 196616 | tf_op jit(solution)/shard_map/ppermute | solution.py:231
  5.4 6.9 %collective-permute-start.1 = (bf16[32,1024]{1,0:T(8,128)(2,1)S(1)}, bf16[32,1024]{1,0:T(8,128)(2,1)S(1)}, u32[]{:S(2)}, u32[]{:S(2)}) collective-permute-start(bf16[32,1024]{1,0:T(8,128)(2,1)S(1)} %get-tuple-element.87), channel_id=1, source_target_pairs={{0,12},{1,13},{2,14},{3,15},{4,8},{5,9},{6,10},{7,11},{8,4},{9,5},... | collective-permute-start | bytes 196616 | tf_op jit(solution)/shard_map/ppermute | solution.py:231
  7.9 7.7 %collective-permute-start.2 = (bf16[16,1024]{1,0:T(8,128)(2,1)S(1)}, bf16[16,1024]{1,0:T(8,128)(2,1)S(1)}, u32[]{:S(2)}, u32[]{:S(2)}) collective-permute-start(bf16[16,1024]{1,0:T(8,128)(2,1)S(1)} %get-tuple-element.88), channel_id=1, source_target_pairs={{0,3},{1,14},{2,5},{3,0},{4,7},{5,2},{6,9},{7,4},{8,11},{9,6},{10,... | collective-permute-start | bytes 98312 | tf_op jit(solution)/shard_map/ppermute | solution.py:231
  8.3 7.3 %collective-permute-start.3 = (bf16[16,1024]{1,0:T(8,128)(2,1)S(1)}, bf16[16,1024]{1,0:T(8,128)(2,1)S(1)}, u32[]{:S(2)}, u32[]{:S(2)}) collective-permute-start(bf16[16,1024]{1,0:T(8,128)(2,1)S(1)} %get-tuple-element.89), channel_id=1, source_target_pairs={{0,11},{1,6},{2,13},{3,8},{4,15},{5,10},{6,1},{7,12},{8,3},{9,14},... | collective-permute-start | bytes 98312 | tf_op jit(solution)/shard_map/ppermute | solution.py:231
  9.2 6.4 %collective-permute-start.4 = (bf16[16,1024]{1,0:T(8,128)(2,1)S(1)}, bf16[16,1024]{1,0:T(8,128)(2,1)S(1)}, u32[]{:S(2)}, u32[]{:S(2)}) collective-permute-start(bf16[16,1024]{1,0:T(8,128)(2,1)S(1)} %get-tuple-element.90), channel_id=1, source_target_pairs={{0,15},{1,2},{2,1},{3,4},{4,3},{5,6},{6,5},{7,8},{8,7},{9,10},{10,... | collective-permute-start | bytes 98312 | tf_op jit(solution)/shard_map/ppermute | solution.py:231
  12.0 5.2 %collective-permute-start.5 = (bf16[16,1024]{1,0:T(8,128)(2,1)S(1)}, bf16[16,1024]{1,0:T(8,128)(2,1)S(1)}, u32[]{:S(2)}, u32[]{:S(2)}) collective-permute-start(bf16[16,1024]{1,0:T(8,128)(2,1)S(1)} %get-tuple-element.91), channel_id=1, source_target_pairs={{0,8},{1,9},{2,10},{3,11},{4,12},{5,13},{6,14},{7,15},{8,0},{9,1},... | collective-permute-start | bytes 98312 | tf_op jit(solution)/shard_map/ppermute | solution.py:231
  12.3 4.8 %collective-permute-start.6 = (bf16[48,1024]{1,0:T(8,128)(2,1)S(1)}, bf16[48,1024]{1,0:T(8,128)(2,1)S(1)}, u32[]{:S(2)}, u32[]{:S(2)}) collective-permute-start(bf16[48,1024]{1,0:T(8,128)(2,1)S(1)} %lay_together.3), channel_id=1, source_target_pairs={{0,1},{1,0},{2,3},{3,2},{4,5},{5,4},{6,7},{7,6},{8,9},{9,8},{10,11... | collective-permute-start | bytes 294920 | tf_op jit(solution)/shard_map/ppermute | solution.py:231
  19.9 6.9 %collective-permute-start.7 = (bf16[32,1024]{1,0:T(8,128)(2,1)S(1)}, bf16[32,1024]{1,0:T(8,128)(2,1)S(1)}, u32[]{:S(2)}, u32[]{:S(2)}) collective-permute-start(bf16[32,1024]{1,0:T(8,128)(2,1)S(1)} %get-tuple-element.103), channel_id=1, source_target_pairs={{0,12},{1,13},{2,14},{3,15},{4,8},{5,9},{6,10},{7,11},{8,4},{9,5},... | collective-permute-start | bytes 196616 | tf_op jit(solution)/shard_map/ppermute | solution.py:231
  21.8 5.0 %collective-permute-start.8 = (bf16[32,1024]{1,0:T(8,128)(2,1)S(1)}, bf16[32,1024]{1,0:T(8,128)(2,1)S(1)}, u32[]{:S(2)}, u32[]{:S(2)}) collective-permute-start(bf16[32,1024]{1,0:T(8,128)(2,1)S(1)} %get-tuple-element.104), channel_id=1, source_target_pairs={{0,4},{1,5},{2,6},{3,7},{4,0},{5,1},{6,2},{7,3},{8,12},{9,13},{10,... | collective-permute-start | bytes 196616 | tf_op jit(solution)/shard_map/ppermute | solution.py:231
  21.8 8.1 %collective-permute-start.10 = (bf16[16,1024]{1,0:T(8,128)(2,1)S(1)}, bf16[16,1024]{1,0:T(8,128)(2,1)S(1)}, u32[]{:S(2)}, u32[]{:S(2)}) collective-permute-start(bf16[16,1024]{1,0:T(8,128)(2,1)S(1)} %get-tuple-element.106), channel_id=1, source_target_pairs={{0,3},{1,14},{2,5},{3,0},{4,7},{5,2},{6,9},{7,4},{8,11},{9,6},{10,... | collective-permute-start | bytes 98312 | tf_op jit(solution)/shard_map/ppermute | solution.py:231
  21.8 8.1 %collective-permute-start.11 = (bf16[16,1024]{1,0:T(8,128)(2,1)S(1)}, bf16[16,1024]{1,0:T(8,128)(2,1)S(1)}, u32[]{:S(2)}, u32[]{:S(2)}) collective-permute-start(bf16[16,1024]{1,0:T(8,128)(2,1)S(1)} %get-tuple-element.107), channel_id=1, source_target_pairs={{0,11},{1,6},{2,13},{3,8},{4,15},{5,10},{6,1},{7,12},{8,3},{9,14},... | collective-permute-start | bytes 98312 | tf_op jit(solution)/shard_map/ppermute | solution.py:231
  25.5 6.0 %collective-permute-start.12 = (bf16[16,1024]{1,0:T(8,128)(2,1)S(1)}, bf16[16,1024]{1,0:T(8,128)(2,1)S(1)}, u32[]{:S(2)}, u32[]{:S(2)}) collective-permute-start(bf16[16,1024]{1,0:T(8,128)(2,1)S(1)} %get-tuple-element.108), channel_id=1, source_target_pairs={{0,15},{1,2},{2,1},{3,4},{4,3},{5,6},{6,5},{7,8},{8,7},{9,10},{10,... | collective-permute-start | bytes 98312 | tf_op jit(solution)/shard_map/ppermute | solution.py:231
  26.8 4.8 %collective-permute-start.9 = (bf16[16,1024]{1,0:T(8,128)(2,1)S(1)}, bf16[16,1024]{1,0:T(8,128)(2,1)S(1)}, u32[]{:S(2)}, u32[]{:S(2)}) collective-permute-start(bf16[16,1024]{1,0:T(8,128)(2,1)S(1)} %get-tuple-element.105), channel_id=1, source_target_pairs={{0,8},{1,9},{2,10},{3,11},{4,12},{5,13},{6,14},{7,15},{8,0},{9,1},... | collective-permute-start | bytes 98312 | tf_op jit(solution)/shard_map/ppermute | solution.py:231
  26.9 4.8 %collective-permute-start.13 = (bf16[48,1024]{1,0:T(8,128)(2,1)S(1)}, bf16[48,1024]{1,0:T(8,128)(2,1)S(1)}, u32[]{:S(2)}, u32[]{:S(2)}) collective-permute-start(bf16[48,1024]{1,0:T(8,128)(2,1)S(1)} %lay_together.4), channel_id=1, source_target_pairs={{0,1},{1,0},{2,3},{3,2},{4,5},{5,4},{6,7},{7,6},{8,9},{9,8},{10,11... | collective-permute-start | bytes 294920 | tf_op jit(solution)/shard_map/ppermute | solution.py:231
  36.2 6.4 %collective-permute-start.14 = (bf16[32,512]{1,0:T(8,128)(2,1)S(1)}, bf16[32,512]{1,0:T(8,128)(2,1)S(1)}, u32[]{:S(2)}, u32[]{:S(2)}) collective-permute-start(bf16[32,512]{1,0:T(8,128)(2,1)S(1)} %get-tuple-element.143), channel_id=1, source_target_pairs={{0,12},{1,13},{2,14},{3,15},{4,8},{5,9},{6,10},{7,11},{8,4},{9,5},... | collective-permute-start | bytes 98312 | tf_op jit(solution)/shard_map/ppermute | solution.py:231
  37.9 6.6 %collective-permute-start.15 = (bf16[32,512]{1,0:T(8,128)(2,1)S(1)}, bf16[32,512]{1,0:T(8,128)(2,1)S(1)}, u32[]{:S(2)}, u32[]{:S(2)}) collective-permute-start(bf16[32,512]{1,0:T(8,128)(2,1)S(1)} %get-tuple-element.144), channel_id=1, source_target_pairs={{0,4},{1,5},{2,6},{3,7},{4,0},{5,1},{6,2},{7,3},{8,12},{9,13},{10,... | collective-permute-start | bytes 98312 | tf_op jit(solution)/shard_map/ppermute | solution.py:231
  38.0 8.4 %collective-permute-start.16 = (bf16[16,512]{1,0:T(8,128)(2,1)S(1)}, bf16[16,512]{1,0:T(8,128)(2,1)S(1)}, u32[]{:S(2)}, u32[]{:S(2)}) collective-permute-start(bf16[16,512]{1,0:T(8,128)(2,1)S(1)} %get-tuple-element.145), channel_id=1, source_target_pairs={{0,15},{1,2},{2,1},{3,4},{4,3},{5,6},{6,5},{7,8},{8,7},{9,10},{10,... | collective-permute-start | bytes 49160 | tf_op jit(solution)/shard_map/ppermute | solution.py:231
  40.3 6.1 %collective-permute-start.17 = (bf16[16,512]{1,0:T(8,128)(2,1)S(1)}, bf16[16,512]{1,0:T(8,128)(2,1)S(1)}, u32[]{:S(2)}, u32[]{:S(2)}) collective-permute-start(bf16[16,512]{1,0:T(8,128)(2,1)S(1)} %get-tuple-element.146), channel_id=1, source_target_pairs={{0,3},{1,14},{2,5},{3,0},{4,7},{5,2},{6,9},{7,4},{8,11},{9,6},{10,... | collective-permute-start | bytes 49160 | tf_op jit(solution)/shard_map/ppermute | solution.py:231
  41.1 5.4 %collective-permute-start.18 = (bf16[16,512]{1,0:T(8,128)(2,1)S(1)}, bf16[16,512]{1,0:T(8,128)(2,1)S(1)}, u32[]{:S(2)}, u32[]{:S(2)}) collective-permute-start(bf16[16,512]{1,0:T(8,128)(2,1)S(1)} %get-tuple-element.147), channel_id=1, source_target_pairs={{0,11},{1,6},{2,13},{3,8},{4,15},{5,10},{6,1},{7,12},{8,3},{9,14},... | collective-permute-start | bytes 49160 | tf_op jit(solution)/shard_map/ppermute | solution.py:231
  42.6 4.9 %collective-permute-start.19 = (bf16[16,512]{1,0:T(8,128)(2,1)S(1)}, bf16[16,512]{1,0:T(8,128)(2,1)S(1)}, u32[]{:S(2)}, u32[]{:S(2)}) collective-permute-start(bf16[16,512]{1,0:T(8,128)(2,1)S(1)} %get-tuple-element.148), channel_id=1, source_target_pairs={{0,8},{1,9},{2,10},{3,11},{4,12},{5,13},{6,14},{7,15},{8,0},{9,1},... | collective-permute-start | bytes 49160 | tf_op jit(solution)/shard_map/ppermute | solution.py:231
  44.5 3.0 %collective-permute-start.20 = (bf16[48,512]{1,0:T(8,128)(2,1)S(1)}, bf16[48,512]{1,0:T(8,128)(2,1)S(1)}, u32[]{:S(2)}, u32[]{:S(2)}) collective-permute-start(bf16[48,512]{1,0:T(8,128)(2,1)S(1)} %lay_together.5), channel_id=1, source_target_pairs={{0,1},{1,0},{2,3},{3,2},{4,5},{5,4},{6,7},{7,6},{8,9},{9,8},{10,11... | collective-permute-start | bytes 147464 | tf_op jit(solution)/shard_map/ppermute | solution.py:231
  (15 other events, 164.1 us)

commit v22 on v21

--- a/solution.py
+++ b/solution.py
@@ -230,7 +230,7 @@
         pairs = [(s, (s + rows[s // TW % 2][s % 2]) % peer_count) for s in peers]
         return lax.ppermute(part, "tile", pairs)
 
-    steady = ("late", "early", "opposite", "ahead", "five", "behind", "own")
+    steady = ("late", "early", "opposite", "behind", "ahead", "five", "own")
     closing = ("late", "early", "behind", "ahead", "five", "opposite", "own")
     staggered = ("early", "late", "ahead", "five", "behind", "opposite", "own")
     arrived_count = 7
@@ -278,7 +278,7 @@
         def by_parity(even, odd_one):
             return jnp.where(odd, message(odd_one), message(even))
 
-        late_pair, early_pair, opposite, ahead_three, five_off, behind_one, own_chip = [
+        late_pair, early_pair, opposite, behind_one, ahead_three, five_off, own_chip = [
             refs[name] for name in steady
         ]
         first, second = slice(0, width), slice(width, 2 * width)
@@ -297,7 +297,7 @@
         odd, odd_row = place_bits()
         passed = refs[-1]
         refs = dict(zip([name for name in order if name != "own"], refs))
-        late_pair, early_pair, opposite, ahead_three, five_off, behind_one = [
+        late_pair, early_pair, opposite, behind_one, ahead_three, five_off = [
             refs[name] for name in steady if name != "own"
         ]
         first, second = slice(0, width), slice(width, 2 * width)

time: 48.6 us -> 48 us (0.988)
  transfers between devices with their start and end apart: 21 -> 21, of which waited for: 4 -> 6; matrix products, arithmetic and copies ran while one was open for 0% -> 0% of each run, Pallas kernels for 14% -> 14%
where the time goes in v22:
time: 48 us; the launch traced here: 47.8 us
  starting transfers between devices  26 us (54%)
  Pallas kernels  16.7 us (35%)
  waiting for transfers between devices  4.11 us (9%)
  between operations  0.98 us (2%)
    ppermute x21, starting transfers between devices, permute(): return lax.ppermute(part, 'tile', pairs)  26 us
    pallas_call x10, Pallas kernels, call(): pl.pallas_call(kernel, name=name, in_specs=specs, out_specs=[pl.BlockSpec...  15.7 us
    ppermute x21, waiting for transfers between devices, permute(): return lax.ppermute(part, 'tile', pairs)  4.11 us
    pallas_call x1, Pallas kernels, per_device(): pl.pallas_call(finish, name='add_returned', in_specs=[pl.BlockSpec(memory...  0.99 us
  transfers between devices with their start and end apart: 21, of which 6 were waited for; matrix products, arithmetic and copies ran while one was open for 0% of the time, Pallas kernels for 14%

profile of v22, /device:TPU:0, one launch (start us, length us, event | category | flops | bytes accessed | tf_op | source)
XLA Modules:
  0.0 47.8 jit_solution(14953839654420166915)
XLA Ops:
  0.6 1.4 %pack_rows.1 = (bf16[256,256]{1,0:T(8,128)(2,1)S(1)}, bf16[32,1024]{1,0:T(8,128)(2,1)S(1)}, bf16[32,1024]{1,0:T(8,128)(2,1)S(1)}, bf16[16,1024]{1,0:T(8,128)(2,1...) custom-call(s32[9,16]{1,0:T(8,128)} %refs_0_.2, ...), custom_call_target="tpu_custom_call" | custom-call | flops 75497472 | bytes 950884 | tf_op jit(solution)/shard_map/pack_rows/pallas_call | solution.py:172
  2.3 3.1 %collective-permute-start = (bf16[32,1024]{1,0:T(8,128)(2,1)S(1)}, bf16[32,1024]{1,0:T(8,128)(2,1)S(1)}, u32[]{:S(2)}, u32[]{:S(2)}) collective-permute-start(bf16[32,1024]{1,0:T(8,128)(2,1)S(1)} %get-tuple-element.86), channel_id=1, source_target_pairs={{0,4},{1,5},{2,6},{3,7},{4,0},{5,1},{6,2},{7,3},{8,12},{9,13},{10,... | collective-permute-start | bytes 196616 | tf_op jit(solution)/shard_map/ppermute | solution.py:231
  5.4 2.5 %collective-permute-start.1 = (bf16[32,1024]{1,0:T(8,128)(2,1)S(1)}, bf16[32,1024]{1,0:T(8,128)(2,1)S(1)}, u32[]{:S(2)}, u32[]{:S(2)}) collective-permute-start(bf16[32,1024]{1,0:T(8,128)(2,1)S(1)} %get-tuple-element.87), channel_id=1, source_target_pairs={{0,12},{1,13},{2,14},{3,15},{4,8},{5,9},{6,10},{7,11},{8,4},{9,5},... | collective-permute-start | bytes 196616 | tf_op jit(solution)/shard_map/ppermute | solution.py:231
  8.3 0.9 %collective-permute-start.3 = (bf16[16,1024]{1,0:T(8,128)(2,1)S(1)}, bf16[16,1024]{1,0:T(8,128)(2,1)S(1)}, u32[]{:S(2)}, u32[]{:S(2)}) collective-permute-start(bf16[16,1024]{1,0:T(8,128)(2,1)S(1)} %get-tuple-element.89), channel_id=1, source_target_pairs={{0,11},{1,6},{2,13},{3,8},{4,15},{5,10},{6,1},{7,12},{8,3},{9,14},... | collective-permute-start | bytes 98312 | tf_op jit(solution)/shard_map/ppermute | solution.py:231
  9.2 2.8 %collective-permute-start.4 = (bf16[16,1024]{1,0:T(8,128)(2,1)S(1)}, bf16[16,1024]{1,0:T(8,128)(2,1)S(1)}, u32[]{:S(2)}, u32[]{:S(2)}) collective-permute-start(bf16[16,1024]{1,0:T(8,128)(2,1)S(1)} %get-tuple-element.90), channel_id=1, source_target_pairs={{0,15},{1,2},{2,1},{3,4},{4,3},{5,6},{6,5},{7,8},{8,7},{9,10},{10,... | collective-permute-start | bytes 98312 | tf_op jit(solution)/shard_map/ppermute | solution.py:231
  12.3 1.1 %collective-permute-start.6 = (bf16[48,1024]{1,0:T(8,128)(2,1)S(1)}, bf16[48,1024]{1,0:T(8,128)(2,1)S(1)}, u32[]{:S(2)}, u32[]{:S(2)}) collective-permute-start(bf16[48,1024]{1,0:T(8,128)(2,1)S(1)} %lay_together.3), channel_id=1, source_target_pairs={{0,1},{1,0},{2,3},{3,2},{4,5},{5,4},{6,7},{7,6},{8,9},{9,8},{10,11... | collective-permute-start | bytes 294920 | tf_op jit(solution)/shard_map/ppermute | solution.py:231
  13.6 2.0 %local_products.1 = (f32[384,512]{1,0:T(8,128)S(1)}, f32[768,512]{1,0:T(8,128)S(1)}, f32[64,512]{1,0:T(8,128)S(1)}, bf16[384,512]{1,0:T(8,128)(2,1)S(1)}, bf16[5...) custom-call(bf16[256,256]{1,0:T(8,128)(2,1)S(1)} %get-tuple-element., ...), custom_call_target="tpu_custom_call" | custom-call | flops 1275068416 | bytes 14279680 | tf_op jit(solution)/shard_map/local_products/pallas_call | solution.py:172
  15.6 1.5 %collective-permute-done.5.refs_5_ = bf16[16,1024]{1,0:T(8,128)(2,1)S(1)} collective-permute-done((bf16[16,1024]{1,0:T(8,128)(2,1)S(1)}, bf16[16,1024]{1,0:T(8,128)(2,1)S(1)}, u32[]{:S(2)}, u32[]{:S(2)}) %collective-permute-start.5) | collective-permute-done | bytes 32800 | tf_op jit(solution)/shard_map/ppermute | solution.py:231
  17.1 2.7 %edges_forward.1 = (bf16[32,1024]{1,0:T(8,128)(2,1)S(1)}, bf16[32,1024]{1,0:T(8,128)(2,1)S(1)}, bf16[16,1024]{1,0:T(8,128)(2,1)S(1)}, bf16[16,1024]{1,0:T(8,128)...) custom-call(bf16[32,1024]{1,0:T(8,128)(2,1)S(1)} %collective-permute, ...), custom_call_target="tpu_custom_call" | custom-call | flops 1207959552 | bytes 16667392 | tf_op jit(solution)/shard_map/edges_forward/pallas_call | solution.py:172
  19.9 1.9 %collective-permute-start.7 = (bf16[32,1024]{1,0:T(8,128)(2,1)S(1)}, bf16[32,1024]{1,0:T(8,128)(2,1)S(1)}, u32[]{:S(2)}, u32[]{:S(2)}) collective-permute-start(bf16[32,1024]{1,0:T(8,128)(2,1)S(1)} %get-tuple-element.103), channel_id=1, source_target_pairs={{0,12},{1,13},{2,14},{3,15},{4,8},{5,9},{6,10},{7,11},{8,4},{9,5},... | collective-permute-start | bytes 196616 | tf_op jit(solution)/shard_map/ppermute | solution.py:231
  21.8 0.6 %collective-permute-start.10 = (bf16[16,1024]{1,0:T(8,128)(2,1)S(1)}, bf16[16,1024]{1,0:T(8,128)(2,1)S(1)}, u32[]{:S(2)}, u32[]{:S(2)}) collective-permute-start(bf16[16,1024]{1,0:T(8,128)(2,1)S(1)} %get-tuple-element.106), channel_id=1, source_target_pairs={{0,15},{1,2},{2,1},{3,4},{4,3},{5,6},{6,5},{7,8},{8,7},{9,10},{10,... | collective-permute-start | bytes 98312 | tf_op jit(solution)/shard_map/ppermute | solution.py:231
  22.4 2.6 %collective-permute-start.11 = (bf16[16,1024]{1,0:T(8,128)(2,1)S(1)}, bf16[16,1024]{1,0:T(8,128)(2,1)S(1)}, u32[]{:S(2)}, u32[]{:S(2)}) collective-permute-start(bf16[16,1024]{1,0:T(8,128)(2,1)S(1)} %get-tuple-element.107), channel_id=1, source_target_pairs={{0,3},{1,14},{2,5},{3,0},{4,7},{5,2},{6,9},{7,4},{8,11},{9,6},{10,... | collective-permute-start | bytes 98312 | tf_op jit(solution)/shard_map/ppermute | solution.py:231
  25.5 0.7 %collective-permute-done.7.refs_1_.refs_0_ = bf16[32,1024]{1,0:T(8,128)(2,1)S(1)} collective-permute-done((bf16[32,1024]{1,0:T(8,128)(2,1)S(1)}, bf16[32,1024]{1,0:T(8,128)(2,1)S(1)}, u32[]{:S(2)}, u32[]{:S(2)}) %collective-permute-start.7) | collective-permute-done | bytes 65568 | tf_op jit(solution)/shard_map/ppermute | solution.py:231
  26.2 1.2 %collective-permute-start.9 = (bf16[16,1024]{1,0:T(8,128)(2,1)S(1)}, bf16[16,1024]{1,0:T(8,128)(2,1)S(1)}, u32[]{:S(2)}, u32[]{:S(2)}) collective-permute-start(bf16[16,1024]{1,0:T(8,128)(2,1)S(1)} %get-tuple-element.105), channel_id=1, source_target_pairs={{0,8},{1,9},{2,10},{3,11},{4,12},{5,13},{6,14},{7,15},{8,0},{9,1},... | collective-permute-start | bytes 98312 | tf_op jit(solution)/shard_map/ppermute | solution.py:231
  27.5 2.9 %slopes_and_nodes.1 = (f32[256,512]{1,0:T(8,128)S(1)}, f32[400,512]{1,0:T(8,128)S(1)}, bf16[400,512]{1,0:T(8,128)(2,1)S(1)}, f32[400,512]{1,0:T(8,128)S(1)}, bf1...) custom-call(bf16[32,1024]{1,0:T(8,128)(2,1)S(1)} %collective-permute, ...), custom_call_target="tpu_custom_call" | custom-call | flops 1677721600 | bytes 17809408 | tf_op jit(solution)/shard_map/slopes_and_nodes/pallas_call | solution.py:172
  30.4 0.6 %collective-permute-done.12.refs_5_ = bf16[16,1024]{1,0:T(8,128)(2,1)S(1)} collective-permute-done((bf16[16,1024]{1,0:T(8,128)(2,1)S(1)}, bf16[16,1024]{1,0:T(8,128)(2,1)S(1)}, u32[]{:S(2)}, u32[]{:S(2)}) %collective-permute-start.12) | collective-permute-done | bytes 32800 | tf_op jit(solution)/shard_map/ppermute | solution.py:231
  31.4 4.6 %edges_backward.1 = (bf16[32,512]{1,0:T(8,128)(2,1)S(1)}, bf16[32,512]{1,0:T(8,128)(2,1)S(1)}, bf16[16,512]{1,0:T(8,128)(2,1)S(1)}, bf16[16,512]{1,0:T(8,128)(2,...) custom-call(bf16[32,1024]{1,0:T(8,128)(2,1)S(1)} %collective-permute, ...), custom_call_target="tpu_custom_call" | custom-call | flops 2449473536 | bytes 19813120 | tf_op jit(solution)/shard_map/edges_backward/pallas_call | solution.py:172
  35.9 2.3 %collective-permute-start.14 = (bf16[32,512]{1,0:T(8,128)(2,1)S(1)}, bf16[32,512]{1,0:T(8,128)(2,1)S(1)}, u32[]{:S(2)}, u32[]{:S(2)}) collective-permute-start(bf16[32,512]{1,0:T(8,128)(2,1)S(1)} %get-tuple-element.143), channel_id=1, source_target_pairs={{0,12},{1,13},{2,14},{3,15},{4,8},{5,9},{6,10},{7,11},{8,4},{9,5},... | collective-permute-start | bytes 98312 | tf_op jit(solution)/shard_map/ppermute | solution.py:231
  38.3 1.4 %collective-permute-start.16 = (bf16[16,512]{1,0:T(8,128)(2,1)S(1)}, bf16[16,512]{1,0:T(8,128)(2,1)S(1)}, u32[]{:S(2)}, u32[]{:S(2)}) collective-permute-start(bf16[16,512]{1,0:T(8,128)(2,1)S(1)} %get-tuple-element.145), channel_id=1, source_target_pairs={{0,15},{1,2},{2,1},{3,4},{4,3},{5,6},{6,5},{7,8},{8,7},{9,10},{10,... | collective-permute-start | bytes 49160 | tf_op jit(solution)/shard_map/ppermute | solution.py:231
  39.6 1.9 %collective-permute-start.17 = (bf16[16,512]{1,0:T(8,128)(2,1)S(1)}, bf16[16,512]{1,0:T(8,128)(2,1)S(1)}, u32[]{:S(2)}, u32[]{:S(2)}) collective-permute-start(bf16[16,512]{1,0:T(8,128)(2,1)S(1)} %get-tuple-element.146), channel_id=1, source_target_pairs={{0,3},{1,14},{2,5},{3,0},{4,7},{5,2},{6,9},{7,4},{8,11},{9,6},{10,... | collective-permute-start | bytes 49160 | tf_op jit(solution)/shard_map/ppermute | solution.py:231
  41.9 1.9 %collective-permute-start.19 = (bf16[16,512]{1,0:T(8,128)(2,1)S(1)}, bf16[16,512]{1,0:T(8,128)(2,1)S(1)}, u32[]{:S(2)}, u32[]{:S(2)}) collective-permute-start(bf16[16,512]{1,0:T(8,128)(2,1)S(1)} %get-tuple-element.148), channel_id=1, source_target_pairs={{0,8},{1,9},{2,10},{3,11},{4,12},{5,13},{6,14},{7,15},{8,0},{9,1},... | collective-permute-start | bytes 49160 | tf_op jit(solution)/shard_map/ppermute | solution.py:231
  43.9 1.9 %local_gradients.1 = (f32[256,512]{1,0:T(8,128)S(1)}, f32[64,512]{1,0:T(8,128)}, bf16[256,512]{1,0:T(8,128)(2,1)}) custom-call(bf16[256,512]{1,0:T(8,128)(2,1)S(1)} %copy-done.4, f32[400,512]{1,0:T(8,128)S(1)} %get-tuple-element.135.refs_1_, bf16[256,512]{1,0:T(8,128)(2,1)S(1)} %copy-done.5, bf16[400,512]{1,0:T(8,128)(2,1)S(1)} %get-tuple-element.136.refs_3_, ...), custom_call_target="tpu_custom_call" | custom-call | flops 1677721600 | bytes 12042240 | tf_op jit(solution)/shard_map/local_gradients/pallas_call | solution.py:172
  45.9 0.6 %collective-permute-done.18.refs_4_ = bf16[16,512]{1,0:T(8,128)(2,1)S(1)} collective-permute-done((bf16[16,512]{1,0:T(8,128)(2,1)S(1)}, bf16[16,512]{1,0:T(8,128)(2,1)S(1)}, u32[]{:S(2)}, u32[]{:S(2)}) %collective-permute-start.18) | collective-permute-done | bytes 16416 | tf_op jit(solution)/shard_map/ppermute | solution.py:231
  46.8 1.0 %add_returned.1 = f32[256,512]{1,0:T(8,128)} custom-call(bf16[32,512]{1,0:T(8,128)(2,1)S(1)} %collective-permute-done.14.refs_1_.refs_0_, bf16[32,512]{1,0:T(8,128)(2,1)S(1)} %collective-permute-done.15.refs_2_.refs_1_, bf16[16,512]{1,0:T(8,128)(2,1)S(1)} %collective-permute-done.16.refs_2_, bf16[16,512]{1,0:T(8,128)(2,1)S(1)} %collective-permute-done.17.refs_3_, ...), custom_call_target="tpu_custom_call" | custom-call | tf_op jit(solution)/shard_map/add_returned/pallas_call | solution.py:946
  (65 shorter events, 2.8 us)
Async XLA Ops:
  2.1 11.4 %copy-start = (bf16[1536,512]{1,0:T(8,128)(2,1)S(1)}, bf16[1536,512]{1,0:T(8,128)(2,1)}, u32[]{:S(2)}) copy-start(bf16[1536,512]{1,0:T(8,128)(2,1)} %refs_12_.3) | copy-start | bytes 4718596
  2.1 11.4 %copy-start.1 = (bf16[1536,512]{1,0:T(8,128)(2,1)S(1)}, bf16[1536,512]{1,0:T(8,128)(2,1)}, u32[]{:S(2)}) copy-start(bf16[1536,512]{1,0:T(8,128)(2,1)} %refs_14_.7) | copy-start | bytes 4718596
  2.1 11.4 %copy-start.2 = (bf16[1024,512]{1,0:T(8,128)(2,1)S(1)}, bf16[1024,512]{1,0:T(8,128)(2,1)}, u32[]{:S(2)}) copy-start(bf16[1024,512]{1,0:T(8,128)(2,1)} %refs_13_.5) | copy-start | bytes 3145732
  2.3 9.6 %collective-permute-start = (bf16[32,1024]{1,0:T(8,128)(2,1)S(1)}, bf16[32,1024]{1,0:T(8,128)(2,1)S(1)}, u32[]{:S(2)}, u32[]{:S(2)}) collective-permute-start(bf16[32,1024]{1,0:T(8,128)(2,1)S(1)} %get-tuple-element.86), channel_id=1, source_target_pairs={{0,4},{1,5},{2,6},{3,7},{4,0},{5,1},{6,2},{7,3},{8,12},{9,13},{10,... | collective-permute-start | bytes 196616 | tf_op jit(solution)/shard_map/ppermute | solution.py:231
  5.4 6.9 %collective-permute-start.1 = (bf16[32,1024]{1,0:T(8,128)(2,1)S(1)}, bf16[32,1024]{1,0:T(8,128)(2,1)S(1)}, u32[]{:S(2)}, u32[]{:S(2)}) collective-permute-start(bf16[32,1024]{1,0:T(8,128)(2,1)S(1)} %get-tuple-element.87), channel_id=1, source_target_pairs={{0,12},{1,13},{2,14},{3,15},{4,8},{5,9},{6,10},{7,11},{8,4},{9,5},... | collective-permute-start | bytes 196616 | tf_op jit(solution)/shard_map/ppermute | solution.py:231
  7.9 7.7 %collective-permute-start.2 = (bf16[16,1024]{1,0:T(8,128)(2,1)S(1)}, bf16[16,1024]{1,0:T(8,128)(2,1)S(1)}, u32[]{:S(2)}, u32[]{:S(2)}) collective-permute-start(bf16[16,1024]{1,0:T(8,128)(2,1)S(1)} %get-tuple-element.88), channel_id=1, source_target_pairs={{0,3},{1,14},{2,5},{3,0},{4,7},{5,2},{6,9},{7,4},{8,11},{9,6},{10,... | collective-permute-start | bytes 98312 | tf_op jit(solution)/shard_map/ppermute | solution.py:231
  8.3 7.3 %collective-permute-start.3 = (bf16[16,1024]{1,0:T(8,128)(2,1)S(1)}, bf16[16,1024]{1,0:T(8,128)(2,1)S(1)}, u32[]{:S(2)}, u32[]{:S(2)}) collective-permute-start(bf16[16,1024]{1,0:T(8,128)(2,1)S(1)} %get-tuple-element.89), channel_id=1, source_target_pairs={{0,11},{1,6},{2,13},{3,8},{4,15},{5,10},{6,1},{7,12},{8,3},{9,14},... | collective-permute-start | bytes 98312 | tf_op jit(solution)/shard_map/ppermute | solution.py:231
  9.2 6.4 %collective-permute-start.4 = (bf16[16,1024]{1,0:T(8,128)(2,1)S(1)}, bf16[16,1024]{1,0:T(8,128)(2,1)S(1)}, u32[]{:S(2)}, u32[]{:S(2)}) collective-permute-start(bf16[16,1024]{1,0:T(8,128)(2,1)S(1)} %get-tuple-element.90), channel_id=1, source_target_pairs={{0,15},{1,2},{2,1},{3,4},{4,3},{5,6},{6,5},{7,8},{8,7},{9,10},{10,... | collective-permute-start | bytes 98312 | tf_op jit(solution)/shard_map/ppermute | solution.py:231
  12.0 5.2 %collective-permute-start.5 = (bf16[16,1024]{1,0:T(8,128)(2,1)S(1)}, bf16[16,1024]{1,0:T(8,128)(2,1)S(1)}, u32[]{:S(2)}, u32[]{:S(2)}) collective-permute-start(bf16[16,1024]{1,0:T(8,128)(2,1)S(1)} %get-tuple-element.91), channel_id=1, source_target_pairs={{0,8},{1,9},{2,10},{3,11},{4,12},{5,13},{6,14},{7,15},{8,0},{9,1},... | collective-permute-start | bytes 98312 | tf_op jit(solution)/shard_map/ppermute | solution.py:231
  12.3 4.8 %collective-permute-start.6 = (bf16[48,1024]{1,0:T(8,128)(2,1)S(1)}, bf16[48,1024]{1,0:T(8,128)(2,1)S(1)}, u32[]{:S(2)}, u32[]{:S(2)}) collective-permute-start(bf16[48,1024]{1,0:T(8,128)(2,1)S(1)} %lay_together.3), channel_id=1, source_target_pairs={{0,1},{1,0},{2,3},{3,2},{4,5},{5,4},{6,7},{7,6},{8,9},{9,8},{10,11... | collective-permute-start | bytes 294920 | tf_op jit(solution)/shard_map/ppermute | solution.py:231
  19.9 6.3 %collective-permute-start.7 = (bf16[32,1024]{1,0:T(8,128)(2,1)S(1)}, bf16[32,1024]{1,0:T(8,128)(2,1)S(1)}, u32[]{:S(2)}, u32[]{:S(2)}) collective-permute-start(bf16[32,1024]{1,0:T(8,128)(2,1)S(1)} %get-tuple-element.103), channel_id=1, source_target_pairs={{0,12},{1,13},{2,14},{3,15},{4,8},{5,9},{6,10},{7,11},{8,4},{9,5},... | collective-permute-start | bytes 196616 | tf_op jit(solution)/shard_map/ppermute | solution.py:231
  21.8 5.6 %collective-permute-start.8 = (bf16[32,1024]{1,0:T(8,128)(2,1)S(1)}, bf16[32,1024]{1,0:T(8,128)(2,1)S(1)}, u32[]{:S(2)}, u32[]{:S(2)}) collective-permute-start(bf16[32,1024]{1,0:T(8,128)(2,1)S(1)} %get-tuple-element.104), channel_id=1, source_target_pairs={{0,4},{1,5},{2,6},{3,7},{4,0},{5,1},{6,2},{7,3},{8,12},{9,13},{10,... | collective-permute-start | bytes 196616 | tf_op jit(solution)/shard_map/ppermute | solution.py:231
  21.8 8.6 %collective-permute-start.10 = (bf16[16,1024]{1,0:T(8,128)(2,1)S(1)}, bf16[16,1024]{1,0:T(8,128)(2,1)S(1)}, u32[]{:S(2)}, u32[]{:S(2)}) collective-permute-start(bf16[16,1024]{1,0:T(8,128)(2,1)S(1)} %get-tuple-element.106), channel_id=1, source_target_pairs={{0,15},{1,2},{2,1},{3,4},{4,3},{5,6},{6,5},{7,8},{8,7},{9,10},{10,... | collective-permute-start | bytes 98312 | tf_op jit(solution)/shard_map/ppermute | solution.py:231
  22.4 8.0 %collective-permute-start.11 = (bf16[16,1024]{1,0:T(8,128)(2,1)S(1)}, bf16[16,1024]{1,0:T(8,128)(2,1)S(1)}, u32[]{:S(2)}, u32[]{:S(2)}) collective-permute-start(bf16[16,1024]{1,0:T(8,128)(2,1)S(1)} %get-tuple-element.107), channel_id=1, source_target_pairs={{0,3},{1,14},{2,5},{3,0},{4,7},{5,2},{6,9},{7,4},{8,11},{9,6},{10,... | collective-permute-start | bytes 98312 | tf_op jit(solution)/shard_map/ppermute | solution.py:231
  25.0 6.0 %collective-permute-start.12 = (bf16[16,1024]{1,0:T(8,128)(2,1)S(1)}, bf16[16,1024]{1,0:T(8,128)(2,1)S(1)}, u32[]{:S(2)}, u32[]{:S(2)}) collective-permute-start(bf16[16,1024]{1,0:T(8,128)(2,1)S(1)} %get-tuple-element.108), channel_id=1, source_target_pairs={{0,11},{1,6},{2,13},{3,8},{4,15},{5,10},{6,1},{7,12},{8,3},{9,14},... | collective-permute-start | bytes 98312 | tf_op jit(solution)/shard_map/ppermute | solution.py:231
  26.2 5.2 %collective-permute-start.9 = (bf16[16,1024]{1,0:T(8,128)(2,1)S(1)}, bf16[16,1024]{1,0:T(8,128)(2,1)S(1)}, u32[]{:S(2)}, u32[]{:S(2)}) collective-permute-start(bf16[16,1024]{1,0:T(8,128)(2,1)S(1)} %get-tuple-element.105), channel_id=1, source_target_pairs={{0,8},{1,9},{2,10},{3,11},{4,12},{5,13},{6,14},{7,15},{8,0},{9,1},... | collective-permute-start | bytes 98312 | tf_op jit(solution)/shard_map/ppermute | solution.py:231
  27.4 4.0 %collective-permute-start.13 = (bf16[48,1024]{1,0:T(8,128)(2,1)S(1)}, bf16[48,1024]{1,0:T(8,128)(2,1)S(1)}, u32[]{:S(2)}, u32[]{:S(2)}) collective-permute-start(bf16[48,1024]{1,0:T(8,128)(2,1)S(1)} %lay_together.4), channel_id=1, source_target_pairs={{0,1},{1,0},{2,3},{3,2},{4,5},{5,4},{6,7},{7,6},{8,9},{9,8},{10,11... | collective-permute-start | bytes 294920 | tf_op jit(solution)/shard_map/ppermute | solution.py:231
  35.9 6.0 %collective-permute-start.14 = (bf16[32,512]{1,0:T(8,128)(2,1)S(1)}, bf16[32,512]{1,0:T(8,128)(2,1)S(1)}, u32[]{:S(2)}, u32[]{:S(2)}) collective-permute-start(bf16[32,512]{1,0:T(8,128)(2,1)S(1)} %get-tuple-element.143), channel_id=1, source_target_pairs={{0,12},{1,13},{2,14},{3,15},{4,8},{5,9},{6,10},{7,11},{8,4},{9,5},... | collective-permute-start | bytes 98312 | tf_op jit(solution)/shard_map/ppermute | solution.py:231
  38.3 5.6 %collective-permute-start.15 = (bf16[32,512]{1,0:T(8,128)(2,1)S(1)}, bf16[32,512]{1,0:T(8,128)(2,1)S(1)}, u32[]{:S(2)}, u32[]{:S(2)}) collective-permute-start(bf16[32,512]{1,0:T(8,128)(2,1)S(1)} %get-tuple-element.144), channel_id=1, source_target_pairs={{0,4},{1,5},{2,6},{3,7},{4,0},{5,1},{6,2},{7,3},{8,12},{9,13},{10,... | collective-permute-start | bytes 98312 | tf_op jit(solution)/shard_map/ppermute | solution.py:231
  38.3 7.6 %collective-permute-start.16 = (bf16[16,512]{1,0:T(8,128)(2,1)S(1)}, bf16[16,512]{1,0:T(8,128)(2,1)S(1)}, u32[]{:S(2)}, u32[]{:S(2)}) collective-permute-start(bf16[16,512]{1,0:T(8,128)(2,1)S(1)} %get-tuple-element.145), channel_id=1, source_target_pairs={{0,15},{1,2},{2,1},{3,4},{4,3},{5,6},{6,5},{7,8},{8,7},{9,10},{10,... | collective-permute-start | bytes 49160 | tf_op jit(solution)/shard_map/ppermute | solution.py:231
  39.6 6.2 %collective-permute-start.17 = (bf16[16,512]{1,0:T(8,128)(2,1)S(1)}, bf16[16,512]{1,0:T(8,128)(2,1)S(1)}, u32[]{:S(2)}, u32[]{:S(2)}) collective-permute-start(bf16[16,512]{1,0:T(8,128)(2,1)S(1)} %get-tuple-element.146), channel_id=1, source_target_pairs={{0,3},{1,14},{2,5},{3,0},{4,7},{5,2},{6,9},{7,4},{8,11},{9,6},{10,... | collective-permute-start | bytes 49160 | tf_op jit(solution)/shard_map/ppermute | solution.py:231
  41.5 5.0 %collective-permute-start.18 = (bf16[16,512]{1,0:T(8,128)(2,1)S(1)}, bf16[16,512]{1,0:T(8,128)(2,1)S(1)}, u32[]{:S(2)}, u32[]{:S(2)}) collective-permute-start(bf16[16,512]{1,0:T(8,128)(2,1)S(1)} %get-tuple-element.147), channel_id=1, source_target_pairs={{0,11},{1,6},{2,13},{3,8},{4,15},{5,10},{6,1},{7,12},{8,3},{9,14},... | collective-permute-start | bytes 49160 | tf_op jit(solution)/shard_map/ppermute | solution.py:231
  41.9 4.9 %collective-permute-start.19 = (bf16[16,512]{1,0:T(8,128)(2,1)S(1)}, bf16[16,512]{1,0:T(8,128)(2,1)S(1)}, u32[]{:S(2)}, u32[]{:S(2)}) collective-permute-start(bf16[16,512]{1,0:T(8,128)(2,1)S(1)} %get-tuple-element.148), channel_id=1, source_target_pairs={{0,8},{1,9},{2,10},{3,11},{4,12},{5,13},{6,14},{7,15},{8,0},{9,1},... | collective-permute-start | bytes 49160 | tf_op jit(solution)/shard_map/ppermute | solution.py:231
  43.9 3.0 %collective-permute-start.20 = (bf16[48,512]{1,0:T(8,128)(2,1)S(1)}, bf16[48,512]{1,0:T(8,128)(2,1)S(1)}, u32[]{:S(2)}, u32[]{:S(2)}) collective-permute-start(bf16[48,512]{1,0:T(8,128)(2,1)S(1)} %lay_together.5), channel_id=1, source_target_pairs={{0,1},{1,0},{2,3},{3,2},{4,5},{5,4},{6,7},{7,6},{8,9},{9,8},{10,11... | collective-permute-start | bytes 147464 | tf_op jit(solution)/shard_map/ppermute | solution.py:231
  (15 other events, 166.3 us)
